TPU v7x, 32 devices: a whole 2x2x4 slice. The times are simulated.
32 devices in a mesh: groups: 2 (over y), blk: 4 (over z), col: 2 (over x), ch: 2 (over core).
Axes of the slice: x: 2, y: 2, z: 4, core: 2. Of those that a mesh axis runs over, the one named last changes fastest.
Arguments:
- grad_out: bfloat16 [512, 64, 256], P(('groups', 'blk'), 'col', 'ch'), parts along dimension 0, may hold values from -6 to 6
- saved_input: bfloat16 [4, 4, 16, 12, 12, 256], P(('groups', 'col'), 'blk', None, None, None, 'ch'), parts along dimension 0, may hold values from -6 to 6
- saved_pre: bfloat16 [4, 4, 16, 10, 10, 256], P(('groups', 'col'), 'blk', None, None, None, 'ch'), parts along dimension 0, may hold values from -6 to 6
- first_weight: bfloat16 [9, 256, 256], P(None, 'ch'), may hold values from -0.125 to 0.125
- second_weight: bfloat16 [9, 256, 256], P(None, 'ch'), may hold values from -0.125 to 0.125
- assignment: int32 [4, 4, 16], P(('groups', 'col')), parts along dimension 0, may hold values from 0 to 127, as said below
Outputs:
- grad_in: bfloat16 [512, 64, 256], P(('groups', 'blk'), 'col', 'ch'), parts along dimension 0
- grad_first: float32 [18, 256, 256], P('groups', 'ch'), parts along dimension 0
- grad_second: float32 [18, 256, 256], P('groups', 'ch'), parts along dimension 0
There are 2 independent parts, one for each index of `groups`. A program takes and returns all parts, laid end to end along the dimension named above; an argument that names none is the same for every part. Nothing has to cross between parts.
Inputs may be any that keep to these rules, and one draw needn't show every extreme that they name: `assignment`: an entry r * 32 + p of column c names the block at position p (row-major over the 8 x 4 blocks) of the tile at owner row r of column c. Within one column every block is named at most once and exactly half of the column's blocks are named. In the list of one worker no owner row appears more than 8 times, and in every draw some owner row appears exactly 8 times in some worker's list.
All inputs are finite; a program needn't handle non-finite values.
Results may differ from a plain program's by a relative error of at most 0.0044.
Values may be sent and summed in bfloat16 or wider, within the bound.
No kernel may reach another device: no remote copies, remote signals or barrier semaphores. Data moves between devices by JAX's collectives and lax.ppermute only.
A program may use at most 64 MiB of HBM per device.

v0:
```python
import math

import jax
import jax.numpy as jnp
from jax import lax
from jax.sharding import PartitionSpec as P

BLOCK = 8
TILE_ROWS = 8
TILE_COLS = 4
TILE_BLOCKS = 32
PER_WORKER = 16
MIDDLE = 10
OUTER = 12


def extended_2(value, sides, width):
    for axis, dim in sides:
        size, length = (lax.axis_size(axis), value.shape[dim])
        up = [(i, (i + 1) % size) for i in range(size - 1)]
        down = [(j, i) for i, j in up]
        last = lax.slice_in_dim(value, length - width, length, axis=dim)
        leading = lax.slice_in_dim(value, 0, width, axis=dim)
        before = lax.ppermute(last, axis, up)
        after = lax.ppermute(leading, axis, down)
        value = jnp.concatenate([before, value, after], axis=dim)
    return value


def tap_slices(padded, extent):
    return [
        padded[:, row_off : row_off + extent, col_off : col_off + extent, :]
        for row_off in range(3)
        for col_off in range(3)
    ]


def transposed_conv(values, weight, extent):
    padded = jnp.pad(values, ((0, 0), (2, 2), (2, 2), (0, 0)))
    pieces = tap_slices(padded, extent)
    running = jnp.einsum("bpqo,io->bpqi", pieces[0], weight[8], preferred_element_type=jnp.float32)
    for number in range(1, 9):
        running = running + jnp.einsum(
            "bpqo,io->bpqi", pieces[number], weight[8 - number], preferred_element_type=jnp.float32
        )
    return running


def weight_terms(inputs, gradients, extent):
    pieces = tap_slices(inputs, extent)
    return jnp.stack(
        [
            jnp.einsum("bpqi,bpqo->io", shifted, gradients, preferred_element_type=jnp.float32)
            for shifted in pieces
        ]
    )


def fold_edges(values, along):
    extent = values.shape[along]
    middle_part = lax.slice_in_dim(values, 4, extent - 4, axis=along)
    low_rim = lax.slice_in_dim(values, 0, 2, axis=along)
    high_rim = lax.slice_in_dim(values, extent - 2, extent, axis=along)
    filler_shape = list(middle_part.shape)
    filler_shape[along] = middle_part.shape[along] - 4
    filler = jnp.zeros(filler_shape, values.dtype)
    return middle_part + jnp.concatenate([low_rim, filler, high_rim], axis=along)


def shards(grad_out, saved_input, saved_pre, first_weight, second_weight, assignment):
    owner_rows = lax.axis_size("blk")
    column_count = lax.axis_size("col")
    worker_id = lax.axis_index("blk")
    column = lax.axis_index("col")
    capacity = max(2, TILE_BLOCKS // owner_rows)
    routing = assignment[0]
    owners = routing // TILE_BLOCKS
    places = routing % TILE_BLOCKS
    earlier = jnp.arange(PER_WORKER)[None, :] < jnp.arange(PER_WORKER)[:, None]
    same_owner = owners[:, :, None] == owners[:, None, :]
    slot_rank = jnp.sum(same_owner & earlier[None], axis=2)
    is_mine = owners == worker_id
    slot_hits = is_mine[:, :, None] & (slot_rank[:, :, None] == jnp.arange(capacity)[None, None, :])
    send_place = jnp.sum(jnp.where(slot_hits, places[:, :, None], 0), axis=1)
    send_live = jnp.any(slot_hits, axis=1)
    source = lax.all_gather(grad_out, "ch", axis=2, tiled=True)
    chan_width = source.shape[2]
    blocks_all = source.reshape(TILE_ROWS, BLOCK, TILE_COLS, BLOCK, chan_width).transpose(
        0, 2, 1, 3, 4
    )
    blocks_all = blocks_all.reshape(TILE_BLOCKS, BLOCK, BLOCK, chan_width)
    outgoing = blocks_all[send_place.reshape(-1)].reshape(
        owner_rows, capacity, BLOCK, BLOCK, chan_width
    )
    incoming = lax.all_to_all(outgoing, "blk", split_axis=0, concat_axis=0, tiled=True)
    slot_owners = owners[worker_id]
    slot_order = slot_rank[worker_id]
    slot_places = places[worker_id]
    slot_index = slot_owners * capacity + slot_order
    received = incoming.reshape(owner_rows * capacity, BLOCK, BLOCK, chan_width)[slot_index]
    height = owner_rows * TILE_ROWS * BLOCK
    breadth = column_count * TILE_COLS * BLOCK
    block_row = slot_owners * TILE_ROWS + slot_places // TILE_COLS
    block_col = column * TILE_COLS + slot_places % TILE_COLS
    offsets = jnp.arange(MIDDLE) - 1
    row_global = block_row[:, None] * BLOCK + offsets[None, :]
    col_global = block_col[:, None] * BLOCK + offsets[None, :]
    row_ok = (row_global >= 0) & (row_global < height)
    col_ok = (col_global >= 0) & (col_global < breadth)
    inside = (row_ok[:, :, None] & col_ok[:, None, :])[..., None]
    pre_act = saved_pre.reshape(PER_WORKER, MIDDLE, MIDDLE, saved_pre.shape[5])
    saved_tiles = saved_input.reshape(PER_WORKER, OUTER, OUTER, saved_input.shape[5])
    live_mask = (pre_act > 0) & inside
    act_grad = transposed_conv(received, second_weight, MIDDLE)
    pre_grad = jnp.where(live_mask, act_grad, 0.0).astype(jnp.bfloat16)
    relu_act = jnp.where(live_mask, pre_act, jnp.zeros_like(pre_act))
    second_terms = weight_terms(relu_act, received, BLOCK)
    pre_grad_full = lax.all_gather(pre_grad, "ch", axis=3, tiled=True)
    input_grad = transposed_conv(pre_grad_full, first_weight, OUTER).astype(jnp.bfloat16)
    first_terms = weight_terms(saved_tiles, pre_grad_full, MIDDLE)
    half_width = input_grad.shape[3]
    back_buffer = (
        jnp.zeros((owner_rows * capacity, OUTER, OUTER, half_width), jnp.bfloat16)
        .at[slot_index]
        .set(input_grad)
    )
    back_buffer = back_buffer.reshape(owner_rows, capacity, OUTER, OUTER, half_width)
    returned = lax.all_to_all(back_buffer, "blk", split_axis=0, concat_axis=0, tiled=True)
    pad_rows = TILE_ROWS * BLOCK + 4
    pad_cols = TILE_COLS * BLOCK + 4
    place_flat = send_place.reshape(-1)
    live_flat = send_live.reshape(-1)
    tile_row = place_flat // TILE_COLS * BLOCK
    tile_col = place_flat % TILE_COLS * BLOCK
    pixel_span = jnp.arange(OUTER)
    flat_index = (
        (tile_row[:, None, None] + pixel_span[None, :, None]) * pad_cols
        + tile_col[:, None, None]
        + pixel_span[None, None, :]
    )
    flat_index = jnp.where(live_flat[:, None, None], flat_index, pad_rows * pad_cols)
    canvas = jnp.zeros((pad_rows * pad_cols, half_width), jnp.float32)
    canvas = canvas.at[flat_index.reshape(-1)].add(
        returned.reshape(-1, half_width).astype(jnp.float32), mode="drop"
    )
    canvas = canvas.reshape(pad_rows, pad_cols, half_width)
    extended = extended_2(canvas.astype(jnp.bfloat16), (("blk", 0),), 2).astype(canvas.dtype)
    folded = fold_edges(extended, 0)
    widened = extended_2(folded.astype(jnp.bfloat16), (("col", 1),), 2).astype(folded.dtype)
    summed = fold_edges(widened, 1)
    grad_in = (grad_out.astype(jnp.float32) + summed).astype(jnp.bfloat16)
    grad_scale = 1.0 / math.sqrt(owner_rows * column_count * PER_WORKER * BLOCK * BLOCK)
    grad_first, grad_second = lax.psum(
        (first_terms * grad_scale, second_terms * grad_scale), ("blk", "col")
    )
    return (grad_in, grad_first, grad_second)


def solution(mesh):
    return jax.shard_map(
        shards,
        mesh=mesh,
        in_specs=(
            P(("groups", "blk"), "col", "ch"),
            P(("groups", "col"), "blk", None, None, None, "ch"),
            P(("groups", "col"), "blk", None, None, None, "ch"),
            P(None, "ch", None),
            P(None, "ch", None),
            P(("groups", "col"), None, None),
        ),
        out_specs=(
            P(("groups", "blk"), "col", "ch"),
            P("groups", "ch", None),
            P("groups", "ch", None),
        ),
        check_vma=False,
    )
```

profile of v0, /device:TPU:0, one launch (start us, length us, event | category | flops | bytes accessed | tf_op | source)
XLA Modules:
  0.0 220.2 jit_solution(10696830174690236893)
XLA Ops:
  9.8 11.5 %all-gather.2.cloned.1.call-done = bf16[64,32,256]{2,1,0:T(8,128)(2,1)} async-done(((bf16[64,32,128]{2,1,0:T(8,128)(2,1)}), bf16[64,32,256]{2,1,0:T(8,128)(2,1)}) %all-gather.2.cloned.1.call-update) | async-done | bytes 1048592 | tf_op jit(solution)/shard_map/all_gather | solution.py:86
  21.3 1.3 copy.90
  22.6 1.6 gather_fusion
  24.2 5.0 %all-to-all-start = ((bf16[4,8,8,8,256]{4,3,2,1,0:T(8,128)(2,1)}), bf16[4,8,8,8,256]{4,3,2,1,0:T(8,128)(2,1)S(1)}, u32[]{:S(2)}, u32[]{:S(2)}) async-start(bf16[4,8,8,8,256]{4,3,2,1,0:T(8,128)(2,1)} %bitcast.10), calls=%async_computation | async-start | bytes 2097152 | tf_op jit(solution)/shard_map/all_to_all | solution.py:95
  29.7 25.7 %all-to-all-done = bf16[4,8,8,8,256]{4,3,2,1,0:T(8,128)(2,1)S(1)} async-done(((bf16[4,8,8,8,256]{4,3,2,1,0:T(8,128)(2,1)}), bf16[4,8,8,8,256]{4,3,2,1,0:T(8,128)(2,1)S(1)}, u32[]{:S(2)}, u32[]{:S(2)}) %all-to-all-start) | async-done | bytes 1048608 | tf_op jit(solution)/shard_map/all_to_all | solution.py:95
  60.3 1.2 fusion.12
  62.2 2.5 %all_gather.7 = bf16[16,10,10,256]{3,0,2,1:T(8,128)(2,1)S(1)} all-gather(bf16[16,10,10,128]{3,0,2,1:T(8,128)(2,1)S(1)} %fusion.3), channel_id=1, replica_groups=mesh['groups'=2,'blk'=4,'col'=2,'ch'=2] {'ch'}, dimensions={3}, use_global_device_ids=true | all-gather | bytes 1228800 | tf_op jit(solution)/shard_map/all_gather | solution.py:118
  70.3 2.2 scatter_fusion
  72.5 2.4 %copy.93 = bf16[4,8,12,12,128]{4,1,3,2,0:T(8,128)(2,1)} copy(bf16[4,8,12,12,128]{4,3,2,1,0:T(8,128)(2,1)S(1)} %bitcast.355) | data formatting | bytes 2359296 | tf_op jit(solution)/shard_map/reshape | solution.py:127
  74.9 4.4 %all-to-all-start.1 = ((bf16[4,8,12,12,128]{4,1,3,2,0:T(8,128)(2,1)}), bf16[4,8,12,12,128]{4,1,3,2,0:T(8,128)(2,1)}, u32[]{:S(2)}, u32[]{:S(2)}) async-start(bf16[4,8,12,12,128]{4,1,3,2,0:T(8,128)(2,1)} %copy.93), calls=%async_computation.1 | async-start | bytes 2359296 | tf_op jit(solution)/shard_map/all_to_all | solution.py:128
  90.3 1.2 broadcast_multiply_fusion
  92.0 32.1 %all-to-all-done.1 = bf16[4,8,12,12,128]{4,1,3,2,0:T(8,128)(2,1)} async-done(((bf16[4,8,12,12,128]{4,1,3,2,0:T(8,128)(2,1)}), bf16[4,8,12,12,128]{4,1,3,2,0:T(8,128)(2,1)}, u32[]{:S(2)}, u32[]{:S(2)}) %all-to-all-start.1) | async-done | bytes 1179680 | tf_op jit(solution)/shard_map/all_to_all | solution.py:128
  124.2 1.6 copy.94
  125.8 1.5 reshape.498
  127.3 25.6 %scatter_custom_fusion.1 = f32[2448,128]{1,0:T(8,128)S(1)} fusion(s32[4608]{0:T(1024)S(1)} %fusion.74, f32[4608,128]{1,0:T(8,128)} %reshape.498, f32[]{:T(128)} %constant.95.clone.1), kind=kCustom, calls=%fused_computation.68 | custom fusion | flops 589824 | bytes 1253888 | tf_op jit(solution)/shard_map/scatter-add | solution.py:143
  153.1 1.3 collective-permute-start.1
  154.4 4.5 %collective-permute-start = (bf16[2,36,128]{2,1,0:T(8,128)(2,1)S(1)}, bf16[2,36,128]{2,1,0:T(8,128)(2,1)S(1)}, u32[]{:S(2)}, u32[]{:S(2)}) collective-permute-start(bf16[2,36,128]{2,1,0:T(8,128)(2,1)S(1)} %slice.235), channel_id=1, source_target_pairs={{0,4},{4,8},{8,12},{1,5},{5,9},{9,13},{2,6},{6,10},{10,14},{3,7},{... | collective-permute-start | bytes 55304 | tf_op jit(solution)/shard_map/ppermute | solution.py:24
  159.2 1.3 collective-permute-done
  160.8 1.3 collective-permute-start.3
  162.1 4.5 %collective-permute-start.2 = (bf16[64,2,128]{2,1,0:T(2,128)(2,1)S(1)}, bf16[64,2,128]{2,1,0:T(2,128)(2,1)S(1)}, u32[]{:S(2)}, u32[]{:S(2)}) collective-permute-start(bf16[64,2,128]{2,1,0:T(2,128)(2,1)S(1)} %get-tuple-element.26), channel_id=1, source_target_pairs={{0,2},{1,3},{4,6},{5,7},{8,10},{9,11},{12,14},{13,15},{16,18},{17,... | collective-permute-start | bytes 98312 | tf_op jit(solution)/shard_map/ppermute | solution.py:24
  166.8 1.5 collective-permute-done.2
  170.6 38.6 %all-reduce.5.cloned.1.call-done = (f32[9,128,256]{1,2,0:T(8,128)}, f32[9,128,256]{1,2,0:T(8,128)}) async-done(((f32[9,128,256]{1,2,0:T(8,128)}, f32[9,128,256]{1,2,0:T(8,128)}), (f32[9,128,256]{1,2,0:T(8,128)}, f32[9,128,256]{1,2,0:T(8,128)})) %all-reduce.5.cloned.1.call-update) | async-done | bytes 2359312 | tf_op jit(solution)/shard_map/psum | solution.py:153
  209.2 2.7 %copy.113 = f32[9,128,256]{2,1,0:T(8,128)} copy(f32[9,128,256]{1,2,0:T(8,128)} %get-tuple-element.18) | data formatting | bytes 2359296
  212.0 1.4 copy.114
  (97 shorter events, 28.5 us)
Async XLA Ops:
  7.2 14.1 %all-gather.2.cloned.1.call-start = ((), (), s32[]{:S(2)}) async-start(), calls=%async_computation.2 | async-start | bytes 1572864 | tf_op jit(solution)/shard_map/all_gather | solution.py:86
  24.2 31.8 %copy-start.4 = (bf16[9,128,256]{2,1,0:T(8,128)(2,1)S(1)}, bf16[9,128,256]{2,1,0:T(8,128)(2,1)}, u32[]{:S(2)}) copy-start(bf16[9,128,256]{2,1,0:T(8,128)(2,1)} %param.10) | copy-start | bytes 1769476
  24.2 31.2 %all-to-all-start = ((bf16[4,8,8,8,256]{4,3,2,1,0:T(8,128)(2,1)}), bf16[4,8,8,8,256]{4,3,2,1,0:T(8,128)(2,1)S(1)}, u32[]{:S(2)}, u32[]{:S(2)}) async-start(bf16[4,8,8,8,256]{4,3,2,1,0:T(8,128)(2,1)} %bitcast.10), calls=%async_computation | async-start | bytes 2097152 | tf_op jit(solution)/shard_map/all_to_all | solution.py:95
  59.3 1.0 copy-start.6
  62.2 2.5 %copy-start.3 = (bf16[9,128,256]{2,1,0:T(8,128)(2,1)S(1)}, bf16[9,128,256]{2,1,0:T(8,128)(2,1)}, u32[]{:S(2)}) copy-start(bf16[9,128,256]{2,1,0:T(8,128)(2,1)} %param.9) | copy-start | bytes 1769476
  74.9 4.6 %copy-start.5 = (bf16[1,1,16,12,12,128]{5,2,4,3,1,0:T(8,128)(2,1)S(1)}, bf16[1,1,16,12,12,128]{5,2,4,3,1,0:T(8,128)(2,1)}, u32[]{:S(2)}) copy-start(bf16[1,1,16,12,12,128]{5,2,4,3,1,0:T(8,128)(2,1)} %param.7) | copy-start | bytes 1769476
  74.9 49.3 %all-to-all-start.1 = ((bf16[4,8,12,12,128]{4,1,3,2,0:T(8,128)(2,1)}), bf16[4,8,12,12,128]{4,1,3,2,0:T(8,128)(2,1)}, u32[]{:S(2)}, u32[]{:S(2)}) async-start(bf16[4,8,12,12,128]{4,1,3,2,0:T(8,128)(2,1)} %copy.93), calls=%async_computation.1 | async-start | bytes 2359296 | tf_op jit(solution)/shard_map/all_to_all | solution.py:128
  79.3 129.9 %all-reduce.5.cloned.1.call-start = ((), (), s32[]{:S(2)}) async-start(), calls=%async_computation.3 | async-start | bytes 4718592 | tf_op jit(solution)/shard_map/psum | solution.py:153
  82.7 1.3 copy-start.2
  153.1 6.1 %collective-permute-start.1 = (bf16[2,36,128]{2,1,0:T(8,128)(2,1)S(1)}, bf16[2,36,128]{2,1,0:T(8,128)(2,1)S(1)}, u32[]{:S(2)}, u32[]{:S(2)}) collective-permute-start(bf16[2,36,128]{2,1,0:T(8,128)(2,1)S(1)} %slice.237), channel_id=1, source_target_pairs={{4,0},{8,4},{12,8},{5,1},{9,5},{13,9},{6,2},{10,6},{14,10},{7,3},{... | collective-permute-start | bytes 55304 | tf_op jit(solution)/shard_map/ppermute | solution.py:25
  154.4 6.0 %collective-permute-start = (bf16[2,36,128]{2,1,0:T(8,128)(2,1)S(1)}, bf16[2,36,128]{2,1,0:T(8,128)(2,1)S(1)}, u32[]{:S(2)}, u32[]{:S(2)}) collective-permute-start(bf16[2,36,128]{2,1,0:T(8,128)(2,1)S(1)} %slice.235), channel_id=1, source_target_pairs={{0,4},{4,8},{8,12},{1,5},{5,9},{9,13},{2,6},{6,10},{10,14},{3,7},{... | collective-permute-start | bytes 55304 | tf_op jit(solution)/shard_map/ppermute | solution.py:24
  160.8 5.9 %collective-permute-start.3 = (bf16[64,2,128]{2,1,0:T(2,128)(2,1)S(1)}, bf16[64,2,128]{2,1,0:T(2,128)(2,1)S(1)}, u32[]{:S(2)}, u32[]{:S(2)}) collective-permute-start(bf16[64,2,128]{2,1,0:T(2,128)(2,1)S(1)} %get-tuple-element.27), channel_id=1, source_target_pairs={{2,0},{3,1},{6,4},{7,5},{10,8},{11,9},{14,12},{15,13},{18,16},{19,... | collective-permute-start | bytes 98312 | tf_op jit(solution)/shard_map/ppermute | solution.py:25
  162.1 6.1 %collective-permute-start.2 = (bf16[64,2,128]{2,1,0:T(2,128)(2,1)S(1)}, bf16[64,2,128]{2,1,0:T(2,128)(2,1)S(1)}, u32[]{:S(2)}, u32[]{:S(2)}) collective-permute-start(bf16[64,2,128]{2,1,0:T(2,128)(2,1)S(1)} %get-tuple-element.26), channel_id=1, source_target_pairs={{0,2},{1,3},{4,6},{5,7},{8,10},{9,11},{12,14},{13,15},{16,18},{17,... | collective-permute-start | bytes 98312 | tf_op jit(solution)/shard_map/ppermute | solution.py:24
  168.4 1.0 copy-start
  209.2 2.8 %copy-start.1 = (f32[9,128,256]{1,2,0:T(8,128)S(1)}, f32[9,128,256]{1,2,0:T(8,128)}, u32[]{:S(2)}) copy-start(f32[9,128,256]{1,2,0:T(8,128)} %get-tuple-element.19) | copy-start | bytes 3538948
Sparse Core Ops, SparseCore 0:
  9.5 11.6 all-gather.1
  91.7 117.5 all-reduce.4
where the time goes:
time: 221 us; the launch traced here: 220 us
  waiting for transfers between devices  111 us (50%)
  other arithmetic  32.3 us (15%)
  starting transfers between devices  21.4 us (10%)
  local copies, waits for them, and re-layouts  19.7 us (9%)
  matrix products  18.5 us (8%)
  between operations  14.5 us (7%)
  blocking collectives  2.53 us (1%)
    psum x1, waiting for transfers between devices, shards(): lax.psum((first_terms * grad_scale, second_terms * grad_scale), ('blk', '...  38.6 us
    all_to_all x1, waiting for transfers between devices, shards(): lax.all_to_all(back_buffer, 'blk', split_axis=0, concat_axis=0, tiled=True)  32.1 us
    all_to_all x1, waiting for transfers between devices, shards(): lax.all_to_all(outgoing, 'blk', split_axis=0, concat_axis=0, tiled=True)  25.7 us
    scatter-add x1, other arithmetic, shards(): canvas.at[flat_index.reshape(-1)]  25.6 us
    all_gather x1, waiting for transfers between devices, shards(): source = lax.all_gather(grad_out, 'ch', axis=2, tiled=True)  11.5 us
    dot_general x18, matrix products, weight_terms(): jnp.einsum('bpqi,bpqo->io', shifted, gradients, preferred_element_type=jn...  9.98 us
    ppermute x2, starting transfers between devices, extended_2(): before = lax.ppermute(last, axis, up)  9.09 us
    dot_general x16, matrix products, transposed_conv(): jnp.einsum('bpqo,io->bpqi', pieces[number], weight[8 - number], preferred...  7.61 us
  transfers between devices with their start and end apart: 8, of which 6 were waited for; matrix products, arithmetic and copies ran while one was open for 20% of the time, Pallas kernels for 0%

commit v1 on v0

v1 whole, which is shorter than its diff:
```python
import functools
import math

import jax
import jax.numpy as jnp
from jax import lax
from jax.experimental import pallas as pl
from jax.experimental.pallas import tpu as pltpu
from jax.sharding import PartitionSpec as P

BLOCK = 8
TILE_ROWS = 8
TILE_COLS = 4
TILE_BLOCKS = 32
PER_WORKER = 16
MIDDLE = 10
OUTER = 12
HALF = 128
FULL = 256
DEAD = -4096
WIDE = 40

BF16 = jnp.bfloat16
F32 = jnp.float32
I32 = jnp.int32

VMEM = pl.BlockSpec(memory_space=pltpu.VMEM)
SMEM = pl.BlockSpec(memory_space=pltpu.SMEM)


def call(body, outs, specs, scratch, cost, name):
    return pl.pallas_call(
        body,
        out_shape=outs,
        in_specs=specs,
        out_specs=jax.tree.map(lambda _: VMEM, outs),
        scratch_shapes=scratch,
        compiler_params=pltpu.CompilerParams(vmem_limit_bytes=48 * 1024 * 1024),
        cost_estimate=pl.CostEstimate(flops=cost[0], bytes_accessed=cost[1], transcendentals=0),
        name=name,
    )


def iota(shape, dim):
    return lax.broadcasted_iota(I32, shape, dim)


def one_hot(hits):
    return jnp.where(hits, 1.0, 0.0).astype(BF16)


def dot(a, b):
    return jnp.dot(a, b, preferred_element_type=F32)


def dot_nt(a, b):
    return lax.dot_general(a, b, (((1,), (1,)), ((), ())), preferred_element_type=F32)


def dot_tn(a, b):
    return lax.dot_general(a, b, (((0,), (0,)), ((), ())), preferred_element_type=F32)


def owner_table(routing, table, owners, capacity):
    me = lax.axis_index("blk")

    def clear(number, carry):
        table[number] = DEAD
        return carry

    lax.fori_loop(0, owners * capacity, clear, 0)

    def worker(number, carry):
        count = jnp.int32(0)
        for slot in range(PER_WORKER):
            code = routing[number, slot]
            hit = (code // TILE_BLOCKS) == me
            table[jnp.where(hit, number * capacity + count, owners * capacity)] = code % TILE_BLOCKS
            count = count + jnp.where(hit, 1, 0)
        return carry

    lax.fori_loop(0, owners, worker, 0)


def worker_codes(routing, counts, owners):
    me = lax.axis_index("blk")

    def clear(number, carry):
        counts[number] = 0
        return carry

    lax.fori_loop(0, owners, clear, 0)
    slots = []
    for slot in range(PER_WORKER):
        code = routing[me, slot]
        owner = code // TILE_BLOCKS
        rank = counts[owner]
        counts[owner] = rank + 1
        slots.append((owner, code % TILE_BLOCKS, rank))
    return slots


def pack_cotangents(owners, capacity, routing, tile, out, table):
    owner_table(routing, table, owners, capacity)
    rows = BLOCK * capacity
    row, lane = iota((rows, FULL), 0), iota((rows, FULL), 1)
    picks = []
    for worker in range(owners):
        target = jnp.full((rows, FULL), DEAD, I32)
        for rank in range(capacity):
            place = table[worker * capacity + rank] * BLOCK
            target = jnp.where(row % capacity == rank, place, target)
        picks.append(one_hot(lane == target + row // capacity))
    pick = jnp.concatenate(picks, axis=0)
    for u in range(0, BLOCK, 2):
        pair = [
            jnp.concatenate([tile[r, u + k] for r in range(TILE_ROWS)], axis=0) for k in range(2)
        ]
        moved = dot(pick, jnp.concatenate(pair, axis=1)).astype(BF16)
        for worker in range(owners):
            part = moved[worker * rows : (worker + 1) * rows]
            out[worker, u] = part[:, :HALF]
            out[worker, u + 1] = part[:, HALF:]


def pack_saved(owners, columns, capacity, wide, routing, saved, masked, out, counts, table):
    column = lax.axis_index("col")

    def clear(number, carry):
        table[number] = DEAD
        return carry

    lax.fori_loop(0, owners * capacity, clear, 0)
    slots = worker_codes(routing, counts, owners)
    rows = MIDDLE * PER_WORKER
    row = iota((rows, HALF), 0)
    flags = jnp.zeros((rows, HALF), I32)
    for slot, (owner, place, rank) in enumerate(slots):
        table[owner * capacity + rank] = slot
        block_row, block_col = place // TILE_COLS, place % TILE_COLS
        flag = (
            jnp.where((owner == 0) & (block_row == 0), 1, 0)
            + jnp.where((owner == owners - 1) & (block_row == TILE_ROWS - 1), 2, 0)
            + jnp.where((column == 0) & (block_col == 0), 4, 0)
            + jnp.where((column == columns - 1) & (block_col == TILE_COLS - 1), 8, 0)
        )
        flags = jnp.where(row % PER_WORKER == slot, flag, flags)
    across = row // PER_WORKER
    outside = (((flags & 4) != 0) & (across == 0)) | (((flags & 8) != 0) & (across == MIDDLE - 1))
    for m in range(MIDDLE):
        here = outside
        if m == 0:
            here = here | ((flags & 1) != 0)
        if m == MIDDLE - 1:
            here = here | ((flags & 2) != 0)
        masked[m] = jnp.where(here, 0.0, saved[m].astype(F32)).astype(BF16)
    size = wide * capacity
    row, lane = iota((size, FULL), 0), iota((size, FULL), 1)
    picks = []
    for owner in range(owners):
        target = jnp.full((size, FULL), DEAD, I32)
        for rank in range(capacity):
            target = jnp.where(row % capacity == rank, table[owner * capacity + rank], target)
        at = row // capacity
        picks.append(one_hot((lane == target + at * PER_WORKER) & (at < MIDDLE)))
    pick = jnp.concatenate(picks, axis=0)
    filler = jnp.zeros((FULL - rows, FULL), BF16)
    for m in range(0, MIDDLE, 2):
        pair = jnp.concatenate([masked[m], masked[m + 1]], axis=1)
        moved = dot(pick, jnp.concatenate([pair, filler], axis=0)).astype(BF16)
        for owner in range(owners):
            part = moved[owner * size : (owner + 1) * size]
            out[owner, m] = part[:, :HALF]
            out[owner, m + 1] = part[:, HALF:]


def ordered(own, other, axis):
    first = lax.axis_index("ch") == 0
    return jnp.concatenate(
        [jnp.where(first, own, other), jnp.where(first, other, own)], axis=axis
    )


def second_gradient(scale, owners, capacity, routing, own, other, masked, cot, out, counts):
    slots = worker_codes(routing, counts, owners)
    rows, inner = BLOCK * PER_WORKER, owners * BLOCK * capacity
    row, lane = iota((rows, inner), 0), iota((rows, inner), 1)
    target = jnp.full((rows, inner), DEAD, I32)
    for slot, (owner, place, rank) in enumerate(slots):
        target = jnp.where(
            row % PER_WORKER == slot, owner * (BLOCK * capacity) + rank, target
        )
    pick = one_hot(lane == target + (row // PER_WORKER) * capacity)
    for u in range(BLOCK):
        got = jnp.concatenate(
            [ordered(own[o, u], other[o, u], 1) for o in range(owners)], axis=0
        )
        cot[u] = dot(pick, got).astype(BF16)
    grads = cot[...].reshape(BLOCK * rows, FULL)
    for tap in range(9):
        dy, dx = tap // 3, tap % 3
        window = masked[dy : dy + BLOCK, dx : dx + BLOCK].reshape(BLOCK * rows, HALF)
        window = jnp.maximum(window, jnp.zeros_like(window))
        out[tap] = (dot_tn(window, grads) * scale).astype(BF16)


def first_gradient(
    scale, cot, masked, masked_other, weight, weight_other, saved, out, total, pre, full
):
    rows = BLOCK * BLOCK * PER_WORKER
    full[...] = ordered(weight[...], weight_other[...], 1)
    total[...] = jnp.zeros_like(total)
    for tap in range(9):
        dy, dx = tap // 3, tap % 3
        part = dot_nt(cot[...].reshape(rows, FULL), full[tap])
        spot = (slice(dy, dy + BLOCK), slice(dx, dx + BLOCK))
        total[spot] = total[spot] + part.reshape(BLOCK, BLOCK, PER_WORKER, FULL)
    for m in range(MIDDLE):
        live = ordered(masked[m], masked_other[m], 2).astype(F32) > 0
        pre[m] = jnp.where(live, total[m], 0.0).astype(BF16)
    size = MIDDLE * MIDDLE * PER_WORKER
    grads = pre[...].reshape(size, FULL)
    for tap in range(9):
        dy, dx = tap // 3, tap % 3
        window = saved[dy : dy + MIDDLE, dx : dx + MIDDLE].reshape(size, HALF)
        out[tap] = (dot_tn(window, grads) * scale).astype(BF16)


def owner_canvas(
    owners, capacity, wide, routing, tile, tile_other, got, got_other, second, second_other, first,
    canvas, table, cot, total, pre, full, grown,
):
    owner_table(routing, table, owners, capacity)
    row, lane = iota((FULL, FULL), 0), iota((FULL, FULL), 1)
    turn = one_hot(lane == (row % TILE_BLOCKS) * BLOCK + row // TILE_BLOCKS)
    for u in range(BLOCK):
        block = jnp.concatenate(
            [ordered(tile[r, u], tile_other[r, u], 1) for r in range(TILE_ROWS)], axis=0
        )
        cot[u] = dot(turn, block).astype(BF16)
    full[...] = ordered(second[...], second_other[...], 1)
    rows = BLOCK * BLOCK * TILE_BLOCKS
    total[...] = jnp.zeros_like(total)
    for tap in range(9):
        dy, dx = tap // 3, tap % 3
        part = dot_nt(cot[...].reshape(rows, FULL), full[tap])
        spot = (slice(dy, dy + BLOCK), slice(dx, dx + BLOCK))
        total[spot] = total[spot] + part.reshape(BLOCK, BLOCK, TILE_BLOCKS, FULL)
    size, into = wide * capacity, MIDDLE * TILE_BLOCKS
    row, lane = iota((size, into), 0), iota((size, into), 1)
    picks = []
    for worker in range(owners):
        target = jnp.full((size, into), DEAD, I32)
        for rank in range(capacity):
            target = jnp.where(row % capacity == rank, table[worker * capacity + rank], target)
        at = row // capacity
        hits = (lane == target + at * TILE_BLOCKS) & (at < MIDDLE)
        picks.append(jnp.where(hits, 1.0, 0.0))
    pick = jnp.concatenate(picks, axis=0).T.astype(BF16)
    for m in range(MIDDLE):
        block = jnp.concatenate(
            [ordered(got[w, m], got_other[w, m], 1) for w in range(owners)], axis=0
        )
        live = dot(pick, block).reshape(MIDDLE, TILE_BLOCKS, FULL) > 0
        pre[m] = jnp.where(live, total[m], 0.0).astype(BF16)
    size = MIDDLE * MIDDLE * TILE_BLOCKS
    grown[...] = jnp.zeros_like(grown)
    for tap in range(9):
        dy, dx = tap // 3, tap % 3
        part = dot_nt(pre[...].reshape(size, FULL), first[tap])
        spot = (slice(dy, dy + MIDDLE), slice(dx, dx + MIDDLE))
        grown[spot] = grown[spot] + part.reshape(MIDDLE, MIDDLE, TILE_BLOCKS, HALF)
    height, depth = TILE_ROWS * WIDE, OUTER * TILE_BLOCKS
    row, lane = iota((height, depth), 0), iota((height, depth), 1)
    at_row, at_col = row // WIDE, row % WIDE
    n, place = lane // TILE_BLOCKS, lane % TILE_BLOCKS
    column = (place % TILE_COLS) * BLOCK + n - 2
    column = jnp.where(column < 0, column + 36, column)
    fold = one_hot((at_row == place // TILE_COLS) & (at_col == column))
    canvas[...] = jnp.zeros_like(canvas)
    for m in range(0, OUTER, 2):
        pair = jnp.concatenate(
            [grown[m + k].reshape(depth, HALF).astype(BF16) for k in range(2)], axis=1
        )
        laid = dot(fold, pair).reshape(TILE_ROWS, WIDE, FULL)
        for r in range(TILE_ROWS):
            for k in range(2):
                canvas[r * BLOCK + m + k] += laid[r, :, k * HALF : (k + 1) * HALF]


def swap(value):
    return lax.ppermute(value, "ch", [(0, 1), (1, 0)])


def neighbours(axis):
    size = lax.axis_size(axis)
    up = [(i, (i + 1) % size) for i in range(size - 1)]
    return up, [(j, i) for i, j in up]


def shards(grad_out, saved_input, saved_pre, first_weight, second_weight, assignment):
    owners = lax.axis_size("blk")
    columns = lax.axis_size("col")
    capacity = max(2, TILE_BLOCKS // owners)
    wide = MIDDLE if (MIDDLE * capacity) % 16 == 0 else 16
    scale = 1.0 / math.sqrt(owners * columns * PER_WORKER * BLOCK * BLOCK)
    routing = assignment[0]
    shape = jax.ShapeDtypeStruct
    tables = [pltpu.SMEM((owners * capacity + 1,), I32)]
    counts = [pltpu.SMEM((owners,), I32)]

    tile = grad_out.reshape(TILE_ROWS, BLOCK, TILE_COLS * BLOCK, HALF)
    outgoing = call(
        functools.partial(pack_cotangents, owners, capacity),
        shape((owners, BLOCK, BLOCK * capacity, HALF), BF16),
        [SMEM, VMEM], tables, (2**28, 2**20), "pack_cotangents",
    )(routing, tile)
    incoming = lax.all_to_all(outgoing, "blk", split_axis=0, concat_axis=0, tiled=True)

    saved_slots = saved_pre[0, 0].transpose(1, 2, 0, 3)
    masked, to_owners = call(
        functools.partial(pack_saved, owners, columns, capacity, wide),
        (
            shape((MIDDLE, MIDDLE * PER_WORKER, HALF), BF16),
            shape((owners, MIDDLE, wide * capacity, HALF), BF16),
        ),
        [SMEM, VMEM], counts + tables, (2**28, 2**20), "pack_saved",
    )(routing, saved_slots.reshape(MIDDLE, MIDDLE * PER_WORKER, HALF))
    masked = masked.reshape(MIDDLE, MIDDLE, PER_WORKER, HALF)
    second_other = swap(second_weight)
    masked_other = swap(masked)
    tile_other = swap(tile)

    incoming_other = swap(incoming)
    at_owner = lax.all_to_all(to_owners, "blk", split_axis=0, concat_axis=0, tiled=True)
    cot, grad_second = call(
        functools.partial(second_gradient, scale, owners, capacity),
        (
            shape((BLOCK, BLOCK * PER_WORKER, FULL), BF16),
            shape((9, HALF, FULL), BF16),
        ),
        [SMEM, VMEM, VMEM, VMEM], counts, (2**30, 2**21), "second_gradient",
    )(routing, incoming, incoming_other, masked)
    grad_second = lax.psum(grad_second, ("blk", "col"))

    saved_tiles = saved_input[0, 0].transpose(1, 2, 0, 3)
    grad_first = call(
        functools.partial(first_gradient, scale),
        shape((9, HALF, FULL), BF16),
        [VMEM] * 6,
        [
            pltpu.VMEM((MIDDLE, MIDDLE, PER_WORKER, FULL), F32),
            pltpu.VMEM((MIDDLE, MIDDLE, PER_WORKER, FULL), BF16),
            pltpu.VMEM((9, FULL, FULL), BF16),
        ],
        (2**31, 2**22), "first_gradient",
    )(cot, masked, masked_other, second_weight, second_other, saved_tiles)
    grad_first = lax.psum(grad_first, ("blk", "col"))

    at_owner_other = swap(at_owner)
    height = TILE_ROWS * BLOCK + 4
    canvas = call(
        functools.partial(owner_canvas, owners, capacity, wide),
        shape((height, WIDE, HALF), F32),
        [SMEM] + [VMEM] * 7,
        tables
        + [
            pltpu.VMEM((BLOCK, FULL, FULL), BF16),
            pltpu.VMEM((MIDDLE, MIDDLE, TILE_BLOCKS, FULL), F32),
            pltpu.VMEM((MIDDLE, MIDDLE, TILE_BLOCKS, FULL), BF16),
            pltpu.VMEM((9, FULL, FULL), BF16),
            pltpu.VMEM((OUTER, OUTER, TILE_BLOCKS, HALF), F32),
        ],
        (2**32, 2**23), "owner_canvas",
    )(routing, tile, tile_other, at_owner, at_owner_other, second_weight, second_other, first_weight)

    up, down = neighbours("blk")
    from_above = lax.ppermute(canvas[height - 2 :].astype(BF16), "blk", up).astype(F32)
    from_below = lax.ppermute(canvas[:2].astype(BF16), "blk", down).astype(F32)
    inner = canvas[2 : height - 2]
    inner = inner.at[:2].add(from_above).at[-2:].add(from_below)
    up, down = neighbours("col")
    from_left = lax.ppermute(inner[:, 32:34].astype(BF16), "col", up).astype(F32)
    from_right = lax.ppermute(inner[:, 34:36].astype(BF16), "col", down).astype(F32)
    inner = inner[:, :32].at[:, :2].add(from_left).at[:, -2:].add(from_right)
    grad_in = (grad_out.astype(F32) + inner).astype(BF16)
    return (grad_in, grad_first.astype(F32), grad_second.astype(F32))


def solution(mesh):
    return jax.shard_map(
        shards,
        mesh=mesh,
        in_specs=(
            P(("groups", "blk"), "col", "ch"),
            P(("groups", "col"), "blk", None, None, None, "ch"),
            P(("groups", "col"), "blk", None, None, None, "ch"),
            P(None, "ch", None),
            P(None, "ch", None),
            P(("groups", "col"), None, None),
        ),
        out_specs=(
            P(("groups", "blk"), "col", "ch"),
            P("groups", "ch", None),
            P("groups", "ch", None),
        ),
        check_vma=False,
    )
```

time: 221 us -> 175 us (0.79)
  other arithmetic: 32.3 us -> 4.67 us
  Pallas kernels: 0 us -> 25.2 us
  matrix products: 18.5 us -> 0 us
  local copies, waits for them, and re-layouts: 19.7 us -> 5.75 us
  waiting for transfers between devices: 111 us -> 106 us
  starting transfers between devices: 21.4 us -> 18.5 us
  blocking collectives: 2.53 us -> 0 us
    psum x1, waiting for transfers between devices: 38.6 us -> 64.4 us  [shards(): grad_first = lax.psum(grad_first, ('blk', 'col'))]
    scatter-add x1 -> x4, other arithmetic: 25.6 us -> 0.17 us  [the longest x2 0.15 us: shards(): inner = inner[:, :32].at[:, :2].add(from_left).at[:, -2:].add(from_right)]
    pallas_call x0 -> x5, Pallas kernels: none -> 25.2 us  [the longest x1 12.3 us: shards(): call(functools.partial(owner_canvas, owners, capacity, wide), shape((heig...]
    dot_general x36 -> x0, matrix products: 18.5 us -> none  [the longest x18 9.98 us: weight_terms(): jnp.einsum('bpqi,bpqo->io', shifted, gradients, preferred_element_type=jn...]
    all_to_all x1, waiting for transfers between devices: 32.1 us -> 18.4 us  [shards(): lax.all_to_all(to_owners, 'blk', split_axis=0, concat_axis=0, tiled=True)]
    all_to_all x1, waiting for transfers between devices: 25.7 us -> 13.8 us  [shards(): lax.all_to_all(outgoing, 'blk', split_axis=0, concat_axis=0, tiled=True)]
    all_gather x1 -> x0, waiting for transfers between devices: 11.5 us -> none  [shards(): source = lax.all_gather(grad_out, 'ch', axis=2, tiled=True)]
    ppermute x4 -> x9, waiting for transfers between devices: 2.75 us -> 9.69 us  [the longest x1 4.35 us: shards(): from_below = lax.ppermute(canvas[:2].astype(BF16), 'blk', down).astype(F32)]
  transfers between devices with their start and end apart: 8 -> 12, of which waited for: 6 -> 7; matrix products, arithmetic and copies ran while one was open for 20% -> 1% of each run, Pallas kernels for 0% -> 13%
where the time goes in v1:
time: 175 us
  waiting for transfers between devices  106 us (61%)
  Pallas kernels  25.2 us (14%)
  starting transfers between devices  18.5 us (11%)
  between operations  14.2 us (8%)
  local copies, waits for them, and re-layouts  5.75 us (3%)
  other arithmetic  4.67 us (3%)
    psum x1, waiting for transfers between devices, shards(): grad_first = lax.psum(grad_first, ('blk', 'col'))  64.4 us
    all_to_all x1, waiting for transfers between devices, shards(): lax.all_to_all(to_owners, 'blk', split_axis=0, concat_axis=0, tiled=True)  18.4 us
    all_to_all x1, waiting for transfers between devices, shards(): lax.all_to_all(outgoing, 'blk', split_axis=0, concat_axis=0, tiled=True)  13.8 us
    pallas_call x1, Pallas kernels, shards(): call(functools.partial(owner_canvas, owners, capacity, wide), shape((heig...  12.3 us
    all_to_all x1, starting transfers between devices, shards(): lax.all_to_all(to_owners, 'blk', split_axis=0, concat_axis=0, tiled=True)  6.32 us
    unnamed x24, local copies, waits for them, and re-layouts  5.49 us
    pallas_call x1, Pallas kernels, shards(): call(functools.partial(first_gradient, scale), shape((9, HALF, FULL), BF1...  5.39 us
    ppermute x1, waiting for transfers between devices, shards(): from_below = lax.ppermute(canvas[:2].astype(BF16), 'blk', down).astype(F32)  4.35 us
  transfers between devices with their start and end apart: 12, of which 7 were waited for; matrix products, arithmetic and copies ran while one was open for 1% of the time, Pallas kernels for 13%

profile of v1, /device:TPU:0, one launch (start us, length us, event | category | flops | bytes accessed | tf_op | source)
XLA Modules:
  0.0 174.7 jit_solution(10945552557910777496)
XLA Ops:
  7.8 1.0 copy-done.8
  8.9 2.5 %pack_saved.1 = (bf16[10,160,128]{2,1,0:T(8,128)(2,1)S(1)}, bf16[4,10,80,128]{3,2,1,0:T(8,128)(2,1)}) custom-call(s32[4,16]{1,0:T(4,128)S(1)} %bitcast.14, bf16[10,160,128]{2,1,0:T(8,128)(2,1)S(1)} %bitcast.19), custom_call_target="tpu_custom_call" | custom-call | flops 268435456 | bytes 1048576 | tf_op jit(solution)/shard_map/pack_saved/pallas_call | solution.py:321
  12.1 6.3 %all-to-all-start = ((bf16[4,10,80,128]{3,2,1,0:T(8,128)(2,1)}), bf16[4,10,80,128]{3,2,1,0:T(8,128)(2,1)S(1)}, u32[]{:S(2)}, u32[]{:S(2)}) async-start(bf16[4,10,80,128]{3,2,1,0:T(8,128)(2,1)} %get-tuple-element.55), calls=%async_computation | async-start | bytes 1638400 | tf_op jit(solution)/shard_map/all_to_all | solution.py:335
  18.4 2.4 %pack_cotangents.1 = bf16[4,8,64,128]{3,2,1,0:T(8,128)(2,1)} custom-call(s32[4,16]{1,0:T(4,128)S(1)} %bitcast.15, bf16[8,8,32,128]{3,2,1,0:T(8,128)(2,1)S(1)} %bitcast.11), custom_call_target="tpu_custom_call" | custom-call | flops 268435456 | bytes 1048576 | tf_op jit(solution)/shard_map/pack_cotangents/pallas_call | solution.py:313
  20.8 18.4 %all-to-all-done.got = bf16[4,10,80,128]{3,2,1,0:T(8,128)(2,1)S(1)} async-done(((bf16[4,10,80,128]{3,2,1,0:T(8,128)(2,1)}), bf16[4,10,80,128]{3,2,1,0:T(8,128)(2,1)S(1)}, u32[]{:S(2)}, u32[]{:S(2)}) %all-to-all-start) | async-done | bytes 819232 | tf_op jit(solution)/shard_map/all_to_all | solution.py:335
  39.2 3.5 %all-to-all-start.1 = ((bf16[4,8,64,128]{3,2,1,0:T(8,128)(2,1)}), bf16[4,8,64,128]{3,2,1,0:T(8,128)(2,1)S(1)}, u32[]{:S(2)}, u32[]{:S(2)}) async-start(bf16[4,8,64,128]{3,2,1,0:T(8,128)(2,1)} %pack_cotangents.1), calls=%async_computation.1 | async-start | bytes 1048576 | tf_op jit(solution)/shard_map/all_to_all | solution.py:318
  42.8 13.8 %all-to-all-done.1.own = bf16[4,8,64,128]{3,2,1,0:T(8,128)(2,1)S(1)} async-done(((bf16[4,8,64,128]{3,2,1,0:T(8,128)(2,1)}), bf16[4,8,64,128]{3,2,1,0:T(8,128)(2,1)S(1)}, u32[]{:S(2)}, u32[]{:S(2)}) %all-to-all-start.1) | async-done | bytes 524320 | tf_op jit(solution)/shard_map/all_to_all | solution.py:318
  57.7 0.9 collective-permute-done.7.other
  58.5 1.0 copy-done.10
  59.5 2.6 %second_gradient.1 = (bf16[8,128,256]{2,1,0:T(8,128)(2,1)S(1)}, bf16[9,128,256]{2,1,0:T(8,128)(2,1)}) custom-call(s32[4,16]{1,0:T(4,128)S(1)} %bitcast.16, bf16[4,8,64,128]{3,2,1,0:T(8,128)(2,1)S(1)} %all-to-all-done.1.own, bf16[4,8,64,128]{3,2,1,0:T(8,128)(2,1)S(1)} %collective-permute-done.7.other, bf16[10,10,16,128]{3,2,1,0:T(8,128)(2,1)S(1)} %bitcast.21), custom_call_target="tpu_custom_call" | custom-call | flops 1073741824 | bytes 2097152 | tf_op jit(solution)/shard_map/second_gradient/pallas_call | solution.py:336
  62.2 0.9 copy-done.3
  63.1 1.1 copy-done.4
  64.2 12.3 %owner_canvas.1 = f32[68,40,128]{2,1,0:T(8,128)S(1)} custom-call(s32[4,16]{1,0:T(4,128)S(1)} %bitcast.17, bf16[8,8,32,128]{3,2,1,0:T(8,128)(2,1)S(1)} %bitcast.13, bf16[8,8,32,128]{3,2,1,0:T(8,128)(2,1)S(1)} %collective-permute-done.tile_other, bf16[4,10,80,128]{3,2,1,0:T(8,128)(2,1)S(1)} %all-to-all-done.got, bf16[4,10,80,128]{3,2,1,0:T(8,128)(2,1)S(1)} %copy-done.4, ...), custom_call_target="tpu_custom_call" | custom-call | flops 4294967296 | bytes 8388608 | tf_op jit(solution)/shard_map/owner_canvas/pallas_call | solution.py:362
  76.7 1.6 collective-permute-start.3
  78.3 5.4 %first_gradient.1 = bf16[9,128,256]{2,1,0:T(8,128)(2,1)} custom-call(bf16[8,128,256]{2,1,0:T(8,128)(2,1)S(1)} %get-tuple-element.57.cot, bf16[10,10,16,128]{3,2,1,0:T(8,128)(2,1)S(1)} %bitcast.22, bf16[10,10,16,128]{3,2,1,0:T(8,128)(2,1)S(1)} %collective-permute-done.8.masked_other, bf16[9,128,256]{2,1,0:T(8,128)(2,1)S(1)} %copy-done.6, ...), custom_call_target="tpu_custom_call" | custom-call | flops 2147483648 | bytes 4194304 | tf_op jit(solution)/shard_map/first_gradient/pallas_call | solution.py:347
  83.8 1.3 collective-permute-start.4
  85.1 4.4 %collective-permute-done.4 = bf16[2,40,128]{2,1,0:T(8,128)(2,1)S(1)} collective-permute-done((bf16[2,40,128]{2,1,0:T(8,128)(2,1)S(1)}, bf16[2,40,128]{2,1,0:T(8,128)(2,1)S(1)}, u32[]{:S(2)}, u32[]{:S(2)}) %collective-permute-start.4) | collective-permute-done | bytes 20512 | tf_op jit(solution)/shard_map/ppermute | solution.py:379
  89.7 3.4 %collective-permute-start.5 = (bf16[64,2,128]{2,1,0:T(2,128)(2,1)S(1)}, bf16[64,2,128]{2,1,0:T(2,128)(2,1)S(1)}, u32[]{:S(2)}, u32[]{:S(2)}) collective-permute-start(bf16[64,2,128]{2,1,0:T(2,128)(2,1)S(1)} %get-tuple-element.64), channel_id=1, source_target_pairs={{0,2},{1,3},{4,6},{5,7},{8,10},{9,11},{12,14},{13,15},{16,18},{17,... | collective-permute-start | bytes 98312 | tf_op jit(solution)/shard_map/ppermute | solution.py:383
  93.2 1.3 collective-permute-start.6
  94.7 4.3 %collective-permute-done.6 = bf16[64,2,128]{2,1,0:T(2,128)(2,1)S(1)} collective-permute-done((bf16[64,2,128]{2,1,0:T(2,128)(2,1)S(1)}, bf16[64,2,128]{2,1,0:T(2,128)(2,1)S(1)}, u32[]{:S(2)}, u32[]{:S(2)}) %collective-permute-start.6) | collective-permute-done | bytes 32800 | tf_op jit(solution)/shard_map/ppermute | solution.py:384
  99.1 1.0 add_convert_fusion
  100.1 64.4 %all-reduce.3.cloned.1.call-done = (bf16[9,128,256]{2,1,0:T(8,128)(2,1)}, bf16[9,128,256]{2,1,0:T(8,128)(2,1)}) async-done(((bf16[9,128,256]{2,1,0:T(8,128)(2,1)}, bf16[9,128,256]{2,1,0:T(8,128)(2,1)}), (bf16[9,128,256]{2,1,0:T(8,128)(2,1)}, bf16[9,128,256]{2,1,0:T(8,128)(2,1)})) %all-reduce.3.cloned.1.call-update) | async-done | bytes 1179664 | tf_op jit(solution)/shard_map/psum | solution.py:358
  164.5 2.2 %convert_element_type.34 = f32[9,128,256]{2,1,0:T(8,128)} convert(bf16[9,128,256]{2,1,0:T(8,128)(2,1)} %get-tuple-element.59) | non-fusion elementwise | flops 294912 | bytes 1769472 | tf_op jit(solution)/shard_map/convert_element_type | solution.py:387
  166.7 1.1 convert_element_type.35
  (43 shorter events, 3.4 us)
Async XLA Ops:
  7.2 0.7 copy-start.1
  7.8 1.0 copy-start.8
  8.8 9.5 %copy-start = (bf16[64,32,128]{2,1,0:T(8,128)(2,1)S(1)}, bf16[64,32,128]{2,1,0:T(8,128)(2,1)}, u32[]{:S(2)}) copy-start(bf16[64,32,128]{2,1,0:T(8,128)(2,1)} %param.14) | copy-start | bytes 1572868
  8.9 9.5 %copy-start.2 = (s32[1,4,16]{2,1,0:T(4,128)S(1)}, s32[1,4,16]{2,1,0:T(4,128)}, u32[]{:S(2)}) copy-start(s32[1,4,16]{2,1,0:T(4,128)} %param.19) | copy-start | bytes 772
  11.3 0.8 copy-start.9
  12.1 27.1 %all-to-all-start = ((bf16[4,10,80,128]{3,2,1,0:T(8,128)(2,1)}), bf16[4,10,80,128]{3,2,1,0:T(8,128)(2,1)S(1)}, u32[]{:S(2)}, u32[]{:S(2)}) async-start(bf16[4,10,80,128]{3,2,1,0:T(8,128)(2,1)} %get-tuple-element.55), calls=%async_computation | async-start | bytes 1638400 | tf_op jit(solution)/shard_map/all_to_all | solution.py:335
  18.4 38.3 %copy-start.6 = (bf16[9,128,256]{2,1,0:T(8,128)(2,1)S(1)}, bf16[9,128,256]{2,1,0:T(8,128)(2,1)}, u32[]{:S(2)}) copy-start(bf16[9,128,256]{2,1,0:T(8,128)(2,1)} %weight.1) | copy-start | bytes 1769476
  39.2 17.4 %all-to-all-start.1 = ((bf16[4,8,64,128]{3,2,1,0:T(8,128)(2,1)}), bf16[4,8,64,128]{3,2,1,0:T(8,128)(2,1)S(1)}, u32[]{:S(2)}, u32[]{:S(2)}) async-start(bf16[4,8,64,128]{3,2,1,0:T(8,128)(2,1)} %pack_cotangents.1), calls=%async_computation.1 | async-start | bytes 1048576 | tf_op jit(solution)/shard_map/all_to_all | solution.py:318
  42.7 121.8 %all-reduce.3.cloned.1.call-start = ((), (), s32[]{:S(2)}) async-start(), calls=%async_computation.2 | async-start | bytes 2359296 | tf_op jit(solution)/shard_map/psum | solution.py:358
  42.7 19.4 %collective-permute-start.1 = (bf16[4,10,80,128]{3,2,1,0:T(8,128)(2,1)S(1)}, bf16[4,10,80,128]{3,2,1,0:T(8,128)(2,1)S(1)}, u32[]{:S(2)}, u32[]{:S(2)}) collective-permute-start(bf16[4,10,80,128]{3,2,1,0:T(8,128)(2,1)S(1)} %all-to-all-done.got), channel_id=1, source_target_pairs={{0,1},{1,0},{2,3},{3,2},{4,5},{5,4},{6,7},{7,6},{8,9},{9,8},{10,11... | collective-permute-start | bytes 2457608 | tf_op jit(solution)/shard_map/ppermute | solution.py:292
  56.6 1.9 %collective-permute-start.7 = (bf16[4,8,64,128]{3,2,1,0:T(8,128)(2,1)S(1)}, bf16[4,8,64,128]{3,2,1,0:T(8,128)(2,1)S(1)}, u32[]{:S(2)}, u32[]{:S(2)}) collective-permute-start(bf16[4,8,64,128]{3,2,1,0:T(8,128)(2,1)S(1)} %all-to-all-done.1.own), channel_id=1, source_target_pairs={{0,1},{1,0},{2,3},{3,2},{4,5},{5,4},{6,7},{7,6},{8,9},{9,8},{10,11... | collective-permute-start | bytes 1572872 | tf_op jit(solution)/shard_map/ppermute | solution.py:292
  56.6 5.5 %collective-permute-start.2 = (bf16[9,128,256]{2,1,0:T(8,128)(2,1)S(1)}, bf16[9,128,256]{2,1,0:T(8,128)(2,1)S(1)}, u32[]{:S(2)}, u32[]{:S(2)}) collective-permute-start(bf16[9,128,256]{2,1,0:T(8,128)(2,1)S(1)} %copy-done.6), channel_id=1, source_target_pairs={{0,1},{1,0},{2,3},{3,2},{4,5},{5,4},{6,7},{7,6},{8,9},{9,8},{10,11... | collective-permute-start | bytes 1769480 | tf_op jit(solution)/shard_map/ppermute | solution.py:292
  57.1 5.0 %collective-permute-start = (bf16[8,8,32,128]{3,2,1,0:T(8,128)(2,1)S(1)}, bf16[8,8,32,128]{3,2,1,0:T(8,128)(2,1)S(1)}, u32[]{:S(2)}, u32[]{:S(2)}) collective-permute-start(bf16[8,8,32,128]{3,2,1,0:T(8,128)(2,1)S(1)} %bitcast.12), channel_id=1, source_target_pairs={{0,1},{1,0},{2,3},{3,2},{4,5},{5,4},{6,7},{7,6},{8,9},{9,8},{10,11... | collective-permute-start | bytes 1572872 | tf_op jit(solution)/shard_map/ppermute | solution.py:292
  57.2 5.9 %copy-start.5 = (bf16[9,128,256]{2,1,0:T(8,128)(2,1)S(1)}, bf16[9,128,256]{2,1,0:T(8,128)(2,1)}, u32[]{:S(2)}) copy-start(bf16[9,128,256]{2,1,0:T(8,128)(2,1)} %first.1) | copy-start | bytes 1769476
  57.2 21.1 %collective-permute-start.8 = (bf16[10,10,16,128]{3,2,1,0:T(8,128)(2,1)}, bf16[10,10,16,128]{3,2,1,0:T(8,128)(2,1)S(1)}, u32[]{:S(2)}, u32[]{:S(2)}) collective-permute-start(bf16[10,10,16,128]{3,2,1,0:T(8,128)(2,1)} %bitcast.20), channel_id=1, source_target_pairs={{0,1},{1,0},{2,3},{3,2},{4,5},{5,4},{6,7},{7,6},{8,9},{9,8},{10,11... | collective-permute-start | bytes 1228808 | tf_op jit(solution)/shard_map/ppermute | solution.py:292
  58.5 1.0 copy-start.10
  62.2 0.9 copy-start.3
  63.1 1.1 copy-start.4
  76.6 1.8 %copy-start.7 = (bf16[1,1,16,12,12,128]{5,2,4,3,1,0:T(8,128)(2,1)S(1)}, bf16[1,1,16,12,12,128]{5,2,4,3,1,0:T(8,128)(2,1)}, u32[]{:S(2)}) copy-start(bf16[1,1,16,12,12,128]{5,2,4,3,1,0:T(8,128)(2,1)} %param.15) | copy-start | bytes 1769476
  76.7 8.4 %collective-permute-start.3 = (bf16[2,40,128]{2,1,0:T(8,128)(2,1)S(1)}, bf16[2,40,128]{2,1,0:T(8,128)(2,1)S(1)}, u32[]{:S(2)}, u32[]{:S(2)}) collective-permute-start(bf16[2,40,128]{2,1,0:T(8,128)(2,1)S(1)} %get-tuple-element.62), channel_id=1, source_target_pairs={{0,4},{4,8},{8,12},{1,5},{5,9},{9,13},{2,6},{6,10},{10,14},{3,7},{... | collective-permute-start | bytes 61448 | tf_op jit(solution)/shard_map/ppermute | solution.py:378
  83.8 5.7 %collective-permute-start.4 = (bf16[2,40,128]{2,1,0:T(8,128)(2,1)S(1)}, bf16[2,40,128]{2,1,0:T(8,128)(2,1)S(1)}, u32[]{:S(2)}, u32[]{:S(2)}) collective-permute-start(bf16[2,40,128]{2,1,0:T(8,128)(2,1)S(1)} %get-tuple-element.61), channel_id=1, source_target_pairs={{4,0},{8,4},{12,8},{5,1},{9,5},{13,9},{6,2},{10,6},{14,10},{7,3},{... | collective-permute-start | bytes 61448 | tf_op jit(solution)/shard_map/ppermute | solution.py:379
  89.7 5.0 %collective-permute-start.5 = (bf16[64,2,128]{2,1,0:T(2,128)(2,1)S(1)}, bf16[64,2,128]{2,1,0:T(2,128)(2,1)S(1)}, u32[]{:S(2)}, u32[]{:S(2)}) collective-permute-start(bf16[64,2,128]{2,1,0:T(2,128)(2,1)S(1)} %get-tuple-element.64), channel_id=1, source_target_pairs={{0,2},{1,3},{4,6},{5,7},{8,10},{9,11},{12,14},{13,15},{16,18},{17,... | collective-permute-start | bytes 98312 | tf_op jit(solution)/shard_map/ppermute | solution.py:383
  93.2 5.8 %collective-permute-start.6 = (bf16[64,2,128]{2,1,0:T(2,128)(2,1)S(1)}, bf16[64,2,128]{2,1,0:T(2,128)(2,1)S(1)}, u32[]{:S(2)}, u32[]{:S(2)}) collective-permute-start(bf16[64,2,128]{2,1,0:T(2,128)(2,1)S(1)} %get-tuple-element.63), channel_id=1, source_target_pairs={{2,0},{3,1},{6,4},{7,5},{10,8},{11,9},{14,12},{15,13},{18,16},{19,... | collective-permute-start | bytes 98312 | tf_op jit(solution)/shard_map/ppermute | solution.py:384
  164.5 2.3 %copy-start.11 = (bf16[9,128,256]{2,1,0:T(8,128)(2,1)S(1)}, bf16[9,128,256]{2,1,0:T(8,128)(2,1)}, u32[]{:S(2)}) copy-start(bf16[9,128,256]{2,1,0:T(8,128)(2,1)} %get-tuple-element.60) | copy-start | bytes 1769476
Sparse Core Ops, SparseCore 0:
  83.8 80.5 all-reduce.2

commit v2 on v1

--- a/solution.py
+++ b/solution.py
@@ -100,12 +100,22 @@
     return slots
 
 
-def pack_cotangents(owners, capacity, routing, tile, out, table):
+def views(refs, count):
+    return list(refs) if len(refs) == count else [refs[0].at[k] for k in range(count)]
+
+
+def partner(axis, step, permuted):
+    return step ^ lax.axis_index(axis) if permuted else step
+
+
+def pack_cotangents(owners, capacity, permuted, routing, tile, *refs):
+    outs, table = refs[:-1], refs[-1]
     owner_table(routing, table, owners, capacity)
     rows = BLOCK * capacity
     row, lane = iota((rows, FULL), 0), iota((rows, FULL), 1)
     picks = []
-    for worker in range(owners):
+    for step in range(owners):
+        worker = partner("blk", step, permuted)
         target = jnp.full((rows, FULL), DEAD, I32)
         for rank in range(capacity):
             place = table[worker * capacity + rank] * BLOCK
@@ -117,13 +127,14 @@
             jnp.concatenate([tile[r, u + k] for r in range(TILE_ROWS)], axis=0) for k in range(2)
         ]
         moved = dot(pick, jnp.concatenate(pair, axis=1)).astype(BF16)
-        for worker in range(owners):
-            part = moved[worker * rows : (worker + 1) * rows]
-            out[worker, u] = part[:, :HALF]
-            out[worker, u + 1] = part[:, HALF:]
-
-
-def pack_saved(owners, columns, capacity, wide, routing, saved, masked, out, counts, table):
+        for step, out in enumerate(views(outs, owners)):
+            part = moved[step * rows : (step + 1) * rows]
+            out[u] = part[:, :HALF]
+            out[u + 1] = part[:, HALF:]
+
+
+def pack_saved(owners, columns, capacity, wide, permuted, routing, saved, masked, *refs):
+    outs, counts, table = refs[:-2], refs[-2], refs[-1]
     column = lax.axis_index("col")
 
     def clear(number, carry):
@@ -157,7 +168,8 @@
     size = wide * capacity
     row, lane = iota((size, FULL), 0), iota((size, FULL), 1)
     picks = []
-    for owner in range(owners):
+    for step in range(owners):
+        owner = partner("blk", step, permuted)
         target = jnp.full((size, FULL), DEAD, I32)
         for rank in range(capacity):
             target = jnp.where(row % capacity == rank, table[owner * capacity + rank], target)
@@ -168,10 +180,10 @@
     for m in range(0, MIDDLE, 2):
         pair = jnp.concatenate([masked[m], masked[m + 1]], axis=1)
         moved = dot(pick, jnp.concatenate([pair, filler], axis=0)).astype(BF16)
-        for owner in range(owners):
-            part = moved[owner * size : (owner + 1) * size]
-            out[owner, m] = part[:, :HALF]
-            out[owner, m + 1] = part[:, HALF:]
+        for step, out in enumerate(views(outs, owners)):
+            part = moved[step * size : (step + 1) * size]
+            out[m] = part[:, :HALF]
+            out[m + 1] = part[:, HALF:]
 
 
 def ordered(own, other, axis):
@@ -181,19 +193,36 @@
     )
 
 
-def second_gradient(scale, owners, capacity, routing, own, other, masked, cot, out, counts):
+def halves(value, keep, send, tap):
+    low, high = value[: HALF // 2], value[HALF // 2 :]
+    mine = lax.axis_index("col") == 0
+    keep[tap] = jnp.where(mine, low, high)
+    send[tap] = jnp.where(mine, high, low).astype(BF16)
+
+
+def emit(value, outs, tap):
+    if len(outs) == 2:
+        halves(value, outs[0], outs[1], tap)
+    else:
+        outs[0][tap] = value
+
+
+def second_gradient(scale, owners, capacity, permuted, routing, *refs):
+    parts = 1 if not permuted else owners
+    own, other = views(refs[:parts], owners), views(refs[parts : 2 * parts], owners)
+    masked, cot = refs[2 * parts : 2 * parts + 2]
+    outs, counts = refs[2 * parts + 2 : -1], refs[-1]
     slots = worker_codes(routing, counts, owners)
     rows, inner = BLOCK * PER_WORKER, owners * BLOCK * capacity
     row, lane = iota((rows, inner), 0), iota((rows, inner), 1)
     target = jnp.full((rows, inner), DEAD, I32)
     for slot, (owner, place, rank) in enumerate(slots):
-        target = jnp.where(
-            row % PER_WORKER == slot, owner * (BLOCK * capacity) + rank, target
-        )
+        step = partner("blk", owner, permuted)
+        target = jnp.where(row % PER_WORKER == slot, step * (BLOCK * capacity) + rank, target)
     pick = one_hot(lane == target + (row // PER_WORKER) * capacity)
     for u in range(BLOCK):
         got = jnp.concatenate(
-            [ordered(own[o, u], other[o, u], 1) for o in range(owners)], axis=0
+            [ordered(own[o][u], other[o][u], 1) for o in range(owners)], axis=0
         )
         cot[u] = dot(pick, got).astype(BF16)
     grads = cot[...].reshape(BLOCK * rows, FULL)
@@ -201,12 +230,13 @@
         dy, dx = tap // 3, tap % 3
         window = masked[dy : dy + BLOCK, dx : dx + BLOCK].reshape(BLOCK * rows, HALF)
         window = jnp.maximum(window, jnp.zeros_like(window))
-        out[tap] = (dot_tn(window, grads) * scale).astype(BF16)
+        emit(dot_tn(window, grads) * scale, outs, tap)
 
 
 def first_gradient(
-    scale, cot, masked, masked_other, weight, weight_other, saved, out, total, pre, full
+    scale, cot, masked, masked_other, weight, weight_other, saved, *refs
 ):
+    outs, (total, pre, full) = refs[:-3], refs[-3:]
     rows = BLOCK * BLOCK * PER_WORKER
     full[...] = ordered(weight[...], weight_other[...], 1)
     total[...] = jnp.zeros_like(total)
@@ -223,14 +253,10 @@
     for tap in range(9):
         dy, dx = tap // 3, tap % 3
         window = saved[dy : dy + MIDDLE, dx : dx + MIDDLE].reshape(size, HALF)
-        out[tap] = (dot_tn(window, grads) * scale).astype(BF16)
-
-
-def owner_canvas(
-    owners, capacity, wide, routing, tile, tile_other, got, got_other, second, second_other, first,
-    canvas, table, cot, total, pre, full, grown,
-):
-    owner_table(routing, table, owners, capacity)
+        emit(dot_tn(window, grads) * scale, outs, tap)
+
+
+def owner_spread(tile, tile_other, second, second_other, total, cot, full):
     row, lane = iota((FULL, FULL), 0), iota((FULL, FULL), 1)
     turn = one_hot(lane == (row % TILE_BLOCKS) * BLOCK + row // TILE_BLOCKS)
     for u in range(BLOCK):
@@ -246,10 +272,18 @@
         part = dot_nt(cot[...].reshape(rows, FULL), full[tap])
         spot = (slice(dy, dy + BLOCK), slice(dx, dx + BLOCK))
         total[spot] = total[spot] + part.reshape(BLOCK, BLOCK, TILE_BLOCKS, FULL)
+
+
+def owner_canvas(owners, capacity, wide, permuted, routing, *refs):
+    parts = 1 if not permuted else owners
+    got, got_other = views(refs[:parts], owners), views(refs[parts : 2 * parts], owners)
+    total, first, canvas, table, pre, grown = refs[2 * parts :]
+    owner_table(routing, table, owners, capacity)
     size, into = wide * capacity, MIDDLE * TILE_BLOCKS
     row, lane = iota((size, into), 0), iota((size, into), 1)
     picks = []
-    for worker in range(owners):
+    for step in range(owners):
+        worker = partner("blk", step, permuted)
         target = jnp.full((size, into), DEAD, I32)
         for rank in range(capacity):
             target = jnp.where(row % capacity == rank, table[worker * capacity + rank], target)
@@ -259,7 +293,7 @@
     pick = jnp.concatenate(picks, axis=0).T.astype(BF16)
     for m in range(MIDDLE):
         block = jnp.concatenate(
-            [ordered(got[w, m], got_other[w, m], 1) for w in range(owners)], axis=0
+            [ordered(got[w][m], got_other[w][m], 1) for w in range(owners)], axis=0
         )
         live = dot(pick, block).reshape(MIDDLE, TILE_BLOCKS, FULL) > 0
         pre[m] = jnp.where(live, total[m], 0.0).astype(BF16)
@@ -288,8 +322,48 @@
                 canvas[r * BLOCK + m + k] += laid[r, :, k * HALF : (k + 1) * HALF]
 
 
-def swap(value):
-    return lax.ppermute(value, "ch", [(0, 1), (1, 0)])
+def add_columns(columns_of, *refs):
+    kept, got, outs, sums = refs[:2], refs[2:4], refs[4:-1], refs[-1]
+    for k in range(2):
+        sums[k] = kept[k][...] + got[k][...].astype(F32)
+    size = HALF // 2 // len(outs)
+    for step, out in enumerate(outs):
+        at = pl.multiple_of(partner("blk", step, True) * size, size)
+        part = sums[:, :, pl.ds(at, size), :]
+        out[...] = part if step == 0 else part.astype(BF16)
+
+
+def add_workers(kept, *refs):
+    got, outs = refs[:-2], refs[-2:]
+    for k in range(2):
+        value = kept[k]
+        for part in got:
+            value = value + part[k].astype(F32)
+        outs[k][...] = value.astype(BF16)
+
+
+def lay_parts(*refs):
+    parts, out = refs[:-1], refs[-1]
+    size = HALF // 2 // len(parts)
+    for step, part in enumerate(parts):
+        at = pl.multiple_of(partner("blk", step, True) * size, size)
+        out[:, pl.ds(at, size), :] = part[...]
+
+
+def lay_halves(own, other, out):
+    mine = lax.axis_index("col") == 0
+    for tap in range(9):
+        out[tap, : HALF // 2] = jnp.where(mine, own[tap], other[tap]).astype(F32)
+        out[tap, HALF // 2 :] = jnp.where(mine, other[tap], own[tap]).astype(F32)
+
+
+def swap(value, axis="ch"):
+    return lax.ppermute(value, axis, [(0, 1), (1, 0)])
+
+
+def flip(value, axis, step):
+    size = lax.axis_size(axis)
+    return lax.ppermute(value, axis, [(i, i ^ step) for i in range(size)])
 
 
 def neighbours(axis):
@@ -304,75 +378,118 @@
     capacity = max(2, TILE_BLOCKS // owners)
     wide = MIDDLE if (MIDDLE * capacity) % 16 == 0 else 16
     scale = 1.0 / math.sqrt(owners * columns * PER_WORKER * BLOCK * BLOCK)
+    permuted = owners == 4 and columns == 2
+    parts = owners if permuted else 1
     routing = assignment[0]
     shape = jax.ShapeDtypeStruct
     tables = [pltpu.SMEM((owners * capacity + 1,), I32)]
     counts = [pltpu.SMEM((owners,), I32)]
 
+    def pieces(*dims):
+        return [shape(dims, BF16)] * owners if permuted else [shape((owners,) + dims, BF16)]
+
+    def exchange(values):
+        if permuted:
+            return [values[0]] + [flip(values[k], "blk", k) for k in range(1, owners)]
+        return [lax.all_to_all(values[0], "blk", split_axis=0, concat_axis=0, tiled=True)]
+
     tile = grad_out.reshape(TILE_ROWS, BLOCK, TILE_COLS * BLOCK, HALF)
     outgoing = call(
-        functools.partial(pack_cotangents, owners, capacity),
-        shape((owners, BLOCK, BLOCK * capacity, HALF), BF16),
-        [SMEM, VMEM], tables, (2**28, 2**20), "pack_cotangents",
+        functools.partial(pack_cotangents, owners, capacity, permuted),
+        pieces(BLOCK, BLOCK * capacity, HALF),
+        [SMEM, VMEM], tables, (2**30, 2**21), "pack_cotangents",
     )(routing, tile)
-    incoming = lax.all_to_all(outgoing, "blk", split_axis=0, concat_axis=0, tiled=True)
+    incoming = exchange(outgoing)
 
     saved_slots = saved_pre[0, 0].transpose(1, 2, 0, 3)
-    masked, to_owners = call(
-        functools.partial(pack_saved, owners, columns, capacity, wide),
-        (
-            shape((MIDDLE, MIDDLE * PER_WORKER, HALF), BF16),
-            shape((owners, MIDDLE, wide * capacity, HALF), BF16),
-        ),
-        [SMEM, VMEM], counts + tables, (2**28, 2**20), "pack_saved",
+    masked, *to_owners = call(
+        functools.partial(pack_saved, owners, columns, capacity, wide, permuted),
+        [shape((MIDDLE, MIDDLE * PER_WORKER, HALF), BF16)] + pieces(MIDDLE, wide * capacity, HALF),
+        [SMEM, VMEM], counts + tables, (2**30, 2**21), "pack_saved",
     )(routing, saved_slots.reshape(MIDDLE, MIDDLE * PER_WORKER, HALF))
     masked = masked.reshape(MIDDLE, MIDDLE, PER_WORKER, HALF)
     second_other = swap(second_weight)
     masked_other = swap(masked)
     tile_other = swap(tile)
-
-    incoming_other = swap(incoming)
-    at_owner = lax.all_to_all(to_owners, "blk", split_axis=0, concat_axis=0, tiled=True)
-    cot, grad_second = call(
-        functools.partial(second_gradient, scale, owners, capacity),
-        (
-            shape((BLOCK, BLOCK * PER_WORKER, FULL), BF16),
-            shape((9, HALF, FULL), BF16),
-        ),
-        [SMEM, VMEM, VMEM, VMEM], counts, (2**30, 2**21), "second_gradient",
-    )(routing, incoming, incoming_other, masked)
-    grad_second = lax.psum(grad_second, ("blk", "col"))
+    total = call(
+        owner_spread,
+        shape((MIDDLE, MIDDLE, TILE_BLOCKS, FULL), F32),
+        [VMEM] * 4,
+        [pltpu.VMEM((BLOCK, FULL, FULL), BF16), pltpu.VMEM((9, FULL, FULL), BF16)],
+        (2**32, 2**23), "owner_spread",
+    )(tile, tile_other, second_weight, second_other)
+
+    incoming_other = [swap(value) for value in incoming]
+    to_owners, incoming = lax.optimization_barrier((to_owners, incoming))
+    at_owner = exchange(to_owners)
+
+    if permuted:
+        halved = [shape((9, HALF // 2, FULL), F32), shape((9, HALF // 2, FULL), BF16)]
+    else:
+        halved = [shape((9, HALF, FULL), F32)]
+    cot, *second_terms = call(
+        functools.partial(second_gradient, scale, owners, capacity, permuted),
+        [shape((BLOCK, BLOCK * PER_WORKER, FULL), BF16)] + halved,
+        [SMEM] + [VMEM] * (2 * parts + 1), counts, (2**31, 2**21), "second_gradient",
+    )(routing, *incoming, *incoming_other, masked)
 
     saved_tiles = saved_input[0, 0].transpose(1, 2, 0, 3)
-    grad_first = call(
+    first_terms = call(
         functools.partial(first_gradient, scale),
-        shape((9, HALF, FULL), BF16),
+        halved,
         [VMEM] * 6,
         [
             pltpu.VMEM((MIDDLE, MIDDLE, PER_WORKER, FULL), F32),
             pltpu.VMEM((MIDDLE, MIDDLE, PER_WORKER, FULL), BF16),
             pltpu.VMEM((9, FULL, FULL), BF16),
         ],
-        (2**31, 2**22), "first_gradient",
+        (2**32, 2**22), "first_gradient",
     )(cot, masked, masked_other, second_weight, second_other, saved_tiles)
-    grad_first = lax.psum(grad_first, ("blk", "col"))
-
-    at_owner_other = swap(at_owner)
+
+    if permuted:
+        size = HALF // 2 // owners
+        part = (2, 9, size, FULL)
+        second_got, first_got = swap(second_terms[1], "col"), swap(first_terms[1], "col")
+        kept, *sends = call(
+            functools.partial(add_columns, columns),
+            [shape(part, F32)] + [shape(part, BF16)] * (owners - 1),
+            [VMEM] * 4, [pltpu.VMEM((2, 9, HALF // 2, FULL), F32)], (2**28, 2**22), "add_columns",
+        )(second_terms[0], first_terms[0], second_got, first_got)
+        got = [flip(value, "blk", k + 1) for k, value in enumerate(sends)]
+        sums = call(
+            add_workers, [shape(part[1:], BF16)] * 2, [VMEM] * owners, [], (2**26, 2**20),
+            "add_workers",
+        )(kept, *got)
+        grads = []
+        for value in sums:
+            spread = [value] + [flip(value, "blk", k) for k in range(1, owners)]
+            half = call(
+                lay_parts, shape((9, HALF // 2, FULL), BF16), [VMEM] * owners, [], (2**26, 2**20),
+                "lay_parts",
+            )(*spread)
+            grads.append(
+                call(
+                    lay_halves, shape((9, HALF, FULL), F32), [VMEM] * 2, [], (2**26, 2**21),
+                    "lay_halves",
+                )(half, swap(half, "col"))
+            )
+        grad_second, grad_first = grads
+    else:
+        grad_first, grad_second = lax.psum((first_terms[0], second_terms[0]), ("blk", "col"))
+
+    at_owner_other = [swap(value) for value in at_owner]
     height = TILE_ROWS * BLOCK + 4
     canvas = call(
-        functools.partial(owner_canvas, owners, capacity, wide),
+        functools.partial(owner_canvas, owners, capacity, wide, permuted),
         shape((height, WIDE, HALF), F32),
-        [SMEM] + [VMEM] * 7,
+        [SMEM] + [VMEM] * (2 * parts + 2),
         tables
         + [
-            pltpu.VMEM((BLOCK, FULL, FULL), BF16),
-            pltpu.VMEM((MIDDLE, MIDDLE, TILE_BLOCKS, FULL), F32),
             pltpu.VMEM((MIDDLE, MIDDLE, TILE_BLOCKS, FULL), BF16),
-            pltpu.VMEM((9, FULL, FULL), BF16),
             pltpu.VMEM((OUTER, OUTER, TILE_BLOCKS, HALF), F32),
         ],
         (2**32, 2**23), "owner_canvas",
-    )(routing, tile, tile_other, at_owner, at_owner_other, second_weight, second_other, first_weight)
+    )(routing, *at_owner, *at_owner_other, total, first_weight)
 
     up, down = neighbours("blk")
     from_above = lax.ppermute(canvas[height - 2 :].astype(BF16), "blk", up).astype(F32)
@@ -384,7 +501,7 @@
     from_right = lax.ppermute(inner[:, 34:36].astype(BF16), "col", down).astype(F32)
     inner = inner[:, :32].at[:, :2].add(from_left).at[:, -2:].add(from_right)
     grad_in = (grad_out.astype(F32) + inner).astype(BF16)
-    return (grad_in, grad_first.astype(F32), grad_second.astype(F32))
+    return (grad_in, grad_first, grad_second)
 
 
 def solution(mesh):

time: 175 us -> 120 us (0.69)
  waiting for transfers between devices: 106 us -> 41.6 us
  starting transfers between devices: 18.5 us -> 45.9 us
  between operations: 14.2 us -> 0.88 us
  other arithmetic: 4.67 us -> 2.34 us
  local copies, waits for them, and re-layouts: 5.75 us -> 3.57 us
    psum x1 -> x0, waiting for transfers between devices: 64.4 us -> none  [shards(): grad_first = lax.psum(grad_first, ('blk', 'col'))]
    ppermute x5 -> x30, waiting for transfers between devices: 0.89 us -> 41.5 us  [the longest x15 36.6 us: flip(): return lax.ppermute(value, axis, [(i, i ^ step) for i in range(size)])]
    ppermute x5 -> x30, starting transfers between devices: 1.09 us -> 35.7 us  [the longest x15 26.3 us: flip(): return lax.ppermute(value, axis, [(i, i ^ step) for i in range(size)])]
    all_to_all x2 -> x0, waiting for transfers between devices: 32.2 us -> none  [the longest x1 18.4 us: shards(): lax.all_to_all(to_owners, 'blk', split_axis=0, concat_axis=0, tiled=True)]
    all_to_all x2 -> x0, starting transfers between devices: 9.79 us -> none  [the longest x1 6.32 us: shards(): lax.all_to_all(to_owners, 'blk', split_axis=0, concat_axis=0, tiled=True)]
    ppermute x1, waiting for transfers between devices: 4.35 us -> 0.01 us  [shards(): from_below = lax.ppermute(canvas[:2].astype(BF16), 'blk', down).astype(F32)]
    ppermute x1, waiting for transfers between devices: 4.3 us -> 0.01 us  [shards(): lax.ppermute(inner[:, 34:36].astype(BF16), 'col', down).astype(F32)]
    ppermute x1, starting transfers between devices: 1.6 us -> 5.18 us  [shards(): lax.ppermute(canvas[height - 2:].astype(BF16), 'blk', up).astype(F32)]
  transfers between devices with their start and end apart: 12 -> 34, of which waited for: 7 -> 12; matrix products, arithmetic and copies ran while one was open for 1% -> 2% of each run, Pallas kernels for 13% -> 18%
where the time goes in v2:
time: 120 us
  starting transfers between devices  45.9 us (38%)
  waiting for transfers between devices  41.6 us (35%)
  Pallas kernels  25.3 us (21%)
  local copies, waits for them, and re-layouts  3.57 us (3%)
  other arithmetic  2.34 us (2%)
    ppermute x15, waiting for transfers between devices, flip(): return lax.ppermute(value, axis, [(i, i ^ step) for i in range(size)])  36.6 us
    ppermute x15, starting transfers between devices, flip(): return lax.ppermute(value, axis, [(i, i ^ step) for i in range(size)])  26.3 us
    ppermute x15, starting transfers between devices, swap(): return lax.ppermute(value, axis, [(0, 1), (1, 0)])  9.4 us
    pallas_call x1, Pallas kernels, shards(): call(functools.partial(owner_canvas, owners, capacity, wide, permuted), s...  8.64 us
    ppermute x1, starting transfers between devices, shards(): lax.ppermute(canvas[height - 2:].astype(BF16), 'blk', up).astype(F32)  5.18 us
    ppermute x15, waiting for transfers between devices, swap(): return lax.ppermute(value, axis, [(0, 1), (1, 0)])  4.96 us
    pallas_call x1, Pallas kernels, shards(): call(functools.partial(first_gradient, scale), halved, [VMEM] * 6, [pltpu...  4.57 us
    pallas_call x1, Pallas kernels, shards(): call(owner_spread, shape((MIDDLE, MIDDLE, TILE_BLOCKS, FULL), F32), [VMEM...  3.95 us
  transfers between devices with their start and end apart: 34, of which 12 were waited for; matrix products, arithmetic and copies ran while one was open for 2% of the time, Pallas kernels for 18%

profile of v2, /device:TPU:0, one launch (start us, length us, event | category | flops | bytes accessed | tf_op | source)
XLA Modules:
  0.0 119.5 jit_solution(4377058602664575645)
XLA Ops:
  1.3 2.2 %pack_cotangents.1 = (bf16[8,64,128]{2,1,0:T(8,128)(2,1)S(1)}, bf16[8,64,128]{2,1,0:T(8,128)(2,1)S(1)}, bf16[8,64,128]{2,1,0:T(8,128)(2,1)S(1)}, bf16[8,64,128]{2,1,0:T(8,128)(2,1)S(1)}) custom-call(s32[4,16]{1,0:T(4,128)S(1)} %bitcast.16, bf16[8,8,32,128]{3,2,1,0:T(8,128)(2,1)} %bitcast.4.tile), custom_call_target="tpu_custom_call" | custom-call | flops 1073741824 | bytes 2097152 | tf_op jit(solution)/shard_map/pack_cotangents/pallas_call | solution.py:397
  3.5 3.1 %collective-permute-start = (bf16[8,64,128]{2,1,0:T(8,128)(2,1)S(1)}, bf16[8,64,128]{2,1,0:T(8,128)(2,1)S(1)}, u32[]{:S(2)}, u32[]{:S(2)}) collective-permute-start(bf16[8,64,128]{2,1,0:T(8,128)(2,1)S(1)} %get-tuple-element.84), channel_id=1, source_target_pairs={{0,4},{4,0},{8,12},{12,8},{1,5},{5,1},{9,13},{13,9},{2,6},{6,2},{1... | collective-permute-start | bytes 393224 | tf_op jit(solution)/shard_map/ppermute | solution.py:366
  7.1 2.6 %collective-permute-start.1 = (bf16[8,64,128]{2,1,0:T(8,128)(2,1)S(1)}, bf16[8,64,128]{2,1,0:T(8,128)(2,1)S(1)}, u32[]{:S(2)}, u32[]{:S(2)}) collective-permute-start(bf16[8,64,128]{2,1,0:T(8,128)(2,1)S(1)} %get-tuple-element.85), channel_id=1, source_target_pairs={{0,8},{4,12},{8,0},{12,4},{1,9},{5,13},{9,1},{13,5},{2,10},{6,14},... | collective-permute-start | bytes 393224 | tf_op jit(solution)/shard_map/ppermute | solution.py:366
  10.1 9.7 %collective-permute-done.1.refs_2_ = bf16[8,64,128]{2,1,0:T(8,128)(2,1)S(1)} collective-permute-done((bf16[8,64,128]{2,1,0:T(8,128)(2,1)S(1)}, bf16[8,64,128]{2,1,0:T(8,128)(2,1)S(1)}, u32[]{:S(2)}, u32[]{:S(2)}) %collective-permute-start.1) | collective-permute-done | bytes 131104 | tf_op jit(solution)/shard_map/ppermute | solution.py:366
  21.9 2.6 %collective-permute-start.3 = (bf16[10,80,128]{2,1,0:T(8,128)(2,1)S(1)}, bf16[10,80,128]{2,1,0:T(8,128)(2,1)S(1)}, u32[]{:S(2)}, u32[]{:S(2)}) collective-permute-start(bf16[10,80,128]{2,1,0:T(8,128)(2,1)S(1)} %get-tuple-element.88), channel_id=1, source_target_pairs={{0,4},{4,0},{8,12},{12,8},{1,5},{5,1},{9,13},{13,9},{2,6},{6,2},{1... | collective-permute-start | bytes 614408 | tf_op jit(solution)/shard_map/ppermute | solution.py:366
  27.2 1.8 %second_gradient.1 = (bf16[8,128,256]{2,1,0:T(8,128)(2,1)S(1)}, f32[9,64,256]{2,1,0:T(8,128)S(1)}, bf16[9,64,256]{2,1,0:T(8,128)(2,1)S(1)}) custom-call(s32[4,16]{1,0:T(4,128)S(1)} %bitcast.18, bf16[8,64,128]{2,1,0:T(8,128)(2,1)S(1)} %get-tuple-element.91.refs_0_, bf16[8,64,128]{2,1,0:T(8,128)(2,1)S(1)} %collective-permute-done.refs_1_, ...), custom_call_target="tpu_custom_call" | custom-call | flops 2147483648 | bytes 2097152 | tf_op jit(solution)/shard_map/second_gradient/pallas_call | solution.py:430
  29.0 4.5 %collective-permute-done.3.refs_1_ = bf16[10,80,128]{2,1,0:T(8,128)(2,1)S(1)} collective-permute-done((bf16[10,80,128]{2,1,0:T(8,128)(2,1)S(1)}, bf16[10,80,128]{2,1,0:T(8,128)(2,1)S(1)}, u32[]{:S(2)}, u32[]{:S(2)}) %collective-permute-start.3) | collective-permute-done | bytes 204832 | tf_op jit(solution)/shard_map/ppermute | solution.py:366
  33.5 8.7 %collective-permute-done.4.refs_2_ = bf16[10,80,128]{2,1,0:T(8,128)(2,1)S(1)} collective-permute-done((bf16[10,80,128]{2,1,0:T(8,128)(2,1)S(1)}, bf16[10,80,128]{2,1,0:T(8,128)(2,1)S(1)}, u32[]{:S(2)}, u32[]{:S(2)}) %collective-permute-start.4) | collective-permute-done | bytes 204832 | tf_op jit(solution)/shard_map/ppermute | solution.py:366
  43.3 4.0 %owner_spread.1.refs_8_ = f32[10,10,32,256]{3,2,1,0:T(8,128)S(1)} custom-call(bf16[8,8,32,128]{3,2,1,0:T(8,128)(2,1)} %bitcast.4.tile, bf16[8,8,32,128]{3,2,1,0:T(8,128)(2,1)S(1)} %collective-permute-done.10.tile_other, bf16[9,128,256]{2,1,0:T(8,128)(2,1)S(1)} %copy-done.1, bf16[9,128,256]{2,1,0:T(8,128)(2,1)S(1)} %collective-permute-done.11.second_other.weight_other), custom_call_target="tpu_custom_call" | custom-call | flops 4294967296 | bytes 8388608 | tf_op jit(solution)/shard_map/owner_spread/pallas_call | solution.py:414
  47.2 1.7 %copy-done.6 = f32[10,10,32,256]{3,2,1,0:T(8,128)} copy-done((f32[10,10,32,256]{3,2,1,0:T(8,128)}, f32[10,10,32,256]{3,2,1,0:T(8,128)S(1)}, u32[]{:S(2)}) %copy-start.6) | copy-done | bytes 3276824
  50.4 8.6 %owner_canvas.1 = f32[68,40,128]{2,1,0:T(8,128)S(1)} custom-call(s32[4,16]{1,0:T(4,128)S(1)} %bitcast.19, bf16[10,80,128]{2,1,0:T(8,128)(2,1)S(1)} %get-tuple-element.87.refs_0_, bf16[10,80,128]{2,1,0:T(8,128)(2,1)S(1)} %collective-permute-done.3.refs_1_, bf16[10,80,128]{2,1,0:T(8,128)(2,1)S(1)} %collective-permute-done.4.refs_2_, ...), custom_call_target="tpu_custom_call" | custom-call | flops 4294967296 | bytes 8388608 | tf_op jit(solution)/shard_map/owner_canvas/pallas_call | solution.py:482
  60.1 4.6 %first_gradient.1 = (f32[9,64,256]{2,1,0:T(8,128)S(1)}, bf16[9,64,256]{2,1,0:T(8,128)(2,1)S(1)}) custom-call(bf16[8,128,256]{2,1,0:T(8,128)(2,1)S(1)} %get-tuple-element.97.cot, bf16[10,10,16,128]{3,2,1,0:T(8,128)(2,1)S(1)} %bitcast.15, bf16[10,10,16,128]{3,2,1,0:T(8,128)(2,1)S(1)} %collective-permute-done.20.masked_other, ...), custom_call_target="tpu_custom_call" | custom-call | flops 4294967296 | bytes 4194304 | tf_op jit(solution)/shard_map/first_gradient/pallas_call | solution.py:437
  65.3 5.2 %collective-permute-start.12 = (bf16[2,40,128]{2,1,0:T(8,128)(2,1)S(1)}, bf16[2,40,128]{2,1,0:T(8,128)(2,1)S(1)}, u32[]{:S(2)}, u32[]{:S(2)}) collective-permute-start(bf16[2,40,128]{2,1,0:T(8,128)(2,1)S(1)} %get-tuple-element.108), channel_id=1, source_target_pairs={{0,4},{4,8},{8,12},{1,5},{5,9},{9,13},{2,6},{6,10},{10,14},{3,7},{... | collective-permute-start | bytes 61448 | tf_op jit(solution)/shard_map/ppermute | solution.py:495
  73.7 3.7 %collective-permute-start.23 = (bf16[2,9,16,256]{3,2,1,0:T(8,128)(2,1)S(1)}, bf16[2,9,16,256]{3,2,1,0:T(8,128)(2,1)S(1)}, u32[]{:S(2)}, u32[]{:S(2)}) collective-permute-start(bf16[2,9,16,256]{3,2,1,0:T(8,128)(2,1)S(1)} %get-tuple-element.102), channel_id=1, source_target_pairs={{0,4},{4,0},{8,12},{12,8},{1,5},{5,1},{9,13},{13,9},{2,6},{6,2},{1... | collective-permute-start | bytes 442376 | tf_op jit(solution)/shard_map/ppermute | solution.py:366
  80.0 2.4 %collective-permute-done.23.refs_0_ = bf16[2,9,16,256]{3,2,1,0:T(8,128)(2,1)S(1)} collective-permute-done((bf16[2,9,16,256]{3,2,1,0:T(8,128)(2,1)S(1)}, bf16[2,9,16,256]{3,2,1,0:T(8,128)(2,1)S(1)}, u32[]{:S(2)}, u32[]{:S(2)}) %collective-permute-start.23) | collective-permute-done | bytes 147488 | tf_op jit(solution)/shard_map/ppermute | solution.py:366
  82.4 8.6 %collective-permute-done.24.refs_1_ = bf16[2,9,16,256]{3,2,1,0:T(8,128)(2,1)S(1)} collective-permute-done((bf16[2,9,16,256]{3,2,1,0:T(8,128)(2,1)S(1)}, bf16[2,9,16,256]{3,2,1,0:T(8,128)(2,1)S(1)}, u32[]{:S(2)}, u32[]{:S(2)}) %collective-permute-start.24) | collective-permute-done | bytes 147488 | tf_op jit(solution)/shard_map/ppermute | solution.py:366
  91.1 2.2 %collective-permute-start.26 = (bf16[9,16,256]{2,1,0:T(8,128)(2,1)S(1)}, bf16[9,16,256]{2,1,0:T(8,128)(2,1)S(1)}, u32[]{:S(2)}, u32[]{:S(2)}) collective-permute-start(bf16[9,16,256]{2,1,0:T(8,128)(2,1)S(1)} %get-tuple-element.105.refs_0_), channel_id=1, source_target_pairs={{0,4},{4,0},{8,12},{12,8},{1,5},{5,1},{9,13},{13,9},{2,6},{6,2},{1... | collective-permute-start | bytes 221192 | tf_op jit(solution)/shard_map/ppermute | solution.py:366
  94.5 2.4 %collective-permute-start.14 = (bf16[64,2,128]{2,1,0:T(2,128)(2,1)S(1)}, bf16[64,2,128]{2,1,0:T(2,128)(2,1)S(1)}, u32[]{:S(2)}, u32[]{:S(2)}) collective-permute-start(bf16[64,2,128]{2,1,0:T(2,128)(2,1)S(1)} %get-tuple-element.110), channel_id=1, source_target_pairs={{0,2},{1,3},{4,6},{5,7},{8,10},{9,11},{12,14},{13,15},{16,18},{17,... | collective-permute-start | bytes 98312 | tf_op jit(solution)/shard_map/ppermute | solution.py:500
  100.8 2.0 %collective-permute-start.31 = (bf16[9,16,256]{2,1,0:T(8,128)(2,1)S(1)}, bf16[9,16,256]{2,1,0:T(8,128)(2,1)S(1)}, u32[]{:S(2)}, u32[]{:S(2)}) collective-permute-start(bf16[9,16,256]{2,1,0:T(8,128)(2,1)S(1)} %get-tuple-element.106.refs_0_), channel_id=1, source_target_pairs={{0,8},{4,12},{8,0},{12,4},{1,9},{5,13},{9,1},{13,5},{2,10},{6,14},... | collective-permute-start | bytes 221192 | tf_op jit(solution)/shard_map/ppermute | solution.py:366
  104.7 2.7 %collective-permute-start.29 = (bf16[9,64,256]{2,1,0:T(8,128)(2,1)S(1)}, bf16[9,64,256]{2,1,0:T(8,128)(2,1)S(1)}, u32[]{:S(2)}, u32[]{:S(2)}) collective-permute-start(bf16[9,64,256]{2,1,0:T(8,128)(2,1)S(1)} %lay_parts.2.own), channel_id=1, source_target_pairs={{0,2},{2,0},{1,3},{3,1},{4,6},{6,4},{5,7},{7,5},{8,10},{10,8},{9,1... | collective-permute-start | bytes 884744 | tf_op jit(solution)/shard_map/ppermute | solution.py:361
  107.4 1.9 %collective-permute-done.31.refs_2_ = bf16[9,16,256]{2,1,0:T(8,128)(2,1)S(1)} collective-permute-done((bf16[9,16,256]{2,1,0:T(8,128)(2,1)S(1)}, bf16[9,16,256]{2,1,0:T(8,128)(2,1)S(1)}, u32[]{:S(2)}, u32[]{:S(2)}) %collective-permute-start.31) | collective-permute-done | bytes 73760 | tf_op jit(solution)/shard_map/ppermute | solution.py:366
  109.3 2.5 %collective-permute-start.33 = (bf16[9,64,256]{2,1,0:T(8,128)(2,1)S(1)}, bf16[9,64,256]{2,1,0:T(8,128)(2,1)S(1)}, u32[]{:S(2)}, u32[]{:S(2)}) collective-permute-start(bf16[9,64,256]{2,1,0:T(8,128)(2,1)S(1)} %lay_parts.3.own), channel_id=1, source_target_pairs={{0,2},{2,0},{1,3},{3,1},{4,6},{6,4},{5,7},{7,5},{8,10},{10,8},{9,1... | collective-permute-start | bytes 884744 | tf_op jit(solution)/shard_map/ppermute | solution.py:361
  111.9 2.0 %add_convert_fusion = bf16[64,32,128]{2,1,0:T(8,128)(2,1)} fusion(f32[64,32,128]{2,1,0:T(8,128)S(1)} %fusion, bf16[64,32,128]{2,1,0:T(8,128)(2,1)} %param.14), kind=kLoop, calls=%fused_computation | loop fusion | flops 786432 | bytes 2097152 | tf_op jit(solution)/shard_map/convert_element_type | solution.py:503
  116.1 2.3 %collective-permute-done.33.other = bf16[9,64,256]{2,1,0:T(8,128)(2,1)S(1)} collective-permute-done((bf16[9,64,256]{2,1,0:T(8,128)(2,1)S(1)}, bf16[9,64,256]{2,1,0:T(8,128)(2,1)S(1)}, u32[]{:S(2)}, u32[]{:S(2)}) %collective-permute-start.33) | collective-permute-done | bytes 294944 | tf_op jit(solution)/shard_map/ppermute | solution.py:361
  (81 shorter events, 26.7 us)
Async XLA Ops:
  6.6 36.2 %collective-permute-start.11 = (bf16[9,128,256]{2,1,0:T(8,128)(2,1)S(1)}, bf16[9,128,256]{2,1,0:T(8,128)(2,1)S(1)}, u32[]{:S(2)}, u32[]{:S(2)}) collective-permute-start(bf16[9,128,256]{2,1,0:T(8,128)(2,1)S(1)} %copy-done.1), channel_id=1, source_target_pairs={{0,1},{1,0},{2,3},{3,2},{4,5},{5,4},{6,7},{7,6},{8,9},{9,8},{10,11... | collective-permute-start | bytes 1769480 | tf_op jit(solution)/shard_map/ppermute | solution.py:361
  6.6 36.1 %collective-permute-start.10 = (bf16[8,8,32,128]{3,2,1,0:T(8,128)(2,1)}, bf16[8,8,32,128]{3,2,1,0:T(8,128)(2,1)S(1)}, u32[]{:S(2)}, u32[]{:S(2)}) collective-permute-start(bf16[8,8,32,128]{3,2,1,0:T(8,128)(2,1)} %bitcast.4.tile), channel_id=1, source_target_pairs={{0,1},{1,0},{2,3},{3,2},{4,5},{5,4},{6,7},{7,6},{8,9},{9,8},{10,11... | collective-permute-start | bytes 1572872 | tf_op jit(solution)/shard_map/ppermute | solution.py:361
  7.1 12.7 %collective-permute-start.1 = (bf16[8,64,128]{2,1,0:T(8,128)(2,1)S(1)}, bf16[8,64,128]{2,1,0:T(8,128)(2,1)S(1)}, u32[]{:S(2)}, u32[]{:S(2)}) collective-permute-start(bf16[8,64,128]{2,1,0:T(8,128)(2,1)S(1)} %get-tuple-element.85), channel_id=1, source_target_pairs={{0,8},{4,12},{8,0},{12,4},{1,9},{5,13},{9,1},{13,5},{2,10},{6,14},... | collective-permute-start | bytes 393224 | tf_op jit(solution)/shard_map/ppermute | solution.py:366
  9.7 10.1 %collective-permute-start.2 = (bf16[8,64,128]{2,1,0:T(8,128)(2,1)S(1)}, bf16[8,64,128]{2,1,0:T(8,128)(2,1)S(1)}, u32[]{:S(2)}, u32[]{:S(2)}) collective-permute-start(bf16[8,64,128]{2,1,0:T(8,128)(2,1)S(1)} %get-tuple-element.86), channel_id=1, source_target_pairs={{0,12},{4,8},{8,4},{12,0},{1,13},{5,9},{9,5},{13,1},{2,14},{6,10},... | collective-permute-start | bytes 393224 | tf_op jit(solution)/shard_map/ppermute | solution.py:366
  10.1 10.2 %collective-permute-start.16 = (bf16[8,64,128]{2,1,0:T(8,128)(2,1)S(1)}, bf16[8,64,128]{2,1,0:T(8,128)(2,1)S(1)}, u32[]{:S(2)}, u32[]{:S(2)}) collective-permute-start(bf16[8,64,128]{2,1,0:T(8,128)(2,1)S(1)} %get-tuple-element.91.refs_0_), channel_id=1, source_target_pairs={{0,1},{1,0},{2,3},{3,2},{4,5},{5,4},{6,7},{7,6},{8,9},{9,8},{10,11... | collective-permute-start | bytes 393224 | tf_op jit(solution)/shard_map/ppermute | solution.py:361
  21.9 11.6 %collective-permute-start.3 = (bf16[10,80,128]{2,1,0:T(8,128)(2,1)S(1)}, bf16[10,80,128]{2,1,0:T(8,128)(2,1)S(1)}, u32[]{:S(2)}, u32[]{:S(2)}) collective-permute-start(bf16[10,80,128]{2,1,0:T(8,128)(2,1)S(1)} %get-tuple-element.88), channel_id=1, source_target_pairs={{0,4},{4,0},{8,12},{12,8},{1,5},{5,1},{9,13},{13,9},{2,6},{6,2},{1... | collective-permute-start | bytes 614408 | tf_op jit(solution)/shard_map/ppermute | solution.py:366
  24.6 17.7 %collective-permute-start.4 = (bf16[10,80,128]{2,1,0:T(8,128)(2,1)S(1)}, bf16[10,80,128]{2,1,0:T(8,128)(2,1)S(1)}, u32[]{:S(2)}, u32[]{:S(2)}) collective-permute-start(bf16[10,80,128]{2,1,0:T(8,128)(2,1)S(1)} %get-tuple-element.89), channel_id=1, source_target_pairs={{0,8},{4,12},{8,0},{12,4},{1,9},{5,13},{9,1},{13,5},{2,10},{6,14},... | collective-permute-start | bytes 614408 | tf_op jit(solution)/shard_map/ppermute | solution.py:366
  25.7 16.5 %collective-permute-start.5 = (bf16[10,80,128]{2,1,0:T(8,128)(2,1)S(1)}, bf16[10,80,128]{2,1,0:T(8,128)(2,1)S(1)}, u32[]{:S(2)}, u32[]{:S(2)}) collective-permute-start(bf16[10,80,128]{2,1,0:T(8,128)(2,1)S(1)} %get-tuple-element.90), channel_id=1, source_target_pairs={{0,12},{4,8},{8,4},{12,0},{1,13},{5,9},{9,5},{13,1},{2,14},{6,10},... | collective-permute-start | bytes 614408 | tf_op jit(solution)/shard_map/ppermute | solution.py:366
  33.5 25.6 %collective-permute-start.20 = (bf16[10,10,16,128]{3,2,1,0:T(8,128)(2,1)S(1)}, bf16[10,10,16,128]{3,2,1,0:T(8,128)(2,1)S(1)}, u32[]{:S(2)}, u32[]{:S(2)}) collective-permute-start(bf16[10,10,16,128]{3,2,1,0:T(8,128)(2,1)S(1)} %bitcast.14), channel_id=1, source_target_pairs={{0,1},{1,0},{2,3},{3,2},{4,5},{5,4},{6,7},{7,6},{8,9},{9,8},{10,11... | collective-permute-start | bytes 1228808 | tf_op jit(solution)/shard_map/ppermute | solution.py:361
  42.2 8.2 %collective-permute-start.7 = (bf16[10,80,128]{2,1,0:T(8,128)(2,1)S(1)}, bf16[10,80,128]{2,1,0:T(8,128)(2,1)S(1)}, u32[]{:S(2)}, u32[]{:S(2)}) collective-permute-start(bf16[10,80,128]{2,1,0:T(8,128)(2,1)S(1)} %collective-permute-done.3.refs_1_), channel_id=1, source_target_pairs={{0,1},{1,0},{2,3},{3,2},{4,5},{5,4},{6,7},{7,6},{8,9},{9,8},{10,11... | collective-permute-start | bytes 614408 | tf_op jit(solution)/shard_map/ppermute | solution.py:361
  42.7 7.6 %collective-permute-start.8 = (bf16[10,80,128]{2,1,0:T(8,128)(2,1)S(1)}, bf16[10,80,128]{2,1,0:T(8,128)(2,1)S(1)}, u32[]{:S(2)}, u32[]{:S(2)}) collective-permute-start(bf16[10,80,128]{2,1,0:T(8,128)(2,1)S(1)} %collective-permute-done.4.refs_2_), channel_id=1, source_target_pairs={{0,1},{1,0},{2,3},{3,2},{4,5},{5,4},{6,7},{7,6},{8,9},{9,8},{10,11... | collective-permute-start | bytes 614408 | tf_op jit(solution)/shard_map/ppermute | solution.py:361
  48.9 23.1 %collective-permute-start.21 = (bf16[9,64,256]{2,1,0:T(8,128)(2,1)S(1)}, bf16[9,64,256]{2,1,0:T(8,128)(2,1)S(1)}, u32[]{:S(2)}, u32[]{:S(2)}) collective-permute-start(bf16[9,64,256]{2,1,0:T(8,128)(2,1)S(1)} %get-tuple-element.99), channel_id=1, source_target_pairs={{0,2},{2,0},{1,3},{3,1},{4,6},{6,4},{5,7},{7,5},{8,10},{10,8},{9,1... | collective-permute-start | bytes 884744 | tf_op jit(solution)/shard_map/ppermute | solution.py:361
  64.7 8.8 %collective-permute-start.22 = (bf16[9,64,256]{2,1,0:T(8,128)(2,1)S(1)}, bf16[9,64,256]{2,1,0:T(8,128)(2,1)S(1)}, u32[]{:S(2)}, u32[]{:S(2)}) collective-permute-start(bf16[9,64,256]{2,1,0:T(8,128)(2,1)S(1)} %get-tuple-element.100), channel_id=1, source_target_pairs={{0,2},{2,0},{1,3},{3,1},{4,6},{6,4},{5,7},{7,5},{8,10},{10,8},{9,1... | collective-permute-start | bytes 884744 | tf_op jit(solution)/shard_map/ppermute | solution.py:361
  70.6 9.3 %collective-permute-start.13 = (bf16[2,40,128]{2,1,0:T(8,128)(2,1)S(1)}, bf16[2,40,128]{2,1,0:T(8,128)(2,1)S(1)}, u32[]{:S(2)}, u32[]{:S(2)}) collective-permute-start(bf16[2,40,128]{2,1,0:T(8,128)(2,1)S(1)} %get-tuple-element.107), channel_id=1, source_target_pairs={{4,0},{8,4},{12,8},{5,1},{9,5},{13,9},{6,2},{10,6},{14,10},{7,3},{... | collective-permute-start | bytes 61448 | tf_op jit(solution)/shard_map/ppermute | solution.py:496
  73.7 8.7 %collective-permute-start.23 = (bf16[2,9,16,256]{3,2,1,0:T(8,128)(2,1)S(1)}, bf16[2,9,16,256]{3,2,1,0:T(8,128)(2,1)S(1)}, u32[]{:S(2)}, u32[]{:S(2)}) collective-permute-start(bf16[2,9,16,256]{3,2,1,0:T(8,128)(2,1)S(1)} %get-tuple-element.102), channel_id=1, source_target_pairs={{0,4},{4,0},{8,12},{12,8},{1,5},{5,1},{9,13},{13,9},{2,6},{6,2},{1... | collective-permute-start | bytes 442376 | tf_op jit(solution)/shard_map/ppermute | solution.py:366
  77.4 13.6 %collective-permute-start.24 = (bf16[2,9,16,256]{3,2,1,0:T(8,128)(2,1)S(1)}, bf16[2,9,16,256]{3,2,1,0:T(8,128)(2,1)S(1)}, u32[]{:S(2)}, u32[]{:S(2)}) collective-permute-start(bf16[2,9,16,256]{3,2,1,0:T(8,128)(2,1)S(1)} %get-tuple-element.103), channel_id=1, source_target_pairs={{0,8},{4,12},{8,0},{12,4},{1,9},{5,13},{9,1},{13,5},{2,10},{6,14},... | collective-permute-start | bytes 442376 | tf_op jit(solution)/shard_map/ppermute | solution.py:366
  78.5 12.5 %collective-permute-start.25 = (bf16[2,9,16,256]{3,2,1,0:T(8,128)(2,1)S(1)}, bf16[2,9,16,256]{3,2,1,0:T(8,128)(2,1)S(1)}, u32[]{:S(2)}, u32[]{:S(2)}) collective-permute-start(bf16[2,9,16,256]{3,2,1,0:T(8,128)(2,1)S(1)} %get-tuple-element.104), channel_id=1, source_target_pairs={{0,12},{4,8},{8,4},{12,0},{1,13},{5,9},{9,5},{13,1},{2,14},{6,10},... | collective-permute-start | bytes 442376 | tf_op jit(solution)/shard_map/ppermute | solution.py:366
  91.1 9.7 %collective-permute-start.26 = (bf16[9,16,256]{2,1,0:T(8,128)(2,1)S(1)}, bf16[9,16,256]{2,1,0:T(8,128)(2,1)S(1)}, u32[]{:S(2)}, u32[]{:S(2)}) collective-permute-start(bf16[9,16,256]{2,1,0:T(8,128)(2,1)S(1)} %get-tuple-element.105.refs_0_), channel_id=1, source_target_pairs={{0,4},{4,0},{8,12},{12,8},{1,5},{5,1},{9,13},{13,9},{2,6},{6,2},{1... | collective-permute-start | bytes 221192 | tf_op jit(solution)/shard_map/ppermute | solution.py:366
  93.3 9.5 %collective-permute-start.27 = (bf16[9,16,256]{2,1,0:T(8,128)(2,1)S(1)}, bf16[9,16,256]{2,1,0:T(8,128)(2,1)S(1)}, u32[]{:S(2)}, u32[]{:S(2)}) collective-permute-start(bf16[9,16,256]{2,1,0:T(8,128)(2,1)S(1)} %get-tuple-element.105.refs_0_), channel_id=1, source_target_pairs={{0,8},{4,12},{8,0},{12,4},{1,9},{5,13},{9,1},{13,5},{2,10},{6,14},... | collective-permute-start | bytes 221192 | tf_op jit(solution)/shard_map/ppermute | solution.py:366
  97.1 14.8 %collective-permute-start.15 = (bf16[64,2,128]{2,1,0:T(2,128)(2,1)S(1)}, bf16[64,2,128]{2,1,0:T(2,128)(2,1)S(1)}, u32[]{:S(2)}, u32[]{:S(2)}) collective-permute-start(bf16[64,2,128]{2,1,0:T(2,128)(2,1)S(1)} %get-tuple-element.109), channel_id=1, source_target_pairs={{2,0},{3,1},{6,4},{7,5},{10,8},{11,9},{14,12},{15,13},{18,16},{19,... | collective-permute-start | bytes 98312 | tf_op jit(solution)/shard_map/ppermute | solution.py:501
  99.8 7.6 %collective-permute-start.30 = (bf16[9,16,256]{2,1,0:T(8,128)(2,1)S(1)}, bf16[9,16,256]{2,1,0:T(8,128)(2,1)S(1)}, u32[]{:S(2)}, u32[]{:S(2)}) collective-permute-start(bf16[9,16,256]{2,1,0:T(8,128)(2,1)S(1)} %get-tuple-element.106.refs_0_), channel_id=1, source_target_pairs={{0,4},{4,0},{8,12},{12,8},{1,5},{5,1},{9,13},{13,9},{2,6},{6,2},{1... | collective-permute-start | bytes 221192 | tf_op jit(solution)/shard_map/ppermute | solution.py:366
  100.8 8.5 %collective-permute-start.31 = (bf16[9,16,256]{2,1,0:T(8,128)(2,1)S(1)}, bf16[9,16,256]{2,1,0:T(8,128)(2,1)S(1)}, u32[]{:S(2)}, u32[]{:S(2)}) collective-permute-start(bf16[9,16,256]{2,1,0:T(8,128)(2,1)S(1)} %get-tuple-element.106.refs_0_), channel_id=1, source_target_pairs={{0,8},{4,12},{8,0},{12,4},{1,9},{5,13},{9,1},{13,5},{2,10},{6,14},... | collective-permute-start | bytes 221192 | tf_op jit(solution)/shard_map/ppermute | solution.py:366
  104.7 10.3 %collective-permute-start.29 = (bf16[9,64,256]{2,1,0:T(8,128)(2,1)S(1)}, bf16[9,64,256]{2,1,0:T(8,128)(2,1)S(1)}, u32[]{:S(2)}, u32[]{:S(2)}) collective-permute-start(bf16[9,64,256]{2,1,0:T(8,128)(2,1)S(1)} %lay_parts.2.own), channel_id=1, source_target_pairs={{0,2},{2,0},{1,3},{3,1},{4,6},{6,4},{5,7},{7,5},{8,10},{10,8},{9,1... | collective-permute-start | bytes 884744 | tf_op jit(solution)/shard_map/ppermute | solution.py:361
  109.3 9.1 %collective-permute-start.33 = (bf16[9,64,256]{2,1,0:T(8,128)(2,1)S(1)}, bf16[9,64,256]{2,1,0:T(8,128)(2,1)S(1)}, u32[]{:S(2)}, u32[]{:S(2)}) collective-permute-start(bf16[9,64,256]{2,1,0:T(8,128)(2,1)S(1)} %lay_parts.3.own), channel_id=1, source_target_pairs={{0,2},{2,0},{1,3},{3,1},{4,6},{6,4},{5,7},{7,5},{8,10},{10,8},{9,1... | collective-permute-start | bytes 884744 | tf_op jit(solution)/shard_map/ppermute | solution.py:361
  (17 other events, 128.5 us)

commit v3 on v2

--- a/solution.py
+++ b/solution.py
@@ -322,39 +322,43 @@
                 canvas[r * BLOCK + m + k] += laid[r, :, k * HALF : (k + 1) * HALF]
 
 
-def add_columns(columns_of, *refs):
-    kept, got, outs, sums = refs[:2], refs[2:4], refs[4:-1], refs[-1]
-    for k in range(2):
-        sums[k] = kept[k][...] + got[k][...].astype(F32)
-    size = HALF // 2 // len(outs)
-    for step, out in enumerate(outs):
-        at = pl.multiple_of(partner("blk", step, True) * size, size)
-        part = sums[:, :, pl.ds(at, size), :]
-        out[...] = part if step == 0 else part.astype(BF16)
-
-
-def add_workers(kept, *refs):
-    got, outs = refs[:-2], refs[-2:]
-    for k in range(2):
-        value = kept[k]
-        for part in got:
-            value = value + part[k].astype(F32)
-        outs[k][...] = value.astype(BF16)
-
-
-def lay_parts(*refs):
-    parts, out = refs[:-1], refs[-1]
-    size = HALF // 2 // len(parts)
-    for step, part in enumerate(parts):
-        at = pl.multiple_of(partner("blk", step, True) * size, size)
-        out[:, pl.ds(at, size), :] = part[...]
-
-
-def lay_halves(own, other, out):
-    mine = lax.axis_index("col") == 0
-    for tap in range(9):
-        out[tap, : HALF // 2] = jnp.where(mine, own[tap], other[tap]).astype(F32)
-        out[tap, HALF // 2 :] = jnp.where(mine, other[tap], own[tap]).astype(F32)
+def bit_of(axis, step):
+    return (lax.axis_index(axis) // step) % 2
+
+
+def add_split(step, kept, got, keep, send):
+    low_mine = bit_of("blk", step) == 0
+    half = kept.shape[1] // 2
+    for tap in range(9):
+        value = kept[tap] + got[tap].astype(F32)
+        low, high = value[:half], value[half:]
+        keep[tap] = jnp.where(low_mine, low, high)
+        send[tap] = jnp.where(low_mine, high, low).astype(BF16)
+
+
+def add_last(kept, got, out):
+    out[...] = (kept[...] + got[...].astype(F32)).astype(BF16)
+
+
+def join(step, own, other, out):
+    low_mine = bit_of("blk", step) == 0
+    half = own.shape[1]
+    for tap in range(9):
+        out[tap, :half] = jnp.where(low_mine, own[tap], other[tap])
+        out[tap, half:] = jnp.where(low_mine, other[tap], own[tap])
+
+
+def lay(own, beside, across, across_beside, out):
+    size = own.shape[1]
+    column, side = lax.axis_index("col"), bit_of("blk", 1)
+    for value, c, z in (
+        (own, column, side),
+        (beside, column, 1 - side),
+        (across, 1 - column, side),
+        (across_beside, 1 - column, 1 - side),
+    ):
+        at = pl.multiple_of(c * (2 * size) + z * size, size)
+        out[:, pl.ds(at, size), :] = value[...].astype(F32)
 
 
 def swap(value, axis="ch"):
@@ -390,38 +394,41 @@
 
     def exchange(values):
         if permuted:
-            return [values[0]] + [flip(values[k], "blk", k) for k in range(1, owners)]
+            return [values[0]] + [flip(values[k], "blk", k) for k in (1, 2, 3)]
         return [lax.all_to_all(values[0], "blk", split_axis=0, concat_axis=0, tiled=True)]
 
     tile = grad_out.reshape(TILE_ROWS, BLOCK, TILE_COLS * BLOCK, HALF)
     outgoing = call(
         functools.partial(pack_cotangents, owners, capacity, permuted),
         pieces(BLOCK, BLOCK * capacity, HALF),
-        [SMEM, VMEM], tables, (2**30, 2**21), "pack_cotangents",
+        [SMEM, VMEM], tables, (1, 1), "pack_cotangents",
     )(routing, tile)
+    tie = lax.optimization_barrier
+    saved_slots = saved_pre[0, 0].transpose(1, 2, 0, 3)
+    outgoing, saved_slots, second_mine, tile_mine = tie(
+        (outgoing, saved_slots, second_weight, tile)
+    )
     incoming = exchange(outgoing)
-
-    saved_slots = saved_pre[0, 0].transpose(1, 2, 0, 3)
     masked, *to_owners = call(
         functools.partial(pack_saved, owners, columns, capacity, wide, permuted),
         [shape((MIDDLE, MIDDLE * PER_WORKER, HALF), BF16)] + pieces(MIDDLE, wide * capacity, HALF),
-        [SMEM, VMEM], counts + tables, (2**30, 2**21), "pack_saved",
+        [SMEM, VMEM], counts + tables, (1, 1), "pack_saved",
     )(routing, saved_slots.reshape(MIDDLE, MIDDLE * PER_WORKER, HALF))
     masked = masked.reshape(MIDDLE, MIDDLE, PER_WORKER, HALF)
-    second_other = swap(second_weight)
+    second_other = swap(second_mine)
     masked_other = swap(masked)
-    tile_other = swap(tile)
+    tile_other = swap(tile_mine)
     total = call(
         owner_spread,
         shape((MIDDLE, MIDDLE, TILE_BLOCKS, FULL), F32),
         [VMEM] * 4,
         [pltpu.VMEM((BLOCK, FULL, FULL), BF16), pltpu.VMEM((9, FULL, FULL), BF16)],
-        (2**32, 2**23), "owner_spread",
+        (1, 1), "owner_spread",
     )(tile, tile_other, second_weight, second_other)
 
+    incoming, far, total, masked_other = tie((incoming, to_owners[2:], total, masked_other))
     incoming_other = [swap(value) for value in incoming]
-    to_owners, incoming = lax.optimization_barrier((to_owners, incoming))
-    at_owner = exchange(to_owners)
+    at_owner = exchange(to_owners[:2] + far)
 
     if permuted:
         halved = [shape((9, HALF // 2, FULL), F32), shape((9, HALF // 2, FULL), BF16)]
@@ -430,7 +437,7 @@
     cot, *second_terms = call(
         functools.partial(second_gradient, scale, owners, capacity, permuted),
         [shape((BLOCK, BLOCK * PER_WORKER, FULL), BF16)] + halved,
-        [SMEM] + [VMEM] * (2 * parts + 1), counts, (2**31, 2**21), "second_gradient",
+        [SMEM] + [VMEM] * (2 * parts + 1), counts, (1, 1), "second_gradient",
     )(routing, *incoming, *incoming_other, masked)
 
     saved_tiles = saved_input[0, 0].transpose(1, 2, 0, 3)
@@ -443,37 +450,39 @@
             pltpu.VMEM((MIDDLE, MIDDLE, PER_WORKER, FULL), BF16),
             pltpu.VMEM((9, FULL, FULL), BF16),
         ],
-        (2**32, 2**22), "first_gradient",
+        (1, 1), "first_gradient",
     )(cot, masked, masked_other, second_weight, second_other, saved_tiles)
 
     if permuted:
-        size = HALF // 2 // owners
-        part = (2, 9, size, FULL)
-        second_got, first_got = swap(second_terms[1], "col"), swap(first_terms[1], "col")
-        kept, *sends = call(
-            functools.partial(add_columns, columns),
-            [shape(part, F32)] + [shape(part, BF16)] * (owners - 1),
-            [VMEM] * 4, [pltpu.VMEM((2, 9, HALF // 2, FULL), F32)], (2**28, 2**22), "add_columns",
-        )(second_terms[0], first_terms[0], second_got, first_got)
-        got = [flip(value, "blk", k + 1) for k, value in enumerate(sends)]
-        sums = call(
-            add_workers, [shape(part[1:], BF16)] * 2, [VMEM] * owners, [], (2**26, 2**20),
-            "add_workers",
-        )(kept, *got)
-        grads = []
-        for value in sums:
-            spread = [value] + [flip(value, "blk", k) for k in range(1, owners)]
-            half = call(
-                lay_parts, shape((9, HALF // 2, FULL), BF16), [VMEM] * owners, [], (2**26, 2**20),
-                "lay_parts",
-            )(*spread)
-            grads.append(
-                call(
-                    lay_halves, shape((9, HALF, FULL), F32), [VMEM] * 2, [], (2**26, 2**21),
-                    "lay_halves",
-                )(half, swap(half, "col"))
-            )
-        grad_second, grad_first = grads
+
+        def small(body, rows, kinds, name, *values):
+            outs = [shape((9, rows, FULL), kind) for kind in kinds]
+            return call(body, outs, [VMEM] * len(values), [], (1, 1), name)(*values)
+
+        def split(step, kept, got):
+            rows = kept.shape[1] // 2
+            return small(functools.partial(add_split, step), rows, (F32, BF16), "add_split", kept, got)
+
+        def finish(kept, got):
+            [own] = small(add_last, kept.shape[1], (BF16,), "add_last", kept, got)
+            other = flip(own, "blk", 2)
+            [own] = small(functools.partial(join, 2), 2 * own.shape[1], (BF16,), "join", own, other)
+            beside = flip(own, "blk", 1)
+            across, across_beside = swap(own, "col"), swap(beside, "col")
+            return small(lay, HALF, (F32,), "lay", own, beside, across, across_beside)[0]
+
+        second_got = swap(second_terms[1], "col")
+        first_send, second_got, at_owner[1], at_owner[3] = tie(
+            (first_terms[1], second_got, at_owner[1], at_owner[3])
+        )
+        first_got = swap(first_send, "col")
+        second_kept, second_send = split(1, second_terms[0], second_got)
+        second_kept, second_send = split(2, second_kept, flip(second_send, "blk", 1))
+        first_kept, first_send = split(1, first_terms[0], first_got)
+        first_send, at_owner = tie((first_send, at_owner))
+        first_kept, first_send = split(2, first_kept, flip(first_send, "blk", 1))
+        grad_second = finish(second_kept, flip(second_send, "blk", 2))
+        grad_first = finish(first_kept, flip(first_send, "blk", 2))
     else:
         grad_first, grad_second = lax.psum((first_terms[0], second_terms[0]), ("blk", "col"))
 
@@ -488,7 +497,7 @@
             pltpu.VMEM((MIDDLE, MIDDLE, TILE_BLOCKS, FULL), BF16),
             pltpu.VMEM((OUTER, OUTER, TILE_BLOCKS, HALF), F32),
         ],
-        (2**32, 2**23), "owner_canvas",
+        (1, 1), "owner_canvas",
     )(routing, *at_owner, *at_owner_other, total, first_weight)
 
     up, down = neighbours("blk")

time: 120 us -> 106 us (0.88)
  starting transfers between devices: 45.9 us -> 37.2 us
  waiting for transfers between devices: 41.6 us -> 36.2 us
    ppermute x15 -> x14, waiting for transfers between devices: 36.6 us -> 23.3 us  [flip(): return lax.ppermute(value, axis, [(i, i ^ step) for i in range(size)])]
    ppermute x15 -> x14, starting transfers between devices: 26.3 us -> 21.8 us  [flip(): return lax.ppermute(value, axis, [(i, i ^ step) for i in range(size)])]
    ppermute x1, waiting for transfers between devices: 0.01 us -> 4.35 us  [shards(): from_below = lax.ppermute(canvas[:2].astype(BF16), 'blk', down).astype(F32)]
    ppermute x15 -> x17, waiting for transfers between devices: 4.96 us -> 8.47 us  [swap(): return lax.ppermute(value, axis, [(0, 1), (1, 0)])]
    ppermute x1, starting transfers between devices: 5.18 us -> 2.03 us  [shards(): lax.ppermute(canvas[height - 2:].astype(BF16), 'blk', up).astype(F32)]
    ppermute x15 -> x17, starting transfers between devices: 9.4 us -> 7.39 us  [swap(): return lax.ppermute(value, axis, [(0, 1), (1, 0)])]
    pallas_call x6 -> x10, Pallas kernels: 2.52 us -> 2.55 us  [small(): return call(body, outs, [VMEM] * len(values), [], (1, 1), name)(*values)]
  transfers between devices with their start and end apart: 34 -> 35, of which waited for: 12 -> 13; matrix products, arithmetic and copies ran while one was open for 2% -> 2% of each run, Pallas kernels for 18% -> 19%
where the time goes in v3:
time: 106 us
  starting transfers between devices  37.2 us (35%)
  waiting for transfers between devices  36.2 us (34%)
  Pallas kernels  25.3 us (24%)
  local copies, waits for them, and re-layouts  3.69 us (3%)
  other arithmetic  2.35 us (2%)
    ppermute x14, waiting for transfers between devices, flip(): return lax.ppermute(value, axis, [(i, i ^ step) for i in range(size)])  23.3 us
    ppermute x14, starting transfers between devices, flip(): return lax.ppermute(value, axis, [(i, i ^ step) for i in range(size)])  21.8 us
    pallas_call x1, Pallas kernels, shards(): call(functools.partial(owner_canvas, owners, capacity, wide, permuted), s...  8.65 us
    ppermute x17, waiting for transfers between devices, swap(): return lax.ppermute(value, axis, [(0, 1), (1, 0)])  8.47 us
    ppermute x17, starting transfers between devices, swap(): return lax.ppermute(value, axis, [(0, 1), (1, 0)])  7.39 us
    pallas_call x1, Pallas kernels, shards(): call(functools.partial(first_gradient, scale), halved, [VMEM] * 6, [pltpu...  4.63 us
    ppermute x1, waiting for transfers between devices, shards(): from_below = lax.ppermute(canvas[:2].astype(BF16), 'blk', down).astype(F32)  4.35 us
    pallas_call x1, Pallas kernels, shards(): call(owner_spread, shape((MIDDLE, MIDDLE, TILE_BLOCKS, FULL), F32), [VMEM...  3.97 us
  transfers between devices with their start and end apart: 35, of which 13 were waited for; matrix products, arithmetic and copies ran while one was open for 2% of the time, Pallas kernels for 19%

profile of v3, /device:TPU:0, one launch (start us, length us, event | category | flops | bytes accessed | tf_op | source)
XLA Modules:
  0.0 105.7 jit_solution(10874044947867458197)
XLA Ops:
  1.4 2.1 %pack_cotangents.1 = (bf16[8,64,128]{2,1,0:T(8,128)(2,1)S(1)}, bf16[8,64,128]{2,1,0:T(8,128)(2,1)S(1)}, bf16[8,64,128]{2,1,0:T(8,128)(2,1)S(1)}, bf16[8,64,128]{2,1,0:T(8,128)(2,1)S(1)}) custom-call(s32[4,16]{1,0:T(4,128)S(1)} %bitcast.15, bf16[8,8,32,128]{3,2,1,0:T(8,128)(2,1)} %bitcast.1.tile), custom_call_target="tpu_custom_call" | custom-call | flops 1 | bytes 1 | tf_op jit(solution)/shard_map/pack_cotangents/pallas_call | solution.py:401
  7.2 2.6 %collective-permute-start = (bf16[8,64,128]{2,1,0:T(8,128)(2,1)S(1)}, bf16[8,64,128]{2,1,0:T(8,128)(2,1)S(1)}, u32[]{:S(2)}, u32[]{:S(2)}) collective-permute-start(bf16[8,64,128]{2,1,0:T(8,128)(2,1)S(1)} %get-tuple-element.102), channel_id=1, source_target_pairs={{0,4},{4,0},{8,12},{12,8},{1,5},{5,1},{9,13},{13,9},{2,6},{6,2},{1... | collective-permute-start | bytes 393224 | tf_op jit(solution)/shard_map/ppermute | solution.py:370
  9.8 2.6 %collective-permute-start.1 = (bf16[8,64,128]{2,1,0:T(8,128)(2,1)S(1)}, bf16[8,64,128]{2,1,0:T(8,128)(2,1)S(1)}, u32[]{:S(2)}, u32[]{:S(2)}) collective-permute-start(bf16[8,64,128]{2,1,0:T(8,128)(2,1)S(1)} %get-tuple-element.103), channel_id=1, source_target_pairs={{0,8},{4,12},{8,0},{12,4},{1,9},{5,13},{9,1},{13,5},{2,10},{6,14},... | collective-permute-start | bytes 393224 | tf_op jit(solution)/shard_map/ppermute | solution.py:370
  12.4 4.0 %owner_spread.1.refs_8_ = f32[10,10,32,256]{3,2,1,0:T(8,128)S(1)} custom-call(bf16[8,8,32,128]{3,2,1,0:T(8,128)(2,1)} %bitcast.1.tile, bf16[8,8,32,128]{3,2,1,0:T(8,128)(2,1)S(1)} %collective-permute-done.3.tile_other, bf16[9,128,256]{2,1,0:T(8,128)(2,1)S(1)} %copy-done.1, bf16[9,128,256]{2,1,0:T(8,128)(2,1)S(1)} %collective-permute-done.4.second_other.weight_other), custom_call_target="tpu_custom_call" | custom-call | flops 1 | bytes 1 | tf_op jit(solution)/shard_map/owner_spread/pallas_call | solution.py:421
  18.1 4.6 %collective-permute-done.1.refs_2_ = bf16[8,64,128]{2,1,0:T(8,128)(2,1)S(1)} collective-permute-done((bf16[8,64,128]{2,1,0:T(8,128)(2,1)S(1)}, bf16[8,64,128]{2,1,0:T(8,128)(2,1)S(1)}, u32[]{:S(2)}, u32[]{:S(2)}) %collective-permute-start.1) | collective-permute-done | bytes 131104 | tf_op jit(solution)/shard_map/ppermute | solution.py:370
  24.8 1.8 %second_gradient.1 = (bf16[8,128,256]{2,1,0:T(8,128)(2,1)S(1)}, f32[9,64,256]{2,1,0:T(8,128)S(1)}, bf16[9,64,256]{2,1,0:T(8,128)(2,1)S(1)}) custom-call(s32[4,16]{1,0:T(4,128)S(1)} %bitcast.17, bf16[8,64,128]{2,1,0:T(8,128)(2,1)S(1)} %get-tuple-element.111.refs_0_, bf16[8,64,128]{2,1,0:T(8,128)(2,1)S(1)} %collective-permute-done.refs_1_, ...), custom_call_target="tpu_custom_call" | custom-call | flops 1 | bytes 1 | tf_op jit(solution)/shard_map/second_gradient/pallas_call | solution.py:437
  28.2 2.6 %collective-permute-start.11 = (bf16[10,80,128]{2,1,0:T(8,128)(2,1)S(1)}, bf16[10,80,128]{2,1,0:T(8,128)(2,1)S(1)}, u32[]{:S(2)}, u32[]{:S(2)}) collective-permute-start(bf16[10,80,128]{2,1,0:T(8,128)(2,1)S(1)} %get-tuple-element.120), channel_id=1, source_target_pairs={{0,4},{4,0},{8,12},{12,8},{1,5},{5,1},{9,13},{13,9},{2,6},{6,2},{1... | collective-permute-start | bytes 614408 | tf_op jit(solution)/shard_map/ppermute | solution.py:370
  30.8 2.5 %collective-permute-start.12 = (bf16[10,80,128]{2,1,0:T(8,128)(2,1)S(1)}, bf16[10,80,128]{2,1,0:T(8,128)(2,1)S(1)}, u32[]{:S(2)}, u32[]{:S(2)}) collective-permute-start(bf16[10,80,128]{2,1,0:T(8,128)(2,1)S(1)} %get-tuple-element.121), channel_id=1, source_target_pairs={{0,12},{4,8},{8,4},{12,0},{1,13},{5,9},{9,5},{13,1},{2,14},{6,10},... | collective-permute-start | bytes 614408 | tf_op jit(solution)/shard_map/ppermute | solution.py:370
  33.2 4.6 %first_gradient.1 = (f32[9,64,256]{2,1,0:T(8,128)S(1)}, bf16[9,64,256]{2,1,0:T(8,128)(2,1)S(1)}) custom-call(bf16[8,128,256]{2,1,0:T(8,128)(2,1)S(1)} %get-tuple-element.115.cot, bf16[10,10,16,128]{3,2,1,0:T(8,128)(2,1)S(1)} %bitcast.12, bf16[10,10,16,128]{3,2,1,0:T(8,128)(2,1)S(1)} %collective-permute-done.5.masked_other, ...), custom_call_target="tpu_custom_call" | custom-call | flops 1 | bytes 1 | tf_op jit(solution)/shard_map/first_gradient/pallas_call | solution.py:444
  37.9 4.7 %collective-permute-done.12.refs_3_ = bf16[10,80,128]{2,1,0:T(8,128)(2,1)S(1)} collective-permute-done((bf16[10,80,128]{2,1,0:T(8,128)(2,1)S(1)}, bf16[10,80,128]{2,1,0:T(8,128)(2,1)S(1)}, u32[]{:S(2)}, u32[]{:S(2)}) %collective-permute-start.12) | collective-permute-done | bytes 204832 | tf_op jit(solution)/shard_map/ppermute | solution.py:370
  45.3 5.4 %collective-permute-done.13.got = bf16[9,64,256]{2,1,0:T(8,128)(2,1)S(1)} collective-permute-done((bf16[9,64,256]{2,1,0:T(8,128)(2,1)S(1)}, bf16[9,64,256]{2,1,0:T(8,128)(2,1)S(1)}, u32[]{:S(2)}, u32[]{:S(2)}) %collective-permute-start.13) | collective-permute-done | bytes 294944 | tf_op jit(solution)/shard_map/ppermute | solution.py:365
  50.8 2.3 %collective-permute-done.14.refs_2_ = bf16[10,80,128]{2,1,0:T(8,128)(2,1)S(1)} collective-permute-done((bf16[10,80,128]{2,1,0:T(8,128)(2,1)S(1)}, bf16[10,80,128]{2,1,0:T(8,128)(2,1)S(1)}, u32[]{:S(2)}, u32[]{:S(2)}) %collective-permute-start.14) | collective-permute-done | bytes 204832 | tf_op jit(solution)/shard_map/ppermute | solution.py:370
  54.3 6.4 %collective-permute-done.30.got = bf16[9,16,256]{2,1,0:T(8,128)(2,1)S(1)} collective-permute-done((bf16[9,16,256]{2,1,0:T(8,128)(2,1)S(1)}, bf16[9,16,256]{2,1,0:T(8,128)(2,1)S(1)}, u32[]{:S(2)}, u32[]{:S(2)}) %collective-permute-start.30) | collective-permute-done | bytes 73760 | tf_op jit(solution)/shard_map/ppermute | solution.py:370
  60.8 2.0 %collective-permute-start.23 = (bf16[9,32,256]{2,1,0:T(8,128)(2,1)S(1)}, bf16[9,32,256]{2,1,0:T(8,128)(2,1)S(1)}, u32[]{:S(2)}, u32[]{:S(2)}) collective-permute-start(bf16[9,32,256]{2,1,0:T(8,128)(2,1)S(1)} %get-tuple-element.134), channel_id=1, source_target_pairs={{0,4},{4,0},{8,12},{12,8},{1,5},{5,1},{9,13},{13,9},{2,6},{6,2},{1... | collective-permute-start | bytes 442376 | tf_op jit(solution)/shard_map/ppermute | solution.py:370
  62.8 8.7 %owner_canvas.1 = f32[68,40,128]{2,1,0:T(8,128)S(1)} custom-call(s32[4,16]{1,0:T(4,128)S(1)} %bitcast.18, bf16[10,80,128]{2,1,0:T(8,128)(2,1)S(1)} %get-tuple-element.128.refs_0_, bf16[10,80,128]{2,1,0:T(8,128)(2,1)S(1)} %collective-permute-done.11.refs_1_, bf16[10,80,128]{2,1,0:T(8,128)(2,1)S(1)} %collective-permute-done.14.refs_2_, ...), custom_call_target="tpu_custom_call" | custom-call | flops 1 | bytes 1 | tf_op jit(solution)/shard_map/owner_canvas/pallas_call | solution.py:491
  71.6 2.0 %collective-permute-start.19 = (bf16[2,40,128]{2,1,0:T(8,128)(2,1)S(1)}, bf16[2,40,128]{2,1,0:T(8,128)(2,1)S(1)}, u32[]{:S(2)}, u32[]{:S(2)}) collective-permute-start(bf16[2,40,128]{2,1,0:T(8,128)(2,1)S(1)} %get-tuple-element.144), channel_id=1, source_target_pairs={{0,4},{4,8},{8,12},{1,5},{5,9},{9,13},{2,6},{6,10},{10,14},{3,7},{... | collective-permute-start | bytes 61448 | tf_op jit(solution)/shard_map/ppermute | solution.py:504
  78.1 4.4 %collective-permute-done.20 = bf16[2,40,128]{2,1,0:T(8,128)(2,1)S(1)} collective-permute-done((bf16[2,40,128]{2,1,0:T(8,128)(2,1)S(1)}, bf16[2,40,128]{2,1,0:T(8,128)(2,1)S(1)}, u32[]{:S(2)}, u32[]{:S(2)}) %collective-permute-start.20) | collective-permute-done | bytes 20512 | tf_op jit(solution)/shard_map/ppermute | solution.py:505
  82.6 3.4 %collective-permute-start.21 = (bf16[64,2,128]{2,1,0:T(2,128)(2,1)S(1)}, bf16[64,2,128]{2,1,0:T(2,128)(2,1)S(1)}, u32[]{:S(2)}, u32[]{:S(2)}) collective-permute-start(bf16[64,2,128]{2,1,0:T(2,128)(2,1)S(1)} %get-tuple-element.146), channel_id=1, source_target_pairs={{0,2},{1,3},{4,6},{5,7},{8,10},{9,11},{12,14},{13,15},{16,18},{17,... | collective-permute-start | bytes 98312 | tf_op jit(solution)/shard_map/ppermute | solution.py:509
  86.1 2.0 %collective-permute-start.34 = (bf16[9,32,256]{2,1,0:T(8,128)(2,1)S(1)}, bf16[9,32,256]{2,1,0:T(8,128)(2,1)S(1)}, u32[]{:S(2)}, u32[]{:S(2)}) collective-permute-start(bf16[9,32,256]{2,1,0:T(8,128)(2,1)S(1)} %collective-permute-done.32.beside), channel_id=1, source_target_pairs={{0,2},{2,0},{1,3},{3,1},{4,6},{6,4},{5,7},{7,5},{8,10},{10,8},{9,1... | collective-permute-start | bytes 442376 | tf_op jit(solution)/shard_map/ppermute | solution.py:365
  91.2 2.3 %collective-permute-done.25.other = bf16[9,16,256]{2,1,0:T(8,128)(2,1)S(1)} collective-permute-done((bf16[9,16,256]{2,1,0:T(8,128)(2,1)S(1)}, bf16[9,16,256]{2,1,0:T(8,128)(2,1)S(1)}, u32[]{:S(2)}, u32[]{:S(2)}) %collective-permute-start.25) | collective-permute-done | bytes 73760 | tf_op jit(solution)/shard_map/ppermute | solution.py:370
  93.5 2.8 %collective-permute-start.26 = (bf16[9,32,256]{2,1,0:T(8,128)(2,1)S(1)}, bf16[9,32,256]{2,1,0:T(8,128)(2,1)S(1)}, u32[]{:S(2)}, u32[]{:S(2)}) collective-permute-start(bf16[9,32,256]{2,1,0:T(8,128)(2,1)S(1)} %join.2.own), channel_id=1, source_target_pairs={{0,4},{4,0},{8,12},{12,8},{1,5},{5,1},{9,13},{13,9},{2,6},{6,2},{1... | collective-permute-start | bytes 442376 | tf_op jit(solution)/shard_map/ppermute | solution.py:370
  96.5 2.9 %collective-permute-done.26.beside = bf16[9,32,256]{2,1,0:T(8,128)(2,1)S(1)} collective-permute-done((bf16[9,32,256]{2,1,0:T(8,128)(2,1)S(1)}, bf16[9,32,256]{2,1,0:T(8,128)(2,1)S(1)}, u32[]{:S(2)}, u32[]{:S(2)}) %collective-permute-start.26) | collective-permute-done | bytes 147488 | tf_op jit(solution)/shard_map/ppermute | solution.py:370
  99.4 2.0 %add_convert_fusion = bf16[64,32,128]{2,1,0:T(8,128)(2,1)} fusion(f32[64,32,128]{2,1,0:T(8,128)S(1)} %fusion, bf16[64,32,128]{2,1,0:T(8,128)(2,1)} %param.14), kind=kLoop, calls=%fused_computation | loop fusion | flops 786432 | bytes 2097152 | tf_op jit(solution)/shard_map/convert_element_type | solution.py:512
  102.6 2.0 %collective-permute-done.28.across_beside = bf16[9,32,256]{2,1,0:T(8,128)(2,1)S(1)} collective-permute-done((bf16[9,32,256]{2,1,0:T(8,128)(2,1)S(1)}, bf16[9,32,256]{2,1,0:T(8,128)(2,1)S(1)}, u32[]{:S(2)}, u32[]{:S(2)}) %collective-permute-start.28) | collective-permute-done | bytes 147488 | tf_op jit(solution)/shard_map/ppermute | solution.py:365
  (87 shorter events, 24.0 us)
Async XLA Ops:
  3.5 8.9 %collective-permute-start.3 = (bf16[8,8,32,128]{3,2,1,0:T(8,128)(2,1)}, bf16[8,8,32,128]{3,2,1,0:T(8,128)(2,1)S(1)}, u32[]{:S(2)}, u32[]{:S(2)}) collective-permute-start(bf16[8,8,32,128]{3,2,1,0:T(8,128)(2,1)} %bitcast.1.tile), channel_id=1, source_target_pairs={{0,1},{1,0},{2,3},{3,2},{4,5},{5,4},{6,7},{7,6},{8,9},{9,8},{10,11... | collective-permute-start | bytes 1572872 | tf_op jit(solution)/shard_map/ppermute | solution.py:365
  4.0 8.4 %collective-permute-start.4 = (bf16[9,128,256]{2,1,0:T(8,128)(2,1)}, bf16[9,128,256]{2,1,0:T(8,128)(2,1)S(1)}, u32[]{:S(2)}, u32[]{:S(2)}) collective-permute-start(bf16[9,128,256]{2,1,0:T(8,128)(2,1)} %weight.1), channel_id=1, source_target_pairs={{0,1},{1,0},{2,3},{3,2},{4,5},{5,4},{6,7},{7,6},{8,9},{9,8},{10,11... | collective-permute-start | bytes 1769480 | tf_op jit(solution)/shard_map/ppermute | solution.py:365
  6.7 16.1 %collective-permute-start.5 = (bf16[10,10,16,128]{3,2,1,0:T(8,128)(2,1)S(1)}, bf16[10,10,16,128]{3,2,1,0:T(8,128)(2,1)S(1)}, u32[]{:S(2)}, u32[]{:S(2)}) collective-permute-start(bf16[10,10,16,128]{3,2,1,0:T(8,128)(2,1)S(1)} %bitcast.10), channel_id=1, source_target_pairs={{0,1},{1,0},{2,3},{3,2},{4,5},{5,4},{6,7},{7,6},{8,9},{9,8},{10,11... | collective-permute-start | bytes 1228808 | tf_op jit(solution)/shard_map/ppermute | solution.py:365
  7.2 10.9 %collective-permute-start = (bf16[8,64,128]{2,1,0:T(8,128)(2,1)S(1)}, bf16[8,64,128]{2,1,0:T(8,128)(2,1)S(1)}, u32[]{:S(2)}, u32[]{:S(2)}) collective-permute-start(bf16[8,64,128]{2,1,0:T(8,128)(2,1)S(1)} %get-tuple-element.102), channel_id=1, source_target_pairs={{0,4},{4,0},{8,12},{12,8},{1,5},{5,1},{9,13},{13,9},{2,6},{6,2},{1... | collective-permute-start | bytes 393224 | tf_op jit(solution)/shard_map/ppermute | solution.py:370
  9.8 12.9 %collective-permute-start.1 = (bf16[8,64,128]{2,1,0:T(8,128)(2,1)S(1)}, bf16[8,64,128]{2,1,0:T(8,128)(2,1)S(1)}, u32[]{:S(2)}, u32[]{:S(2)}) collective-permute-start(bf16[8,64,128]{2,1,0:T(8,128)(2,1)S(1)} %get-tuple-element.103), channel_id=1, source_target_pairs={{0,8},{4,12},{8,0},{12,4},{1,9},{5,13},{9,1},{13,5},{2,10},{6,14},... | collective-permute-start | bytes 393224 | tf_op jit(solution)/shard_map/ppermute | solution.py:370
  12.4 10.3 %collective-permute-start.2 = (bf16[8,64,128]{2,1,0:T(8,128)(2,1)S(1)}, bf16[8,64,128]{2,1,0:T(8,128)(2,1)S(1)}, u32[]{:S(2)}, u32[]{:S(2)}) collective-permute-start(bf16[8,64,128]{2,1,0:T(8,128)(2,1)S(1)} %get-tuple-element.104), channel_id=1, source_target_pairs={{0,12},{4,8},{8,4},{12,0},{1,13},{5,9},{9,5},{13,1},{2,14},{6,10},... | collective-permute-start | bytes 393224 | tf_op jit(solution)/shard_map/ppermute | solution.py:370
  26.6 16.0 %collective-permute-start.10 = (bf16[9,64,256]{2,1,0:T(8,128)(2,1)S(1)}, bf16[9,64,256]{2,1,0:T(8,128)(2,1)S(1)}, u32[]{:S(2)}, u32[]{:S(2)}) collective-permute-start(bf16[9,64,256]{2,1,0:T(8,128)(2,1)S(1)} %get-tuple-element.119), channel_id=1, source_target_pairs={{0,2},{2,0},{1,3},{3,1},{4,6},{6,4},{5,7},{7,5},{8,10},{10,8},{9,1... | collective-permute-start | bytes 884744 | tf_op jit(solution)/shard_map/ppermute | solution.py:365
  28.2 9.7 %collective-permute-start.11 = (bf16[10,80,128]{2,1,0:T(8,128)(2,1)S(1)}, bf16[10,80,128]{2,1,0:T(8,128)(2,1)S(1)}, u32[]{:S(2)}, u32[]{:S(2)}) collective-permute-start(bf16[10,80,128]{2,1,0:T(8,128)(2,1)S(1)} %get-tuple-element.120), channel_id=1, source_target_pairs={{0,4},{4,0},{8,12},{12,8},{1,5},{5,1},{9,13},{13,9},{2,6},{6,2},{1... | collective-permute-start | bytes 614408 | tf_op jit(solution)/shard_map/ppermute | solution.py:370
  30.8 11.9 %collective-permute-start.12 = (bf16[10,80,128]{2,1,0:T(8,128)(2,1)S(1)}, bf16[10,80,128]{2,1,0:T(8,128)(2,1)S(1)}, u32[]{:S(2)}, u32[]{:S(2)}) collective-permute-start(bf16[10,80,128]{2,1,0:T(8,128)(2,1)S(1)} %get-tuple-element.121), channel_id=1, source_target_pairs={{0,12},{4,8},{8,4},{12,0},{1,13},{5,9},{9,5},{13,1},{2,14},{6,10},... | collective-permute-start | bytes 614408 | tf_op jit(solution)/shard_map/ppermute | solution.py:370
  42.6 8.1 %collective-permute-start.13 = (bf16[9,64,256]{2,1,0:T(8,128)(2,1)S(1)}, bf16[9,64,256]{2,1,0:T(8,128)(2,1)S(1)}, u32[]{:S(2)}, u32[]{:S(2)}) collective-permute-start(bf16[9,64,256]{2,1,0:T(8,128)(2,1)S(1)} %get-tuple-element.122), channel_id=1, source_target_pairs={{0,2},{2,0},{1,3},{3,1},{4,6},{6,4},{5,7},{7,5},{8,10},{10,8},{9,1... | collective-permute-start | bytes 884744 | tf_op jit(solution)/shard_map/ppermute | solution.py:365
  43.2 10.0 %collective-permute-start.14 = (bf16[10,80,128]{2,1,0:T(8,128)(2,1)S(1)}, bf16[10,80,128]{2,1,0:T(8,128)(2,1)S(1)}, u32[]{:S(2)}, u32[]{:S(2)}) collective-permute-start(bf16[10,80,128]{2,1,0:T(8,128)(2,1)S(1)} %get-tuple-element.126), channel_id=1, source_target_pairs={{0,8},{4,12},{8,0},{12,4},{1,9},{5,13},{9,1},{13,5},{2,10},{6,14},... | collective-permute-start | bytes 614408 | tf_op jit(solution)/shard_map/ppermute | solution.py:370
  43.8 10.3 %collective-permute-start.29 = (bf16[9,32,256]{2,1,0:T(8,128)(2,1)S(1)}, bf16[9,32,256]{2,1,0:T(8,128)(2,1)S(1)}, u32[]{:S(2)}, u32[]{:S(2)}) collective-permute-start(bf16[9,32,256]{2,1,0:T(8,128)(2,1)S(1)} %get-tuple-element.140), channel_id=1, source_target_pairs={{0,4},{4,0},{8,12},{12,8},{1,5},{5,1},{9,13},{13,9},{2,6},{6,2},{1... | collective-permute-start | bytes 442376 | tf_op jit(solution)/shard_map/ppermute | solution.py:370
  53.1 7.7 %collective-permute-start.15 = (bf16[10,80,128]{2,1,0:T(8,128)(2,1)S(1)}, bf16[10,80,128]{2,1,0:T(8,128)(2,1)S(1)}, u32[]{:S(2)}, u32[]{:S(2)}) collective-permute-start(bf16[10,80,128]{2,1,0:T(8,128)(2,1)S(1)} %get-tuple-element.128.refs_0_), channel_id=1, source_target_pairs={{0,1},{1,0},{2,3},{3,2},{4,5},{5,4},{6,7},{7,6},{8,9},{9,8},{10,11... | collective-permute-start | bytes 614408 | tf_op jit(solution)/shard_map/ppermute | solution.py:365
  53.1 9.6 %collective-permute-start.16 = (bf16[10,80,128]{2,1,0:T(8,128)(2,1)S(1)}, bf16[10,80,128]{2,1,0:T(8,128)(2,1)S(1)}, u32[]{:S(2)}, u32[]{:S(2)}) collective-permute-start(bf16[10,80,128]{2,1,0:T(8,128)(2,1)S(1)} %collective-permute-done.11.refs_1_), channel_id=1, source_target_pairs={{0,1},{1,0},{2,3},{3,2},{4,5},{5,4},{6,7},{7,6},{8,9},{9,8},{10,11... | collective-permute-start | bytes 614408 | tf_op jit(solution)/shard_map/ppermute | solution.py:365
  53.6 9.1 %collective-permute-start.17 = (bf16[10,80,128]{2,1,0:T(8,128)(2,1)S(1)}, bf16[10,80,128]{2,1,0:T(8,128)(2,1)S(1)}, u32[]{:S(2)}, u32[]{:S(2)}) collective-permute-start(bf16[10,80,128]{2,1,0:T(8,128)(2,1)S(1)} %collective-permute-done.14.refs_2_), channel_id=1, source_target_pairs={{0,1},{1,0},{2,3},{3,2},{4,5},{5,4},{6,7},{7,6},{8,9},{9,8},{10,11... | collective-permute-start | bytes 614408 | tf_op jit(solution)/shard_map/ppermute | solution.py:365
  53.6 9.1 %collective-permute-start.18 = (bf16[10,80,128]{2,1,0:T(8,128)(2,1)S(1)}, bf16[10,80,128]{2,1,0:T(8,128)(2,1)S(1)}, u32[]{:S(2)}, u32[]{:S(2)}) collective-permute-start(bf16[10,80,128]{2,1,0:T(8,128)(2,1)S(1)} %collective-permute-done.12.refs_3_), channel_id=1, source_target_pairs={{0,1},{1,0},{2,3},{3,2},{4,5},{5,4},{6,7},{7,6},{8,9},{9,8},{10,11... | collective-permute-start | bytes 614408 | tf_op jit(solution)/shard_map/ppermute | solution.py:365
  60.7 12.9 %collective-permute-start.31 = (bf16[9,16,256]{2,1,0:T(8,128)(2,1)S(1)}, bf16[9,16,256]{2,1,0:T(8,128)(2,1)S(1)}, u32[]{:S(2)}, u32[]{:S(2)}) collective-permute-start(bf16[9,16,256]{2,1,0:T(8,128)(2,1)S(1)} %add_last.3.own), channel_id=1, source_target_pairs={{0,8},{4,12},{8,0},{12,4},{1,9},{5,13},{9,1},{13,5},{2,10},{6,14},... | collective-permute-start | bytes 221192 | tf_op jit(solution)/shard_map/ppermute | solution.py:370
  60.8 14.3 %collective-permute-start.23 = (bf16[9,32,256]{2,1,0:T(8,128)(2,1)S(1)}, bf16[9,32,256]{2,1,0:T(8,128)(2,1)S(1)}, u32[]{:S(2)}, u32[]{:S(2)}) collective-permute-start(bf16[9,32,256]{2,1,0:T(8,128)(2,1)S(1)} %get-tuple-element.134), channel_id=1, source_target_pairs={{0,4},{4,0},{8,12},{12,8},{1,5},{5,1},{9,13},{13,9},{2,6},{6,2},{1... | collective-permute-start | bytes 442376 | tf_op jit(solution)/shard_map/ppermute | solution.py:370
  71.6 6.5 %collective-permute-start.19 = (bf16[2,40,128]{2,1,0:T(8,128)(2,1)S(1)}, bf16[2,40,128]{2,1,0:T(8,128)(2,1)S(1)}, u32[]{:S(2)}, u32[]{:S(2)}) collective-permute-start(bf16[2,40,128]{2,1,0:T(8,128)(2,1)S(1)} %get-tuple-element.144), channel_id=1, source_target_pairs={{0,4},{4,8},{8,12},{1,5},{5,9},{9,13},{2,6},{6,10},{10,14},{3,7},{... | collective-permute-start | bytes 61448 | tf_op jit(solution)/shard_map/ppermute | solution.py:504
  73.7 12.5 %collective-permute-start.32 = (bf16[9,32,256]{2,1,0:T(8,128)(2,1)S(1)}, bf16[9,32,256]{2,1,0:T(8,128)(2,1)S(1)}, u32[]{:S(2)}, u32[]{:S(2)}) collective-permute-start(bf16[9,32,256]{2,1,0:T(8,128)(2,1)S(1)} %join.3.own), channel_id=1, source_target_pairs={{0,4},{4,0},{8,12},{12,8},{1,5},{5,1},{9,13},{13,9},{2,6},{6,2},{1... | collective-permute-start | bytes 442376 | tf_op jit(solution)/shard_map/ppermute | solution.py:370
  75.2 13.0 %collective-permute-start.24 = (bf16[9,16,256]{2,1,0:T(8,128)(2,1)S(1)}, bf16[9,16,256]{2,1,0:T(8,128)(2,1)S(1)}, u32[]{:S(2)}, u32[]{:S(2)}) collective-permute-start(bf16[9,16,256]{2,1,0:T(8,128)(2,1)S(1)} %get-tuple-element.136), channel_id=1, source_target_pairs={{0,8},{4,12},{8,0},{12,4},{1,9},{5,13},{9,1},{13,5},{2,10},{6,14},... | collective-permute-start | bytes 221192 | tf_op jit(solution)/shard_map/ppermute | solution.py:370
  82.6 8.5 %collective-permute-start.21 = (bf16[64,2,128]{2,1,0:T(2,128)(2,1)S(1)}, bf16[64,2,128]{2,1,0:T(2,128)(2,1)S(1)}, u32[]{:S(2)}, u32[]{:S(2)}) collective-permute-start(bf16[64,2,128]{2,1,0:T(2,128)(2,1)S(1)} %get-tuple-element.146), channel_id=1, source_target_pairs={{0,2},{1,3},{4,6},{5,7},{8,10},{9,11},{12,14},{13,15},{16,18},{17,... | collective-permute-start | bytes 98312 | tf_op jit(solution)/shard_map/ppermute | solution.py:509
  86.0 15.4 %collective-permute-start.33 = (bf16[9,32,256]{2,1,0:T(8,128)(2,1)S(1)}, bf16[9,32,256]{2,1,0:T(8,128)(2,1)S(1)}, u32[]{:S(2)}, u32[]{:S(2)}) collective-permute-start(bf16[9,32,256]{2,1,0:T(8,128)(2,1)S(1)} %join.3.own), channel_id=1, source_target_pairs={{0,2},{2,0},{1,3},{3,1},{4,6},{6,4},{5,7},{7,5},{8,10},{10,8},{9,1... | collective-permute-start | bytes 442376 | tf_op jit(solution)/shard_map/ppermute | solution.py:365
  86.1 15.3 %collective-permute-start.34 = (bf16[9,32,256]{2,1,0:T(8,128)(2,1)S(1)}, bf16[9,32,256]{2,1,0:T(8,128)(2,1)S(1)}, u32[]{:S(2)}, u32[]{:S(2)}) collective-permute-start(bf16[9,32,256]{2,1,0:T(8,128)(2,1)S(1)} %collective-permute-done.32.beside), channel_id=1, source_target_pairs={{0,2},{2,0},{1,3},{3,1},{4,6},{6,4},{5,7},{7,5},{8,10},{10,8},{9,1... | collective-permute-start | bytes 442376 | tf_op jit(solution)/shard_map/ppermute | solution.py:365
  (18 other events, 120.3 us)

commit v4 on v2

--- a/solution.py
+++ b/solution.py
@@ -274,6 +274,27 @@
         total[spot] = total[spot] + part.reshape(BLOCK, BLOCK, TILE_BLOCKS, FULL)
 
 
+def prepare(owners, columns, capacity, wide, permuted, routing, saved, *refs):
+    (tile, tile_other, second, second_other), refs = refs[:4], refs[4:]
+    masked, outs = refs[0], refs[1:-6]
+    total, counts, table, spread, cot, full = refs[-6:]
+    pack_saved(owners, columns, capacity, wide, permuted, routing, saved, masked, *outs, counts, table)
+    owner_spread(tile, tile_other, second, second_other, spread, cot, full)
+    total[...] = spread[...].astype(BF16)
+
+
+def worker(scale, owners, capacity, permuted, routing, *refs):
+    parts = 1 if not permuted else owners
+    inputs, refs = refs[: 2 * parts], refs[2 * parts :]
+    (masked, masked_other, weight, weight_other, saved), refs = refs[:5], refs[5:]
+    outs, (counts, cot, total, pre, full) = refs[:-5], refs[-5:]
+    pairs = [[out.at[k] for out in outs] for k in range(2)]
+    second_gradient(scale, owners, capacity, permuted, routing, *inputs, masked, cot, *pairs[0], counts)
+    first_gradient(
+        scale, cot, masked, masked_other, weight, weight_other, saved, *pairs[1], total, pre, full
+    )
+
+
 def owner_canvas(owners, capacity, wide, permuted, routing, *refs):
     parts = 1 if not permuted else owners
     got, got_other = views(refs[:parts], owners), views(refs[parts : 2 * parts], owners)
@@ -296,7 +317,7 @@
             [ordered(got[w][m], got_other[w][m], 1) for w in range(owners)], axis=0
         )
         live = dot(pick, block).reshape(MIDDLE, TILE_BLOCKS, FULL) > 0
-        pre[m] = jnp.where(live, total[m], 0.0).astype(BF16)
+        pre[m] = jnp.where(live, total[m].astype(F32), 0.0).astype(BF16)
     size = MIDDLE * MIDDLE * TILE_BLOCKS
     grown[...] = jnp.zeros_like(grown)
     for tap in range(9):
@@ -322,14 +343,15 @@
                 canvas[r * BLOCK + m + k] += laid[r, :, k * HALF : (k + 1) * HALF]
 
 
-def add_columns(columns_of, *refs):
-    kept, got, outs, sums = refs[:2], refs[2:4], refs[4:-1], refs[-1]
-    for k in range(2):
-        sums[k] = kept[k][...] + got[k][...].astype(F32)
+def bit_of(axis, step):
+    return (lax.axis_index(axis) // step) % 2
+
+
+def add_columns(kept, got, *outs):
     size = HALF // 2 // len(outs)
     for step, out in enumerate(outs):
         at = pl.multiple_of(partner("blk", step, True) * size, size)
-        part = sums[:, :, pl.ds(at, size), :]
+        part = kept[:, :, pl.ds(at, size), :] + got[:, :, pl.ds(at, size), :].astype(F32)
         out[...] = part if step == 0 else part.astype(BF16)
 
 
@@ -390,92 +412,96 @@
 
     def exchange(values):
         if permuted:
-            return [values[0]] + [flip(values[k], "blk", k) for k in range(1, owners)]
+            return [values[0]] + [flip(values[k], "blk", k) for k in (1, 2, 3)]
         return [lax.all_to_all(values[0], "blk", split_axis=0, concat_axis=0, tiled=True)]
 
+    tie = lax.optimization_barrier
     tile = grad_out.reshape(TILE_ROWS, BLOCK, TILE_COLS * BLOCK, HALF)
+    second_other, tile_other = swap(second_weight), swap(tile)
     outgoing = call(
         functools.partial(pack_cotangents, owners, capacity, permuted),
         pieces(BLOCK, BLOCK * capacity, HALF),
-        [SMEM, VMEM], tables, (2**30, 2**21), "pack_cotangents",
+        [SMEM, VMEM], tables, (1, 1), "pack_cotangents",
     )(routing, tile)
+    saved_slots = saved_pre[0, 0].transpose(1, 2, 0, 3)
+    outgoing, saved_slots = tie((outgoing, saved_slots))
     incoming = exchange(outgoing)
 
-    saved_slots = saved_pre[0, 0].transpose(1, 2, 0, 3)
-    masked, *to_owners = call(
-        functools.partial(pack_saved, owners, columns, capacity, wide, permuted),
-        [shape((MIDDLE, MIDDLE * PER_WORKER, HALF), BF16)] + pieces(MIDDLE, wide * capacity, HALF),
-        [SMEM, VMEM], counts + tables, (2**30, 2**21), "pack_saved",
-    )(routing, saved_slots.reshape(MIDDLE, MIDDLE * PER_WORKER, HALF))
+    masked, *to_owners, total = call(
+        functools.partial(prepare, owners, columns, capacity, wide, permuted),
+        [shape((MIDDLE, MIDDLE * PER_WORKER, HALF), BF16)]
+        + pieces(MIDDLE, wide * capacity, HALF)
+        + [shape((MIDDLE, MIDDLE, TILE_BLOCKS, FULL), BF16)],
+        [SMEM] + [VMEM] * 5,
+        counts
+        + tables
+        + [
+            pltpu.VMEM((MIDDLE, MIDDLE, TILE_BLOCKS, FULL), F32),
+            pltpu.VMEM((BLOCK, FULL, FULL), BF16),
+            pltpu.VMEM((9, FULL, FULL), BF16),
+        ],
+        (1, 1), "prepare",
+    )(
+        routing, saved_slots.reshape(MIDDLE, MIDDLE * PER_WORKER, HALF),
+        tile, tile_other, second_weight, second_other,
+    )
     masked = masked.reshape(MIDDLE, MIDDLE, PER_WORKER, HALF)
-    second_other = swap(second_weight)
+    incoming, to_owners, total, masked = tie((incoming, to_owners, total, masked))
+    incoming_other = [swap(value) for value in incoming]
     masked_other = swap(masked)
-    tile_other = swap(tile)
-    total = call(
-        owner_spread,
-        shape((MIDDLE, MIDDLE, TILE_BLOCKS, FULL), F32),
-        [VMEM] * 4,
-        [pltpu.VMEM((BLOCK, FULL, FULL), BF16), pltpu.VMEM((9, FULL, FULL), BF16)],
-        (2**32, 2**23), "owner_spread",
-    )(tile, tile_other, second_weight, second_other)
-
-    incoming_other = [swap(value) for value in incoming]
-    to_owners, incoming = lax.optimization_barrier((to_owners, incoming))
     at_owner = exchange(to_owners)
 
+    saved_tiles = saved_input[0, 0].transpose(1, 2, 0, 3)
     if permuted:
-        halved = [shape((9, HALF // 2, FULL), F32), shape((9, HALF // 2, FULL), BF16)]
+        halved = (2, 9, HALF // 2, FULL)
+        halved = [shape(halved, F32), shape(halved, BF16)]
     else:
-        halved = [shape((9, HALF, FULL), F32)]
-    cot, *second_terms = call(
-        functools.partial(second_gradient, scale, owners, capacity, permuted),
-        [shape((BLOCK, BLOCK * PER_WORKER, FULL), BF16)] + halved,
-        [SMEM] + [VMEM] * (2 * parts + 1), counts, (2**31, 2**21), "second_gradient",
-    )(routing, *incoming, *incoming_other, masked)
-
-    saved_tiles = saved_input[0, 0].transpose(1, 2, 0, 3)
-    first_terms = call(
-        functools.partial(first_gradient, scale),
+        halved = [shape((2, 9, HALF, FULL), F32)]
+    terms = call(
+        functools.partial(worker, scale, owners, capacity, permuted),
         halved,
-        [VMEM] * 6,
-        [
+        [SMEM] + [VMEM] * (2 * parts + 5),
+        counts
+        + [
+            pltpu.VMEM((BLOCK, BLOCK * PER_WORKER, FULL), BF16),
             pltpu.VMEM((MIDDLE, MIDDLE, PER_WORKER, FULL), F32),
             pltpu.VMEM((MIDDLE, MIDDLE, PER_WORKER, FULL), BF16),
             pltpu.VMEM((9, FULL, FULL), BF16),
         ],
-        (2**32, 2**22), "first_gradient",
-    )(cot, masked, masked_other, second_weight, second_other, saved_tiles)
+        (1, 1), "worker",
+    )(
+        routing, *incoming, *incoming_other, masked, masked_other, second_weight, second_other,
+        saved_tiles,
+    )
 
     if permuted:
-        size = HALF // 2 // owners
-        part = (2, 9, size, FULL)
-        second_got, first_got = swap(second_terms[1], "col"), swap(first_terms[1], "col")
+        part = (2, 9, HALF // 2 // owners, FULL)
+        send, at_owner[1], at_owner[2] = tie((terms[1], at_owner[1], at_owner[2]))
+        got = swap(send, "col")
         kept, *sends = call(
-            functools.partial(add_columns, columns),
-            [shape(part, F32)] + [shape(part, BF16)] * (owners - 1),
-            [VMEM] * 4, [pltpu.VMEM((2, 9, HALF // 2, FULL), F32)], (2**28, 2**22), "add_columns",
-        )(second_terms[0], first_terms[0], second_got, first_got)
+            add_columns, [shape(part, F32)] + [shape(part, BF16)] * (owners - 1),
+            [VMEM] * 2, [], (1, 1), "add_columns",
+        )(terms[0], got)
+        sends, at_owner = tie((sends, at_owner))
         got = [flip(value, "blk", k + 1) for k, value in enumerate(sends)]
         sums = call(
-            add_workers, [shape(part[1:], BF16)] * 2, [VMEM] * owners, [], (2**26, 2**20),
-            "add_workers",
+            add_workers, [shape(part[1:], BF16)] * 2, [VMEM] * owners, [], (1, 1), "add_workers",
         )(kept, *got)
         grads = []
         for value in sums:
             spread = [value] + [flip(value, "blk", k) for k in range(1, owners)]
             half = call(
-                lay_parts, shape((9, HALF // 2, FULL), BF16), [VMEM] * owners, [], (2**26, 2**20),
+                lay_parts, shape((9, HALF // 2, FULL), BF16), [VMEM] * owners, [], (1, 1),
                 "lay_parts",
             )(*spread)
             grads.append(
                 call(
-                    lay_halves, shape((9, HALF, FULL), F32), [VMEM] * 2, [], (2**26, 2**21),
-                    "lay_halves",
+                    lay_halves, shape((9, HALF, FULL), F32), [VMEM] * 2, [], (1, 1), "lay_halves",
                 )(half, swap(half, "col"))
             )
         grad_second, grad_first = grads
     else:
-        grad_first, grad_second = lax.psum((first_terms[0], second_terms[0]), ("blk", "col"))
+        grad_first, grad_second = lax.psum((terms[0][1], terms[0][0]), ("blk", "col"))
 
     at_owner_other = [swap(value) for value in at_owner]
     height = TILE_ROWS * BLOCK + 4
@@ -488,7 +514,7 @@
             pltpu.VMEM((MIDDLE, MIDDLE, TILE_BLOCKS, FULL), BF16),
             pltpu.VMEM((OUTER, OUTER, TILE_BLOCKS, HALF), F32),
         ],
-        (2**32, 2**23), "owner_canvas",
+        (1, 1), "owner_canvas",
     )(routing, *at_owner, *at_owner_other, total, first_weight)
 
     up, down = neighbours("blk")

time: 120 us -> 103 us (0.86)
  waiting for transfers between devices: 41.6 us -> 33.5 us
  starting transfers between devices: 45.9 us -> 39.8 us
  Pallas kernels: 25.3 us -> 22.1 us
  local copies, waits for them, and re-layouts: 3.57 us -> 5.1 us
    ppermute x15, waiting for transfers between devices: 36.6 us -> 12.2 us  [flip(): return lax.ppermute(value, axis, [(i, i ^ step) for i in range(size)])]
    ppermute x1, waiting for transfers between devices: 0.01 us -> 7.21 us  [shards(): lax.ppermute(inner[:, 34:36].astype(BF16), 'col', down).astype(F32)]
    ppermute x15 -> x14, waiting for transfers between devices: 4.96 us -> 9.77 us  [swap(): return lax.ppermute(value, axis, [(0, 1), (1, 0)])]
    ppermute x1, waiting for transfers between devices: 0.01 us -> 4.36 us  [shards(): from_below = lax.ppermute(canvas[:2].astype(BF16), 'blk', down).astype(F32)]
    ppermute x15 -> x14, starting transfers between devices: 9.4 us -> 6.32 us  [swap(): return lax.ppermute(value, axis, [(0, 1), (1, 0)])]
    ppermute x1, starting transfers between devices: 5.18 us -> 2.61 us  [shards(): lax.ppermute(canvas[height - 2:].astype(BF16), 'blk', up).astype(F32)]
    unnamed x14 -> x18, local copies, waits for them, and re-layouts: 3.31 us -> 4.84 us
    pallas_call x8 -> x6, Pallas kernels: 14.4 us -> 12.9 us  [the longest x1 6.26 us: shards(): call(functools.partial(worker, scale, owners, capacity, permuted), halved...]
  transfers between devices with their start and end apart: 34 -> 33, of which waited for: 12 -> 10; matrix products, arithmetic and copies ran while one was open for 2% -> 2% of each run, Pallas kernels for 18% -> 20%
where the time goes in v4:
time: 103 us
  starting transfers between devices  39.8 us (39%)
  waiting for transfers between devices  33.5 us (33%)
  Pallas kernels  22.1 us (21%)
  local copies, waits for them, and re-layouts  5.1 us (5%)
  other arithmetic  1.29 us (1%)
    ppermute x15, starting transfers between devices, flip(): return lax.ppermute(value, axis, [(i, i ^ step) for i in range(size)])  24.9 us
    ppermute x15, waiting for transfers between devices, flip(): return lax.ppermute(value, axis, [(i, i ^ step) for i in range(size)])  12.2 us
    ppermute x14, waiting for transfers between devices, swap(): return lax.ppermute(value, axis, [(0, 1), (1, 0)])  9.77 us
    pallas_call x1, Pallas kernels, shards(): call(functools.partial(owner_canvas, owners, capacity, wide, permuted), s...  7.46 us
    ppermute x1, waiting for transfers between devices, shards(): lax.ppermute(inner[:, 34:36].astype(BF16), 'col', down).astype(F32)  7.21 us
    ppermute x14, starting transfers between devices, swap(): return lax.ppermute(value, axis, [(0, 1), (1, 0)])  6.32 us
    pallas_call x1, Pallas kernels, shards(): call(functools.partial(worker, scale, owners, capacity, permuted), halved...  6.26 us
    unnamed x18, local copies, waits for them, and re-layouts  4.84 us
  transfers between devices with their start and end apart: 33, of which 10 were waited for; matrix products, arithmetic and copies ran while one was open for 2% of the time, Pallas kernels for 20%

profile of v4, /device:TPU:0, one launch (start us, length us, event | category | flops | bytes accessed | tf_op | source)
XLA Modules:
  0.0 102.7 jit_solution(4536303586362916304)
XLA Ops:
  3.0 1.6 %pack_cotangents.1 = (bf16[8,64,128]{2,1,0:T(8,128)(2,1)S(1)}, bf16[8,64,128]{2,1,0:T(8,128)(2,1)S(1)}, bf16[8,64,128]{2,1,0:T(8,128)(2,1)S(1)}, bf16[8,64,128]{2,1,0:T(8,128)(2,1)S(1)}) custom-call(s32[4,16]{1,0:T(4,128)S(1)} %bitcast.17, bf16[8,8,32,128]{3,2,1,0:T(8,128)(2,1)S(1)} %bitcast.11), custom_call_target="tpu_custom_call" | custom-call | flops 1 | bytes 1 | tf_op jit(solution)/shard_map/pack_cotangents/pallas_call | solution.py:421
  4.6 3.1 %collective-permute-start = (bf16[8,64,128]{2,1,0:T(8,128)(2,1)S(1)}, bf16[8,64,128]{2,1,0:T(8,128)(2,1)S(1)}, u32[]{:S(2)}, u32[]{:S(2)}) collective-permute-start(bf16[8,64,128]{2,1,0:T(8,128)(2,1)S(1)} %get-tuple-element.99), channel_id=1, source_target_pairs={{0,4},{4,0},{8,12},{12,8},{1,5},{5,1},{9,13},{13,9},{2,6},{6,2},{1... | collective-permute-start | bytes 393224 | tf_op jit(solution)/shard_map/ppermute | solution.py:388
  7.6 2.6 %collective-permute-start.1 = (bf16[8,64,128]{2,1,0:T(8,128)(2,1)S(1)}, bf16[8,64,128]{2,1,0:T(8,128)(2,1)S(1)}, u32[]{:S(2)}, u32[]{:S(2)}) collective-permute-start(bf16[8,64,128]{2,1,0:T(8,128)(2,1)S(1)} %get-tuple-element.100), channel_id=1, source_target_pairs={{0,8},{4,12},{8,0},{12,4},{1,9},{5,13},{9,1},{13,5},{2,10},{6,14},... | collective-permute-start | bytes 393224 | tf_op jit(solution)/shard_map/ppermute | solution.py:388
  13.3 4.3 %prepare.1 = (bf16[10,160,128]{2,1,0:T(8,128)(2,1)S(1)}, bf16[10,80,128]{2,1,0:T(8,128)(2,1)S(1)}, bf16[10,80,128]{2,1,0:T(8,128)(2,1)S(1)}, bf16[10,80,128]{2,1...) custom-call(s32[4,16]{1,0:T(4,128)S(1)} %bitcast.18, ...), custom_call_target="tpu_custom_call" | custom-call | flops 1 | bytes 1 | tf_op jit(solution)/shard_map/prepare/pallas_call | solution.py:430
  17.7 2.9 %collective-permute-done.1.refs_2_ = bf16[8,64,128]{2,1,0:T(8,128)(2,1)S(1)} collective-permute-done((bf16[8,64,128]{2,1,0:T(8,128)(2,1)S(1)}, bf16[8,64,128]{2,1,0:T(8,128)(2,1)S(1)}, u32[]{:S(2)}, u32[]{:S(2)}) %collective-permute-start.1) | collective-permute-done | bytes 131104 | tf_op jit(solution)/shard_map/ppermute | solution.py:388
  21.1 2.2 %collective-permute-start.10 = (bf16[10,80,128]{2,1,0:T(8,128)(2,1)S(1)}, bf16[10,80,128]{2,1,0:T(8,128)(2,1)S(1)}, u32[]{:S(2)}, u32[]{:S(2)}) collective-permute-start(bf16[10,80,128]{2,1,0:T(8,128)(2,1)S(1)} %get-tuple-element.116), channel_id=1, source_target_pairs={{0,4},{4,0},{8,12},{12,8},{1,5},{5,1},{9,13},{13,9},{2,6},{6,2},{1... | collective-permute-start | bytes 614408 | tf_op jit(solution)/shard_map/ppermute | solution.py:388
  25.9 6.3 %worker.1 = (f32[2,9,64,256]{3,2,1,0:T(8,128)S(1)}, bf16[2,9,64,256]{3,2,1,0:T(8,128)(2,1)S(1)}) custom-call(s32[4,16]{1,0:T(4,128)S(1)} %bitcast.19, bf16[8,64,128]{2,1,0:T(8,128)(2,1)S(1)} %get-tuple-element.109.refs_0_, bf16[8,64,128]{2,1,0:T(8,128)(2,1)S(1)} %collective-permute-done.refs_1_, bf16[8,64,128]{2,1,0:T(8,128)(2,1)S(1)} %collective-permute-done.1.refs_2_, ...), custom_call_target="tpu_custom_call" | custom-call | flops 1 | bytes 1 | tf_op jit(solution)/shard_map/worker/pallas_call | solution.py:460
  33.3 2.5 %collective-permute-done.11.refs_2_ = bf16[10,80,128]{2,1,0:T(8,128)(2,1)S(1)} collective-permute-done((bf16[10,80,128]{2,1,0:T(8,128)(2,1)S(1)}, bf16[10,80,128]{2,1,0:T(8,128)(2,1)S(1)}, u32[]{:S(2)}, u32[]{:S(2)}) %collective-permute-start.11) | collective-permute-done | bytes 204832 | tf_op jit(solution)/shard_map/ppermute | solution.py:388
  35.8 1.5 %collective-permute-start.12 = (bf16[2,9,64,256]{3,2,1,0:T(8,128)(2,1)S(1)}, bf16[2,9,64,256]{3,2,1,0:T(8,128)(2,1)S(1)}, u32[]{:S(2)}, u32[]{:S(2)}) collective-permute-start(bf16[2,9,64,256]{3,2,1,0:T(8,128)(2,1)S(1)} %get-tuple-element.118), channel_id=1, source_target_pairs={{0,2},{2,0},{1,3},{3,1},{4,6},{6,4},{5,7},{7,5},{8,10},{10,8},{9,1... | collective-permute-start | bytes 1769480 | tf_op jit(solution)/shard_map/ppermute | solution.py:383
  37.3 2.5 %collective-permute-start.13 = (bf16[10,80,128]{2,1,0:T(8,128)(2,1)S(1)}, bf16[10,80,128]{2,1,0:T(8,128)(2,1)S(1)}, u32[]{:S(2)}, u32[]{:S(2)}) collective-permute-start(bf16[10,80,128]{2,1,0:T(8,128)(2,1)S(1)} %get-tuple-element.125), channel_id=1, source_target_pairs={{0,12},{4,8},{8,4},{12,0},{1,13},{5,9},{9,5},{13,1},{2,14},{6,10},... | collective-permute-start | bytes 614408 | tf_op jit(solution)/shard_map/ppermute | solution.py:388
  39.8 8.7 %collective-permute-done.12.got = bf16[2,9,64,256]{3,2,1,0:T(8,128)(2,1)S(1)} collective-permute-done((bf16[2,9,64,256]{3,2,1,0:T(8,128)(2,1)S(1)}, bf16[2,9,64,256]{3,2,1,0:T(8,128)(2,1)S(1)}, u32[]{:S(2)}, u32[]{:S(2)}) %collective-permute-start.12) | collective-permute-done | bytes 589856 | tf_op jit(solution)/shard_map/ppermute | solution.py:383
  49.7 2.7 %collective-permute-start.22 = (bf16[2,9,16,256]{3,2,1,0:T(8,128)(2,1)S(1)}, bf16[2,9,16,256]{3,2,1,0:T(8,128)(2,1)S(1)}, u32[]{:S(2)}, u32[]{:S(2)}) collective-permute-start(bf16[2,9,16,256]{3,2,1,0:T(8,128)(2,1)S(1)} %get-tuple-element.132), channel_id=1, source_target_pairs={{0,4},{4,0},{8,12},{12,8},{1,5},{5,1},{9,13},{13,9},{2,6},{6,2},{1... | collective-permute-start | bytes 442376 | tf_op jit(solution)/shard_map/ppermute | solution.py:388
  52.4 2.3 %collective-permute-start.23 = (bf16[2,9,16,256]{3,2,1,0:T(8,128)(2,1)S(1)}, bf16[2,9,16,256]{3,2,1,0:T(8,128)(2,1)S(1)}, u32[]{:S(2)}, u32[]{:S(2)}) collective-permute-start(bf16[2,9,16,256]{3,2,1,0:T(8,128)(2,1)S(1)} %get-tuple-element.133), channel_id=1, source_target_pairs={{0,8},{4,12},{8,0},{12,4},{1,9},{5,13},{9,1},{13,5},{2,10},{6,14},... | collective-permute-start | bytes 442376 | tf_op jit(solution)/shard_map/ppermute | solution.py:388
  55.2 7.5 %owner_canvas.1 = f32[68,40,128]{2,1,0:T(8,128)S(1)} custom-call(s32[4,16]{1,0:T(4,128)S(1)} %bitcast.20, bf16[10,80,128]{2,1,0:T(8,128)(2,1)S(1)} %get-tuple-element.126.refs_0_, bf16[10,80,128]{2,1,0:T(8,128)(2,1)S(1)} %collective-permute-done.10.refs_1_, bf16[10,80,128]{2,1,0:T(8,128)(2,1)S(1)} %collective-permute-done.11.refs_2_, ...), custom_call_target="tpu_custom_call" | custom-call | flops 1 | bytes 1 | tf_op jit(solution)/shard_map/owner_canvas/pallas_call | solution.py:508
  62.8 2.6 %collective-permute-start.18 = (bf16[2,40,128]{2,1,0:T(8,128)(2,1)S(1)}, bf16[2,40,128]{2,1,0:T(8,128)(2,1)S(1)}, u32[]{:S(2)}, u32[]{:S(2)}) collective-permute-start(bf16[2,40,128]{2,1,0:T(8,128)(2,1)S(1)} %get-tuple-element.138), channel_id=1, source_target_pairs={{0,4},{4,8},{8,12},{1,5},{5,9},{9,13},{2,6},{6,10},{10,14},{3,7},{... | collective-permute-start | bytes 61448 | tf_op jit(solution)/shard_map/ppermute | solution.py:521
  66.4 2.2 %collective-permute-start.27 = (bf16[9,16,256]{2,1,0:T(8,128)(2,1)S(1)}, bf16[9,16,256]{2,1,0:T(8,128)(2,1)S(1)}, u32[]{:S(2)}, u32[]{:S(2)}) collective-permute-start(bf16[9,16,256]{2,1,0:T(8,128)(2,1)S(1)} %get-tuple-element.135.refs_0_), channel_id=1, source_target_pairs={{0,12},{4,8},{8,4},{12,0},{1,13},{5,9},{9,5},{13,1},{2,14},{6,10},... | collective-permute-start | bytes 221192 | tf_op jit(solution)/shard_map/ppermute | solution.py:388
  68.7 1.9 %collective-permute-start.26 = (bf16[9,16,256]{2,1,0:T(8,128)(2,1)S(1)}, bf16[9,16,256]{2,1,0:T(8,128)(2,1)S(1)}, u32[]{:S(2)}, u32[]{:S(2)}) collective-permute-start(bf16[9,16,256]{2,1,0:T(8,128)(2,1)S(1)} %get-tuple-element.135.refs_0_), channel_id=1, source_target_pairs={{0,8},{4,12},{8,0},{12,4},{1,9},{5,13},{9,1},{13,5},{2,10},{6,14},... | collective-permute-start | bytes 221192 | tf_op jit(solution)/shard_map/ppermute | solution.py:388
  70.9 2.4 %collective-permute-start.31 = (bf16[9,16,256]{2,1,0:T(8,128)(2,1)S(1)}, bf16[9,16,256]{2,1,0:T(8,128)(2,1)S(1)}, u32[]{:S(2)}, u32[]{:S(2)}) collective-permute-start(bf16[9,16,256]{2,1,0:T(8,128)(2,1)S(1)} %get-tuple-element.136.refs_0_), channel_id=1, source_target_pairs={{0,12},{4,8},{8,4},{12,0},{1,13},{5,9},{9,5},{13,1},{2,14},{6,10},... | collective-permute-start | bytes 221192 | tf_op jit(solution)/shard_map/ppermute | solution.py:388
  73.4 1.3 %collective-permute-start.19 = (bf16[2,40,128]{2,1,0:T(8,128)(2,1)S(1)}, bf16[2,40,128]{2,1,0:T(8,128)(2,1)S(1)}, u32[]{:S(2)}, u32[]{:S(2)}) collective-permute-start(bf16[2,40,128]{2,1,0:T(8,128)(2,1)S(1)} %get-tuple-element.137), channel_id=1, source_target_pairs={{4,0},{8,4},{12,8},{5,1},{9,5},{13,9},{6,2},{10,6},{14,10},{7,3},{... | collective-permute-start | bytes 61448 | tf_op jit(solution)/shard_map/ppermute | solution.py:522
  74.7 4.4 %collective-permute-done.19 = bf16[2,40,128]{2,1,0:T(8,128)(2,1)S(1)} collective-permute-done((bf16[2,40,128]{2,1,0:T(8,128)(2,1)S(1)}, bf16[2,40,128]{2,1,0:T(8,128)(2,1)S(1)}, u32[]{:S(2)}, u32[]{:S(2)}) %collective-permute-start.19) | collective-permute-done | bytes 20512 | tf_op jit(solution)/shard_map/ppermute | solution.py:522
  80.4 4.7 %collective-permute-done.30.refs_2_ = bf16[9,16,256]{2,1,0:T(8,128)(2,1)S(1)} collective-permute-done((bf16[9,16,256]{2,1,0:T(8,128)(2,1)S(1)}, bf16[9,16,256]{2,1,0:T(8,128)(2,1)S(1)}, u32[]{:S(2)}, u32[]{:S(2)}) %collective-permute-start.30) | collective-permute-done | bytes 73760 | tf_op jit(solution)/shard_map/ppermute | solution.py:388
  85.1 3.4 %collective-permute-start.20 = (bf16[64,2,128]{2,1,0:T(2,128)(2,1)S(1)}, bf16[64,2,128]{2,1,0:T(2,128)(2,1)S(1)}, u32[]{:S(2)}, u32[]{:S(2)}) collective-permute-start(bf16[64,2,128]{2,1,0:T(2,128)(2,1)S(1)} %get-tuple-element.140), channel_id=1, source_target_pairs={{0,2},{1,3},{4,6},{5,7},{8,10},{9,11},{12,14},{13,15},{16,18},{17,... | collective-permute-start | bytes 98312 | tf_op jit(solution)/shard_map/ppermute | solution.py:526
  88.7 2.1 %collective-permute-start.28 = (bf16[9,64,256]{2,1,0:T(8,128)(2,1)S(1)}, bf16[9,64,256]{2,1,0:T(8,128)(2,1)S(1)}, u32[]{:S(2)}, u32[]{:S(2)}) collective-permute-start(bf16[9,64,256]{2,1,0:T(8,128)(2,1)S(1)} %lay_parts.2.own), channel_id=1, source_target_pairs={{0,2},{2,0},{1,3},{3,1},{4,6},{6,4},{5,7},{7,5},{8,10},{10,8},{9,1... | collective-permute-start | bytes 884744 | tf_op jit(solution)/shard_map/ppermute | solution.py:383
  92.3 7.2 %collective-permute-done.21 = bf16[64,2,128]{2,1,0:T(2,128)(2,1)S(1)} collective-permute-done((bf16[64,2,128]{2,1,0:T(2,128)(2,1)S(1)}, bf16[64,2,128]{2,1,0:T(2,128)(2,1)S(1)}, u32[]{:S(2)}, u32[]{:S(2)}) %collective-permute-start.21) | collective-permute-done | bytes 32800 | tf_op jit(solution)/shard_map/ppermute | solution.py:527
  (81 shorter events, 19.2 us)
Async XLA Ops:
  0.6 9.6 %collective-permute-start.4 = (bf16[9,128,256]{2,1,0:T(8,128)(2,1)}, bf16[9,128,256]{2,1,0:T(8,128)(2,1)S(1)}, u32[]{:S(2)}, u32[]{:S(2)}) collective-permute-start(bf16[9,128,256]{2,1,0:T(8,128)(2,1)} %refs_10_.1), channel_id=1, source_target_pairs={{0,1},{1,0},{2,3},{3,2},{4,5},{5,4},{6,7},{7,6},{8,9},{9,8},{10,11... | collective-permute-start | bytes 1769480 | tf_op jit(solution)/shard_map/ppermute | solution.py:383
  1.1 9.1 %collective-permute-start.3 = (bf16[8,8,32,128]{3,2,1,0:T(8,128)(2,1)}, bf16[8,8,32,128]{3,2,1,0:T(8,128)(2,1)S(1)}, u32[]{:S(2)}, u32[]{:S(2)}) collective-permute-start(bf16[8,8,32,128]{3,2,1,0:T(8,128)(2,1)} %bitcast.10), channel_id=1, source_target_pairs={{0,1},{1,0},{2,3},{3,2},{4,5},{5,4},{6,7},{7,6},{8,9},{9,8},{10,11... | collective-permute-start | bytes 1572872 | tf_op jit(solution)/shard_map/ppermute | solution.py:383
  4.6 13.1 %collective-permute-start = (bf16[8,64,128]{2,1,0:T(8,128)(2,1)S(1)}, bf16[8,64,128]{2,1,0:T(8,128)(2,1)S(1)}, u32[]{:S(2)}, u32[]{:S(2)}) collective-permute-start(bf16[8,64,128]{2,1,0:T(8,128)(2,1)S(1)} %get-tuple-element.99), channel_id=1, source_target_pairs={{0,4},{4,0},{8,12},{12,8},{1,5},{5,1},{9,13},{13,9},{2,6},{6,2},{1... | collective-permute-start | bytes 393224 | tf_op jit(solution)/shard_map/ppermute | solution.py:388
  7.6 12.9 %collective-permute-start.1 = (bf16[8,64,128]{2,1,0:T(8,128)(2,1)S(1)}, bf16[8,64,128]{2,1,0:T(8,128)(2,1)S(1)}, u32[]{:S(2)}, u32[]{:S(2)}) collective-permute-start(bf16[8,64,128]{2,1,0:T(8,128)(2,1)S(1)} %get-tuple-element.100), channel_id=1, source_target_pairs={{0,8},{4,12},{8,0},{12,4},{1,9},{5,13},{9,1},{13,5},{2,10},{6,14},... | collective-permute-start | bytes 393224 | tf_op jit(solution)/shard_map/ppermute | solution.py:388
  10.2 10.3 %collective-permute-start.2 = (bf16[8,64,128]{2,1,0:T(8,128)(2,1)S(1)}, bf16[8,64,128]{2,1,0:T(8,128)(2,1)S(1)}, u32[]{:S(2)}, u32[]{:S(2)}) collective-permute-start(bf16[8,64,128]{2,1,0:T(8,128)(2,1)S(1)} %get-tuple-element.101), channel_id=1, source_target_pairs={{0,12},{4,8},{8,4},{12,0},{1,13},{5,9},{9,5},{13,1},{2,14},{6,10},... | collective-permute-start | bytes 393224 | tf_op jit(solution)/shard_map/ppermute | solution.py:388
  21.1 12.2 %collective-permute-start.10 = (bf16[10,80,128]{2,1,0:T(8,128)(2,1)S(1)}, bf16[10,80,128]{2,1,0:T(8,128)(2,1)S(1)}, u32[]{:S(2)}, u32[]{:S(2)}) collective-permute-start(bf16[10,80,128]{2,1,0:T(8,128)(2,1)S(1)} %get-tuple-element.116), channel_id=1, source_target_pairs={{0,4},{4,0},{8,12},{12,8},{1,5},{5,1},{9,13},{13,9},{2,6},{6,2},{1... | collective-permute-start | bytes 614408 | tf_op jit(solution)/shard_map/ppermute | solution.py:388
  23.3 12.5 %collective-permute-start.11 = (bf16[10,80,128]{2,1,0:T(8,128)(2,1)S(1)}, bf16[10,80,128]{2,1,0:T(8,128)(2,1)S(1)}, u32[]{:S(2)}, u32[]{:S(2)}) collective-permute-start(bf16[10,80,128]{2,1,0:T(8,128)(2,1)S(1)} %get-tuple-element.117), channel_id=1, source_target_pairs={{0,8},{4,12},{8,0},{12,4},{1,9},{5,13},{9,1},{13,5},{2,10},{6,14},... | collective-permute-start | bytes 614408 | tf_op jit(solution)/shard_map/ppermute | solution.py:388
  35.8 12.6 %collective-permute-start.12 = (bf16[2,9,64,256]{3,2,1,0:T(8,128)(2,1)S(1)}, bf16[2,9,64,256]{3,2,1,0:T(8,128)(2,1)S(1)}, u32[]{:S(2)}, u32[]{:S(2)}) collective-permute-start(bf16[2,9,64,256]{3,2,1,0:T(8,128)(2,1)S(1)} %get-tuple-element.118), channel_id=1, source_target_pairs={{0,2},{2,0},{1,3},{3,1},{4,6},{6,4},{5,7},{7,5},{8,10},{10,8},{9,1... | collective-permute-start | bytes 1769480 | tf_op jit(solution)/shard_map/ppermute | solution.py:383
  37.3 11.3 %collective-permute-start.13 = (bf16[10,80,128]{2,1,0:T(8,128)(2,1)S(1)}, bf16[10,80,128]{2,1,0:T(8,128)(2,1)S(1)}, u32[]{:S(2)}, u32[]{:S(2)}) collective-permute-start(bf16[10,80,128]{2,1,0:T(8,128)(2,1)S(1)} %get-tuple-element.125), channel_id=1, source_target_pairs={{0,12},{4,8},{8,4},{12,0},{1,13},{5,9},{9,5},{13,1},{2,14},{6,10},... | collective-permute-start | bytes 614408 | tf_op jit(solution)/shard_map/ppermute | solution.py:388
  48.7 6.1 %collective-permute-start.15 = (bf16[10,80,128]{2,1,0:T(8,128)(2,1)S(1)}, bf16[10,80,128]{2,1,0:T(8,128)(2,1)S(1)}, u32[]{:S(2)}, u32[]{:S(2)}) collective-permute-start(bf16[10,80,128]{2,1,0:T(8,128)(2,1)S(1)} %collective-permute-done.10.refs_1_), channel_id=1, source_target_pairs={{0,1},{1,0},{2,3},{3,2},{4,5},{5,4},{6,7},{7,6},{8,9},{9,8},{10,11... | collective-permute-start | bytes 614408 | tf_op jit(solution)/shard_map/ppermute | solution.py:383
  49.7 15.7 %collective-permute-start.22 = (bf16[2,9,16,256]{3,2,1,0:T(8,128)(2,1)S(1)}, bf16[2,9,16,256]{3,2,1,0:T(8,128)(2,1)S(1)}, u32[]{:S(2)}, u32[]{:S(2)}) collective-permute-start(bf16[2,9,16,256]{3,2,1,0:T(8,128)(2,1)S(1)} %get-tuple-element.132), channel_id=1, source_target_pairs={{0,4},{4,0},{8,12},{12,8},{1,5},{5,1},{9,13},{13,9},{2,6},{6,2},{1... | collective-permute-start | bytes 442376 | tf_op jit(solution)/shard_map/ppermute | solution.py:388
  52.4 14.0 %collective-permute-start.23 = (bf16[2,9,16,256]{3,2,1,0:T(8,128)(2,1)S(1)}, bf16[2,9,16,256]{3,2,1,0:T(8,128)(2,1)S(1)}, u32[]{:S(2)}, u32[]{:S(2)}) collective-permute-start(bf16[2,9,16,256]{3,2,1,0:T(8,128)(2,1)S(1)} %get-tuple-element.133), channel_id=1, source_target_pairs={{0,8},{4,12},{8,0},{12,4},{1,9},{5,13},{9,1},{13,5},{2,10},{6,14},... | collective-permute-start | bytes 442376 | tf_op jit(solution)/shard_map/ppermute | solution.py:388
  54.7 11.6 %collective-permute-start.24 = (bf16[2,9,16,256]{3,2,1,0:T(8,128)(2,1)S(1)}, bf16[2,9,16,256]{3,2,1,0:T(8,128)(2,1)S(1)}, u32[]{:S(2)}, u32[]{:S(2)}) collective-permute-start(bf16[2,9,16,256]{3,2,1,0:T(8,128)(2,1)S(1)} %get-tuple-element.134), channel_id=1, source_target_pairs={{0,12},{4,8},{8,4},{12,0},{1,13},{5,9},{9,5},{13,1},{2,14},{6,10},... | collective-permute-start | bytes 442376 | tf_op jit(solution)/shard_map/ppermute | solution.py:388
  62.8 10.6 %collective-permute-start.18 = (bf16[2,40,128]{2,1,0:T(8,128)(2,1)S(1)}, bf16[2,40,128]{2,1,0:T(8,128)(2,1)S(1)}, u32[]{:S(2)}, u32[]{:S(2)}) collective-permute-start(bf16[2,40,128]{2,1,0:T(8,128)(2,1)S(1)} %get-tuple-element.138), channel_id=1, source_target_pairs={{0,4},{4,8},{8,12},{1,5},{5,9},{9,13},{2,6},{6,10},{10,14},{3,7},{... | collective-permute-start | bytes 61448 | tf_op jit(solution)/shard_map/ppermute | solution.py:521
  66.4 22.2 %collective-permute-start.27 = (bf16[9,16,256]{2,1,0:T(8,128)(2,1)S(1)}, bf16[9,16,256]{2,1,0:T(8,128)(2,1)S(1)}, u32[]{:S(2)}, u32[]{:S(2)}) collective-permute-start(bf16[9,16,256]{2,1,0:T(8,128)(2,1)S(1)} %get-tuple-element.135.refs_0_), channel_id=1, source_target_pairs={{0,12},{4,8},{8,4},{12,0},{1,13},{5,9},{9,5},{13,1},{2,14},{6,10},... | collective-permute-start | bytes 221192 | tf_op jit(solution)/shard_map/ppermute | solution.py:388
  68.7 20.0 %collective-permute-start.26 = (bf16[9,16,256]{2,1,0:T(8,128)(2,1)S(1)}, bf16[9,16,256]{2,1,0:T(8,128)(2,1)S(1)}, u32[]{:S(2)}, u32[]{:S(2)}) collective-permute-start(bf16[9,16,256]{2,1,0:T(8,128)(2,1)S(1)} %get-tuple-element.135.refs_0_), channel_id=1, source_target_pairs={{0,8},{4,12},{8,0},{12,4},{1,9},{5,13},{9,1},{13,5},{2,10},{6,14},... | collective-permute-start | bytes 221192 | tf_op jit(solution)/shard_map/ppermute | solution.py:388
  70.5 18.1 %collective-permute-start.25 = (bf16[9,16,256]{2,1,0:T(8,128)(2,1)S(1)}, bf16[9,16,256]{2,1,0:T(8,128)(2,1)S(1)}, u32[]{:S(2)}, u32[]{:S(2)}) collective-permute-start(bf16[9,16,256]{2,1,0:T(8,128)(2,1)S(1)} %get-tuple-element.135.refs_0_), channel_id=1, source_target_pairs={{0,4},{4,0},{8,12},{12,8},{1,5},{5,1},{9,13},{13,9},{2,6},{6,2},{1... | collective-permute-start | bytes 221192 | tf_op jit(solution)/shard_map/ppermute | solution.py:388
  70.9 9.0 %collective-permute-start.31 = (bf16[9,16,256]{2,1,0:T(8,128)(2,1)S(1)}, bf16[9,16,256]{2,1,0:T(8,128)(2,1)S(1)}, u32[]{:S(2)}, u32[]{:S(2)}) collective-permute-start(bf16[9,16,256]{2,1,0:T(8,128)(2,1)S(1)} %get-tuple-element.136.refs_0_), channel_id=1, source_target_pairs={{0,12},{4,8},{8,4},{12,0},{1,13},{5,9},{9,5},{13,1},{2,14},{6,10},... | collective-permute-start | bytes 221192 | tf_op jit(solution)/shard_map/ppermute | solution.py:388
  79.0 6.0 %collective-permute-start.30 = (bf16[9,16,256]{2,1,0:T(8,128)(2,1)S(1)}, bf16[9,16,256]{2,1,0:T(8,128)(2,1)S(1)}, u32[]{:S(2)}, u32[]{:S(2)}) collective-permute-start(bf16[9,16,256]{2,1,0:T(8,128)(2,1)S(1)} %get-tuple-element.136.refs_0_), channel_id=1, source_target_pairs={{0,8},{4,12},{8,0},{12,4},{1,9},{5,13},{9,1},{13,5},{2,10},{6,14},... | collective-permute-start | bytes 221192 | tf_op jit(solution)/shard_map/ppermute | solution.py:388
  79.9 8.6 %collective-permute-start.29 = (bf16[9,16,256]{2,1,0:T(8,128)(2,1)S(1)}, bf16[9,16,256]{2,1,0:T(8,128)(2,1)S(1)}, u32[]{:S(2)}, u32[]{:S(2)}) collective-permute-start(bf16[9,16,256]{2,1,0:T(8,128)(2,1)S(1)} %get-tuple-element.136.refs_0_), channel_id=1, source_target_pairs={{0,4},{4,0},{8,12},{12,8},{1,5},{5,1},{9,13},{13,9},{2,6},{6,2},{1... | collective-permute-start | bytes 221192 | tf_op jit(solution)/shard_map/ppermute | solution.py:388
  85.1 7.1 %collective-permute-start.20 = (bf16[64,2,128]{2,1,0:T(2,128)(2,1)S(1)}, bf16[64,2,128]{2,1,0:T(2,128)(2,1)S(1)}, u32[]{:S(2)}, u32[]{:S(2)}) collective-permute-start(bf16[64,2,128]{2,1,0:T(2,128)(2,1)S(1)} %get-tuple-element.140), channel_id=1, source_target_pairs={{0,2},{1,3},{4,6},{5,7},{8,10},{9,11},{12,14},{13,15},{16,18},{17,... | collective-permute-start | bytes 98312 | tf_op jit(solution)/shard_map/ppermute | solution.py:526
  88.5 13.1 %collective-permute-start.32 = (bf16[9,64,256]{2,1,0:T(8,128)(2,1)S(1)}, bf16[9,64,256]{2,1,0:T(8,128)(2,1)S(1)}, u32[]{:S(2)}, u32[]{:S(2)}) collective-permute-start(bf16[9,64,256]{2,1,0:T(8,128)(2,1)S(1)} %lay_parts.3.own), channel_id=1, source_target_pairs={{0,2},{2,0},{1,3},{3,1},{4,6},{6,4},{5,7},{7,5},{8,10},{10,8},{9,1... | collective-permute-start | bytes 884744 | tf_op jit(solution)/shard_map/ppermute | solution.py:383
  88.7 11.8 %collective-permute-start.28 = (bf16[9,64,256]{2,1,0:T(8,128)(2,1)S(1)}, bf16[9,64,256]{2,1,0:T(8,128)(2,1)S(1)}, u32[]{:S(2)}, u32[]{:S(2)}) collective-permute-start(bf16[9,64,256]{2,1,0:T(8,128)(2,1)S(1)} %lay_parts.2.own), channel_id=1, source_target_pairs={{0,2},{2,0},{1,3},{3,1},{4,6},{6,4},{5,7},{7,5},{8,10},{10,8},{9,1... | collective-permute-start | bytes 884744 | tf_op jit(solution)/shard_map/ppermute | solution.py:383
  90.9 8.6 %collective-permute-start.21 = (bf16[64,2,128]{2,1,0:T(2,128)(2,1)S(1)}, bf16[64,2,128]{2,1,0:T(2,128)(2,1)S(1)}, u32[]{:S(2)}, u32[]{:S(2)}) collective-permute-start(bf16[64,2,128]{2,1,0:T(2,128)(2,1)S(1)} %get-tuple-element.139), channel_id=1, source_target_pairs={{2,0},{3,1},{6,4},{7,5},{10,8},{11,9},{14,12},{15,13},{18,16},{19,... | collective-permute-start | bytes 98312 | tf_op jit(solution)/shard_map/ppermute | solution.py:527
  (18 other events, 100.6 us)

commit v5 on v4

--- a/solution.py
+++ b/solution.py
@@ -18,6 +18,9 @@
 HALF = 128
 FULL = 256
 DEAD = -4096
+HIGH = 68
+RIM = 48
+PART = 288
 WIDE = 40
 
 BF16 = jnp.bfloat16
@@ -256,7 +259,7 @@
         emit(dot_tn(window, grads) * scale, outs, tap)
 
 
-def owner_spread(tile, tile_other, second, second_other, total, cot, full):
+def owner_spread(tile, tile_other, second, second_other, out, total, cot, full):
     row, lane = iota((FULL, FULL), 0), iota((FULL, FULL), 1)
     turn = one_hot(lane == (row % TILE_BLOCKS) * BLOCK + row // TILE_BLOCKS)
     for u in range(BLOCK):
@@ -272,15 +275,7 @@
         part = dot_nt(cot[...].reshape(rows, FULL), full[tap])
         spot = (slice(dy, dy + BLOCK), slice(dx, dx + BLOCK))
         total[spot] = total[spot] + part.reshape(BLOCK, BLOCK, TILE_BLOCKS, FULL)
-
-
-def prepare(owners, columns, capacity, wide, permuted, routing, saved, *refs):
-    (tile, tile_other, second, second_other), refs = refs[:4], refs[4:]
-    masked, outs = refs[0], refs[1:-6]
-    total, counts, table, spread, cot, full = refs[-6:]
-    pack_saved(owners, columns, capacity, wide, permuted, routing, saved, masked, *outs, counts, table)
-    owner_spread(tile, tile_other, second, second_other, spread, cot, full)
-    total[...] = spread[...].astype(BF16)
+    out[...] = total[...].astype(BF16)
 
 
 def worker(scale, owners, capacity, permuted, routing, *refs):
@@ -295,10 +290,16 @@
     )
 
 
+def adjacent(step):
+    me = lax.axis_index("blk")
+    return (me ^ step) == me - 1, (me ^ step) == me + 1
+
+
 def owner_canvas(owners, capacity, wide, permuted, routing, *refs):
     parts = 1 if not permuted else owners
     got, got_other = views(refs[:parts], owners), views(refs[parts : 2 * parts], owners)
-    total, first, canvas, table, pre, grown = refs[2 * parts :]
+    total, first, canvas = refs[2 * parts : 2 * parts + 3]
+    rims, (table, pre, grown) = refs[2 * parts + 3 : -3], refs[-3:]
     owner_table(routing, table, owners, capacity)
     size, into = wide * capacity, MIDDLE * TILE_BLOCKS
     row, lane = iota((size, into), 0), iota((size, into), 1)
@@ -341,6 +342,12 @@
         for r in range(TILE_ROWS):
             for k in range(2):
                 canvas[r * BLOCK + m + k] += laid[r, :, k * HALF : (k + 1) * HALF]
+    for k, rim in enumerate(rims):
+        above, below = adjacent(2 * k + 1)
+        top = jnp.concatenate([canvas[0], canvas[1]], axis=1)
+        bottom = jnp.concatenate([canvas[HIGH - 2], canvas[HIGH - 1]], axis=1)
+        rim[:WIDE] = jnp.where(below, bottom, jnp.where(above, top, 0.0)).astype(BF16)
+        rim[WIDE:] = jnp.zeros((RIM - WIDE, FULL), BF16)
 
 
 def bit_of(axis, step):
@@ -355,28 +362,63 @@
         out[...] = part if step == 0 else part.astype(BF16)
 
 
-def add_workers(kept, *refs):
-    got, outs = refs[:-2], refs[-2:]
-    for k in range(2):
-        value = kept[k]
-        for part in got:
-            value = value + part[k].astype(F32)
-        outs[k][...] = value.astype(BF16)
-
-
-def lay_parts(*refs):
-    parts, out = refs[:-1], refs[-1]
-    size = HALF // 2 // len(parts)
-    for step, part in enumerate(parts):
-        at = pl.multiple_of(partner("blk", step, True) * size, size)
-        out[:, pl.ds(at, size), :] = part[...]
-
-
-def lay_halves(own, other, out):
-    mine = lax.axis_index("col") == 0
-    for tap in range(9):
-        out[tap, : HALF // 2] = jnp.where(mine, own[tap], other[tap]).astype(F32)
-        out[tap, HALF // 2 :] = jnp.where(mine, other[tap], own[tap]).astype(F32)
+def add_workers(kept, got_1, got_2, got_3, rim_1, rim_3, out, out_1, out_3):
+    value = kept[...]
+    for part in (got_1, got_2, got_3):
+        value = value + part[...].astype(F32)
+    value = value.astype(BF16).reshape(PART, FULL)
+    out[...] = value
+    for message, rim in ((out_1, rim_1), (out_3, rim_3)):
+        message[:PART] = value
+        message[PART:] = rim[...]
+
+
+def column_message(canvas, got_1, got_3, out, rim, strip):
+    out[:PART] = got_3[:PART]
+    for j in range(2):
+        c = 32 + 2 * lax.axis_index("col") + j
+        strip[...] = canvas[pl.ds(2 * WIDE + c, 64, stride=WIDE), :]
+        for step, got in ((1, got_1), (3, got_3)):
+            rim[...] = got[PART:].astype(F32)
+            row = rim[pl.ds(c, 1), :]
+            above, below = adjacent(step)
+            top, bottom = jnp.where(above, row, 0.0), jnp.where(below, row, 0.0)
+            strip[0:1] += top[:, :HALF]
+            strip[1:2] += top[:, HALF:]
+            strip[62:63] += bottom[:, :HALF]
+            strip[63:64] += bottom[:, HALF:]
+        out[PART:, j * HALF : (j + 1) * HALF] = strip[...].astype(BF16)
+
+
+def close(tile, canvas, got_1, got_3, across, out, total):
+    rows = TILE_ROWS * BLOCK * 32
+    inner = canvas[2 : HIGH - 2, :32, :].reshape(rows, HALF)
+    total[...] = tile[...].reshape(rows, HALF).astype(F32) + inner
+    for step, got in ((1, got_1), (3, got_3)):
+        rim = got[PART : PART + 32].astype(F32)
+        above, below = adjacent(step)
+        top, bottom = jnp.where(above, rim, 0.0), jnp.where(below, rim, 0.0)
+        total[0:32] += top[:, :HALF]
+        total[32:64] += top[:, HALF:]
+        total[rows - 64 : rows - 32] += bottom[:, :HALF]
+        total[rows - 32 : rows] += bottom[:, HALF:]
+    strip = across[PART:].astype(F32)
+    at = jnp.where(lax.axis_index("col") == 0, 30, 0)
+    for j in range(2):
+        spot = (pl.ds(at + j, 64, stride=32), slice(None))
+        total[spot] = total[spot] + strip[:, j * HALF : (j + 1) * HALF]
+    out[...] = total[...].astype(BF16).reshape(out.shape)
+
+
+def lay(*refs):
+    outs = refs[-2:]
+    size, column = HALF // 8, lax.axis_index("col")
+    for k, part in enumerate(refs[:-2]):
+        place = (column if k < 4 else 1 - column) * 4 + partner("blk", k % 4, True)
+        at = pl.multiple_of(place * size, size)
+        value = part[:PART].astype(F32).reshape(2, 9, size, FULL)
+        for out, grad in zip(outs, (0, 1)):
+            out[:, pl.ds(at, size), :] = value[grad]
 
 
 def swap(value, axis="ch"):
@@ -427,26 +469,13 @@
     outgoing, saved_slots = tie((outgoing, saved_slots))
     incoming = exchange(outgoing)
 
-    masked, *to_owners, total = call(
-        functools.partial(prepare, owners, columns, capacity, wide, permuted),
-        [shape((MIDDLE, MIDDLE * PER_WORKER, HALF), BF16)]
-        + pieces(MIDDLE, wide * capacity, HALF)
-        + [shape((MIDDLE, MIDDLE, TILE_BLOCKS, FULL), BF16)],
-        [SMEM] + [VMEM] * 5,
-        counts
-        + tables
-        + [
-            pltpu.VMEM((MIDDLE, MIDDLE, TILE_BLOCKS, FULL), F32),
-            pltpu.VMEM((BLOCK, FULL, FULL), BF16),
-            pltpu.VMEM((9, FULL, FULL), BF16),
-        ],
-        (1, 1), "prepare",
-    )(
-        routing, saved_slots.reshape(MIDDLE, MIDDLE * PER_WORKER, HALF),
-        tile, tile_other, second_weight, second_other,
-    )
+    masked, *to_owners = call(
+        functools.partial(pack_saved, owners, columns, capacity, wide, permuted),
+        [shape((MIDDLE, MIDDLE * PER_WORKER, HALF), BF16)] + pieces(MIDDLE, wide * capacity, HALF),
+        [SMEM, VMEM], counts + tables, (1, 1), "pack_saved",
+    )(routing, saved_slots.reshape(MIDDLE, MIDDLE * PER_WORKER, HALF))
     masked = masked.reshape(MIDDLE, MIDDLE, PER_WORKER, HALF)
-    incoming, to_owners, total, masked = tie((incoming, to_owners, total, masked))
+    incoming, to_owners, masked = tie((incoming, to_owners, masked))
     incoming_other = [swap(value) for value in incoming]
     masked_other = swap(masked)
     at_owner = exchange(to_owners)
@@ -475,52 +504,73 @@
     )
 
     if permuted:
+        terms = list(terms)
+        terms[1], at_owner[2] = tie((terms[1], at_owner[2]))
+    at_owner, tile_here = tie((at_owner, tile))
+    total = call(
+        owner_spread,
+        shape((MIDDLE, MIDDLE, TILE_BLOCKS, FULL), BF16),
+        [VMEM] * 4,
+        [
+            pltpu.VMEM((MIDDLE, MIDDLE, TILE_BLOCKS, FULL), F32),
+            pltpu.VMEM((BLOCK, FULL, FULL), BF16),
+            pltpu.VMEM((9, FULL, FULL), BF16),
+        ],
+        (1, 1), "owner_spread",
+    )(tile_here, tile_other, second_weight, second_other)
+
+    def owner(at_owner):
+        at_owner_other = [swap(value) for value in at_owner]
+        return call(
+            functools.partial(owner_canvas, owners, capacity, wide, permuted),
+            [shape((HIGH, WIDE, HALF), F32)] + [shape((RIM, FULL), BF16)] * (2 if permuted else 0),
+            [SMEM] + [VMEM] * (2 * parts + 2),
+            tables
+            + [
+                pltpu.VMEM((MIDDLE, MIDDLE, TILE_BLOCKS, FULL), BF16),
+                pltpu.VMEM((OUTER, OUTER, TILE_BLOCKS, HALF), F32),
+            ],
+            (1, 1), "owner_canvas",
+        )(routing, *at_owner, *at_owner_other, total, first_weight)
+
+    if permuted:
         part = (2, 9, HALF // 2 // owners, FULL)
-        send, at_owner[1], at_owner[2] = tie((terms[1], at_owner[1], at_owner[2]))
-        got = swap(send, "col")
+        got = swap(terms[1], "col")
+        total, got = tie((total, got))
         kept, *sends = call(
             add_columns, [shape(part, F32)] + [shape(part, BF16)] * (owners - 1),
             [VMEM] * 2, [], (1, 1), "add_columns",
         )(terms[0], got)
         sends, at_owner = tie((sends, at_owner))
         got = [flip(value, "blk", k + 1) for k, value in enumerate(sends)]
-        sums = call(
-            add_workers, [shape(part[1:], BF16)] * 2, [VMEM] * owners, [], (1, 1), "add_workers",
-        )(kept, *got)
-        grads = []
-        for value in sums:
-            spread = [value] + [flip(value, "blk", k) for k in range(1, owners)]
-            half = call(
-                lay_parts, shape((9, HALF // 2, FULL), BF16), [VMEM] * owners, [], (1, 1),
-                "lay_parts",
-            )(*spread)
-            grads.append(
-                call(
-                    lay_halves, shape((9, HALF, FULL), F32), [VMEM] * 2, [], (1, 1), "lay_halves",
-                )(half, swap(half, "col"))
-            )
-        grad_second, grad_first = grads
-    else:
-        grad_first, grad_second = lax.psum((terms[0][1], terms[0][0]), ("blk", "col"))
-
-    at_owner_other = [swap(value) for value in at_owner]
-    height = TILE_ROWS * BLOCK + 4
-    canvas = call(
-        functools.partial(owner_canvas, owners, capacity, wide, permuted),
-        shape((height, WIDE, HALF), F32),
-        [SMEM] + [VMEM] * (2 * parts + 2),
-        tables
-        + [
-            pltpu.VMEM((MIDDLE, MIDDLE, TILE_BLOCKS, FULL), BF16),
-            pltpu.VMEM((OUTER, OUTER, TILE_BLOCKS, HALF), F32),
-        ],
-        (1, 1), "owner_canvas",
-    )(routing, *at_owner, *at_owner_other, total, first_weight)
-
+        canvas, *rims = owner(at_owner)
+        message = shape((PART, FULL), BF16)
+        wider = shape((PART + RIM, FULL), BF16)
+        own, *wides = call(
+            add_workers, [message, wider, wider], [VMEM] * 6, [], (1, 1), "add_workers",
+        )(kept, *got, *rims)
+        got = [flip(value, "blk", k) for k, value in ((1, wides[0]), (2, own), (3, wides[1]))]
+        last = call(
+            column_message, shape((PART + 64, FULL), BF16), [VMEM] * 3,
+            [pltpu.VMEM((RIM, FULL), F32), pltpu.VMEM((64, HALF), F32)],
+            (1, 1), "column_message",
+        )(canvas.reshape(HIGH * WIDE, HALF), got[0], got[2])
+        across = [swap(value, "col") for value in (own, got[0][:PART], got[1], last)]
+        grad_in = call(
+            close, shape(grad_out.shape, BF16), [VMEM] * 5,
+            [pltpu.VMEM((TILE_ROWS * BLOCK * 32, HALF), F32)], (1, 1), "close",
+        )(grad_out, canvas, got[0], got[2], across[3])
+        grad_second, grad_first = call(
+            lay, [shape((9, HALF, FULL), F32)] * 2, [VMEM] * 8, [], (1, 1), "lay",
+        )(own, *got, *across)
+        return (grad_in, grad_first, grad_second)
+
+    grad_first, grad_second = lax.psum((terms[0][1], terms[0][0]), ("blk", "col"))
+    [canvas] = owner(at_owner)
     up, down = neighbours("blk")
-    from_above = lax.ppermute(canvas[height - 2 :].astype(BF16), "blk", up).astype(F32)
+    from_above = lax.ppermute(canvas[HIGH - 2 :].astype(BF16), "blk", up).astype(F32)
     from_below = lax.ppermute(canvas[:2].astype(BF16), "blk", down).astype(F32)
-    inner = canvas[2 : height - 2]
+    inner = canvas[2 : HIGH - 2]
     inner = inner.at[:2].add(from_above).at[-2:].add(from_below)
     up, down = neighbours("col")
     from_left = lax.ppermute(inner[:, 32:34].astype(BF16), "col", up).astype(F32)

time: 103 us -> 96.9 us (0.941)
  starting transfers between devices: 39.8 us -> 28.1 us
  waiting for transfers between devices: 33.5 us -> 41.2 us
  other arithmetic: 1.29 us -> 0 us
  local copies, waits for them, and re-layouts: 5.1 us -> 3.81 us
    ppermute x15 -> x12, waiting for transfers between devices: 12.2 us -> 33.9 us  [flip(): return lax.ppermute(value, axis, [(i, i ^ step) for i in range(size)])]
    ppermute x4 -> x0, waiting for transfers between devices: 11.6 us -> none  [the longest x1 7.21 us: shards(): lax.ppermute(inner[:, 34:36].astype(BF16), 'col', down).astype(F32)]
    ppermute x4 -> x0, starting transfers between devices: 8.58 us -> none  [the longest x1 3.39 us: shards(): lax.ppermute(inner[:, 32:34].astype(BF16), 'col', up).astype(F32)]
    ppermute x15 -> x12, starting transfers between devices: 24.9 us -> 19.8 us  [flip(): return lax.ppermute(value, axis, [(i, i ^ step) for i in range(size)])]
    ppermute x14 -> x16, waiting for transfers between devices: 9.77 us -> 7.34 us  [swap(): return lax.ppermute(value, axis, [(0, 1), (1, 0)])]
    ppermute x14 -> x16, starting transfers between devices: 6.32 us -> 8.29 us  [swap(): return lax.ppermute(value, axis, [(0, 1), (1, 0)])]
    unnamed x18 -> x16, local copies, waits for them, and re-layouts: 4.84 us -> 3.8 us
  transfers between devices with their start and end apart: 33 -> 28, of which waited for: 10 -> 15; matrix products, arithmetic and copies ran while one was open for 2% -> 0% of each run, Pallas kernels for 20% -> 22%
where the time goes in v5:
time: 96.9 us; the launch traced here: 96.6 us
  waiting for transfers between devices  41.2 us (43%)
  starting transfers between devices  28.1 us (29%)
  Pallas kernels  22.7 us (23%)
  local copies, waits for them, and re-layouts  3.81 us (4%)
    ppermute x12, waiting for transfers between devices, flip(): return lax.ppermute(value, axis, [(i, i ^ step) for i in range(size)])  33.9 us
    ppermute x12, starting transfers between devices, flip(): return lax.ppermute(value, axis, [(i, i ^ step) for i in range(size)])  19.8 us
    ppermute x16, starting transfers between devices, swap(): return lax.ppermute(value, axis, [(0, 1), (1, 0)])  8.29 us
    pallas_call x1, Pallas kernels, owner(): call(functools.partial(owner_canvas, owners, capacity, wide, permuted), [...  7.47 us
    ppermute x16, waiting for transfers between devices, swap(): return lax.ppermute(value, axis, [(0, 1), (1, 0)])  7.34 us
    pallas_call x1, Pallas kernels, shards(): call(functools.partial(worker, scale, owners, capacity, permuted), halved...  6.24 us
    unnamed x16, local copies, waits for them, and re-layouts  3.8 us
    pallas_call x1, Pallas kernels, shards(): call(owner_spread, shape((MIDDLE, MIDDLE, TILE_BLOCKS, FULL), BF16), [VME...  2.93 us
  transfers between devices with their start and end apart: 28, of which 15 were waited for; matrix products, arithmetic and copies ran while one was open for 0% of the time, Pallas kernels for 22%

profile of v5, /device:TPU:0, one launch (start us, length us, event | category | flops | bytes accessed | tf_op | source)
XLA Modules:
  0.0 96.6 jit_solution(16081773180914807786)
XLA Ops:
  2.9 1.6 %pack_cotangents.1 = (bf16[8,64,128]{2,1,0:T(8,128)(2,1)S(1)}, bf16[8,64,128]{2,1,0:T(8,128)(2,1)S(1)}, bf16[8,64,128]{2,1,0:T(8,128)(2,1)S(1)}, bf16[8,64,128]{2,1,0:T(8,128)(2,1)S(1)}) custom-call(s32[4,16]{1,0:T(4,128)S(1)} %bitcast.19, bf16[8,8,32,128]{3,2,1,0:T(8,128)(2,1)S(1)} %bitcast.12), custom_call_target="tpu_custom_call" | custom-call | flops 1 | bytes 1 | tf_op jit(solution)/shard_map/pack_cotangents/pallas_call | solution.py:463
  4.5 2.7 %collective-permute-start = (bf16[8,64,128]{2,1,0:T(8,128)(2,1)S(1)}, bf16[8,64,128]{2,1,0:T(8,128)(2,1)S(1)}, u32[]{:S(2)}, u32[]{:S(2)}) collective-permute-start(bf16[8,64,128]{2,1,0:T(8,128)(2,1)S(1)} %get-tuple-element.61), channel_id=1, source_target_pairs={{0,4},{4,0},{8,12},{12,8},{1,5},{5,1},{9,13},{13,9},{2,6},{6,2},{1... | collective-permute-start | bytes 393224 | tf_op jit(solution)/shard_map/ppermute | solution.py:430
  7.1 2.6 %collective-permute-start.1 = (bf16[8,64,128]{2,1,0:T(8,128)(2,1)S(1)}, bf16[8,64,128]{2,1,0:T(8,128)(2,1)S(1)}, u32[]{:S(2)}, u32[]{:S(2)}) collective-permute-start(bf16[8,64,128]{2,1,0:T(8,128)(2,1)S(1)} %get-tuple-element.62), channel_id=1, source_target_pairs={{0,8},{4,12},{8,0},{12,4},{1,9},{5,13},{9,1},{13,5},{2,10},{6,14},... | collective-permute-start | bytes 393224 | tf_op jit(solution)/shard_map/ppermute | solution.py:430
  10.7 1.6 %pack_saved.1 = (bf16[10,160,128]{2,1,0:T(8,128)(2,1)S(1)}, bf16[10,80,128]{2,1,0:T(8,128)(2,1)S(1)}, bf16[10,80,128]{2,1,0:T(8,128)(2,1)S(1)}, bf16[10,80,128]{2,1,0:T(8,128)(2,1)S(1)}, bf16[10,80,128]{2,1,0:T(8,128)(2,1)S(1)}) custom-call(s32[4,16]{1,0:T(4,128)S(1)} %bitcast.20, bf16[10,160,128]{2,1,0:T(8,128)(2,1)S(1)} %bitcast.18), custom_call_target="tpu_custom_call" | custom-call | flops 1 | bytes 1 | tf_op jit(solution)/shard_map/pack_saved/pallas_call | solution.py:472
  13.6 6.5 %collective-permute-done.1.refs_2_ = bf16[8,64,128]{2,1,0:T(8,128)(2,1)S(1)} collective-permute-done((bf16[8,64,128]{2,1,0:T(8,128)(2,1)S(1)}, bf16[8,64,128]{2,1,0:T(8,128)(2,1)S(1)}, u32[]{:S(2)}, u32[]{:S(2)}) %collective-permute-start.1) | collective-permute-done | bytes 131104 | tf_op jit(solution)/shard_map/ppermute | solution.py:430
  20.5 3.7 %collective-permute-start.10 = (bf16[10,80,128]{2,1,0:T(8,128)(2,1)S(1)}, bf16[10,80,128]{2,1,0:T(8,128)(2,1)S(1)}, u32[]{:S(2)}, u32[]{:S(2)}) collective-permute-start(bf16[10,80,128]{2,1,0:T(8,128)(2,1)S(1)} %get-tuple-element.79), channel_id=1, source_target_pairs={{0,8},{4,12},{8,0},{12,4},{1,9},{5,13},{9,1},{13,5},{2,10},{6,14},... | collective-permute-start | bytes 614408 | tf_op jit(solution)/shard_map/ppermute | solution.py:430
  26.9 6.2 %worker.1 = (f32[2,9,64,256]{3,2,1,0:T(8,128)S(1)}, bf16[2,9,64,256]{3,2,1,0:T(8,128)(2,1)S(1)}) custom-call(s32[4,16]{1,0:T(4,128)S(1)} %bitcast.21, bf16[8,64,128]{2,1,0:T(8,128)(2,1)S(1)} %get-tuple-element.70.refs_0_, bf16[8,64,128]{2,1,0:T(8,128)(2,1)S(1)} %collective-permute-done.refs_1_, bf16[8,64,128]{2,1,0:T(8,128)(2,1)S(1)} %collective-permute-done.1.refs_2_, ...), custom_call_target="tpu_custom_call" | custom-call | flops 1 | bytes 1 | tf_op jit(solution)/shard_map/worker/pallas_call | solution.py:489
  34.3 1.5 %collective-permute-start.13 = (bf16[2,9,64,256]{3,2,1,0:T(8,128)(2,1)S(1)}, bf16[2,9,64,256]{3,2,1,0:T(8,128)(2,1)S(1)}, u32[]{:S(2)}, u32[]{:S(2)}) collective-permute-start(bf16[2,9,64,256]{3,2,1,0:T(8,128)(2,1)S(1)} %get-tuple-element.83), channel_id=1, source_target_pairs={{0,2},{2,0},{1,3},{3,1},{4,6},{6,4},{5,7},{7,5},{8,10},{10,8},{9,1... | collective-permute-start | bytes 1769480 | tf_op jit(solution)/shard_map/ppermute | solution.py:425
  37.3 8.3 %collective-permute-done.11.refs_3_ = bf16[10,80,128]{2,1,0:T(8,128)(2,1)S(1)} collective-permute-done((bf16[10,80,128]{2,1,0:T(8,128)(2,1)S(1)}, bf16[10,80,128]{2,1,0:T(8,128)(2,1)S(1)}, u32[]{:S(2)}, u32[]{:S(2)}) %collective-permute-start.11) | collective-permute-done | bytes 204832 | tf_op jit(solution)/shard_map/ppermute | solution.py:430
  45.6 3.3 %collective-permute-done.9.refs_1_ = bf16[10,80,128]{2,1,0:T(8,128)(2,1)S(1)} collective-permute-done((bf16[10,80,128]{2,1,0:T(8,128)(2,1)S(1)}, bf16[10,80,128]{2,1,0:T(8,128)(2,1)S(1)}, u32[]{:S(2)}, u32[]{:S(2)}) %collective-permute-start.9) | collective-permute-done | bytes 204832 | tf_op jit(solution)/shard_map/ppermute | solution.py:430
  48.9 2.9 %owner_spread.1.refs_8_ = bf16[10,10,32,256]{3,2,1,0:T(8,128)(2,1)S(1)} custom-call(bf16[8,8,32,128]{3,2,1,0:T(8,128)(2,1)S(1)} %bitcast.14, bf16[8,8,32,128]{3,2,1,0:T(8,128)(2,1)S(1)} %collective-permute-done.12.tile_other, bf16[9,128,256]{2,1,0:T(8,128)(2,1)S(1)} %copy-done.2, bf16[9,128,256]{2,1,0:T(8,128)(2,1)S(1)} %collective-permute-done.8.refs_11_.second_other), custom_call_target="tpu_custom_call" | custom-call | flops 1 | bytes 1 | tf_op jit(solution)/shard_map/owner_spread/pallas_call | solution.py:510
  53.5 2.3 %collective-permute-start.19 = (bf16[2,9,16,256]{3,2,1,0:T(8,128)(2,1)S(1)}, bf16[2,9,16,256]{3,2,1,0:T(8,128)(2,1)S(1)}, u32[]{:S(2)}, u32[]{:S(2)}) collective-permute-start(bf16[2,9,16,256]{3,2,1,0:T(8,128)(2,1)S(1)} %get-tuple-element.100), channel_id=1, source_target_pairs={{0,8},{4,12},{8,0},{12,4},{1,9},{5,13},{9,1},{13,5},{2,10},{6,14},... | collective-permute-start | bytes 442376 | tf_op jit(solution)/shard_map/ppermute | solution.py:430
  55.9 1.6 %collective-permute-start.20 = (bf16[2,9,16,256]{3,2,1,0:T(8,128)(2,1)S(1)}, bf16[2,9,16,256]{3,2,1,0:T(8,128)(2,1)S(1)}, u32[]{:S(2)}, u32[]{:S(2)}) collective-permute-start(bf16[2,9,16,256]{3,2,1,0:T(8,128)(2,1)S(1)} %get-tuple-element.101), channel_id=1, source_target_pairs={{0,12},{4,8},{8,4},{12,0},{1,13},{5,9},{9,5},{13,1},{2,14},{6,10},... | collective-permute-start | bytes 442376 | tf_op jit(solution)/shard_map/ppermute | solution.py:430
  57.5 7.5 %owner_canvas.1 = (f32[68,40,128]{2,1,0:T(8,128)S(1)}, bf16[48,256]{1,0:T(8,128)(2,1)S(1)}, bf16[48,256]{1,0:T(8,128)(2,1)S(1)}) custom-call(s32[4,16]{1,0:T(4,128)S(1)} %bitcast.22, bf16[10,80,128]{2,1,0:T(8,128)(2,1)S(1)} %get-tuple-element.92.refs_0_, bf16[10,80,128]{2,1,0:T(8,128)(2,1)S(1)} %collective-permute-done.9.refs_1_, ...), custom_call_target="tpu_custom_call" | custom-call | flops 1 | bytes 1 | tf_op jit(solution)/shard_map/owner_canvas/pallas_call | solution.py:524
  65.0 2.5 %collective-permute-done.19.got_2 = bf16[2,9,16,256]{3,2,1,0:T(8,128)(2,1)S(1)} collective-permute-done((bf16[2,9,16,256]{3,2,1,0:T(8,128)(2,1)S(1)}, bf16[2,9,16,256]{3,2,1,0:T(8,128)(2,1)S(1)}, u32[]{:S(2)}, u32[]{:S(2)}) %collective-permute-start.19) | collective-permute-done | bytes 147488 | tf_op jit(solution)/shard_map/ppermute | solution.py:430
  67.6 3.0 %collective-permute-start.21 = (bf16[336,256]{1,0:T(8,128)(2,1)S(1)}, bf16[336,256]{1,0:T(8,128)(2,1)S(1)}, u32[]{:S(2)}, u32[]{:S(2)}) collective-permute-start(bf16[336,256]{1,0:T(8,128)(2,1)S(1)} %get-tuple-element.104), channel_id=1, source_target_pairs={{0,4},{4,0},{8,12},{12,8},{1,5},{5,1},{9,13},{13,9},{2,6},{6,2},{1... | collective-permute-start | bytes 516104 | tf_op jit(solution)/shard_map/ppermute | solution.py:430
  70.5 2.1 %collective-permute-start.22 = (bf16[336,256]{1,0:T(8,128)(2,1)S(1)}, bf16[336,256]{1,0:T(8,128)(2,1)S(1)}, u32[]{:S(2)}, u32[]{:S(2)}) collective-permute-start(bf16[336,256]{1,0:T(8,128)(2,1)S(1)} %get-tuple-element.105), channel_id=1, source_target_pairs={{0,12},{4,8},{8,4},{12,0},{1,13},{5,9},{9,5},{13,1},{2,14},{6,10},... | collective-permute-start | bytes 516104 | tf_op jit(solution)/shard_map/ppermute | solution.py:430
  72.7 2.7 %collective-permute-done.21.got_1.refs_1_ = bf16[336,256]{1,0:T(8,128)(2,1)S(1)} collective-permute-done((bf16[336,256]{1,0:T(8,128)(2,1)S(1)}, bf16[336,256]{1,0:T(8,128)(2,1)S(1)}, u32[]{:S(2)}, u32[]{:S(2)}) %collective-permute-start.21) | collective-permute-done | bytes 172064 | tf_op jit(solution)/shard_map/ppermute | solution.py:430
  75.4 6.2 %collective-permute-done.22.got_3.refs_3_ = bf16[336,256]{1,0:T(8,128)(2,1)S(1)} collective-permute-done((bf16[336,256]{1,0:T(8,128)(2,1)S(1)}, bf16[336,256]{1,0:T(8,128)(2,1)S(1)}, u32[]{:S(2)}, u32[]{:S(2)}) %collective-permute-start.22) | collective-permute-done | bytes 172064 | tf_op jit(solution)/shard_map/ppermute | solution.py:430
  83.7 2.0 %collective-permute-done.24.refs_2_ = bf16[288,256]{1,0:T(8,128)(2,1)S(1)} collective-permute-done((bf16[288,256]{1,0:T(8,128)(2,1)S(1)}, bf16[288,256]{1,0:T(8,128)(2,1)S(1)}, u32[]{:S(2)}, u32[]{:S(2)}) %collective-permute-start.24) | collective-permute-done | bytes 147488 | tf_op jit(solution)/shard_map/ppermute | solution.py:430
  86.2 1.5 %collective-permute-start.26 = (bf16[288,256]{1,0:T(8,128)(2,1)S(1)}, bf16[288,256]{1,0:T(8,128)(2,1)S(1)}, u32[]{:S(2)}, u32[]{:S(2)}) collective-permute-start(bf16[288,256]{1,0:T(8,128)(2,1)S(1)} %slice.4), channel_id=1, source_target_pairs={{0,2},{2,0},{1,3},{3,1},{4,6},{6,4},{5,7},{7,5},{8,10},{10,8},{9,1... | collective-permute-start | bytes 442376 | tf_op jit(solution)/shard_map/ppermute | solution.py:425
  90.0 3.2 %collective-permute-done.27.refs_6_ = bf16[288,256]{1,0:T(8,128)(2,1)S(1)} collective-permute-done((bf16[288,256]{1,0:T(8,128)(2,1)S(1)}, bf16[288,256]{1,0:T(8,128)(2,1)S(1)}, u32[]{:S(2)}, u32[]{:S(2)}) %collective-permute-start.27) | collective-permute-done | bytes 147488 | tf_op jit(solution)/shard_map/ppermute | solution.py:425
  93.2 1.8 %collective-permute-done.26.refs_5_ = bf16[288,256]{1,0:T(8,128)(2,1)S(1)} collective-permute-done((bf16[288,256]{1,0:T(8,128)(2,1)S(1)}, bf16[288,256]{1,0:T(8,128)(2,1)S(1)}, u32[]{:S(2)}, u32[]{:S(2)}) %collective-permute-start.26) | collective-permute-done | bytes 147488 | tf_op jit(solution)/shard_map/ppermute | solution.py:425
  95.1 1.6 %lay.1 = (f32[9,128,256]{2,1,0:T(8,128)}, f32[9,128,256]{2,1,0:T(8,128)}) custom-call(bf16[288,256]{1,0:T(8,128)(2,1)S(1)} %get-tuple-element.106.refs_0_, bf16[336,256]{1,0:T(8,128)(2,1)S(1)} %collective-permute-done.21.got_1.refs_1_, bf16[288,256]{1,0:T(8,128)(2,1)S(1)} %collective-permute-done.24.refs_2_, ...), custom_call_target="tpu_custom_call" | custom-call | flops 1 | bytes 1 | tf_op jit(solution)/shard_map/lay/pallas_call | solution.py:563
  (59 shorter events, 17.1 us)
Async XLA Ops:
  0.6 25.2 %collective-permute-start.8 = (bf16[9,128,256]{2,1,0:T(8,128)(2,1)}, bf16[9,128,256]{2,1,0:T(8,128)(2,1)S(1)}, u32[]{:S(2)}, u32[]{:S(2)}) collective-permute-start(bf16[9,128,256]{2,1,0:T(8,128)(2,1)} %second.1), channel_id=1, source_target_pairs={{0,1},{1,0},{2,3},{3,2},{4,5},{5,4},{6,7},{7,6},{8,9},{9,8},{10,11... | collective-permute-start | bytes 1769480 | tf_op jit(solution)/shard_map/ppermute | solution.py:425
  4.5 9.1 %collective-permute-start = (bf16[8,64,128]{2,1,0:T(8,128)(2,1)S(1)}, bf16[8,64,128]{2,1,0:T(8,128)(2,1)S(1)}, u32[]{:S(2)}, u32[]{:S(2)}) collective-permute-start(bf16[8,64,128]{2,1,0:T(8,128)(2,1)S(1)} %get-tuple-element.61), channel_id=1, source_target_pairs={{0,4},{4,0},{8,12},{12,8},{1,5},{5,1},{9,13},{13,9},{2,6},{6,2},{1... | collective-permute-start | bytes 393224 | tf_op jit(solution)/shard_map/ppermute | solution.py:430
  7.1 12.9 %collective-permute-start.1 = (bf16[8,64,128]{2,1,0:T(8,128)(2,1)S(1)}, bf16[8,64,128]{2,1,0:T(8,128)(2,1)S(1)}, u32[]{:S(2)}, u32[]{:S(2)}) collective-permute-start(bf16[8,64,128]{2,1,0:T(8,128)(2,1)S(1)} %get-tuple-element.62), channel_id=1, source_target_pairs={{0,8},{4,12},{8,0},{12,4},{1,9},{5,13},{9,1},{13,5},{2,10},{6,14},... | collective-permute-start | bytes 393224 | tf_op jit(solution)/shard_map/ppermute | solution.py:430
  9.7 10.3 %collective-permute-start.2 = (bf16[8,64,128]{2,1,0:T(8,128)(2,1)S(1)}, bf16[8,64,128]{2,1,0:T(8,128)(2,1)S(1)}, u32[]{:S(2)}, u32[]{:S(2)}) collective-permute-start(bf16[8,64,128]{2,1,0:T(8,128)(2,1)S(1)} %get-tuple-element.63), channel_id=1, source_target_pairs={{0,12},{4,8},{8,4},{12,0},{1,13},{5,9},{9,5},{13,1},{2,14},{6,10},... | collective-permute-start | bytes 393224 | tf_op jit(solution)/shard_map/ppermute | solution.py:430
  20.0 5.8 %collective-permute-start.7 = (bf16[10,10,16,128]{3,2,1,0:T(8,128)(2,1)S(1)}, bf16[10,10,16,128]{3,2,1,0:T(8,128)(2,1)S(1)}, u32[]{:S(2)}, u32[]{:S(2)}) collective-permute-start(bf16[10,10,16,128]{3,2,1,0:T(8,128)(2,1)S(1)} %bitcast.16), channel_id=1, source_target_pairs={{0,1},{1,0},{2,3},{3,2},{4,5},{5,4},{6,7},{7,6},{8,9},{9,8},{10,11... | collective-permute-start | bytes 1228808 | tf_op jit(solution)/shard_map/ppermute | solution.py:425
  20.0 4.2 %collective-permute-start.3 = (bf16[8,64,128]{2,1,0:T(8,128)(2,1)S(1)}, bf16[8,64,128]{2,1,0:T(8,128)(2,1)S(1)}, u32[]{:S(2)}, u32[]{:S(2)}) collective-permute-start(bf16[8,64,128]{2,1,0:T(8,128)(2,1)S(1)} %get-tuple-element.70.refs_0_), channel_id=1, source_target_pairs={{0,1},{1,0},{2,3},{3,2},{4,5},{5,4},{6,7},{7,6},{8,9},{9,8},{10,11... | collective-permute-start | bytes 393224 | tf_op jit(solution)/shard_map/ppermute | solution.py:425
  20.5 3.9 %collective-permute-start.4 = (bf16[8,64,128]{2,1,0:T(8,128)(2,1)S(1)}, bf16[8,64,128]{2,1,0:T(8,128)(2,1)S(1)}, u32[]{:S(2)}, u32[]{:S(2)}) collective-permute-start(bf16[8,64,128]{2,1,0:T(8,128)(2,1)S(1)} %collective-permute-done.refs_1_), channel_id=1, source_target_pairs={{0,1},{1,0},{2,3},{3,2},{4,5},{5,4},{6,7},{7,6},{8,9},{9,8},{10,11... | collective-permute-start | bytes 393224 | tf_op jit(solution)/shard_map/ppermute | solution.py:425
  20.5 13.8 %collective-permute-start.10 = (bf16[10,80,128]{2,1,0:T(8,128)(2,1)S(1)}, bf16[10,80,128]{2,1,0:T(8,128)(2,1)S(1)}, u32[]{:S(2)}, u32[]{:S(2)}) collective-permute-start(bf16[10,80,128]{2,1,0:T(8,128)(2,1)S(1)} %get-tuple-element.79), channel_id=1, source_target_pairs={{0,8},{4,12},{8,0},{12,4},{1,9},{5,13},{9,1},{13,5},{2,10},{6,14},... | collective-permute-start | bytes 614408 | tf_op jit(solution)/shard_map/ppermute | solution.py:430
  34.3 17.5 %collective-permute-start.13 = (bf16[2,9,64,256]{3,2,1,0:T(8,128)(2,1)S(1)}, bf16[2,9,64,256]{3,2,1,0:T(8,128)(2,1)S(1)}, u32[]{:S(2)}, u32[]{:S(2)}) collective-permute-start(bf16[2,9,64,256]{3,2,1,0:T(8,128)(2,1)S(1)} %get-tuple-element.83), channel_id=1, source_target_pairs={{0,2},{2,0},{1,3},{3,1},{4,6},{6,4},{5,7},{7,5},{8,10},{10,8},{9,1... | collective-permute-start | bytes 1769480 | tf_op jit(solution)/shard_map/ppermute | solution.py:425
  35.8 13.1 %collective-permute-start.12 = (bf16[8,8,32,128]{3,2,1,0:T(8,128)(2,1)S(1)}, bf16[8,8,32,128]{3,2,1,0:T(8,128)(2,1)S(1)}, u32[]{:S(2)}, u32[]{:S(2)}) collective-permute-start(bf16[8,8,32,128]{3,2,1,0:T(8,128)(2,1)S(1)} %bitcast.13), channel_id=1, source_target_pairs={{0,1},{1,0},{2,3},{3,2},{4,5},{5,4},{6,7},{7,6},{8,9},{9,8},{10,11... | collective-permute-start | bytes 1572872 | tf_op jit(solution)/shard_map/ppermute | solution.py:425
  35.8 9.7 %collective-permute-start.11 = (bf16[10,80,128]{2,1,0:T(8,128)(2,1)S(1)}, bf16[10,80,128]{2,1,0:T(8,128)(2,1)S(1)}, u32[]{:S(2)}, u32[]{:S(2)}) collective-permute-start(bf16[10,80,128]{2,1,0:T(8,128)(2,1)S(1)} %get-tuple-element.81), channel_id=1, source_target_pairs={{0,12},{4,8},{8,4},{12,0},{1,13},{5,9},{9,5},{13,1},{2,14},{6,10},... | collective-permute-start | bytes 614408 | tf_op jit(solution)/shard_map/ppermute | solution.py:430
  37.3 11.6 %collective-permute-start.9 = (bf16[10,80,128]{2,1,0:T(8,128)(2,1)S(1)}, bf16[10,80,128]{2,1,0:T(8,128)(2,1)S(1)}, u32[]{:S(2)}, u32[]{:S(2)}) collective-permute-start(bf16[10,80,128]{2,1,0:T(8,128)(2,1)S(1)} %get-tuple-element.77), channel_id=1, source_target_pairs={{0,4},{4,0},{8,12},{12,8},{1,5},{5,1},{9,13},{13,9},{2,6},{6,2},{1... | collective-permute-start | bytes 614408 | tf_op jit(solution)/shard_map/ppermute | solution.py:430
  52.6 4.9 %collective-permute-start.16 = (bf16[10,80,128]{2,1,0:T(8,128)(2,1)S(1)}, bf16[10,80,128]{2,1,0:T(8,128)(2,1)S(1)}, u32[]{:S(2)}, u32[]{:S(2)}) collective-permute-start(bf16[10,80,128]{2,1,0:T(8,128)(2,1)S(1)} %collective-permute-done.10.refs_2_), channel_id=1, source_target_pairs={{0,1},{1,0},{2,3},{3,2},{4,5},{5,4},{6,7},{7,6},{8,9},{9,8},{10,11... | collective-permute-start | bytes 614408 | tf_op jit(solution)/shard_map/ppermute | solution.py:425
  52.7 4.8 %collective-permute-start.17 = (bf16[10,80,128]{2,1,0:T(8,128)(2,1)S(1)}, bf16[10,80,128]{2,1,0:T(8,128)(2,1)S(1)}, u32[]{:S(2)}, u32[]{:S(2)}) collective-permute-start(bf16[10,80,128]{2,1,0:T(8,128)(2,1)S(1)} %collective-permute-done.11.refs_3_), channel_id=1, source_target_pairs={{0,1},{1,0},{2,3},{3,2},{4,5},{5,4},{6,7},{7,6},{8,9},{9,8},{10,11... | collective-permute-start | bytes 614408 | tf_op jit(solution)/shard_map/ppermute | solution.py:425
  53.1 11.9 %collective-permute-start.18 = (bf16[2,9,16,256]{3,2,1,0:T(8,128)(2,1)S(1)}, bf16[2,9,16,256]{3,2,1,0:T(8,128)(2,1)S(1)}, u32[]{:S(2)}, u32[]{:S(2)}) collective-permute-start(bf16[2,9,16,256]{3,2,1,0:T(8,128)(2,1)S(1)} %get-tuple-element.99), channel_id=1, source_target_pairs={{0,4},{4,0},{8,12},{12,8},{1,5},{5,1},{9,13},{13,9},{2,6},{6,2},{1... | collective-permute-start | bytes 442376 | tf_op jit(solution)/shard_map/ppermute | solution.py:430
  53.5 14.0 %collective-permute-start.19 = (bf16[2,9,16,256]{3,2,1,0:T(8,128)(2,1)S(1)}, bf16[2,9,16,256]{3,2,1,0:T(8,128)(2,1)S(1)}, u32[]{:S(2)}, u32[]{:S(2)}) collective-permute-start(bf16[2,9,16,256]{3,2,1,0:T(8,128)(2,1)S(1)} %get-tuple-element.100), channel_id=1, source_target_pairs={{0,8},{4,12},{8,0},{12,4},{1,9},{5,13},{9,1},{13,5},{2,10},{6,14},... | collective-permute-start | bytes 442376 | tf_op jit(solution)/shard_map/ppermute | solution.py:430
  55.9 11.6 %collective-permute-start.20 = (bf16[2,9,16,256]{3,2,1,0:T(8,128)(2,1)S(1)}, bf16[2,9,16,256]{3,2,1,0:T(8,128)(2,1)S(1)}, u32[]{:S(2)}, u32[]{:S(2)}) collective-permute-start(bf16[2,9,16,256]{3,2,1,0:T(8,128)(2,1)S(1)} %get-tuple-element.101), channel_id=1, source_target_pairs={{0,12},{4,8},{8,4},{12,0},{1,13},{5,9},{9,5},{13,1},{2,14},{6,10},... | collective-permute-start | bytes 442376 | tf_op jit(solution)/shard_map/ppermute | solution.py:430
  67.6 7.8 %collective-permute-start.21 = (bf16[336,256]{1,0:T(8,128)(2,1)S(1)}, bf16[336,256]{1,0:T(8,128)(2,1)S(1)}, u32[]{:S(2)}, u32[]{:S(2)}) collective-permute-start(bf16[336,256]{1,0:T(8,128)(2,1)S(1)} %get-tuple-element.104), channel_id=1, source_target_pairs={{0,4},{4,0},{8,12},{12,8},{1,5},{5,1},{9,13},{13,9},{2,6},{6,2},{1... | collective-permute-start | bytes 516104 | tf_op jit(solution)/shard_map/ppermute | solution.py:430
  70.5 11.0 %collective-permute-start.22 = (bf16[336,256]{1,0:T(8,128)(2,1)S(1)}, bf16[336,256]{1,0:T(8,128)(2,1)S(1)}, u32[]{:S(2)}, u32[]{:S(2)}) collective-permute-start(bf16[336,256]{1,0:T(8,128)(2,1)S(1)} %get-tuple-element.105), channel_id=1, source_target_pairs={{0,12},{4,8},{8,4},{12,0},{1,13},{5,9},{9,5},{13,1},{2,14},{6,10},... | collective-permute-start | bytes 516104 | tf_op jit(solution)/shard_map/ppermute | solution.py:430
  72.7 13.0 %collective-permute-start.24 = (bf16[288,256]{1,0:T(8,128)(2,1)S(1)}, bf16[288,256]{1,0:T(8,128)(2,1)S(1)}, u32[]{:S(2)}, u32[]{:S(2)}) collective-permute-start(bf16[288,256]{1,0:T(8,128)(2,1)S(1)} %get-tuple-element.106.refs_0_), channel_id=1, source_target_pairs={{0,8},{4,12},{8,0},{12,4},{1,9},{5,13},{9,1},{13,5},{2,10},{6,14},... | collective-permute-start | bytes 442376 | tf_op jit(solution)/shard_map/ppermute | solution.py:430
  81.6 6.2 %collective-permute-start.23 = (bf16[352,256]{1,0:T(8,128)(2,1)S(1)}, bf16[352,256]{1,0:T(8,128)(2,1)S(1)}, u32[]{:S(2)}, u32[]{:S(2)}) collective-permute-start(bf16[352,256]{1,0:T(8,128)(2,1)S(1)} %column_message.1), channel_id=1, source_target_pairs={{0,2},{2,0},{1,3},{3,1},{4,6},{6,4},{5,7},{7,5},{8,10},{10,8},{9,1... | collective-permute-start | bytes 540680 | tf_op jit(solution)/shard_map/ppermute | solution.py:425
  82.2 7.9 %collective-permute-start.25 = (bf16[288,256]{1,0:T(8,128)(2,1)S(1)}, bf16[288,256]{1,0:T(8,128)(2,1)S(1)}, u32[]{:S(2)}, u32[]{:S(2)}) collective-permute-start(bf16[288,256]{1,0:T(8,128)(2,1)S(1)} %get-tuple-element.106.refs_0_), channel_id=1, source_target_pairs={{0,2},{2,0},{1,3},{3,1},{4,6},{6,4},{5,7},{7,5},{8,10},{10,8},{9,1... | collective-permute-start | bytes 442376 | tf_op jit(solution)/shard_map/ppermute | solution.py:425
  85.7 7.6 %collective-permute-start.27 = (bf16[288,256]{1,0:T(8,128)(2,1)S(1)}, bf16[288,256]{1,0:T(8,128)(2,1)S(1)}, u32[]{:S(2)}, u32[]{:S(2)}) collective-permute-start(bf16[288,256]{1,0:T(8,128)(2,1)S(1)} %collective-permute-done.24.refs_2_), channel_id=1, source_target_pairs={{0,2},{2,0},{1,3},{3,1},{4,6},{6,4},{5,7},{7,5},{8,10},{10,8},{9,1... | collective-permute-start | bytes 442376 | tf_op jit(solution)/shard_map/ppermute | solution.py:425
  86.2 8.8 %collective-permute-start.26 = (bf16[288,256]{1,0:T(8,128)(2,1)S(1)}, bf16[288,256]{1,0:T(8,128)(2,1)S(1)}, u32[]{:S(2)}, u32[]{:S(2)}) collective-permute-start(bf16[288,256]{1,0:T(8,128)(2,1)S(1)} %slice.4), channel_id=1, source_target_pairs={{0,2},{2,0},{1,3},{3,1},{4,6},{6,4},{5,7},{7,5},{8,10},{10,8},{9,1... | collective-permute-start | bytes 442376 | tf_op jit(solution)/shard_map/ppermute | solution.py:425
  (12 other events, 55.0 us)

commit v6 on v5

--- a/solution.py
+++ b/solution.py
@@ -28,6 +28,7 @@
 I32 = jnp.int32
 
 VMEM = pl.BlockSpec(memory_space=pltpu.VMEM)
+HBM = pl.BlockSpec(memory_space=pltpu.HBM)
 SMEM = pl.BlockSpec(memory_space=pltpu.SMEM)
 
 
@@ -111,8 +112,10 @@
     return step ^ lax.axis_index(axis) if permuted else step
 
 
-def pack_cotangents(owners, capacity, permuted, routing, tile, *refs):
-    outs, table = refs[:-1], refs[-1]
+def pack_cotangents(owners, capacity, permuted, routing, source, *refs):
+    outs, (table, tile, arrived) = refs[:-3], refs[-3:]
+    fetch = pltpu.make_async_copy(source, tile, arrived)
+    fetch.start()
     owner_table(routing, table, owners, capacity)
     rows = BLOCK * capacity
     row, lane = iota((rows, FULL), 0), iota((rows, FULL), 1)
@@ -125,6 +128,7 @@
             target = jnp.where(row % capacity == rank, place, target)
         picks.append(one_hot(lane == target + row // capacity))
     pick = jnp.concatenate(picks, axis=0)
+    fetch.wait()
     for u in range(0, BLOCK, 2):
         pair = [
             jnp.concatenate([tile[r, u + k] for r in range(TILE_ROWS)], axis=0) for k in range(2)
@@ -281,10 +285,13 @@
 def worker(scale, owners, capacity, permuted, routing, *refs):
     parts = 1 if not permuted else owners
     inputs, refs = refs[: 2 * parts], refs[2 * parts :]
-    (masked, masked_other, weight, weight_other, saved), refs = refs[:5], refs[5:]
-    outs, (counts, cot, total, pre, full) = refs[:-5], refs[-5:]
+    (masked, masked_other, weight, weight_other, source), refs = refs[:5], refs[5:]
+    outs, (counts, cot, total, pre, full, saved, arrived) = refs[:-7], refs[-7:]
+    fetch = pltpu.make_async_copy(source, saved, arrived)
+    fetch.start()
     pairs = [[out.at[k] for out in outs] for k in range(2)]
     second_gradient(scale, owners, capacity, permuted, routing, *inputs, masked, cot, *pairs[0], counts)
+    fetch.wait()
     first_gradient(
         scale, cot, masked, masked_other, weight, weight_other, saved, *pairs[1], total, pre, full
     )
@@ -362,7 +369,7 @@
         out[...] = part if step == 0 else part.astype(BF16)
 
 
-def add_workers(kept, got_1, got_2, got_3, rim_1, rim_3, out, out_1, out_3):
+def add_workers(kept, got_3, got_2, got_1, rim_1, rim_3, out, out_1, out_3):
     value = kept[...]
     for part in (got_1, got_2, got_3):
         value = value + part[...].astype(F32)
@@ -454,7 +461,7 @@
 
     def exchange(values):
         if permuted:
-            return [values[0]] + [flip(values[k], "blk", k) for k in (1, 2, 3)]
+            return list(values[:1]) + [flip(values[k], "blk", k) for k in (3, 2, 1)][::-1]
         return [lax.all_to_all(values[0], "blk", split_axis=0, concat_axis=0, tiled=True)]
 
     tie = lax.optimization_barrier
@@ -463,8 +470,9 @@
     outgoing = call(
         functools.partial(pack_cotangents, owners, capacity, permuted),
         pieces(BLOCK, BLOCK * capacity, HALF),
-        [SMEM, VMEM], tables, (1, 1), "pack_cotangents",
-    )(routing, tile)
+        [SMEM, HBM], tables + [pltpu.VMEM(tile.shape, BF16), pltpu.SemaphoreType.DMA],
+        (1, 1), "pack_cotangents",
+    )(routing, pltpu.with_memory_space_constraint(tile, pltpu.HBM))
     saved_slots = saved_pre[0, 0].transpose(1, 2, 0, 3)
     outgoing, saved_slots = tie((outgoing, saved_slots))
     incoming = exchange(outgoing)
@@ -475,7 +483,8 @@
         [SMEM, VMEM], counts + tables, (1, 1), "pack_saved",
     )(routing, saved_slots.reshape(MIDDLE, MIDDLE * PER_WORKER, HALF))
     masked = masked.reshape(MIDDLE, MIDDLE, PER_WORKER, HALF)
-    incoming, to_owners, masked = tie((incoming, to_owners, masked))
+    incoming, to_owners, masked = tie((incoming[::-1], to_owners[::-1], masked))
+    incoming, to_owners = incoming[::-1], to_owners[::-1]
     incoming_other = [swap(value) for value in incoming]
     masked_other = swap(masked)
     at_owner = exchange(to_owners)
@@ -489,24 +498,26 @@
     terms = call(
         functools.partial(worker, scale, owners, capacity, permuted),
         halved,
-        [SMEM] + [VMEM] * (2 * parts + 5),
+        [SMEM] + [VMEM] * (2 * parts + 4) + [HBM],
         counts
         + [
             pltpu.VMEM((BLOCK, BLOCK * PER_WORKER, FULL), BF16),
             pltpu.VMEM((MIDDLE, MIDDLE, PER_WORKER, FULL), F32),
             pltpu.VMEM((MIDDLE, MIDDLE, PER_WORKER, FULL), BF16),
             pltpu.VMEM((9, FULL, FULL), BF16),
+            pltpu.VMEM(saved_tiles.shape, BF16),
+            pltpu.SemaphoreType.DMA,
         ],
         (1, 1), "worker",
     )(
         routing, *incoming, *incoming_other, masked, masked_other, second_weight, second_other,
-        saved_tiles,
+        pltpu.with_memory_space_constraint(saved_tiles, pltpu.HBM),
     )
 
     if permuted:
         terms = list(terms)
         terms[1], at_owner[2] = tie((terms[1], at_owner[2]))
-    at_owner, tile_here = tie((at_owner, tile))
+    terms, tile_here = tie((terms, tile))
     total = call(
         owner_spread,
         shape((MIDDLE, MIDDLE, TILE_BLOCKS, FULL), BF16),
@@ -536,26 +547,29 @@
     if permuted:
         part = (2, 9, HALF // 2 // owners, FULL)
         got = swap(terms[1], "col")
-        total, got = tie((total, got))
+        total, got, at_owner = tie((total, got, at_owner))
         kept, *sends = call(
             add_columns, [shape(part, F32)] + [shape(part, BF16)] * (owners - 1),
             [VMEM] * 2, [], (1, 1), "add_columns",
         )(terms[0], got)
         sends, at_owner = tie((sends, at_owner))
-        got = [flip(value, "blk", k + 1) for k, value in enumerate(sends)]
+        got = [flip(sends[k - 1], "blk", k) for k in (3, 2, 1)]
         canvas, *rims = owner(at_owner)
         message = shape((PART, FULL), BF16)
         wider = shape((PART + RIM, FULL), BF16)
         own, *wides = call(
             add_workers, [message, wider, wider], [VMEM] * 6, [], (1, 1), "add_workers",
         )(kept, *got, *rims)
-        got = [flip(value, "blk", k) for k, value in ((1, wides[0]), (2, own), (3, wides[1]))]
+        got = [flip(value, "blk", k) for k, value in ((3, wides[1]), (2, own), (1, wides[0]))][::-1]
+        across = [swap(own, "col"), swap(got[0][:PART], "col")]
+        got, across = tie((got[::-1], across))
+        got = got[::-1]
         last = call(
             column_message, shape((PART + 64, FULL), BF16), [VMEM] * 3,
             [pltpu.VMEM((RIM, FULL), F32), pltpu.VMEM((64, HALF), F32)],
             (1, 1), "column_message",
         )(canvas.reshape(HIGH * WIDE, HALF), got[0], got[2])
-        across = [swap(value, "col") for value in (own, got[0][:PART], got[1], last)]
+        across += [swap(got[1], "col"), swap(last, "col")]
         grad_in = call(
             close, shape(grad_out.shape, BF16), [VMEM] * 5,
             [pltpu.VMEM((TILE_ROWS * BLOCK * 32, HALF), F32)], (1, 1), "close",

time: 96.9 us -> 92 us (0.949)
  starting transfers between devices: 28.1 us -> 22.9 us
  local copies, waits for them, and re-layouts: 3.81 us -> 1.72 us
  waiting for transfers between devices: 41.2 us -> 43 us
    ppermute x12, starting transfers between devices: 19.8 us -> 14.7 us  [flip(): return lax.ppermute(value, axis, [(i, i ^ step) for i in range(size)])]
    ppermute x16, waiting for transfers between devices: 7.34 us -> 10.2 us  [swap(): return lax.ppermute(value, axis, [(0, 1), (1, 0)])]
    unnamed x16 -> x12, local copies, waits for them, and re-layouts: 3.8 us -> 1.71 us
    ppermute x12, waiting for transfers between devices: 33.9 us -> 32.8 us  [flip(): return lax.ppermute(value, axis, [(i, i ^ step) for i in range(size)])]
  transfers between devices with their start and end apart: 28 -> 28, of which waited for: 15 -> 14; matrix products, arithmetic and copies ran while one was open for 0% -> 0% of each run, Pallas kernels for 22% -> 23%
where the time goes in v6:
time: 92 us; the launch traced here: 91.8 us
  waiting for transfers between devices  43 us (47%)
  Pallas kernels  23.3 us (25%)
  starting transfers between devices  22.9 us (25%)
  local copies, waits for them, and re-layouts  1.72 us (2%)
    ppermute x12, waiting for transfers between devices, flip(): return lax.ppermute(value, axis, [(i, i ^ step) for i in range(size)])  32.8 us
    ppermute x12, starting transfers between devices, flip(): return lax.ppermute(value, axis, [(i, i ^ step) for i in range(size)])  14.7 us
    ppermute x16, waiting for transfers between devices, swap(): return lax.ppermute(value, axis, [(0, 1), (1, 0)])  10.2 us
    ppermute x16, starting transfers between devices, swap(): return lax.ppermute(value, axis, [(0, 1), (1, 0)])  8.2 us
    pallas_call x1, Pallas kernels, owner(): call(functools.partial(owner_canvas, owners, capacity, wide, permuted), [...  7.47 us
    pallas_call x1, Pallas kernels, shards(): call(functools.partial(worker, scale, owners, capacity, permuted), halved...  6.52 us
    pallas_call x1, Pallas kernels, shards(): call(owner_spread, shape((MIDDLE, MIDDLE, TILE_BLOCKS, FULL), BF16), [VME...  2.93 us
    pallas_call x1, Pallas kernels, shards(): call(functools.partial(pack_cotangents, owners, capacity, permuted), piec...  1.92 us
  transfers between devices with their start and end apart: 28, of which 14 were waited for; matrix products, arithmetic and copies ran while one was open for 0% of the time, Pallas kernels for 23%

profile of v6, /device:TPU:0, one launch (start us, length us, event | category | flops | bytes accessed | tf_op | source)
XLA Modules:
  0.0 91.8 jit_solution(14463171733049658806)
XLA Ops:
  1.8 1.9 %pack_cotangents.1 = (bf16[8,64,128]{2,1,0:T(8,128)(2,1)S(1)}, bf16[8,64,128]{2,1,0:T(8,128)(2,1)S(1)}, bf16[8,64,128]{2,1,0:T(8,128)(2,1)S(1)}, bf16[8,64,128]{2,1,0:T(8,128)(2,1)S(1)}) custom-call(s32[4,16]{1,0:T(4,128)S(1)} %bitcast.18, bf16[8,8,32,128]{3,2,1,0:T(8,128)(2,1)} %bitcast.12), custom_call_target="tpu_custom_call" | custom-call | flops 1 | bytes 1 | tf_op jit(solution)/shard_map/pack_cotangents/pallas_call | solution.py:470
  3.8 4.7 %collective-permute-start = (bf16[8,64,128]{2,1,0:T(8,128)(2,1)S(1)}, bf16[8,64,128]{2,1,0:T(8,128)(2,1)S(1)}, u32[]{:S(2)}, u32[]{:S(2)}) collective-permute-start(bf16[8,64,128]{2,1,0:T(8,128)(2,1)S(1)} %get-tuple-element.67), channel_id=1, source_target_pairs={{0,12},{4,8},{8,4},{12,0},{1,13},{5,9},{9,5},{13,1},{2,14},{6,10},... | collective-permute-start | bytes 393224 | tf_op jit(solution)/shard_map/ppermute | solution.py:437
  10.1 1.6 %pack_saved.1 = (bf16[10,160,128]{2,1,0:T(8,128)(2,1)S(1)}, bf16[10,80,128]{2,1,0:T(8,128)(2,1)S(1)}, bf16[10,80,128]{2,1,0:T(8,128)(2,1)S(1)}, bf16[10,80,128]{2,1,0:T(8,128)(2,1)S(1)}, bf16[10,80,128]{2,1,0:T(8,128)(2,1)S(1)}) custom-call(s32[4,16]{1,0:T(4,128)S(1)} %bitcast.19, bf16[10,160,128]{2,1,0:T(8,128)(2,1)S(1)} %bitcast.17), custom_call_target="tpu_custom_call" | custom-call | flops 1 | bytes 1 | tf_op jit(solution)/shard_map/pack_saved/pallas_call | solution.py:480
  11.7 1.2 %collective-permute-done.refs_3_ = bf16[8,64,128]{2,1,0:T(8,128)(2,1)S(1)} collective-permute-done((bf16[8,64,128]{2,1,0:T(8,128)(2,1)S(1)}, bf16[8,64,128]{2,1,0:T(8,128)(2,1)S(1)}, u32[]{:S(2)}, u32[]{:S(2)}) %collective-permute-start) | collective-permute-done | bytes 131104 | tf_op jit(solution)/shard_map/ppermute | solution.py:437
  12.9 7.2 %collective-permute-done.1.refs_2_ = bf16[8,64,128]{2,1,0:T(8,128)(2,1)S(1)} collective-permute-done((bf16[8,64,128]{2,1,0:T(8,128)(2,1)S(1)}, bf16[8,64,128]{2,1,0:T(8,128)(2,1)S(1)}, u32[]{:S(2)}, u32[]{:S(2)}) %collective-permute-start.1) | collective-permute-done | bytes 131104 | tf_op jit(solution)/shard_map/ppermute | solution.py:437
  20.7 1.4 %collective-permute-done.3.refs_4_ = bf16[8,64,128]{2,1,0:T(8,128)(2,1)S(1)} collective-permute-done((bf16[8,64,128]{2,1,0:T(8,128)(2,1)S(1)}, bf16[8,64,128]{2,1,0:T(8,128)(2,1)S(1)}, u32[]{:S(2)}, u32[]{:S(2)}) %collective-permute-start.3) | collective-permute-done | bytes 131104 | tf_op jit(solution)/shard_map/ppermute | solution.py:432
  23.7 6.5 %worker.1 = (f32[2,9,64,256]{3,2,1,0:T(8,128)S(1)}, bf16[2,9,64,256]{3,2,1,0:T(8,128)(2,1)S(1)}) custom-call(s32[4,16]{1,0:T(4,128)S(1)} %bitcast.20, bf16[8,64,128]{2,1,0:T(8,128)(2,1)S(1)} %get-tuple-element.77.refs_0_, bf16[8,64,128]{2,1,0:T(8,128)(2,1)S(1)} %collective-permute-done.2.refs_1_, bf16[8,64,128]{2,1,0:T(8,128)(2,1)S(1)} %collective-permute-done.1.refs_2_, ...), custom_call_target="tpu_custom_call" | custom-call | flops 1 | bytes 1 | tf_op jit(solution)/shard_map/worker/pallas_call | solution.py:498
  30.2 3.1 %collective-permute-done.9.refs_2_ = bf16[10,80,128]{2,1,0:T(8,128)(2,1)S(1)} collective-permute-done((bf16[10,80,128]{2,1,0:T(8,128)(2,1)S(1)}, bf16[10,80,128]{2,1,0:T(8,128)(2,1)S(1)}, u32[]{:S(2)}, u32[]{:S(2)}) %collective-permute-start.9) | collective-permute-done | bytes 204832 | tf_op jit(solution)/shard_map/ppermute | solution.py:437
  33.3 1.5 %collective-permute-start.11 = (bf16[2,9,64,256]{3,2,1,0:T(8,128)(2,1)S(1)}, bf16[2,9,64,256]{3,2,1,0:T(8,128)(2,1)S(1)}, u32[]{:S(2)}, u32[]{:S(2)}) collective-permute-start(bf16[2,9,64,256]{3,2,1,0:T(8,128)(2,1)S(1)} %get-tuple-element.88), channel_id=1, source_target_pairs={{0,2},{2,0},{1,3},{3,1},{4,6},{6,4},{5,7},{7,5},{8,10},{10,8},{9,1... | collective-permute-start | bytes 1769480 | tf_op jit(solution)/shard_map/ppermute | solution.py:432
  34.8 1.4 %collective-permute-start.13 = (bf16[10,80,128]{2,1,0:T(8,128)(2,1)S(1)}, bf16[10,80,128]{2,1,0:T(8,128)(2,1)S(1)}, u32[]{:S(2)}, u32[]{:S(2)}) collective-permute-start(bf16[10,80,128]{2,1,0:T(8,128)(2,1)S(1)} %get-tuple-element.92), channel_id=1, source_target_pairs={{0,12},{4,8},{8,4},{12,0},{1,13},{5,9},{9,5},{13,1},{2,14},{6,10},... | collective-permute-start | bytes 614408 | tf_op jit(solution)/shard_map/ppermute | solution.py:437
  36.7 2.9 %owner_spread.1.refs_8_ = bf16[10,10,32,256]{3,2,1,0:T(8,128)(2,1)S(1)} custom-call(bf16[8,8,32,128]{3,2,1,0:T(8,128)(2,1)S(1)} %bitcast.14, bf16[8,8,32,128]{3,2,1,0:T(8,128)(2,1)S(1)} %collective-permute-done.10.tile_other, bf16[9,128,256]{2,1,0:T(8,128)(2,1)S(1)} %copy-done.1, bf16[9,128,256]{2,1,0:T(8,128)(2,1)S(1)} %collective-permute-done.8.refs_11_.second_other), custom_call_target="tpu_custom_call" | custom-call | flops 1 | bytes 1 | tf_op jit(solution)/shard_map/owner_spread/pallas_call | solution.py:521
  39.7 7.0 %collective-permute-done.12.refs_1_ = bf16[10,80,128]{2,1,0:T(8,128)(2,1)S(1)} collective-permute-done((bf16[10,80,128]{2,1,0:T(8,128)(2,1)S(1)}, bf16[10,80,128]{2,1,0:T(8,128)(2,1)S(1)}, u32[]{:S(2)}, u32[]{:S(2)}) %collective-permute-start.12) | collective-permute-done | bytes 204832 | tf_op jit(solution)/shard_map/ppermute | solution.py:437
  46.7 1.9 %collective-permute-done.11.got = bf16[2,9,64,256]{3,2,1,0:T(8,128)(2,1)S(1)} collective-permute-done((bf16[2,9,64,256]{3,2,1,0:T(8,128)(2,1)S(1)}, bf16[2,9,64,256]{3,2,1,0:T(8,128)(2,1)S(1)}, u32[]{:S(2)}, u32[]{:S(2)}) %collective-permute-start.11) | collective-permute-done | bytes 589856 | tf_op jit(solution)/shard_map/ppermute | solution.py:432
  49.8 1.3 %collective-permute-start.18 = (bf16[2,9,16,256]{3,2,1,0:T(8,128)(2,1)S(1)}, bf16[2,9,16,256]{3,2,1,0:T(8,128)(2,1)S(1)}, u32[]{:S(2)}, u32[]{:S(2)}) collective-permute-start(bf16[2,9,16,256]{3,2,1,0:T(8,128)(2,1)S(1)} %get-tuple-element.108), channel_id=1, source_target_pairs={{0,12},{4,8},{8,4},{12,0},{1,13},{5,9},{9,5},{13,1},{2,14},{6,10},... | collective-permute-start | bytes 442376 | tf_op jit(solution)/shard_map/ppermute | solution.py:437
  51.2 3.0 %collective-permute-start.20 = (bf16[2,9,16,256]{3,2,1,0:T(8,128)(2,1)S(1)}, bf16[2,9,16,256]{3,2,1,0:T(8,128)(2,1)S(1)}, u32[]{:S(2)}, u32[]{:S(2)}) collective-permute-start(bf16[2,9,16,256]{3,2,1,0:T(8,128)(2,1)S(1)} %get-tuple-element.110), channel_id=1, source_target_pairs={{0,4},{4,0},{8,12},{12,8},{1,5},{5,1},{9,13},{13,9},{2,6},{6,2},{1... | collective-permute-start | bytes 442376 | tf_op jit(solution)/shard_map/ppermute | solution.py:437
  54.2 7.5 %owner_canvas.1 = (f32[68,40,128]{2,1,0:T(8,128)S(1)}, bf16[48,256]{1,0:T(8,128)(2,1)S(1)}, bf16[48,256]{1,0:T(8,128)(2,1)S(1)}) custom-call(s32[4,16]{1,0:T(4,128)S(1)} %bitcast.21, bf16[10,80,128]{2,1,0:T(8,128)(2,1)S(1)} %get-tuple-element.101.refs_0_, bf16[10,80,128]{2,1,0:T(8,128)(2,1)S(1)} %collective-permute-done.12.refs_1_, ...), custom_call_target="tpu_custom_call" | custom-call | flops 1 | bytes 1 | tf_op jit(solution)/shard_map/owner_canvas/pallas_call | solution.py:535
  61.7 2.7 %collective-permute-done.19.got_2 = bf16[2,9,16,256]{3,2,1,0:T(8,128)(2,1)S(1)} collective-permute-done((bf16[2,9,16,256]{3,2,1,0:T(8,128)(2,1)S(1)}, bf16[2,9,16,256]{3,2,1,0:T(8,128)(2,1)S(1)}, u32[]{:S(2)}, u32[]{:S(2)}) %collective-permute-start.19) | collective-permute-done | bytes 147488 | tf_op jit(solution)/shard_map/ppermute | solution.py:437
  64.6 1.5 %collective-permute-start.21 = (bf16[336,256]{1,0:T(8,128)(2,1)S(1)}, bf16[336,256]{1,0:T(8,128)(2,1)S(1)}, u32[]{:S(2)}, u32[]{:S(2)}) collective-permute-start(bf16[336,256]{1,0:T(8,128)(2,1)S(1)} %get-tuple-element.113), channel_id=1, source_target_pairs={{0,12},{4,8},{8,4},{12,0},{1,13},{5,9},{9,5},{13,1},{2,14},{6,10},... | collective-permute-start | bytes 516104 | tf_op jit(solution)/shard_map/ppermute | solution.py:437
  66.0 2.0 %collective-permute-start.22 = (bf16[288,256]{1,0:T(8,128)(2,1)S(1)}, bf16[288,256]{1,0:T(8,128)(2,1)S(1)}, u32[]{:S(2)}, u32[]{:S(2)}) collective-permute-start(bf16[288,256]{1,0:T(8,128)(2,1)S(1)} %get-tuple-element.114.refs_0_), channel_id=1, source_target_pairs={{0,8},{4,12},{8,0},{12,4},{1,9},{5,13},{9,1},{13,5},{2,10},{6,14},... | collective-permute-start | bytes 442376 | tf_op jit(solution)/shard_map/ppermute | solution.py:437
  69.0 4.3 %collective-permute-done.23.got_1.refs_1_ = bf16[336,256]{1,0:T(8,128)(2,1)S(1)} collective-permute-done((bf16[336,256]{1,0:T(8,128)(2,1)S(1)}, bf16[336,256]{1,0:T(8,128)(2,1)S(1)}, u32[]{:S(2)}, u32[]{:S(2)}) %collective-permute-start.23) | collective-permute-done | bytes 172064 | tf_op jit(solution)/shard_map/ppermute | solution.py:437
  74.4 7.3 %collective-permute-done.22.refs_2_ = bf16[288,256]{1,0:T(8,128)(2,1)S(1)} collective-permute-done((bf16[288,256]{1,0:T(8,128)(2,1)S(1)}, bf16[288,256]{1,0:T(8,128)(2,1)S(1)}, u32[]{:S(2)}, u32[]{:S(2)}) %collective-permute-start.22) | collective-permute-done | bytes 147488 | tf_op jit(solution)/shard_map/ppermute | solution.py:437
  81.7 1.3 %collective-permute-start.26 = (bf16[352,256]{1,0:T(8,128)(2,1)S(1)}, bf16[352,256]{1,0:T(8,128)(2,1)S(1)}, u32[]{:S(2)}, u32[]{:S(2)}) collective-permute-start(bf16[352,256]{1,0:T(8,128)(2,1)S(1)} %column_message.1), channel_id=1, source_target_pairs={{0,2},{2,0},{1,3},{3,1},{4,6},{6,4},{5,7},{7,5},{8,10},{10,8},{9,1... | collective-permute-start | bytes 540680 | tf_op jit(solution)/shard_map/ppermute | solution.py:432
  83.8 4.8 %collective-permute-done.26.across.refs_7_ = bf16[352,256]{1,0:T(8,128)(2,1)S(1)} collective-permute-done((bf16[352,256]{1,0:T(8,128)(2,1)S(1)}, bf16[352,256]{1,0:T(8,128)(2,1)S(1)}, u32[]{:S(2)}, u32[]{:S(2)}) %collective-permute-start.26) | collective-permute-done | bytes 180256 | tf_op jit(solution)/shard_map/ppermute | solution.py:432
  90.2 1.6 %lay.1 = (f32[9,128,256]{2,1,0:T(8,128)}, f32[9,128,256]{2,1,0:T(8,128)}) custom-call(bf16[288,256]{1,0:T(8,128)(2,1)S(1)} %get-tuple-element.114.refs_0_, bf16[336,256]{1,0:T(8,128)(2,1)S(1)} %collective-permute-done.23.got_1.refs_1_, bf16[288,256]{1,0:T(8,128)(2,1)S(1)} %collective-permute-done.22.refs_2_, ...), custom_call_target="tpu_custom_call" | custom-call | flops 1 | bytes 1 | tf_op jit(solution)/shard_map/lay/pallas_call | solution.py:577
  (55 shorter events, 11.2 us)
Async XLA Ops:
  0.6 23.0 %collective-permute-start.8 = (bf16[9,128,256]{2,1,0:T(8,128)(2,1)}, bf16[9,128,256]{2,1,0:T(8,128)(2,1)S(1)}, u32[]{:S(2)}, u32[]{:S(2)}) collective-permute-start(bf16[9,128,256]{2,1,0:T(8,128)(2,1)} %second.1), channel_id=1, source_target_pairs={{0,1},{1,0},{2,3},{3,2},{4,5},{5,4},{6,7},{7,6},{8,9},{9,8},{10,11... | collective-permute-start | bytes 1769480 | tf_op jit(solution)/shard_map/ppermute | solution.py:432
  3.8 9.2 %collective-permute-start = (bf16[8,64,128]{2,1,0:T(8,128)(2,1)S(1)}, bf16[8,64,128]{2,1,0:T(8,128)(2,1)S(1)}, u32[]{:S(2)}, u32[]{:S(2)}) collective-permute-start(bf16[8,64,128]{2,1,0:T(8,128)(2,1)S(1)} %get-tuple-element.67), channel_id=1, source_target_pairs={{0,12},{4,8},{8,4},{12,0},{1,13},{5,9},{9,5},{13,1},{2,14},{6,10},... | collective-permute-start | bytes 393224 | tf_op jit(solution)/shard_map/ppermute | solution.py:437
  8.5 11.7 %collective-permute-start.1 = (bf16[8,64,128]{2,1,0:T(8,128)(2,1)S(1)}, bf16[8,64,128]{2,1,0:T(8,128)(2,1)S(1)}, u32[]{:S(2)}, u32[]{:S(2)}) collective-permute-start(bf16[8,64,128]{2,1,0:T(8,128)(2,1)S(1)} %get-tuple-element.68), channel_id=1, source_target_pairs={{0,8},{4,12},{8,0},{12,4},{1,9},{5,13},{9,1},{13,5},{2,10},{6,14},... | collective-permute-start | bytes 393224 | tf_op jit(solution)/shard_map/ppermute | solution.py:437
  8.5 11.7 %collective-permute-start.2 = (bf16[8,64,128]{2,1,0:T(8,128)(2,1)S(1)}, bf16[8,64,128]{2,1,0:T(8,128)(2,1)S(1)}, u32[]{:S(2)}, u32[]{:S(2)}) collective-permute-start(bf16[8,64,128]{2,1,0:T(8,128)(2,1)S(1)} %get-tuple-element.69), channel_id=1, source_target_pairs={{0,4},{4,0},{8,12},{12,8},{1,5},{5,1},{9,13},{13,9},{2,6},{6,2},{1... | collective-permute-start | bytes 393224 | tf_op jit(solution)/shard_map/ppermute | solution.py:437
  20.2 3.5 %collective-permute-start.7 = (bf16[10,10,16,128]{3,2,1,0:T(8,128)(2,1)S(1)}, bf16[10,10,16,128]{3,2,1,0:T(8,128)(2,1)S(1)}, u32[]{:S(2)}, u32[]{:S(2)}) collective-permute-start(bf16[10,10,16,128]{3,2,1,0:T(8,128)(2,1)S(1)} %bitcast.15), channel_id=1, source_target_pairs={{0,1},{1,0},{2,3},{3,2},{4,5},{5,4},{6,7},{7,6},{8,9},{9,8},{10,11... | collective-permute-start | bytes 1228808 | tf_op jit(solution)/shard_map/ppermute | solution.py:432
  20.2 1.9 %collective-permute-start.3 = (bf16[8,64,128]{2,1,0:T(8,128)(2,1)S(1)}, bf16[8,64,128]{2,1,0:T(8,128)(2,1)S(1)}, u32[]{:S(2)}, u32[]{:S(2)}) collective-permute-start(bf16[8,64,128]{2,1,0:T(8,128)(2,1)S(1)} %get-tuple-element.77.refs_0_), channel_id=1, source_target_pairs={{0,1},{1,0},{2,3},{3,2},{4,5},{5,4},{6,7},{7,6},{8,9},{9,8},{10,11... | collective-permute-start | bytes 393224 | tf_op jit(solution)/shard_map/ppermute | solution.py:432
  20.7 12.6 %collective-permute-start.9 = (bf16[10,80,128]{2,1,0:T(8,128)(2,1)S(1)}, bf16[10,80,128]{2,1,0:T(8,128)(2,1)S(1)}, u32[]{:S(2)}, u32[]{:S(2)}) collective-permute-start(bf16[10,80,128]{2,1,0:T(8,128)(2,1)S(1)} %get-tuple-element.84), channel_id=1, source_target_pairs={{0,8},{4,12},{8,0},{12,4},{1,9},{5,13},{9,1},{13,5},{2,10},{6,14},... | collective-permute-start | bytes 614408 | tf_op jit(solution)/shard_map/ppermute | solution.py:437
  33.3 15.3 %collective-permute-start.11 = (bf16[2,9,64,256]{3,2,1,0:T(8,128)(2,1)S(1)}, bf16[2,9,64,256]{3,2,1,0:T(8,128)(2,1)S(1)}, u32[]{:S(2)}, u32[]{:S(2)}) collective-permute-start(bf16[2,9,64,256]{3,2,1,0:T(8,128)(2,1)S(1)} %get-tuple-element.88), channel_id=1, source_target_pairs={{0,2},{2,0},{1,3},{3,1},{4,6},{6,4},{5,7},{7,5},{8,10},{10,8},{9,1... | collective-permute-start | bytes 1769480 | tf_op jit(solution)/shard_map/ppermute | solution.py:432
  34.8 11.9 %collective-permute-start.12 = (bf16[10,80,128]{2,1,0:T(8,128)(2,1)S(1)}, bf16[10,80,128]{2,1,0:T(8,128)(2,1)S(1)}, u32[]{:S(2)}, u32[]{:S(2)}) collective-permute-start(bf16[10,80,128]{2,1,0:T(8,128)(2,1)S(1)} %get-tuple-element.90), channel_id=1, source_target_pairs={{0,4},{4,0},{8,12},{12,8},{1,5},{5,1},{9,13},{13,9},{2,6},{6,2},{1... | collective-permute-start | bytes 614408 | tf_op jit(solution)/shard_map/ppermute | solution.py:437
  34.8 11.9 %collective-permute-start.13 = (bf16[10,80,128]{2,1,0:T(8,128)(2,1)S(1)}, bf16[10,80,128]{2,1,0:T(8,128)(2,1)S(1)}, u32[]{:S(2)}, u32[]{:S(2)}) collective-permute-start(bf16[10,80,128]{2,1,0:T(8,128)(2,1)S(1)} %get-tuple-element.92), channel_id=1, source_target_pairs={{0,12},{4,8},{8,4},{12,0},{1,13},{5,9},{9,5},{13,1},{2,14},{6,10},... | collective-permute-start | bytes 614408 | tf_op jit(solution)/shard_map/ppermute | solution.py:437
  48.7 2.4 %collective-permute-start.14 = (bf16[10,80,128]{2,1,0:T(8,128)(2,1)S(1)}, bf16[10,80,128]{2,1,0:T(8,128)(2,1)S(1)}, u32[]{:S(2)}, u32[]{:S(2)}) collective-permute-start(bf16[10,80,128]{2,1,0:T(8,128)(2,1)S(1)} %get-tuple-element.101.refs_0_), channel_id=1, source_target_pairs={{0,1},{1,0},{2,3},{3,2},{4,5},{5,4},{6,7},{7,6},{8,9},{9,8},{10,11... | collective-permute-start | bytes 614408 | tf_op jit(solution)/shard_map/ppermute | solution.py:432
  48.8 2.4 %collective-permute-start.15 = (bf16[10,80,128]{2,1,0:T(8,128)(2,1)S(1)}, bf16[10,80,128]{2,1,0:T(8,128)(2,1)S(1)}, u32[]{:S(2)}, u32[]{:S(2)}) collective-permute-start(bf16[10,80,128]{2,1,0:T(8,128)(2,1)S(1)} %collective-permute-done.12.refs_1_), channel_id=1, source_target_pairs={{0,1},{1,0},{2,3},{3,2},{4,5},{5,4},{6,7},{7,6},{8,9},{9,8},{10,11... | collective-permute-start | bytes 614408 | tf_op jit(solution)/shard_map/ppermute | solution.py:432
  49.3 4.9 %collective-permute-start.16 = (bf16[10,80,128]{2,1,0:T(8,128)(2,1)S(1)}, bf16[10,80,128]{2,1,0:T(8,128)(2,1)S(1)}, u32[]{:S(2)}, u32[]{:S(2)}) collective-permute-start(bf16[10,80,128]{2,1,0:T(8,128)(2,1)S(1)} %collective-permute-done.9.refs_2_), channel_id=1, source_target_pairs={{0,1},{1,0},{2,3},{3,2},{4,5},{5,4},{6,7},{7,6},{8,9},{9,8},{10,11... | collective-permute-start | bytes 614408 | tf_op jit(solution)/shard_map/ppermute | solution.py:432
  49.4 4.8 %collective-permute-start.17 = (bf16[10,80,128]{2,1,0:T(8,128)(2,1)S(1)}, bf16[10,80,128]{2,1,0:T(8,128)(2,1)S(1)}, u32[]{:S(2)}, u32[]{:S(2)}) collective-permute-start(bf16[10,80,128]{2,1,0:T(8,128)(2,1)S(1)} %collective-permute-done.13.refs_3_), channel_id=1, source_target_pairs={{0,1},{1,0},{2,3},{3,2},{4,5},{5,4},{6,7},{7,6},{8,9},{9,8},{10,11... | collective-permute-start | bytes 614408 | tf_op jit(solution)/shard_map/ppermute | solution.py:432
  49.8 11.9 %collective-permute-start.18 = (bf16[2,9,16,256]{3,2,1,0:T(8,128)(2,1)S(1)}, bf16[2,9,16,256]{3,2,1,0:T(8,128)(2,1)S(1)}, u32[]{:S(2)}, u32[]{:S(2)}) collective-permute-start(bf16[2,9,16,256]{3,2,1,0:T(8,128)(2,1)S(1)} %get-tuple-element.108), channel_id=1, source_target_pairs={{0,12},{4,8},{8,4},{12,0},{1,13},{5,9},{9,5},{13,1},{2,14},{6,10},... | collective-permute-start | bytes 442376 | tf_op jit(solution)/shard_map/ppermute | solution.py:437
  51.2 13.2 %collective-permute-start.19 = (bf16[2,9,16,256]{3,2,1,0:T(8,128)(2,1)S(1)}, bf16[2,9,16,256]{3,2,1,0:T(8,128)(2,1)S(1)}, u32[]{:S(2)}, u32[]{:S(2)}) collective-permute-start(bf16[2,9,16,256]{3,2,1,0:T(8,128)(2,1)S(1)} %get-tuple-element.109), channel_id=1, source_target_pairs={{0,8},{4,12},{8,0},{12,4},{1,9},{5,13},{9,1},{13,5},{2,10},{6,14},... | collective-permute-start | bytes 442376 | tf_op jit(solution)/shard_map/ppermute | solution.py:437
  51.2 13.2 %collective-permute-start.20 = (bf16[2,9,16,256]{3,2,1,0:T(8,128)(2,1)S(1)}, bf16[2,9,16,256]{3,2,1,0:T(8,128)(2,1)S(1)}, u32[]{:S(2)}, u32[]{:S(2)}) collective-permute-start(bf16[2,9,16,256]{3,2,1,0:T(8,128)(2,1)S(1)} %get-tuple-element.110), channel_id=1, source_target_pairs={{0,4},{4,0},{8,12},{12,8},{1,5},{5,1},{9,13},{13,9},{2,6},{6,2},{1... | collective-permute-start | bytes 442376 | tf_op jit(solution)/shard_map/ppermute | solution.py:437
  64.5 8.8 %collective-permute-start.23 = (bf16[336,256]{1,0:T(8,128)(2,1)S(1)}, bf16[336,256]{1,0:T(8,128)(2,1)S(1)}, u32[]{:S(2)}, u32[]{:S(2)}) collective-permute-start(bf16[336,256]{1,0:T(8,128)(2,1)S(1)} %get-tuple-element.115), channel_id=1, source_target_pairs={{0,4},{4,0},{8,12},{12,8},{1,5},{5,1},{9,13},{13,9},{2,6},{6,2},{1... | collective-permute-start | bytes 516104 | tf_op jit(solution)/shard_map/ppermute | solution.py:437
  64.6 17.1 %collective-permute-start.21 = (bf16[336,256]{1,0:T(8,128)(2,1)S(1)}, bf16[336,256]{1,0:T(8,128)(2,1)S(1)}, u32[]{:S(2)}, u32[]{:S(2)}) collective-permute-start(bf16[336,256]{1,0:T(8,128)(2,1)S(1)} %get-tuple-element.113), channel_id=1, source_target_pairs={{0,12},{4,8},{8,4},{12,0},{1,13},{5,9},{9,5},{13,1},{2,14},{6,10},... | collective-permute-start | bytes 516104 | tf_op jit(solution)/shard_map/ppermute | solution.py:437
  66.0 15.6 %collective-permute-start.22 = (bf16[288,256]{1,0:T(8,128)(2,1)S(1)}, bf16[288,256]{1,0:T(8,128)(2,1)S(1)}, u32[]{:S(2)}, u32[]{:S(2)}) collective-permute-start(bf16[288,256]{1,0:T(8,128)(2,1)S(1)} %get-tuple-element.114.refs_0_), channel_id=1, source_target_pairs={{0,8},{4,12},{8,0},{12,4},{1,9},{5,13},{9,1},{13,5},{2,10},{6,14},... | collective-permute-start | bytes 442376 | tf_op jit(solution)/shard_map/ppermute | solution.py:437
  68.0 13.6 %collective-permute-start.24 = (bf16[288,256]{1,0:T(8,128)(2,1)S(1)}, bf16[288,256]{1,0:T(8,128)(2,1)S(1)}, u32[]{:S(2)}, u32[]{:S(2)}) collective-permute-start(bf16[288,256]{1,0:T(8,128)(2,1)S(1)} %get-tuple-element.114.refs_0_), channel_id=1, source_target_pairs={{0,2},{2,0},{1,3},{3,1},{4,6},{6,4},{5,7},{7,5},{8,10},{10,8},{9,1... | collective-permute-start | bytes 442376 | tf_op jit(solution)/shard_map/ppermute | solution.py:432
  73.3 8.4 %collective-permute-start.25 = (bf16[288,256]{1,0:T(8,128)(2,1)S(1)}, bf16[288,256]{1,0:T(8,128)(2,1)S(1)}, u32[]{:S(2)}, u32[]{:S(2)}) collective-permute-start(bf16[288,256]{1,0:T(8,128)(2,1)S(1)} %slice.4), channel_id=1, source_target_pairs={{0,2},{2,0},{1,3},{3,1},{4,6},{6,4},{5,7},{7,5},{8,10},{10,8},{9,1... | collective-permute-start | bytes 442376 | tf_op jit(solution)/shard_map/ppermute | solution.py:432
  81.7 6.9 %collective-permute-start.26 = (bf16[352,256]{1,0:T(8,128)(2,1)S(1)}, bf16[352,256]{1,0:T(8,128)(2,1)S(1)}, u32[]{:S(2)}, u32[]{:S(2)}) collective-permute-start(bf16[352,256]{1,0:T(8,128)(2,1)S(1)} %column_message.1), channel_id=1, source_target_pairs={{0,2},{2,0},{1,3},{3,1},{4,6},{6,4},{5,7},{7,5},{8,10},{10,8},{9,1... | collective-permute-start | bytes 540680 | tf_op jit(solution)/shard_map/ppermute | solution.py:432
  83.1 7.1 %collective-permute-start.27 = (bf16[288,256]{1,0:T(8,128)(2,1)S(1)}, bf16[288,256]{1,0:T(8,128)(2,1)S(1)}, u32[]{:S(2)}, u32[]{:S(2)}) collective-permute-start(bf16[288,256]{1,0:T(8,128)(2,1)S(1)} %collective-permute-done.22.refs_2_), channel_id=1, source_target_pairs={{0,2},{2,0},{1,3},{3,1},{4,6},{6,4},{5,7},{7,5},{8,10},{10,8},{9,1... | collective-permute-start | bytes 442376 | tf_op jit(solution)/shard_map/ppermute | solution.py:432
  (10 other events, 71.2 us)

commit v7 on v6

--- a/solution.py
+++ b/solution.py
@@ -20,6 +20,8 @@
 DEAD = -4096
 HIGH = 68
 RIM = 48
+FIRST = 4
+ROWS = 16
 PART = 288
 WIDE = 40
 
@@ -106,6 +108,14 @@
 
 def views(refs, count):
     return list(refs) if len(refs) == count else [refs[0].at[k] for k in range(count)]
+
+
+def rows_of(refs, count):
+    if len(refs) == count + 1:
+        return [[ref.at[m] for m in range(MIDDLE)] for ref in refs[:-2]] + [
+            [ref.at[m] for ref in refs[-2:] for m in range(ref.shape[0])]
+        ]
+    return [[ref.at[m] for m in range(MIDDLE)] for ref in views(refs, count)]
 
 
 def partner(axis, step, permuted):
@@ -187,10 +197,10 @@
     for m in range(0, MIDDLE, 2):
         pair = jnp.concatenate([masked[m], masked[m + 1]], axis=1)
         moved = dot(pick, jnp.concatenate([pair, filler], axis=0)).astype(BF16)
-        for step, out in enumerate(views(outs, owners)):
+        for step, out in enumerate(rows_of(outs, owners)):
             part = moved[step * size : (step + 1) * size]
-            out[m] = part[:, :HALF]
-            out[m + 1] = part[:, HALF:]
+            out[m][...] = part[:, :HALF]
+            out[m + 1][...] = part[:, HALF:]
 
 
 def ordered(own, other, axis):
@@ -200,18 +210,21 @@
     )
 
 
-def halves(value, keep, send, tap):
+def deal(value, kept, sent, grad, tap):
     low, high = value[: HALF // 2], value[HALF // 2 :]
     mine = lax.axis_index("col") == 0
-    keep[tap] = jnp.where(mine, low, high)
-    send[tap] = jnp.where(mine, high, low).astype(BF16)
-
-
-def emit(value, outs, tap):
+    keep, send = jnp.where(mine, low, high), jnp.where(mine, high, low).astype(BF16)
+    for k in range(4):
+        step, rows = partner("blk", k, True), slice(k * ROWS, (k + 1) * ROWS)
+        kept[step, grad, tap] = keep[rows]
+        sent[step, grad, tap] = send[rows]
+
+
+def emit(value, outs, grad, tap):
     if len(outs) == 2:
-        halves(value, outs[0], outs[1], tap)
+        deal(value, outs[0], outs[1], grad, tap)
     else:
-        outs[0][tap] = value
+        outs[0][grad, tap] = value
 
 
 def second_gradient(scale, owners, capacity, permuted, routing, *refs):
@@ -237,7 +250,7 @@
         dy, dx = tap // 3, tap % 3
         window = masked[dy : dy + BLOCK, dx : dx + BLOCK].reshape(BLOCK * rows, HALF)
         window = jnp.maximum(window, jnp.zeros_like(window))
-        emit(dot_tn(window, grads) * scale, outs, tap)
+        emit(dot_tn(window, grads) * scale, outs, 0, tap)
 
 
 def first_gradient(
@@ -260,7 +273,7 @@
     for tap in range(9):
         dy, dx = tap // 3, tap % 3
         window = saved[dy : dy + MIDDLE, dx : dx + MIDDLE].reshape(size, HALF)
-        emit(dot_tn(window, grads) * scale, outs, tap)
+        emit(dot_tn(window, grads) * scale, outs, 1, tap)
 
 
 def owner_spread(tile, tile_other, second, second_other, out, total, cot, full):
@@ -286,15 +299,23 @@
     parts = 1 if not permuted else owners
     inputs, refs = refs[: 2 * parts], refs[2 * parts :]
     (masked, masked_other, weight, weight_other, source), refs = refs[:5], refs[5:]
+    if permuted:
+        refs, sent = refs[:-1], refs[-1]
     outs, (counts, cot, total, pre, full, saved, arrived) = refs[:-7], refs[-7:]
+    if permuted:
+        kept, near, far = outs
+        outs = (kept, sent)
     fetch = pltpu.make_async_copy(source, saved, arrived)
     fetch.start()
-    pairs = [[out.at[k] for out in outs] for k in range(2)]
-    second_gradient(scale, owners, capacity, permuted, routing, *inputs, masked, cot, *pairs[0], counts)
+    second_gradient(scale, owners, capacity, permuted, routing, *inputs, masked, cot, *outs, counts)
     fetch.wait()
     first_gradient(
-        scale, cot, masked, masked_other, weight, weight_other, saved, *pairs[1], total, pre, full
+        scale, cot, masked, masked_other, weight, weight_other, saved, *outs, total, pre, full
     )
+    if permuted:
+        for k in range(2):
+            near[k] = sent[2 * k]
+            far[k] = sent[2 * k + 1]
 
 
 def adjacent(step):
@@ -303,8 +324,8 @@
 
 
 def owner_canvas(owners, capacity, wide, permuted, routing, *refs):
-    parts = 1 if not permuted else owners
-    got, got_other = views(refs[:parts], owners), views(refs[parts : 2 * parts], owners)
+    parts = 1 if not permuted else owners + 1
+    got, got_other = rows_of(refs[:parts], owners), rows_of(refs[parts : 2 * parts], owners)
     total, first, canvas = refs[2 * parts : 2 * parts + 3]
     rims, (table, pre, grown) = refs[2 * parts + 3 : -3], refs[-3:]
     owner_table(routing, table, owners, capacity)
@@ -322,17 +343,21 @@
     pick = jnp.concatenate(picks, axis=0).T.astype(BF16)
     for m in range(MIDDLE):
         block = jnp.concatenate(
-            [ordered(got[w][m], got_other[w][m], 1) for w in range(owners)], axis=0
+            [ordered(got[w][m][...], got_other[w][m][...], 1) for w in range(owners)], axis=0
         )
         live = dot(pick, block).reshape(MIDDLE, TILE_BLOCKS, FULL) > 0
         pre[m] = jnp.where(live, total[m].astype(F32), 0.0).astype(BF16)
     size = MIDDLE * MIDDLE * TILE_BLOCKS
     grown[...] = jnp.zeros_like(grown)
-    for tap in range(9):
-        dy, dx = tap // 3, tap % 3
-        part = dot_nt(pre[...].reshape(size, FULL), first[tap])
-        spot = (slice(dy, dy + MIDDLE), slice(dx, dx + MIDDLE))
-        grown[spot] = grown[spot] + part.reshape(MIDDLE, MIDDLE, TILE_BLOCKS, HALF)
+    for tap in range(0, 9, 2):
+        taps = range(tap, min(tap + 2, 9))
+        weight = jnp.concatenate([first[k] for k in taps], axis=0)
+        part = dot_nt(pre[...].reshape(size, FULL), weight)
+        for k in taps:
+            dy, dx = k // 3, k % 3
+            spot = (slice(dy, dy + MIDDLE), slice(dx, dx + MIDDLE))
+            here = part[:, (k - tap) * HALF : (k - tap + 1) * HALF]
+            grown[spot] = grown[spot] + here.reshape(MIDDLE, MIDDLE, TILE_BLOCKS, HALF)
     height, depth = TILE_ROWS * WIDE, OUTER * TILE_BLOCKS
     row, lane = iota((height, depth), 0), iota((height, depth), 1)
     at_row, at_col = row // WIDE, row % WIDE
@@ -357,23 +382,19 @@
         rim[WIDE:] = jnp.zeros((RIM - WIDE, FULL), BF16)
 
 
-def bit_of(axis, step):
-    return (lax.axis_index(axis) // step) % 2
-
-
-def add_columns(kept, got, *outs):
-    size = HALF // 2 // len(outs)
-    for step, out in enumerate(outs):
-        at = pl.multiple_of(partner("blk", step, True) * size, size)
-        part = kept[:, :, pl.ds(at, size), :] + got[:, :, pl.ds(at, size), :].astype(F32)
-        out[...] = part if step == 0 else part.astype(BF16)
-
-
-def add_workers(kept, got_3, got_2, got_1, rim_1, rim_3, out, out_1, out_3):
-    value = kept[...]
-    for part in (got_1, got_2, got_3):
-        value = value + part[...].astype(F32)
-    value = value.astype(BF16).reshape(PART, FULL)
+def add_far(kept, got, out):
+    for k in range(2):
+        out[k] = (kept[2 * k + 1] + got[k].astype(F32)).astype(BF16)
+
+
+def add_near(kept, got, passed, keep, send):
+    for k, out in enumerate((keep, send)):
+        value = kept[2 * k] + got[k].astype(F32) + passed[k].astype(F32)
+        out[...] = value.astype(out.dtype)
+
+
+def add_workers(kept, got, rim_1, rim_3, out, out_1, out_3):
+    value = (kept[...] + got[...].astype(F32)).astype(BF16).reshape(PART, FULL)
     out[...] = value
     for message, rim in ((out_1, rim_1), (out_3, rim_3)):
         message[:PART] = value
@@ -477,9 +498,12 @@
     outgoing, saved_slots = tie((outgoing, saved_slots))
     incoming = exchange(outgoing)
 
+    saved_pieces = pieces(MIDDLE, wide * capacity, HALF)
+    if permuted:
+        saved_pieces[3:] = [shape((m, wide * capacity, HALF), BF16) for m in (FIRST, MIDDLE - FIRST)]
     masked, *to_owners = call(
         functools.partial(pack_saved, owners, columns, capacity, wide, permuted),
-        [shape((MIDDLE, MIDDLE * PER_WORKER, HALF), BF16)] + pieces(MIDDLE, wide * capacity, HALF),
+        [shape((MIDDLE, MIDDLE * PER_WORKER, HALF), BF16)] + saved_pieces,
         [SMEM, VMEM], counts + tables, (1, 1), "pack_saved",
     )(routing, saved_slots.reshape(MIDDLE, MIDDLE * PER_WORKER, HALF))
     masked = masked.reshape(MIDDLE, MIDDLE, PER_WORKER, HALF)
@@ -487,12 +511,16 @@
     incoming, to_owners = incoming[::-1], to_owners[::-1]
     incoming_other = [swap(value) for value in incoming]
     masked_other = swap(masked)
-    at_owner = exchange(to_owners)
+    if permuted:
+        at_owner = list(to_owners[:1])
+        at_owner += [flip(value, "blk", k) for k, value in zip((1, 2, 3, 3), to_owners[1:])]
+    else:
+        at_owner = exchange(to_owners)
 
     saved_tiles = saved_input[0, 0].transpose(1, 2, 0, 3)
     if permuted:
-        halved = (2, 9, HALF // 2, FULL)
-        halved = [shape(halved, F32), shape(halved, BF16)]
+        part = (2, 9, ROWS, FULL)
+        halved = [shape((4,) + part, F32)] + [shape((2,) + part, BF16)] * 2
     else:
         halved = [shape((2, 9, HALF, FULL), F32)]
     terms = call(
@@ -507,7 +535,8 @@
             pltpu.VMEM((9, FULL, FULL), BF16),
             pltpu.VMEM(saved_tiles.shape, BF16),
             pltpu.SemaphoreType.DMA,
-        ],
+        ]
+        + ([pltpu.VMEM((4,) + part, BF16)] if permuted else []),
         (1, 1), "worker",
     )(
         routing, *incoming, *incoming_other, masked, masked_other, second_weight, second_other,
@@ -515,9 +544,11 @@
     )
 
     if permuted:
-        terms = list(terms)
-        terms[1], at_owner[2] = tie((terms[1], at_owner[2]))
-    terms, tile_here = tie((terms, tile))
+        kept, near, far = terms
+        far, at_owner[2] = tie((far, at_owner[2]))
+        kept, far, tile_here = tie((kept, far, tile))
+    else:
+        terms, tile_here = tie((terms, tile))
     total = call(
         owner_spread,
         shape((MIDDLE, MIDDLE, TILE_BLOCKS, FULL), BF16),
@@ -535,7 +566,7 @@
         return call(
             functools.partial(owner_canvas, owners, capacity, wide, permuted),
             [shape((HIGH, WIDE, HALF), F32)] + [shape((RIM, FULL), BF16)] * (2 if permuted else 0),
-            [SMEM] + [VMEM] * (2 * parts + 2),
+            [SMEM] + [VMEM] * (2 * len(at_owner) + 2),
             tables
             + [
                 pltpu.VMEM((MIDDLE, MIDDLE, TILE_BLOCKS, FULL), BF16),
@@ -545,23 +576,30 @@
         )(routing, *at_owner, *at_owner_other, total, first_weight)
 
     if permuted:
-        part = (2, 9, HALF // 2 // owners, FULL)
-        got = swap(terms[1], "col")
-        total, got, at_owner = tie((total, got, at_owner))
-        kept, *sends = call(
-            add_columns, [shape(part, F32)] + [shape(part, BF16)] * (owners - 1),
-            [VMEM] * 2, [], (1, 1), "add_columns",
-        )(terms[0], got)
-        sends, at_owner = tie((sends, at_owner))
-        got = [flip(sends[k - 1], "blk", k) for k in (3, 2, 1)]
+        far_got = swap(far, "col")
+        total, far_got = tie((total, far_got))
+        [passed] = call(add_far, [shape((2,) + part, BF16)], [VMEM] * 2, [], (1, 1), "add_far")(
+            kept, far_got
+        )
+        near, at_owner[1], at_owner[3], _ = tie((near, at_owner[1], at_owner[3], passed))
+        near_got, passed = swap(near, "col"), flip(passed, "blk", 1)
+        keep, send = call(
+            add_near, [shape(part, F32), shape(part, BF16)], [VMEM] * 3, [], (1, 1), "add_near",
+        )(kept, near_got, passed)
+        send, at_owner[4] = tie((send, at_owner[4]))
+        got = flip(send, "blk", 2)
+        at_owner, _ = tie((at_owner, send))
         canvas, *rims = owner(at_owner)
         message = shape((PART, FULL), BF16)
         wider = shape((PART + RIM, FULL), BF16)
         own, *wides = call(
-            add_workers, [message, wider, wider], [VMEM] * 6, [], (1, 1), "add_workers",
-        )(kept, *got, *rims)
-        got = [flip(value, "blk", k) for k, value in ((3, wides[1]), (2, own), (1, wides[0]))][::-1]
-        across = [swap(own, "col"), swap(got[0][:PART], "col")]
+            add_workers, [message, wider, wider], [VMEM] * 4, [], (1, 1), "add_workers",
+        )(keep, got, *rims)
+        got_2, got_1 = flip(wides[1], "blk", 2), flip(wides[0], "blk", 1)
+        across = [swap(own, "col")]
+        got_2, across = tie((got_2, across))
+        got = [got_1, got_2, flip(got_2, "blk", 1)]
+        across += [swap(got_1, "col"), swap(got_2, "col")]
         got, across = tie((got[::-1], across))
         got = got[::-1]
         last = call(
@@ -569,7 +607,7 @@
             [pltpu.VMEM((RIM, FULL), F32), pltpu.VMEM((64, HALF), F32)],
             (1, 1), "column_message",
         )(canvas.reshape(HIGH * WIDE, HALF), got[0], got[2])
-        across += [swap(got[1], "col"), swap(last, "col")]
+        across += [swap(last, "col")]
         grad_in = call(
             close, shape(grad_out.shape, BF16), [VMEM] * 5,
             [pltpu.VMEM((TILE_ROWS * BLOCK * 32, HALF), F32)], (1, 1), "close",

time: 92 us -> 95.6 us (1.039)
  waiting for transfers between devices: 43 us -> 50.4 us
  Pallas kernels: 23.3 us -> 21.5 us
  starting transfers between devices: 22.9 us -> 21.1 us
    ppermute x16 -> x18, waiting for transfers between devices: 10.2 us -> 23.9 us  [swap(): return lax.ppermute(value, axis, [(0, 1), (1, 0)])]
    ppermute x12, waiting for transfers between devices: 32.8 us -> 26.5 us  [flip(): return lax.ppermute(value, axis, [(i, i ^ step) for i in range(size)])]
    ppermute x12, starting transfers between devices: 14.7 us -> 11.1 us  [flip(): return lax.ppermute(value, axis, [(i, i ^ step) for i in range(size)])]
    pallas_call x1, Pallas kernels: 7.47 us -> 5.55 us  [owner(): call(functools.partial(owner_canvas, owners, capacity, wide, permuted), [...]
    ppermute x16 -> x18, starting transfers between devices: 8.2 us -> 10 us  [swap(): return lax.ppermute(value, axis, [(0, 1), (1, 0)])]
  transfers between devices with their start and end apart: 28 -> 30, of which waited for: 14 -> 21; matrix products, arithmetic and copies ran while one was open for 0% -> 0% of each run, Pallas kernels for 23% -> 20%
where the time goes in v7:
time: 95.6 us; the launch traced here: 95.4 us
  waiting for transfers between devices  50.4 us (53%)
  Pallas kernels  21.5 us (22%)
  starting transfers between devices  21.1 us (22%)
  local copies, waits for them, and re-layouts  1.7 us (2%)
    ppermute x12, waiting for transfers between devices, flip(): return lax.ppermute(value, axis, [(i, i ^ step) for i in range(size)])  26.5 us
    ppermute x18, waiting for transfers between devices, swap(): return lax.ppermute(value, axis, [(0, 1), (1, 0)])  23.9 us
    ppermute x12, starting transfers between devices, flip(): return lax.ppermute(value, axis, [(i, i ^ step) for i in range(size)])  11.1 us
    ppermute x18, starting transfers between devices, swap(): return lax.ppermute(value, axis, [(0, 1), (1, 0)])  10 us
    pallas_call x1, Pallas kernels, shards(): call(functools.partial(worker, scale, owners, capacity, permuted), halved...  6.58 us
    pallas_call x1, Pallas kernels, owner(): call(functools.partial(owner_canvas, owners, capacity, wide, permuted), [...  5.55 us
    pallas_call x1, Pallas kernels, shards(): call(owner_spread, shape((MIDDLE, MIDDLE, TILE_BLOCKS, FULL), BF16), [VME...  2.93 us
    pallas_call x1, Pallas kernels, shards(): call(functools.partial(pack_cotangents, owners, capacity, permuted), piec...  1.92 us
  transfers between devices with their start and end apart: 30, of which 21 were waited for; matrix products, arithmetic and copies ran while one was open for 0% of the time, Pallas kernels for 20%

profile of v7, /device:TPU:0, one launch (start us, length us, event | category | flops | bytes accessed | tf_op | source)
XLA Modules:
  0.0 95.4 jit_solution(11456137425407253981)
XLA Ops:
  1.8 1.9 %pack_cotangents.1 = (bf16[8,64,128]{2,1,0:T(8,128)(2,1)S(1)}, bf16[8,64,128]{2,1,0:T(8,128)(2,1)S(1)}, bf16[8,64,128]{2,1,0:T(8,128)(2,1)S(1)}, bf16[8,64,128]{2,1,0:T(8,128)(2,1)S(1)}) custom-call(s32[4,16]{1,0:T(4,128)S(1)} %bitcast.18, bf16[8,8,32,128]{3,2,1,0:T(8,128)(2,1)} %bitcast.12), custom_call_target="tpu_custom_call" | custom-call | flops 1 | bytes 1 | tf_op jit(solution)/shard_map/pack_cotangents/pallas_call | solution.py:491
  3.8 4.7 %collective-permute-start = (bf16[8,64,128]{2,1,0:T(8,128)(2,1)S(1)}, bf16[8,64,128]{2,1,0:T(8,128)(2,1)S(1)}, u32[]{:S(2)}, u32[]{:S(2)}) collective-permute-start(bf16[8,64,128]{2,1,0:T(8,128)(2,1)S(1)} %get-tuple-element.70), channel_id=1, source_target_pairs={{0,12},{4,8},{8,4},{12,0},{1,13},{5,9},{9,5},{13,1},{2,14},{6,10},... | collective-permute-start | bytes 393224 | tf_op jit(solution)/shard_map/ppermute | solution.py:458
  10.1 1.6 %pack_saved.1 = (bf16[10,160,128]{2,1,0:T(8,128)(2,1)S(1)}, bf16[10,80,128]{2,1,0:T(8,128)(2,1)S(1)}, bf16[10,80,128]{2,1,0:T(8,128)(2,1)S(1)}, bf16[10,80,128]{...) custom-call(s32[4,16]{1,0:T(4,128)S(1)} %bitcast.19, ...), custom_call_target="tpu_custom_call" | custom-call | flops 1 | bytes 1 | tf_op jit(solution)/shard_map/pack_saved/pallas_call | solution.py:504
  12.9 7.2 %collective-permute-done.1.refs_2_ = bf16[8,64,128]{2,1,0:T(8,128)(2,1)S(1)} collective-permute-done((bf16[8,64,128]{2,1,0:T(8,128)(2,1)S(1)}, bf16[8,64,128]{2,1,0:T(8,128)(2,1)S(1)}, u32[]{:S(2)}, u32[]{:S(2)}) %collective-permute-start.1) | collective-permute-done | bytes 131104 | tf_op jit(solution)/shard_map/ppermute | solution.py:458
  22.7 1.5 %collective-permute-done.6.refs_7_ = bf16[8,64,128]{2,1,0:T(8,128)(2,1)S(1)} collective-permute-done((bf16[8,64,128]{2,1,0:T(8,128)(2,1)S(1)}, bf16[8,64,128]{2,1,0:T(8,128)(2,1)S(1)}, u32[]{:S(2)}, u32[]{:S(2)}) %collective-permute-start.6) | collective-permute-done | bytes 131104 | tf_op jit(solution)/shard_map/ppermute | solution.py:453
  24.2 6.6 %worker.1 = (f32[4,2,9,16,256]{4,3,2,1,0:T(8,128)S(1)}, bf16[2,2,9,16,256]{4,3,2,1,0:T(8,128)(2,1)S(1)}, bf16[2,2,9,16,256]{4,3,2,1,0:T(8,128)(2,1)S(1)}) custom-call(s32[4,16]{1,0:T(4,128)S(1)} %bitcast.20, bf16[8,64,128]{2,1,0:T(8,128)(2,1)S(1)} %get-tuple-element.82.refs_0_, bf16[8,64,128]{2,1,0:T(8,128)(2,1)S(1)} %collective-permute-done.2.refs_1_, ...), custom_call_target="tpu_custom_call" | custom-call | flops 1 | bytes 1 | tf_op jit(solution)/shard_map/worker/pallas_call | solution.py:526
  30.8 3.9 %collective-permute-done.11.refs_2_ = bf16[10,80,128]{2,1,0:T(8,128)(2,1)S(1)} collective-permute-done((bf16[10,80,128]{2,1,0:T(8,128)(2,1)S(1)}, bf16[10,80,128]{2,1,0:T(8,128)(2,1)S(1)}, u32[]{:S(2)}, u32[]{:S(2)}) %collective-permute-start.11) | collective-permute-done | bytes 204832 | tf_op jit(solution)/shard_map/ppermute | solution.py:458
  34.7 1.5 %collective-permute-start.13 = (bf16[2,2,9,16,256]{4,3,2,1,0:T(8,128)(2,1)S(1)}, bf16[2,2,9,16,256]{4,3,2,1,0:T(8,128)(2,1)S(1)}, u32[]{:S(2)}, u32[]{:S(2)}) collective-permute-start(bf16[2,2,9,16,256]{4,3,2,1,0:T(8,128)(2,1)S(1)} %get-tuple-element.96), channel_id=1, source_target_pairs={{0,2},{2,0},{1,3},{3,1},{4,6},{6,4},{5,7},{7,5},{8,10},{10,8},{9,1... | collective-permute-start | bytes 884744 | tf_op jit(solution)/shard_map/ppermute | solution.py:453
  36.2 1.3 %collective-permute-start.10 = (bf16[4,80,128]{2,1,0:T(8,128)(2,1)S(1)}, bf16[4,80,128]{2,1,0:T(8,128)(2,1)S(1)}, u32[]{:S(2)}, u32[]{:S(2)}) collective-permute-start(bf16[4,80,128]{2,1,0:T(8,128)(2,1)S(1)} %get-tuple-element.89), channel_id=1, source_target_pairs={{0,12},{4,8},{8,4},{12,0},{1,13},{5,9},{9,5},{13,1},{2,14},{6,10},... | collective-permute-start | bytes 245768 | tf_op jit(solution)/shard_map/ppermute | solution.py:458
  37.6 2.9 %owner_spread.1.refs_10_ = bf16[10,10,32,256]{3,2,1,0:T(8,128)(2,1)S(1)} custom-call(bf16[8,8,32,128]{3,2,1,0:T(8,128)(2,1)S(1)} %bitcast.14, bf16[8,8,32,128]{3,2,1,0:T(8,128)(2,1)S(1)} %collective-permute-done.12.tile_other, bf16[9,128,256]{2,1,0:T(8,128)(2,1)S(1)} %copy-done.1, bf16[9,128,256]{2,1,0:T(8,128)(2,1)S(1)} %collective-permute-done.8.refs_11_.second_other), custom_call_target="tpu_custom_call" | custom-call | flops 1 | bytes 1 | tf_op jit(solution)/shard_map/owner_spread/pallas_call | solution.py:552
  40.5 3.2 %collective-permute-done.13.got = bf16[2,2,9,16,256]{4,3,2,1,0:T(8,128)(2,1)S(1)} collective-permute-done((bf16[2,2,9,16,256]{4,3,2,1,0:T(8,128)(2,1)S(1)}, bf16[2,2,9,16,256]{4,3,2,1,0:T(8,128)(2,1)S(1)}, u32[]{:S(2)}, u32[]{:S(2)}) %collective-permute-start.13) | collective-permute-done | bytes 294944 | tf_op jit(solution)/shard_map/ppermute | solution.py:453
  45.4 2.0 %collective-permute-start.16 = (bf16[6,80,128]{2,1,0:T(8,128)(2,1)S(1)}, bf16[6,80,128]{2,1,0:T(8,128)(2,1)S(1)}, u32[]{:S(2)}, u32[]{:S(2)}) collective-permute-start(bf16[6,80,128]{2,1,0:T(8,128)(2,1)S(1)} %get-tuple-element.103), channel_id=1, source_target_pairs={{0,12},{4,8},{8,4},{12,0},{1,13},{5,9},{9,5},{13,1},{2,14},{6,10},... | collective-permute-start | bytes 368648 | tf_op jit(solution)/shard_map/ppermute | solution.py:458
  47.4 4.8 %collective-permute-done.14.got = bf16[2,2,9,16,256]{4,3,2,1,0:T(8,128)(2,1)S(1)} collective-permute-done((bf16[2,2,9,16,256]{4,3,2,1,0:T(8,128)(2,1)S(1)}, bf16[2,2,9,16,256]{4,3,2,1,0:T(8,128)(2,1)S(1)}, u32[]{:S(2)}, u32[]{:S(2)}) %collective-permute-start.14) | collective-permute-done | bytes 294944 | tf_op jit(solution)/shard_map/ppermute | solution.py:453
  52.2 2.4 %collective-permute-done.15.passed = bf16[2,2,9,16,256]{4,3,2,1,0:T(8,128)(2,1)S(1)} collective-permute-done((bf16[2,2,9,16,256]{4,3,2,1,0:T(8,128)(2,1)S(1)}, bf16[2,2,9,16,256]{4,3,2,1,0:T(8,128)(2,1)S(1)}, u32[]{:S(2)}, u32[]{:S(2)}) %collective-permute-start.15) | collective-permute-done | bytes 294944 | tf_op jit(solution)/shard_map/ppermute | solution.py:458
  58.5 5.5 %owner_canvas.1 = (f32[68,40,128]{2,1,0:T(8,128)S(1)}, bf16[48,256]{1,0:T(8,128)(2,1)S(1)}, bf16[48,256]{1,0:T(8,128)(2,1)S(1)}) custom-call(s32[4,16]{1,0:T(4,128)S(1)} %bitcast.21, bf16[10,80,128]{2,1,0:T(8,128)(2,1)S(1)} %get-tuple-element.106.refs_0_, bf16[10,80,128]{2,1,0:T(8,128)(2,1)S(1)} %collective-permute-done.9.refs_1_, ...), custom_call_target="tpu_custom_call" | custom-call | flops 1 | bytes 1 | tf_op jit(solution)/shard_map/owner_canvas/pallas_call | solution.py:566
  64.1 2.1 %collective-permute-done.22.got = bf16[2,9,16,256]{3,2,1,0:T(8,128)(2,1)S(1)} collective-permute-done((bf16[2,9,16,256]{3,2,1,0:T(8,128)(2,1)S(1)}, bf16[2,9,16,256]{3,2,1,0:T(8,128)(2,1)S(1)}, u32[]{:S(2)}, u32[]{:S(2)}) %collective-permute-start.22) | collective-permute-done | bytes 147488 | tf_op jit(solution)/shard_map/ppermute | solution.py:458
  66.9 1.7 %collective-permute-start.26 = (bf16[336,256]{1,0:T(8,128)(2,1)S(1)}, bf16[336,256]{1,0:T(8,128)(2,1)S(1)}, u32[]{:S(2)}, u32[]{:S(2)}) collective-permute-start(bf16[336,256]{1,0:T(8,128)(2,1)S(1)} %get-tuple-element.119), channel_id=1, source_target_pairs={{0,4},{4,0},{8,12},{12,8},{1,5},{5,1},{9,13},{13,9},{2,6},{6,2},{1... | collective-permute-start | bytes 516104 | tf_op jit(solution)/shard_map/ppermute | solution.py:458
  68.5 1.4 %collective-permute-start.24 = (bf16[288,256]{1,0:T(8,128)(2,1)S(1)}, bf16[288,256]{1,0:T(8,128)(2,1)S(1)}, u32[]{:S(2)}, u32[]{:S(2)}) collective-permute-start(bf16[288,256]{1,0:T(8,128)(2,1)S(1)} %get-tuple-element.117.refs_0_), channel_id=1, source_target_pairs={{0,2},{2,0},{1,3},{3,1},{4,6},{6,4},{5,7},{7,5},{8,10},{10,8},{9,1... | collective-permute-start | bytes 442376 | tf_op jit(solution)/shard_map/ppermute | solution.py:453
  70.0 3.8 %collective-permute-done.24.refs_4_ = bf16[288,256]{1,0:T(8,128)(2,1)S(1)} collective-permute-done((bf16[288,256]{1,0:T(8,128)(2,1)S(1)}, bf16[288,256]{1,0:T(8,128)(2,1)S(1)}, u32[]{:S(2)}, u32[]{:S(2)}) %collective-permute-start.24) | collective-permute-done | bytes 147488 | tf_op jit(solution)/shard_map/ppermute | solution.py:453
  73.8 3.3 %collective-permute-done.23.refs_2_ = bf16[336,256]{1,0:T(8,128)(2,1)S(1)} collective-permute-done((bf16[336,256]{1,0:T(8,128)(2,1)S(1)}, bf16[336,256]{1,0:T(8,128)(2,1)S(1)}, u32[]{:S(2)}, u32[]{:S(2)}) %collective-permute-start.23) | collective-permute-done | bytes 172064 | tf_op jit(solution)/shard_map/ppermute | solution.py:458
  79.1 4.3 %collective-permute-done.25.got_3.refs_3_ = bf16[336,256]{1,0:T(8,128)(2,1)S(1)} collective-permute-done((bf16[336,256]{1,0:T(8,128)(2,1)S(1)}, bf16[336,256]{1,0:T(8,128)(2,1)S(1)}, u32[]{:S(2)}, u32[]{:S(2)}) %collective-permute-start.25) | collective-permute-done | bytes 172064 | tf_op jit(solution)/shard_map/ppermute | solution.py:458
  84.3 2.8 %collective-permute-done.28.refs_6_ = bf16[336,256]{1,0:T(8,128)(2,1)S(1)} collective-permute-done((bf16[336,256]{1,0:T(8,128)(2,1)S(1)}, bf16[336,256]{1,0:T(8,128)(2,1)S(1)}, u32[]{:S(2)}, u32[]{:S(2)}) %collective-permute-start.28) | collective-permute-done | bytes 172064 | tf_op jit(solution)/shard_map/ppermute | solution.py:453
  88.4 4.3 %collective-permute-done.29.across.refs_7_ = bf16[352,256]{1,0:T(8,128)(2,1)S(1)} collective-permute-done((bf16[352,256]{1,0:T(8,128)(2,1)S(1)}, bf16[352,256]{1,0:T(8,128)(2,1)S(1)}, u32[]{:S(2)}, u32[]{:S(2)}) %collective-permute-start.29) | collective-permute-done | bytes 180256 | tf_op jit(solution)/shard_map/ppermute | solution.py:453
  93.9 1.6 %lay.1 = (f32[9,128,256]{2,1,0:T(8,128)}, f32[9,128,256]{2,1,0:T(8,128)}) custom-call(bf16[288,256]{1,0:T(8,128)(2,1)S(1)} %get-tuple-element.117.refs_0_, bf16[336,256]{1,0:T(8,128)(2,1)S(1)} %collective-permute-done.26.got_1.refs_1_, bf16[336,256]{1,0:T(8,128)(2,1)S(1)} %collective-permute-done.23.refs_2_, ...), custom_call_target="tpu_custom_call" | custom-call | flops 1 | bytes 1 | tf_op jit(solution)/shard_map/lay/pallas_call | solution.py:615
  (59 shorter events, 18.4 us)
Async XLA Ops:
  0.6 23.6 %collective-permute-start.8 = (bf16[9,128,256]{2,1,0:T(8,128)(2,1)}, bf16[9,128,256]{2,1,0:T(8,128)(2,1)S(1)}, u32[]{:S(2)}, u32[]{:S(2)}) collective-permute-start(bf16[9,128,256]{2,1,0:T(8,128)(2,1)} %second.1), channel_id=1, source_target_pairs={{0,1},{1,0},{2,3},{3,2},{4,5},{5,4},{6,7},{7,6},{8,9},{9,8},{10,11... | collective-permute-start | bytes 1769480 | tf_op jit(solution)/shard_map/ppermute | solution.py:453
  3.8 9.2 %collective-permute-start = (bf16[8,64,128]{2,1,0:T(8,128)(2,1)S(1)}, bf16[8,64,128]{2,1,0:T(8,128)(2,1)S(1)}, u32[]{:S(2)}, u32[]{:S(2)}) collective-permute-start(bf16[8,64,128]{2,1,0:T(8,128)(2,1)S(1)} %get-tuple-element.70), channel_id=1, source_target_pairs={{0,12},{4,8},{8,4},{12,0},{1,13},{5,9},{9,5},{13,1},{2,14},{6,10},... | collective-permute-start | bytes 393224 | tf_op jit(solution)/shard_map/ppermute | solution.py:458
  8.5 11.7 %collective-permute-start.1 = (bf16[8,64,128]{2,1,0:T(8,128)(2,1)S(1)}, bf16[8,64,128]{2,1,0:T(8,128)(2,1)S(1)}, u32[]{:S(2)}, u32[]{:S(2)}) collective-permute-start(bf16[8,64,128]{2,1,0:T(8,128)(2,1)S(1)} %get-tuple-element.71), channel_id=1, source_target_pairs={{0,8},{4,12},{8,0},{12,4},{1,9},{5,13},{9,1},{13,5},{2,10},{6,14},... | collective-permute-start | bytes 393224 | tf_op jit(solution)/shard_map/ppermute | solution.py:458
  8.5 11.7 %collective-permute-start.2 = (bf16[8,64,128]{2,1,0:T(8,128)(2,1)S(1)}, bf16[8,64,128]{2,1,0:T(8,128)(2,1)S(1)}, u32[]{:S(2)}, u32[]{:S(2)}) collective-permute-start(bf16[8,64,128]{2,1,0:T(8,128)(2,1)S(1)} %get-tuple-element.72), channel_id=1, source_target_pairs={{0,4},{4,0},{8,12},{12,8},{1,5},{5,1},{9,13},{13,9},{2,6},{6,2},{1... | collective-permute-start | bytes 393224 | tf_op jit(solution)/shard_map/ppermute | solution.py:458
  20.2 4.0 %collective-permute-start.7 = (bf16[10,10,16,128]{3,2,1,0:T(8,128)(2,1)S(1)}, bf16[10,10,16,128]{3,2,1,0:T(8,128)(2,1)S(1)}, u32[]{:S(2)}, u32[]{:S(2)}) collective-permute-start(bf16[10,10,16,128]{3,2,1,0:T(8,128)(2,1)S(1)} %bitcast.15), channel_id=1, source_target_pairs={{0,1},{1,0},{2,3},{3,2},{4,5},{5,4},{6,7},{7,6},{8,9},{9,8},{10,11... | collective-permute-start | bytes 1228808 | tf_op jit(solution)/shard_map/ppermute | solution.py:453
  22.1 15.5 %collective-permute-start.12 = (bf16[8,8,32,128]{3,2,1,0:T(8,128)(2,1)}, bf16[8,8,32,128]{3,2,1,0:T(8,128)(2,1)S(1)}, u32[]{:S(2)}, u32[]{:S(2)}) collective-permute-start(bf16[8,8,32,128]{3,2,1,0:T(8,128)(2,1)} %bitcast.13), channel_id=1, source_target_pairs={{0,1},{1,0},{2,3},{3,2},{4,5},{5,4},{6,7},{7,6},{8,9},{9,8},{10,11... | collective-permute-start | bytes 1572872 | tf_op jit(solution)/shard_map/ppermute | solution.py:453
  22.3 12.4 %collective-permute-start.11 = (bf16[10,80,128]{2,1,0:T(8,128)(2,1)S(1)}, bf16[10,80,128]{2,1,0:T(8,128)(2,1)S(1)}, u32[]{:S(2)}, u32[]{:S(2)}) collective-permute-start(bf16[10,80,128]{2,1,0:T(8,128)(2,1)S(1)} %get-tuple-element.92), channel_id=1, source_target_pairs={{0,8},{4,12},{8,0},{12,4},{1,9},{5,13},{9,1},{13,5},{2,10},{6,14},... | collective-permute-start | bytes 614408 | tf_op jit(solution)/shard_map/ppermute | solution.py:458
  34.7 9.0 %collective-permute-start.13 = (bf16[2,2,9,16,256]{4,3,2,1,0:T(8,128)(2,1)S(1)}, bf16[2,2,9,16,256]{4,3,2,1,0:T(8,128)(2,1)S(1)}, u32[]{:S(2)}, u32[]{:S(2)}) collective-permute-start(bf16[2,2,9,16,256]{4,3,2,1,0:T(8,128)(2,1)S(1)} %get-tuple-element.96), channel_id=1, source_target_pairs={{0,2},{2,0},{1,3},{3,1},{4,6},{6,4},{5,7},{7,5},{8,10},{10,8},{9,1... | collective-permute-start | bytes 884744 | tf_op jit(solution)/shard_map/ppermute | solution.py:453
  36.2 8.5 %collective-permute-start.9 = (bf16[10,80,128]{2,1,0:T(8,128)(2,1)S(1)}, bf16[10,80,128]{2,1,0:T(8,128)(2,1)S(1)}, u32[]{:S(2)}, u32[]{:S(2)}) collective-permute-start(bf16[10,80,128]{2,1,0:T(8,128)(2,1)S(1)} %get-tuple-element.88), channel_id=1, source_target_pairs={{0,4},{4,0},{8,12},{12,8},{1,5},{5,1},{9,13},{13,9},{2,6},{6,2},{1... | collective-permute-start | bytes 614408 | tf_op jit(solution)/shard_map/ppermute | solution.py:458
  36.2 8.2 %collective-permute-start.10 = (bf16[4,80,128]{2,1,0:T(8,128)(2,1)S(1)}, bf16[4,80,128]{2,1,0:T(8,128)(2,1)S(1)}, u32[]{:S(2)}, u32[]{:S(2)}) collective-permute-start(bf16[4,80,128]{2,1,0:T(8,128)(2,1)S(1)} %get-tuple-element.89), channel_id=1, source_target_pairs={{0,12},{4,8},{8,4},{12,0},{1,13},{5,9},{9,5},{13,1},{2,14},{6,10},... | collective-permute-start | bytes 245768 | tf_op jit(solution)/shard_map/ppermute | solution.py:458
  44.7 7.4 %collective-permute-start.14 = (bf16[2,2,9,16,256]{4,3,2,1,0:T(8,128)(2,1)S(1)}, bf16[2,2,9,16,256]{4,3,2,1,0:T(8,128)(2,1)S(1)}, u32[]{:S(2)}, u32[]{:S(2)}) collective-permute-start(bf16[2,2,9,16,256]{4,3,2,1,0:T(8,128)(2,1)S(1)} %get-tuple-element.101), channel_id=1, source_target_pairs={{0,2},{2,0},{1,3},{3,1},{4,6},{6,4},{5,7},{7,5},{8,10},{10,8},{9,1... | collective-permute-start | bytes 884744 | tf_op jit(solution)/shard_map/ppermute | solution.py:453
  45.4 9.2 %collective-permute-start.15 = (bf16[2,2,9,16,256]{4,3,2,1,0:T(8,128)(2,1)S(1)}, bf16[2,2,9,16,256]{4,3,2,1,0:T(8,128)(2,1)S(1)}, u32[]{:S(2)}, u32[]{:S(2)}) collective-permute-start(bf16[2,2,9,16,256]{4,3,2,1,0:T(8,128)(2,1)S(1)} %add_far.1), channel_id=1, source_target_pairs={{0,4},{4,0},{8,12},{12,8},{1,5},{5,1},{9,13},{13,9},{2,6},{6,2},{1... | collective-permute-start | bytes 884744 | tf_op jit(solution)/shard_map/ppermute | solution.py:458
  45.4 10.5 %collective-permute-start.16 = (bf16[6,80,128]{2,1,0:T(8,128)(2,1)S(1)}, bf16[6,80,128]{2,1,0:T(8,128)(2,1)S(1)}, u32[]{:S(2)}, u32[]{:S(2)}) collective-permute-start(bf16[6,80,128]{2,1,0:T(8,128)(2,1)S(1)} %get-tuple-element.103), channel_id=1, source_target_pairs={{0,12},{4,8},{8,4},{12,0},{1,13},{5,9},{9,5},{13,1},{2,14},{6,10},... | collective-permute-start | bytes 368648 | tf_op jit(solution)/shard_map/ppermute | solution.py:458
  55.9 2.6 %collective-permute-start.17 = (bf16[10,80,128]{2,1,0:T(8,128)(2,1)S(1)}, bf16[10,80,128]{2,1,0:T(8,128)(2,1)S(1)}, u32[]{:S(2)}, u32[]{:S(2)}) collective-permute-start(bf16[10,80,128]{2,1,0:T(8,128)(2,1)S(1)} %get-tuple-element.106.refs_0_), channel_id=1, source_target_pairs={{0,1},{1,0},{2,3},{3,2},{4,5},{5,4},{6,7},{7,6},{8,9},{9,8},{10,11... | collective-permute-start | bytes 614408 | tf_op jit(solution)/shard_map/ppermute | solution.py:453
  56.4 2.1 %collective-permute-start.18 = (bf16[10,80,128]{2,1,0:T(8,128)(2,1)S(1)}, bf16[10,80,128]{2,1,0:T(8,128)(2,1)S(1)}, u32[]{:S(2)}, u32[]{:S(2)}) collective-permute-start(bf16[10,80,128]{2,1,0:T(8,128)(2,1)S(1)} %collective-permute-done.9.refs_1_), channel_id=1, source_target_pairs={{0,1},{1,0},{2,3},{3,2},{4,5},{5,4},{6,7},{7,6},{8,9},{9,8},{10,11... | collective-permute-start | bytes 614408 | tf_op jit(solution)/shard_map/ppermute | solution.py:453
  56.4 2.1 %collective-permute-start.19 = (bf16[10,80,128]{2,1,0:T(8,128)(2,1)S(1)}, bf16[10,80,128]{2,1,0:T(8,128)(2,1)S(1)}, u32[]{:S(2)}, u32[]{:S(2)}) collective-permute-start(bf16[10,80,128]{2,1,0:T(8,128)(2,1)S(1)} %collective-permute-done.11.refs_2_), channel_id=1, source_target_pairs={{0,1},{1,0},{2,3},{3,2},{4,5},{5,4},{6,7},{7,6},{8,9},{9,8},{10,11... | collective-permute-start | bytes 614408 | tf_op jit(solution)/shard_map/ppermute | solution.py:453
  56.9 9.3 %collective-permute-start.22 = (bf16[2,9,16,256]{3,2,1,0:T(8,128)(2,1)S(1)}, bf16[2,9,16,256]{3,2,1,0:T(8,128)(2,1)S(1)}, u32[]{:S(2)}, u32[]{:S(2)}) collective-permute-start(bf16[2,9,16,256]{3,2,1,0:T(8,128)(2,1)S(1)} %get-tuple-element.105), channel_id=1, source_target_pairs={{0,8},{4,12},{8,0},{12,4},{1,9},{5,13},{9,1},{13,5},{2,10},{6,14},... | collective-permute-start | bytes 442376 | tf_op jit(solution)/shard_map/ppermute | solution.py:458
  66.2 10.9 %collective-permute-start.23 = (bf16[336,256]{1,0:T(8,128)(2,1)S(1)}, bf16[336,256]{1,0:T(8,128)(2,1)S(1)}, u32[]{:S(2)}, u32[]{:S(2)}) collective-permute-start(bf16[336,256]{1,0:T(8,128)(2,1)S(1)} %get-tuple-element.116), channel_id=1, source_target_pairs={{0,8},{4,12},{8,0},{12,4},{1,9},{5,13},{9,1},{13,5},{2,10},{6,14},... | collective-permute-start | bytes 516104 | tf_op jit(solution)/shard_map/ppermute | solution.py:458
  66.9 10.2 %collective-permute-start.26 = (bf16[336,256]{1,0:T(8,128)(2,1)S(1)}, bf16[336,256]{1,0:T(8,128)(2,1)S(1)}, u32[]{:S(2)}, u32[]{:S(2)}) collective-permute-start(bf16[336,256]{1,0:T(8,128)(2,1)S(1)} %get-tuple-element.119), channel_id=1, source_target_pairs={{0,4},{4,0},{8,12},{12,8},{1,5},{5,1},{9,13},{13,9},{2,6},{6,2},{1... | collective-permute-start | bytes 516104 | tf_op jit(solution)/shard_map/ppermute | solution.py:458
  68.5 5.2 %collective-permute-start.24 = (bf16[288,256]{1,0:T(8,128)(2,1)S(1)}, bf16[288,256]{1,0:T(8,128)(2,1)S(1)}, u32[]{:S(2)}, u32[]{:S(2)}) collective-permute-start(bf16[288,256]{1,0:T(8,128)(2,1)S(1)} %get-tuple-element.117.refs_0_), channel_id=1, source_target_pairs={{0,2},{2,0},{1,3},{3,1},{4,6},{6,4},{5,7},{7,5},{8,10},{10,8},{9,1... | collective-permute-start | bytes 442376 | tf_op jit(solution)/shard_map/ppermute | solution.py:453
  77.0 6.3 %collective-permute-start.25 = (bf16[336,256]{1,0:T(8,128)(2,1)S(1)}, bf16[336,256]{1,0:T(8,128)(2,1)S(1)}, u32[]{:S(2)}, u32[]{:S(2)}) collective-permute-start(bf16[336,256]{1,0:T(8,128)(2,1)S(1)} %collective-permute-done.23.refs_2_), channel_id=1, source_target_pairs={{0,4},{4,0},{8,12},{12,8},{1,5},{5,1},{9,13},{13,9},{2,6},{6,2},{1... | collective-permute-start | bytes 516104 | tf_op jit(solution)/shard_map/ppermute | solution.py:458
  77.0 7.2 %collective-permute-start.27 = (bf16[336,256]{1,0:T(8,128)(2,1)S(1)}, bf16[336,256]{1,0:T(8,128)(2,1)S(1)}, u32[]{:S(2)}, u32[]{:S(2)}) collective-permute-start(bf16[336,256]{1,0:T(8,128)(2,1)S(1)} %collective-permute-done.26.got_1.refs_1_), channel_id=1, source_target_pairs={{0,2},{2,0},{1,3},{3,1},{4,6},{6,4},{5,7},{7,5},{8,10},{10,8},{9,1... | collective-permute-start | bytes 516104 | tf_op jit(solution)/shard_map/ppermute | solution.py:453
  78.3 8.7 %collective-permute-start.28 = (bf16[336,256]{1,0:T(8,128)(2,1)S(1)}, bf16[336,256]{1,0:T(8,128)(2,1)S(1)}, u32[]{:S(2)}, u32[]{:S(2)}) collective-permute-start(bf16[336,256]{1,0:T(8,128)(2,1)S(1)} %collective-permute-done.23.refs_2_), channel_id=1, source_target_pairs={{0,2},{2,0},{1,3},{3,1},{4,6},{6,4},{5,7},{7,5},{8,10},{10,8},{9,1... | collective-permute-start | bytes 516104 | tf_op jit(solution)/shard_map/ppermute | solution.py:453
  87.1 5.7 %collective-permute-start.29 = (bf16[352,256]{1,0:T(8,128)(2,1)S(1)}, bf16[352,256]{1,0:T(8,128)(2,1)S(1)}, u32[]{:S(2)}, u32[]{:S(2)}) collective-permute-start(bf16[352,256]{1,0:T(8,128)(2,1)S(1)} %column_message.1), channel_id=1, source_target_pairs={{0,2},{2,0},{1,3},{3,1},{4,6},{6,4},{5,7},{7,5},{8,10},{10,8},{9,1... | collective-permute-start | bytes 540680 | tf_op jit(solution)/shard_map/ppermute | solution.py:453
  (12 other events, 77.7 us)

commit v8 on v7

--- a/solution.py
+++ b/solution.py
@@ -20,7 +20,6 @@
 DEAD = -4096
 HIGH = 68
 RIM = 48
-FIRST = 4
 ROWS = 16
 PART = 288
 WIDE = 40
@@ -108,14 +107,6 @@
 
 def views(refs, count):
     return list(refs) if len(refs) == count else [refs[0].at[k] for k in range(count)]
-
-
-def rows_of(refs, count):
-    if len(refs) == count + 1:
-        return [[ref.at[m] for m in range(MIDDLE)] for ref in refs[:-2]] + [
-            [ref.at[m] for ref in refs[-2:] for m in range(ref.shape[0])]
-        ]
-    return [[ref.at[m] for m in range(MIDDLE)] for ref in views(refs, count)]
 
 
 def partner(axis, step, permuted):
@@ -197,10 +188,10 @@
     for m in range(0, MIDDLE, 2):
         pair = jnp.concatenate([masked[m], masked[m + 1]], axis=1)
         moved = dot(pick, jnp.concatenate([pair, filler], axis=0)).astype(BF16)
-        for step, out in enumerate(rows_of(outs, owners)):
+        for step, out in enumerate(views(outs, owners)):
             part = moved[step * size : (step + 1) * size]
-            out[m][...] = part[:, :HALF]
-            out[m + 1][...] = part[:, HALF:]
+            out[m] = part[:, :HALF]
+            out[m + 1] = part[:, HALF:]
 
 
 def ordered(own, other, axis):
@@ -313,9 +304,8 @@
         scale, cot, masked, masked_other, weight, weight_other, saved, *outs, total, pre, full
     )
     if permuted:
-        for k in range(2):
-            near[k] = sent[2 * k]
-            far[k] = sent[2 * k + 1]
+        near[...] = sent[:2]
+        far[...] = sent[2:]
 
 
 def adjacent(step):
@@ -324,8 +314,8 @@
 
 
 def owner_canvas(owners, capacity, wide, permuted, routing, *refs):
-    parts = 1 if not permuted else owners + 1
-    got, got_other = rows_of(refs[:parts], owners), rows_of(refs[parts : 2 * parts], owners)
+    parts = 1 if not permuted else owners
+    got, got_other = views(refs[:parts], owners), views(refs[parts : 2 * parts], owners)
     total, first, canvas = refs[2 * parts : 2 * parts + 3]
     rims, (table, pre, grown) = refs[2 * parts + 3 : -3], refs[-3:]
     owner_table(routing, table, owners, capacity)
@@ -343,7 +333,7 @@
     pick = jnp.concatenate(picks, axis=0).T.astype(BF16)
     for m in range(MIDDLE):
         block = jnp.concatenate(
-            [ordered(got[w][m][...], got_other[w][m][...], 1) for w in range(owners)], axis=0
+            [ordered(got[w][m], got_other[w][m], 1) for w in range(owners)], axis=0
         )
         live = dot(pick, block).reshape(MIDDLE, TILE_BLOCKS, FULL) > 0
         pre[m] = jnp.where(live, total[m].astype(F32), 0.0).astype(BF16)
@@ -382,19 +372,21 @@
         rim[WIDE:] = jnp.zeros((RIM - WIDE, FULL), BF16)
 
 
-def add_far(kept, got, out):
-    for k in range(2):
-        out[k] = (kept[2 * k + 1] + got[k].astype(F32)).astype(BF16)
-
-
-def add_near(kept, got, passed, keep, send):
-    for k, out in enumerate((keep, send)):
-        value = kept[2 * k] + got[k].astype(F32) + passed[k].astype(F32)
-        out[...] = value.astype(out.dtype)
-
-
-def add_workers(kept, got, rim_1, rim_3, out, out_1, out_3):
-    value = (kept[...] + got[...].astype(F32)).astype(BF16).reshape(PART, FULL)
+def add_far(kept, got, *sends):
+    for k, out in enumerate(sends):
+        out[...] = (kept[2 + k] + got[k].astype(F32)).astype(BF16)
+
+
+def add_near(kept, got, keep, send):
+    keep[...] = kept[0] + got[0].astype(F32)
+    send[...] = (kept[1] + got[1].astype(F32)).astype(BF16)
+
+
+def add_workers(kept, got_3, got_2, got_1, rim_1, rim_3, out, out_1, out_3):
+    value = kept[...]
+    for part in (got_3, got_2, got_1):
+        value = value + part[...].astype(F32)
+    value = value.astype(BF16).reshape(PART, FULL)
     out[...] = value
     for message, rim in ((out_1, rim_1), (out_3, rim_3)):
         message[:PART] = value
@@ -498,12 +490,9 @@
     outgoing, saved_slots = tie((outgoing, saved_slots))
     incoming = exchange(outgoing)
 
-    saved_pieces = pieces(MIDDLE, wide * capacity, HALF)
-    if permuted:
-        saved_pieces[3:] = [shape((m, wide * capacity, HALF), BF16) for m in (FIRST, MIDDLE - FIRST)]
     masked, *to_owners = call(
         functools.partial(pack_saved, owners, columns, capacity, wide, permuted),
-        [shape((MIDDLE, MIDDLE * PER_WORKER, HALF), BF16)] + saved_pieces,
+        [shape((MIDDLE, MIDDLE * PER_WORKER, HALF), BF16)] + pieces(MIDDLE, wide * capacity, HALF),
         [SMEM, VMEM], counts + tables, (1, 1), "pack_saved",
     )(routing, saved_slots.reshape(MIDDLE, MIDDLE * PER_WORKER, HALF))
     masked = masked.reshape(MIDDLE, MIDDLE, PER_WORKER, HALF)
@@ -511,11 +500,7 @@
     incoming, to_owners = incoming[::-1], to_owners[::-1]
     incoming_other = [swap(value) for value in incoming]
     masked_other = swap(masked)
-    if permuted:
-        at_owner = list(to_owners[:1])
-        at_owner += [flip(value, "blk", k) for k, value in zip((1, 2, 3, 3), to_owners[1:])]
-    else:
-        at_owner = exchange(to_owners)
+    at_owner = exchange(to_owners)
 
     saved_tiles = saved_input[0, 0].transpose(1, 2, 0, 3)
     if permuted:
@@ -576,30 +561,26 @@
         )(routing, *at_owner, *at_owner_other, total, first_weight)
 
     if permuted:
-        far_got = swap(far, "col")
+        far_got, near_got = swap(far, "col"), swap(near, "col")
         total, far_got = tie((total, far_got))
-        [passed] = call(add_far, [shape((2,) + part, BF16)], [VMEM] * 2, [], (1, 1), "add_far")(
+        sends = call(add_far, [shape(part, BF16)] * 2, [VMEM] * 2, [], (1, 1), "add_far")(
             kept, far_got
         )
-        near, at_owner[1], at_owner[3], _ = tie((near, at_owner[1], at_owner[3], passed))
-        near_got, passed = swap(near, "col"), flip(passed, "blk", 1)
+        sends, at_owner[3], at_owner[1] = tie((sends[::-1], at_owner[3], at_owner[1]))
+        got = [flip(sends[0], "blk", 3), flip(sends[1], "blk", 2)]
+        canvas, *rims = owner(at_owner)
+        near_got, canvas = tie((near_got, canvas))
         keep, send = call(
-            add_near, [shape(part, F32), shape(part, BF16)], [VMEM] * 3, [], (1, 1), "add_near",
-        )(kept, near_got, passed)
-        send, at_owner[4] = tie((send, at_owner[4]))
-        got = flip(send, "blk", 2)
-        at_owner, _ = tie((at_owner, send))
-        canvas, *rims = owner(at_owner)
+            add_near, [shape(part, F32), shape(part, BF16)], [VMEM] * 2, [], (1, 1), "add_near",
+        )(kept, near_got)
+        got.append(flip(send, "blk", 1))
         message = shape((PART, FULL), BF16)
         wider = shape((PART + RIM, FULL), BF16)
         own, *wides = call(
-            add_workers, [message, wider, wider], [VMEM] * 4, [], (1, 1), "add_workers",
-        )(keep, got, *rims)
-        got_2, got_1 = flip(wides[1], "blk", 2), flip(wides[0], "blk", 1)
-        across = [swap(own, "col")]
-        got_2, across = tie((got_2, across))
-        got = [got_1, got_2, flip(got_2, "blk", 1)]
-        across += [swap(got_1, "col"), swap(got_2, "col")]
+            add_workers, [message, wider, wider], [VMEM] * 6, [], (1, 1), "add_workers",
+        )(keep, *got, *rims)
+        got = [flip(value, "blk", k) for k, value in ((3, wides[1]), (2, own), (1, wides[0]))][::-1]
+        across = [swap(own, "col"), swap(got[0][:PART], "col")]
         got, across = tie((got[::-1], across))
         got = got[::-1]
         last = call(
@@ -607,7 +588,7 @@
             [pltpu.VMEM((RIM, FULL), F32), pltpu.VMEM((64, HALF), F32)],
             (1, 1), "column_message",
         )(canvas.reshape(HIGH * WIDE, HALF), got[0], got[2])
-        across += [swap(last, "col")]
+        across += [swap(got[1], "col"), swap(last, "col")]
         grad_in = call(
             close, shape(grad_out.shape, BF16), [VMEM] * 5,
             [pltpu.VMEM((TILE_ROWS * BLOCK * 32, HALF), F32)], (1, 1), "close",

time: 95.6 us -> 92.1 us (0.963)
  waiting for transfers between devices: 50.4 us -> 45.6 us
  starting transfers between devices: 21.1 us -> 22.4 us
    ppermute x18 -> x17, waiting for transfers between devices: 23.9 us -> 10.8 us  [swap(): return lax.ppermute(value, axis, [(0, 1), (1, 0)])]
    ppermute x12, waiting for transfers between devices: 26.5 us -> 34.8 us  [flip(): return lax.ppermute(value, axis, [(i, i ^ step) for i in range(size)])]
    ppermute x12, starting transfers between devices: 11.1 us -> 14.7 us  [flip(): return lax.ppermute(value, axis, [(i, i ^ step) for i in range(size)])]
    ppermute x18 -> x17, starting transfers between devices: 10 us -> 7.65 us  [swap(): return lax.ppermute(value, axis, [(0, 1), (1, 0)])]
  transfers between devices with their start and end apart: 30 -> 29, of which waited for: 21 -> 15; matrix products, arithmetic and copies ran while one was open for 0% -> 0% of each run, Pallas kernels for 20% -> 21%
where the time goes in v8:
time: 92.1 us; the launch traced here: 91.9 us
  waiting for transfers between devices  45.6 us (50%)
  starting transfers between devices  22.4 us (24%)
  Pallas kernels  21.4 us (23%)
  local copies, waits for them, and re-layouts  1.71 us (2%)
    ppermute x12, waiting for transfers between devices, flip(): return lax.ppermute(value, axis, [(i, i ^ step) for i in range(size)])  34.8 us
    ppermute x12, starting transfers between devices, flip(): return lax.ppermute(value, axis, [(i, i ^ step) for i in range(size)])  14.7 us
    ppermute x17, waiting for transfers between devices, swap(): return lax.ppermute(value, axis, [(0, 1), (1, 0)])  10.8 us
    ppermute x17, starting transfers between devices, swap(): return lax.ppermute(value, axis, [(0, 1), (1, 0)])  7.65 us
    pallas_call x1, Pallas kernels, shards(): call(functools.partial(worker, scale, owners, capacity, permuted), halved...  6.58 us
    pallas_call x1, Pallas kernels, owner(): call(functools.partial(owner_canvas, owners, capacity, wide, permuted), [...  5.54 us
    pallas_call x1, Pallas kernels, shards(): call(owner_spread, shape((MIDDLE, MIDDLE, TILE_BLOCKS, FULL), BF16), [VME...  2.93 us
    pallas_call x1, Pallas kernels, shards(): call(functools.partial(pack_cotangents, owners, capacity, permuted), piec...  1.92 us
  transfers between devices with their start and end apart: 29, of which 15 were waited for; matrix products, arithmetic and copies ran while one was open for 0% of the time, Pallas kernels for 21%

profile of v8, /device:TPU:0, one launch (start us, length us, event | category | flops | bytes accessed | tf_op | source)
XLA Modules:
  0.0 91.9 jit_solution(4339643185508090086)
XLA Ops:
  1.8 1.9 %pack_cotangents.1 = (bf16[8,64,128]{2,1,0:T(8,128)(2,1)S(1)}, bf16[8,64,128]{2,1,0:T(8,128)(2,1)S(1)}, bf16[8,64,128]{2,1,0:T(8,128)(2,1)S(1)}, bf16[8,64,128]{2,1,0:T(8,128)(2,1)S(1)}) custom-call(s32[4,16]{1,0:T(4,128)S(1)} %bitcast.18, bf16[8,8,32,128]{3,2,1,0:T(8,128)(2,1)} %bitcast.12), custom_call_target="tpu_custom_call" | custom-call | flops 1 | bytes 1 | tf_op jit(solution)/shard_map/pack_cotangents/pallas_call | solution.py:483
  3.8 4.7 %collective-permute-start = (bf16[8,64,128]{2,1,0:T(8,128)(2,1)S(1)}, bf16[8,64,128]{2,1,0:T(8,128)(2,1)S(1)}, u32[]{:S(2)}, u32[]{:S(2)}) collective-permute-start(bf16[8,64,128]{2,1,0:T(8,128)(2,1)S(1)} %get-tuple-element.63), channel_id=1, source_target_pairs={{0,12},{4,8},{8,4},{12,0},{1,13},{5,9},{9,5},{13,1},{2,14},{6,10},... | collective-permute-start | bytes 393224 | tf_op jit(solution)/shard_map/ppermute | solution.py:450
  10.1 1.6 %pack_saved.1 = (bf16[10,160,128]{2,1,0:T(8,128)(2,1)S(1)}, bf16[10,80,128]{2,1,0:T(8,128)(2,1)S(1)}, bf16[10,80,128]{2,1,0:T(8,128)(2,1)S(1)}, bf16[10,80,128]{2,1,0:T(8,128)(2,1)S(1)}, bf16[10,80,128]{2,1,0:T(8,128)(2,1)S(1)}) custom-call(s32[4,16]{1,0:T(4,128)S(1)} %bitcast.19, bf16[10,160,128]{2,1,0:T(8,128)(2,1)S(1)} %bitcast.17), custom_call_target="tpu_custom_call" | custom-call | flops 1 | bytes 1 | tf_op jit(solution)/shard_map/pack_saved/pallas_call | solution.py:493
  12.9 7.2 %collective-permute-done.1.refs_2_ = bf16[8,64,128]{2,1,0:T(8,128)(2,1)S(1)} collective-permute-done((bf16[8,64,128]{2,1,0:T(8,128)(2,1)S(1)}, bf16[8,64,128]{2,1,0:T(8,128)(2,1)S(1)}, u32[]{:S(2)}, u32[]{:S(2)}) %collective-permute-start.1) | collective-permute-done | bytes 131104 | tf_op jit(solution)/shard_map/ppermute | solution.py:450
  22.7 1.5 %collective-permute-done.6.refs_7_ = bf16[8,64,128]{2,1,0:T(8,128)(2,1)S(1)} collective-permute-done((bf16[8,64,128]{2,1,0:T(8,128)(2,1)S(1)}, bf16[8,64,128]{2,1,0:T(8,128)(2,1)S(1)}, u32[]{:S(2)}, u32[]{:S(2)}) %collective-permute-start.6) | collective-permute-done | bytes 131104 | tf_op jit(solution)/shard_map/ppermute | solution.py:445
  24.2 6.6 %worker.1 = (f32[4,2,9,16,256]{4,3,2,1,0:T(8,128)S(1)}, bf16[2,2,9,16,256]{4,3,2,1,0:T(8,128)(2,1)S(1)}, bf16[2,2,9,16,256]{4,3,2,1,0:T(8,128)(2,1)S(1)}) custom-call(s32[4,16]{1,0:T(4,128)S(1)} %bitcast.20, bf16[8,64,128]{2,1,0:T(8,128)(2,1)S(1)} %get-tuple-element.73.refs_0_, bf16[8,64,128]{2,1,0:T(8,128)(2,1)S(1)} %collective-permute-done.2.refs_1_, ...), custom_call_target="tpu_custom_call" | custom-call | flops 1 | bytes 1 | tf_op jit(solution)/shard_map/worker/pallas_call | solution.py:511
  30.8 3.9 %collective-permute-done.10.refs_2_ = bf16[10,80,128]{2,1,0:T(8,128)(2,1)S(1)} collective-permute-done((bf16[10,80,128]{2,1,0:T(8,128)(2,1)S(1)}, bf16[10,80,128]{2,1,0:T(8,128)(2,1)S(1)}, u32[]{:S(2)}, u32[]{:S(2)}) %collective-permute-start.10) | collective-permute-done | bytes 204832 | tf_op jit(solution)/shard_map/ppermute | solution.py:450
  34.7 1.5 %collective-permute-start.12 = (bf16[2,2,9,16,256]{4,3,2,1,0:T(8,128)(2,1)S(1)}, bf16[2,2,9,16,256]{4,3,2,1,0:T(8,128)(2,1)S(1)}, u32[]{:S(2)}, u32[]{:S(2)}) collective-permute-start(bf16[2,2,9,16,256]{4,3,2,1,0:T(8,128)(2,1)S(1)} %get-tuple-element.86), channel_id=1, source_target_pairs={{0,2},{2,0},{1,3},{3,1},{4,6},{6,4},{5,7},{7,5},{8,10},{10,8},{9,1... | collective-permute-start | bytes 884744 | tf_op jit(solution)/shard_map/ppermute | solution.py:445
  36.2 1.3 %collective-permute-start.13 = (bf16[10,80,128]{2,1,0:T(8,128)(2,1)S(1)}, bf16[10,80,128]{2,1,0:T(8,128)(2,1)S(1)}, u32[]{:S(2)}, u32[]{:S(2)}) collective-permute-start(bf16[10,80,128]{2,1,0:T(8,128)(2,1)S(1)} %get-tuple-element.90), channel_id=1, source_target_pairs={{0,12},{4,8},{8,4},{12,0},{1,13},{5,9},{9,5},{13,1},{2,14},{6,10},... | collective-permute-start | bytes 614408 | tf_op jit(solution)/shard_map/ppermute | solution.py:450
  38.1 2.9 %owner_spread.1.refs_8_ = bf16[10,10,32,256]{3,2,1,0:T(8,128)(2,1)S(1)} custom-call(bf16[8,8,32,128]{3,2,1,0:T(8,128)(2,1)S(1)} %bitcast.14, bf16[8,8,32,128]{3,2,1,0:T(8,128)(2,1)S(1)} %collective-permute-done.11.tile_other, bf16[9,128,256]{2,1,0:T(8,128)(2,1)S(1)} %copy-done.1, bf16[9,128,256]{2,1,0:T(8,128)(2,1)S(1)} %collective-permute-done.8.refs_11_.second_other), custom_call_target="tpu_custom_call" | custom-call | flops 1 | bytes 1 | tf_op jit(solution)/shard_map/owner_spread/pallas_call | solution.py:537
  41.1 3.5 %collective-permute-done.12.got = bf16[2,2,9,16,256]{4,3,2,1,0:T(8,128)(2,1)S(1)} collective-permute-done((bf16[2,2,9,16,256]{4,3,2,1,0:T(8,128)(2,1)S(1)}, bf16[2,2,9,16,256]{4,3,2,1,0:T(8,128)(2,1)S(1)}, u32[]{:S(2)}, u32[]{:S(2)}) %collective-permute-start.12) | collective-permute-done | bytes 294944 | tf_op jit(solution)/shard_map/ppermute | solution.py:445
  44.7 1.3 %collective-permute-done.13.refs_3_ = bf16[10,80,128]{2,1,0:T(8,128)(2,1)S(1)} collective-permute-done((bf16[10,80,128]{2,1,0:T(8,128)(2,1)S(1)}, bf16[10,80,128]{2,1,0:T(8,128)(2,1)S(1)}, u32[]{:S(2)}, u32[]{:S(2)}) %collective-permute-start.13) | collective-permute-done | bytes 204832 | tf_op jit(solution)/shard_map/ppermute | solution.py:450
  46.0 2.4 %collective-permute-done.14.refs_1_ = bf16[10,80,128]{2,1,0:T(8,128)(2,1)S(1)} collective-permute-done((bf16[10,80,128]{2,1,0:T(8,128)(2,1)S(1)}, bf16[10,80,128]{2,1,0:T(8,128)(2,1)S(1)}, u32[]{:S(2)}, u32[]{:S(2)}) %collective-permute-start.14) | collective-permute-done | bytes 204832 | tf_op jit(solution)/shard_map/ppermute | solution.py:450
  49.0 2.2 %collective-permute-start.19 = (bf16[2,9,16,256]{3,2,1,0:T(8,128)(2,1)S(1)}, bf16[2,9,16,256]{3,2,1,0:T(8,128)(2,1)S(1)}, u32[]{:S(2)}, u32[]{:S(2)}) collective-permute-start(bf16[2,9,16,256]{3,2,1,0:T(8,128)(2,1)S(1)} %get-tuple-element.100), channel_id=1, source_target_pairs={{0,12},{4,8},{8,4},{12,0},{1,13},{5,9},{9,5},{13,1},{2,14},{6,10},... | collective-permute-start | bytes 442376 | tf_op jit(solution)/shard_map/ppermute | solution.py:450
  51.2 5.5 %owner_canvas.1 = (f32[68,40,128]{2,1,0:T(8,128)S(1)}, bf16[48,256]{1,0:T(8,128)(2,1)S(1)}, bf16[48,256]{1,0:T(8,128)(2,1)S(1)}) custom-call(s32[4,16]{1,0:T(4,128)S(1)} %bitcast.21, bf16[10,80,128]{2,1,0:T(8,128)(2,1)S(1)} %get-tuple-element.79.refs_0_, bf16[10,80,128]{2,1,0:T(8,128)(2,1)S(1)} %collective-permute-done.14.refs_1_, ...), custom_call_target="tpu_custom_call" | custom-call | flops 1 | bytes 1 | tf_op jit(solution)/shard_map/owner_canvas/pallas_call | solution.py:551
  56.8 2.3 %collective-permute-start.21 = (bf16[2,9,16,256]{3,2,1,0:T(8,128)(2,1)S(1)}, bf16[2,9,16,256]{3,2,1,0:T(8,128)(2,1)S(1)}, u32[]{:S(2)}, u32[]{:S(2)}) collective-permute-start(bf16[2,9,16,256]{3,2,1,0:T(8,128)(2,1)S(1)} %get-tuple-element.102), channel_id=1, source_target_pairs={{0,4},{4,0},{8,12},{12,8},{1,5},{5,1},{9,13},{13,9},{2,6},{6,2},{1... | collective-permute-start | bytes 442376 | tf_op jit(solution)/shard_map/ppermute | solution.py:450
  59.1 5.0 %collective-permute-done.20.got_2 = bf16[2,9,16,256]{3,2,1,0:T(8,128)(2,1)S(1)} collective-permute-done((bf16[2,9,16,256]{3,2,1,0:T(8,128)(2,1)S(1)}, bf16[2,9,16,256]{3,2,1,0:T(8,128)(2,1)S(1)}, u32[]{:S(2)}, u32[]{:S(2)}) %collective-permute-start.20) | collective-permute-done | bytes 147488 | tf_op jit(solution)/shard_map/ppermute | solution.py:450
  64.1 1.6 %collective-permute-done.21.got_1 = bf16[2,9,16,256]{3,2,1,0:T(8,128)(2,1)S(1)} collective-permute-done((bf16[2,9,16,256]{3,2,1,0:T(8,128)(2,1)S(1)}, bf16[2,9,16,256]{3,2,1,0:T(8,128)(2,1)S(1)}, u32[]{:S(2)}, u32[]{:S(2)}) %collective-permute-start.21) | collective-permute-done | bytes 147488 | tf_op jit(solution)/shard_map/ppermute | solution.py:450
  65.8 2.3 %collective-permute-start.22 = (bf16[336,256]{1,0:T(8,128)(2,1)S(1)}, bf16[336,256]{1,0:T(8,128)(2,1)S(1)}, u32[]{:S(2)}, u32[]{:S(2)}) collective-permute-start(bf16[336,256]{1,0:T(8,128)(2,1)S(1)} %get-tuple-element.105), channel_id=1, source_target_pairs={{0,12},{4,8},{8,4},{12,0},{1,13},{5,9},{9,5},{13,1},{2,14},{6,10},... | collective-permute-start | bytes 516104 | tf_op jit(solution)/shard_map/ppermute | solution.py:450
  69.8 3.8 %collective-permute-done.24.got_1.refs_1_ = bf16[336,256]{1,0:T(8,128)(2,1)S(1)} collective-permute-done((bf16[336,256]{1,0:T(8,128)(2,1)S(1)}, bf16[336,256]{1,0:T(8,128)(2,1)S(1)}, u32[]{:S(2)}, u32[]{:S(2)}) %collective-permute-start.24) | collective-permute-done | bytes 172064 | tf_op jit(solution)/shard_map/ppermute | solution.py:450
  74.3 8.2 %collective-permute-done.23.refs_2_ = bf16[288,256]{1,0:T(8,128)(2,1)S(1)} collective-permute-done((bf16[288,256]{1,0:T(8,128)(2,1)S(1)}, bf16[288,256]{1,0:T(8,128)(2,1)S(1)}, u32[]{:S(2)}, u32[]{:S(2)}) %collective-permute-start.23) | collective-permute-done | bytes 147488 | tf_op jit(solution)/shard_map/ppermute | solution.py:450
  83.2 1.5 %collective-permute-start.28 = (bf16[288,256]{1,0:T(8,128)(2,1)S(1)}, bf16[288,256]{1,0:T(8,128)(2,1)S(1)}, u32[]{:S(2)}, u32[]{:S(2)}) collective-permute-start(bf16[288,256]{1,0:T(8,128)(2,1)S(1)} %collective-permute-done.23.refs_2_), channel_id=1, source_target_pairs={{0,2},{2,0},{1,3},{3,1},{4,6},{6,4},{5,7},{7,5},{8,10},{10,8},{9,1... | collective-permute-start | bytes 442376 | tf_op jit(solution)/shard_map/ppermute | solution.py:445
  84.6 4.1 %collective-permute-done.27.across.refs_7_ = bf16[352,256]{1,0:T(8,128)(2,1)S(1)} collective-permute-done((bf16[352,256]{1,0:T(8,128)(2,1)S(1)}, bf16[352,256]{1,0:T(8,128)(2,1)S(1)}, u32[]{:S(2)}, u32[]{:S(2)}) %collective-permute-start.27) | collective-permute-done | bytes 180256 | tf_op jit(solution)/shard_map/ppermute | solution.py:445
  90.4 1.6 %lay.1 = (f32[9,128,256]{2,1,0:T(8,128)}, f32[9,128,256]{2,1,0:T(8,128)}) custom-call(bf16[288,256]{1,0:T(8,128)(2,1)S(1)} %get-tuple-element.106.refs_0_, bf16[336,256]{1,0:T(8,128)(2,1)S(1)} %collective-permute-done.24.got_1.refs_1_, bf16[288,256]{1,0:T(8,128)(2,1)S(1)} %collective-permute-done.23.refs_2_, ...), custom_call_target="tpu_custom_call" | custom-call | flops 1 | bytes 1 | tf_op jit(solution)/shard_map/lay/pallas_call | solution.py:596
  (58 shorter events, 12.6 us)
Async XLA Ops:
  0.6 23.6 %collective-permute-start.8 = (bf16[9,128,256]{2,1,0:T(8,128)(2,1)}, bf16[9,128,256]{2,1,0:T(8,128)(2,1)S(1)}, u32[]{:S(2)}, u32[]{:S(2)}) collective-permute-start(bf16[9,128,256]{2,1,0:T(8,128)(2,1)} %second.1), channel_id=1, source_target_pairs={{0,1},{1,0},{2,3},{3,2},{4,5},{5,4},{6,7},{7,6},{8,9},{9,8},{10,11... | collective-permute-start | bytes 1769480 | tf_op jit(solution)/shard_map/ppermute | solution.py:445
  3.8 9.2 %collective-permute-start = (bf16[8,64,128]{2,1,0:T(8,128)(2,1)S(1)}, bf16[8,64,128]{2,1,0:T(8,128)(2,1)S(1)}, u32[]{:S(2)}, u32[]{:S(2)}) collective-permute-start(bf16[8,64,128]{2,1,0:T(8,128)(2,1)S(1)} %get-tuple-element.63), channel_id=1, source_target_pairs={{0,12},{4,8},{8,4},{12,0},{1,13},{5,9},{9,5},{13,1},{2,14},{6,10},... | collective-permute-start | bytes 393224 | tf_op jit(solution)/shard_map/ppermute | solution.py:450
  8.5 11.7 %collective-permute-start.1 = (bf16[8,64,128]{2,1,0:T(8,128)(2,1)S(1)}, bf16[8,64,128]{2,1,0:T(8,128)(2,1)S(1)}, u32[]{:S(2)}, u32[]{:S(2)}) collective-permute-start(bf16[8,64,128]{2,1,0:T(8,128)(2,1)S(1)} %get-tuple-element.64), channel_id=1, source_target_pairs={{0,8},{4,12},{8,0},{12,4},{1,9},{5,13},{9,1},{13,5},{2,10},{6,14},... | collective-permute-start | bytes 393224 | tf_op jit(solution)/shard_map/ppermute | solution.py:450
  8.5 11.7 %collective-permute-start.2 = (bf16[8,64,128]{2,1,0:T(8,128)(2,1)S(1)}, bf16[8,64,128]{2,1,0:T(8,128)(2,1)S(1)}, u32[]{:S(2)}, u32[]{:S(2)}) collective-permute-start(bf16[8,64,128]{2,1,0:T(8,128)(2,1)S(1)} %get-tuple-element.65), channel_id=1, source_target_pairs={{0,4},{4,0},{8,12},{12,8},{1,5},{5,1},{9,13},{13,9},{2,6},{6,2},{1... | collective-permute-start | bytes 393224 | tf_op jit(solution)/shard_map/ppermute | solution.py:450
  20.2 4.0 %collective-permute-start.7 = (bf16[10,10,16,128]{3,2,1,0:T(8,128)(2,1)S(1)}, bf16[10,10,16,128]{3,2,1,0:T(8,128)(2,1)S(1)}, u32[]{:S(2)}, u32[]{:S(2)}) collective-permute-start(bf16[10,10,16,128]{3,2,1,0:T(8,128)(2,1)S(1)} %bitcast.15), channel_id=1, source_target_pairs={{0,1},{1,0},{2,3},{3,2},{4,5},{5,4},{6,7},{7,6},{8,9},{9,8},{10,11... | collective-permute-start | bytes 1228808 | tf_op jit(solution)/shard_map/ppermute | solution.py:445
  22.1 16.0 %collective-permute-start.11 = (bf16[8,8,32,128]{3,2,1,0:T(8,128)(2,1)}, bf16[8,8,32,128]{3,2,1,0:T(8,128)(2,1)S(1)}, u32[]{:S(2)}, u32[]{:S(2)}) collective-permute-start(bf16[8,8,32,128]{3,2,1,0:T(8,128)(2,1)} %bitcast.13), channel_id=1, source_target_pairs={{0,1},{1,0},{2,3},{3,2},{4,5},{5,4},{6,7},{7,6},{8,9},{9,8},{10,11... | collective-permute-start | bytes 1572872 | tf_op jit(solution)/shard_map/ppermute | solution.py:445
  22.3 12.4 %collective-permute-start.10 = (bf16[10,80,128]{2,1,0:T(8,128)(2,1)S(1)}, bf16[10,80,128]{2,1,0:T(8,128)(2,1)S(1)}, u32[]{:S(2)}, u32[]{:S(2)}) collective-permute-start(bf16[10,80,128]{2,1,0:T(8,128)(2,1)S(1)} %get-tuple-element.82), channel_id=1, source_target_pairs={{0,8},{4,12},{8,0},{12,4},{1,9},{5,13},{9,1},{13,5},{2,10},{6,14},... | collective-permute-start | bytes 614408 | tf_op jit(solution)/shard_map/ppermute | solution.py:450
  34.7 9.9 %collective-permute-start.12 = (bf16[2,2,9,16,256]{4,3,2,1,0:T(8,128)(2,1)S(1)}, bf16[2,2,9,16,256]{4,3,2,1,0:T(8,128)(2,1)S(1)}, u32[]{:S(2)}, u32[]{:S(2)}) collective-permute-start(bf16[2,2,9,16,256]{4,3,2,1,0:T(8,128)(2,1)S(1)} %get-tuple-element.86), channel_id=1, source_target_pairs={{0,2},{2,0},{1,3},{3,1},{4,6},{6,4},{5,7},{7,5},{8,10},{10,8},{9,1... | collective-permute-start | bytes 884744 | tf_op jit(solution)/shard_map/ppermute | solution.py:445
  36.2 9.8 %collective-permute-start.13 = (bf16[10,80,128]{2,1,0:T(8,128)(2,1)S(1)}, bf16[10,80,128]{2,1,0:T(8,128)(2,1)S(1)}, u32[]{:S(2)}, u32[]{:S(2)}) collective-permute-start(bf16[10,80,128]{2,1,0:T(8,128)(2,1)S(1)} %get-tuple-element.90), channel_id=1, source_target_pairs={{0,12},{4,8},{8,4},{12,0},{1,13},{5,9},{9,5},{13,1},{2,14},{6,10},... | collective-permute-start | bytes 614408 | tf_op jit(solution)/shard_map/ppermute | solution.py:450
  37.6 10.9 %collective-permute-start.14 = (bf16[10,80,128]{2,1,0:T(8,128)(2,1)S(1)}, bf16[10,80,128]{2,1,0:T(8,128)(2,1)S(1)}, u32[]{:S(2)}, u32[]{:S(2)}) collective-permute-start(bf16[10,80,128]{2,1,0:T(8,128)(2,1)S(1)} %get-tuple-element.91), channel_id=1, source_target_pairs={{0,4},{4,0},{8,12},{12,8},{1,5},{5,1},{9,13},{13,9},{2,6},{6,2},{1... | collective-permute-start | bytes 614408 | tf_op jit(solution)/shard_map/ppermute | solution.py:450
  37.6 19.2 %collective-permute-start.9 = (bf16[2,2,9,16,256]{4,3,2,1,0:T(8,128)(2,1)S(1)}, bf16[2,2,9,16,256]{4,3,2,1,0:T(8,128)(2,1)S(1)}, u32[]{:S(2)}, u32[]{:S(2)}) collective-permute-start(bf16[2,2,9,16,256]{4,3,2,1,0:T(8,128)(2,1)S(1)} %get-tuple-element.78), channel_id=1, source_target_pairs={{0,2},{2,0},{1,3},{3,1},{4,6},{6,4},{5,7},{7,5},{8,10},{10,8},{9,1... | collective-permute-start | bytes 884744 | tf_op jit(solution)/shard_map/ppermute | solution.py:445
  38.1 10.8 %collective-permute-start.15 = (bf16[10,80,128]{2,1,0:T(8,128)(2,1)S(1)}, bf16[10,80,128]{2,1,0:T(8,128)(2,1)S(1)}, u32[]{:S(2)}, u32[]{:S(2)}) collective-permute-start(bf16[10,80,128]{2,1,0:T(8,128)(2,1)S(1)} %get-tuple-element.79.refs_0_), channel_id=1, source_target_pairs={{0,1},{1,0},{2,3},{3,2},{4,5},{5,4},{6,7},{7,6},{8,9},{9,8},{10,11... | collective-permute-start | bytes 614408 | tf_op jit(solution)/shard_map/ppermute | solution.py:445
  44.6 6.5 %collective-permute-start.17 = (bf16[10,80,128]{2,1,0:T(8,128)(2,1)S(1)}, bf16[10,80,128]{2,1,0:T(8,128)(2,1)S(1)}, u32[]{:S(2)}, u32[]{:S(2)}) collective-permute-start(bf16[10,80,128]{2,1,0:T(8,128)(2,1)S(1)} %collective-permute-done.10.refs_2_), channel_id=1, source_target_pairs={{0,1},{1,0},{2,3},{3,2},{4,5},{5,4},{6,7},{7,6},{8,9},{9,8},{10,11... | collective-permute-start | bytes 614408 | tf_op jit(solution)/shard_map/ppermute | solution.py:445
  48.4 2.7 %collective-permute-start.18 = (bf16[10,80,128]{2,1,0:T(8,128)(2,1)S(1)}, bf16[10,80,128]{2,1,0:T(8,128)(2,1)S(1)}, u32[]{:S(2)}, u32[]{:S(2)}) collective-permute-start(bf16[10,80,128]{2,1,0:T(8,128)(2,1)S(1)} %collective-permute-done.13.refs_3_), channel_id=1, source_target_pairs={{0,1},{1,0},{2,3},{3,2},{4,5},{5,4},{6,7},{7,6},{8,9},{9,8},{10,11... | collective-permute-start | bytes 614408 | tf_op jit(solution)/shard_map/ppermute | solution.py:445
  49.0 10.1 %collective-permute-start.19 = (bf16[2,9,16,256]{3,2,1,0:T(8,128)(2,1)S(1)}, bf16[2,9,16,256]{3,2,1,0:T(8,128)(2,1)S(1)}, u32[]{:S(2)}, u32[]{:S(2)}) collective-permute-start(bf16[2,9,16,256]{3,2,1,0:T(8,128)(2,1)S(1)} %get-tuple-element.100), channel_id=1, source_target_pairs={{0,12},{4,8},{8,4},{12,0},{1,13},{5,9},{9,5},{13,1},{2,14},{6,10},... | collective-permute-start | bytes 442376 | tf_op jit(solution)/shard_map/ppermute | solution.py:450
  51.1 13.0 %collective-permute-start.20 = (bf16[2,9,16,256]{3,2,1,0:T(8,128)(2,1)S(1)}, bf16[2,9,16,256]{3,2,1,0:T(8,128)(2,1)S(1)}, u32[]{:S(2)}, u32[]{:S(2)}) collective-permute-start(bf16[2,9,16,256]{3,2,1,0:T(8,128)(2,1)S(1)} %get-tuple-element.101), channel_id=1, source_target_pairs={{0,8},{4,12},{8,0},{12,4},{1,9},{5,13},{9,1},{13,5},{2,10},{6,14},... | collective-permute-start | bytes 442376 | tf_op jit(solution)/shard_map/ppermute | solution.py:450
  56.8 8.9 %collective-permute-start.21 = (bf16[2,9,16,256]{3,2,1,0:T(8,128)(2,1)S(1)}, bf16[2,9,16,256]{3,2,1,0:T(8,128)(2,1)S(1)}, u32[]{:S(2)}, u32[]{:S(2)}) collective-permute-start(bf16[2,9,16,256]{3,2,1,0:T(8,128)(2,1)S(1)} %get-tuple-element.102), channel_id=1, source_target_pairs={{0,4},{4,0},{8,12},{12,8},{1,5},{5,1},{9,13},{13,9},{2,6},{6,2},{1... | collective-permute-start | bytes 442376 | tf_op jit(solution)/shard_map/ppermute | solution.py:450
  65.8 7.9 %collective-permute-start.24 = (bf16[336,256]{1,0:T(8,128)(2,1)S(1)}, bf16[336,256]{1,0:T(8,128)(2,1)S(1)}, u32[]{:S(2)}, u32[]{:S(2)}) collective-permute-start(bf16[336,256]{1,0:T(8,128)(2,1)S(1)} %get-tuple-element.107), channel_id=1, source_target_pairs={{0,4},{4,0},{8,12},{12,8},{1,5},{5,1},{9,13},{13,9},{2,6},{6,2},{1... | collective-permute-start | bytes 516104 | tf_op jit(solution)/shard_map/ppermute | solution.py:450
  65.8 16.7 %collective-permute-start.22 = (bf16[336,256]{1,0:T(8,128)(2,1)S(1)}, bf16[336,256]{1,0:T(8,128)(2,1)S(1)}, u32[]{:S(2)}, u32[]{:S(2)}) collective-permute-start(bf16[336,256]{1,0:T(8,128)(2,1)S(1)} %get-tuple-element.105), channel_id=1, source_target_pairs={{0,12},{4,8},{8,4},{12,0},{1,13},{5,9},{9,5},{13,1},{2,14},{6,10},... | collective-permute-start | bytes 516104 | tf_op jit(solution)/shard_map/ppermute | solution.py:450
  68.1 6.2 %collective-permute-start.25 = (bf16[288,256]{1,0:T(8,128)(2,1)S(1)}, bf16[288,256]{1,0:T(8,128)(2,1)S(1)}, u32[]{:S(2)}, u32[]{:S(2)}) collective-permute-start(bf16[288,256]{1,0:T(8,128)(2,1)S(1)} %get-tuple-element.106.refs_0_), channel_id=1, source_target_pairs={{0,2},{2,0},{1,3},{3,1},{4,6},{6,4},{5,7},{7,5},{8,10},{10,8},{9,1... | collective-permute-start | bytes 442376 | tf_op jit(solution)/shard_map/ppermute | solution.py:445
  68.6 13.9 %collective-permute-start.23 = (bf16[288,256]{1,0:T(8,128)(2,1)S(1)}, bf16[288,256]{1,0:T(8,128)(2,1)S(1)}, u32[]{:S(2)}, u32[]{:S(2)}) collective-permute-start(bf16[288,256]{1,0:T(8,128)(2,1)S(1)} %get-tuple-element.106.refs_0_), channel_id=1, source_target_pairs={{0,8},{4,12},{8,0},{12,4},{1,9},{5,13},{9,1},{13,5},{2,10},{6,14},... | collective-permute-start | bytes 442376 | tf_op jit(solution)/shard_map/ppermute | solution.py:450
  73.7 8.8 %collective-permute-start.26 = (bf16[288,256]{1,0:T(8,128)(2,1)S(1)}, bf16[288,256]{1,0:T(8,128)(2,1)S(1)}, u32[]{:S(2)}, u32[]{:S(2)}) collective-permute-start(bf16[288,256]{1,0:T(8,128)(2,1)S(1)} %slice.4), channel_id=1, source_target_pairs={{0,2},{2,0},{1,3},{3,1},{4,6},{6,4},{5,7},{7,5},{8,10},{10,8},{9,1... | collective-permute-start | bytes 442376 | tf_op jit(solution)/shard_map/ppermute | solution.py:445
  82.6 6.2 %collective-permute-start.27 = (bf16[352,256]{1,0:T(8,128)(2,1)S(1)}, bf16[352,256]{1,0:T(8,128)(2,1)S(1)}, u32[]{:S(2)}, u32[]{:S(2)}) collective-permute-start(bf16[352,256]{1,0:T(8,128)(2,1)S(1)} %column_message.1), channel_id=1, source_target_pairs={{0,2},{2,0},{1,3},{3,1},{4,6},{6,4},{5,7},{7,5},{8,10},{10,8},{9,1... | collective-permute-start | bytes 540680 | tf_op jit(solution)/shard_map/ppermute | solution.py:445
  83.2 7.2 %collective-permute-start.28 = (bf16[288,256]{1,0:T(8,128)(2,1)S(1)}, bf16[288,256]{1,0:T(8,128)(2,1)S(1)}, u32[]{:S(2)}, u32[]{:S(2)}) collective-permute-start(bf16[288,256]{1,0:T(8,128)(2,1)S(1)} %collective-permute-done.23.refs_2_), channel_id=1, source_target_pairs={{0,2},{2,0},{1,3},{3,1},{4,6},{6,4},{5,7},{7,5},{8,10},{10,8},{9,1... | collective-permute-start | bytes 442376 | tf_op jit(solution)/shard_map/ppermute | solution.py:445
  (11 other events, 69.1 us)

commit v9 on v8

--- a/solution.py
+++ b/solution.py
@@ -141,21 +141,11 @@
             out[u + 1] = part[:, HALF:]
 
 
-def pack_saved(owners, columns, capacity, wide, permuted, routing, saved, masked, *refs):
-    outs, counts, table = refs[:-2], refs[-2], refs[-1]
+def outside_image(slots, owners, columns):
     column = lax.axis_index("col")
-
-    def clear(number, carry):
-        table[number] = DEAD
-        return carry
-
-    lax.fori_loop(0, owners * capacity, clear, 0)
-    slots = worker_codes(routing, counts, owners)
-    rows = MIDDLE * PER_WORKER
-    row = iota((rows, HALF), 0)
-    flags = jnp.zeros((rows, HALF), I32)
+    row = iota((MIDDLE * PER_WORKER, HALF), 0)
+    flags = jnp.zeros_like(row)
     for slot, (owner, place, rank) in enumerate(slots):
-        table[owner * capacity + rank] = slot
         block_row, block_col = place // TILE_COLS, place % TILE_COLS
         flag = (
             jnp.where((owner == 0) & (block_row == 0), 1, 0)
@@ -165,14 +155,33 @@
         )
         flags = jnp.where(row % PER_WORKER == slot, flag, flags)
     across = row // PER_WORKER
-    outside = (((flags & 4) != 0) & (across == 0)) | (((flags & 8) != 0) & (across == MIDDLE - 1))
+    sides = (((flags & 4) != 0) & (across == 0)) | (((flags & 8) != 0) & (across == MIDDLE - 1))
+
+    def here(m):
+        if m == 0:
+            return sides | ((flags & 1) != 0)
+        if m == MIDDLE - 1:
+            return sides | ((flags & 2) != 0)
+        return sides
+
+    return here
+
+
+def pack_saved(owners, columns, capacity, wide, permuted, routing, saved, masked, *refs):
+    outs, counts, table = refs[:-2], refs[-2], refs[-1]
+
+    def clear(number, carry):
+        table[number] = DEAD
+        return carry
+
+    lax.fori_loop(0, owners * capacity, clear, 0)
+    slots = worker_codes(routing, counts, owners)
+    rows = MIDDLE * PER_WORKER
+    for slot, (owner, place, rank) in enumerate(slots):
+        table[owner * capacity + rank] = slot
+    outside = outside_image(slots, owners, columns)
     for m in range(MIDDLE):
-        here = outside
-        if m == 0:
-            here = here | ((flags & 1) != 0)
-        if m == MIDDLE - 1:
-            here = here | ((flags & 2) != 0)
-        masked[m] = jnp.where(here, 0.0, saved[m].astype(F32)).astype(BF16)
+        masked[m] = jnp.where(outside(m), 0.0, saved[m].astype(F32)).astype(BF16)
     size = wide * capacity
     row, lane = iota((size, FULL), 0), iota((size, FULL), 1)
     picks = []
@@ -237,15 +246,19 @@
         )
         cot[u] = dot(pick, got).astype(BF16)
     grads = cot[...].reshape(BLOCK * rows, FULL)
-    for tap in range(9):
-        dy, dx = tap // 3, tap % 3
-        window = masked[dy : dy + BLOCK, dx : dx + BLOCK].reshape(BLOCK * rows, HALF)
-        window = jnp.maximum(window, jnp.zeros_like(window))
-        emit(dot_tn(window, grads) * scale, outs, 0, tap)
+    for dy in range(3):
+        windows = [
+            masked[dy : dy + BLOCK, dx * PER_WORKER : (dx + BLOCK) * PER_WORKER] for dx in range(3)
+        ]
+        window = jnp.concatenate([w.reshape(BLOCK * rows, HALF) for w in windows], axis=1)
+        value = dot_tn(jnp.maximum(window, jnp.zeros_like(window)), grads) * scale
+        for dx in range(3):
+            emit(value[dx * HALF : (dx + 1) * HALF], outs, 0, 3 * dy + dx)
+    return slots
 
 
 def first_gradient(
-    scale, cot, masked, masked_other, weight, weight_other, saved, *refs
+    scale, outside, cot, masked, saved_other, weight, weight_other, saved, *refs
 ):
     outs, (total, pre, full) = refs[:-3], refs[-3:]
     rows = BLOCK * BLOCK * PER_WORKER
@@ -257,14 +270,18 @@
         spot = (slice(dy, dy + BLOCK), slice(dx, dx + BLOCK))
         total[spot] = total[spot] + part.reshape(BLOCK, BLOCK, PER_WORKER, FULL)
     for m in range(MIDDLE):
-        live = ordered(masked[m], masked_other[m], 2).astype(F32) > 0
-        pre[m] = jnp.where(live, total[m], 0.0).astype(BF16)
+        other = jnp.where(outside(m), 0.0, saved_other[m].astype(F32)).astype(BF16)
+        live = ordered(masked[m], other, 1).astype(F32) > 0
+        value = jnp.where(live, total[m].reshape(MIDDLE * PER_WORKER, FULL), 0.0)
+        pre[m] = value.astype(BF16).reshape(MIDDLE, PER_WORKER, FULL)
     size = MIDDLE * MIDDLE * PER_WORKER
     grads = pre[...].reshape(size, FULL)
-    for tap in range(9):
-        dy, dx = tap // 3, tap % 3
-        window = saved[dy : dy + MIDDLE, dx : dx + MIDDLE].reshape(size, HALF)
-        emit(dot_tn(window, grads) * scale, outs, 1, tap)
+    for dy in range(3):
+        windows = [saved[dy : dy + MIDDLE, dx : dx + MIDDLE] for dx in range(3)]
+        window = jnp.concatenate([w.reshape(size, HALF) for w in windows], axis=1)
+        value = dot_tn(window, grads) * scale
+        for dx in range(3):
+            emit(value[dx * HALF : (dx + 1) * HALF], outs, 1, 3 * dy + dx)
 
 
 def owner_spread(tile, tile_other, second, second_other, out, total, cot, full):
@@ -286,10 +303,10 @@
     out[...] = total[...].astype(BF16)
 
 
-def worker(scale, owners, capacity, permuted, routing, *refs):
+def worker(scale, owners, columns, capacity, permuted, routing, *refs):
     parts = 1 if not permuted else owners
     inputs, refs = refs[: 2 * parts], refs[2 * parts :]
-    (masked, masked_other, weight, weight_other, source), refs = refs[:5], refs[5:]
+    (masked, saved_other, weight, weight_other, source), refs = refs[:5], refs[5:]
     if permuted:
         refs, sent = refs[:-1], refs[-1]
     outs, (counts, cot, total, pre, full, saved, arrived) = refs[:-7], refs[-7:]
@@ -298,10 +315,13 @@
         outs = (kept, sent)
     fetch = pltpu.make_async_copy(source, saved, arrived)
     fetch.start()
-    second_gradient(scale, owners, capacity, permuted, routing, *inputs, masked, cot, *outs, counts)
+    slots = second_gradient(
+        scale, owners, capacity, permuted, routing, *inputs, masked, cot, *outs, counts
+    )
     fetch.wait()
     first_gradient(
-        scale, cot, masked, masked_other, weight, weight_other, saved, *outs, total, pre, full
+        scale, outside_image(slots, owners, columns), cot, masked, saved_other, weight, weight_other,
+        saved, *outs, total, pre, full,
     )
     if permuted:
         near[...] = sent[:2]
@@ -430,15 +450,32 @@
     out[...] = total[...].astype(BF16).reshape(out.shape)
 
 
+def rows_at(number):
+    column = lax.axis_index("col")
+    place = (column if number < 4 else 1 - column) * 4 + partner("blk", number % 4, True)
+    return pl.ds(pl.multiple_of(place * ROWS, ROWS), ROWS)
+
+
 def lay(*refs):
-    outs = refs[-2:]
-    size, column = HALF // 8, lax.axis_index("col")
-    for k, part in enumerate(refs[:-2]):
-        place = (column if k < 4 else 1 - column) * 4 + partner("blk", k % 4, True)
-        at = pl.multiple_of(place * size, size)
-        value = part[:PART].astype(F32).reshape(2, 9, size, FULL)
-        for out, grad in zip(outs, (0, 1)):
-            out[:, pl.ds(at, size), :] = value[grad]
+    for number, part in enumerate(refs[:-2]):
+        value = part[:PART].astype(F32).reshape(2, 9, ROWS, FULL)
+        for out, grad in zip(refs[-2:], (0, 1)):
+            out[:, rows_at(number), :] = value[grad]
+
+
+def finish(tile, canvas, got_1, got_3, last, late, old_0, old_1, out, out_0, out_1, total, laid, sems):
+    copies = []
+    for k, (number, part) in enumerate(((6, late), (7, last))):
+        laid[k] = part[:PART].astype(F32).reshape(2, 9, ROWS, FULL)
+        for grad, dest in enumerate((out_0, out_1)):
+            copy = pltpu.make_async_copy(
+                laid.at[k, grad], dest.at[:, rows_at(number), :], sems.at[k, grad]
+            )
+            copy.start()
+            copies.append(copy)
+    close(tile, canvas, got_1, got_3, last, out, total)
+    for copy in copies:
+        copy.wait()
 
 
 def swap(value, axis="ch"):
@@ -487,19 +524,21 @@
         (1, 1), "pack_cotangents",
     )(routing, pltpu.with_memory_space_constraint(tile, pltpu.HBM))
     saved_slots = saved_pre[0, 0].transpose(1, 2, 0, 3)
-    outgoing, saved_slots = tie((outgoing, saved_slots))
+    saved_slots = saved_slots.reshape(MIDDLE, MIDDLE * PER_WORKER, HALF)
+    outgoing, saved_here = tie((outgoing, saved_slots))
+    saved_other = swap(saved_slots)
     incoming = exchange(outgoing)
 
     masked, *to_owners = call(
         functools.partial(pack_saved, owners, columns, capacity, wide, permuted),
         [shape((MIDDLE, MIDDLE * PER_WORKER, HALF), BF16)] + pieces(MIDDLE, wide * capacity, HALF),
         [SMEM, VMEM], counts + tables, (1, 1), "pack_saved",
-    )(routing, saved_slots.reshape(MIDDLE, MIDDLE * PER_WORKER, HALF))
-    masked = masked.reshape(MIDDLE, MIDDLE, PER_WORKER, HALF)
-    incoming, to_owners, masked = tie((incoming[::-1], to_owners[::-1], masked))
-    incoming, to_owners = incoming[::-1], to_owners[::-1]
-    incoming_other = [swap(value) for value in incoming]
-    masked_other = swap(masked)
+    )(routing, saved_here)
+    incoming_other = [swap(incoming[0])] if permuted else []
+    *rest, to_owners = tie((*incoming[len(incoming_other) :][::-1], to_owners[::-1]))
+    incoming = incoming[: len(incoming_other)] + rest[::-1]
+    to_owners = to_owners[::-1]
+    incoming_other += [swap(value) for value in rest[::-1]]
     at_owner = exchange(to_owners)
 
     saved_tiles = saved_input[0, 0].transpose(1, 2, 0, 3)
@@ -509,7 +548,7 @@
     else:
         halved = [shape((2, 9, HALF, FULL), F32)]
     terms = call(
-        functools.partial(worker, scale, owners, capacity, permuted),
+        functools.partial(worker, scale, owners, columns, capacity, permuted),
         halved,
         [SMEM] + [VMEM] * (2 * parts + 4) + [HBM],
         counts
@@ -524,7 +563,7 @@
         + ([pltpu.VMEM((4,) + part, BF16)] if permuted else []),
         (1, 1), "worker",
     )(
-        routing, *incoming, *incoming_other, masked, masked_other, second_weight, second_other,
+        routing, *incoming, *incoming_other, masked, saved_other, second_weight, second_other,
         pltpu.with_memory_space_constraint(saved_tiles, pltpu.HBM),
     )
 
@@ -579,23 +618,34 @@
         own, *wides = call(
             add_workers, [message, wider, wider], [VMEM] * 6, [], (1, 1), "add_workers",
         )(keep, *got, *rims)
-        got = [flip(value, "blk", k) for k, value in ((3, wides[1]), (2, own), (1, wides[0]))][::-1]
-        across = [swap(own, "col"), swap(got[0][:PART], "col")]
-        got, across = tie((got[::-1], across))
-        got = got[::-1]
+        got_3, got_2, got_1 = flip(wides[1], "blk", 3), flip(own, "blk", 2), flip(wides[0], "blk", 1)
+        across = [swap(own, "col"), swap(got_1[:PART], "col")]
+        got_3, got_2, got_1, across = tie((got_3, got_2, got_1, across))
+        got = [got_1, got_2, got_3]
         last = call(
             column_message, shape((PART + 64, FULL), BF16), [VMEM] * 3,
             [pltpu.VMEM((RIM, FULL), F32), pltpu.VMEM((64, HALF), F32)],
             (1, 1), "column_message",
         )(canvas.reshape(HIGH * WIDE, HALF), got[0], got[2])
         across += [swap(got[1], "col"), swap(last, "col")]
-        grad_in = call(
-            close, shape(grad_out.shape, BF16), [VMEM] * 5,
-            [pltpu.VMEM((TILE_ROWS * BLOCK * 32, HALF), F32)], (1, 1), "close",
-        )(grad_out, canvas, got[0], got[2], across[3])
-        grad_second, grad_first = call(
-            lay, [shape((9, HALF, FULL), F32)] * 2, [VMEM] * 8, [], (1, 1), "lay",
-        )(own, *got, *across)
+        early = call(
+            lay, [shape((9, HALF, FULL), F32)] * 2, [VMEM] * 6, [], (1, 1), "lay",
+        )(own, *got, *across[:2])
+        grad_in, grad_second, grad_first = pl.pallas_call(
+            finish,
+            out_shape=[shape(grad_out.shape, BF16)] + [shape((9, HALF, FULL), F32)] * 2,
+            in_specs=[VMEM] * 6 + [HBM] * 2,
+            out_specs=[VMEM] + [HBM] * 2,
+            scratch_shapes=[
+                pltpu.VMEM((TILE_ROWS * BLOCK * 32, HALF), F32),
+                pltpu.VMEM((2, 2, 9, ROWS, FULL), F32),
+                pltpu.SemaphoreType.DMA((2, 2)),
+            ],
+            input_output_aliases={6: 1, 7: 2},
+            compiler_params=pltpu.CompilerParams(vmem_limit_bytes=48 * 1024 * 1024),
+            cost_estimate=pl.CostEstimate(flops=1, bytes_accessed=1, transcendentals=0),
+            name="finish",
+        )(grad_out, canvas, got[0], got[2], across[3], across[2], *early)
         return (grad_in, grad_first, grad_second)
 
     grad_first, grad_second = lax.psum((terms[0][1], terms[0][0]), ("blk", "col"))

time: 92.1 us -> 91.7 us (level)
  waiting for transfers between devices: 45.6 us -> 42.2 us
  starting transfers between devices: 22.4 us -> 24.7 us
    ppermute x12, starting transfers between devices: 14.7 us -> 17.9 us  [flip(): return lax.ppermute(value, axis, [(i, i ^ step) for i in range(size)])]
    ppermute x17, waiting for transfers between devices: 10.8 us -> 8.85 us  [swap(): return lax.ppermute(value, axis, [(0, 1), (1, 0)])]
    ppermute x12, waiting for transfers between devices: 34.8 us -> 33.3 us  [flip(): return lax.ppermute(value, axis, [(i, i ^ step) for i in range(size)])]
  transfers between devices with their start and end apart: 29 -> 29, of which waited for: 15 -> 13; matrix products, arithmetic and copies ran while one was open for 0% -> 0% of each run, Pallas kernels for 21% -> 22%
where the time goes in v9:
time: 91.7 us; the launch traced here: 91.5 us
  waiting for transfers between devices  42.2 us (46%)
  starting transfers between devices  24.7 us (27%)
  Pallas kernels  21.9 us (24%)
  local copies, waits for them, and re-layouts  1.71 us (2%)
  between operations  0.94 us (1%)
    ppermute x12, waiting for transfers between devices, flip(): return lax.ppermute(value, axis, [(i, i ^ step) for i in range(size)])  33.3 us
    ppermute x12, starting transfers between devices, flip(): return lax.ppermute(value, axis, [(i, i ^ step) for i in range(size)])  17.9 us
    ppermute x17, waiting for transfers between devices, swap(): return lax.ppermute(value, axis, [(0, 1), (1, 0)])  8.85 us
    ppermute x17, starting transfers between devices, swap(): return lax.ppermute(value, axis, [(0, 1), (1, 0)])  6.87 us
    pallas_call x1, Pallas kernels, shards(): call(functools.partial(worker, scale, owners, columns, capacity, permuted...  6.53 us
    pallas_call x1, Pallas kernels, owner(): call(functools.partial(owner_canvas, owners, capacity, wide, permuted), [...  5.54 us
    pallas_call x1, Pallas kernels, shards(): call(owner_spread, shape((MIDDLE, MIDDLE, TILE_BLOCKS, FULL), BF16), [VME...  2.93 us
    pallas_call x1, Pallas kernels, shards(): call(functools.partial(pack_cotangents, owners, capacity, permuted), piec...  1.92 us
  transfers between devices with their start and end apart: 29, of which 13 were waited for; matrix products, arithmetic and copies ran while one was open for 0% of the time, Pallas kernels for 22%

profile of v9, /device:TPU:0, one launch (start us, length us, event | category | flops | bytes accessed | tf_op | source)
XLA Modules:
  0.0 91.5 jit_solution(7332313193237067878)
XLA Ops:
  1.8 1.9 %pack_cotangents.1 = (bf16[8,64,128]{2,1,0:T(8,128)(2,1)S(1)}, bf16[8,64,128]{2,1,0:T(8,128)(2,1)S(1)}, bf16[8,64,128]{2,1,0:T(8,128)(2,1)S(1)}, bf16[8,64,128]{2,1,0:T(8,128)(2,1)S(1)}) custom-call(s32[4,16]{1,0:T(4,128)S(1)} %bitcast.17, bf16[8,8,32,128]{3,2,1,0:T(8,128)(2,1)} %bitcast.12), custom_call_target="tpu_custom_call" | custom-call | flops 1 | bytes 1 | tf_op jit(solution)/shard_map/pack_cotangents/pallas_call | solution.py:520
  3.8 4.7 %collective-permute-start = (bf16[8,64,128]{2,1,0:T(8,128)(2,1)S(1)}, bf16[8,64,128]{2,1,0:T(8,128)(2,1)S(1)}, u32[]{:S(2)}, u32[]{:S(2)}) collective-permute-start(bf16[8,64,128]{2,1,0:T(8,128)(2,1)S(1)} %get-tuple-element.65), channel_id=1, source_target_pairs={{0,12},{4,8},{8,4},{12,0},{1,13},{5,9},{9,5},{13,1},{2,14},{6,10},... | collective-permute-start | bytes 393224 | tf_op jit(solution)/shard_map/ppermute | solution.py:487
  9.1 3.8 %collective-permute-done.refs_3_ = bf16[8,64,128]{2,1,0:T(8,128)(2,1)S(1)} collective-permute-done((bf16[8,64,128]{2,1,0:T(8,128)(2,1)S(1)}, bf16[8,64,128]{2,1,0:T(8,128)(2,1)S(1)}, u32[]{:S(2)}, u32[]{:S(2)}) %collective-permute-start) | collective-permute-done | bytes 131104 | tf_op jit(solution)/shard_map/ppermute | solution.py:487
  13.9 1.6 %pack_saved.1 = (bf16[10,160,128]{2,1,0:T(8,128)(2,1)S(1)}, bf16[10,80,128]{2,1,0:T(8,128)(2,1)S(1)}, bf16[10,80,128]{2,1,0:T(8,128)(2,1)S(1)}, bf16[10,80,128]{2,1,0:T(8,128)(2,1)S(1)}, bf16[10,80,128]{2,1,0:T(8,128)(2,1)S(1)}) custom-call(s32[4,16]{1,0:T(4,128)S(1)} %bitcast.18, bf16[10,160,128]{2,1,0:T(8,128)(2,1)S(1)} %bitcast.16), custom_call_target="tpu_custom_call" | custom-call | flops 1 | bytes 1 | tf_op jit(solution)/shard_map/pack_saved/pallas_call | solution.py:532
  15.5 4.7 %collective-permute-done.1.refs_2_ = bf16[8,64,128]{2,1,0:T(8,128)(2,1)S(1)} collective-permute-done((bf16[8,64,128]{2,1,0:T(8,128)(2,1)S(1)}, bf16[8,64,128]{2,1,0:T(8,128)(2,1)S(1)}, u32[]{:S(2)}, u32[]{:S(2)}) %collective-permute-start.1) | collective-permute-done | bytes 131104 | tf_op jit(solution)/shard_map/ppermute | solution.py:487
  21.5 2.0 %collective-permute-start.10 = (bf16[10,80,128]{2,1,0:T(8,128)(2,1)S(1)}, bf16[10,80,128]{2,1,0:T(8,128)(2,1)S(1)}, u32[]{:S(2)}, u32[]{:S(2)}) collective-permute-start(bf16[10,80,128]{2,1,0:T(8,128)(2,1)S(1)} %get-tuple-element.81), channel_id=1, source_target_pairs={{0,8},{4,12},{8,0},{12,4},{1,9},{5,13},{9,1},{13,5},{2,10},{6,14},... | collective-permute-start | bytes 614408 | tf_op jit(solution)/shard_map/ppermute | solution.py:487
  24.9 6.5 %worker.1 = (f32[4,2,9,16,256]{4,3,2,1,0:T(8,128)S(1)}, bf16[2,2,9,16,256]{4,3,2,1,0:T(8,128)(2,1)S(1)}, bf16[2,2,9,16,256]{4,3,2,1,0:T(8,128)(2,1)S(1)}) custom-call(s32[4,16]{1,0:T(4,128)S(1)} %bitcast.19, bf16[8,64,128]{2,1,0:T(8,128)(2,1)S(1)} %get-tuple-element.64.refs_0_, bf16[8,64,128]{2,1,0:T(8,128)(2,1)S(1)} %collective-permute-done.2.refs_1_, ...), custom_call_target="tpu_custom_call" | custom-call | flops 1 | bytes 1 | tf_op jit(solution)/shard_map/worker/pallas_call | solution.py:550
  31.5 2.5 %collective-permute-done.10.refs_2_ = bf16[10,80,128]{2,1,0:T(8,128)(2,1)S(1)} collective-permute-done((bf16[10,80,128]{2,1,0:T(8,128)(2,1)S(1)}, bf16[10,80,128]{2,1,0:T(8,128)(2,1)S(1)}, u32[]{:S(2)}, u32[]{:S(2)}) %collective-permute-start.10) | collective-permute-done | bytes 204832 | tf_op jit(solution)/shard_map/ppermute | solution.py:487
  34.0 1.5 %collective-permute-start.12 = (bf16[2,2,9,16,256]{4,3,2,1,0:T(8,128)(2,1)S(1)}, bf16[2,2,9,16,256]{4,3,2,1,0:T(8,128)(2,1)S(1)}, u32[]{:S(2)}, u32[]{:S(2)}) collective-permute-start(bf16[2,2,9,16,256]{4,3,2,1,0:T(8,128)(2,1)S(1)} %get-tuple-element.85), channel_id=1, source_target_pairs={{0,2},{2,0},{1,3},{3,1},{4,6},{6,4},{5,7},{7,5},{8,10},{10,8},{9,1... | collective-permute-start | bytes 884744 | tf_op jit(solution)/shard_map/ppermute | solution.py:482
  35.4 2.5 %collective-permute-start.13 = (bf16[10,80,128]{2,1,0:T(8,128)(2,1)S(1)}, bf16[10,80,128]{2,1,0:T(8,128)(2,1)S(1)}, u32[]{:S(2)}, u32[]{:S(2)}) collective-permute-start(bf16[10,80,128]{2,1,0:T(8,128)(2,1)S(1)} %get-tuple-element.89), channel_id=1, source_target_pairs={{0,12},{4,8},{8,4},{12,0},{1,13},{5,9},{9,5},{13,1},{2,14},{6,10},... | collective-permute-start | bytes 614408 | tf_op jit(solution)/shard_map/ppermute | solution.py:487
  38.5 2.9 %owner_spread.1.refs_8_ = bf16[10,10,32,256]{3,2,1,0:T(8,128)(2,1)S(1)} custom-call(bf16[8,8,32,128]{3,2,1,0:T(8,128)(2,1)S(1)} %bitcast.14, bf16[8,8,32,128]{3,2,1,0:T(8,128)(2,1)S(1)} %collective-permute-done.11.tile_other, bf16[9,128,256]{2,1,0:T(8,128)(2,1)S(1)} %copy-done.1, bf16[9,128,256]{2,1,0:T(8,128)(2,1)S(1)} %collective-permute-done.8.refs_11_.second_other), custom_call_target="tpu_custom_call" | custom-call | flops 1 | bytes 1 | tf_op jit(solution)/shard_map/owner_spread/pallas_call | solution.py:576
  41.4 2.5 %collective-permute-done.12.got = bf16[2,2,9,16,256]{4,3,2,1,0:T(8,128)(2,1)S(1)} collective-permute-done((bf16[2,2,9,16,256]{4,3,2,1,0:T(8,128)(2,1)S(1)}, bf16[2,2,9,16,256]{4,3,2,1,0:T(8,128)(2,1)S(1)}, u32[]{:S(2)}, u32[]{:S(2)}) %collective-permute-start.12) | collective-permute-done | bytes 294944 | tf_op jit(solution)/shard_map/ppermute | solution.py:482
  45.3 2.6 %collective-permute-done.14.refs_1_ = bf16[10,80,128]{2,1,0:T(8,128)(2,1)S(1)} collective-permute-done((bf16[10,80,128]{2,1,0:T(8,128)(2,1)S(1)}, bf16[10,80,128]{2,1,0:T(8,128)(2,1)S(1)}, u32[]{:S(2)}, u32[]{:S(2)}) %collective-permute-start.14) | collective-permute-done | bytes 204832 | tf_op jit(solution)/shard_map/ppermute | solution.py:487
  48.3 1.6 %collective-permute-start.19 = (bf16[2,9,16,256]{3,2,1,0:T(8,128)(2,1)S(1)}, bf16[2,9,16,256]{3,2,1,0:T(8,128)(2,1)S(1)}, u32[]{:S(2)}, u32[]{:S(2)}) collective-permute-start(bf16[2,9,16,256]{3,2,1,0:T(8,128)(2,1)S(1)} %get-tuple-element.99), channel_id=1, source_target_pairs={{0,12},{4,8},{8,4},{12,0},{1,13},{5,9},{9,5},{13,1},{2,14},{6,10},... | collective-permute-start | bytes 442376 | tf_op jit(solution)/shard_map/ppermute | solution.py:487
  50.4 5.5 %owner_canvas.1 = (f32[68,40,128]{2,1,0:T(8,128)S(1)}, bf16[48,256]{1,0:T(8,128)(2,1)S(1)}, bf16[48,256]{1,0:T(8,128)(2,1)S(1)}) custom-call(s32[4,16]{1,0:T(4,128)S(1)} %bitcast.20, bf16[10,80,128]{2,1,0:T(8,128)(2,1)S(1)} %get-tuple-element.78.refs_0_, bf16[10,80,128]{2,1,0:T(8,128)(2,1)S(1)} %collective-permute-done.14.refs_1_, ...), custom_call_target="tpu_custom_call" | custom-call | flops 1 | bytes 1 | tf_op jit(solution)/shard_map/owner_canvas/pallas_call | solution.py:590
  56.1 2.4 %collective-permute-start.21 = (bf16[2,9,16,256]{3,2,1,0:T(8,128)(2,1)S(1)}, bf16[2,9,16,256]{3,2,1,0:T(8,128)(2,1)S(1)}, u32[]{:S(2)}, u32[]{:S(2)}) collective-permute-start(bf16[2,9,16,256]{3,2,1,0:T(8,128)(2,1)S(1)} %get-tuple-element.101), channel_id=1, source_target_pairs={{0,4},{4,0},{8,12},{12,8},{1,5},{5,1},{9,13},{13,9},{2,6},{6,2},{1... | collective-permute-start | bytes 442376 | tf_op jit(solution)/shard_map/ppermute | solution.py:487
  58.4 5.3 %collective-permute-done.20.got_2 = bf16[2,9,16,256]{3,2,1,0:T(8,128)(2,1)S(1)} collective-permute-done((bf16[2,9,16,256]{3,2,1,0:T(8,128)(2,1)S(1)}, bf16[2,9,16,256]{3,2,1,0:T(8,128)(2,1)S(1)}, u32[]{:S(2)}, u32[]{:S(2)}) %collective-permute-start.20) | collective-permute-done | bytes 147488 | tf_op jit(solution)/shard_map/ppermute | solution.py:487
  65.2 1.7 %collective-permute-start.22 = (bf16[336,256]{1,0:T(8,128)(2,1)S(1)}, bf16[336,256]{1,0:T(8,128)(2,1)S(1)}, u32[]{:S(2)}, u32[]{:S(2)}) collective-permute-start(bf16[336,256]{1,0:T(8,128)(2,1)S(1)} %get-tuple-element.104), channel_id=1, source_target_pairs={{0,12},{4,8},{8,4},{12,0},{1,13},{5,9},{9,5},{13,1},{2,14},{6,10},... | collective-permute-start | bytes 516104 | tf_op jit(solution)/shard_map/ppermute | solution.py:487
  67.5 1.8 %collective-permute-start.23 = (bf16[288,256]{1,0:T(8,128)(2,1)S(1)}, bf16[288,256]{1,0:T(8,128)(2,1)S(1)}, u32[]{:S(2)}, u32[]{:S(2)}) collective-permute-start(bf16[288,256]{1,0:T(8,128)(2,1)S(1)} %get-tuple-element.105.refs_0_), channel_id=1, source_target_pairs={{0,8},{4,12},{8,0},{12,4},{1,9},{5,13},{9,1},{13,5},{2,10},{6,14},... | collective-permute-start | bytes 442376 | tf_op jit(solution)/shard_map/ppermute | solution.py:487
  69.2 4.0 %collective-permute-done.24.got_1.refs_1_ = bf16[336,256]{1,0:T(8,128)(2,1)S(1)} collective-permute-done((bf16[336,256]{1,0:T(8,128)(2,1)S(1)}, bf16[336,256]{1,0:T(8,128)(2,1)S(1)}, u32[]{:S(2)}, u32[]{:S(2)}) %collective-permute-start.24) | collective-permute-done | bytes 172064 | tf_op jit(solution)/shard_map/ppermute | solution.py:487
  73.9 7.9 %collective-permute-done.23.refs_2_ = bf16[288,256]{1,0:T(8,128)(2,1)S(1)} collective-permute-done((bf16[288,256]{1,0:T(8,128)(2,1)S(1)}, bf16[288,256]{1,0:T(8,128)(2,1)S(1)}, u32[]{:S(2)}, u32[]{:S(2)}) %collective-permute-start.23) | collective-permute-done | bytes 147488 | tf_op jit(solution)/shard_map/ppermute | solution.py:487
  83.9 1.5 %lay.1 = (f32[9,128,256]{2,1,0:T(8,128)}, f32[9,128,256]{2,1,0:T(8,128)}) custom-call(bf16[288,256]{1,0:T(8,128)(2,1)S(1)} %get-tuple-element.105.refs_0_, bf16[336,256]{1,0:T(8,128)(2,1)S(1)} %collective-permute-done.24.got_1.refs_1_, bf16[288,256]{1,0:T(8,128)(2,1)S(1)} %collective-permute-done.23.refs_2_, ...), custom_call_target="tpu_custom_call" | custom-call | flops 1 | bytes 1 | tf_op jit(solution)/shard_map/lay/pallas_call | solution.py:631
  85.4 4.2 %collective-permute-done.28.late = bf16[288,256]{1,0:T(8,128)(2,1)S(1)} collective-permute-done((bf16[288,256]{1,0:T(8,128)(2,1)S(1)}, bf16[288,256]{1,0:T(8,128)(2,1)S(1)}, u32[]{:S(2)}, u32[]{:S(2)}) %collective-permute-start.28) | collective-permute-done | bytes 147488 | tf_op jit(solution)/shard_map/ppermute | solution.py:482
  89.7 1.7 %finish.1 = (bf16[64,32,128]{2,1,0:T(8,128)(2,1)}, f32[9,128,256]{2,1,0:T(8,128)}, f32[9,128,256]{2,1,0:T(8,128)}) custom-call(bf16[64,32,128]{2,1,0:T(8,128)(2,1)S(1)} %copy-done, f32[68,40,128]{2,1,0:T(8,128)S(1)} %get-tuple-element.96.canvas, ...), custom_call_target="tpu_custom_call", output_to_operand_aliasing={{1}: (6, {}), {2}: (7, {})} | custom-call | flops 1 | bytes 1 | tf_op jit(solution)/shard_map/finish/pallas_call | solution.py:634
  (58 shorter events, 13.3 us)
Async XLA Ops:
  0.6 24.3 %collective-permute-start.8 = (bf16[9,128,256]{2,1,0:T(8,128)(2,1)}, bf16[9,128,256]{2,1,0:T(8,128)(2,1)S(1)}, u32[]{:S(2)}, u32[]{:S(2)}) collective-permute-start(bf16[9,128,256]{2,1,0:T(8,128)(2,1)} %second.1), channel_id=1, source_target_pairs={{0,1},{1,0},{2,3},{3,2},{4,5},{5,4},{6,7},{7,6},{8,9},{9,8},{10,11... | collective-permute-start | bytes 1769480 | tf_op jit(solution)/shard_map/ppermute | solution.py:482
  3.8 9.2 %collective-permute-start = (bf16[8,64,128]{2,1,0:T(8,128)(2,1)S(1)}, bf16[8,64,128]{2,1,0:T(8,128)(2,1)S(1)}, u32[]{:S(2)}, u32[]{:S(2)}) collective-permute-start(bf16[8,64,128]{2,1,0:T(8,128)(2,1)S(1)} %get-tuple-element.65), channel_id=1, source_target_pairs={{0,12},{4,8},{8,4},{12,0},{1,13},{5,9},{9,5},{13,1},{2,14},{6,10},... | collective-permute-start | bytes 393224 | tf_op jit(solution)/shard_map/ppermute | solution.py:487
  8.5 11.7 %collective-permute-start.1 = (bf16[8,64,128]{2,1,0:T(8,128)(2,1)S(1)}, bf16[8,64,128]{2,1,0:T(8,128)(2,1)S(1)}, u32[]{:S(2)}, u32[]{:S(2)}) collective-permute-start(bf16[8,64,128]{2,1,0:T(8,128)(2,1)S(1)} %get-tuple-element.66), channel_id=1, source_target_pairs={{0,8},{4,12},{8,0},{12,4},{1,9},{5,13},{9,1},{13,5},{2,10},{6,14},... | collective-permute-start | bytes 393224 | tf_op jit(solution)/shard_map/ppermute | solution.py:487
  8.5 11.7 %collective-permute-start.2 = (bf16[8,64,128]{2,1,0:T(8,128)(2,1)S(1)}, bf16[8,64,128]{2,1,0:T(8,128)(2,1)S(1)}, u32[]{:S(2)}, u32[]{:S(2)}) collective-permute-start(bf16[8,64,128]{2,1,0:T(8,128)(2,1)S(1)} %get-tuple-element.67), channel_id=1, source_target_pairs={{0,4},{4,0},{8,12},{12,8},{1,5},{5,1},{9,13},{13,9},{2,6},{6,2},{1... | collective-permute-start | bytes 393224 | tf_op jit(solution)/shard_map/ppermute | solution.py:487
  9.1 15.8 %collective-permute-start.7 = (bf16[10,160,128]{2,1,0:T(8,128)(2,1)}, bf16[10,160,128]{2,1,0:T(8,128)(2,1)S(1)}, u32[]{:S(2)}, u32[]{:S(2)}) collective-permute-start(bf16[10,160,128]{2,1,0:T(8,128)(2,1)} %bitcast.15), channel_id=1, source_target_pairs={{0,1},{1,0},{2,3},{3,2},{4,5},{5,4},{6,7},{7,6},{8,9},{9,8},{10,11... | collective-permute-start | bytes 1228808 | tf_op jit(solution)/shard_map/ppermute | solution.py:482
  12.9 7.8 %collective-permute-start.3 = (bf16[8,64,128]{2,1,0:T(8,128)(2,1)S(1)}, bf16[8,64,128]{2,1,0:T(8,128)(2,1)S(1)}, u32[]{:S(2)}, u32[]{:S(2)}) collective-permute-start(bf16[8,64,128]{2,1,0:T(8,128)(2,1)S(1)} %get-tuple-element.64.refs_0_), channel_id=1, source_target_pairs={{0,1},{1,0},{2,3},{3,2},{4,5},{5,4},{6,7},{7,6},{8,9},{9,8},{10,11... | collective-permute-start | bytes 393224 | tf_op jit(solution)/shard_map/ppermute | solution.py:482
  20.7 17.8 %collective-permute-start.11 = (bf16[8,8,32,128]{3,2,1,0:T(8,128)(2,1)}, bf16[8,8,32,128]{3,2,1,0:T(8,128)(2,1)S(1)}, u32[]{:S(2)}, u32[]{:S(2)}) collective-permute-start(bf16[8,8,32,128]{3,2,1,0:T(8,128)(2,1)} %bitcast.13), channel_id=1, source_target_pairs={{0,1},{1,0},{2,3},{3,2},{4,5},{5,4},{6,7},{7,6},{8,9},{9,8},{10,11... | collective-permute-start | bytes 1572872 | tf_op jit(solution)/shard_map/ppermute | solution.py:482
  21.5 12.4 %collective-permute-start.10 = (bf16[10,80,128]{2,1,0:T(8,128)(2,1)S(1)}, bf16[10,80,128]{2,1,0:T(8,128)(2,1)S(1)}, u32[]{:S(2)}, u32[]{:S(2)}) collective-permute-start(bf16[10,80,128]{2,1,0:T(8,128)(2,1)S(1)} %get-tuple-element.81), channel_id=1, source_target_pairs={{0,8},{4,12},{8,0},{12,4},{1,9},{5,13},{9,1},{13,5},{2,10},{6,14},... | collective-permute-start | bytes 614408 | tf_op jit(solution)/shard_map/ppermute | solution.py:487
  34.0 9.9 %collective-permute-start.12 = (bf16[2,2,9,16,256]{4,3,2,1,0:T(8,128)(2,1)S(1)}, bf16[2,2,9,16,256]{4,3,2,1,0:T(8,128)(2,1)S(1)}, u32[]{:S(2)}, u32[]{:S(2)}) collective-permute-start(bf16[2,2,9,16,256]{4,3,2,1,0:T(8,128)(2,1)S(1)} %get-tuple-element.85), channel_id=1, source_target_pairs={{0,2},{2,0},{1,3},{3,1},{4,6},{6,4},{5,7},{7,5},{8,10},{10,8},{9,1... | collective-permute-start | bytes 884744 | tf_op jit(solution)/shard_map/ppermute | solution.py:482
  35.4 9.8 %collective-permute-start.13 = (bf16[10,80,128]{2,1,0:T(8,128)(2,1)S(1)}, bf16[10,80,128]{2,1,0:T(8,128)(2,1)S(1)}, u32[]{:S(2)}, u32[]{:S(2)}) collective-permute-start(bf16[10,80,128]{2,1,0:T(8,128)(2,1)S(1)} %get-tuple-element.89), channel_id=1, source_target_pairs={{0,12},{4,8},{8,4},{12,0},{1,13},{5,9},{9,5},{13,1},{2,14},{6,10},... | collective-permute-start | bytes 614408 | tf_op jit(solution)/shard_map/ppermute | solution.py:487
  37.9 9.9 %collective-permute-start.14 = (bf16[10,80,128]{2,1,0:T(8,128)(2,1)S(1)}, bf16[10,80,128]{2,1,0:T(8,128)(2,1)S(1)}, u32[]{:S(2)}, u32[]{:S(2)}) collective-permute-start(bf16[10,80,128]{2,1,0:T(8,128)(2,1)S(1)} %get-tuple-element.90), channel_id=1, source_target_pairs={{0,4},{4,0},{8,12},{12,8},{1,5},{5,1},{9,13},{13,9},{2,6},{6,2},{1... | collective-permute-start | bytes 614408 | tf_op jit(solution)/shard_map/ppermute | solution.py:487
  37.9 18.1 %collective-permute-start.9 = (bf16[2,2,9,16,256]{4,3,2,1,0:T(8,128)(2,1)S(1)}, bf16[2,2,9,16,256]{4,3,2,1,0:T(8,128)(2,1)S(1)}, u32[]{:S(2)}, u32[]{:S(2)}) collective-permute-start(bf16[2,2,9,16,256]{4,3,2,1,0:T(8,128)(2,1)S(1)} %get-tuple-element.77), channel_id=1, source_target_pairs={{0,2},{2,0},{1,3},{3,1},{4,6},{6,4},{5,7},{7,5},{8,10},{10,8},{9,1... | collective-permute-start | bytes 884744 | tf_op jit(solution)/shard_map/ppermute | solution.py:482
  38.5 9.9 %collective-permute-start.15 = (bf16[10,80,128]{2,1,0:T(8,128)(2,1)S(1)}, bf16[10,80,128]{2,1,0:T(8,128)(2,1)S(1)}, u32[]{:S(2)}, u32[]{:S(2)}) collective-permute-start(bf16[10,80,128]{2,1,0:T(8,128)(2,1)S(1)} %get-tuple-element.78.refs_0_), channel_id=1, source_target_pairs={{0,1},{1,0},{2,3},{3,2},{4,5},{5,4},{6,7},{7,6},{8,9},{9,8},{10,11... | collective-permute-start | bytes 614408 | tf_op jit(solution)/shard_map/ppermute | solution.py:482
  43.9 6.1 %collective-permute-start.17 = (bf16[10,80,128]{2,1,0:T(8,128)(2,1)S(1)}, bf16[10,80,128]{2,1,0:T(8,128)(2,1)S(1)}, u32[]{:S(2)}, u32[]{:S(2)}) collective-permute-start(bf16[10,80,128]{2,1,0:T(8,128)(2,1)S(1)} %collective-permute-done.10.refs_2_), channel_id=1, source_target_pairs={{0,1},{1,0},{2,3},{3,2},{4,5},{5,4},{6,7},{7,6},{8,9},{9,8},{10,11... | collective-permute-start | bytes 614408 | tf_op jit(solution)/shard_map/ppermute | solution.py:482
  48.3 10.1 %collective-permute-start.19 = (bf16[2,9,16,256]{3,2,1,0:T(8,128)(2,1)S(1)}, bf16[2,9,16,256]{3,2,1,0:T(8,128)(2,1)S(1)}, u32[]{:S(2)}, u32[]{:S(2)}) collective-permute-start(bf16[2,9,16,256]{3,2,1,0:T(8,128)(2,1)S(1)} %get-tuple-element.99), channel_id=1, source_target_pairs={{0,12},{4,8},{8,4},{12,0},{1,13},{5,9},{9,5},{13,1},{2,14},{6,10},... | collective-permute-start | bytes 442376 | tf_op jit(solution)/shard_map/ppermute | solution.py:487
  50.0 13.8 %collective-permute-start.20 = (bf16[2,9,16,256]{3,2,1,0:T(8,128)(2,1)S(1)}, bf16[2,9,16,256]{3,2,1,0:T(8,128)(2,1)S(1)}, u32[]{:S(2)}, u32[]{:S(2)}) collective-permute-start(bf16[2,9,16,256]{3,2,1,0:T(8,128)(2,1)S(1)} %get-tuple-element.100), channel_id=1, source_target_pairs={{0,8},{4,12},{8,0},{12,4},{1,9},{5,13},{9,1},{13,5},{2,10},{6,14},... | collective-permute-start | bytes 442376 | tf_op jit(solution)/shard_map/ppermute | solution.py:487
  56.1 9.0 %collective-permute-start.21 = (bf16[2,9,16,256]{3,2,1,0:T(8,128)(2,1)S(1)}, bf16[2,9,16,256]{3,2,1,0:T(8,128)(2,1)S(1)}, u32[]{:S(2)}, u32[]{:S(2)}) collective-permute-start(bf16[2,9,16,256]{3,2,1,0:T(8,128)(2,1)S(1)} %get-tuple-element.101), channel_id=1, source_target_pairs={{0,4},{4,0},{8,12},{12,8},{1,5},{5,1},{9,13},{13,9},{2,6},{6,2},{1... | collective-permute-start | bytes 442376 | tf_op jit(solution)/shard_map/ppermute | solution.py:487
  65.1 8.1 %collective-permute-start.24 = (bf16[336,256]{1,0:T(8,128)(2,1)S(1)}, bf16[336,256]{1,0:T(8,128)(2,1)S(1)}, u32[]{:S(2)}, u32[]{:S(2)}) collective-permute-start(bf16[336,256]{1,0:T(8,128)(2,1)S(1)} %get-tuple-element.106), channel_id=1, source_target_pairs={{0,4},{4,0},{8,12},{12,8},{1,5},{5,1},{9,13},{13,9},{2,6},{6,2},{1... | collective-permute-start | bytes 516104 | tf_op jit(solution)/shard_map/ppermute | solution.py:487
  65.2 16.5 %collective-permute-start.22 = (bf16[336,256]{1,0:T(8,128)(2,1)S(1)}, bf16[336,256]{1,0:T(8,128)(2,1)S(1)}, u32[]{:S(2)}, u32[]{:S(2)}) collective-permute-start(bf16[336,256]{1,0:T(8,128)(2,1)S(1)} %get-tuple-element.104), channel_id=1, source_target_pairs={{0,12},{4,8},{8,4},{12,0},{1,13},{5,9},{9,5},{13,1},{2,14},{6,10},... | collective-permute-start | bytes 516104 | tf_op jit(solution)/shard_map/ppermute | solution.py:487
  66.9 7.0 %collective-permute-start.25 = (bf16[288,256]{1,0:T(8,128)(2,1)S(1)}, bf16[288,256]{1,0:T(8,128)(2,1)S(1)}, u32[]{:S(2)}, u32[]{:S(2)}) collective-permute-start(bf16[288,256]{1,0:T(8,128)(2,1)S(1)} %get-tuple-element.105.refs_0_), channel_id=1, source_target_pairs={{0,2},{2,0},{1,3},{3,1},{4,6},{6,4},{5,7},{7,5},{8,10},{10,8},{9,1... | collective-permute-start | bytes 442376 | tf_op jit(solution)/shard_map/ppermute | solution.py:482
  67.5 14.3 %collective-permute-start.23 = (bf16[288,256]{1,0:T(8,128)(2,1)S(1)}, bf16[288,256]{1,0:T(8,128)(2,1)S(1)}, u32[]{:S(2)}, u32[]{:S(2)}) collective-permute-start(bf16[288,256]{1,0:T(8,128)(2,1)S(1)} %get-tuple-element.105.refs_0_), channel_id=1, source_target_pairs={{0,8},{4,12},{8,0},{12,4},{1,9},{5,13},{9,1},{13,5},{2,10},{6,14},... | collective-permute-start | bytes 442376 | tf_op jit(solution)/shard_map/ppermute | solution.py:487
  73.3 8.5 %collective-permute-start.26 = (bf16[288,256]{1,0:T(8,128)(2,1)S(1)}, bf16[288,256]{1,0:T(8,128)(2,1)S(1)}, u32[]{:S(2)}, u32[]{:S(2)}) collective-permute-start(bf16[288,256]{1,0:T(8,128)(2,1)S(1)} %slice.4), channel_id=1, source_target_pairs={{0,2},{2,0},{1,3},{3,1},{4,6},{6,4},{5,7},{7,5},{8,10},{10,8},{9,1... | collective-permute-start | bytes 442376 | tf_op jit(solution)/shard_map/ppermute | solution.py:482
  81.8 7.8 %collective-permute-start.27 = (bf16[352,256]{1,0:T(8,128)(2,1)S(1)}, bf16[352,256]{1,0:T(8,128)(2,1)S(1)}, u32[]{:S(2)}, u32[]{:S(2)}) collective-permute-start(bf16[352,256]{1,0:T(8,128)(2,1)S(1)} %column_message.1), channel_id=1, source_target_pairs={{0,2},{2,0},{1,3},{3,1},{4,6},{6,4},{5,7},{7,5},{8,10},{10,8},{9,1... | collective-permute-start | bytes 540680 | tf_op jit(solution)/shard_map/ppermute | solution.py:482
  82.4 7.2 %collective-permute-start.28 = (bf16[288,256]{1,0:T(8,128)(2,1)S(1)}, bf16[288,256]{1,0:T(8,128)(2,1)S(1)}, u32[]{:S(2)}, u32[]{:S(2)}) collective-permute-start(bf16[288,256]{1,0:T(8,128)(2,1)S(1)} %collective-permute-done.23.refs_2_), channel_id=1, source_target_pairs={{0,2},{2,0},{1,3},{3,1},{4,6},{6,4},{5,7},{7,5},{8,10},{10,8},{9,1... | collective-permute-start | bytes 442376 | tf_op jit(solution)/shard_map/ppermute | solution.py:482
  (11 other events, 68.8 us)

commit v10 on v9

--- a/solution.py
+++ b/solution.py
@@ -227,6 +227,28 @@
         outs[0][grad, tap] = value
 
 
+def spread(padded, weight, total, places):
+    height, size = padded.shape[0], total.shape[1]
+    for dy in range(3):
+        windows, taps = [], []
+        for dx in range(3):
+            at = (2 - dx) * places
+            windows.append(padded[:, at : at + size].reshape(height * size, FULL))
+            taps.append(weight[3 * dy + dx])
+        part = dot_nt(jnp.concatenate(windows, axis=1), jnp.concatenate(taps, axis=1))
+        part = part.reshape(height, size, total.shape[2])
+        if dy == 0:
+            total[:height] = part
+            total[height:] = jnp.zeros((2, size, total.shape[2]), F32)
+        else:
+            total[dy : dy + height] += part
+
+
+def pad_sides(padded, places):
+    for side in (slice(0, 2 * places), slice(padded.shape[1] - 2 * places, None)):
+        padded[:, side] = jnp.zeros((padded.shape[0], 2 * places, FULL), BF16)
+
+
 def second_gradient(scale, owners, capacity, permuted, routing, *refs):
     parts = 1 if not permuted else owners
     own, other = views(refs[:parts], owners), views(refs[parts : 2 * parts], owners)
@@ -244,8 +266,9 @@
         got = jnp.concatenate(
             [ordered(own[o][u], other[o][u], 1) for o in range(owners)], axis=0
         )
-        cot[u] = dot(pick, got).astype(BF16)
-    grads = cot[...].reshape(BLOCK * rows, FULL)
+        cot[u, 2 * PER_WORKER : 2 * PER_WORKER + rows] = dot(pick, got).astype(BF16)
+    pad_sides(cot, PER_WORKER)
+    grads = cot[:, 2 * PER_WORKER : 2 * PER_WORKER + rows].reshape(BLOCK * rows, FULL)
     for dy in range(3):
         windows = [
             masked[dy : dy + BLOCK, dx * PER_WORKER : (dx + BLOCK) * PER_WORKER] for dx in range(3)
@@ -261,18 +284,12 @@
     scale, outside, cot, masked, saved_other, weight, weight_other, saved, *refs
 ):
     outs, (total, pre, full) = refs[:-3], refs[-3:]
-    rows = BLOCK * BLOCK * PER_WORKER
     full[...] = ordered(weight[...], weight_other[...], 1)
-    total[...] = jnp.zeros_like(total)
-    for tap in range(9):
-        dy, dx = tap // 3, tap % 3
-        part = dot_nt(cot[...].reshape(rows, FULL), full[tap])
-        spot = (slice(dy, dy + BLOCK), slice(dx, dx + BLOCK))
-        total[spot] = total[spot] + part.reshape(BLOCK, BLOCK, PER_WORKER, FULL)
+    spread(cot, full, total, PER_WORKER)
     for m in range(MIDDLE):
         other = jnp.where(outside(m), 0.0, saved_other[m].astype(F32)).astype(BF16)
         live = ordered(masked[m], other, 1).astype(F32) > 0
-        value = jnp.where(live, total[m].reshape(MIDDLE * PER_WORKER, FULL), 0.0)
+        value = jnp.where(live, total[m], 0.0)
         pre[m] = value.astype(BF16).reshape(MIDDLE, PER_WORKER, FULL)
     size = MIDDLE * MIDDLE * PER_WORKER
     grads = pre[...].reshape(size, FULL)
@@ -291,16 +308,18 @@
         block = jnp.concatenate(
             [ordered(tile[r, u], tile_other[r, u], 1) for r in range(TILE_ROWS)], axis=0
         )
-        cot[u] = dot(turn, block).astype(BF16)
+        cot[u, 2 * TILE_BLOCKS : (2 + BLOCK) * TILE_BLOCKS] = dot(turn, block).astype(BF16)
+    pad_sides(cot, TILE_BLOCKS)
     full[...] = ordered(second[...], second_other[...], 1)
-    rows = BLOCK * BLOCK * TILE_BLOCKS
-    total[...] = jnp.zeros_like(total)
-    for tap in range(9):
-        dy, dx = tap // 3, tap % 3
-        part = dot_nt(cot[...].reshape(rows, FULL), full[tap])
-        spot = (slice(dy, dy + BLOCK), slice(dx, dx + BLOCK))
-        total[spot] = total[spot] + part.reshape(BLOCK, BLOCK, TILE_BLOCKS, FULL)
-    out[...] = total[...].astype(BF16)
+    spread(cot, full, total, TILE_BLOCKS)
+    out[...] = total[...].astype(BF16).reshape(out.shape)
+
+
+def prepare(owners, columns, capacity, wide, permuted, routing, saved, *refs):
+    (tile, tile_other, second, second_other, masked), refs = refs[:5], refs[5:]
+    outs, (out, counts, table, total, cot, full) = refs[:-6], refs[-6:]
+    pack_saved(owners, columns, capacity, wide, permuted, routing, saved, masked, *outs, counts, table)
+    owner_spread(tile, tile_other, second, second_other, out, total, cot, full)
 
 
 def worker(scale, owners, columns, capacity, permuted, routing, *refs):
@@ -355,19 +374,10 @@
         block = jnp.concatenate(
             [ordered(got[w][m], got_other[w][m], 1) for w in range(owners)], axis=0
         )
-        live = dot(pick, block).reshape(MIDDLE, TILE_BLOCKS, FULL) > 0
-        pre[m] = jnp.where(live, total[m].astype(F32), 0.0).astype(BF16)
-    size = MIDDLE * MIDDLE * TILE_BLOCKS
-    grown[...] = jnp.zeros_like(grown)
-    for tap in range(0, 9, 2):
-        taps = range(tap, min(tap + 2, 9))
-        weight = jnp.concatenate([first[k] for k in taps], axis=0)
-        part = dot_nt(pre[...].reshape(size, FULL), weight)
-        for k in taps:
-            dy, dx = k // 3, k % 3
-            spot = (slice(dy, dy + MIDDLE), slice(dx, dx + MIDDLE))
-            here = part[:, (k - tap) * HALF : (k - tap + 1) * HALF]
-            grown[spot] = grown[spot] + here.reshape(MIDDLE, MIDDLE, TILE_BLOCKS, HALF)
+        value = jnp.where(dot(pick, block) > 0, total[m].reshape(into, FULL).astype(F32), 0.0)
+        pre[m, 2 * TILE_BLOCKS : 2 * TILE_BLOCKS + into] = value.astype(BF16)
+    pad_sides(pre, TILE_BLOCKS)
+    spread(pre, first, grown, TILE_BLOCKS)
     height, depth = TILE_ROWS * WIDE, OUTER * TILE_BLOCKS
     row, lane = iota((height, depth), 0), iota((height, depth), 1)
     at_row, at_col = row // WIDE, row % WIDE
@@ -378,7 +388,7 @@
     canvas[...] = jnp.zeros_like(canvas)
     for m in range(0, OUTER, 2):
         pair = jnp.concatenate(
-            [grown[m + k].reshape(depth, HALF).astype(BF16) for k in range(2)], axis=1
+            [grown[m + k].astype(BF16) for k in range(2)], axis=1
         )
         laid = dot(fold, pair).reshape(TILE_ROWS, WIDE, FULL)
         for r in range(TILE_ROWS):
@@ -529,16 +539,24 @@
     saved_other = swap(saved_slots)
     incoming = exchange(outgoing)
 
-    masked, *to_owners = call(
-        functools.partial(pack_saved, owners, columns, capacity, wide, permuted),
-        [shape((MIDDLE, MIDDLE * PER_WORKER, HALF), BF16)] + pieces(MIDDLE, wide * capacity, HALF),
-        [SMEM, VMEM], counts + tables, (1, 1), "pack_saved",
-    )(routing, saved_here)
-    incoming_other = [swap(incoming[0])] if permuted else []
-    *rest, to_owners = tie((*incoming[len(incoming_other) :][::-1], to_owners[::-1]))
-    incoming = incoming[: len(incoming_other)] + rest[::-1]
-    to_owners = to_owners[::-1]
-    incoming_other += [swap(value) for value in rest[::-1]]
+    masked, *to_owners, total = call(
+        functools.partial(prepare, owners, columns, capacity, wide, permuted),
+        [shape((MIDDLE, MIDDLE * PER_WORKER, HALF), BF16)]
+        + pieces(MIDDLE, wide * capacity, HALF)
+        + [shape((MIDDLE, MIDDLE, TILE_BLOCKS, FULL), BF16)],
+        [SMEM] + [VMEM] * 5,
+        counts
+        + tables
+        + [
+            pltpu.VMEM((MIDDLE, MIDDLE * TILE_BLOCKS, FULL), F32),
+            pltpu.VMEM((BLOCK, OUTER * TILE_BLOCKS, FULL), BF16),
+            pltpu.VMEM((9, FULL, FULL), BF16),
+        ],
+        (1, 1), "prepare",
+    )(routing, saved_here, tile, tile_other, second_weight, second_other)
+    incoming, to_owners, total = tie((incoming[::-1], to_owners[::-1], total))
+    incoming, to_owners = incoming[::-1], to_owners[::-1]
+    incoming_other = [swap(value) for value in incoming]
     at_owner = exchange(to_owners)
 
     saved_tiles = saved_input[0, 0].transpose(1, 2, 0, 3)
@@ -553,8 +571,8 @@
         [SMEM] + [VMEM] * (2 * parts + 4) + [HBM],
         counts
         + [
-            pltpu.VMEM((BLOCK, BLOCK * PER_WORKER, FULL), BF16),
-            pltpu.VMEM((MIDDLE, MIDDLE, PER_WORKER, FULL), F32),
+            pltpu.VMEM((BLOCK, OUTER * PER_WORKER, FULL), BF16),
+            pltpu.VMEM((MIDDLE, MIDDLE * PER_WORKER, FULL), F32),
             pltpu.VMEM((MIDDLE, MIDDLE, PER_WORKER, FULL), BF16),
             pltpu.VMEM((9, FULL, FULL), BF16),
             pltpu.VMEM(saved_tiles.shape, BF16),
@@ -569,21 +587,7 @@
 
     if permuted:
         kept, near, far = terms
-        far, at_owner[2] = tie((far, at_owner[2]))
-        kept, far, tile_here = tie((kept, far, tile))
-    else:
-        terms, tile_here = tie((terms, tile))
-    total = call(
-        owner_spread,
-        shape((MIDDLE, MIDDLE, TILE_BLOCKS, FULL), BF16),
-        [VMEM] * 4,
-        [
-            pltpu.VMEM((MIDDLE, MIDDLE, TILE_BLOCKS, FULL), F32),
-            pltpu.VMEM((BLOCK, FULL, FULL), BF16),
-            pltpu.VMEM((9, FULL, FULL), BF16),
-        ],
-        (1, 1), "owner_spread",
-    )(tile_here, tile_other, second_weight, second_other)
+        far, at_owner[2], at_owner[1] = tie((far, at_owner[2], at_owner[1]))
 
     def owner(at_owner):
         at_owner_other = [swap(value) for value in at_owner]
@@ -593,19 +597,18 @@
             [SMEM] + [VMEM] * (2 * len(at_owner) + 2),
             tables
             + [
-                pltpu.VMEM((MIDDLE, MIDDLE, TILE_BLOCKS, FULL), BF16),
-                pltpu.VMEM((OUTER, OUTER, TILE_BLOCKS, HALF), F32),
+                pltpu.VMEM((MIDDLE, (OUTER + 2) * TILE_BLOCKS, FULL), BF16),
+                pltpu.VMEM((OUTER, OUTER * TILE_BLOCKS, HALF), F32),
             ],
             (1, 1), "owner_canvas",
         )(routing, *at_owner, *at_owner_other, total, first_weight)
 
     if permuted:
         far_got, near_got = swap(far, "col"), swap(near, "col")
-        total, far_got = tie((total, far_got))
         sends = call(add_far, [shape(part, BF16)] * 2, [VMEM] * 2, [], (1, 1), "add_far")(
             kept, far_got
         )
-        sends, at_owner[3], at_owner[1] = tie((sends[::-1], at_owner[3], at_owner[1]))
+        sends, at_owner[3] = tie((sends[::-1], at_owner[3]))
         got = [flip(sends[0], "blk", 3), flip(sends[1], "blk", 2)]
         canvas, *rims = owner(at_owner)
         near_got, canvas = tie((near_got, canvas))
@@ -618,8 +621,8 @@
         own, *wides = call(
             add_workers, [message, wider, wider], [VMEM] * 6, [], (1, 1), "add_workers",
         )(keep, *got, *rims)
-        got_3, got_2, got_1 = flip(wides[1], "blk", 3), flip(own, "blk", 2), flip(wides[0], "blk", 1)
-        across = [swap(own, "col"), swap(got_1[:PART], "col")]
+        got_2, got_3, got_1 = flip(own, "blk", 2), flip(wides[1], "blk", 3), flip(wides[0], "blk", 1)
+        across = [swap(value, "col") for value in (own, got_1[:PART], got_2)]
         got_3, got_2, got_1, across = tie((got_3, got_2, got_1, across))
         got = [got_1, got_2, got_3]
         last = call(
@@ -627,7 +630,7 @@
             [pltpu.VMEM((RIM, FULL), F32), pltpu.VMEM((64, HALF), F32)],
             (1, 1), "column_message",
         )(canvas.reshape(HIGH * WIDE, HALF), got[0], got[2])
-        across += [swap(got[1], "col"), swap(last, "col")]
+        across += [swap(last, "col")]
         early = call(
             lay, [shape((9, HALF, FULL), F32)] * 2, [VMEM] * 6, [], (1, 1), "lay",
         )(own, *got, *across[:2])

time: 91.7 us -> 93 us (1.014)
  waiting for transfers between devices: 42.2 us -> 35.8 us
  Pallas kernels: 21.9 us -> 25.4 us
  local copies, waits for them, and re-layouts: 1.71 us -> 3.82 us
  starting transfers between devices: 24.7 us -> 26.7 us
    ppermute x12, waiting for transfers between devices: 33.3 us -> 20.6 us  [flip(): return lax.ppermute(value, axis, [(i, i ^ step) for i in range(size)])]
    ppermute x17, waiting for transfers between devices: 8.85 us -> 15.2 us  [swap(): return lax.ppermute(value, axis, [(0, 1), (1, 0)])]
    pallas_call x1, Pallas kernels: 5.54 us -> 8.2 us  [owner(): call(functools.partial(owner_canvas, owners, capacity, wide, permuted), [...]
    unnamed x12 -> x16, local copies, waits for them, and re-layouts: 1.7 us -> 3.81 us
    ppermute x17, starting transfers between devices: 6.87 us -> 7.96 us  [swap(): return lax.ppermute(value, axis, [(0, 1), (1, 0)])]
    pallas_call x2 -> x1, Pallas kernels: 4.5 us -> 4.92 us  [shards(): call(functools.partial(prepare, owners, columns, capacity, wide, permuted...]
  transfers between devices with their start and end apart: 29 -> 29, of which waited for: 13 -> 13; matrix products, arithmetic and copies ran while one was open for 0% -> 0% of each run, Pallas kernels for 22% -> 25%
where the time goes in v10:
time: 93 us; the launch traced here: 92.7 us
  waiting for transfers between devices  35.8 us (38%)
  starting transfers between devices  26.7 us (29%)
  Pallas kernels  25.4 us (27%)
  local copies, waits for them, and re-layouts  3.82 us (4%)
  between operations  0.93 us (1%)
    ppermute x12, waiting for transfers between devices, flip(): return lax.ppermute(value, axis, [(i, i ^ step) for i in range(size)])  20.6 us
    ppermute x12, starting transfers between devices, flip(): return lax.ppermute(value, axis, [(i, i ^ step) for i in range(size)])  18.8 us
    ppermute x17, waiting for transfers between devices, swap(): return lax.ppermute(value, axis, [(0, 1), (1, 0)])  15.2 us
    pallas_call x1, Pallas kernels, owner(): call(functools.partial(owner_canvas, owners, capacity, wide, permuted), [...  8.2 us
    ppermute x17, starting transfers between devices, swap(): return lax.ppermute(value, axis, [(0, 1), (1, 0)])  7.96 us
    pallas_call x1, Pallas kernels, shards(): call(functools.partial(worker, scale, owners, columns, capacity, permuted...  6.92 us
    pallas_call x1, Pallas kernels, shards(): call(functools.partial(prepare, owners, columns, capacity, wide, permuted...  4.92 us
    unnamed x16, local copies, waits for them, and re-layouts  3.81 us
  transfers between devices with their start and end apart: 29, of which 13 were waited for; matrix products, arithmetic and copies ran while one was open for 0% of the time, Pallas kernels for 25%

profile of v10, /device:TPU:0, one launch (start us, length us, event | category | flops | bytes accessed | tf_op | source)
XLA Modules:
  0.0 92.7 jit_solution(12424368439131658616)
XLA Ops:
  2.3 1.9 %pack_cotangents.1 = (bf16[8,64,128]{2,1,0:T(8,128)(2,1)S(1)}, bf16[8,64,128]{2,1,0:T(8,128)(2,1)S(1)}, bf16[8,64,128]{2,1,0:T(8,128)(2,1)S(1)}, bf16[8,64,128]{2,1,0:T(8,128)(2,1)S(1)}) custom-call(s32[4,16]{1,0:T(4,128)S(1)} %bitcast.17, bf16[8,8,32,128]{3,2,1,0:T(8,128)(2,1)} %bitcast.13), custom_call_target="tpu_custom_call" | custom-call | flops 1 | bytes 1 | tf_op jit(solution)/shard_map/pack_cotangents/pallas_call | solution.py:530
  4.3 4.7 %collective-permute-start = (bf16[8,64,128]{2,1,0:T(8,128)(2,1)S(1)}, bf16[8,64,128]{2,1,0:T(8,128)(2,1)S(1)}, u32[]{:S(2)}, u32[]{:S(2)}) collective-permute-start(bf16[8,64,128]{2,1,0:T(8,128)(2,1)S(1)} %get-tuple-element.63), channel_id=1, source_target_pairs={{0,12},{4,8},{8,4},{12,0},{1,13},{5,9},{9,5},{13,1},{2,14},{6,10},... | collective-permute-start | bytes 393224 | tf_op jit(solution)/shard_map/ppermute | solution.py:497
  12.8 4.9 %prepare.1 = (bf16[10,160,128]{2,1,0:T(8,128)(2,1)S(1)}, bf16[10,80,128]{2,1,0:T(8,128)(2,1)S(1)}, bf16[10,80,128]{2,1,0:T(8,128)(2,1)S(1)}, bf16[10,80,128]{2,1...) custom-call(s32[4,16]{1,0:T(4,128)S(1)} %bitcast.18, ...), custom_call_target="tpu_custom_call" | custom-call | flops 1 | bytes 1 | tf_op jit(solution)/shard_map/prepare/pallas_call | solution.py:542
  17.7 3.0 %collective-permute-done.1.refs_2_ = bf16[8,64,128]{2,1,0:T(8,128)(2,1)S(1)} collective-permute-done((bf16[8,64,128]{2,1,0:T(8,128)(2,1)S(1)}, bf16[8,64,128]{2,1,0:T(8,128)(2,1)S(1)}, u32[]{:S(2)}, u32[]{:S(2)}) %collective-permute-start.1) | collective-permute-done | bytes 131104 | tf_op jit(solution)/shard_map/ppermute | solution.py:497
  20.7 3.0 %collective-permute-start.12 = (bf16[10,80,128]{2,1,0:T(8,128)(2,1)S(1)}, bf16[10,80,128]{2,1,0:T(8,128)(2,1)S(1)}, u32[]{:S(2)}, u32[]{:S(2)}) collective-permute-start(bf16[10,80,128]{2,1,0:T(8,128)(2,1)S(1)} %get-tuple-element.82), channel_id=1, source_target_pairs={{0,4},{4,0},{8,12},{12,8},{1,5},{5,1},{9,13},{13,9},{2,6},{6,2},{1... | collective-permute-start | bytes 614408 | tf_op jit(solution)/shard_map/ppermute | solution.py:497
  25.6 6.9 %worker.1 = (f32[4,2,9,16,256]{4,3,2,1,0:T(8,128)S(1)}, bf16[2,2,9,16,256]{4,3,2,1,0:T(8,128)(2,1)S(1)}, bf16[2,2,9,16,256]{4,3,2,1,0:T(8,128)(2,1)S(1)}) custom-call(s32[4,16]{1,0:T(4,128)S(1)} %bitcast.19, bf16[8,64,128]{2,1,0:T(8,128)(2,1)S(1)} %get-tuple-element.73.refs_0_, bf16[8,64,128]{2,1,0:T(8,128)(2,1)S(1)} %collective-permute-done.2.refs_1_, ...), custom_call_target="tpu_custom_call" | custom-call | flops 1 | bytes 1 | tf_op jit(solution)/shard_map/worker/pallas_call | solution.py:568
  33.6 1.5 %collective-permute-start.13 = (bf16[2,2,9,16,256]{4,3,2,1,0:T(8,128)(2,1)S(1)}, bf16[2,2,9,16,256]{4,3,2,1,0:T(8,128)(2,1)S(1)}, u32[]{:S(2)}, u32[]{:S(2)}) collective-permute-start(bf16[2,2,9,16,256]{4,3,2,1,0:T(8,128)(2,1)S(1)} %get-tuple-element.86), channel_id=1, source_target_pairs={{0,2},{2,0},{1,3},{3,1},{4,6},{6,4},{5,7},{7,5},{8,10},{10,8},{9,1... | collective-permute-start | bytes 884744 | tf_op jit(solution)/shard_map/ppermute | solution.py:492
  35.1 1.5 %collective-permute-start.14 = (bf16[10,80,128]{2,1,0:T(8,128)(2,1)S(1)}, bf16[10,80,128]{2,1,0:T(8,128)(2,1)S(1)}, u32[]{:S(2)}, u32[]{:S(2)}) collective-permute-start(bf16[10,80,128]{2,1,0:T(8,128)(2,1)S(1)} %get-tuple-element.89), channel_id=1, source_target_pairs={{0,12},{4,8},{8,4},{12,0},{1,13},{5,9},{9,5},{13,1},{2,14},{6,10},... | collective-permute-start | bytes 614408 | tf_op jit(solution)/shard_map/ppermute | solution.py:497
  37.6 5.9 %collective-permute-done.13.got = bf16[2,2,9,16,256]{4,3,2,1,0:T(8,128)(2,1)S(1)} collective-permute-done((bf16[2,2,9,16,256]{4,3,2,1,0:T(8,128)(2,1)S(1)}, bf16[2,2,9,16,256]{4,3,2,1,0:T(8,128)(2,1)S(1)}, u32[]{:S(2)}, u32[]{:S(2)}) %collective-permute-start.13) | collective-permute-done | bytes 294944 | tf_op jit(solution)/shard_map/ppermute | solution.py:492
  44.1 1.5 %collective-permute-start.19 = (bf16[2,9,16,256]{3,2,1,0:T(8,128)(2,1)S(1)}, bf16[2,9,16,256]{3,2,1,0:T(8,128)(2,1)S(1)}, u32[]{:S(2)}, u32[]{:S(2)}) collective-permute-start(bf16[2,9,16,256]{3,2,1,0:T(8,128)(2,1)S(1)} %get-tuple-element.96), channel_id=1, source_target_pairs={{0,12},{4,8},{8,4},{12,0},{1,13},{5,9},{9,5},{13,1},{2,14},{6,10},... | collective-permute-start | bytes 442376 | tf_op jit(solution)/shard_map/ppermute | solution.py:497
  45.6 1.3 %collective-permute-start.20 = (bf16[2,9,16,256]{3,2,1,0:T(8,128)(2,1)S(1)}, bf16[2,9,16,256]{3,2,1,0:T(8,128)(2,1)S(1)}, u32[]{:S(2)}, u32[]{:S(2)}) collective-permute-start(bf16[2,9,16,256]{3,2,1,0:T(8,128)(2,1)S(1)} %get-tuple-element.97), channel_id=1, source_target_pairs={{0,8},{4,12},{8,0},{12,4},{1,9},{5,13},{9,1},{13,5},{2,10},{6,14},... | collective-permute-start | bytes 442376 | tf_op jit(solution)/shard_map/ppermute | solution.py:497
  47.0 8.2 %owner_canvas.1 = (f32[68,40,128]{2,1,0:T(8,128)S(1)}, bf16[48,256]{1,0:T(8,128)(2,1)S(1)}, bf16[48,256]{1,0:T(8,128)(2,1)S(1)}) custom-call(s32[4,16]{1,0:T(4,128)S(1)} %bitcast.20, bf16[10,80,128]{2,1,0:T(8,128)(2,1)S(1)} %get-tuple-element.79.refs_0_, bf16[10,80,128]{2,1,0:T(8,128)(2,1)S(1)} %collective-permute-done.12.refs_1_, ...), custom_call_target="tpu_custom_call" | custom-call | flops 1 | bytes 1 | tf_op jit(solution)/shard_map/owner_canvas/pallas_call | solution.py:594
  55.3 1.7 %collective-permute-start.21 = (bf16[2,9,16,256]{3,2,1,0:T(8,128)(2,1)S(1)}, bf16[2,9,16,256]{3,2,1,0:T(8,128)(2,1)S(1)}, u32[]{:S(2)}, u32[]{:S(2)}) collective-permute-start(bf16[2,9,16,256]{3,2,1,0:T(8,128)(2,1)S(1)} %get-tuple-element.98), channel_id=1, source_target_pairs={{0,4},{4,0},{8,12},{12,8},{1,5},{5,1},{9,13},{13,9},{2,6},{6,2},{1... | collective-permute-start | bytes 442376 | tf_op jit(solution)/shard_map/ppermute | solution.py:497
  56.9 3.8 %collective-permute-done.20.got_2 = bf16[2,9,16,256]{3,2,1,0:T(8,128)(2,1)S(1)} collective-permute-done((bf16[2,9,16,256]{3,2,1,0:T(8,128)(2,1)S(1)}, bf16[2,9,16,256]{3,2,1,0:T(8,128)(2,1)S(1)}, u32[]{:S(2)}, u32[]{:S(2)}) %collective-permute-start.20) | collective-permute-done | bytes 147488 | tf_op jit(solution)/shard_map/ppermute | solution.py:497
  60.8 3.0 %collective-permute-done.21.got_1 = bf16[2,9,16,256]{3,2,1,0:T(8,128)(2,1)S(1)} collective-permute-done((bf16[2,9,16,256]{3,2,1,0:T(8,128)(2,1)S(1)}, bf16[2,9,16,256]{3,2,1,0:T(8,128)(2,1)S(1)}, u32[]{:S(2)}, u32[]{:S(2)}) %collective-permute-start.21) | collective-permute-done | bytes 147488 | tf_op jit(solution)/shard_map/ppermute | solution.py:497
  64.0 2.7 %collective-permute-start.23 = (bf16[288,256]{1,0:T(8,128)(2,1)S(1)}, bf16[288,256]{1,0:T(8,128)(2,1)S(1)}, u32[]{:S(2)}, u32[]{:S(2)}) collective-permute-start(bf16[288,256]{1,0:T(8,128)(2,1)S(1)} %get-tuple-element.102.refs_0_), channel_id=1, source_target_pairs={{0,8},{4,12},{8,0},{12,4},{1,9},{5,13},{9,1},{13,5},{2,10},{6,14},... | collective-permute-start | bytes 442376 | tf_op jit(solution)/shard_map/ppermute | solution.py:497
  66.6 1.7 %collective-permute-start.22 = (bf16[336,256]{1,0:T(8,128)(2,1)S(1)}, bf16[336,256]{1,0:T(8,128)(2,1)S(1)}, u32[]{:S(2)}, u32[]{:S(2)}) collective-permute-start(bf16[336,256]{1,0:T(8,128)(2,1)S(1)} %get-tuple-element.101), channel_id=1, source_target_pairs={{0,12},{4,8},{8,4},{12,0},{1,13},{5,9},{9,5},{13,1},{2,14},{6,10},... | collective-permute-start | bytes 516104 | tf_op jit(solution)/shard_map/ppermute | solution.py:497
  68.9 9.6 %collective-permute-done.23.refs_2_ = bf16[288,256]{1,0:T(8,128)(2,1)S(1)} collective-permute-done((bf16[288,256]{1,0:T(8,128)(2,1)S(1)}, bf16[288,256]{1,0:T(8,128)(2,1)S(1)}, u32[]{:S(2)}, u32[]{:S(2)}) %collective-permute-start.23) | collective-permute-done | bytes 147488 | tf_op jit(solution)/shard_map/ppermute | solution.py:497
  79.1 1.5 %collective-permute-start.26 = (bf16[288,256]{1,0:T(8,128)(2,1)S(1)}, bf16[288,256]{1,0:T(8,128)(2,1)S(1)}, u32[]{:S(2)}, u32[]{:S(2)}) collective-permute-start(bf16[288,256]{1,0:T(8,128)(2,1)S(1)} %slice.4), channel_id=1, source_target_pairs={{0,2},{2,0},{1,3},{3,1},{4,6},{6,4},{5,7},{7,5},{8,10},{10,8},{9,1... | collective-permute-start | bytes 442376 | tf_op jit(solution)/shard_map/ppermute | solution.py:492
  80.6 3.0 %collective-permute-done.27.late = bf16[288,256]{1,0:T(8,128)(2,1)S(1)} collective-permute-done((bf16[288,256]{1,0:T(8,128)(2,1)S(1)}, bf16[288,256]{1,0:T(8,128)(2,1)S(1)}, u32[]{:S(2)}, u32[]{:S(2)}) %collective-permute-start.27) | collective-permute-done | bytes 147488 | tf_op jit(solution)/shard_map/ppermute | solution.py:492
  83.7 1.6 %collective-permute-done.26.refs_5_ = bf16[288,256]{1,0:T(8,128)(2,1)S(1)} collective-permute-done((bf16[288,256]{1,0:T(8,128)(2,1)S(1)}, bf16[288,256]{1,0:T(8,128)(2,1)S(1)}, u32[]{:S(2)}, u32[]{:S(2)}) %collective-permute-start.26) | collective-permute-done | bytes 147488 | tf_op jit(solution)/shard_map/ppermute | solution.py:492
  85.9 1.5 %lay.1 = (f32[9,128,256]{2,1,0:T(8,128)}, f32[9,128,256]{2,1,0:T(8,128)}) custom-call(bf16[288,256]{1,0:T(8,128)(2,1)S(1)} %get-tuple-element.102.refs_0_, bf16[336,256]{1,0:T(8,128)(2,1)S(1)} %collective-permute-done.24.got_1.refs_1_, bf16[288,256]{1,0:T(8,128)(2,1)S(1)} %collective-permute-done.23.refs_2_, ...), custom_call_target="tpu_custom_call" | custom-call | flops 1 | bytes 1 | tf_op jit(solution)/shard_map/lay/pallas_call | solution.py:634
  87.4 3.4 %collective-permute-done.28.last = bf16[352,256]{1,0:T(8,128)(2,1)S(1)} collective-permute-done((bf16[352,256]{1,0:T(8,128)(2,1)S(1)}, bf16[352,256]{1,0:T(8,128)(2,1)S(1)}, u32[]{:S(2)}, u32[]{:S(2)}) %collective-permute-start.28) | collective-permute-done | bytes 180256 | tf_op jit(solution)/shard_map/ppermute | solution.py:492
  90.9 1.7 %finish.1 = (bf16[64,32,128]{2,1,0:T(8,128)(2,1)}, f32[9,128,256]{2,1,0:T(8,128)}, f32[9,128,256]{2,1,0:T(8,128)}) custom-call(bf16[64,32,128]{2,1,0:T(8,128)(2,1)S(1)} %copy-done.1, f32[68,40,128]{2,1,0:T(8,128)S(1)} %get-tuple-element.93.canvas, ...), custom_call_target="tpu_custom_call", output_to_operand_aliasing={{1}: (6, {}), {2}: (7, {})} | custom-call | flops 1 | bytes 1 | tf_op jit(solution)/shard_map/finish/pallas_call | solution.py:637
  (61 shorter events, 12.1 us)
Async XLA Ops:
  0.6 8.4 %collective-permute-start.3 = (bf16[8,8,32,128]{3,2,1,0:T(8,128)(2,1)}, bf16[8,8,32,128]{3,2,1,0:T(8,128)(2,1)S(1)}, u32[]{:S(2)}, u32[]{:S(2)}) collective-permute-start(bf16[8,8,32,128]{3,2,1,0:T(8,128)(2,1)} %bitcast.12), channel_id=1, source_target_pairs={{0,1},{1,0},{2,3},{3,2},{4,5},{5,4},{6,7},{7,6},{8,9},{9,8},{10,11... | collective-permute-start | bytes 1572872 | tf_op jit(solution)/shard_map/ppermute | solution.py:492
  1.1 8.5 %collective-permute-start.4 = (bf16[9,128,256]{2,1,0:T(8,128)(2,1)}, bf16[9,128,256]{2,1,0:T(8,128)(2,1)S(1)}, u32[]{:S(2)}, u32[]{:S(2)}) collective-permute-start(bf16[9,128,256]{2,1,0:T(8,128)(2,1)} %refs_10_.1), channel_id=1, source_target_pairs={{0,1},{1,0},{2,3},{3,2},{4,5},{5,4},{6,7},{7,6},{8,9},{9,8},{10,11... | collective-permute-start | bytes 1769480 | tf_op jit(solution)/shard_map/ppermute | solution.py:492
  1.2 22.5 %collective-permute-start.9 = (bf16[10,160,128]{2,1,0:T(8,128)(2,1)}, bf16[10,160,128]{2,1,0:T(8,128)(2,1)S(1)}, u32[]{:S(2)}, u32[]{:S(2)}) collective-permute-start(bf16[10,160,128]{2,1,0:T(8,128)(2,1)} %bitcast.15), channel_id=1, source_target_pairs={{0,1},{1,0},{2,3},{3,2},{4,5},{5,4},{6,7},{7,6},{8,9},{9,8},{10,11... | collective-permute-start | bytes 1228808 | tf_op jit(solution)/shard_map/ppermute | solution.py:492
  4.3 13.4 %collective-permute-start = (bf16[8,64,128]{2,1,0:T(8,128)(2,1)S(1)}, bf16[8,64,128]{2,1,0:T(8,128)(2,1)S(1)}, u32[]{:S(2)}, u32[]{:S(2)}) collective-permute-start(bf16[8,64,128]{2,1,0:T(8,128)(2,1)S(1)} %get-tuple-element.63), channel_id=1, source_target_pairs={{0,12},{4,8},{8,4},{12,0},{1,13},{5,9},{9,5},{13,1},{2,14},{6,10},... | collective-permute-start | bytes 393224 | tf_op jit(solution)/shard_map/ppermute | solution.py:497
  9.0 11.7 %collective-permute-start.1 = (bf16[8,64,128]{2,1,0:T(8,128)(2,1)S(1)}, bf16[8,64,128]{2,1,0:T(8,128)(2,1)S(1)}, u32[]{:S(2)}, u32[]{:S(2)}) collective-permute-start(bf16[8,64,128]{2,1,0:T(8,128)(2,1)S(1)} %get-tuple-element.64), channel_id=1, source_target_pairs={{0,8},{4,12},{8,0},{12,4},{1,9},{5,13},{9,1},{13,5},{2,10},{6,14},... | collective-permute-start | bytes 393224 | tf_op jit(solution)/shard_map/ppermute | solution.py:497
  9.0 11.7 %collective-permute-start.2 = (bf16[8,64,128]{2,1,0:T(8,128)(2,1)S(1)}, bf16[8,64,128]{2,1,0:T(8,128)(2,1)S(1)}, u32[]{:S(2)}, u32[]{:S(2)}) collective-permute-start(bf16[8,64,128]{2,1,0:T(8,128)(2,1)S(1)} %get-tuple-element.65), channel_id=1, source_target_pairs={{0,4},{4,0},{8,12},{12,8},{1,5},{5,1},{9,13},{13,9},{2,6},{6,2},{1... | collective-permute-start | bytes 393224 | tf_op jit(solution)/shard_map/ppermute | solution.py:497
  20.7 3.6 %collective-permute-start.5 = (bf16[8,64,128]{2,1,0:T(8,128)(2,1)S(1)}, bf16[8,64,128]{2,1,0:T(8,128)(2,1)S(1)}, u32[]{:S(2)}, u32[]{:S(2)}) collective-permute-start(bf16[8,64,128]{2,1,0:T(8,128)(2,1)S(1)} %get-tuple-element.73.refs_0_), channel_id=1, source_target_pairs={{0,1},{1,0},{2,3},{3,2},{4,5},{5,4},{6,7},{7,6},{8,9},{9,8},{10,11... | collective-permute-start | bytes 393224 | tf_op jit(solution)/shard_map/ppermute | solution.py:492
  20.7 12.7 %collective-permute-start.11 = (bf16[10,80,128]{2,1,0:T(8,128)(2,1)S(1)}, bf16[10,80,128]{2,1,0:T(8,128)(2,1)S(1)}, u32[]{:S(2)}, u32[]{:S(2)}) collective-permute-start(bf16[10,80,128]{2,1,0:T(8,128)(2,1)S(1)} %get-tuple-element.81), channel_id=1, source_target_pairs={{0,8},{4,12},{8,0},{12,4},{1,9},{5,13},{9,1},{13,5},{2,10},{6,14},... | collective-permute-start | bytes 614408 | tf_op jit(solution)/shard_map/ppermute | solution.py:497
  20.7 12.9 %collective-permute-start.12 = (bf16[10,80,128]{2,1,0:T(8,128)(2,1)S(1)}, bf16[10,80,128]{2,1,0:T(8,128)(2,1)S(1)}, u32[]{:S(2)}, u32[]{:S(2)}) collective-permute-start(bf16[10,80,128]{2,1,0:T(8,128)(2,1)S(1)} %get-tuple-element.82), channel_id=1, source_target_pairs={{0,4},{4,0},{8,12},{12,8},{1,5},{5,1},{9,13},{13,9},{2,6},{6,2},{1... | collective-permute-start | bytes 614408 | tf_op jit(solution)/shard_map/ppermute | solution.py:497
  33.6 9.9 %collective-permute-start.13 = (bf16[2,2,9,16,256]{4,3,2,1,0:T(8,128)(2,1)S(1)}, bf16[2,2,9,16,256]{4,3,2,1,0:T(8,128)(2,1)S(1)}, u32[]{:S(2)}, u32[]{:S(2)}) collective-permute-start(bf16[2,2,9,16,256]{4,3,2,1,0:T(8,128)(2,1)S(1)} %get-tuple-element.86), channel_id=1, source_target_pairs={{0,2},{2,0},{1,3},{3,1},{4,6},{6,4},{5,7},{7,5},{8,10},{10,8},{9,1... | collective-permute-start | bytes 884744 | tf_op jit(solution)/shard_map/ppermute | solution.py:492
  35.1 8.5 %collective-permute-start.14 = (bf16[10,80,128]{2,1,0:T(8,128)(2,1)S(1)}, bf16[10,80,128]{2,1,0:T(8,128)(2,1)S(1)}, u32[]{:S(2)}, u32[]{:S(2)}) collective-permute-start(bf16[10,80,128]{2,1,0:T(8,128)(2,1)S(1)} %get-tuple-element.89), channel_id=1, source_target_pairs={{0,12},{4,8},{8,4},{12,0},{1,13},{5,9},{9,5},{13,1},{2,14},{6,10},... | collective-permute-start | bytes 614408 | tf_op jit(solution)/shard_map/ppermute | solution.py:497
  36.6 18.6 %collective-permute-start.10 = (bf16[2,2,9,16,256]{4,3,2,1,0:T(8,128)(2,1)S(1)}, bf16[2,2,9,16,256]{4,3,2,1,0:T(8,128)(2,1)S(1)}, u32[]{:S(2)}, u32[]{:S(2)}) collective-permute-start(bf16[2,2,9,16,256]{4,3,2,1,0:T(8,128)(2,1)S(1)} %get-tuple-element.78), channel_id=1, source_target_pairs={{0,2},{2,0},{1,3},{3,1},{4,6},{6,4},{5,7},{7,5},{8,10},{10,8},{9,1... | collective-permute-start | bytes 884744 | tf_op jit(solution)/shard_map/ppermute | solution.py:492
  37.1 7.1 %collective-permute-start.15 = (bf16[10,80,128]{2,1,0:T(8,128)(2,1)S(1)}, bf16[10,80,128]{2,1,0:T(8,128)(2,1)S(1)}, u32[]{:S(2)}, u32[]{:S(2)}) collective-permute-start(bf16[10,80,128]{2,1,0:T(8,128)(2,1)S(1)} %get-tuple-element.79.refs_0_), channel_id=1, source_target_pairs={{0,1},{1,0},{2,3},{3,2},{4,5},{5,4},{6,7},{7,6},{8,9},{9,8},{10,11... | collective-permute-start | bytes 614408 | tf_op jit(solution)/shard_map/ppermute | solution.py:492
  37.1 8.5 %collective-permute-start.16 = (bf16[10,80,128]{2,1,0:T(8,128)(2,1)S(1)}, bf16[10,80,128]{2,1,0:T(8,128)(2,1)S(1)}, u32[]{:S(2)}, u32[]{:S(2)}) collective-permute-start(bf16[10,80,128]{2,1,0:T(8,128)(2,1)S(1)} %collective-permute-done.12.refs_1_), channel_id=1, source_target_pairs={{0,1},{1,0},{2,3},{3,2},{4,5},{5,4},{6,7},{7,6},{8,9},{9,8},{10,11... | collective-permute-start | bytes 614408 | tf_op jit(solution)/shard_map/ppermute | solution.py:492
  44.1 12.8 %collective-permute-start.19 = (bf16[2,9,16,256]{3,2,1,0:T(8,128)(2,1)S(1)}, bf16[2,9,16,256]{3,2,1,0:T(8,128)(2,1)S(1)}, u32[]{:S(2)}, u32[]{:S(2)}) collective-permute-start(bf16[2,9,16,256]{3,2,1,0:T(8,128)(2,1)S(1)} %get-tuple-element.96), channel_id=1, source_target_pairs={{0,12},{4,8},{8,4},{12,0},{1,13},{5,9},{9,5},{13,1},{2,14},{6,10},... | collective-permute-start | bytes 442376 | tf_op jit(solution)/shard_map/ppermute | solution.py:497
  45.6 15.1 %collective-permute-start.20 = (bf16[2,9,16,256]{3,2,1,0:T(8,128)(2,1)S(1)}, bf16[2,9,16,256]{3,2,1,0:T(8,128)(2,1)S(1)}, u32[]{:S(2)}, u32[]{:S(2)}) collective-permute-start(bf16[2,9,16,256]{3,2,1,0:T(8,128)(2,1)S(1)} %get-tuple-element.97), channel_id=1, source_target_pairs={{0,8},{4,12},{8,0},{12,4},{1,9},{5,13},{9,1},{13,5},{2,10},{6,14},... | collective-permute-start | bytes 442376 | tf_op jit(solution)/shard_map/ppermute | solution.py:497
  55.3 8.5 %collective-permute-start.21 = (bf16[2,9,16,256]{3,2,1,0:T(8,128)(2,1)S(1)}, bf16[2,9,16,256]{3,2,1,0:T(8,128)(2,1)S(1)}, u32[]{:S(2)}, u32[]{:S(2)}) collective-permute-start(bf16[2,9,16,256]{3,2,1,0:T(8,128)(2,1)S(1)} %get-tuple-element.98), channel_id=1, source_target_pairs={{0,4},{4,0},{8,12},{12,8},{1,5},{5,1},{9,13},{13,9},{2,6},{6,2},{1... | collective-permute-start | bytes 442376 | tf_op jit(solution)/shard_map/ppermute | solution.py:497
  63.9 15.2 %collective-permute-start.24 = (bf16[336,256]{1,0:T(8,128)(2,1)S(1)}, bf16[336,256]{1,0:T(8,128)(2,1)S(1)}, u32[]{:S(2)}, u32[]{:S(2)}) collective-permute-start(bf16[336,256]{1,0:T(8,128)(2,1)S(1)} %get-tuple-element.103), channel_id=1, source_target_pairs={{0,4},{4,0},{8,12},{12,8},{1,5},{5,1},{9,13},{13,9},{2,6},{6,2},{1... | collective-permute-start | bytes 516104 | tf_op jit(solution)/shard_map/ppermute | solution.py:497
  64.0 14.6 %collective-permute-start.23 = (bf16[288,256]{1,0:T(8,128)(2,1)S(1)}, bf16[288,256]{1,0:T(8,128)(2,1)S(1)}, u32[]{:S(2)}, u32[]{:S(2)}) collective-permute-start(bf16[288,256]{1,0:T(8,128)(2,1)S(1)} %get-tuple-element.102.refs_0_), channel_id=1, source_target_pairs={{0,8},{4,12},{8,0},{12,4},{1,9},{5,13},{9,1},{13,5},{2,10},{6,14},... | collective-permute-start | bytes 442376 | tf_op jit(solution)/shard_map/ppermute | solution.py:497
  66.6 14.0 %collective-permute-start.22 = (bf16[336,256]{1,0:T(8,128)(2,1)S(1)}, bf16[336,256]{1,0:T(8,128)(2,1)S(1)}, u32[]{:S(2)}, u32[]{:S(2)}) collective-permute-start(bf16[336,256]{1,0:T(8,128)(2,1)S(1)} %get-tuple-element.101), channel_id=1, source_target_pairs={{0,12},{4,8},{8,4},{12,0},{1,13},{5,9},{9,5},{13,1},{2,14},{6,10},... | collective-permute-start | bytes 516104 | tf_op jit(solution)/shard_map/ppermute | solution.py:497
  68.3 12.3 %collective-permute-start.25 = (bf16[288,256]{1,0:T(8,128)(2,1)S(1)}, bf16[288,256]{1,0:T(8,128)(2,1)S(1)}, u32[]{:S(2)}, u32[]{:S(2)}) collective-permute-start(bf16[288,256]{1,0:T(8,128)(2,1)S(1)} %get-tuple-element.102.refs_0_), channel_id=1, source_target_pairs={{0,2},{2,0},{1,3},{3,1},{4,6},{6,4},{5,7},{7,5},{8,10},{10,8},{9,1... | collective-permute-start | bytes 442376 | tf_op jit(solution)/shard_map/ppermute | solution.py:492
  78.5 5.1 %collective-permute-start.27 = (bf16[288,256]{1,0:T(8,128)(2,1)S(1)}, bf16[288,256]{1,0:T(8,128)(2,1)S(1)}, u32[]{:S(2)}, u32[]{:S(2)}) collective-permute-start(bf16[288,256]{1,0:T(8,128)(2,1)S(1)} %collective-permute-done.23.refs_2_), channel_id=1, source_target_pairs={{0,2},{2,0},{1,3},{3,1},{4,6},{6,4},{5,7},{7,5},{8,10},{10,8},{9,1... | collective-permute-start | bytes 442376 | tf_op jit(solution)/shard_map/ppermute | solution.py:492
  79.1 6.2 %collective-permute-start.26 = (bf16[288,256]{1,0:T(8,128)(2,1)S(1)}, bf16[288,256]{1,0:T(8,128)(2,1)S(1)}, u32[]{:S(2)}, u32[]{:S(2)}) collective-permute-start(bf16[288,256]{1,0:T(8,128)(2,1)S(1)} %slice.4), channel_id=1, source_target_pairs={{0,2},{2,0},{1,3},{3,1},{4,6},{6,4},{5,7},{7,5},{8,10},{10,8},{9,1... | collective-permute-start | bytes 442376 | tf_op jit(solution)/shard_map/ppermute | solution.py:492
  85.3 5.6 %collective-permute-start.28 = (bf16[352,256]{1,0:T(8,128)(2,1)S(1)}, bf16[352,256]{1,0:T(8,128)(2,1)S(1)}, u32[]{:S(2)}, u32[]{:S(2)}) collective-permute-start(bf16[352,256]{1,0:T(8,128)(2,1)S(1)} %column_message.1), channel_id=1, source_target_pairs={{0,2},{2,0},{1,3},{3,1},{4,6},{6,4},{5,7},{7,5},{8,10},{10,8},{9,1... | collective-permute-start | bytes 540680 | tf_op jit(solution)/shard_map/ppermute | solution.py:492
  (13 other events, 62.1 us)

commit v11 on v10

--- a/solution.py
+++ b/solution.py
@@ -227,26 +227,19 @@
         outs[0][grad, tap] = value
 
 
-def spread(padded, weight, total, places):
-    height, size = padded.shape[0], total.shape[1]
-    for dy in range(3):
-        windows, taps = [], []
-        for dx in range(3):
-            at = (2 - dx) * places
-            windows.append(padded[:, at : at + size].reshape(height * size, FULL))
-            taps.append(weight[3 * dy + dx])
-        part = dot_nt(jnp.concatenate(windows, axis=1), jnp.concatenate(taps, axis=1))
-        part = part.reshape(height, size, total.shape[2])
-        if dy == 0:
-            total[:height] = part
-            total[height:] = jnp.zeros((2, size, total.shape[2]), F32)
-        else:
-            total[dy : dy + height] += part
-
-
-def pad_sides(padded, places):
-    for side in (slice(0, 2 * places), slice(padded.shape[1] - 2 * places, None)):
-        padded[:, side] = jnp.zeros((padded.shape[0], 2 * places, FULL), BF16)
+def spread(values, weight, total, places):
+    height, extent = values.shape[:2]
+    inputs = values[...].reshape(height * extent, FULL)
+    width = weight.shape[1]
+    group = FULL // width
+    total[...] = jnp.zeros_like(total)
+    for tap in range(0, 9, group):
+        taps = range(tap, min(tap + group, 9))
+        part = dot_nt(inputs, jnp.concatenate([weight[k] for k in taps], axis=0))
+        for k in taps:
+            spot = (slice(k // 3, k // 3 + height), pl.ds(k % 3 * places, extent))
+            here = part[:, (k - tap) * width : (k - tap + 1) * width]
+            total[spot] = total[spot] + here.reshape(height, extent, width)
 
 
 def second_gradient(scale, owners, capacity, permuted, routing, *refs):
@@ -266,9 +259,8 @@
         got = jnp.concatenate(
             [ordered(own[o][u], other[o][u], 1) for o in range(owners)], axis=0
         )
-        cot[u, 2 * PER_WORKER : 2 * PER_WORKER + rows] = dot(pick, got).astype(BF16)
-    pad_sides(cot, PER_WORKER)
-    grads = cot[:, 2 * PER_WORKER : 2 * PER_WORKER + rows].reshape(BLOCK * rows, FULL)
+        cot[u] = dot(pick, got).astype(BF16)
+    grads = cot[...].reshape(BLOCK * rows, FULL)
     for dy in range(3):
         windows = [
             masked[dy : dy + BLOCK, dx * PER_WORKER : (dx + BLOCK) * PER_WORKER] for dx in range(3)
@@ -308,8 +300,7 @@
         block = jnp.concatenate(
             [ordered(tile[r, u], tile_other[r, u], 1) for r in range(TILE_ROWS)], axis=0
         )
-        cot[u, 2 * TILE_BLOCKS : (2 + BLOCK) * TILE_BLOCKS] = dot(turn, block).astype(BF16)
-    pad_sides(cot, TILE_BLOCKS)
+        cot[u] = dot(turn, block).astype(BF16)
     full[...] = ordered(second[...], second_other[...], 1)
     spread(cot, full, total, TILE_BLOCKS)
     out[...] = total[...].astype(BF16).reshape(out.shape)
@@ -375,8 +366,7 @@
             [ordered(got[w][m], got_other[w][m], 1) for w in range(owners)], axis=0
         )
         value = jnp.where(dot(pick, block) > 0, total[m].reshape(into, FULL).astype(F32), 0.0)
-        pre[m, 2 * TILE_BLOCKS : 2 * TILE_BLOCKS + into] = value.astype(BF16)
-    pad_sides(pre, TILE_BLOCKS)
+        pre[m] = value.astype(BF16)
     spread(pre, first, grown, TILE_BLOCKS)
     height, depth = TILE_ROWS * WIDE, OUTER * TILE_BLOCKS
     row, lane = iota((height, depth), 0), iota((height, depth), 1)
@@ -549,7 +539,7 @@
         + tables
         + [
             pltpu.VMEM((MIDDLE, MIDDLE * TILE_BLOCKS, FULL), F32),
-            pltpu.VMEM((BLOCK, OUTER * TILE_BLOCKS, FULL), BF16),
+            pltpu.VMEM((BLOCK, BLOCK * TILE_BLOCKS, FULL), BF16),
             pltpu.VMEM((9, FULL, FULL), BF16),
         ],
         (1, 1), "prepare",
@@ -571,7 +561,7 @@
         [SMEM] + [VMEM] * (2 * parts + 4) + [HBM],
         counts
         + [
-            pltpu.VMEM((BLOCK, OUTER * PER_WORKER, FULL), BF16),
+            pltpu.VMEM((BLOCK, BLOCK * PER_WORKER, FULL), BF16),
             pltpu.VMEM((MIDDLE, MIDDLE * PER_WORKER, FULL), F32),
             pltpu.VMEM((MIDDLE, MIDDLE, PER_WORKER, FULL), BF16),
             pltpu.VMEM((9, FULL, FULL), BF16),
@@ -597,7 +587,7 @@
             [SMEM] + [VMEM] * (2 * len(at_owner) + 2),
             tables
             + [
-                pltpu.VMEM((MIDDLE, (OUTER + 2) * TILE_BLOCKS, FULL), BF16),
+                pltpu.VMEM((MIDDLE, MIDDLE * TILE_BLOCKS, FULL), BF16),
                 pltpu.VMEM((OUTER, OUTER * TILE_BLOCKS, HALF), F32),
             ],
             (1, 1), "owner_canvas",
@@ -622,7 +612,7 @@
             add_workers, [message, wider, wider], [VMEM] * 6, [], (1, 1), "add_workers",
         )(keep, *got, *rims)
         got_2, got_3, got_1 = flip(own, "blk", 2), flip(wides[1], "blk", 3), flip(wides[0], "blk", 1)
-        across = [swap(value, "col") for value in (own, got_1[:PART], got_2)]
+        across = [swap(value, "col") for value in (own, got_1[:PART])]
         got_3, got_2, got_1, across = tie((got_3, got_2, got_1, across))
         got = [got_1, got_2, got_3]
         last = call(
@@ -630,7 +620,7 @@
             [pltpu.VMEM((RIM, FULL), F32), pltpu.VMEM((64, HALF), F32)],
             (1, 1), "column_message",
         )(canvas.reshape(HIGH * WIDE, HALF), got[0], got[2])
-        across += [swap(last, "col")]
+        across += [swap(got_2, "col"), swap(last, "col")]
         early = call(
             lay, [shape((9, HALF, FULL), F32)] * 2, [VMEM] * 6, [], (1, 1), "lay",
         )(own, *got, *across[:2])

time: 93 us -> 88 us (0.946)
  Pallas kernels: 25.4 us -> 21.7 us
  waiting for transfers between devices: 35.8 us -> 34.4 us
    ppermute x17, waiting for transfers between devices: 15.2 us -> 11.2 us  [swap(): return lax.ppermute(value, axis, [(0, 1), (1, 0)])]
    pallas_call x1, Pallas kernels: 8.2 us -> 5.54 us  [owner(): call(functools.partial(owner_canvas, owners, capacity, wide, permuted), [...]
    ppermute x12, waiting for transfers between devices: 20.6 us -> 23.2 us  [flip(): return lax.ppermute(value, axis, [(i, i ^ step) for i in range(size)])]
  transfers between devices with their start and end apart: 29 -> 29, of which waited for: 13 -> 12; matrix products, arithmetic and copies ran while one was open for 0% -> 0% of each run, Pallas kernels for 25% -> 23%
where the time goes in v11:
time: 88 us; the launch traced here: 87.6 us
  waiting for transfers between devices  34.4 us (39%)
  starting transfers between devices  26.8 us (30%)
  Pallas kernels  21.7 us (25%)
  local copies, waits for them, and re-layouts  3.82 us (4%)
  between operations  0.93 us (1%)
    ppermute x12, waiting for transfers between devices, flip(): return lax.ppermute(value, axis, [(i, i ^ step) for i in range(size)])  23.2 us
    ppermute x12, starting transfers between devices, flip(): return lax.ppermute(value, axis, [(i, i ^ step) for i in range(size)])  18.3 us
    ppermute x17, waiting for transfers between devices, swap(): return lax.ppermute(value, axis, [(0, 1), (1, 0)])  11.2 us
    ppermute x17, starting transfers between devices, swap(): return lax.ppermute(value, axis, [(0, 1), (1, 0)])  8.48 us
    pallas_call x1, Pallas kernels, shards(): call(functools.partial(worker, scale, owners, columns, capacity, permuted...  6.51 us
    pallas_call x1, Pallas kernels, owner(): call(functools.partial(owner_canvas, owners, capacity, wide, permuted), [...  5.54 us
    pallas_call x1, Pallas kernels, shards(): call(functools.partial(prepare, owners, columns, capacity, wide, permuted...  4.31 us
    unnamed x16, local copies, waits for them, and re-layouts  3.81 us
  transfers between devices with their start and end apart: 29, of which 12 were waited for; matrix products, arithmetic and copies ran while one was open for 0% of the time, Pallas kernels for 23%

profile of v11, /device:TPU:0, one launch (start us, length us, event | category | flops | bytes accessed | tf_op | source)
XLA Modules:
  0.0 87.6 jit_solution(4064651554913698761)
XLA Ops:
  2.3 1.9 %pack_cotangents.1 = (bf16[8,64,128]{2,1,0:T(8,128)(2,1)S(1)}, bf16[8,64,128]{2,1,0:T(8,128)(2,1)S(1)}, bf16[8,64,128]{2,1,0:T(8,128)(2,1)S(1)}, bf16[8,64,128]{2,1,0:T(8,128)(2,1)S(1)}) custom-call(s32[4,16]{1,0:T(4,128)S(1)} %bitcast.17, bf16[8,8,32,128]{3,2,1,0:T(8,128)(2,1)} %bitcast.13), custom_call_target="tpu_custom_call" | custom-call | flops 1 | bytes 1 | tf_op jit(solution)/shard_map/pack_cotangents/pallas_call | solution.py:520
  4.3 4.7 %collective-permute-start = (bf16[8,64,128]{2,1,0:T(8,128)(2,1)S(1)}, bf16[8,64,128]{2,1,0:T(8,128)(2,1)S(1)}, u32[]{:S(2)}, u32[]{:S(2)}) collective-permute-start(bf16[8,64,128]{2,1,0:T(8,128)(2,1)S(1)} %get-tuple-element.62), channel_id=1, source_target_pairs={{0,12},{4,8},{8,4},{12,0},{1,13},{5,9},{9,5},{13,1},{2,14},{6,10},... | collective-permute-start | bytes 393224 | tf_op jit(solution)/shard_map/ppermute | solution.py:487
  12.8 4.3 %prepare.1 = (bf16[10,160,128]{2,1,0:T(8,128)(2,1)S(1)}, bf16[10,80,128]{2,1,0:T(8,128)(2,1)S(1)}, bf16[10,80,128]{2,1,0:T(8,128)(2,1)S(1)}, bf16[10,80,128]{2,1...) custom-call(s32[4,16]{1,0:T(4,128)S(1)} %bitcast.18, ...), custom_call_target="tpu_custom_call" | custom-call | flops 1 | bytes 1 | tf_op jit(solution)/shard_map/prepare/pallas_call | solution.py:532
  17.1 3.6 %collective-permute-done.1.refs_2_ = bf16[8,64,128]{2,1,0:T(8,128)(2,1)S(1)} collective-permute-done((bf16[8,64,128]{2,1,0:T(8,128)(2,1)S(1)}, bf16[8,64,128]{2,1,0:T(8,128)(2,1)S(1)}, u32[]{:S(2)}, u32[]{:S(2)}) %collective-permute-start.1) | collective-permute-done | bytes 131104 | tf_op jit(solution)/shard_map/ppermute | solution.py:487
  20.7 3.0 %collective-permute-start.12 = (bf16[10,80,128]{2,1,0:T(8,128)(2,1)S(1)}, bf16[10,80,128]{2,1,0:T(8,128)(2,1)S(1)}, u32[]{:S(2)}, u32[]{:S(2)}) collective-permute-start(bf16[10,80,128]{2,1,0:T(8,128)(2,1)S(1)} %get-tuple-element.81), channel_id=1, source_target_pairs={{0,4},{4,0},{8,12},{12,8},{1,5},{5,1},{9,13},{13,9},{2,6},{6,2},{1... | collective-permute-start | bytes 614408 | tf_op jit(solution)/shard_map/ppermute | solution.py:487
  25.6 6.5 %worker.1 = (f32[4,2,9,16,256]{4,3,2,1,0:T(8,128)S(1)}, bf16[2,2,9,16,256]{4,3,2,1,0:T(8,128)(2,1)S(1)}, bf16[2,2,9,16,256]{4,3,2,1,0:T(8,128)(2,1)S(1)}) custom-call(s32[4,16]{1,0:T(4,128)S(1)} %bitcast.19, bf16[8,64,128]{2,1,0:T(8,128)(2,1)S(1)} %get-tuple-element.72.refs_0_, bf16[8,64,128]{2,1,0:T(8,128)(2,1)S(1)} %collective-permute-done.2.refs_1_, ...), custom_call_target="tpu_custom_call" | custom-call | flops 1 | bytes 1 | tf_op jit(solution)/shard_map/worker/pallas_call | solution.py:558
  32.2 1.3 %collective-permute-done.11.refs_2_ = bf16[10,80,128]{2,1,0:T(8,128)(2,1)S(1)} collective-permute-done((bf16[10,80,128]{2,1,0:T(8,128)(2,1)S(1)}, bf16[10,80,128]{2,1,0:T(8,128)(2,1)S(1)}, u32[]{:S(2)}, u32[]{:S(2)}) %collective-permute-start.11) | collective-permute-done | bytes 204832 | tf_op jit(solution)/shard_map/ppermute | solution.py:487
  33.6 1.5 %collective-permute-start.13 = (bf16[2,2,9,16,256]{4,3,2,1,0:T(8,128)(2,1)S(1)}, bf16[2,2,9,16,256]{4,3,2,1,0:T(8,128)(2,1)S(1)}, u32[]{:S(2)}, u32[]{:S(2)}) collective-permute-start(bf16[2,2,9,16,256]{4,3,2,1,0:T(8,128)(2,1)S(1)} %get-tuple-element.85), channel_id=1, source_target_pairs={{0,2},{2,0},{1,3},{3,1},{4,6},{6,4},{5,7},{7,5},{8,10},{10,8},{9,1... | collective-permute-start | bytes 884744 | tf_op jit(solution)/shard_map/ppermute | solution.py:482
  35.1 1.5 %collective-permute-start.14 = (bf16[10,80,128]{2,1,0:T(8,128)(2,1)S(1)}, bf16[10,80,128]{2,1,0:T(8,128)(2,1)S(1)}, u32[]{:S(2)}, u32[]{:S(2)}) collective-permute-start(bf16[10,80,128]{2,1,0:T(8,128)(2,1)S(1)} %get-tuple-element.88), channel_id=1, source_target_pairs={{0,12},{4,8},{8,4},{12,0},{1,13},{5,9},{9,5},{13,1},{2,14},{6,10},... | collective-permute-start | bytes 614408 | tf_op jit(solution)/shard_map/ppermute | solution.py:487
  37.6 5.9 %collective-permute-done.13.got = bf16[2,2,9,16,256]{4,3,2,1,0:T(8,128)(2,1)S(1)} collective-permute-done((bf16[2,2,9,16,256]{4,3,2,1,0:T(8,128)(2,1)S(1)}, bf16[2,2,9,16,256]{4,3,2,1,0:T(8,128)(2,1)S(1)}, u32[]{:S(2)}, u32[]{:S(2)}) %collective-permute-start.13) | collective-permute-done | bytes 294944 | tf_op jit(solution)/shard_map/ppermute | solution.py:482
  44.1 1.5 %collective-permute-start.19 = (bf16[2,9,16,256]{3,2,1,0:T(8,128)(2,1)S(1)}, bf16[2,9,16,256]{3,2,1,0:T(8,128)(2,1)S(1)}, u32[]{:S(2)}, u32[]{:S(2)}) collective-permute-start(bf16[2,9,16,256]{3,2,1,0:T(8,128)(2,1)S(1)} %get-tuple-element.95), channel_id=1, source_target_pairs={{0,12},{4,8},{8,4},{12,0},{1,13},{5,9},{9,5},{13,1},{2,14},{6,10},... | collective-permute-start | bytes 442376 | tf_op jit(solution)/shard_map/ppermute | solution.py:487
  45.6 1.3 %collective-permute-start.20 = (bf16[2,9,16,256]{3,2,1,0:T(8,128)(2,1)S(1)}, bf16[2,9,16,256]{3,2,1,0:T(8,128)(2,1)S(1)}, u32[]{:S(2)}, u32[]{:S(2)}) collective-permute-start(bf16[2,9,16,256]{3,2,1,0:T(8,128)(2,1)S(1)} %get-tuple-element.96), channel_id=1, source_target_pairs={{0,8},{4,12},{8,0},{12,4},{1,9},{5,13},{9,1},{13,5},{2,10},{6,14},... | collective-permute-start | bytes 442376 | tf_op jit(solution)/shard_map/ppermute | solution.py:487
  46.9 5.5 %owner_canvas.1 = (f32[68,40,128]{2,1,0:T(8,128)S(1)}, bf16[48,256]{1,0:T(8,128)(2,1)S(1)}, bf16[48,256]{1,0:T(8,128)(2,1)S(1)}) custom-call(s32[4,16]{1,0:T(4,128)S(1)} %bitcast.20, bf16[10,80,128]{2,1,0:T(8,128)(2,1)S(1)} %get-tuple-element.78.refs_0_, bf16[10,80,128]{2,1,0:T(8,128)(2,1)S(1)} %collective-permute-done.12.refs_1_, ...), custom_call_target="tpu_custom_call" | custom-call | flops 1 | bytes 1 | tf_op jit(solution)/shard_map/owner_canvas/pallas_call | solution.py:584
  52.5 1.7 %collective-permute-start.21 = (bf16[2,9,16,256]{3,2,1,0:T(8,128)(2,1)S(1)}, bf16[2,9,16,256]{3,2,1,0:T(8,128)(2,1)S(1)}, u32[]{:S(2)}, u32[]{:S(2)}) collective-permute-start(bf16[2,9,16,256]{3,2,1,0:T(8,128)(2,1)S(1)} %get-tuple-element.97), channel_id=1, source_target_pairs={{0,4},{4,0},{8,12},{12,8},{1,5},{5,1},{9,13},{13,9},{2,6},{6,2},{1... | collective-permute-start | bytes 442376 | tf_op jit(solution)/shard_map/ppermute | solution.py:487
  54.3 6.5 %collective-permute-done.20.got_2 = bf16[2,9,16,256]{3,2,1,0:T(8,128)(2,1)S(1)} collective-permute-done((bf16[2,9,16,256]{3,2,1,0:T(8,128)(2,1)S(1)}, bf16[2,9,16,256]{3,2,1,0:T(8,128)(2,1)S(1)}, u32[]{:S(2)}, u32[]{:S(2)}) %collective-permute-start.20) | collective-permute-done | bytes 147488 | tf_op jit(solution)/shard_map/ppermute | solution.py:487
  61.6 2.5 %collective-permute-start.22 = (bf16[336,256]{1,0:T(8,128)(2,1)S(1)}, bf16[336,256]{1,0:T(8,128)(2,1)S(1)}, u32[]{:S(2)}, u32[]{:S(2)}) collective-permute-start(bf16[336,256]{1,0:T(8,128)(2,1)S(1)} %get-tuple-element.100), channel_id=1, source_target_pairs={{0,12},{4,8},{8,4},{12,0},{1,13},{5,9},{9,5},{13,1},{2,14},{6,10},... | collective-permute-start | bytes 516104 | tf_op jit(solution)/shard_map/ppermute | solution.py:487
  64.7 1.4 %collective-permute-start.23 = (bf16[288,256]{1,0:T(8,128)(2,1)S(1)}, bf16[288,256]{1,0:T(8,128)(2,1)S(1)}, u32[]{:S(2)}, u32[]{:S(2)}) collective-permute-start(bf16[288,256]{1,0:T(8,128)(2,1)S(1)} %get-tuple-element.101.refs_0_), channel_id=1, source_target_pairs={{0,8},{4,12},{8,0},{12,4},{1,9},{5,13},{9,1},{13,5},{2,10},{6,14},... | collective-permute-start | bytes 442376 | tf_op jit(solution)/shard_map/ppermute | solution.py:487
  66.1 3.4 %collective-permute-done.24.got_1.refs_1_ = bf16[336,256]{1,0:T(8,128)(2,1)S(1)} collective-permute-done((bf16[336,256]{1,0:T(8,128)(2,1)S(1)}, bf16[336,256]{1,0:T(8,128)(2,1)S(1)}, u32[]{:S(2)}, u32[]{:S(2)}) %collective-permute-start.24) | collective-permute-done | bytes 172064 | tf_op jit(solution)/shard_map/ppermute | solution.py:487
  69.5 1.1 %collective-permute-start.26 = (bf16[288,256]{1,0:T(8,128)(2,1)S(1)}, bf16[288,256]{1,0:T(8,128)(2,1)S(1)}, u32[]{:S(2)}, u32[]{:S(2)}) collective-permute-start(bf16[288,256]{1,0:T(8,128)(2,1)S(1)} %slice.4), channel_id=1, source_target_pairs={{0,2},{2,0},{1,3},{3,1},{4,6},{6,4},{5,7},{7,5},{8,10},{10,8},{9,1... | collective-permute-start | bytes 442376 | tf_op jit(solution)/shard_map/ppermute | solution.py:482
  70.6 7.5 %collective-permute-done.23.refs_2_ = bf16[288,256]{1,0:T(8,128)(2,1)S(1)} collective-permute-done((bf16[288,256]{1,0:T(8,128)(2,1)S(1)}, bf16[288,256]{1,0:T(8,128)(2,1)S(1)}, u32[]{:S(2)}, u32[]{:S(2)}) %collective-permute-start.23) | collective-permute-done | bytes 147488 | tf_op jit(solution)/shard_map/ppermute | solution.py:487
  79.1 1.2 %collective-permute-start.28 = (bf16[288,256]{1,0:T(8,128)(2,1)S(1)}, bf16[288,256]{1,0:T(8,128)(2,1)S(1)}, u32[]{:S(2)}, u32[]{:S(2)}) collective-permute-start(bf16[288,256]{1,0:T(8,128)(2,1)S(1)} %collective-permute-done.23.refs_2_), channel_id=1, source_target_pairs={{0,2},{2,0},{1,3},{3,1},{4,6},{6,4},{5,7},{7,5},{8,10},{10,8},{9,1... | collective-permute-start | bytes 442376 | tf_op jit(solution)/shard_map/ppermute | solution.py:482
  80.3 1.5 %lay.1 = (f32[9,128,256]{2,1,0:T(8,128)}, f32[9,128,256]{2,1,0:T(8,128)}) custom-call(bf16[288,256]{1,0:T(8,128)(2,1)S(1)} %get-tuple-element.101.refs_0_, bf16[336,256]{1,0:T(8,128)(2,1)S(1)} %collective-permute-done.24.got_1.refs_1_, bf16[288,256]{1,0:T(8,128)(2,1)S(1)} %collective-permute-done.23.refs_2_, ...), custom_call_target="tpu_custom_call" | custom-call | flops 1 | bytes 1 | tf_op jit(solution)/shard_map/lay/pallas_call | solution.py:624
  81.8 4.0 %collective-permute-done.28.late = bf16[288,256]{1,0:T(8,128)(2,1)S(1)} collective-permute-done((bf16[288,256]{1,0:T(8,128)(2,1)S(1)}, bf16[288,256]{1,0:T(8,128)(2,1)S(1)}, u32[]{:S(2)}, u32[]{:S(2)}) %collective-permute-start.28) | collective-permute-done | bytes 147488 | tf_op jit(solution)/shard_map/ppermute | solution.py:482
  85.8 1.7 %finish.1 = (bf16[64,32,128]{2,1,0:T(8,128)(2,1)}, f32[9,128,256]{2,1,0:T(8,128)}, f32[9,128,256]{2,1,0:T(8,128)}) custom-call(bf16[64,32,128]{2,1,0:T(8,128)(2,1)S(1)} %copy-done.1, f32[68,40,128]{2,1,0:T(8,128)S(1)} %get-tuple-element.92.canvas, ...), custom_call_target="tpu_custom_call", output_to_operand_aliasing={{1}: (6, {}), {2}: (7, {})} | custom-call | flops 1 | bytes 1 | tf_op jit(solution)/shard_map/finish/pallas_call | solution.py:627
  (61 shorter events, 11.7 us)
Async XLA Ops:
  0.6 8.4 %collective-permute-start.3 = (bf16[8,8,32,128]{3,2,1,0:T(8,128)(2,1)}, bf16[8,8,32,128]{3,2,1,0:T(8,128)(2,1)S(1)}, u32[]{:S(2)}, u32[]{:S(2)}) collective-permute-start(bf16[8,8,32,128]{3,2,1,0:T(8,128)(2,1)} %bitcast.12), channel_id=1, source_target_pairs={{0,1},{1,0},{2,3},{3,2},{4,5},{5,4},{6,7},{7,6},{8,9},{9,8},{10,11... | collective-permute-start | bytes 1572872 | tf_op jit(solution)/shard_map/ppermute | solution.py:482
  1.1 8.5 %collective-permute-start.4 = (bf16[9,128,256]{2,1,0:T(8,128)(2,1)}, bf16[9,128,256]{2,1,0:T(8,128)(2,1)S(1)}, u32[]{:S(2)}, u32[]{:S(2)}) collective-permute-start(bf16[9,128,256]{2,1,0:T(8,128)(2,1)} %refs_10_.1), channel_id=1, source_target_pairs={{0,1},{1,0},{2,3},{3,2},{4,5},{5,4},{6,7},{7,6},{8,9},{9,8},{10,11... | collective-permute-start | bytes 1769480 | tf_op jit(solution)/shard_map/ppermute | solution.py:482
  1.2 22.5 %collective-permute-start.9 = (bf16[10,160,128]{2,1,0:T(8,128)(2,1)}, bf16[10,160,128]{2,1,0:T(8,128)(2,1)S(1)}, u32[]{:S(2)}, u32[]{:S(2)}) collective-permute-start(bf16[10,160,128]{2,1,0:T(8,128)(2,1)} %bitcast.15), channel_id=1, source_target_pairs={{0,1},{1,0},{2,3},{3,2},{4,5},{5,4},{6,7},{7,6},{8,9},{9,8},{10,11... | collective-permute-start | bytes 1228808 | tf_op jit(solution)/shard_map/ppermute | solution.py:482
  4.3 12.8 %collective-permute-start = (bf16[8,64,128]{2,1,0:T(8,128)(2,1)S(1)}, bf16[8,64,128]{2,1,0:T(8,128)(2,1)S(1)}, u32[]{:S(2)}, u32[]{:S(2)}) collective-permute-start(bf16[8,64,128]{2,1,0:T(8,128)(2,1)S(1)} %get-tuple-element.62), channel_id=1, source_target_pairs={{0,12},{4,8},{8,4},{12,0},{1,13},{5,9},{9,5},{13,1},{2,14},{6,10},... | collective-permute-start | bytes 393224 | tf_op jit(solution)/shard_map/ppermute | solution.py:487
  9.0 11.7 %collective-permute-start.1 = (bf16[8,64,128]{2,1,0:T(8,128)(2,1)S(1)}, bf16[8,64,128]{2,1,0:T(8,128)(2,1)S(1)}, u32[]{:S(2)}, u32[]{:S(2)}) collective-permute-start(bf16[8,64,128]{2,1,0:T(8,128)(2,1)S(1)} %get-tuple-element.63), channel_id=1, source_target_pairs={{0,8},{4,12},{8,0},{12,4},{1,9},{5,13},{9,1},{13,5},{2,10},{6,14},... | collective-permute-start | bytes 393224 | tf_op jit(solution)/shard_map/ppermute | solution.py:487
  9.0 11.7 %collective-permute-start.2 = (bf16[8,64,128]{2,1,0:T(8,128)(2,1)S(1)}, bf16[8,64,128]{2,1,0:T(8,128)(2,1)S(1)}, u32[]{:S(2)}, u32[]{:S(2)}) collective-permute-start(bf16[8,64,128]{2,1,0:T(8,128)(2,1)S(1)} %get-tuple-element.64), channel_id=1, source_target_pairs={{0,4},{4,0},{8,12},{12,8},{1,5},{5,1},{9,13},{13,9},{2,6},{6,2},{1... | collective-permute-start | bytes 393224 | tf_op jit(solution)/shard_map/ppermute | solution.py:487
  20.7 3.6 %collective-permute-start.5 = (bf16[8,64,128]{2,1,0:T(8,128)(2,1)S(1)}, bf16[8,64,128]{2,1,0:T(8,128)(2,1)S(1)}, u32[]{:S(2)}, u32[]{:S(2)}) collective-permute-start(bf16[8,64,128]{2,1,0:T(8,128)(2,1)S(1)} %get-tuple-element.72.refs_0_), channel_id=1, source_target_pairs={{0,1},{1,0},{2,3},{3,2},{4,5},{5,4},{6,7},{7,6},{8,9},{9,8},{10,11... | collective-permute-start | bytes 393224 | tf_op jit(solution)/shard_map/ppermute | solution.py:482
  20.7 12.7 %collective-permute-start.11 = (bf16[10,80,128]{2,1,0:T(8,128)(2,1)S(1)}, bf16[10,80,128]{2,1,0:T(8,128)(2,1)S(1)}, u32[]{:S(2)}, u32[]{:S(2)}) collective-permute-start(bf16[10,80,128]{2,1,0:T(8,128)(2,1)S(1)} %get-tuple-element.80), channel_id=1, source_target_pairs={{0,8},{4,12},{8,0},{12,4},{1,9},{5,13},{9,1},{13,5},{2,10},{6,14},... | collective-permute-start | bytes 614408 | tf_op jit(solution)/shard_map/ppermute | solution.py:487
  20.7 12.9 %collective-permute-start.12 = (bf16[10,80,128]{2,1,0:T(8,128)(2,1)S(1)}, bf16[10,80,128]{2,1,0:T(8,128)(2,1)S(1)}, u32[]{:S(2)}, u32[]{:S(2)}) collective-permute-start(bf16[10,80,128]{2,1,0:T(8,128)(2,1)S(1)} %get-tuple-element.81), channel_id=1, source_target_pairs={{0,4},{4,0},{8,12},{12,8},{1,5},{5,1},{9,13},{13,9},{2,6},{6,2},{1... | collective-permute-start | bytes 614408 | tf_op jit(solution)/shard_map/ppermute | solution.py:487
  33.6 9.9 %collective-permute-start.13 = (bf16[2,2,9,16,256]{4,3,2,1,0:T(8,128)(2,1)S(1)}, bf16[2,2,9,16,256]{4,3,2,1,0:T(8,128)(2,1)S(1)}, u32[]{:S(2)}, u32[]{:S(2)}) collective-permute-start(bf16[2,2,9,16,256]{4,3,2,1,0:T(8,128)(2,1)S(1)} %get-tuple-element.85), channel_id=1, source_target_pairs={{0,2},{2,0},{1,3},{3,1},{4,6},{6,4},{5,7},{7,5},{8,10},{10,8},{9,1... | collective-permute-start | bytes 884744 | tf_op jit(solution)/shard_map/ppermute | solution.py:482
  35.1 8.5 %collective-permute-start.14 = (bf16[10,80,128]{2,1,0:T(8,128)(2,1)S(1)}, bf16[10,80,128]{2,1,0:T(8,128)(2,1)S(1)}, u32[]{:S(2)}, u32[]{:S(2)}) collective-permute-start(bf16[10,80,128]{2,1,0:T(8,128)(2,1)S(1)} %get-tuple-element.88), channel_id=1, source_target_pairs={{0,12},{4,8},{8,4},{12,0},{1,13},{5,9},{9,5},{13,1},{2,14},{6,10},... | collective-permute-start | bytes 614408 | tf_op jit(solution)/shard_map/ppermute | solution.py:487
  36.6 15.9 %collective-permute-start.10 = (bf16[2,2,9,16,256]{4,3,2,1,0:T(8,128)(2,1)S(1)}, bf16[2,2,9,16,256]{4,3,2,1,0:T(8,128)(2,1)S(1)}, u32[]{:S(2)}, u32[]{:S(2)}) collective-permute-start(bf16[2,2,9,16,256]{4,3,2,1,0:T(8,128)(2,1)S(1)} %get-tuple-element.77), channel_id=1, source_target_pairs={{0,2},{2,0},{1,3},{3,1},{4,6},{6,4},{5,7},{7,5},{8,10},{10,8},{9,1... | collective-permute-start | bytes 884744 | tf_op jit(solution)/shard_map/ppermute | solution.py:482
  37.1 7.1 %collective-permute-start.15 = (bf16[10,80,128]{2,1,0:T(8,128)(2,1)S(1)}, bf16[10,80,128]{2,1,0:T(8,128)(2,1)S(1)}, u32[]{:S(2)}, u32[]{:S(2)}) collective-permute-start(bf16[10,80,128]{2,1,0:T(8,128)(2,1)S(1)} %get-tuple-element.78.refs_0_), channel_id=1, source_target_pairs={{0,1},{1,0},{2,3},{3,2},{4,5},{5,4},{6,7},{7,6},{8,9},{9,8},{10,11... | collective-permute-start | bytes 614408 | tf_op jit(solution)/shard_map/ppermute | solution.py:482
  37.1 8.5 %collective-permute-start.16 = (bf16[10,80,128]{2,1,0:T(8,128)(2,1)S(1)}, bf16[10,80,128]{2,1,0:T(8,128)(2,1)S(1)}, u32[]{:S(2)}, u32[]{:S(2)}) collective-permute-start(bf16[10,80,128]{2,1,0:T(8,128)(2,1)S(1)} %collective-permute-done.12.refs_1_), channel_id=1, source_target_pairs={{0,1},{1,0},{2,3},{3,2},{4,5},{5,4},{6,7},{7,6},{8,9},{9,8},{10,11... | collective-permute-start | bytes 614408 | tf_op jit(solution)/shard_map/ppermute | solution.py:482
  44.1 10.1 %collective-permute-start.19 = (bf16[2,9,16,256]{3,2,1,0:T(8,128)(2,1)S(1)}, bf16[2,9,16,256]{3,2,1,0:T(8,128)(2,1)S(1)}, u32[]{:S(2)}, u32[]{:S(2)}) collective-permute-start(bf16[2,9,16,256]{3,2,1,0:T(8,128)(2,1)S(1)} %get-tuple-element.95), channel_id=1, source_target_pairs={{0,12},{4,8},{8,4},{12,0},{1,13},{5,9},{9,5},{13,1},{2,14},{6,10},... | collective-permute-start | bytes 442376 | tf_op jit(solution)/shard_map/ppermute | solution.py:487
  45.6 15.1 %collective-permute-start.20 = (bf16[2,9,16,256]{3,2,1,0:T(8,128)(2,1)S(1)}, bf16[2,9,16,256]{3,2,1,0:T(8,128)(2,1)S(1)}, u32[]{:S(2)}, u32[]{:S(2)}) collective-permute-start(bf16[2,9,16,256]{3,2,1,0:T(8,128)(2,1)S(1)} %get-tuple-element.96), channel_id=1, source_target_pairs={{0,8},{4,12},{8,0},{12,4},{1,9},{5,13},{9,1},{13,5},{2,10},{6,14},... | collective-permute-start | bytes 442376 | tf_op jit(solution)/shard_map/ppermute | solution.py:487
  52.5 8.9 %collective-permute-start.21 = (bf16[2,9,16,256]{3,2,1,0:T(8,128)(2,1)S(1)}, bf16[2,9,16,256]{3,2,1,0:T(8,128)(2,1)S(1)}, u32[]{:S(2)}, u32[]{:S(2)}) collective-permute-start(bf16[2,9,16,256]{3,2,1,0:T(8,128)(2,1)S(1)} %get-tuple-element.97), channel_id=1, source_target_pairs={{0,4},{4,0},{8,12},{12,8},{1,5},{5,1},{9,13},{13,9},{2,6},{6,2},{1... | collective-permute-start | bytes 442376 | tf_op jit(solution)/shard_map/ppermute | solution.py:487
  61.5 7.9 %collective-permute-start.24 = (bf16[336,256]{1,0:T(8,128)(2,1)S(1)}, bf16[336,256]{1,0:T(8,128)(2,1)S(1)}, u32[]{:S(2)}, u32[]{:S(2)}) collective-permute-start(bf16[336,256]{1,0:T(8,128)(2,1)S(1)} %get-tuple-element.102), channel_id=1, source_target_pairs={{0,4},{4,0},{8,12},{12,8},{1,5},{5,1},{9,13},{13,9},{2,6},{6,2},{1... | collective-permute-start | bytes 516104 | tf_op jit(solution)/shard_map/ppermute | solution.py:487
  61.6 16.5 %collective-permute-start.22 = (bf16[336,256]{1,0:T(8,128)(2,1)S(1)}, bf16[336,256]{1,0:T(8,128)(2,1)S(1)}, u32[]{:S(2)}, u32[]{:S(2)}) collective-permute-start(bf16[336,256]{1,0:T(8,128)(2,1)S(1)} %get-tuple-element.100), channel_id=1, source_target_pairs={{0,12},{4,8},{8,4},{12,0},{1,13},{5,9},{9,5},{13,1},{2,14},{6,10},... | collective-permute-start | bytes 516104 | tf_op jit(solution)/shard_map/ppermute | solution.py:487
  64.2 6.4 %collective-permute-start.25 = (bf16[288,256]{1,0:T(8,128)(2,1)S(1)}, bf16[288,256]{1,0:T(8,128)(2,1)S(1)}, u32[]{:S(2)}, u32[]{:S(2)}) collective-permute-start(bf16[288,256]{1,0:T(8,128)(2,1)S(1)} %get-tuple-element.101.refs_0_), channel_id=1, source_target_pairs={{0,2},{2,0},{1,3},{3,1},{4,6},{6,4},{5,7},{7,5},{8,10},{10,8},{9,1... | collective-permute-start | bytes 442376 | tf_op jit(solution)/shard_map/ppermute | solution.py:482
  64.7 13.4 %collective-permute-start.23 = (bf16[288,256]{1,0:T(8,128)(2,1)S(1)}, bf16[288,256]{1,0:T(8,128)(2,1)S(1)}, u32[]{:S(2)}, u32[]{:S(2)}) collective-permute-start(bf16[288,256]{1,0:T(8,128)(2,1)S(1)} %get-tuple-element.101.refs_0_), channel_id=1, source_target_pairs={{0,8},{4,12},{8,0},{12,4},{1,9},{5,13},{9,1},{13,5},{2,10},{6,14},... | collective-permute-start | bytes 442376 | tf_op jit(solution)/shard_map/ppermute | solution.py:487
  69.5 8.7 %collective-permute-start.26 = (bf16[288,256]{1,0:T(8,128)(2,1)S(1)}, bf16[288,256]{1,0:T(8,128)(2,1)S(1)}, u32[]{:S(2)}, u32[]{:S(2)}) collective-permute-start(bf16[288,256]{1,0:T(8,128)(2,1)S(1)} %slice.4), channel_id=1, source_target_pairs={{0,2},{2,0},{1,3},{3,1},{4,6},{6,4},{5,7},{7,5},{8,10},{10,8},{9,1... | collective-permute-start | bytes 442376 | tf_op jit(solution)/shard_map/ppermute | solution.py:482
  78.2 7.6 %collective-permute-start.27 = (bf16[352,256]{1,0:T(8,128)(2,1)S(1)}, bf16[352,256]{1,0:T(8,128)(2,1)S(1)}, u32[]{:S(2)}, u32[]{:S(2)}) collective-permute-start(bf16[352,256]{1,0:T(8,128)(2,1)S(1)} %column_message.1), channel_id=1, source_target_pairs={{0,2},{2,0},{1,3},{3,1},{4,6},{6,4},{5,7},{7,5},{8,10},{10,8},{9,1... | collective-permute-start | bytes 540680 | tf_op jit(solution)/shard_map/ppermute | solution.py:482
  79.1 6.7 %collective-permute-start.28 = (bf16[288,256]{1,0:T(8,128)(2,1)S(1)}, bf16[288,256]{1,0:T(8,128)(2,1)S(1)}, u32[]{:S(2)}, u32[]{:S(2)}) collective-permute-start(bf16[288,256]{1,0:T(8,128)(2,1)S(1)} %collective-permute-done.23.refs_2_), channel_id=1, source_target_pairs={{0,2},{2,0},{1,3},{3,1},{4,6},{6,4},{5,7},{7,5},{8,10},{10,8},{9,1... | collective-permute-start | bytes 442376 | tf_op jit(solution)/shard_map/ppermute | solution.py:482
  (13 other events, 64.8 us)

commit v12 on v11

--- a/solution.py
+++ b/solution.py
@@ -227,6 +227,16 @@
         outs[0][grad, tap] = value
 
 
+def weight_gradient(window, grads, scale, outs, grad):
+    turned = grads.T
+    for tap in range(0, 9, 2):
+        taps = range(tap, min(tap + 2, 9))
+        windows = [window(k) for k in taps]
+        value = dot(turned, jnp.concatenate(windows, axis=1)).T * scale
+        for k in taps:
+            emit(value[(k - tap) * HALF : (k - tap + 1) * HALF], outs, grad, k)
+
+
 def spread(values, weight, total, places):
     height, extent = values.shape[:2]
     inputs = values[...].reshape(height * extent, FULL)
@@ -260,15 +270,12 @@
             [ordered(own[o][u], other[o][u], 1) for o in range(owners)], axis=0
         )
         cot[u] = dot(pick, got).astype(BF16)
-    grads = cot[...].reshape(BLOCK * rows, FULL)
-    for dy in range(3):
-        windows = [
-            masked[dy : dy + BLOCK, dx * PER_WORKER : (dx + BLOCK) * PER_WORKER] for dx in range(3)
-        ]
-        window = jnp.concatenate([w.reshape(BLOCK * rows, HALF) for w in windows], axis=1)
-        value = dot_tn(jnp.maximum(window, jnp.zeros_like(window)), grads) * scale
-        for dx in range(3):
-            emit(value[dx * HALF : (dx + 1) * HALF], outs, 0, 3 * dy + dx)
+    def window(tap):
+        dy, dx = tap // 3, tap % 3
+        part = masked[dy : dy + BLOCK, dx * PER_WORKER : (dx + BLOCK) * PER_WORKER]
+        return jnp.maximum(part, jnp.zeros_like(part)).reshape(BLOCK * rows, HALF)
+
+    weight_gradient(window, cot[...].reshape(BLOCK * rows, FULL), scale, outs, 0)
     return slots
 
 
@@ -284,13 +291,12 @@
         value = jnp.where(live, total[m], 0.0)
         pre[m] = value.astype(BF16).reshape(MIDDLE, PER_WORKER, FULL)
     size = MIDDLE * MIDDLE * PER_WORKER
-    grads = pre[...].reshape(size, FULL)
-    for dy in range(3):
-        windows = [saved[dy : dy + MIDDLE, dx : dx + MIDDLE] for dx in range(3)]
-        window = jnp.concatenate([w.reshape(size, HALF) for w in windows], axis=1)
-        value = dot_tn(window, grads) * scale
-        for dx in range(3):
-            emit(value[dx * HALF : (dx + 1) * HALF], outs, 1, 3 * dy + dx)
+
+    def window(tap):
+        dy, dx = tap // 3, tap % 3
+        return saved[dy : dy + MIDDLE, dx : dx + MIDDLE].reshape(size, HALF)
+
+    weight_gradient(window, pre[...].reshape(size, FULL), scale, outs, 1)
 
 
 def owner_spread(tile, tile_other, second, second_other, out, total, cot, full):
@@ -430,10 +436,9 @@
         out[PART:, j * HALF : (j + 1) * HALF] = strip[...].astype(BF16)
 
 
-def close(tile, canvas, got_1, got_3, across, out, total):
+def gather_image(tile, canvas, got_1, got_3, total):
     rows = TILE_ROWS * BLOCK * 32
-    inner = canvas[2 : HIGH - 2, :32, :].reshape(rows, HALF)
-    total[...] = tile[...].reshape(rows, HALF).astype(F32) + inner
+    total[...] = tile[...].astype(F32) + canvas[2 : HIGH - 2, :32, :].reshape(rows, HALF)
     for step, got in ((1, got_1), (3, got_3)):
         rim = got[PART : PART + 32].astype(F32)
         above, below = adjacent(step)
@@ -442,12 +447,6 @@
         total[32:64] += top[:, HALF:]
         total[rows - 64 : rows - 32] += bottom[:, :HALF]
         total[rows - 32 : rows] += bottom[:, HALF:]
-    strip = across[PART:].astype(F32)
-    at = jnp.where(lax.axis_index("col") == 0, 30, 0)
-    for j in range(2):
-        spot = (pl.ds(at + j, 64, stride=32), slice(None))
-        total[spot] = total[spot] + strip[:, j * HALF : (j + 1) * HALF]
-    out[...] = total[...].astype(BF16).reshape(out.shape)
 
 
 def rows_at(number):
@@ -456,14 +455,16 @@
     return pl.ds(pl.multiple_of(place * ROWS, ROWS), ROWS)
 
 
-def lay(*refs):
-    for number, part in enumerate(refs[:-2]):
+def lay(tile, canvas, *refs):
+    parts, total, outs = refs[:-3], refs[-3], refs[-2:]
+    gather_image(tile, canvas, parts[1], parts[3], total)
+    for number, part in enumerate(parts):
         value = part[:PART].astype(F32).reshape(2, 9, ROWS, FULL)
-        for out, grad in zip(refs[-2:], (0, 1)):
+        for out, grad in zip(outs, (0, 1)):
             out[:, rows_at(number), :] = value[grad]
 
 
-def finish(tile, canvas, got_1, got_3, last, late, old_0, old_1, out, out_0, out_1, total, laid, sems):
+def finish(early, last, late, old_0, old_1, out, out_0, out_1, total, laid, sems):
     copies = []
     for k, (number, part) in enumerate(((6, late), (7, last))):
         laid[k] = part[:PART].astype(F32).reshape(2, 9, ROWS, FULL)
@@ -473,7 +474,13 @@
             )
             copy.start()
             copies.append(copy)
-    close(tile, canvas, got_1, got_3, last, out, total)
+    total[...] = early[...]
+    strip = last[PART:].astype(F32)
+    at = jnp.where(lax.axis_index("col") == 0, 30, 0)
+    for j in range(2):
+        spot = (pl.ds(at + j, 64, stride=32), slice(None))
+        total[spot] = total[spot] + strip[:, j * HALF : (j + 1) * HALF]
+    out[...] = total[...].astype(BF16)
     for copy in copies:
         copy.wait()
 
@@ -526,7 +533,7 @@
     saved_slots = saved_pre[0, 0].transpose(1, 2, 0, 3)
     saved_slots = saved_slots.reshape(MIDDLE, MIDDLE * PER_WORKER, HALF)
     outgoing, saved_here = tie((outgoing, saved_slots))
-    saved_other = swap(saved_slots)
+    saved_other = swap(saved_here)
     incoming = exchange(outgoing)
 
     masked, *to_owners, total = call(
@@ -579,8 +586,8 @@
         kept, near, far = terms
         far, at_owner[2], at_owner[1] = tie((far, at_owner[2], at_owner[1]))
 
-    def owner(at_owner):
-        at_owner_other = [swap(value) for value in at_owner]
+    def owner(at_owner, at_owner_other):
+        at_owner_other += [swap(value) for value in at_owner[len(at_owner_other) :]]
         return call(
             functools.partial(owner_canvas, owners, capacity, wide, permuted),
             [shape((HIGH, WIDE, HALF), F32)] + [shape((RIM, FULL), BF16)] * (2 if permuted else 0),
@@ -594,13 +601,15 @@
         )(routing, *at_owner, *at_owner_other, total, first_weight)
 
     if permuted:
-        far_got, near_got = swap(far, "col"), swap(near, "col")
+        others = [swap(value) for value in at_owner[:3]]
+        near, others, far_got = tie((near, others, swap(far, "col")))
+        near_got = swap(near, "col")
         sends = call(add_far, [shape(part, BF16)] * 2, [VMEM] * 2, [], (1, 1), "add_far")(
             kept, far_got
         )
         sends, at_owner[3] = tie((sends[::-1], at_owner[3]))
         got = [flip(sends[0], "blk", 3), flip(sends[1], "blk", 2)]
-        canvas, *rims = owner(at_owner)
+        canvas, *rims = owner(at_owner, others)
         near_got, canvas = tie((near_got, canvas))
         keep, send = call(
             add_near, [shape(part, F32), shape(part, BF16)], [VMEM] * 2, [], (1, 1), "add_near",
@@ -612,7 +621,8 @@
             add_workers, [message, wider, wider], [VMEM] * 6, [], (1, 1), "add_workers",
         )(keep, *got, *rims)
         got_2, got_3, got_1 = flip(own, "blk", 2), flip(wides[1], "blk", 3), flip(wides[0], "blk", 1)
-        across = [swap(value, "col") for value in (own, got_1[:PART])]
+        across = [swap(own, "col")]
+        across.append(flip(across[0], "blk", 1))
         got_3, got_2, got_1, across = tie((got_3, got_2, got_1, across))
         got = [got_1, got_2, got_3]
         last = call(
@@ -621,28 +631,31 @@
             (1, 1), "column_message",
         )(canvas.reshape(HIGH * WIDE, HALF), got[0], got[2])
         across += [swap(got_2, "col"), swap(last, "col")]
+        flat = (TILE_ROWS * BLOCK * 32, HALF)
         early = call(
-            lay, [shape((9, HALF, FULL), F32)] * 2, [VMEM] * 6, [], (1, 1), "lay",
-        )(own, *got, *across[:2])
+            lay, [shape(flat, F32)] + [shape((9, HALF, FULL), F32)] * 2, [VMEM] * 8, [], (1, 1),
+            "lay",
+        )(grad_out.reshape(flat), canvas, own, *got, *across[:2])
         grad_in, grad_second, grad_first = pl.pallas_call(
             finish,
-            out_shape=[shape(grad_out.shape, BF16)] + [shape((9, HALF, FULL), F32)] * 2,
-            in_specs=[VMEM] * 6 + [HBM] * 2,
+            out_shape=[shape(flat, BF16)] + [shape((9, HALF, FULL), F32)] * 2,
+            in_specs=[VMEM] * 3 + [HBM] * 2,
             out_specs=[VMEM] + [HBM] * 2,
             scratch_shapes=[
-                pltpu.VMEM((TILE_ROWS * BLOCK * 32, HALF), F32),
+                pltpu.VMEM(flat, F32),
                 pltpu.VMEM((2, 2, 9, ROWS, FULL), F32),
                 pltpu.SemaphoreType.DMA((2, 2)),
             ],
-            input_output_aliases={6: 1, 7: 2},
+            input_output_aliases={3: 1, 4: 2},
             compiler_params=pltpu.CompilerParams(vmem_limit_bytes=48 * 1024 * 1024),
             cost_estimate=pl.CostEstimate(flops=1, bytes_accessed=1, transcendentals=0),
             name="finish",
-        )(grad_out, canvas, got[0], got[2], across[3], across[2], *early)
+        )(early[0], across[3], across[2], *early[1:])
+        grad_in = grad_in.reshape(grad_out.shape)
         return (grad_in, grad_first, grad_second)
 
     grad_first, grad_second = lax.psum((terms[0][1], terms[0][0]), ("blk", "col"))
-    [canvas] = owner(at_owner)
+    [canvas] = owner(at_owner, [])
     up, down = neighbours("blk")
     from_above = lax.ppermute(canvas[HIGH - 2 :].astype(BF16), "blk", up).astype(F32)
     from_below = lax.ppermute(canvas[:2].astype(BF16), "blk", down).astype(F32)

time: 88 us -> 91.9 us (1.044)
  waiting for transfers between devices: 34.4 us -> 38 us
    ppermute x12 -> x13, waiting for transfers between devices: 23.2 us -> 25.7 us  [flip(): return lax.ppermute(value, axis, [(i, i ^ step) for i in range(size)])]
    ppermute x17 -> x16, waiting for transfers between devices: 11.2 us -> 12.4 us  [swap(): return lax.ppermute(value, axis, [(0, 1), (1, 0)])]
    ppermute x17 -> x16, starting transfers between devices: 8.48 us -> 7.86 us  [swap(): return lax.ppermute(value, axis, [(0, 1), (1, 0)])]
    ppermute x12 -> x13, starting transfers between devices: 18.3 us -> 18.7 us  [flip(): return lax.ppermute(value, axis, [(i, i ^ step) for i in range(size)])]
    unnamed x16 -> x14, local copies, waits for them, and re-layouts: 3.81 us -> 3.8 us
  transfers between devices with their start and end apart: 29 -> 29, of which waited for: 12 -> 15; matrix products, arithmetic and copies ran while one was open for 0% -> 0% of each run, Pallas kernels for 23% -> 22%
where the time goes in v12:
time: 91.9 us; the launch traced here: 91.5 us
  waiting for transfers between devices  38 us (41%)
  starting transfers between devices  26.5 us (29%)
  Pallas kernels  22.3 us (24%)
  local copies, waits for them, and re-layouts  3.8 us (4%)
    ppermute x13, waiting for transfers between devices, flip(): return lax.ppermute(value, axis, [(i, i ^ step) for i in range(size)])  25.7 us
    ppermute x13, starting transfers between devices, flip(): return lax.ppermute(value, axis, [(i, i ^ step) for i in range(size)])  18.7 us
    ppermute x16, waiting for transfers between devices, swap(): return lax.ppermute(value, axis, [(0, 1), (1, 0)])  12.4 us
    ppermute x16, starting transfers between devices, swap(): return lax.ppermute(value, axis, [(0, 1), (1, 0)])  7.86 us
    pallas_call x1, Pallas kernels, shards(): call(functools.partial(worker, scale, owners, columns, capacity, permuted...  6.93 us
    pallas_call x1, Pallas kernels, owner(): call(functools.partial(owner_canvas, owners, capacity, wide, permuted), [...  5.54 us
    pallas_call x1, Pallas kernels, shards(): call(functools.partial(prepare, owners, columns, capacity, wide, permuted...  4.31 us
    unnamed x14, local copies, waits for them, and re-layouts  3.8 us
  transfers between devices with their start and end apart: 29, of which 15 were waited for; matrix products, arithmetic and copies ran while one was open for 0% of the time, Pallas kernels for 22%

profile of v12, /device:TPU:0, one launch (start us, length us, event | category | flops | bytes accessed | tf_op | source)
XLA Modules:
  0.0 91.5 jit_solution(13935488002197304058)
XLA Ops:
  1.9 1.9 %pack_cotangents.1 = (bf16[8,64,128]{2,1,0:T(8,128)(2,1)S(1)}, bf16[8,64,128]{2,1,0:T(8,128)(2,1)S(1)}, bf16[8,64,128]{2,1,0:T(8,128)(2,1)S(1)}, bf16[8,64,128]{2,1,0:T(8,128)(2,1)S(1)}) custom-call(s32[4,16]{1,0:T(4,128)S(1)} %bitcast.20, bf16[8,8,32,128]{3,2,1,0:T(8,128)(2,1)} %bitcast.15), custom_call_target="tpu_custom_call" | custom-call | flops 1 | bytes 1 | tf_op jit(solution)/shard_map/pack_cotangents/pallas_call | solution.py:527
  4.3 4.7 %collective-permute-start = (bf16[8,64,128]{2,1,0:T(8,128)(2,1)S(1)}, bf16[8,64,128]{2,1,0:T(8,128)(2,1)S(1)}, u32[]{:S(2)}, u32[]{:S(2)}) collective-permute-start(bf16[8,64,128]{2,1,0:T(8,128)(2,1)S(1)} %get-tuple-element.68), channel_id=1, source_target_pairs={{0,12},{4,8},{8,4},{12,0},{1,13},{5,9},{9,5},{13,1},{2,14},{6,10},... | collective-permute-start | bytes 393224 | tf_op jit(solution)/shard_map/ppermute | solution.py:494
  12.8 4.3 %prepare.1 = (bf16[10,160,128]{2,1,0:T(8,128)(2,1)S(1)}, bf16[10,80,128]{2,1,0:T(8,128)(2,1)S(1)}, bf16[10,80,128]{2,1,0:T(8,128)(2,1)S(1)}, bf16[10,80,128]{2,1...) custom-call(s32[4,16]{1,0:T(4,128)S(1)} %bitcast.21, ...), custom_call_target="tpu_custom_call" | custom-call | flops 1 | bytes 1 | tf_op jit(solution)/shard_map/prepare/pallas_call | solution.py:539
  17.1 3.6 %collective-permute-done.1.refs_2_ = bf16[8,64,128]{2,1,0:T(8,128)(2,1)S(1)} collective-permute-done((bf16[8,64,128]{2,1,0:T(8,128)(2,1)S(1)}, bf16[8,64,128]{2,1,0:T(8,128)(2,1)S(1)}, u32[]{:S(2)}, u32[]{:S(2)}) %collective-permute-start.1) | collective-permute-done | bytes 131104 | tf_op jit(solution)/shard_map/ppermute | solution.py:494
  20.7 3.0 %collective-permute-start.12 = (bf16[10,80,128]{2,1,0:T(8,128)(2,1)S(1)}, bf16[10,80,128]{2,1,0:T(8,128)(2,1)S(1)}, u32[]{:S(2)}, u32[]{:S(2)}) collective-permute-start(bf16[10,80,128]{2,1,0:T(8,128)(2,1)S(1)} %get-tuple-element.87), channel_id=1, source_target_pairs={{0,4},{4,0},{8,12},{12,8},{1,5},{5,1},{9,13},{13,9},{2,6},{6,2},{1... | collective-permute-start | bytes 614408 | tf_op jit(solution)/shard_map/ppermute | solution.py:494
  25.6 6.9 %worker.1 = (f32[4,2,9,16,256]{4,3,2,1,0:T(8,128)S(1)}, bf16[2,2,9,16,256]{4,3,2,1,0:T(8,128)(2,1)S(1)}, bf16[2,2,9,16,256]{4,3,2,1,0:T(8,128)(2,1)S(1)}) custom-call(s32[4,16]{1,0:T(4,128)S(1)} %bitcast.22, bf16[8,64,128]{2,1,0:T(8,128)(2,1)S(1)} %get-tuple-element.78.refs_0_, bf16[8,64,128]{2,1,0:T(8,128)(2,1)S(1)} %collective-permute-done.2.refs_1_, ...), custom_call_target="tpu_custom_call" | custom-call | flops 1 | bytes 1 | tf_op jit(solution)/shard_map/worker/pallas_call | solution.py:565
  33.6 1.5 %collective-permute-start.15 = (bf16[2,2,9,16,256]{4,3,2,1,0:T(8,128)(2,1)S(1)}, bf16[2,2,9,16,256]{4,3,2,1,0:T(8,128)(2,1)S(1)}, u32[]{:S(2)}, u32[]{:S(2)}) collective-permute-start(bf16[2,2,9,16,256]{4,3,2,1,0:T(8,128)(2,1)S(1)} %get-tuple-element.90), channel_id=1, source_target_pairs={{0,2},{2,0},{1,3},{3,1},{4,6},{6,4},{5,7},{7,5},{8,10},{10,8},{9,1... | collective-permute-start | bytes 884744 | tf_op jit(solution)/shard_map/ppermute | solution.py:489
  35.6 1.5 %collective-permute-start.17 = (bf16[10,80,128]{2,1,0:T(8,128)(2,1)S(1)}, bf16[10,80,128]{2,1,0:T(8,128)(2,1)S(1)}, u32[]{:S(2)}, u32[]{:S(2)}) collective-permute-start(bf16[10,80,128]{2,1,0:T(8,128)(2,1)S(1)} %get-tuple-element.96), channel_id=1, source_target_pairs={{0,12},{4,8},{8,4},{12,0},{1,13},{5,9},{9,5},{13,1},{2,14},{6,10},... | collective-permute-start | bytes 614408 | tf_op jit(solution)/shard_map/ppermute | solution.py:494
  37.1 5.2 %collective-permute-done.15.got = bf16[2,2,9,16,256]{4,3,2,1,0:T(8,128)(2,1)S(1)} collective-permute-done((bf16[2,2,9,16,256]{4,3,2,1,0:T(8,128)(2,1)S(1)}, bf16[2,2,9,16,256]{4,3,2,1,0:T(8,128)(2,1)S(1)}, u32[]{:S(2)}, u32[]{:S(2)}) %collective-permute-start.15) | collective-permute-done | bytes 294944 | tf_op jit(solution)/shard_map/ppermute | solution.py:489
  42.3 1.5 %collective-permute-start.16 = (bf16[2,2,9,16,256]{4,3,2,1,0:T(8,128)(2,1)S(1)}, bf16[2,2,9,16,256]{4,3,2,1,0:T(8,128)(2,1)S(1)}, u32[]{:S(2)}, u32[]{:S(2)}) collective-permute-start(bf16[2,2,9,16,256]{4,3,2,1,0:T(8,128)(2,1)S(1)} %get-tuple-element.91), channel_id=1, source_target_pairs={{0,2},{2,0},{1,3},{3,1},{4,6},{6,4},{5,7},{7,5},{8,10},{10,8},{9,1... | collective-permute-start | bytes 884744 | tf_op jit(solution)/shard_map/ppermute | solution.py:489
  43.9 1.1 %collective-permute-done.17.refs_3_ = bf16[10,80,128]{2,1,0:T(8,128)(2,1)S(1)} collective-permute-done((bf16[10,80,128]{2,1,0:T(8,128)(2,1)S(1)}, bf16[10,80,128]{2,1,0:T(8,128)(2,1)S(1)}, u32[]{:S(2)}, u32[]{:S(2)}) %collective-permute-start.17) | collective-permute-done | bytes 204832 | tf_op jit(solution)/shard_map/ppermute | solution.py:494
  45.0 1.5 %collective-permute-start.19 = (bf16[2,9,16,256]{3,2,1,0:T(8,128)(2,1)S(1)}, bf16[2,9,16,256]{3,2,1,0:T(8,128)(2,1)S(1)}, u32[]{:S(2)}, u32[]{:S(2)}) collective-permute-start(bf16[2,9,16,256]{3,2,1,0:T(8,128)(2,1)S(1)} %get-tuple-element.106), channel_id=1, source_target_pairs={{0,12},{4,8},{8,4},{12,0},{1,13},{5,9},{9,5},{13,1},{2,14},{6,10},... | collective-permute-start | bytes 442376 | tf_op jit(solution)/shard_map/ppermute | solution.py:494
  46.5 1.8 %collective-permute-start.20 = (bf16[2,9,16,256]{3,2,1,0:T(8,128)(2,1)S(1)}, bf16[2,9,16,256]{3,2,1,0:T(8,128)(2,1)S(1)}, u32[]{:S(2)}, u32[]{:S(2)}) collective-permute-start(bf16[2,9,16,256]{3,2,1,0:T(8,128)(2,1)S(1)} %get-tuple-element.107), channel_id=1, source_target_pairs={{0,8},{4,12},{8,0},{12,4},{1,9},{5,13},{9,1},{13,5},{2,10},{6,14},... | collective-permute-start | bytes 442376 | tf_op jit(solution)/shard_map/ppermute | solution.py:494
  48.3 5.5 %owner_canvas.1 = (f32[68,40,128]{2,1,0:T(8,128)S(1)}, bf16[48,256]{1,0:T(8,128)(2,1)S(1)}, bf16[48,256]{1,0:T(8,128)(2,1)S(1)}) custom-call(s32[4,16]{1,0:T(4,128)S(1)} %bitcast.23, bf16[10,80,128]{2,1,0:T(8,128)(2,1)S(1)} %get-tuple-element.84.refs_0_, bf16[10,80,128]{2,1,0:T(8,128)(2,1)S(1)} %collective-permute-done.12.refs_1_, ...), custom_call_target="tpu_custom_call" | custom-call | flops 1 | bytes 1 | tf_op jit(solution)/shard_map/owner_canvas/pallas_call | solution.py:591
  53.9 1.2 %collective-permute-start.21 = (bf16[2,9,16,256]{3,2,1,0:T(8,128)(2,1)S(1)}, bf16[2,9,16,256]{3,2,1,0:T(8,128)(2,1)S(1)}, u32[]{:S(2)}, u32[]{:S(2)}) collective-permute-start(bf16[2,9,16,256]{3,2,1,0:T(8,128)(2,1)S(1)} %get-tuple-element.108), channel_id=1, source_target_pairs={{0,4},{4,0},{8,12},{12,8},{1,5},{5,1},{9,13},{13,9},{2,6},{6,2},{1... | collective-permute-start | bytes 442376 | tf_op jit(solution)/shard_map/ppermute | solution.py:494
  55.1 7.0 %collective-permute-done.20.got_2 = bf16[2,9,16,256]{3,2,1,0:T(8,128)(2,1)S(1)} collective-permute-done((bf16[2,9,16,256]{3,2,1,0:T(8,128)(2,1)S(1)}, bf16[2,9,16,256]{3,2,1,0:T(8,128)(2,1)S(1)}, u32[]{:S(2)}, u32[]{:S(2)}) %collective-permute-start.20) | collective-permute-done | bytes 147488 | tf_op jit(solution)/shard_map/ppermute | solution.py:494
  63.5 2.5 %collective-permute-start.22 = (bf16[336,256]{1,0:T(8,128)(2,1)S(1)}, bf16[336,256]{1,0:T(8,128)(2,1)S(1)}, u32[]{:S(2)}, u32[]{:S(2)}) collective-permute-start(bf16[336,256]{1,0:T(8,128)(2,1)S(1)} %get-tuple-element.112), channel_id=1, source_target_pairs={{0,12},{4,8},{8,4},{12,0},{1,13},{5,9},{9,5},{13,1},{2,14},{6,10},... | collective-permute-start | bytes 516104 | tf_op jit(solution)/shard_map/ppermute | solution.py:494
  66.0 1.9 %collective-permute-start.23 = (bf16[288,256]{1,0:T(8,128)(2,1)S(1)}, bf16[288,256]{1,0:T(8,128)(2,1)S(1)}, u32[]{:S(2)}, u32[]{:S(2)}) collective-permute-start(bf16[288,256]{1,0:T(8,128)(2,1)S(1)} %get-tuple-element.111.refs_0_), channel_id=1, source_target_pairs={{0,8},{4,12},{8,0},{12,4},{1,9},{5,13},{9,1},{13,5},{2,10},{6,14},... | collective-permute-start | bytes 442376 | tf_op jit(solution)/shard_map/ppermute | solution.py:494
  68.1 8.9 %collective-permute-done.23.refs_2_ = bf16[288,256]{1,0:T(8,128)(2,1)S(1)} collective-permute-done((bf16[288,256]{1,0:T(8,128)(2,1)S(1)}, bf16[288,256]{1,0:T(8,128)(2,1)S(1)}, u32[]{:S(2)}, u32[]{:S(2)}) %collective-permute-start.23) | collective-permute-done | bytes 147488 | tf_op jit(solution)/shard_map/ppermute | solution.py:494
  77.6 2.7 %collective-permute-done.26.refs_5_ = bf16[288,256]{1,0:T(8,128)(2,1)S(1)} collective-permute-done((bf16[288,256]{1,0:T(8,128)(2,1)S(1)}, bf16[288,256]{1,0:T(8,128)(2,1)S(1)}, u32[]{:S(2)}, u32[]{:S(2)}) %collective-permute-start.26) | collective-permute-done | bytes 147488 | tf_op jit(solution)/shard_map/ppermute | solution.py:494
  80.4 1.5 %collective-permute-start.27 = (bf16[352,256]{1,0:T(8,128)(2,1)S(1)}, bf16[352,256]{1,0:T(8,128)(2,1)S(1)}, u32[]{:S(2)}, u32[]{:S(2)}) collective-permute-start(bf16[352,256]{1,0:T(8,128)(2,1)S(1)} %column_message.1), channel_id=1, source_target_pairs={{0,2},{2,0},{1,3},{3,1},{4,6},{6,4},{5,7},{7,5},{8,10},{10,8},{9,1... | collective-permute-start | bytes 540680 | tf_op jit(solution)/shard_map/ppermute | solution.py:489
  82.5 1.6 %lay.1 = (f32[2048,128]{1,0:T(8,128)S(1)}, f32[9,128,256]{2,1,0:T(8,128)}, f32[9,128,256]{2,1,0:T(8,128)}) custom-call(bf16[2048,128]{1,0:T(8,128)(2,1)S(1)} %bitcast.17, f32[68,40,128]{2,1,0:T(8,128)S(1)} %get-tuple-element.103.canvas, bf16[288,256]{1,0:T(8,128)(2,1)S(1)} %get-tuple-element.111.refs_0_, ...), custom_call_target="tpu_custom_call" | custom-call | flops 1 | bytes 1 | tf_op jit(solution)/shard_map/lay/pallas_call | solution.py:635
  84.1 5.6 %collective-permute-done.28.late = bf16[288,256]{1,0:T(8,128)(2,1)S(1)} collective-permute-done((bf16[288,256]{1,0:T(8,128)(2,1)S(1)}, bf16[288,256]{1,0:T(8,128)(2,1)S(1)}, u32[]{:S(2)}, u32[]{:S(2)}) %collective-permute-start.28) | collective-permute-done | bytes 147488 | tf_op jit(solution)/shard_map/ppermute | solution.py:489
  89.7 1.7 %finish.1 = (bf16[2048,128]{1,0:T(8,128)(2,1)}, f32[9,128,256]{2,1,0:T(8,128)}, f32[9,128,256]{2,1,0:T(8,128)}) custom-call(f32[2048,128]{1,0:T(8,128)S(1)} %get-tuple-element.119.early, bf16[352,256]{1,0:T(8,128)(2,1)S(1)} %collective-permute-done.27.last, ...), custom_call_target="tpu_custom_call", output_to_operand_aliasing={{1}: (3, {}), {2}: (4, {})} | custom-call | flops 1 | bytes 1 | tf_op jit(solution)/shard_map/finish/pallas_call | solution.py:639
  (58 shorter events, 12.0 us)
Async XLA Ops:
  0.6 8.4 %collective-permute-start.3 = (bf16[8,8,32,128]{3,2,1,0:T(8,128)(2,1)}, bf16[8,8,32,128]{3,2,1,0:T(8,128)(2,1)S(1)}, u32[]{:S(2)}, u32[]{:S(2)}) collective-permute-start(bf16[8,8,32,128]{3,2,1,0:T(8,128)(2,1)} %bitcast.14), channel_id=1, source_target_pairs={{0,1},{1,0},{2,3},{3,2},{4,5},{5,4},{6,7},{7,6},{8,9},{9,8},{10,11... | collective-permute-start | bytes 1572872 | tf_op jit(solution)/shard_map/ppermute | solution.py:489
  1.1 8.5 %collective-permute-start.4 = (bf16[9,128,256]{2,1,0:T(8,128)(2,1)}, bf16[9,128,256]{2,1,0:T(8,128)(2,1)S(1)}, u32[]{:S(2)}, u32[]{:S(2)}) collective-permute-start(bf16[9,128,256]{2,1,0:T(8,128)(2,1)} %refs_10_.1), channel_id=1, source_target_pairs={{0,1},{1,0},{2,3},{3,2},{4,5},{5,4},{6,7},{7,6},{8,9},{9,8},{10,11... | collective-permute-start | bytes 1769480 | tf_op jit(solution)/shard_map/ppermute | solution.py:489
  3.8 19.9 %collective-permute-start.9 = (bf16[10,160,128]{2,1,0:T(8,128)(2,1)}, bf16[10,160,128]{2,1,0:T(8,128)(2,1)S(1)}, u32[]{:S(2)}, u32[]{:S(2)}) collective-permute-start(bf16[10,160,128]{2,1,0:T(8,128)(2,1)} %bitcast.18), channel_id=1, source_target_pairs={{0,1},{1,0},{2,3},{3,2},{4,5},{5,4},{6,7},{7,6},{8,9},{9,8},{10,11... | collective-permute-start | bytes 1228808 | tf_op jit(solution)/shard_map/ppermute | solution.py:489
  4.3 12.8 %collective-permute-start = (bf16[8,64,128]{2,1,0:T(8,128)(2,1)S(1)}, bf16[8,64,128]{2,1,0:T(8,128)(2,1)S(1)}, u32[]{:S(2)}, u32[]{:S(2)}) collective-permute-start(bf16[8,64,128]{2,1,0:T(8,128)(2,1)S(1)} %get-tuple-element.68), channel_id=1, source_target_pairs={{0,12},{4,8},{8,4},{12,0},{1,13},{5,9},{9,5},{13,1},{2,14},{6,10},... | collective-permute-start | bytes 393224 | tf_op jit(solution)/shard_map/ppermute | solution.py:494
  9.0 11.7 %collective-permute-start.1 = (bf16[8,64,128]{2,1,0:T(8,128)(2,1)S(1)}, bf16[8,64,128]{2,1,0:T(8,128)(2,1)S(1)}, u32[]{:S(2)}, u32[]{:S(2)}) collective-permute-start(bf16[8,64,128]{2,1,0:T(8,128)(2,1)S(1)} %get-tuple-element.69), channel_id=1, source_target_pairs={{0,8},{4,12},{8,0},{12,4},{1,9},{5,13},{9,1},{13,5},{2,10},{6,14},... | collective-permute-start | bytes 393224 | tf_op jit(solution)/shard_map/ppermute | solution.py:494
  9.0 11.7 %collective-permute-start.2 = (bf16[8,64,128]{2,1,0:T(8,128)(2,1)S(1)}, bf16[8,64,128]{2,1,0:T(8,128)(2,1)S(1)}, u32[]{:S(2)}, u32[]{:S(2)}) collective-permute-start(bf16[8,64,128]{2,1,0:T(8,128)(2,1)S(1)} %get-tuple-element.70), channel_id=1, source_target_pairs={{0,4},{4,0},{8,12},{12,8},{1,5},{5,1},{9,13},{13,9},{2,6},{6,2},{1... | collective-permute-start | bytes 393224 | tf_op jit(solution)/shard_map/ppermute | solution.py:494
  20.7 3.6 %collective-permute-start.5 = (bf16[8,64,128]{2,1,0:T(8,128)(2,1)S(1)}, bf16[8,64,128]{2,1,0:T(8,128)(2,1)S(1)}, u32[]{:S(2)}, u32[]{:S(2)}) collective-permute-start(bf16[8,64,128]{2,1,0:T(8,128)(2,1)S(1)} %get-tuple-element.78.refs_0_), channel_id=1, source_target_pairs={{0,1},{1,0},{2,3},{3,2},{4,5},{5,4},{6,7},{7,6},{8,9},{9,8},{10,11... | collective-permute-start | bytes 393224 | tf_op jit(solution)/shard_map/ppermute | solution.py:489
  20.7 12.7 %collective-permute-start.11 = (bf16[10,80,128]{2,1,0:T(8,128)(2,1)S(1)}, bf16[10,80,128]{2,1,0:T(8,128)(2,1)S(1)}, u32[]{:S(2)}, u32[]{:S(2)}) collective-permute-start(bf16[10,80,128]{2,1,0:T(8,128)(2,1)S(1)} %get-tuple-element.86), channel_id=1, source_target_pairs={{0,8},{4,12},{8,0},{12,4},{1,9},{5,13},{9,1},{13,5},{2,10},{6,14},... | collective-permute-start | bytes 614408 | tf_op jit(solution)/shard_map/ppermute | solution.py:494
  20.7 12.9 %collective-permute-start.12 = (bf16[10,80,128]{2,1,0:T(8,128)(2,1)S(1)}, bf16[10,80,128]{2,1,0:T(8,128)(2,1)S(1)}, u32[]{:S(2)}, u32[]{:S(2)}) collective-permute-start(bf16[10,80,128]{2,1,0:T(8,128)(2,1)S(1)} %get-tuple-element.87), channel_id=1, source_target_pairs={{0,4},{4,0},{8,12},{12,8},{1,5},{5,1},{9,13},{13,9},{2,6},{6,2},{1... | collective-permute-start | bytes 614408 | tf_op jit(solution)/shard_map/ppermute | solution.py:494
  33.6 8.8 %collective-permute-start.15 = (bf16[2,2,9,16,256]{4,3,2,1,0:T(8,128)(2,1)S(1)}, bf16[2,2,9,16,256]{4,3,2,1,0:T(8,128)(2,1)S(1)}, u32[]{:S(2)}, u32[]{:S(2)}) collective-permute-start(bf16[2,2,9,16,256]{4,3,2,1,0:T(8,128)(2,1)S(1)} %get-tuple-element.90), channel_id=1, source_target_pairs={{0,2},{2,0},{1,3},{3,1},{4,6},{6,4},{5,7},{7,5},{8,10},{10,8},{9,1... | collective-permute-start | bytes 884744 | tf_op jit(solution)/shard_map/ppermute | solution.py:489
  35.1 2.0 %collective-permute-start.10 = (bf16[10,80,128]{2,1,0:T(8,128)(2,1)S(1)}, bf16[10,80,128]{2,1,0:T(8,128)(2,1)S(1)}, u32[]{:S(2)}, u32[]{:S(2)}) collective-permute-start(bf16[10,80,128]{2,1,0:T(8,128)(2,1)S(1)} %get-tuple-element.84.refs_0_), channel_id=1, source_target_pairs={{0,1},{1,0},{2,3},{3,2},{4,5},{5,4},{6,7},{7,6},{8,9},{9,8},{10,11... | collective-permute-start | bytes 614408 | tf_op jit(solution)/shard_map/ppermute | solution.py:489
  35.6 9.4 %collective-permute-start.17 = (bf16[10,80,128]{2,1,0:T(8,128)(2,1)S(1)}, bf16[10,80,128]{2,1,0:T(8,128)(2,1)S(1)}, u32[]{:S(2)}, u32[]{:S(2)}) collective-permute-start(bf16[10,80,128]{2,1,0:T(8,128)(2,1)S(1)} %get-tuple-element.96), channel_id=1, source_target_pairs={{0,12},{4,8},{8,4},{12,0},{1,13},{5,9},{9,5},{13,1},{2,14},{6,10},... | collective-permute-start | bytes 614408 | tf_op jit(solution)/shard_map/ppermute | solution.py:494
  42.3 11.5 %collective-permute-start.16 = (bf16[2,2,9,16,256]{4,3,2,1,0:T(8,128)(2,1)S(1)}, bf16[2,2,9,16,256]{4,3,2,1,0:T(8,128)(2,1)S(1)}, u32[]{:S(2)}, u32[]{:S(2)}) collective-permute-start(bf16[2,2,9,16,256]{4,3,2,1,0:T(8,128)(2,1)S(1)} %get-tuple-element.91), channel_id=1, source_target_pairs={{0,2},{2,0},{1,3},{3,1},{4,6},{6,4},{5,7},{7,5},{8,10},{10,8},{9,1... | collective-permute-start | bytes 884744 | tf_op jit(solution)/shard_map/ppermute | solution.py:489
  45.0 3.3 %collective-permute-start.18 = (bf16[10,80,128]{2,1,0:T(8,128)(2,1)S(1)}, bf16[10,80,128]{2,1,0:T(8,128)(2,1)S(1)}, u32[]{:S(2)}, u32[]{:S(2)}) collective-permute-start(bf16[10,80,128]{2,1,0:T(8,128)(2,1)S(1)} %collective-permute-done.17.refs_3_), channel_id=1, source_target_pairs={{0,1},{1,0},{2,3},{3,2},{4,5},{5,4},{6,7},{7,6},{8,9},{9,8},{10,11... | collective-permute-start | bytes 614408 | tf_op jit(solution)/shard_map/ppermute | solution.py:489
  45.0 10.1 %collective-permute-start.19 = (bf16[2,9,16,256]{3,2,1,0:T(8,128)(2,1)S(1)}, bf16[2,9,16,256]{3,2,1,0:T(8,128)(2,1)S(1)}, u32[]{:S(2)}, u32[]{:S(2)}) collective-permute-start(bf16[2,9,16,256]{3,2,1,0:T(8,128)(2,1)S(1)} %get-tuple-element.106), channel_id=1, source_target_pairs={{0,12},{4,8},{8,4},{12,0},{1,13},{5,9},{9,5},{13,1},{2,14},{6,10},... | collective-permute-start | bytes 442376 | tf_op jit(solution)/shard_map/ppermute | solution.py:494
  46.5 15.6 %collective-permute-start.20 = (bf16[2,9,16,256]{3,2,1,0:T(8,128)(2,1)S(1)}, bf16[2,9,16,256]{3,2,1,0:T(8,128)(2,1)S(1)}, u32[]{:S(2)}, u32[]{:S(2)}) collective-permute-start(bf16[2,9,16,256]{3,2,1,0:T(8,128)(2,1)S(1)} %get-tuple-element.107), channel_id=1, source_target_pairs={{0,8},{4,12},{8,0},{12,4},{1,9},{5,13},{9,1},{13,5},{2,10},{6,14},... | collective-permute-start | bytes 442376 | tf_op jit(solution)/shard_map/ppermute | solution.py:494
  53.9 8.9 %collective-permute-start.21 = (bf16[2,9,16,256]{3,2,1,0:T(8,128)(2,1)S(1)}, bf16[2,9,16,256]{3,2,1,0:T(8,128)(2,1)S(1)}, u32[]{:S(2)}, u32[]{:S(2)}) collective-permute-start(bf16[2,9,16,256]{3,2,1,0:T(8,128)(2,1)S(1)} %get-tuple-element.108), channel_id=1, source_target_pairs={{0,4},{4,0},{8,12},{12,8},{1,5},{5,1},{9,13},{13,9},{2,6},{6,2},{1... | collective-permute-start | bytes 442376 | tf_op jit(solution)/shard_map/ppermute | solution.py:494
  62.9 5.2 %collective-permute-start.25 = (bf16[288,256]{1,0:T(8,128)(2,1)S(1)}, bf16[288,256]{1,0:T(8,128)(2,1)S(1)}, u32[]{:S(2)}, u32[]{:S(2)}) collective-permute-start(bf16[288,256]{1,0:T(8,128)(2,1)S(1)} %get-tuple-element.111.refs_0_), channel_id=1, source_target_pairs={{0,2},{2,0},{1,3},{3,1},{4,6},{6,4},{5,7},{7,5},{8,10},{10,8},{9,1... | collective-permute-start | bytes 442376 | tf_op jit(solution)/shard_map/ppermute | solution.py:489
  63.5 13.6 %collective-permute-start.22 = (bf16[336,256]{1,0:T(8,128)(2,1)S(1)}, bf16[336,256]{1,0:T(8,128)(2,1)S(1)}, u32[]{:S(2)}, u32[]{:S(2)}) collective-permute-start(bf16[336,256]{1,0:T(8,128)(2,1)S(1)} %get-tuple-element.112), channel_id=1, source_target_pairs={{0,12},{4,8},{8,4},{12,0},{1,13},{5,9},{9,5},{13,1},{2,14},{6,10},... | collective-permute-start | bytes 516104 | tf_op jit(solution)/shard_map/ppermute | solution.py:494
  66.0 11.7 %collective-permute-start.24 = (bf16[336,256]{1,0:T(8,128)(2,1)S(1)}, bf16[336,256]{1,0:T(8,128)(2,1)S(1)}, u32[]{:S(2)}, u32[]{:S(2)}) collective-permute-start(bf16[336,256]{1,0:T(8,128)(2,1)S(1)} %get-tuple-element.113), channel_id=1, source_target_pairs={{0,4},{4,0},{8,12},{12,8},{1,5},{5,1},{9,13},{13,9},{2,6},{6,2},{1... | collective-permute-start | bytes 516104 | tf_op jit(solution)/shard_map/ppermute | solution.py:494
  66.0 11.1 %collective-permute-start.23 = (bf16[288,256]{1,0:T(8,128)(2,1)S(1)}, bf16[288,256]{1,0:T(8,128)(2,1)S(1)}, u32[]{:S(2)}, u32[]{:S(2)}) collective-permute-start(bf16[288,256]{1,0:T(8,128)(2,1)S(1)} %get-tuple-element.111.refs_0_), channel_id=1, source_target_pairs={{0,8},{4,12},{8,0},{12,4},{1,9},{5,13},{9,1},{13,5},{2,10},{6,14},... | collective-permute-start | bytes 442376 | tf_op jit(solution)/shard_map/ppermute | solution.py:494
  68.1 12.2 %collective-permute-start.26 = (bf16[288,256]{1,0:T(8,128)(2,1)S(1)}, bf16[288,256]{1,0:T(8,128)(2,1)S(1)}, u32[]{:S(2)}, u32[]{:S(2)}) collective-permute-start(bf16[288,256]{1,0:T(8,128)(2,1)S(1)} %collective-permute-done.25.refs_4_), channel_id=1, source_target_pairs={{0,4},{4,0},{8,12},{12,8},{1,5},{5,1},{9,13},{13,9},{2,6},{6,2},{1... | collective-permute-start | bytes 442376 | tf_op jit(solution)/shard_map/ppermute | solution.py:494
  80.4 9.3 %collective-permute-start.27 = (bf16[352,256]{1,0:T(8,128)(2,1)S(1)}, bf16[352,256]{1,0:T(8,128)(2,1)S(1)}, u32[]{:S(2)}, u32[]{:S(2)}) collective-permute-start(bf16[352,256]{1,0:T(8,128)(2,1)S(1)} %column_message.1), channel_id=1, source_target_pairs={{0,2},{2,0},{1,3},{3,1},{4,6},{6,4},{5,7},{7,5},{8,10},{10,8},{9,1... | collective-permute-start | bytes 540680 | tf_op jit(solution)/shard_map/ppermute | solution.py:489
  81.9 7.8 %collective-permute-start.28 = (bf16[288,256]{1,0:T(8,128)(2,1)S(1)}, bf16[288,256]{1,0:T(8,128)(2,1)S(1)}, u32[]{:S(2)}, u32[]{:S(2)}) collective-permute-start(bf16[288,256]{1,0:T(8,128)(2,1)S(1)} %collective-permute-done.23.refs_2_), channel_id=1, source_target_pairs={{0,2},{2,0},{1,3},{3,1},{4,6},{6,4},{5,7},{7,5},{8,10},{10,8},{9,1... | collective-permute-start | bytes 442376 | tf_op jit(solution)/shard_map/ppermute | solution.py:489
  (12 other events, 59.7 us)

commit v13 on v11

--- a/solution.py
+++ b/solution.py
@@ -113,10 +113,13 @@
     return step ^ lax.axis_index(axis) if permuted else step
 
 
-def pack_cotangents(owners, capacity, permuted, routing, source, *refs):
-    outs, (table, tile, arrived) = refs[:-3], refs[-3:]
-    fetch = pltpu.make_async_copy(source, tile, arrived)
+def pack_cotangents(owners, capacity, permuted, listed, source, *refs):
+    outs, (table, tile, routing, arrived) = refs[:-4], refs[-4:]
+    fetch = pltpu.make_async_copy(source, tile, arrived.at[0])
     fetch.start()
+    lists = pltpu.make_async_copy(listed, routing, arrived.at[1])
+    lists.start()
+    lists.wait()
     owner_table(routing, table, owners, capacity)
     rows = BLOCK * capacity
     row, lane = iota((rows, FULL), 0), iota((rows, FULL), 1)
@@ -230,16 +233,28 @@
 def spread(values, weight, total, places):
     height, extent = values.shape[:2]
     inputs = values[...].reshape(height * extent, FULL)
-    width = weight.shape[1]
-    group = FULL // width
-    total[...] = jnp.zeros_like(total)
-    for tap in range(0, 9, group):
-        taps = range(tap, min(tap + group, 9))
-        part = dot_nt(inputs, jnp.concatenate([weight[k] for k in taps], axis=0))
-        for k in taps:
-            spot = (slice(k // 3, k // 3 + height), pl.ds(k % 3 * places, extent))
-            here = part[:, (k - tap) * width : (k - tap + 1) * width]
-            total[spot] = total[spot] + here.reshape(height, extent, width)
+    width, step = weight.shape[1], places
+    for dy in range(3):
+        taps = jnp.concatenate([weight[3 * dy + dx] for dx in range(3)], axis=0)
+        part = dot_nt(inputs, taps).reshape(height, extent, 3 * width)
+        p, q, r = [part[:, :, dx * width : (dx + 1) * width] for dx in range(3)]
+        sums = [
+            p[:, :step],
+            p[:, step : 2 * step] + q[:, :step],
+            p[:, 2 * step :] + q[:, step : extent - step] + r[:, : extent - 2 * step],
+            q[:, extent - step :] + r[:, extent - 2 * step : extent - step],
+            r[:, extent - step :],
+        ]
+        at = 0
+        for value in sums:
+            size = value.shape[1]
+            here = slice(at, at + size)
+            if dy == 0:
+                total[:height, here] = value
+            else:
+                total[dy : dy + height - 1, here] += value[:-1]
+                total[dy + height - 1, here] = value[height - 1]
+            at += size
 
 
 def second_gradient(scale, owners, capacity, permuted, routing, *refs):
@@ -520,9 +535,15 @@
     outgoing = call(
         functools.partial(pack_cotangents, owners, capacity, permuted),
         pieces(BLOCK, BLOCK * capacity, HALF),
-        [SMEM, HBM], tables + [pltpu.VMEM(tile.shape, BF16), pltpu.SemaphoreType.DMA],
+        [HBM, HBM],
+        tables
+        + [
+            pltpu.VMEM(tile.shape, BF16),
+            pltpu.SMEM(routing.shape, I32),
+            pltpu.SemaphoreType.DMA((2,)),
+        ],
         (1, 1), "pack_cotangents",
-    )(routing, pltpu.with_memory_space_constraint(tile, pltpu.HBM))
+    )(*[pltpu.with_memory_space_constraint(value, pltpu.HBM) for value in (routing, tile)])
     saved_slots = saved_pre[0, 0].transpose(1, 2, 0, 3)
     saved_slots = saved_slots.reshape(MIDDLE, MIDDLE * PER_WORKER, HALF)
     outgoing, saved_here = tie((outgoing, saved_slots))

time: 88 us -> 87.5 us (level)
  transfers between devices with their start and end apart: 29 -> 29, of which waited for: 12 -> 13; matrix products, arithmetic and copies ran while one was open for 0% -> 0% of each run, Pallas kernels for 23% -> 23%
where the time goes in v13:
time: 87.5 us; the launch traced here: 87.2 us
  waiting for transfers between devices  34.2 us (39%)
  starting transfers between devices  26.3 us (30%)
  Pallas kernels  22 us (25%)
  local copies, waits for them, and re-layouts  3.82 us (4%)
  between operations  0.94 us (1%)
    ppermute x12, waiting for transfers between devices, flip(): return lax.ppermute(value, axis, [(i, i ^ step) for i in range(size)])  22.4 us
    ppermute x12, starting transfers between devices, flip(): return lax.ppermute(value, axis, [(i, i ^ step) for i in range(size)])  18.3 us
    ppermute x17, waiting for transfers between devices, swap(): return lax.ppermute(value, axis, [(0, 1), (1, 0)])  11.8 us
    ppermute x17, starting transfers between devices, swap(): return lax.ppermute(value, axis, [(0, 1), (1, 0)])  7.96 us
    pallas_call x1, Pallas kernels, shards(): call(functools.partial(worker, scale, owners, columns, capacity, permuted...  6.51 us
    pallas_call x1, Pallas kernels, owner(): call(functools.partial(owner_canvas, owners, capacity, wide, permuted), [...  5.8 us
    pallas_call x1, Pallas kernels, shards(): call(functools.partial(prepare, owners, columns, capacity, wide, permuted...  4.31 us
    unnamed x16, local copies, waits for them, and re-layouts  3.81 us
  transfers between devices with their start and end apart: 29, of which 13 were waited for; matrix products, arithmetic and copies ran while one was open for 0% of the time, Pallas kernels for 23%

profile of v13, /device:TPU:0, one launch (start us, length us, event | category | flops | bytes accessed | tf_op | source)
XLA Modules:
  0.0 87.2 jit_solution(16323766286721335271)
XLA Ops:
  1.7 1.9 %pack_cotangents.1 = (bf16[8,64,128]{2,1,0:T(8,128)(2,1)S(1)}, bf16[8,64,128]{2,1,0:T(8,128)(2,1)S(1)}, bf16[8,64,128]{2,1,0:T(8,128)(2,1)S(1)}, bf16[8,64,128]{2,1,0:T(8,128)(2,1)S(1)}) custom-call(s32[4,16]{1,0:T(4,128)} %bitcast.17, bf16[8,8,32,128]{3,2,1,0:T(8,128)(2,1)} %bitcast.13), custom_call_target="tpu_custom_call" | custom-call | flops 1 | bytes 1 | tf_op jit(solution)/shard_map/pack_cotangents/pallas_call | solution.py:535
  3.6 4.7 %collective-permute-start = (bf16[8,64,128]{2,1,0:T(8,128)(2,1)S(1)}, bf16[8,64,128]{2,1,0:T(8,128)(2,1)S(1)}, u32[]{:S(2)}, u32[]{:S(2)}) collective-permute-start(bf16[8,64,128]{2,1,0:T(8,128)(2,1)S(1)} %get-tuple-element.62), channel_id=1, source_target_pairs={{0,12},{4,8},{8,4},{12,0},{1,13},{5,9},{9,5},{13,1},{2,14},{6,10},... | collective-permute-start | bytes 393224 | tf_op jit(solution)/shard_map/ppermute | solution.py:502
  10.0 1.1 %copy-done.2 = bf16[9,128,256]{2,1,0:T(8,128)(2,1)S(1)} copy-done((bf16[9,128,256]{2,1,0:T(8,128)(2,1)S(1)}, bf16[9,128,256]{2,1,0:T(8,128)(2,1)}, u32[]{:S(2)}) %copy-start.2) | copy-done | bytes 589848
  12.8 4.3 %prepare.1 = (bf16[10,160,128]{2,1,0:T(8,128)(2,1)S(1)}, bf16[10,80,128]{2,1,0:T(8,128)(2,1)S(1)}, bf16[10,80,128]{2,1,0:T(8,128)(2,1)S(1)}, bf16[10,80,128]{2,1...) custom-call(s32[4,16]{1,0:T(4,128)S(1)} %bitcast.18, ...), custom_call_target="tpu_custom_call" | custom-call | flops 1 | bytes 1 | tf_op jit(solution)/shard_map/prepare/pallas_call | solution.py:553
  17.1 2.9 %collective-permute-done.1.refs_2_ = bf16[8,64,128]{2,1,0:T(8,128)(2,1)S(1)} collective-permute-done((bf16[8,64,128]{2,1,0:T(8,128)(2,1)S(1)}, bf16[8,64,128]{2,1,0:T(8,128)(2,1)S(1)}, u32[]{:S(2)}, u32[]{:S(2)}) %collective-permute-start.1) | collective-permute-done | bytes 131104 | tf_op jit(solution)/shard_map/ppermute | solution.py:502
  20.1 3.0 %collective-permute-start.12 = (bf16[10,80,128]{2,1,0:T(8,128)(2,1)S(1)}, bf16[10,80,128]{2,1,0:T(8,128)(2,1)S(1)}, u32[]{:S(2)}, u32[]{:S(2)}) collective-permute-start(bf16[10,80,128]{2,1,0:T(8,128)(2,1)S(1)} %get-tuple-element.81), channel_id=1, source_target_pairs={{0,4},{4,0},{8,12},{12,8},{1,5},{5,1},{9,13},{13,9},{2,6},{6,2},{1... | collective-permute-start | bytes 614408 | tf_op jit(solution)/shard_map/ppermute | solution.py:502
  25.0 6.5 %worker.1 = (f32[4,2,9,16,256]{4,3,2,1,0:T(8,128)S(1)}, bf16[2,2,9,16,256]{4,3,2,1,0:T(8,128)(2,1)S(1)}, bf16[2,2,9,16,256]{4,3,2,1,0:T(8,128)(2,1)S(1)}) custom-call(s32[4,16]{1,0:T(4,128)S(1)} %bitcast.19, bf16[8,64,128]{2,1,0:T(8,128)(2,1)S(1)} %get-tuple-element.72.refs_0_, bf16[8,64,128]{2,1,0:T(8,128)(2,1)S(1)} %collective-permute-done.2.refs_1_, ...), custom_call_target="tpu_custom_call" | custom-call | flops 1 | bytes 1 | tf_op jit(solution)/shard_map/worker/pallas_call | solution.py:579
  31.5 1.3 %collective-permute-done.11.refs_2_ = bf16[10,80,128]{2,1,0:T(8,128)(2,1)S(1)} collective-permute-done((bf16[10,80,128]{2,1,0:T(8,128)(2,1)S(1)}, bf16[10,80,128]{2,1,0:T(8,128)(2,1)S(1)}, u32[]{:S(2)}, u32[]{:S(2)}) %collective-permute-start.11) | collective-permute-done | bytes 204832 | tf_op jit(solution)/shard_map/ppermute | solution.py:502
  32.9 1.5 %collective-permute-start.13 = (bf16[2,2,9,16,256]{4,3,2,1,0:T(8,128)(2,1)S(1)}, bf16[2,2,9,16,256]{4,3,2,1,0:T(8,128)(2,1)S(1)}, u32[]{:S(2)}, u32[]{:S(2)}) collective-permute-start(bf16[2,2,9,16,256]{4,3,2,1,0:T(8,128)(2,1)S(1)} %get-tuple-element.85), channel_id=1, source_target_pairs={{0,2},{2,0},{1,3},{3,1},{4,6},{6,4},{5,7},{7,5},{8,10},{10,8},{9,1... | collective-permute-start | bytes 884744 | tf_op jit(solution)/shard_map/ppermute | solution.py:497
  34.4 1.5 %collective-permute-start.14 = (bf16[10,80,128]{2,1,0:T(8,128)(2,1)S(1)}, bf16[10,80,128]{2,1,0:T(8,128)(2,1)S(1)}, u32[]{:S(2)}, u32[]{:S(2)}) collective-permute-start(bf16[10,80,128]{2,1,0:T(8,128)(2,1)S(1)} %get-tuple-element.88), channel_id=1, source_target_pairs={{0,12},{4,8},{8,4},{12,0},{1,13},{5,9},{9,5},{13,1},{2,14},{6,10},... | collective-permute-start | bytes 614408 | tf_op jit(solution)/shard_map/ppermute | solution.py:502
  36.9 5.9 %collective-permute-done.13.got = bf16[2,2,9,16,256]{4,3,2,1,0:T(8,128)(2,1)S(1)} collective-permute-done((bf16[2,2,9,16,256]{4,3,2,1,0:T(8,128)(2,1)S(1)}, bf16[2,2,9,16,256]{4,3,2,1,0:T(8,128)(2,1)S(1)}, u32[]{:S(2)}, u32[]{:S(2)}) %collective-permute-start.13) | collective-permute-done | bytes 294944 | tf_op jit(solution)/shard_map/ppermute | solution.py:497
  43.5 1.5 %collective-permute-start.19 = (bf16[2,9,16,256]{3,2,1,0:T(8,128)(2,1)S(1)}, bf16[2,9,16,256]{3,2,1,0:T(8,128)(2,1)S(1)}, u32[]{:S(2)}, u32[]{:S(2)}) collective-permute-start(bf16[2,9,16,256]{3,2,1,0:T(8,128)(2,1)S(1)} %get-tuple-element.95), channel_id=1, source_target_pairs={{0,12},{4,8},{8,4},{12,0},{1,13},{5,9},{9,5},{13,1},{2,14},{6,10},... | collective-permute-start | bytes 442376 | tf_op jit(solution)/shard_map/ppermute | solution.py:502
  45.0 1.3 %collective-permute-start.20 = (bf16[2,9,16,256]{3,2,1,0:T(8,128)(2,1)S(1)}, bf16[2,9,16,256]{3,2,1,0:T(8,128)(2,1)S(1)}, u32[]{:S(2)}, u32[]{:S(2)}) collective-permute-start(bf16[2,9,16,256]{3,2,1,0:T(8,128)(2,1)S(1)} %get-tuple-element.96), channel_id=1, source_target_pairs={{0,8},{4,12},{8,0},{12,4},{1,9},{5,13},{9,1},{13,5},{2,10},{6,14},... | collective-permute-start | bytes 442376 | tf_op jit(solution)/shard_map/ppermute | solution.py:502
  46.3 5.8 %owner_canvas.1 = (f32[68,40,128]{2,1,0:T(8,128)S(1)}, bf16[48,256]{1,0:T(8,128)(2,1)S(1)}, bf16[48,256]{1,0:T(8,128)(2,1)S(1)}) custom-call(s32[4,16]{1,0:T(4,128)S(1)} %bitcast.20, bf16[10,80,128]{2,1,0:T(8,128)(2,1)S(1)} %get-tuple-element.78.refs_0_, bf16[10,80,128]{2,1,0:T(8,128)(2,1)S(1)} %collective-permute-done.12.refs_1_, ...), custom_call_target="tpu_custom_call" | custom-call | flops 1 | bytes 1 | tf_op jit(solution)/shard_map/owner_canvas/pallas_call | solution.py:605
  52.2 1.7 %collective-permute-start.21 = (bf16[2,9,16,256]{3,2,1,0:T(8,128)(2,1)S(1)}, bf16[2,9,16,256]{3,2,1,0:T(8,128)(2,1)S(1)}, u32[]{:S(2)}, u32[]{:S(2)}) collective-permute-start(bf16[2,9,16,256]{3,2,1,0:T(8,128)(2,1)S(1)} %get-tuple-element.97), channel_id=1, source_target_pairs={{0,4},{4,0},{8,12},{12,8},{1,5},{5,1},{9,13},{13,9},{2,6},{6,2},{1... | collective-permute-start | bytes 442376 | tf_op jit(solution)/shard_map/ppermute | solution.py:502
  53.9 6.2 %collective-permute-done.20.got_2 = bf16[2,9,16,256]{3,2,1,0:T(8,128)(2,1)S(1)} collective-permute-done((bf16[2,9,16,256]{3,2,1,0:T(8,128)(2,1)S(1)}, bf16[2,9,16,256]{3,2,1,0:T(8,128)(2,1)S(1)}, u32[]{:S(2)}, u32[]{:S(2)}) %collective-permute-start.20) | collective-permute-done | bytes 147488 | tf_op jit(solution)/shard_map/ppermute | solution.py:502
  61.2 2.5 %collective-permute-start.22 = (bf16[336,256]{1,0:T(8,128)(2,1)S(1)}, bf16[336,256]{1,0:T(8,128)(2,1)S(1)}, u32[]{:S(2)}, u32[]{:S(2)}) collective-permute-start(bf16[336,256]{1,0:T(8,128)(2,1)S(1)} %get-tuple-element.100), channel_id=1, source_target_pairs={{0,12},{4,8},{8,4},{12,0},{1,13},{5,9},{9,5},{13,1},{2,14},{6,10},... | collective-permute-start | bytes 516104 | tf_op jit(solution)/shard_map/ppermute | solution.py:502
  64.3 1.4 %collective-permute-start.23 = (bf16[288,256]{1,0:T(8,128)(2,1)S(1)}, bf16[288,256]{1,0:T(8,128)(2,1)S(1)}, u32[]{:S(2)}, u32[]{:S(2)}) collective-permute-start(bf16[288,256]{1,0:T(8,128)(2,1)S(1)} %get-tuple-element.101.refs_0_), channel_id=1, source_target_pairs={{0,8},{4,12},{8,0},{12,4},{1,9},{5,13},{9,1},{13,5},{2,10},{6,14},... | collective-permute-start | bytes 442376 | tf_op jit(solution)/shard_map/ppermute | solution.py:502
  65.7 3.4 %collective-permute-done.24.got_1.refs_1_ = bf16[336,256]{1,0:T(8,128)(2,1)S(1)} collective-permute-done((bf16[336,256]{1,0:T(8,128)(2,1)S(1)}, bf16[336,256]{1,0:T(8,128)(2,1)S(1)}, u32[]{:S(2)}, u32[]{:S(2)}) %collective-permute-start.24) | collective-permute-done | bytes 172064 | tf_op jit(solution)/shard_map/ppermute | solution.py:502
  70.4 7.4 %collective-permute-done.23.refs_2_ = bf16[288,256]{1,0:T(8,128)(2,1)S(1)} collective-permute-done((bf16[288,256]{1,0:T(8,128)(2,1)S(1)}, bf16[288,256]{1,0:T(8,128)(2,1)S(1)}, u32[]{:S(2)}, u32[]{:S(2)}) %collective-permute-start.23) | collective-permute-done | bytes 147488 | tf_op jit(solution)/shard_map/ppermute | solution.py:502
  78.7 1.2 %collective-permute-start.28 = (bf16[288,256]{1,0:T(8,128)(2,1)S(1)}, bf16[288,256]{1,0:T(8,128)(2,1)S(1)}, u32[]{:S(2)}, u32[]{:S(2)}) collective-permute-start(bf16[288,256]{1,0:T(8,128)(2,1)S(1)} %collective-permute-done.23.refs_2_), channel_id=1, source_target_pairs={{0,2},{2,0},{1,3},{3,1},{4,6},{6,4},{5,7},{7,5},{8,10},{10,8},{9,1... | collective-permute-start | bytes 442376 | tf_op jit(solution)/shard_map/ppermute | solution.py:497
  80.0 1.5 %lay.1 = (f32[9,128,256]{2,1,0:T(8,128)}, f32[9,128,256]{2,1,0:T(8,128)}) custom-call(bf16[288,256]{1,0:T(8,128)(2,1)S(1)} %get-tuple-element.101.refs_0_, bf16[336,256]{1,0:T(8,128)(2,1)S(1)} %collective-permute-done.24.got_1.refs_1_, bf16[288,256]{1,0:T(8,128)(2,1)S(1)} %collective-permute-done.23.refs_2_, ...), custom_call_target="tpu_custom_call" | custom-call | flops 1 | bytes 1 | tf_op jit(solution)/shard_map/lay/pallas_call | solution.py:645
  81.5 4.0 %collective-permute-done.28.late = bf16[288,256]{1,0:T(8,128)(2,1)S(1)} collective-permute-done((bf16[288,256]{1,0:T(8,128)(2,1)S(1)}, bf16[288,256]{1,0:T(8,128)(2,1)S(1)}, u32[]{:S(2)}, u32[]{:S(2)}) %collective-permute-start.28) | collective-permute-done | bytes 147488 | tf_op jit(solution)/shard_map/ppermute | solution.py:497
  85.4 1.7 %finish.1 = (bf16[64,32,128]{2,1,0:T(8,128)(2,1)}, f32[9,128,256]{2,1,0:T(8,128)}, f32[9,128,256]{2,1,0:T(8,128)}) custom-call(bf16[64,32,128]{2,1,0:T(8,128)(2,1)S(1)} %copy-done.1, f32[68,40,128]{2,1,0:T(8,128)S(1)} %get-tuple-element.92.canvas, ...), custom_call_target="tpu_custom_call", output_to_operand_aliasing={{1}: (6, {}), {2}: (7, {})} | custom-call | flops 1 | bytes 1 | tf_op jit(solution)/shard_map/finish/pallas_call | solution.py:648
  (61 shorter events, 12.2 us)
Async XLA Ops:
  0.6 7.7 %collective-permute-start.3 = (bf16[8,8,32,128]{3,2,1,0:T(8,128)(2,1)}, bf16[8,8,32,128]{3,2,1,0:T(8,128)(2,1)S(1)}, u32[]{:S(2)}, u32[]{:S(2)}) collective-permute-start(bf16[8,8,32,128]{3,2,1,0:T(8,128)(2,1)} %bitcast.12), channel_id=1, source_target_pairs={{0,1},{1,0},{2,3},{3,2},{4,5},{5,4},{6,7},{7,6},{8,9},{9,8},{10,11... | collective-permute-start | bytes 1572872 | tf_op jit(solution)/shard_map/ppermute | solution.py:497
  1.1 7.9 %collective-permute-start.4 = (bf16[9,128,256]{2,1,0:T(8,128)(2,1)}, bf16[9,128,256]{2,1,0:T(8,128)(2,1)S(1)}, u32[]{:S(2)}, u32[]{:S(2)}) collective-permute-start(bf16[9,128,256]{2,1,0:T(8,128)(2,1)} %refs_10_.1), channel_id=1, source_target_pairs={{0,1},{1,0},{2,3},{3,2},{4,5},{5,4},{6,7},{7,6},{8,9},{9,8},{10,11... | collective-permute-start | bytes 1769480 | tf_op jit(solution)/shard_map/ppermute | solution.py:497
  1.2 21.9 %collective-permute-start.9 = (bf16[10,160,128]{2,1,0:T(8,128)(2,1)}, bf16[10,160,128]{2,1,0:T(8,128)(2,1)S(1)}, u32[]{:S(2)}, u32[]{:S(2)}) collective-permute-start(bf16[10,160,128]{2,1,0:T(8,128)(2,1)} %bitcast.15), channel_id=1, source_target_pairs={{0,1},{1,0},{2,3},{3,2},{4,5},{5,4},{6,7},{7,6},{8,9},{9,8},{10,11... | collective-permute-start | bytes 1228808 | tf_op jit(solution)/shard_map/ppermute | solution.py:497
  3.6 13.5 %collective-permute-start = (bf16[8,64,128]{2,1,0:T(8,128)(2,1)S(1)}, bf16[8,64,128]{2,1,0:T(8,128)(2,1)S(1)}, u32[]{:S(2)}, u32[]{:S(2)}) collective-permute-start(bf16[8,64,128]{2,1,0:T(8,128)(2,1)S(1)} %get-tuple-element.62), channel_id=1, source_target_pairs={{0,12},{4,8},{8,4},{12,0},{1,13},{5,9},{9,5},{13,1},{2,14},{6,10},... | collective-permute-start | bytes 393224 | tf_op jit(solution)/shard_map/ppermute | solution.py:502
  8.4 11.7 %collective-permute-start.1 = (bf16[8,64,128]{2,1,0:T(8,128)(2,1)S(1)}, bf16[8,64,128]{2,1,0:T(8,128)(2,1)S(1)}, u32[]{:S(2)}, u32[]{:S(2)}) collective-permute-start(bf16[8,64,128]{2,1,0:T(8,128)(2,1)S(1)} %get-tuple-element.63), channel_id=1, source_target_pairs={{0,8},{4,12},{8,0},{12,4},{1,9},{5,13},{9,1},{13,5},{2,10},{6,14},... | collective-permute-start | bytes 393224 | tf_op jit(solution)/shard_map/ppermute | solution.py:502
  8.4 11.7 %collective-permute-start.2 = (bf16[8,64,128]{2,1,0:T(8,128)(2,1)S(1)}, bf16[8,64,128]{2,1,0:T(8,128)(2,1)S(1)}, u32[]{:S(2)}, u32[]{:S(2)}) collective-permute-start(bf16[8,64,128]{2,1,0:T(8,128)(2,1)S(1)} %get-tuple-element.64), channel_id=1, source_target_pairs={{0,4},{4,0},{8,12},{12,8},{1,5},{5,1},{9,13},{13,9},{2,6},{6,2},{1... | collective-permute-start | bytes 393224 | tf_op jit(solution)/shard_map/ppermute | solution.py:502
  20.0 3.6 %collective-permute-start.5 = (bf16[8,64,128]{2,1,0:T(8,128)(2,1)S(1)}, bf16[8,64,128]{2,1,0:T(8,128)(2,1)S(1)}, u32[]{:S(2)}, u32[]{:S(2)}) collective-permute-start(bf16[8,64,128]{2,1,0:T(8,128)(2,1)S(1)} %get-tuple-element.72.refs_0_), channel_id=1, source_target_pairs={{0,1},{1,0},{2,3},{3,2},{4,5},{5,4},{6,7},{7,6},{8,9},{9,8},{10,11... | collective-permute-start | bytes 393224 | tf_op jit(solution)/shard_map/ppermute | solution.py:497
  20.0 12.7 %collective-permute-start.11 = (bf16[10,80,128]{2,1,0:T(8,128)(2,1)S(1)}, bf16[10,80,128]{2,1,0:T(8,128)(2,1)S(1)}, u32[]{:S(2)}, u32[]{:S(2)}) collective-permute-start(bf16[10,80,128]{2,1,0:T(8,128)(2,1)S(1)} %get-tuple-element.80), channel_id=1, source_target_pairs={{0,8},{4,12},{8,0},{12,4},{1,9},{5,13},{9,1},{13,5},{2,10},{6,14},... | collective-permute-start | bytes 614408 | tf_op jit(solution)/shard_map/ppermute | solution.py:502
  20.1 12.9 %collective-permute-start.12 = (bf16[10,80,128]{2,1,0:T(8,128)(2,1)S(1)}, bf16[10,80,128]{2,1,0:T(8,128)(2,1)S(1)}, u32[]{:S(2)}, u32[]{:S(2)}) collective-permute-start(bf16[10,80,128]{2,1,0:T(8,128)(2,1)S(1)} %get-tuple-element.81), channel_id=1, source_target_pairs={{0,4},{4,0},{8,12},{12,8},{1,5},{5,1},{9,13},{13,9},{2,6},{6,2},{1... | collective-permute-start | bytes 614408 | tf_op jit(solution)/shard_map/ppermute | solution.py:502
  32.9 9.9 %collective-permute-start.13 = (bf16[2,2,9,16,256]{4,3,2,1,0:T(8,128)(2,1)S(1)}, bf16[2,2,9,16,256]{4,3,2,1,0:T(8,128)(2,1)S(1)}, u32[]{:S(2)}, u32[]{:S(2)}) collective-permute-start(bf16[2,2,9,16,256]{4,3,2,1,0:T(8,128)(2,1)S(1)} %get-tuple-element.85), channel_id=1, source_target_pairs={{0,2},{2,0},{1,3},{3,1},{4,6},{6,4},{5,7},{7,5},{8,10},{10,8},{9,1... | collective-permute-start | bytes 884744 | tf_op jit(solution)/shard_map/ppermute | solution.py:497
  34.4 8.5 %collective-permute-start.14 = (bf16[10,80,128]{2,1,0:T(8,128)(2,1)S(1)}, bf16[10,80,128]{2,1,0:T(8,128)(2,1)S(1)}, u32[]{:S(2)}, u32[]{:S(2)}) collective-permute-start(bf16[10,80,128]{2,1,0:T(8,128)(2,1)S(1)} %get-tuple-element.88), channel_id=1, source_target_pairs={{0,12},{4,8},{8,4},{12,0},{1,13},{5,9},{9,5},{13,1},{2,14},{6,10},... | collective-permute-start | bytes 614408 | tf_op jit(solution)/shard_map/ppermute | solution.py:502
  35.9 16.2 %collective-permute-start.10 = (bf16[2,2,9,16,256]{4,3,2,1,0:T(8,128)(2,1)S(1)}, bf16[2,2,9,16,256]{4,3,2,1,0:T(8,128)(2,1)S(1)}, u32[]{:S(2)}, u32[]{:S(2)}) collective-permute-start(bf16[2,2,9,16,256]{4,3,2,1,0:T(8,128)(2,1)S(1)} %get-tuple-element.77), channel_id=1, source_target_pairs={{0,2},{2,0},{1,3},{3,1},{4,6},{6,4},{5,7},{7,5},{8,10},{10,8},{9,1... | collective-permute-start | bytes 884744 | tf_op jit(solution)/shard_map/ppermute | solution.py:497
  36.4 7.1 %collective-permute-start.15 = (bf16[10,80,128]{2,1,0:T(8,128)(2,1)S(1)}, bf16[10,80,128]{2,1,0:T(8,128)(2,1)S(1)}, u32[]{:S(2)}, u32[]{:S(2)}) collective-permute-start(bf16[10,80,128]{2,1,0:T(8,128)(2,1)S(1)} %get-tuple-element.78.refs_0_), channel_id=1, source_target_pairs={{0,1},{1,0},{2,3},{3,2},{4,5},{5,4},{6,7},{7,6},{8,9},{9,8},{10,11... | collective-permute-start | bytes 614408 | tf_op jit(solution)/shard_map/ppermute | solution.py:497
  36.4 8.5 %collective-permute-start.16 = (bf16[10,80,128]{2,1,0:T(8,128)(2,1)S(1)}, bf16[10,80,128]{2,1,0:T(8,128)(2,1)S(1)}, u32[]{:S(2)}, u32[]{:S(2)}) collective-permute-start(bf16[10,80,128]{2,1,0:T(8,128)(2,1)S(1)} %collective-permute-done.12.refs_1_), channel_id=1, source_target_pairs={{0,1},{1,0},{2,3},{3,2},{4,5},{5,4},{6,7},{7,6},{8,9},{9,8},{10,11... | collective-permute-start | bytes 614408 | tf_op jit(solution)/shard_map/ppermute | solution.py:497
  43.5 10.4 %collective-permute-start.19 = (bf16[2,9,16,256]{3,2,1,0:T(8,128)(2,1)S(1)}, bf16[2,9,16,256]{3,2,1,0:T(8,128)(2,1)S(1)}, u32[]{:S(2)}, u32[]{:S(2)}) collective-permute-start(bf16[2,9,16,256]{3,2,1,0:T(8,128)(2,1)S(1)} %get-tuple-element.95), channel_id=1, source_target_pairs={{0,12},{4,8},{8,4},{12,0},{1,13},{5,9},{9,5},{13,1},{2,14},{6,10},... | collective-permute-start | bytes 442376 | tf_op jit(solution)/shard_map/ppermute | solution.py:502
  45.0 15.1 %collective-permute-start.20 = (bf16[2,9,16,256]{3,2,1,0:T(8,128)(2,1)S(1)}, bf16[2,9,16,256]{3,2,1,0:T(8,128)(2,1)S(1)}, u32[]{:S(2)}, u32[]{:S(2)}) collective-permute-start(bf16[2,9,16,256]{3,2,1,0:T(8,128)(2,1)S(1)} %get-tuple-element.96), channel_id=1, source_target_pairs={{0,8},{4,12},{8,0},{12,4},{1,9},{5,13},{9,1},{13,5},{2,10},{6,14},... | collective-permute-start | bytes 442376 | tf_op jit(solution)/shard_map/ppermute | solution.py:502
  52.2 8.9 %collective-permute-start.21 = (bf16[2,9,16,256]{3,2,1,0:T(8,128)(2,1)S(1)}, bf16[2,9,16,256]{3,2,1,0:T(8,128)(2,1)S(1)}, u32[]{:S(2)}, u32[]{:S(2)}) collective-permute-start(bf16[2,9,16,256]{3,2,1,0:T(8,128)(2,1)S(1)} %get-tuple-element.97), channel_id=1, source_target_pairs={{0,4},{4,0},{8,12},{12,8},{1,5},{5,1},{9,13},{13,9},{2,6},{6,2},{1... | collective-permute-start | bytes 442376 | tf_op jit(solution)/shard_map/ppermute | solution.py:502
  61.2 7.9 %collective-permute-start.24 = (bf16[336,256]{1,0:T(8,128)(2,1)S(1)}, bf16[336,256]{1,0:T(8,128)(2,1)S(1)}, u32[]{:S(2)}, u32[]{:S(2)}) collective-permute-start(bf16[336,256]{1,0:T(8,128)(2,1)S(1)} %get-tuple-element.102), channel_id=1, source_target_pairs={{0,4},{4,0},{8,12},{12,8},{1,5},{5,1},{9,13},{13,9},{2,6},{6,2},{1... | collective-permute-start | bytes 516104 | tf_op jit(solution)/shard_map/ppermute | solution.py:502
  61.2 16.6 %collective-permute-start.22 = (bf16[336,256]{1,0:T(8,128)(2,1)S(1)}, bf16[336,256]{1,0:T(8,128)(2,1)S(1)}, u32[]{:S(2)}, u32[]{:S(2)}) collective-permute-start(bf16[336,256]{1,0:T(8,128)(2,1)S(1)} %get-tuple-element.100), channel_id=1, source_target_pairs={{0,12},{4,8},{8,4},{12,0},{1,13},{5,9},{9,5},{13,1},{2,14},{6,10},... | collective-permute-start | bytes 516104 | tf_op jit(solution)/shard_map/ppermute | solution.py:502
  63.8 6.6 %collective-permute-start.25 = (bf16[288,256]{1,0:T(8,128)(2,1)S(1)}, bf16[288,256]{1,0:T(8,128)(2,1)S(1)}, u32[]{:S(2)}, u32[]{:S(2)}) collective-permute-start(bf16[288,256]{1,0:T(8,128)(2,1)S(1)} %get-tuple-element.101.refs_0_), channel_id=1, source_target_pairs={{0,2},{2,0},{1,3},{3,1},{4,6},{6,4},{5,7},{7,5},{8,10},{10,8},{9,1... | collective-permute-start | bytes 442376 | tf_op jit(solution)/shard_map/ppermute | solution.py:497
  64.3 13.5 %collective-permute-start.23 = (bf16[288,256]{1,0:T(8,128)(2,1)S(1)}, bf16[288,256]{1,0:T(8,128)(2,1)S(1)}, u32[]{:S(2)}, u32[]{:S(2)}) collective-permute-start(bf16[288,256]{1,0:T(8,128)(2,1)S(1)} %get-tuple-element.101.refs_0_), channel_id=1, source_target_pairs={{0,8},{4,12},{8,0},{12,4},{1,9},{5,13},{9,1},{13,5},{2,10},{6,14},... | collective-permute-start | bytes 442376 | tf_op jit(solution)/shard_map/ppermute | solution.py:502
  69.1 8.7 %collective-permute-start.26 = (bf16[288,256]{1,0:T(8,128)(2,1)S(1)}, bf16[288,256]{1,0:T(8,128)(2,1)S(1)}, u32[]{:S(2)}, u32[]{:S(2)}) collective-permute-start(bf16[288,256]{1,0:T(8,128)(2,1)S(1)} %slice.4), channel_id=1, source_target_pairs={{0,2},{2,0},{1,3},{3,1},{4,6},{6,4},{5,7},{7,5},{8,10},{10,8},{9,1... | collective-permute-start | bytes 442376 | tf_op jit(solution)/shard_map/ppermute | solution.py:497
  77.9 7.6 %collective-permute-start.27 = (bf16[352,256]{1,0:T(8,128)(2,1)S(1)}, bf16[352,256]{1,0:T(8,128)(2,1)S(1)}, u32[]{:S(2)}, u32[]{:S(2)}) collective-permute-start(bf16[352,256]{1,0:T(8,128)(2,1)S(1)} %column_message.1), channel_id=1, source_target_pairs={{0,2},{2,0},{1,3},{3,1},{4,6},{6,4},{5,7},{7,5},{8,10},{10,8},{9,1... | collective-permute-start | bytes 540680 | tf_op jit(solution)/shard_map/ppermute | solution.py:497
  78.7 6.7 %collective-permute-start.28 = (bf16[288,256]{1,0:T(8,128)(2,1)S(1)}, bf16[288,256]{1,0:T(8,128)(2,1)S(1)}, u32[]{:S(2)}, u32[]{:S(2)}) collective-permute-start(bf16[288,256]{1,0:T(8,128)(2,1)S(1)} %collective-permute-done.23.refs_2_), channel_id=1, source_target_pairs={{0,2},{2,0},{1,3},{3,1},{4,6},{6,4},{5,7},{7,5},{8,10},{10,8},{9,1... | collective-permute-start | bytes 442376 | tf_op jit(solution)/shard_map/ppermute | solution.py:497
  (13 other events, 64.1 us)

commit v14 on v13

--- a/solution.py
+++ b/solution.py
@@ -21,7 +21,8 @@
 HIGH = 68
 RIM = 48
 ROWS = 16
-PART = 288
+SOLE = 144
+PART = 2 * SOLE
 WIDE = 40
 
 BF16 = jnp.bfloat16
@@ -417,80 +418,85 @@
     send[...] = (kept[1] + got[1].astype(F32)).astype(BF16)
 
 
-def add_workers(kept, got_3, got_2, got_1, rim_1, rim_3, out, out_1, out_3):
+def add_workers(kept, got_3, got_2, got_1, rim_1, rim_3, out, out_1, out_second, out_3):
     value = kept[...]
     for part in (got_3, got_2, got_1):
         value = value + part[...].astype(F32)
     value = value.astype(BF16).reshape(PART, FULL)
     out[...] = value
-    for message, rim in ((out_1, rim_1), (out_3, rim_3)):
-        message[:PART] = value
-        message[PART:] = rim[...]
-
-
-def column_message(canvas, got_1, got_3, out, rim, strip):
-    out[:PART] = got_3[:PART]
+    out_second[...] = value[:SOLE]
+    out_1[:PART] = value
+    out_1[PART:] = rim_1[...]
+    out_3[:SOLE] = value[SOLE:]
+    out_3[SOLE:] = rim_3[...]
+
+
+def row_rim(message, step):
+    rim = message[message.shape[0] - RIM :].astype(F32)
+    above, below = adjacent(step)
+    return jnp.where(above, rim, 0.0), jnp.where(below, rim, 0.0)
+
+
+def column_message(canvas, got_1, got_3, out, rims, strip):
+    out[:SOLE] = got_3[:SOLE]
+    rims[0], rims[1] = row_rim(got_1, 1)
+    rims[2], rims[3] = row_rim(got_3, 3)
     for j in range(2):
         c = 32 + 2 * lax.axis_index("col") + j
         strip[...] = canvas[pl.ds(2 * WIDE + c, 64, stride=WIDE), :]
-        for step, got in ((1, got_1), (3, got_3)):
-            rim[...] = got[PART:].astype(F32)
-            row = rim[pl.ds(c, 1), :]
-            above, below = adjacent(step)
-            top, bottom = jnp.where(above, row, 0.0), jnp.where(below, row, 0.0)
-            strip[0:1] += top[:, :HALF]
-            strip[1:2] += top[:, HALF:]
-            strip[62:63] += bottom[:, :HALF]
-            strip[63:64] += bottom[:, HALF:]
-        out[PART:, j * HALF : (j + 1) * HALF] = strip[...].astype(BF16)
-
-
-def close(tile, canvas, got_1, got_3, across, out, total):
-    rows = TILE_ROWS * BLOCK * 32
-    inner = canvas[2 : HIGH - 2, :32, :].reshape(rows, HALF)
-    total[...] = tile[...].reshape(rows, HALF).astype(F32) + inner
+        for k in range(4):
+            row, at = rims[k, pl.ds(c, 1), :], 62 * (k % 2)
+            strip[at : at + 1] += row[:, :HALF]
+            strip[at + 1 : at + 2] += row[:, HALF:]
+        out[SOLE:, j * HALF : (j + 1) * HALF] = strip[...].astype(BF16)
+
+
+def sum_image(tile, canvas, total):
+    total[...] = tile[...].astype(F32) + canvas[2 : HIGH - 2, :32, :].reshape(total.shape)
+
+
+def add_row_rims(got_1, got_3, total):
+    rows = total.shape[0]
     for step, got in ((1, got_1), (3, got_3)):
-        rim = got[PART : PART + 32].astype(F32)
-        above, below = adjacent(step)
-        top, bottom = jnp.where(above, rim, 0.0), jnp.where(below, rim, 0.0)
+        top, bottom = [rim[:32] for rim in row_rim(got, step)]
         total[0:32] += top[:, :HALF]
         total[32:64] += top[:, HALF:]
         total[rows - 64 : rows - 32] += bottom[:, :HALF]
         total[rows - 32 : rows] += bottom[:, HALF:]
-    strip = across[PART:].astype(F32)
+
+
+def rows_at(number):
+    column = lax.axis_index("col")
+    place = (column if number < 4 else 1 - column) * 4 + partner("blk", number % 4, True)
+    return pl.ds(pl.multiple_of(place * ROWS, ROWS), ROWS)
+
+
+def lay(*refs):
+    parts, outs = refs[:-2], refs[-2:]
+    own, got_1, got_2, second_3, first_3, across, across_2, across_1, across_3 = parts
+    for number, part in (
+        (0, own), (1, got_1), (2, got_2), (4, across), (5, across_1), (6, across_2)
+    ):
+        value = part[:PART].astype(F32).reshape(2, 9, ROWS, FULL)
+        for out, grad in zip(outs, (0, 1)):
+            out[:, rows_at(number), :] = value[grad]
+    for number, grad, part in ((3, 0, second_3), (7, 0, across_3), (3, 1, first_3)):
+        outs[grad][:, rows_at(number), :] = part[:SOLE].astype(F32).reshape(9, ROWS, FULL)
+
+
+def finish(early, got_1, got_3, last, old, out, dest, total, laid, sem):
+    laid[...] = last[:SOLE].astype(F32).reshape(9, ROWS, FULL)
+    copy = pltpu.make_async_copy(laid, dest.at[:, rows_at(7), :], sem)
+    copy.start()
+    total[...] = early[...]
+    add_row_rims(got_1, got_3, total)
+    strip = last[SOLE:].astype(F32)
     at = jnp.where(lax.axis_index("col") == 0, 30, 0)
     for j in range(2):
         spot = (pl.ds(at + j, 64, stride=32), slice(None))
         total[spot] = total[spot] + strip[:, j * HALF : (j + 1) * HALF]
-    out[...] = total[...].astype(BF16).reshape(out.shape)
-
-
-def rows_at(number):
-    column = lax.axis_index("col")
-    place = (column if number < 4 else 1 - column) * 4 + partner("blk", number % 4, True)
-    return pl.ds(pl.multiple_of(place * ROWS, ROWS), ROWS)
-
-
-def lay(*refs):
-    for number, part in enumerate(refs[:-2]):
-        value = part[:PART].astype(F32).reshape(2, 9, ROWS, FULL)
-        for out, grad in zip(refs[-2:], (0, 1)):
-            out[:, rows_at(number), :] = value[grad]
-
-
-def finish(tile, canvas, got_1, got_3, last, late, old_0, old_1, out, out_0, out_1, total, laid, sems):
-    copies = []
-    for k, (number, part) in enumerate(((6, late), (7, last))):
-        laid[k] = part[:PART].astype(F32).reshape(2, 9, ROWS, FULL)
-        for grad, dest in enumerate((out_0, out_1)):
-            copy = pltpu.make_async_copy(
-                laid.at[k, grad], dest.at[:, rows_at(number), :], sems.at[k, grad]
-            )
-            copy.start()
-            copies.append(copy)
-    close(tile, canvas, got_1, got_3, last, out, total)
-    for copy in copies:
-        copy.wait()
+    out[...] = total[...].astype(BF16)
+    copy.wait()
 
 
 def swap(value, axis="ch"):
@@ -627,39 +633,46 @@
             add_near, [shape(part, F32), shape(part, BF16)], [VMEM] * 2, [], (1, 1), "add_near",
         )(kept, near_got)
         got.append(flip(send, "blk", 1))
-        message = shape((PART, FULL), BF16)
-        wider = shape((PART + RIM, FULL), BF16)
-        own, *wides = call(
-            add_workers, [message, wider, wider], [VMEM] * 6, [], (1, 1), "add_workers",
+        messages = [shape((n, FULL), BF16) for n in (PART, PART + RIM, SOLE, SOLE + RIM)]
+        own, wide_1, second, wide_3 = call(
+            add_workers, messages, [VMEM] * 6, [], (1, 1), "add_workers",
         )(keep, *got, *rims)
-        got_2, got_3, got_1 = flip(own, "blk", 2), flip(wides[1], "blk", 3), flip(wides[0], "blk", 1)
-        across = [swap(value, "col") for value in (own, got_1[:PART])]
-        got_3, got_2, got_1, across = tie((got_3, got_2, got_1, across))
-        got = [got_1, got_2, got_3]
+        second_3, got_2, first_3 = flip(second, "blk", 3), flip(own, "blk", 2), flip(wide_3, "blk", 3)
+        got_1 = flip(wide_1, "blk", 1)
+        flat = (TILE_ROWS * BLOCK * 32, HALF)
+        canvas, _ = tie((canvas, own))
+        image = call(sum_image, shape(flat, F32), [VMEM] * 2, [], (1, 1), "sum_image")(
+            grad_out.reshape(flat), canvas
+        )
+        across = [
+            swap(tie((value, image))[0], "col") for value in (own, got_2, got_1, second_3)
+        ]
+        first_3, got_1, across = tie((first_3, got_1, across))
         last = call(
-            column_message, shape((PART + 64, FULL), BF16), [VMEM] * 3,
-            [pltpu.VMEM((RIM, FULL), F32), pltpu.VMEM((64, HALF), F32)],
+            column_message, shape((SOLE + 64, FULL), BF16), [VMEM] * 3,
+            [pltpu.VMEM((4, RIM, FULL), F32), pltpu.VMEM((64, HALF), F32)],
             (1, 1), "column_message",
-        )(canvas.reshape(HIGH * WIDE, HALF), got[0], got[2])
-        across += [swap(got_2, "col"), swap(last, "col")]
-        early = call(
-            lay, [shape((9, HALF, FULL), F32)] * 2, [VMEM] * 6, [], (1, 1), "lay",
-        )(own, *got, *across[:2])
-        grad_in, grad_second, grad_first = pl.pallas_call(
+        )(canvas.reshape(HIGH * WIDE, HALF), got_1, first_3)
+        last = swap(last, "col")
+        grad_second, grad_first = call(
+            lay, [shape((9, HALF, FULL), F32)] * 2, [VMEM] * 9, [], (1, 1), "lay",
+        )(own, got_1, got_2, second_3, first_3, *across)
+        grad_in, grad_first = pl.pallas_call(
             finish,
-            out_shape=[shape(grad_out.shape, BF16)] + [shape((9, HALF, FULL), F32)] * 2,
-            in_specs=[VMEM] * 6 + [HBM] * 2,
-            out_specs=[VMEM] + [HBM] * 2,
+            out_shape=[shape(flat, BF16), shape((9, HALF, FULL), F32)],
+            in_specs=[VMEM] * 4 + [HBM],
+            out_specs=[VMEM, HBM],
             scratch_shapes=[
-                pltpu.VMEM((TILE_ROWS * BLOCK * 32, HALF), F32),
-                pltpu.VMEM((2, 2, 9, ROWS, FULL), F32),
-                pltpu.SemaphoreType.DMA((2, 2)),
+                pltpu.VMEM(flat, F32),
+                pltpu.VMEM((9, ROWS, FULL), F32),
+                pltpu.SemaphoreType.DMA,
             ],
-            input_output_aliases={6: 1, 7: 2},
+            input_output_aliases={4: 1},
             compiler_params=pltpu.CompilerParams(vmem_limit_bytes=48 * 1024 * 1024),
             cost_estimate=pl.CostEstimate(flops=1, bytes_accessed=1, transcendentals=0),
             name="finish",
-        )(grad_out, canvas, got[0], got[2], across[3], across[2], *early)
+        )(image, got_1, first_3, last, grad_first)
+        grad_in = grad_in.reshape(grad_out.shape)
         return (grad_in, grad_first, grad_second)
 
     grad_first, grad_second = lax.psum((terms[0][1], terms[0][0]), ("blk", "col"))

time: 87.5 us -> 89.7 us (1.025)
  starting transfers between devices: 26.3 us -> 31.1 us
  waiting for transfers between devices: 34.2 us -> 31.6 us
    ppermute x12 -> x13, starting transfers between devices: 18.3 us -> 21.3 us  [flip(): return lax.ppermute(value, axis, [(i, i ^ step) for i in range(size)])]
    ppermute x12 -> x13, waiting for transfers between devices: 22.4 us -> 19.8 us  [flip(): return lax.ppermute(value, axis, [(i, i ^ step) for i in range(size)])]
    ppermute x17 -> x18, starting transfers between devices: 7.96 us -> 9.82 us  [swap(): return lax.ppermute(value, axis, [(0, 1), (1, 0)])]
    ppermute x17 -> x18, waiting for transfers between devices: 11.8 us -> 11.8 us  [swap(): return lax.ppermute(value, axis, [(0, 1), (1, 0)])]
    pallas_call x4 -> x5, Pallas kernels: 3.31 us -> 3.29 us  [the longest x1 1.55 us: shards(): call(lay, [shape((9, HALF, FULL), F32)] * 2, [VMEM] * 9, [], (1, 1), 'lay')]
  transfers between devices with their start and end apart: 29 -> 31, of which waited for: 13 -> 14; matrix products, arithmetic and copies ran while one was open for 0% -> 0% of each run, Pallas kernels for 23% -> 23%
where the time goes in v14:
time: 89.7 us; the launch traced here: 89.4 us
  waiting for transfers between devices  31.6 us (35%)
  starting transfers between devices  31.1 us (35%)
  Pallas kernels  22 us (25%)
  local copies, waits for them, and re-layouts  3.81 us (4%)
  between operations  0.94 us (1%)
    ppermute x13, starting transfers between devices, flip(): return lax.ppermute(value, axis, [(i, i ^ step) for i in range(size)])  21.3 us
    ppermute x13, waiting for transfers between devices, flip(): return lax.ppermute(value, axis, [(i, i ^ step) for i in range(size)])  19.8 us
    ppermute x18, waiting for transfers between devices, swap(): return lax.ppermute(value, axis, [(0, 1), (1, 0)])  11.8 us
    ppermute x18, starting transfers between devices, swap(): return lax.ppermute(value, axis, [(0, 1), (1, 0)])  9.82 us
    pallas_call x1, Pallas kernels, shards(): call(functools.partial(worker, scale, owners, columns, capacity, permuted...  6.51 us
    pallas_call x1, Pallas kernels, owner(): call(functools.partial(owner_canvas, owners, capacity, wide, permuted), [...  5.8 us
    pallas_call x1, Pallas kernels, shards(): call(functools.partial(prepare, owners, columns, capacity, wide, permuted...  4.31 us
    unnamed x16, local copies, waits for them, and re-layouts  3.81 us
  transfers between devices with their start and end apart: 31, of which 14 were waited for; matrix products, arithmetic and copies ran while one was open for 0% of the time, Pallas kernels for 23%

profile of v14, /device:TPU:0, one launch (start us, length us, event | category | flops | bytes accessed | tf_op | source)
XLA Modules:
  0.0 89.4 jit_solution(2732810968840956074)
XLA Ops:
  1.7 1.9 %pack_cotangents.1 = (bf16[8,64,128]{2,1,0:T(8,128)(2,1)S(1)}, bf16[8,64,128]{2,1,0:T(8,128)(2,1)S(1)}, bf16[8,64,128]{2,1,0:T(8,128)(2,1)S(1)}, bf16[8,64,128]{2,1,0:T(8,128)(2,1)S(1)}) custom-call(s32[4,16]{1,0:T(4,128)} %bitcast.20, bf16[8,8,32,128]{3,2,1,0:T(8,128)(2,1)} %bitcast.15), custom_call_target="tpu_custom_call" | custom-call | flops 1 | bytes 1 | tf_op jit(solution)/shard_map/pack_cotangents/pallas_call | solution.py:541
  3.6 4.7 %collective-permute-start = (bf16[8,64,128]{2,1,0:T(8,128)(2,1)S(1)}, bf16[8,64,128]{2,1,0:T(8,128)(2,1)S(1)}, u32[]{:S(2)}, u32[]{:S(2)}) collective-permute-start(bf16[8,64,128]{2,1,0:T(8,128)(2,1)S(1)} %get-tuple-element.68), channel_id=1, source_target_pairs={{0,12},{4,8},{8,4},{12,0},{1,13},{5,9},{9,5},{13,1},{2,14},{6,10},... | collective-permute-start | bytes 393224 | tf_op jit(solution)/shard_map/ppermute | solution.py:508
  12.8 4.3 %prepare.1 = (bf16[10,160,128]{2,1,0:T(8,128)(2,1)S(1)}, bf16[10,80,128]{2,1,0:T(8,128)(2,1)S(1)}, bf16[10,80,128]{2,1,0:T(8,128)(2,1)S(1)}, bf16[10,80,128]{2,1...) custom-call(s32[4,16]{1,0:T(4,128)S(1)} %bitcast.21, ...), custom_call_target="tpu_custom_call" | custom-call | flops 1 | bytes 1 | tf_op jit(solution)/shard_map/prepare/pallas_call | solution.py:559
  17.1 2.9 %collective-permute-done.1.refs_2_ = bf16[8,64,128]{2,1,0:T(8,128)(2,1)S(1)} collective-permute-done((bf16[8,64,128]{2,1,0:T(8,128)(2,1)S(1)}, bf16[8,64,128]{2,1,0:T(8,128)(2,1)S(1)}, u32[]{:S(2)}, u32[]{:S(2)}) %collective-permute-start.1) | collective-permute-done | bytes 131104 | tf_op jit(solution)/shard_map/ppermute | solution.py:508
  20.1 3.0 %collective-permute-start.12 = (bf16[10,80,128]{2,1,0:T(8,128)(2,1)S(1)}, bf16[10,80,128]{2,1,0:T(8,128)(2,1)S(1)}, u32[]{:S(2)}, u32[]{:S(2)}) collective-permute-start(bf16[10,80,128]{2,1,0:T(8,128)(2,1)S(1)} %get-tuple-element.87), channel_id=1, source_target_pairs={{0,4},{4,0},{8,12},{12,8},{1,5},{5,1},{9,13},{13,9},{2,6},{6,2},{1... | collective-permute-start | bytes 614408 | tf_op jit(solution)/shard_map/ppermute | solution.py:508
  25.0 6.5 %worker.1 = (f32[4,2,9,16,256]{4,3,2,1,0:T(8,128)S(1)}, bf16[2,2,9,16,256]{4,3,2,1,0:T(8,128)(2,1)S(1)}, bf16[2,2,9,16,256]{4,3,2,1,0:T(8,128)(2,1)S(1)}) custom-call(s32[4,16]{1,0:T(4,128)S(1)} %bitcast.22, bf16[8,64,128]{2,1,0:T(8,128)(2,1)S(1)} %get-tuple-element.78.refs_0_, bf16[8,64,128]{2,1,0:T(8,128)(2,1)S(1)} %collective-permute-done.2.refs_1_, ...), custom_call_target="tpu_custom_call" | custom-call | flops 1 | bytes 1 | tf_op jit(solution)/shard_map/worker/pallas_call | solution.py:585
  31.5 1.3 %collective-permute-done.11.refs_2_ = bf16[10,80,128]{2,1,0:T(8,128)(2,1)S(1)} collective-permute-done((bf16[10,80,128]{2,1,0:T(8,128)(2,1)S(1)}, bf16[10,80,128]{2,1,0:T(8,128)(2,1)S(1)}, u32[]{:S(2)}, u32[]{:S(2)}) %collective-permute-start.11) | collective-permute-done | bytes 204832 | tf_op jit(solution)/shard_map/ppermute | solution.py:508
  32.9 1.5 %collective-permute-start.13 = (bf16[2,2,9,16,256]{4,3,2,1,0:T(8,128)(2,1)S(1)}, bf16[2,2,9,16,256]{4,3,2,1,0:T(8,128)(2,1)S(1)}, u32[]{:S(2)}, u32[]{:S(2)}) collective-permute-start(bf16[2,2,9,16,256]{4,3,2,1,0:T(8,128)(2,1)S(1)} %get-tuple-element.91), channel_id=1, source_target_pairs={{0,2},{2,0},{1,3},{3,1},{4,6},{6,4},{5,7},{7,5},{8,10},{10,8},{9,1... | collective-permute-start | bytes 884744 | tf_op jit(solution)/shard_map/ppermute | solution.py:503
  34.4 1.5 %collective-permute-start.14 = (bf16[10,80,128]{2,1,0:T(8,128)(2,1)S(1)}, bf16[10,80,128]{2,1,0:T(8,128)(2,1)S(1)}, u32[]{:S(2)}, u32[]{:S(2)}) collective-permute-start(bf16[10,80,128]{2,1,0:T(8,128)(2,1)S(1)} %get-tuple-element.94), channel_id=1, source_target_pairs={{0,12},{4,8},{8,4},{12,0},{1,13},{5,9},{9,5},{13,1},{2,14},{6,10},... | collective-permute-start | bytes 614408 | tf_op jit(solution)/shard_map/ppermute | solution.py:508
  36.9 5.9 %collective-permute-done.13.got = bf16[2,2,9,16,256]{4,3,2,1,0:T(8,128)(2,1)S(1)} collective-permute-done((bf16[2,2,9,16,256]{4,3,2,1,0:T(8,128)(2,1)S(1)}, bf16[2,2,9,16,256]{4,3,2,1,0:T(8,128)(2,1)S(1)}, u32[]{:S(2)}, u32[]{:S(2)}) %collective-permute-start.13) | collective-permute-done | bytes 294944 | tf_op jit(solution)/shard_map/ppermute | solution.py:503
  43.5 1.5 %collective-permute-start.19 = (bf16[2,9,16,256]{3,2,1,0:T(8,128)(2,1)S(1)}, bf16[2,9,16,256]{3,2,1,0:T(8,128)(2,1)S(1)}, u32[]{:S(2)}, u32[]{:S(2)}) collective-permute-start(bf16[2,9,16,256]{3,2,1,0:T(8,128)(2,1)S(1)} %get-tuple-element.101), channel_id=1, source_target_pairs={{0,12},{4,8},{8,4},{12,0},{1,13},{5,9},{9,5},{13,1},{2,14},{6,10},... | collective-permute-start | bytes 442376 | tf_op jit(solution)/shard_map/ppermute | solution.py:508
  46.3 5.8 %owner_canvas.1 = (f32[68,40,128]{2,1,0:T(8,128)S(1)}, bf16[48,256]{1,0:T(8,128)(2,1)S(1)}, bf16[48,256]{1,0:T(8,128)(2,1)S(1)}) custom-call(s32[4,16]{1,0:T(4,128)S(1)} %bitcast.23, bf16[10,80,128]{2,1,0:T(8,128)(2,1)S(1)} %get-tuple-element.84.refs_0_, bf16[10,80,128]{2,1,0:T(8,128)(2,1)S(1)} %collective-permute-done.12.refs_1_, ...), custom_call_target="tpu_custom_call" | custom-call | flops 1 | bytes 1 | tf_op jit(solution)/shard_map/owner_canvas/pallas_call | solution.py:611
  52.2 1.7 %collective-permute-start.21 = (bf16[2,9,16,256]{3,2,1,0:T(8,128)(2,1)S(1)}, bf16[2,9,16,256]{3,2,1,0:T(8,128)(2,1)S(1)}, u32[]{:S(2)}, u32[]{:S(2)}) collective-permute-start(bf16[2,9,16,256]{3,2,1,0:T(8,128)(2,1)S(1)} %get-tuple-element.103), channel_id=1, source_target_pairs={{0,4},{4,0},{8,12},{12,8},{1,5},{5,1},{9,13},{13,9},{2,6},{6,2},{1... | collective-permute-start | bytes 442376 | tf_op jit(solution)/shard_map/ppermute | solution.py:508
  53.9 6.2 %collective-permute-done.20.got_2 = bf16[2,9,16,256]{3,2,1,0:T(8,128)(2,1)S(1)} collective-permute-done((bf16[2,9,16,256]{3,2,1,0:T(8,128)(2,1)S(1)}, bf16[2,9,16,256]{3,2,1,0:T(8,128)(2,1)S(1)}, u32[]{:S(2)}, u32[]{:S(2)}) %collective-permute-start.20) | collective-permute-done | bytes 147488 | tf_op jit(solution)/shard_map/ppermute | solution.py:508
  61.2 3.0 %collective-permute-start.25 = (bf16[288,256]{1,0:T(8,128)(2,1)S(1)}, bf16[288,256]{1,0:T(8,128)(2,1)S(1)}, u32[]{:S(2)}, u32[]{:S(2)}) collective-permute-start(bf16[288,256]{1,0:T(8,128)(2,1)S(1)} %get-tuple-element.110.refs_0_), channel_id=1, source_target_pairs={{0,8},{4,12},{8,0},{12,4},{1,9},{5,13},{9,1},{13,5},{2,10},{6,14},... | collective-permute-start | bytes 442376 | tf_op jit(solution)/shard_map/ppermute | solution.py:508
  64.4 5.4 %collective-permute-done.23.got_1.refs_1_ = bf16[336,256]{1,0:T(8,128)(2,1)S(1)} collective-permute-done((bf16[336,256]{1,0:T(8,128)(2,1)S(1)}, bf16[336,256]{1,0:T(8,128)(2,1)S(1)}, u32[]{:S(2)}, u32[]{:S(2)}) %collective-permute-start.23) | collective-permute-done | bytes 172064 | tf_op jit(solution)/shard_map/ppermute | solution.py:508
  70.5 1.8 %collective-permute-start.28 = (bf16[144,256]{1,0:T(8,128)(2,1)S(1)}, bf16[144,256]{1,0:T(8,128)(2,1)S(1)}, u32[]{:S(2)}, u32[]{:S(2)}) collective-permute-start(bf16[144,256]{1,0:T(8,128)(2,1)S(1)} %get-tuple-element.113), channel_id=1, source_target_pairs={{0,12},{4,8},{8,4},{12,0},{1,13},{5,9},{9,5},{13,1},{2,14},{6,10},... | collective-permute-start | bytes 221192 | tf_op jit(solution)/shard_map/ppermute | solution.py:508
  74.3 2.0 %collective-permute-start.22 = (bf16[192,256]{1,0:T(8,128)(2,1)S(1)}, bf16[192,256]{1,0:T(8,128)(2,1)S(1)}, u32[]{:S(2)}, u32[]{:S(2)}) collective-permute-start(bf16[192,256]{1,0:T(8,128)(2,1)S(1)} %get-tuple-element.108), channel_id=1, source_target_pairs={{0,12},{4,8},{8,4},{12,0},{1,13},{5,9},{9,5},{13,1},{2,14},{6,10},... | collective-permute-start | bytes 294920 | tf_op jit(solution)/shard_map/ppermute | solution.py:508
  76.9 1.5 %collective-permute-start.29 = (bf16[144,256]{1,0:T(8,128)(2,1)S(1)}, bf16[144,256]{1,0:T(8,128)(2,1)S(1)}, u32[]{:S(2)}, u32[]{:S(2)}) collective-permute-start(bf16[144,256]{1,0:T(8,128)(2,1)S(1)} %collective-permute-done.28.refs_3_), channel_id=1, source_target_pairs={{0,2},{2,0},{1,3},{3,1},{4,6},{6,4},{5,7},{7,5},{8,10},{10,8},{9,1... | collective-permute-start | bytes 221192 | tf_op jit(solution)/shard_map/ppermute | solution.py:503
  78.4 2.3 %collective-permute-done.22.got_3.refs_4_ = bf16[192,256]{1,0:T(8,128)(2,1)S(1)} collective-permute-done((bf16[192,256]{1,0:T(8,128)(2,1)S(1)}, bf16[192,256]{1,0:T(8,128)(2,1)S(1)}, u32[]{:S(2)}, u32[]{:S(2)}) %collective-permute-start.22) | collective-permute-done | bytes 98336 | tf_op jit(solution)/shard_map/ppermute | solution.py:508
  80.7 2.2 %collective-permute-done.29.refs_8_ = bf16[144,256]{1,0:T(8,128)(2,1)S(1)} collective-permute-done((bf16[144,256]{1,0:T(8,128)(2,1)S(1)}, bf16[144,256]{1,0:T(8,128)(2,1)S(1)}, u32[]{:S(2)}, u32[]{:S(2)}) %collective-permute-start.29) | collective-permute-done | bytes 73760 | tf_op jit(solution)/shard_map/ppermute | solution.py:503
  83.9 1.5 %lay.1 = (f32[9,128,256]{2,1,0:T(8,128)}, f32[9,128,256]{2,1,0:T(8,128)}) custom-call(bf16[288,256]{1,0:T(8,128)(2,1)S(1)} %get-tuple-element.110.refs_0_, bf16[336,256]{1,0:T(8,128)(2,1)S(1)} %collective-permute-done.23.got_1.refs_1_, bf16[288,256]{1,0:T(8,128)(2,1)S(1)} %collective-permute-done.25.refs_2_, ...), custom_call_target="tpu_custom_call" | custom-call | flops 1 | bytes 1 | tf_op jit(solution)/shard_map/lay/pallas_call | solution.py:657
  85.5 2.3 %collective-permute-done.30.last = bf16[208,256]{1,0:T(8,128)(2,1)S(1)} collective-permute-done((bf16[208,256]{1,0:T(8,128)(2,1)S(1)}, bf16[208,256]{1,0:T(8,128)(2,1)S(1)}, u32[]{:S(2)}, u32[]{:S(2)}) %collective-permute-start.30) | collective-permute-done | bytes 106528 | tf_op jit(solution)/shard_map/ppermute | solution.py:503
  87.8 1.5 %finish.1 = (bf16[2048,128]{1,0:T(8,128)(2,1)}, f32[9,128,256]{2,1,0:T(8,128)}) custom-call(f32[2048,128]{1,0:T(8,128)S(1)} %sum_image.1.early, bf16[336,256]{1,0:T(8,128)(2,1)S(1)} %collective-permute-done.23.got_1.refs_1_, bf16[192,256]{1,0:T(8,128)(2,1)S(1)} %collective-permute-done.22.got_3.refs_4_, ...), custom_call_target="tpu_custom_call", output_to_operand_aliasing={{1}: (4, {})} | custom-call | flops 1 | bytes 1 | tf_op jit(solution)/shard_map/finish/pallas_call | solution.py:660
  (65 shorter events, 16.2 us)
Async XLA Ops:
  0.6 7.7 %collective-permute-start.3 = (bf16[8,8,32,128]{3,2,1,0:T(8,128)(2,1)}, bf16[8,8,32,128]{3,2,1,0:T(8,128)(2,1)S(1)}, u32[]{:S(2)}, u32[]{:S(2)}) collective-permute-start(bf16[8,8,32,128]{3,2,1,0:T(8,128)(2,1)} %bitcast.14), channel_id=1, source_target_pairs={{0,1},{1,0},{2,3},{3,2},{4,5},{5,4},{6,7},{7,6},{8,9},{9,8},{10,11... | collective-permute-start | bytes 1572872 | tf_op jit(solution)/shard_map/ppermute | solution.py:503
  1.1 7.9 %collective-permute-start.4 = (bf16[9,128,256]{2,1,0:T(8,128)(2,1)}, bf16[9,128,256]{2,1,0:T(8,128)(2,1)S(1)}, u32[]{:S(2)}, u32[]{:S(2)}) collective-permute-start(bf16[9,128,256]{2,1,0:T(8,128)(2,1)} %refs_10_.1), channel_id=1, source_target_pairs={{0,1},{1,0},{2,3},{3,2},{4,5},{5,4},{6,7},{7,6},{8,9},{9,8},{10,11... | collective-permute-start | bytes 1769480 | tf_op jit(solution)/shard_map/ppermute | solution.py:503
  1.2 21.9 %collective-permute-start.9 = (bf16[10,160,128]{2,1,0:T(8,128)(2,1)}, bf16[10,160,128]{2,1,0:T(8,128)(2,1)S(1)}, u32[]{:S(2)}, u32[]{:S(2)}) collective-permute-start(bf16[10,160,128]{2,1,0:T(8,128)(2,1)} %bitcast.18), channel_id=1, source_target_pairs={{0,1},{1,0},{2,3},{3,2},{4,5},{5,4},{6,7},{7,6},{8,9},{9,8},{10,11... | collective-permute-start | bytes 1228808 | tf_op jit(solution)/shard_map/ppermute | solution.py:503
  3.6 13.5 %collective-permute-start = (bf16[8,64,128]{2,1,0:T(8,128)(2,1)S(1)}, bf16[8,64,128]{2,1,0:T(8,128)(2,1)S(1)}, u32[]{:S(2)}, u32[]{:S(2)}) collective-permute-start(bf16[8,64,128]{2,1,0:T(8,128)(2,1)S(1)} %get-tuple-element.68), channel_id=1, source_target_pairs={{0,12},{4,8},{8,4},{12,0},{1,13},{5,9},{9,5},{13,1},{2,14},{6,10},... | collective-permute-start | bytes 393224 | tf_op jit(solution)/shard_map/ppermute | solution.py:508
  8.4 11.7 %collective-permute-start.1 = (bf16[8,64,128]{2,1,0:T(8,128)(2,1)S(1)}, bf16[8,64,128]{2,1,0:T(8,128)(2,1)S(1)}, u32[]{:S(2)}, u32[]{:S(2)}) collective-permute-start(bf16[8,64,128]{2,1,0:T(8,128)(2,1)S(1)} %get-tuple-element.69), channel_id=1, source_target_pairs={{0,8},{4,12},{8,0},{12,4},{1,9},{5,13},{9,1},{13,5},{2,10},{6,14},... | collective-permute-start | bytes 393224 | tf_op jit(solution)/shard_map/ppermute | solution.py:508
  8.4 11.7 %collective-permute-start.2 = (bf16[8,64,128]{2,1,0:T(8,128)(2,1)S(1)}, bf16[8,64,128]{2,1,0:T(8,128)(2,1)S(1)}, u32[]{:S(2)}, u32[]{:S(2)}) collective-permute-start(bf16[8,64,128]{2,1,0:T(8,128)(2,1)S(1)} %get-tuple-element.70), channel_id=1, source_target_pairs={{0,4},{4,0},{8,12},{12,8},{1,5},{5,1},{9,13},{13,9},{2,6},{6,2},{1... | collective-permute-start | bytes 393224 | tf_op jit(solution)/shard_map/ppermute | solution.py:508
  20.0 12.7 %collective-permute-start.11 = (bf16[10,80,128]{2,1,0:T(8,128)(2,1)S(1)}, bf16[10,80,128]{2,1,0:T(8,128)(2,1)S(1)}, u32[]{:S(2)}, u32[]{:S(2)}) collective-permute-start(bf16[10,80,128]{2,1,0:T(8,128)(2,1)S(1)} %get-tuple-element.86), channel_id=1, source_target_pairs={{0,8},{4,12},{8,0},{12,4},{1,9},{5,13},{9,1},{13,5},{2,10},{6,14},... | collective-permute-start | bytes 614408 | tf_op jit(solution)/shard_map/ppermute | solution.py:508
  20.1 12.9 %collective-permute-start.12 = (bf16[10,80,128]{2,1,0:T(8,128)(2,1)S(1)}, bf16[10,80,128]{2,1,0:T(8,128)(2,1)S(1)}, u32[]{:S(2)}, u32[]{:S(2)}) collective-permute-start(bf16[10,80,128]{2,1,0:T(8,128)(2,1)S(1)} %get-tuple-element.87), channel_id=1, source_target_pairs={{0,4},{4,0},{8,12},{12,8},{1,5},{5,1},{9,13},{13,9},{2,6},{6,2},{1... | collective-permute-start | bytes 614408 | tf_op jit(solution)/shard_map/ppermute | solution.py:508
  32.9 9.9 %collective-permute-start.13 = (bf16[2,2,9,16,256]{4,3,2,1,0:T(8,128)(2,1)S(1)}, bf16[2,2,9,16,256]{4,3,2,1,0:T(8,128)(2,1)S(1)}, u32[]{:S(2)}, u32[]{:S(2)}) collective-permute-start(bf16[2,2,9,16,256]{4,3,2,1,0:T(8,128)(2,1)S(1)} %get-tuple-element.91), channel_id=1, source_target_pairs={{0,2},{2,0},{1,3},{3,1},{4,6},{6,4},{5,7},{7,5},{8,10},{10,8},{9,1... | collective-permute-start | bytes 884744 | tf_op jit(solution)/shard_map/ppermute | solution.py:503
  34.4 8.5 %collective-permute-start.14 = (bf16[10,80,128]{2,1,0:T(8,128)(2,1)S(1)}, bf16[10,80,128]{2,1,0:T(8,128)(2,1)S(1)}, u32[]{:S(2)}, u32[]{:S(2)}) collective-permute-start(bf16[10,80,128]{2,1,0:T(8,128)(2,1)S(1)} %get-tuple-element.94), channel_id=1, source_target_pairs={{0,12},{4,8},{8,4},{12,0},{1,13},{5,9},{9,5},{13,1},{2,14},{6,10},... | collective-permute-start | bytes 614408 | tf_op jit(solution)/shard_map/ppermute | solution.py:508
  35.9 16.2 %collective-permute-start.10 = (bf16[2,2,9,16,256]{4,3,2,1,0:T(8,128)(2,1)S(1)}, bf16[2,2,9,16,256]{4,3,2,1,0:T(8,128)(2,1)S(1)}, u32[]{:S(2)}, u32[]{:S(2)}) collective-permute-start(bf16[2,2,9,16,256]{4,3,2,1,0:T(8,128)(2,1)S(1)} %get-tuple-element.83), channel_id=1, source_target_pairs={{0,2},{2,0},{1,3},{3,1},{4,6},{6,4},{5,7},{7,5},{8,10},{10,8},{9,1... | collective-permute-start | bytes 884744 | tf_op jit(solution)/shard_map/ppermute | solution.py:503
  36.4 7.1 %collective-permute-start.15 = (bf16[10,80,128]{2,1,0:T(8,128)(2,1)S(1)}, bf16[10,80,128]{2,1,0:T(8,128)(2,1)S(1)}, u32[]{:S(2)}, u32[]{:S(2)}) collective-permute-start(bf16[10,80,128]{2,1,0:T(8,128)(2,1)S(1)} %get-tuple-element.84.refs_0_), channel_id=1, source_target_pairs={{0,1},{1,0},{2,3},{3,2},{4,5},{5,4},{6,7},{7,6},{8,9},{9,8},{10,11... | collective-permute-start | bytes 614408 | tf_op jit(solution)/shard_map/ppermute | solution.py:503
  36.4 8.5 %collective-permute-start.16 = (bf16[10,80,128]{2,1,0:T(8,128)(2,1)S(1)}, bf16[10,80,128]{2,1,0:T(8,128)(2,1)S(1)}, u32[]{:S(2)}, u32[]{:S(2)}) collective-permute-start(bf16[10,80,128]{2,1,0:T(8,128)(2,1)S(1)} %collective-permute-done.12.refs_1_), channel_id=1, source_target_pairs={{0,1},{1,0},{2,3},{3,2},{4,5},{5,4},{6,7},{7,6},{8,9},{9,8},{10,11... | collective-permute-start | bytes 614408 | tf_op jit(solution)/shard_map/ppermute | solution.py:503
  43.5 10.4 %collective-permute-start.19 = (bf16[2,9,16,256]{3,2,1,0:T(8,128)(2,1)S(1)}, bf16[2,9,16,256]{3,2,1,0:T(8,128)(2,1)S(1)}, u32[]{:S(2)}, u32[]{:S(2)}) collective-permute-start(bf16[2,9,16,256]{3,2,1,0:T(8,128)(2,1)S(1)} %get-tuple-element.101), channel_id=1, source_target_pairs={{0,12},{4,8},{8,4},{12,0},{1,13},{5,9},{9,5},{13,1},{2,14},{6,10},... | collective-permute-start | bytes 442376 | tf_op jit(solution)/shard_map/ppermute | solution.py:508
  45.0 15.1 %collective-permute-start.20 = (bf16[2,9,16,256]{3,2,1,0:T(8,128)(2,1)S(1)}, bf16[2,9,16,256]{3,2,1,0:T(8,128)(2,1)S(1)}, u32[]{:S(2)}, u32[]{:S(2)}) collective-permute-start(bf16[2,9,16,256]{3,2,1,0:T(8,128)(2,1)S(1)} %get-tuple-element.102), channel_id=1, source_target_pairs={{0,8},{4,12},{8,0},{12,4},{1,9},{5,13},{9,1},{13,5},{2,10},{6,14},... | collective-permute-start | bytes 442376 | tf_op jit(solution)/shard_map/ppermute | solution.py:508
  52.2 8.9 %collective-permute-start.21 = (bf16[2,9,16,256]{3,2,1,0:T(8,128)(2,1)S(1)}, bf16[2,9,16,256]{3,2,1,0:T(8,128)(2,1)S(1)}, u32[]{:S(2)}, u32[]{:S(2)}) collective-permute-start(bf16[2,9,16,256]{3,2,1,0:T(8,128)(2,1)S(1)} %get-tuple-element.103), channel_id=1, source_target_pairs={{0,4},{4,0},{8,12},{12,8},{1,5},{5,1},{9,13},{13,9},{2,6},{6,2},{1... | collective-permute-start | bytes 442376 | tf_op jit(solution)/shard_map/ppermute | solution.py:508
  61.2 8.6 %collective-permute-start.23 = (bf16[336,256]{1,0:T(8,128)(2,1)S(1)}, bf16[336,256]{1,0:T(8,128)(2,1)S(1)}, u32[]{:S(2)}, u32[]{:S(2)}) collective-permute-start(bf16[336,256]{1,0:T(8,128)(2,1)S(1)} %get-tuple-element.109), channel_id=1, source_target_pairs={{0,4},{4,0},{8,12},{12,8},{1,5},{5,1},{9,13},{13,9},{2,6},{6,2},{1... | collective-permute-start | bytes 516104 | tf_op jit(solution)/shard_map/ppermute | solution.py:508
  61.2 12.1 %collective-permute-start.25 = (bf16[288,256]{1,0:T(8,128)(2,1)S(1)}, bf16[288,256]{1,0:T(8,128)(2,1)S(1)}, u32[]{:S(2)}, u32[]{:S(2)}) collective-permute-start(bf16[288,256]{1,0:T(8,128)(2,1)S(1)} %get-tuple-element.110.refs_0_), channel_id=1, source_target_pairs={{0,8},{4,12},{8,0},{12,4},{1,9},{5,13},{9,1},{13,5},{2,10},{6,14},... | collective-permute-start | bytes 442376 | tf_op jit(solution)/shard_map/ppermute | solution.py:508
  69.8 13.2 %collective-permute-start.27 = (bf16[336,256]{1,0:T(8,128)(2,1)S(1)}, bf16[336,256]{1,0:T(8,128)(2,1)S(1)}, u32[]{:S(2)}, u32[]{:S(2)}) collective-permute-start(bf16[336,256]{1,0:T(8,128)(2,1)S(1)} %collective-permute-done.23.got_1.refs_1_), channel_id=1, source_target_pairs={{0,2},{2,0},{1,3},{3,1},{4,6},{6,4},{5,7},{7,5},{8,10},{10,8},{9,1... | collective-permute-start | bytes 516104 | tf_op jit(solution)/shard_map/ppermute | solution.py:503
  70.5 6.5 %collective-permute-start.28 = (bf16[144,256]{1,0:T(8,128)(2,1)S(1)}, bf16[144,256]{1,0:T(8,128)(2,1)S(1)}, u32[]{:S(2)}, u32[]{:S(2)}) collective-permute-start(bf16[144,256]{1,0:T(8,128)(2,1)S(1)} %get-tuple-element.113), channel_id=1, source_target_pairs={{0,12},{4,8},{8,4},{12,0},{1,13},{5,9},{9,5},{13,1},{2,14},{6,10},... | collective-permute-start | bytes 221192 | tf_op jit(solution)/shard_map/ppermute | solution.py:508
  72.3 8.4 %collective-permute-start.24 = (bf16[288,256]{1,0:T(8,128)(2,1)S(1)}, bf16[288,256]{1,0:T(8,128)(2,1)S(1)}, u32[]{:S(2)}, u32[]{:S(2)}) collective-permute-start(bf16[288,256]{1,0:T(8,128)(2,1)S(1)} %get-tuple-element.110.refs_0_), channel_id=1, source_target_pairs={{0,2},{2,0},{1,3},{3,1},{4,6},{6,4},{5,7},{7,5},{8,10},{10,8},{9,1... | collective-permute-start | bytes 442376 | tf_op jit(solution)/shard_map/ppermute | solution.py:503
  73.4 9.6 %collective-permute-start.26 = (bf16[288,256]{1,0:T(8,128)(2,1)S(1)}, bf16[288,256]{1,0:T(8,128)(2,1)S(1)}, u32[]{:S(2)}, u32[]{:S(2)}) collective-permute-start(bf16[288,256]{1,0:T(8,128)(2,1)S(1)} %collective-permute-done.25.refs_2_), channel_id=1, source_target_pairs={{0,2},{2,0},{1,3},{3,1},{4,6},{6,4},{5,7},{7,5},{8,10},{10,8},{9,1... | collective-permute-start | bytes 442376 | tf_op jit(solution)/shard_map/ppermute | solution.py:503
  74.3 6.4 %collective-permute-start.22 = (bf16[192,256]{1,0:T(8,128)(2,1)S(1)}, bf16[192,256]{1,0:T(8,128)(2,1)S(1)}, u32[]{:S(2)}, u32[]{:S(2)}) collective-permute-start(bf16[192,256]{1,0:T(8,128)(2,1)S(1)} %get-tuple-element.108), channel_id=1, source_target_pairs={{0,12},{4,8},{8,4},{12,0},{1,13},{5,9},{9,5},{13,1},{2,14},{6,10},... | collective-permute-start | bytes 294920 | tf_op jit(solution)/shard_map/ppermute | solution.py:508
  76.9 6.0 %collective-permute-start.29 = (bf16[144,256]{1,0:T(8,128)(2,1)S(1)}, bf16[144,256]{1,0:T(8,128)(2,1)S(1)}, u32[]{:S(2)}, u32[]{:S(2)}) collective-permute-start(bf16[144,256]{1,0:T(8,128)(2,1)S(1)} %collective-permute-done.28.refs_3_), channel_id=1, source_target_pairs={{0,2},{2,0},{1,3},{3,1},{4,6},{6,4},{5,7},{7,5},{8,10},{10,8},{9,1... | collective-permute-start | bytes 221192 | tf_op jit(solution)/shard_map/ppermute | solution.py:503
  (15 other events, 77.0 us)

commit v15 on v13

--- a/solution.py
+++ b/solution.py
@@ -114,22 +114,24 @@
 
 
 def pack_cotangents(owners, capacity, permuted, listed, source, *refs):
-    outs, (table, tile, routing, arrived) = refs[:-4], refs[-4:]
+    outs, (places, tile, codes, arrived) = refs[:-4], refs[-4:]
     fetch = pltpu.make_async_copy(source, tile, arrived.at[0])
     fetch.start()
-    lists = pltpu.make_async_copy(listed, routing, arrived.at[1])
+    lists = pltpu.make_async_copy(listed, codes, arrived.at[1])
     lists.start()
     lists.wait()
-    owner_table(routing, table, owners, capacity)
+    hit = (codes[...] // TILE_BLOCKS) == lax.axis_index("blk")
+    places[0] = jnp.where(hit, codes[...] % TILE_BLOCKS + 1, 0)
+    before = (iota((PER_WORKER, PER_WORKER), 0) < iota((PER_WORKER, PER_WORKER), 1))
+    places[1] = dot(one_hot(hit), one_hot(before)).astype(I32)
     rows = BLOCK * capacity
     row, lane = iota((rows, FULL), 0), iota((rows, FULL), 1)
     picks = []
     for step in range(owners):
-        worker = partner("blk", step, permuted)
-        target = jnp.full((rows, FULL), DEAD, I32)
-        for rank in range(capacity):
-            place = table[worker * capacity + rank] * BLOCK
-            target = jnp.where(row % capacity == rank, place, target)
+        at = pl.ds(partner("blk", step, permuted), 1)
+        same = places[1, at, :] == iota((rows, PER_WORKER), 0) % capacity
+        place = jnp.sum(jnp.where(same, places[0, at, :], 0).astype(F32), axis=1, keepdims=True)
+        target = (place.astype(I32) - 1) * BLOCK
         picks.append(one_hot(lane == target + row // capacity))
     pick = jnp.concatenate(picks, axis=0)
     fetch.wait()
@@ -319,13 +321,6 @@
     full[...] = ordered(second[...], second_other[...], 1)
     spread(cot, full, total, TILE_BLOCKS)
     out[...] = total[...].astype(BF16).reshape(out.shape)
-
-
-def prepare(owners, columns, capacity, wide, permuted, routing, saved, *refs):
-    (tile, tile_other, second, second_other, masked), refs = refs[:5], refs[5:]
-    outs, (out, counts, table, total, cot, full) = refs[:-6], refs[-6:]
-    pack_saved(owners, columns, capacity, wide, permuted, routing, saved, masked, *outs, counts, table)
-    owner_spread(tile, tile_other, second, second_other, out, total, cot, full)
 
 
 def worker(scale, owners, columns, capacity, permuted, routing, *refs):
@@ -445,10 +440,11 @@
         out[PART:, j * HALF : (j + 1) * HALF] = strip[...].astype(BF16)
 
 
-def close(tile, canvas, got_1, got_3, across, out, total):
+def gather_image(tile, canvas, got_1, got_3, total):
     rows = TILE_ROWS * BLOCK * 32
-    inner = canvas[2 : HIGH - 2, :32, :].reshape(rows, HALF)
-    total[...] = tile[...].reshape(rows, HALF).astype(F32) + inner
+    total[...] = tile[...].reshape(rows, HALF).astype(F32) + canvas[
+        2 : HIGH - 2, :32, :
+    ].reshape(rows, HALF)
     for step, got in ((1, got_1), (3, got_3)):
         rim = got[PART : PART + 32].astype(F32)
         above, below = adjacent(step)
@@ -457,12 +453,6 @@
         total[32:64] += top[:, HALF:]
         total[rows - 64 : rows - 32] += bottom[:, :HALF]
         total[rows - 32 : rows] += bottom[:, HALF:]
-    strip = across[PART:].astype(F32)
-    at = jnp.where(lax.axis_index("col") == 0, 30, 0)
-    for j in range(2):
-        spot = (pl.ds(at + j, 64, stride=32), slice(None))
-        total[spot] = total[spot] + strip[:, j * HALF : (j + 1) * HALF]
-    out[...] = total[...].astype(BF16).reshape(out.shape)
 
 
 def rows_at(number):
@@ -471,24 +461,40 @@
     return pl.ds(pl.multiple_of(place * ROWS, ROWS), ROWS)
 
 
-def lay(*refs):
-    for number, part in enumerate(refs[:-2]):
+def lay(tile, canvas, *refs):
+    parts, (image, slab), outs, total = refs[:-5], refs[-5:-3], refs[-3:-1], refs[-1]
+    gather_image(tile, canvas, parts[1], parts[3], total)
+    whole = total[...].reshape(image.shape)
+    image[...] = whole.astype(BF16)
+    slab[...] = jnp.where(lax.axis_index("col") == 0, whole[:, 16:], whole[:, :16])
+    for number, part in enumerate(parts):
         value = part[:PART].astype(F32).reshape(2, 9, ROWS, FULL)
-        for out, grad in zip(refs[-2:], (0, 1)):
+        for out, grad in zip(outs, (0, 1)):
             out[:, rows_at(number), :] = value[grad]
 
 
-def finish(tile, canvas, got_1, got_3, last, late, old_0, old_1, out, out_0, out_1, total, laid, sems):
+def finish(slab, last, late, old, old_0, old_1, image, out_0, out_1, total, side, laid, sems):
     copies = []
     for k, (number, part) in enumerate(((6, late), (7, last))):
         laid[k] = part[:PART].astype(F32).reshape(2, 9, ROWS, FULL)
         for grad, dest in enumerate((out_0, out_1)):
-            copy = pltpu.make_async_copy(
-                laid.at[k, grad], dest.at[:, rows_at(number), :], sems.at[k, grad]
+            copies.append(
+                pltpu.make_async_copy(
+                    laid.at[k, grad], dest.at[:, rows_at(number), :], sems.at[k, grad]
+                )
             )
-            copy.start()
-            copies.append(copy)
-    close(tile, canvas, got_1, got_3, last, out, total)
+            copies[-1].start()
+    total[...] = slab[...].reshape(total.shape)
+    strip = last[PART:].astype(F32)
+    left = lax.axis_index("col") == 0
+    at = jnp.where(left, 14, 0)
+    for j in range(2):
+        spot = (pl.ds(at + j, 64, stride=16), slice(None))
+        total[spot] = total[spot] + strip[:, j * HALF : (j + 1) * HALF]
+    side[...] = total[...].astype(BF16).reshape(side.shape)
+    columns = pl.ds(pl.multiple_of(jnp.where(left, 16, 0), 16), 16)
+    copies.append(pltpu.make_async_copy(side, image.at[:, columns, :], sems.at[2, 0]))
+    copies[-1].start()
     for copy in copies:
         copy.wait()
 
@@ -531,15 +537,14 @@
 
     tie = lax.optimization_barrier
     tile = grad_out.reshape(TILE_ROWS, BLOCK, TILE_COLS * BLOCK, HALF)
-    second_other, tile_other = swap(second_weight), swap(tile)
     outgoing = call(
         functools.partial(pack_cotangents, owners, capacity, permuted),
         pieces(BLOCK, BLOCK * capacity, HALF),
         [HBM, HBM],
-        tables
-        + [
+        [
+            pltpu.VMEM((2,) + routing.shape, I32),
             pltpu.VMEM(tile.shape, BF16),
-            pltpu.SMEM(routing.shape, I32),
+            pltpu.VMEM(routing.shape, I32),
             pltpu.SemaphoreType.DMA((2,)),
         ],
         (1, 1), "pack_cotangents",
@@ -547,25 +552,16 @@
     saved_slots = saved_pre[0, 0].transpose(1, 2, 0, 3)
     saved_slots = saved_slots.reshape(MIDDLE, MIDDLE * PER_WORKER, HALF)
     outgoing, saved_here = tie((outgoing, saved_slots))
-    saved_other = swap(saved_slots)
     incoming = exchange(outgoing)
 
-    masked, *to_owners, total = call(
-        functools.partial(prepare, owners, columns, capacity, wide, permuted),
-        [shape((MIDDLE, MIDDLE * PER_WORKER, HALF), BF16)]
-        + pieces(MIDDLE, wide * capacity, HALF)
-        + [shape((MIDDLE, MIDDLE, TILE_BLOCKS, FULL), BF16)],
-        [SMEM] + [VMEM] * 5,
-        counts
-        + tables
-        + [
-            pltpu.VMEM((MIDDLE, MIDDLE * TILE_BLOCKS, FULL), F32),
-            pltpu.VMEM((BLOCK, BLOCK * TILE_BLOCKS, FULL), BF16),
-            pltpu.VMEM((9, FULL, FULL), BF16),
-        ],
-        (1, 1), "prepare",
-    )(routing, saved_here, tile, tile_other, second_weight, second_other)
-    incoming, to_owners, total = tie((incoming[::-1], to_owners[::-1], total))
+    masked, *to_owners = call(
+        functools.partial(pack_saved, owners, columns, capacity, wide, permuted),
+        [shape((MIDDLE, MIDDLE * PER_WORKER, HALF), BF16)] + pieces(MIDDLE, wide * capacity, HALF),
+        [SMEM, VMEM], counts + tables, (1, 1), "pack_saved",
+    )(routing, saved_here)
+    second_other, saved_other = swap(second_weight), swap(saved_slots)
+
+    incoming, to_owners = tie((incoming[::-1], to_owners[::-1]))
     incoming, to_owners = incoming[::-1], to_owners[::-1]
     incoming_other = [swap(value) for value in incoming]
     at_owner = exchange(to_owners)
@@ -599,6 +595,20 @@
     if permuted:
         kept, near, far = terms
         far, at_owner[2], at_owner[1] = tie((far, at_owner[2], at_owner[1]))
+        far, tile_mine, tile_here = tie((far, tile, tile))
+    else:
+        terms, tile_mine, tile_here = tie((terms, tile, tile))
+    total = call(
+        owner_spread,
+        shape((MIDDLE, MIDDLE, TILE_BLOCKS, FULL), BF16),
+        [VMEM] * 4,
+        [
+            pltpu.VMEM((MIDDLE, MIDDLE * TILE_BLOCKS, FULL), F32),
+            pltpu.VMEM((BLOCK, BLOCK * TILE_BLOCKS, FULL), BF16),
+            pltpu.VMEM((9, FULL, FULL), BF16),
+        ],
+        (1, 1), "owner_spread",
+    )(tile_here, swap(tile_mine), second_weight, second_other)
 
     def owner(at_owner):
         at_owner_other = [swap(value) for value in at_owner]
@@ -616,6 +626,7 @@
 
     if permuted:
         far_got, near_got = swap(far, "col"), swap(near, "col")
+        total, far_got = tie((total, far_got))
         sends = call(add_far, [shape(part, BF16)] * 2, [VMEM] * 2, [], (1, 1), "add_far")(
             kept, far_got
         )
@@ -642,24 +653,28 @@
             (1, 1), "column_message",
         )(canvas.reshape(HIGH * WIDE, HALF), got[0], got[2])
         across += [swap(got_2, "col"), swap(last, "col")]
-        early = call(
-            lay, [shape((9, HALF, FULL), F32)] * 2, [VMEM] * 6, [], (1, 1), "lay",
-        )(own, *got, *across[:2])
+        slab = (TILE_ROWS * BLOCK, 16, HALF)
+        weights = [shape((9, HALF, FULL), F32)] * 2
+        early, *outs = call(
+            lay, [shape(grad_out.shape, BF16), shape(slab, F32)] + weights, [VMEM] * 8,
+            [pltpu.VMEM((TILE_ROWS * BLOCK * 32, HALF), F32)], (1, 1), "lay",
+        )(grad_out, canvas, own, *got, *across[:2])
         grad_in, grad_second, grad_first = pl.pallas_call(
             finish,
-            out_shape=[shape(grad_out.shape, BF16)] + [shape((9, HALF, FULL), F32)] * 2,
-            in_specs=[VMEM] * 6 + [HBM] * 2,
-            out_specs=[VMEM] + [HBM] * 2,
+            out_shape=[shape(grad_out.shape, BF16)] + weights,
+            in_specs=[VMEM] * 3 + [HBM] * 3,
+            out_specs=[HBM] * 3,
             scratch_shapes=[
-                pltpu.VMEM((TILE_ROWS * BLOCK * 32, HALF), F32),
+                pltpu.VMEM((TILE_ROWS * BLOCK * 16, HALF), F32),
+                pltpu.VMEM(slab, BF16),
                 pltpu.VMEM((2, 2, 9, ROWS, FULL), F32),
-                pltpu.SemaphoreType.DMA((2, 2)),
+                pltpu.SemaphoreType.DMA((3, 2)),
             ],
-            input_output_aliases={6: 1, 7: 2},
+            input_output_aliases={3: 0, 4: 1, 5: 2},
             compiler_params=pltpu.CompilerParams(vmem_limit_bytes=48 * 1024 * 1024),
             cost_estimate=pl.CostEstimate(flops=1, bytes_accessed=1, transcendentals=0),
             name="finish",
-        )(grad_out, canvas, got[0], got[2], across[3], across[2], *early)
+        )(outs[0], across[3], across[2], early, *outs[1:])
         return (grad_in, grad_first, grad_second)
 
     grad_first, grad_second = lax.psum((terms[0][1], terms[0][0]), ("blk", "col"))

time: 87.5 us -> 87.2 us (level)
  waiting for transfers between devices: 34.2 us -> 38.7 us
  local copies, waits for them, and re-layouts: 3.82 us -> 1.72 us
  starting transfers between devices: 26.3 us -> 24.4 us
    ppermute x12, waiting for transfers between devices: 22.4 us -> 29.6 us  [flip(): return lax.ppermute(value, axis, [(i, i ^ step) for i in range(size)])]
    ppermute x17, waiting for transfers between devices: 11.8 us -> 9.11 us  [swap(): return lax.ppermute(value, axis, [(0, 1), (1, 0)])]
    unnamed x16 -> x12, local copies, waits for them, and re-layouts: 3.81 us -> 1.71 us
    ppermute x17, starting transfers between devices: 7.96 us -> 6.4 us  [swap(): return lax.ppermute(value, axis, [(0, 1), (1, 0)])]
    pallas_call x3 -> x4, Pallas kernels: 7.48 us -> 7.21 us  [the longest x1 2.93 us: shards(): call(owner_spread, shape((MIDDLE, MIDDLE, TILE_BLOCKS, FULL), BF16), [VME...]
  transfers between devices with their start and end apart: 29 -> 29, of which waited for: 13 -> 15; matrix products, arithmetic and copies ran while one was open for 0% -> 0% of each run, Pallas kernels for 23% -> 23%
where the time goes in v15:
time: 87.2 us; the launch traced here: 87 us
  waiting for transfers between devices  38.7 us (44%)
  starting transfers between devices  24.4 us (28%)
  Pallas kernels  21.2 us (24%)
  local copies, waits for them, and re-layouts  1.72 us (2%)
  between operations  0.94 us (1%)
    ppermute x12, waiting for transfers between devices, flip(): return lax.ppermute(value, axis, [(i, i ^ step) for i in range(size)])  29.6 us
    ppermute x12, starting transfers between devices, flip(): return lax.ppermute(value, axis, [(i, i ^ step) for i in range(size)])  18.1 us
    ppermute x17, waiting for transfers between devices, swap(): return lax.ppermute(value, axis, [(0, 1), (1, 0)])  9.11 us
    pallas_call x1, Pallas kernels, shards(): call(functools.partial(worker, scale, owners, columns, capacity, permuted...  6.53 us
    ppermute x17, starting transfers between devices, swap(): return lax.ppermute(value, axis, [(0, 1), (1, 0)])  6.4 us
    pallas_call x1, Pallas kernels, owner(): call(functools.partial(owner_canvas, owners, capacity, wide, permuted), [...  5.8 us
    pallas_call x1, Pallas kernels, shards(): call(owner_spread, shape((MIDDLE, MIDDLE, TILE_BLOCKS, FULL), BF16), [VME...  2.93 us
    pallas_call x1, Pallas kernels, shards(): call(lay, [shape(grad_out.shape, BF16), shape(slab, F32)] + weights, [VME...  1.74 us
  transfers between devices with their start and end apart: 29, of which 15 were waited for; matrix products, arithmetic and copies ran while one was open for 0% of the time, Pallas kernels for 23%

profile of v15, /device:TPU:0, one launch (start us, length us, event | category | flops | bytes accessed | tf_op | source)
XLA Modules:
  0.0 87.0 jit_solution(3720317740571033309)
XLA Ops:
  1.2 1.4 %pack_cotangents.1 = (bf16[8,64,128]{2,1,0:T(8,128)(2,1)S(1)}, bf16[8,64,128]{2,1,0:T(8,128)(2,1)S(1)}, bf16[8,64,128]{2,1,0:T(8,128)(2,1)S(1)}, bf16[8,64,128]{2,1,0:T(8,128)(2,1)S(1)}) custom-call(s32[4,16]{1,0:T(4,128)} %bitcast.17, bf16[8,8,32,128]{3,2,1,0:T(8,128)(2,1)} %bitcast.12), custom_call_target="tpu_custom_call" | custom-call | flops 1 | bytes 1 | tf_op jit(solution)/shard_map/pack_cotangents/pallas_call | solution.py:540
  2.6 4.7 %collective-permute-start = (bf16[8,64,128]{2,1,0:T(8,128)(2,1)S(1)}, bf16[8,64,128]{2,1,0:T(8,128)(2,1)S(1)}, u32[]{:S(2)}, u32[]{:S(2)}) collective-permute-start(bf16[8,64,128]{2,1,0:T(8,128)(2,1)S(1)} %get-tuple-element.67), channel_id=1, source_target_pairs={{0,12},{4,8},{8,4},{12,0},{1,13},{5,9},{9,5},{13,1},{2,14},{6,10},... | collective-permute-start | bytes 393224 | tf_op jit(solution)/shard_map/ppermute | solution.py:508
  9.6 1.6 %pack_saved.1 = (bf16[10,160,128]{2,1,0:T(8,128)(2,1)S(1)}, bf16[10,80,128]{2,1,0:T(8,128)(2,1)S(1)}, bf16[10,80,128]{2,1,0:T(8,128)(2,1)S(1)}, bf16[10,80,128]{2,1,0:T(8,128)(2,1)S(1)}, bf16[10,80,128]{2,1,0:T(8,128)(2,1)S(1)}) custom-call(s32[4,16]{1,0:T(4,128)S(1)} %bitcast.18, bf16[10,160,128]{2,1,0:T(8,128)(2,1)S(1)} %bitcast.16), custom_call_target="tpu_custom_call" | custom-call | flops 1 | bytes 1 | tf_op jit(solution)/shard_map/pack_saved/pallas_call | solution.py:557
  11.8 7.2 %collective-permute-done.1.refs_2_ = bf16[8,64,128]{2,1,0:T(8,128)(2,1)S(1)} collective-permute-done((bf16[8,64,128]{2,1,0:T(8,128)(2,1)S(1)}, bf16[8,64,128]{2,1,0:T(8,128)(2,1)S(1)}, u32[]{:S(2)}, u32[]{:S(2)}) %collective-permute-start.1) | collective-permute-done | bytes 131104 | tf_op jit(solution)/shard_map/ppermute | solution.py:508
  20.5 2.9 %collective-permute-start.11 = (bf16[10,80,128]{2,1,0:T(8,128)(2,1)S(1)}, bf16[10,80,128]{2,1,0:T(8,128)(2,1)S(1)}, u32[]{:S(2)}, u32[]{:S(2)}) collective-permute-start(bf16[10,80,128]{2,1,0:T(8,128)(2,1)S(1)} %get-tuple-element.85), channel_id=1, source_target_pairs={{0,4},{4,0},{8,12},{12,8},{1,5},{5,1},{9,13},{13,9},{2,6},{6,2},{1... | collective-permute-start | bytes 614408 | tf_op jit(solution)/shard_map/ppermute | solution.py:508
  23.4 1.3 %collective-permute-done.6.refs_7_ = bf16[8,64,128]{2,1,0:T(8,128)(2,1)S(1)} collective-permute-done((bf16[8,64,128]{2,1,0:T(8,128)(2,1)S(1)}, bf16[8,64,128]{2,1,0:T(8,128)(2,1)S(1)}, u32[]{:S(2)}, u32[]{:S(2)}) %collective-permute-start.6) | collective-permute-done | bytes 131104 | tf_op jit(solution)/shard_map/ppermute | solution.py:503
  24.8 6.5 %worker.1 = (f32[4,2,9,16,256]{4,3,2,1,0:T(8,128)S(1)}, bf16[2,2,9,16,256]{4,3,2,1,0:T(8,128)(2,1)S(1)}, bf16[2,2,9,16,256]{4,3,2,1,0:T(8,128)(2,1)S(1)}) custom-call(s32[4,16]{1,0:T(4,128)S(1)} %bitcast.19, bf16[8,64,128]{2,1,0:T(8,128)(2,1)S(1)} %get-tuple-element.76.refs_0_, bf16[8,64,128]{2,1,0:T(8,128)(2,1)S(1)} %collective-permute-done.2.refs_1_, ...), custom_call_target="tpu_custom_call" | custom-call | flops 1 | bytes 1 | tf_op jit(solution)/shard_map/worker/pallas_call | solution.py:575
  31.3 1.4 %collective-permute-done.10.refs_2_ = bf16[10,80,128]{2,1,0:T(8,128)(2,1)S(1)} collective-permute-done((bf16[10,80,128]{2,1,0:T(8,128)(2,1)S(1)}, bf16[10,80,128]{2,1,0:T(8,128)(2,1)S(1)}, u32[]{:S(2)}, u32[]{:S(2)}) %collective-permute-start.10) | collective-permute-done | bytes 204832 | tf_op jit(solution)/shard_map/ppermute | solution.py:508
  32.9 1.5 %collective-permute-start.13 = (bf16[2,2,9,16,256]{4,3,2,1,0:T(8,128)(2,1)S(1)}, bf16[2,2,9,16,256]{4,3,2,1,0:T(8,128)(2,1)S(1)}, u32[]{:S(2)}, u32[]{:S(2)}) collective-permute-start(bf16[2,2,9,16,256]{4,3,2,1,0:T(8,128)(2,1)S(1)} %get-tuple-element.92), channel_id=1, source_target_pairs={{0,2},{2,0},{1,3},{3,1},{4,6},{6,4},{5,7},{7,5},{8,10},{10,8},{9,1... | collective-permute-start | bytes 884744 | tf_op jit(solution)/shard_map/ppermute | solution.py:503
  34.4 1.8 %collective-permute-start.14 = (bf16[10,80,128]{2,1,0:T(8,128)(2,1)S(1)}, bf16[10,80,128]{2,1,0:T(8,128)(2,1)S(1)}, u32[]{:S(2)}, u32[]{:S(2)}) collective-permute-start(bf16[10,80,128]{2,1,0:T(8,128)(2,1)S(1)} %get-tuple-element.96), channel_id=1, source_target_pairs={{0,12},{4,8},{8,4},{12,0},{1,13},{5,9},{9,5},{13,1},{2,14},{6,10},... | collective-permute-start | bytes 614408 | tf_op jit(solution)/shard_map/ppermute | solution.py:508
  37.2 2.9 %owner_spread.1.refs_8_ = bf16[10,10,32,256]{3,2,1,0:T(8,128)(2,1)S(1)} custom-call(bf16[8,8,32,128]{3,2,1,0:T(8,128)(2,1)S(1)} %bitcast.14, bf16[8,8,32,128]{3,2,1,0:T(8,128)(2,1)S(1)} %collective-permute-done.12.tile_other, bf16[9,128,256]{2,1,0:T(8,128)(2,1)S(1)} %copy-done.1, bf16[9,128,256]{2,1,0:T(8,128)(2,1)S(1)} %collective-permute-done.8.refs_11_.second_other), custom_call_target="tpu_custom_call" | custom-call | flops 1 | bytes 1 | tf_op jit(solution)/shard_map/owner_spread/pallas_call | solution.py:601
  40.2 2.5 %collective-permute-done.13.got = bf16[2,2,9,16,256]{4,3,2,1,0:T(8,128)(2,1)S(1)} collective-permute-done((bf16[2,2,9,16,256]{4,3,2,1,0:T(8,128)(2,1)S(1)}, bf16[2,2,9,16,256]{4,3,2,1,0:T(8,128)(2,1)S(1)}, u32[]{:S(2)}, u32[]{:S(2)}) %collective-permute-start.13) | collective-permute-done | bytes 294944 | tf_op jit(solution)/shard_map/ppermute | solution.py:503
  43.5 1.8 %collective-permute-start.19 = (bf16[2,9,16,256]{3,2,1,0:T(8,128)(2,1)S(1)}, bf16[2,9,16,256]{3,2,1,0:T(8,128)(2,1)S(1)}, u32[]{:S(2)}, u32[]{:S(2)}) collective-permute-start(bf16[2,9,16,256]{3,2,1,0:T(8,128)(2,1)S(1)} %get-tuple-element.103), channel_id=1, source_target_pairs={{0,12},{4,8},{8,4},{12,0},{1,13},{5,9},{9,5},{13,1},{2,14},{6,10},... | collective-permute-start | bytes 442376 | tf_op jit(solution)/shard_map/ppermute | solution.py:508
  45.3 1.4 %collective-permute-start.20 = (bf16[2,9,16,256]{3,2,1,0:T(8,128)(2,1)S(1)}, bf16[2,9,16,256]{3,2,1,0:T(8,128)(2,1)S(1)}, u32[]{:S(2)}, u32[]{:S(2)}) collective-permute-start(bf16[2,9,16,256]{3,2,1,0:T(8,128)(2,1)S(1)} %get-tuple-element.104), channel_id=1, source_target_pairs={{0,8},{4,12},{8,0},{12,4},{1,9},{5,13},{9,1},{13,5},{2,10},{6,14},... | collective-permute-start | bytes 442376 | tf_op jit(solution)/shard_map/ppermute | solution.py:508
  46.8 5.8 %owner_canvas.1 = (f32[68,40,128]{2,1,0:T(8,128)S(1)}, bf16[48,256]{1,0:T(8,128)(2,1)S(1)}, bf16[48,256]{1,0:T(8,128)(2,1)S(1)}) custom-call(s32[4,16]{1,0:T(4,128)S(1)} %bitcast.20, bf16[10,80,128]{2,1,0:T(8,128)(2,1)S(1)} %get-tuple-element.82.refs_0_, bf16[10,80,128]{2,1,0:T(8,128)(2,1)S(1)} %collective-permute-done.11.refs_1_, ...), custom_call_target="tpu_custom_call" | custom-call | flops 1 | bytes 1 | tf_op jit(solution)/shard_map/owner_canvas/pallas_call | solution.py:615
  52.7 1.2 %collective-permute-start.21 = (bf16[2,9,16,256]{3,2,1,0:T(8,128)(2,1)S(1)}, bf16[2,9,16,256]{3,2,1,0:T(8,128)(2,1)S(1)}, u32[]{:S(2)}, u32[]{:S(2)}) collective-permute-start(bf16[2,9,16,256]{3,2,1,0:T(8,128)(2,1)S(1)} %get-tuple-element.105), channel_id=1, source_target_pairs={{0,4},{4,0},{8,12},{12,8},{1,5},{5,1},{9,13},{13,9},{2,6},{6,2},{1... | collective-permute-start | bytes 442376 | tf_op jit(solution)/shard_map/ppermute | solution.py:508
  53.9 6.7 %collective-permute-done.20.got_2 = bf16[2,9,16,256]{3,2,1,0:T(8,128)(2,1)S(1)} collective-permute-done((bf16[2,9,16,256]{3,2,1,0:T(8,128)(2,1)S(1)}, bf16[2,9,16,256]{3,2,1,0:T(8,128)(2,1)S(1)}, u32[]{:S(2)}, u32[]{:S(2)}) %collective-permute-start.20) | collective-permute-done | bytes 147488 | tf_op jit(solution)/shard_map/ppermute | solution.py:508
  60.6 1.0 %collective-permute-done.21.got_1 = bf16[2,9,16,256]{3,2,1,0:T(8,128)(2,1)S(1)} collective-permute-done((bf16[2,9,16,256]{3,2,1,0:T(8,128)(2,1)S(1)}, bf16[2,9,16,256]{3,2,1,0:T(8,128)(2,1)S(1)}, u32[]{:S(2)}, u32[]{:S(2)}) %collective-permute-start.21) | collective-permute-done | bytes 147488 | tf_op jit(solution)/shard_map/ppermute | solution.py:508
  61.7 2.5 %collective-permute-start.22 = (bf16[336,256]{1,0:T(8,128)(2,1)S(1)}, bf16[336,256]{1,0:T(8,128)(2,1)S(1)}, u32[]{:S(2)}, u32[]{:S(2)}) collective-permute-start(bf16[336,256]{1,0:T(8,128)(2,1)S(1)} %get-tuple-element.109), channel_id=1, source_target_pairs={{0,12},{4,8},{8,4},{12,0},{1,13},{5,9},{9,5},{13,1},{2,14},{6,10},... | collective-permute-start | bytes 516104 | tf_op jit(solution)/shard_map/ppermute | solution.py:508
  65.8 4.0 %collective-permute-done.24.refs_1_.got_1 = bf16[336,256]{1,0:T(8,128)(2,1)S(1)} collective-permute-done((bf16[336,256]{1,0:T(8,128)(2,1)S(1)}, bf16[336,256]{1,0:T(8,128)(2,1)S(1)}, u32[]{:S(2)}, u32[]{:S(2)}) %collective-permute-start.24) | collective-permute-done | bytes 172064 | tf_op jit(solution)/shard_map/ppermute | solution.py:508
  70.5 7.7 %collective-permute-done.23.refs_2_ = bf16[288,256]{1,0:T(8,128)(2,1)S(1)} collective-permute-done((bf16[288,256]{1,0:T(8,128)(2,1)S(1)}, bf16[288,256]{1,0:T(8,128)(2,1)S(1)}, u32[]{:S(2)}, u32[]{:S(2)}) %collective-permute-start.23) | collective-permute-done | bytes 147488 | tf_op jit(solution)/shard_map/ppermute | solution.py:508
  78.6 1.8 %collective-permute-start.28 = (bf16[288,256]{1,0:T(8,128)(2,1)S(1)}, bf16[288,256]{1,0:T(8,128)(2,1)S(1)}, u32[]{:S(2)}, u32[]{:S(2)}) collective-permute-start(bf16[288,256]{1,0:T(8,128)(2,1)S(1)} %collective-permute-done.23.refs_2_), channel_id=1, source_target_pairs={{0,2},{2,0},{1,3},{3,1},{4,6},{6,4},{5,7},{7,5},{8,10},{10,8},{9,1... | collective-permute-start | bytes 442376 | tf_op jit(solution)/shard_map/ppermute | solution.py:503
  80.4 1.7 %lay.1 = (bf16[64,32,128]{2,1,0:T(8,128)(2,1)}, f32[64,16,128]{2,1,0:T(8,128)S(1)}, f32[9,128,256]{2,1,0:T(8,128)}, f32[9,128,256]{2,1,0:T(8,128)}) custom-call(bf16[64,32,128]{2,1,0:T(8,128)(2,1)S(1)} %copy-done, f32[68,40,128]{2,1,0:T(8,128)S(1)} %get-tuple-element.100.canvas, bf16[288,256]{1,0:T(8,128)(2,1)S(1)} %get-tuple-element.108.refs_0_, ...), custom_call_target="tpu_custom_call" | custom-call | flops 1 | bytes 1 | tf_op jit(solution)/shard_map/lay/pallas_call | solution.py:658
  82.1 3.7 %collective-permute-done.28.late = bf16[288,256]{1,0:T(8,128)(2,1)S(1)} collective-permute-done((bf16[288,256]{1,0:T(8,128)(2,1)S(1)}, bf16[288,256]{1,0:T(8,128)(2,1)S(1)}, u32[]{:S(2)}, u32[]{:S(2)}) %collective-permute-start.28) | collective-permute-done | bytes 147488 | tf_op jit(solution)/shard_map/ppermute | solution.py:503
  (58 shorter events, 10.7 us)
Async XLA Ops:
  0.6 24.1 %collective-permute-start.8 = (bf16[9,128,256]{2,1,0:T(8,128)(2,1)}, bf16[9,128,256]{2,1,0:T(8,128)(2,1)S(1)}, u32[]{:S(2)}, u32[]{:S(2)}) collective-permute-start(bf16[9,128,256]{2,1,0:T(8,128)(2,1)} %second.1), channel_id=1, source_target_pairs={{0,1},{1,0},{2,3},{3,2},{4,5},{5,4},{6,7},{7,6},{8,9},{9,8},{10,11... | collective-permute-start | bytes 1769480 | tf_op jit(solution)/shard_map/ppermute | solution.py:503
  2.6 9.2 %collective-permute-start = (bf16[8,64,128]{2,1,0:T(8,128)(2,1)S(1)}, bf16[8,64,128]{2,1,0:T(8,128)(2,1)S(1)}, u32[]{:S(2)}, u32[]{:S(2)}) collective-permute-start(bf16[8,64,128]{2,1,0:T(8,128)(2,1)S(1)} %get-tuple-element.67), channel_id=1, source_target_pairs={{0,12},{4,8},{8,4},{12,0},{1,13},{5,9},{9,5},{13,1},{2,14},{6,10},... | collective-permute-start | bytes 393224 | tf_op jit(solution)/shard_map/ppermute | solution.py:508
  7.3 11.7 %collective-permute-start.1 = (bf16[8,64,128]{2,1,0:T(8,128)(2,1)S(1)}, bf16[8,64,128]{2,1,0:T(8,128)(2,1)S(1)}, u32[]{:S(2)}, u32[]{:S(2)}) collective-permute-start(bf16[8,64,128]{2,1,0:T(8,128)(2,1)S(1)} %get-tuple-element.68), channel_id=1, source_target_pairs={{0,8},{4,12},{8,0},{12,4},{1,9},{5,13},{9,1},{13,5},{2,10},{6,14},... | collective-permute-start | bytes 393224 | tf_op jit(solution)/shard_map/ppermute | solution.py:508
  7.3 11.7 %collective-permute-start.2 = (bf16[8,64,128]{2,1,0:T(8,128)(2,1)S(1)}, bf16[8,64,128]{2,1,0:T(8,128)(2,1)S(1)}, u32[]{:S(2)}, u32[]{:S(2)}) collective-permute-start(bf16[8,64,128]{2,1,0:T(8,128)(2,1)S(1)} %get-tuple-element.69), channel_id=1, source_target_pairs={{0,4},{4,0},{8,12},{12,8},{1,5},{5,1},{9,13},{13,9},{2,6},{6,2},{1... | collective-permute-start | bytes 393224 | tf_op jit(solution)/shard_map/ppermute | solution.py:508
  7.9 16.8 %collective-permute-start.7 = (bf16[10,160,128]{2,1,0:T(8,128)(2,1)}, bf16[10,160,128]{2,1,0:T(8,128)(2,1)S(1)}, u32[]{:S(2)}, u32[]{:S(2)}) collective-permute-start(bf16[10,160,128]{2,1,0:T(8,128)(2,1)} %bitcast.15), channel_id=1, source_target_pairs={{0,1},{1,0},{2,3},{3,2},{4,5},{5,4},{6,7},{7,6},{8,9},{9,8},{10,11... | collective-permute-start | bytes 1228808 | tf_op jit(solution)/shard_map/ppermute | solution.py:503
  19.5 3.9 %collective-permute-start.5 = (bf16[8,64,128]{2,1,0:T(8,128)(2,1)S(1)}, bf16[8,64,128]{2,1,0:T(8,128)(2,1)S(1)}, u32[]{:S(2)}, u32[]{:S(2)}) collective-permute-start(bf16[8,64,128]{2,1,0:T(8,128)(2,1)S(1)} %collective-permute-done.1.refs_2_), channel_id=1, source_target_pairs={{0,1},{1,0},{2,3},{3,2},{4,5},{5,4},{6,7},{7,6},{8,9},{9,8},{10,11... | collective-permute-start | bytes 393224 | tf_op jit(solution)/shard_map/ppermute | solution.py:503
  20.3 12.4 %collective-permute-start.10 = (bf16[10,80,128]{2,1,0:T(8,128)(2,1)S(1)}, bf16[10,80,128]{2,1,0:T(8,128)(2,1)S(1)}, u32[]{:S(2)}, u32[]{:S(2)}) collective-permute-start(bf16[10,80,128]{2,1,0:T(8,128)(2,1)S(1)} %get-tuple-element.84), channel_id=1, source_target_pairs={{0,8},{4,12},{8,0},{12,4},{1,9},{5,13},{9,1},{13,5},{2,10},{6,14},... | collective-permute-start | bytes 614408 | tf_op jit(solution)/shard_map/ppermute | solution.py:508
  20.5 12.3 %collective-permute-start.11 = (bf16[10,80,128]{2,1,0:T(8,128)(2,1)S(1)}, bf16[10,80,128]{2,1,0:T(8,128)(2,1)S(1)}, u32[]{:S(2)}, u32[]{:S(2)}) collective-permute-start(bf16[10,80,128]{2,1,0:T(8,128)(2,1)S(1)} %get-tuple-element.85), channel_id=1, source_target_pairs={{0,4},{4,0},{8,12},{12,8},{1,5},{5,1},{9,13},{13,9},{2,6},{6,2},{1... | collective-permute-start | bytes 614408 | tf_op jit(solution)/shard_map/ppermute | solution.py:508
  32.9 9.8 %collective-permute-start.13 = (bf16[2,2,9,16,256]{4,3,2,1,0:T(8,128)(2,1)S(1)}, bf16[2,2,9,16,256]{4,3,2,1,0:T(8,128)(2,1)S(1)}, u32[]{:S(2)}, u32[]{:S(2)}) collective-permute-start(bf16[2,2,9,16,256]{4,3,2,1,0:T(8,128)(2,1)S(1)} %get-tuple-element.92), channel_id=1, source_target_pairs={{0,2},{2,0},{1,3},{3,1},{4,6},{6,4},{5,7},{7,5},{8,10},{10,8},{9,1... | collective-permute-start | bytes 884744 | tf_op jit(solution)/shard_map/ppermute | solution.py:503
  34.4 9.1 %collective-permute-start.14 = (bf16[10,80,128]{2,1,0:T(8,128)(2,1)S(1)}, bf16[10,80,128]{2,1,0:T(8,128)(2,1)S(1)}, u32[]{:S(2)}, u32[]{:S(2)}) collective-permute-start(bf16[10,80,128]{2,1,0:T(8,128)(2,1)S(1)} %get-tuple-element.96), channel_id=1, source_target_pairs={{0,12},{4,8},{8,4},{12,0},{1,13},{5,9},{9,5},{13,1},{2,14},{6,10},... | collective-permute-start | bytes 614408 | tf_op jit(solution)/shard_map/ppermute | solution.py:508
  36.2 16.4 %collective-permute-start.9 = (bf16[2,2,9,16,256]{4,3,2,1,0:T(8,128)(2,1)S(1)}, bf16[2,2,9,16,256]{4,3,2,1,0:T(8,128)(2,1)S(1)}, u32[]{:S(2)}, u32[]{:S(2)}) collective-permute-start(bf16[2,2,9,16,256]{4,3,2,1,0:T(8,128)(2,1)S(1)} %get-tuple-element.81), channel_id=1, source_target_pairs={{0,2},{2,0},{1,3},{3,1},{4,6},{6,4},{5,7},{7,5},{8,10},{10,8},{9,1... | collective-permute-start | bytes 884744 | tf_op jit(solution)/shard_map/ppermute | solution.py:503
  36.7 6.8 %collective-permute-start.15 = (bf16[10,80,128]{2,1,0:T(8,128)(2,1)S(1)}, bf16[10,80,128]{2,1,0:T(8,128)(2,1)S(1)}, u32[]{:S(2)}, u32[]{:S(2)}) collective-permute-start(bf16[10,80,128]{2,1,0:T(8,128)(2,1)S(1)} %get-tuple-element.82.refs_0_), channel_id=1, source_target_pairs={{0,1},{1,0},{2,3},{3,2},{4,5},{5,4},{6,7},{7,6},{8,9},{9,8},{10,11... | collective-permute-start | bytes 614408 | tf_op jit(solution)/shard_map/ppermute | solution.py:503
  36.7 8.6 %collective-permute-start.16 = (bf16[10,80,128]{2,1,0:T(8,128)(2,1)S(1)}, bf16[10,80,128]{2,1,0:T(8,128)(2,1)S(1)}, u32[]{:S(2)}, u32[]{:S(2)}) collective-permute-start(bf16[10,80,128]{2,1,0:T(8,128)(2,1)S(1)} %collective-permute-done.11.refs_1_), channel_id=1, source_target_pairs={{0,1},{1,0},{2,3},{3,2},{4,5},{5,4},{6,7},{7,6},{8,9},{9,8},{10,11... | collective-permute-start | bytes 614408 | tf_op jit(solution)/shard_map/ppermute | solution.py:503
  42.7 4.1 %collective-permute-start.17 = (bf16[10,80,128]{2,1,0:T(8,128)(2,1)S(1)}, bf16[10,80,128]{2,1,0:T(8,128)(2,1)S(1)}, u32[]{:S(2)}, u32[]{:S(2)}) collective-permute-start(bf16[10,80,128]{2,1,0:T(8,128)(2,1)S(1)} %collective-permute-done.10.refs_2_), channel_id=1, source_target_pairs={{0,1},{1,0},{2,3},{3,2},{4,5},{5,4},{6,7},{7,6},{8,9},{9,8},{10,11... | collective-permute-start | bytes 614408 | tf_op jit(solution)/shard_map/ppermute | solution.py:503
  43.5 10.4 %collective-permute-start.19 = (bf16[2,9,16,256]{3,2,1,0:T(8,128)(2,1)S(1)}, bf16[2,9,16,256]{3,2,1,0:T(8,128)(2,1)S(1)}, u32[]{:S(2)}, u32[]{:S(2)}) collective-permute-start(bf16[2,9,16,256]{3,2,1,0:T(8,128)(2,1)S(1)} %get-tuple-element.103), channel_id=1, source_target_pairs={{0,12},{4,8},{8,4},{12,0},{1,13},{5,9},{9,5},{13,1},{2,14},{6,10},... | collective-permute-start | bytes 442376 | tf_op jit(solution)/shard_map/ppermute | solution.py:508
  45.3 15.3 %collective-permute-start.20 = (bf16[2,9,16,256]{3,2,1,0:T(8,128)(2,1)S(1)}, bf16[2,9,16,256]{3,2,1,0:T(8,128)(2,1)S(1)}, u32[]{:S(2)}, u32[]{:S(2)}) collective-permute-start(bf16[2,9,16,256]{3,2,1,0:T(8,128)(2,1)S(1)} %get-tuple-element.104), channel_id=1, source_target_pairs={{0,8},{4,12},{8,0},{12,4},{1,9},{5,13},{9,1},{13,5},{2,10},{6,14},... | collective-permute-start | bytes 442376 | tf_op jit(solution)/shard_map/ppermute | solution.py:508
  52.7 8.9 %collective-permute-start.21 = (bf16[2,9,16,256]{3,2,1,0:T(8,128)(2,1)S(1)}, bf16[2,9,16,256]{3,2,1,0:T(8,128)(2,1)S(1)}, u32[]{:S(2)}, u32[]{:S(2)}) collective-permute-start(bf16[2,9,16,256]{3,2,1,0:T(8,128)(2,1)S(1)} %get-tuple-element.105), channel_id=1, source_target_pairs={{0,4},{4,0},{8,12},{12,8},{1,5},{5,1},{9,13},{13,9},{2,6},{6,2},{1... | collective-permute-start | bytes 442376 | tf_op jit(solution)/shard_map/ppermute | solution.py:508
  61.7 8.1 %collective-permute-start.24 = (bf16[336,256]{1,0:T(8,128)(2,1)S(1)}, bf16[336,256]{1,0:T(8,128)(2,1)S(1)}, u32[]{:S(2)}, u32[]{:S(2)}) collective-permute-start(bf16[336,256]{1,0:T(8,128)(2,1)S(1)} %get-tuple-element.110), channel_id=1, source_target_pairs={{0,4},{4,0},{8,12},{12,8},{1,5},{5,1},{9,13},{13,9},{2,6},{6,2},{1... | collective-permute-start | bytes 516104 | tf_op jit(solution)/shard_map/ppermute | solution.py:508
  61.7 16.5 %collective-permute-start.22 = (bf16[336,256]{1,0:T(8,128)(2,1)S(1)}, bf16[336,256]{1,0:T(8,128)(2,1)S(1)}, u32[]{:S(2)}, u32[]{:S(2)}) collective-permute-start(bf16[336,256]{1,0:T(8,128)(2,1)S(1)} %get-tuple-element.109), channel_id=1, source_target_pairs={{0,12},{4,8},{8,4},{12,0},{1,13},{5,9},{9,5},{13,1},{2,14},{6,10},... | collective-permute-start | bytes 516104 | tf_op jit(solution)/shard_map/ppermute | solution.py:508
  64.3 6.2 %collective-permute-start.25 = (bf16[288,256]{1,0:T(8,128)(2,1)S(1)}, bf16[288,256]{1,0:T(8,128)(2,1)S(1)}, u32[]{:S(2)}, u32[]{:S(2)}) collective-permute-start(bf16[288,256]{1,0:T(8,128)(2,1)S(1)} %get-tuple-element.108.refs_0_), channel_id=1, source_target_pairs={{0,2},{2,0},{1,3},{3,1},{4,6},{6,4},{5,7},{7,5},{8,10},{10,8},{9,1... | collective-permute-start | bytes 442376 | tf_op jit(solution)/shard_map/ppermute | solution.py:503
  64.8 13.4 %collective-permute-start.23 = (bf16[288,256]{1,0:T(8,128)(2,1)S(1)}, bf16[288,256]{1,0:T(8,128)(2,1)S(1)}, u32[]{:S(2)}, u32[]{:S(2)}) collective-permute-start(bf16[288,256]{1,0:T(8,128)(2,1)S(1)} %get-tuple-element.108.refs_0_), channel_id=1, source_target_pairs={{0,8},{4,12},{8,0},{12,4},{1,9},{5,13},{9,1},{13,5},{2,10},{6,14},... | collective-permute-start | bytes 442376 | tf_op jit(solution)/shard_map/ppermute | solution.py:508
  69.8 8.5 %collective-permute-start.26 = (bf16[288,256]{1,0:T(8,128)(2,1)S(1)}, bf16[288,256]{1,0:T(8,128)(2,1)S(1)}, u32[]{:S(2)}, u32[]{:S(2)}) collective-permute-start(bf16[288,256]{1,0:T(8,128)(2,1)S(1)} %slice.4), channel_id=1, source_target_pairs={{0,2},{2,0},{1,3},{3,1},{4,6},{6,4},{5,7},{7,5},{8,10},{10,8},{9,1... | collective-permute-start | bytes 442376 | tf_op jit(solution)/shard_map/ppermute | solution.py:503
  78.3 7.6 %collective-permute-start.27 = (bf16[352,256]{1,0:T(8,128)(2,1)S(1)}, bf16[352,256]{1,0:T(8,128)(2,1)S(1)}, u32[]{:S(2)}, u32[]{:S(2)}) collective-permute-start(bf16[352,256]{1,0:T(8,128)(2,1)S(1)} %column_message.1), channel_id=1, source_target_pairs={{0,2},{2,0},{1,3},{3,1},{4,6},{6,4},{5,7},{7,5},{8,10},{10,8},{9,1... | collective-permute-start | bytes 540680 | tf_op jit(solution)/shard_map/ppermute | solution.py:503
  78.6 7.3 %collective-permute-start.28 = (bf16[288,256]{1,0:T(8,128)(2,1)S(1)}, bf16[288,256]{1,0:T(8,128)(2,1)S(1)}, u32[]{:S(2)}, u32[]{:S(2)}) collective-permute-start(bf16[288,256]{1,0:T(8,128)(2,1)S(1)} %collective-permute-done.23.refs_2_), channel_id=1, source_target_pairs={{0,2},{2,0},{1,3},{3,1},{4,6},{6,4},{5,7},{7,5},{8,10},{10,8},{9,1... | collective-permute-start | bytes 442376 | tf_op jit(solution)/shard_map/ppermute | solution.py:503
  (11 other events, 58.5 us)

commit v16 on v15

--- a/solution.py
+++ b/solution.py
@@ -278,12 +278,13 @@
         )
         cot[u] = dot(pick, got).astype(BF16)
     grads = cot[...].reshape(BLOCK * rows, FULL)
+    turned = []
+    for dx in range(3):
+        window = masked[:, dx * PER_WORKER : (dx + BLOCK) * PER_WORKER].reshape(MIDDLE * rows, HALF)
+        turned.append(jnp.maximum(window, jnp.zeros_like(window)).T)
+    turned = jnp.concatenate(turned, axis=0)
     for dy in range(3):
-        windows = [
-            masked[dy : dy + BLOCK, dx * PER_WORKER : (dx + BLOCK) * PER_WORKER] for dx in range(3)
-        ]
-        window = jnp.concatenate([w.reshape(BLOCK * rows, HALF) for w in windows], axis=1)
-        value = dot_tn(jnp.maximum(window, jnp.zeros_like(window)), grads) * scale
+        value = dot(turned[:, dy * rows : (dy + BLOCK) * rows], grads) * scale
         for dx in range(3):
             emit(value[dx * HALF : (dx + 1) * HALF], outs, 0, 3 * dy + dx)
     return slots
@@ -398,8 +399,8 @@
         above, below = adjacent(2 * k + 1)
         top = jnp.concatenate([canvas[0], canvas[1]], axis=1)
         bottom = jnp.concatenate([canvas[HIGH - 2], canvas[HIGH - 1]], axis=1)
-        rim[:WIDE] = jnp.where(below, bottom, jnp.where(above, top, 0.0)).astype(BF16)
-        rim[WIDE:] = jnp.zeros((RIM - WIDE, FULL), BF16)
+        here = jnp.where(below, bottom, jnp.where(above, top, 0.0))
+        rim[...] = jnp.concatenate([here, jnp.zeros((RIM - WIDE, FULL), F32)], axis=0).astype(BF16)
 
 
 def add_far(kept, got, *sends):
@@ -484,14 +485,15 @@
                 )
             )
             copies[-1].start()
-    total[...] = slab[...].reshape(total.shape)
+    rows = TILE_ROWS * BLOCK * 16
+    total[:rows] = slab[...].reshape(rows, HALF)
     strip = last[PART:].astype(F32)
     left = lax.axis_index("col") == 0
     at = jnp.where(left, 14, 0)
     for j in range(2):
         spot = (pl.ds(at + j, 64, stride=16), slice(None))
         total[spot] = total[spot] + strip[:, j * HALF : (j + 1) * HALF]
-    side[...] = total[...].astype(BF16).reshape(side.shape)
+    side[...] = total[:rows].astype(BF16).reshape(side.shape)
     columns = pl.ds(pl.multiple_of(jnp.where(left, 16, 0), 16), 16)
     copies.append(pltpu.make_async_copy(side, image.at[:, columns, :], sems.at[2, 0]))
     copies[-1].start()
@@ -665,7 +667,7 @@
             in_specs=[VMEM] * 3 + [HBM] * 3,
             out_specs=[HBM] * 3,
             scratch_shapes=[
-                pltpu.VMEM((TILE_ROWS * BLOCK * 16, HALF), F32),
+                pltpu.VMEM((TILE_ROWS * BLOCK * 16 + 16, HALF), F32),
                 pltpu.VMEM(slab, BF16),
                 pltpu.VMEM((2, 2, 9, ROWS, FULL), F32),
                 pltpu.SemaphoreType.DMA((3, 2)),

time: 87.2 us -> 87.2 us (level)
  no operation moved by 1% of the time
where the time goes in v16:
time: 87.2 us; the launch traced here: 87 us
  waiting for transfers between devices  38.7 us (44%)
  starting transfers between devices  24.4 us (28%)
  Pallas kernels  21.2 us (24%)
  local copies, waits for them, and re-layouts  1.72 us (2%)
  between operations  0.94 us (1%)
    ppermute x12, waiting for transfers between devices, flip(): return lax.ppermute(value, axis, [(i, i ^ step) for i in range(size)])  29.6 us
    ppermute x12, starting transfers between devices, flip(): return lax.ppermute(value, axis, [(i, i ^ step) for i in range(size)])  18.1 us
    ppermute x17, waiting for transfers between devices, swap(): return lax.ppermute(value, axis, [(0, 1), (1, 0)])  9.16 us
    pallas_call x1, Pallas kernels, shards(): call(functools.partial(worker, scale, owners, columns, capacity, permuted...  6.53 us
    ppermute x17, starting transfers between devices, swap(): return lax.ppermute(value, axis, [(0, 1), (1, 0)])  6.34 us
    pallas_call x1, Pallas kernels, owner(): call(functools.partial(owner_canvas, owners, capacity, wide, permuted), [...  5.8 us
    pallas_call x1, Pallas kernels, shards(): call(owner_spread, shape((MIDDLE, MIDDLE, TILE_BLOCKS, FULL), BF16), [VME...  2.93 us
    pallas_call x1, Pallas kernels, shards(): call(lay, [shape(grad_out.shape, BF16), shape(slab, F32)] + weights, [VME...  1.74 us
  transfers between devices with their start and end apart: 29, of which 15 were waited for; matrix products, arithmetic and copies ran while one was open for 0% of the time, Pallas kernels for 23%

profile of v16, /device:TPU:0, one launch (start us, length us, event | category | flops | bytes accessed | tf_op | source)
XLA Modules:
  0.0 87.0 jit_solution(8797051294624135893)
XLA Ops:
  1.2 1.4 %pack_cotangents.1 = (bf16[8,64,128]{2,1,0:T(8,128)(2,1)S(1)}, bf16[8,64,128]{2,1,0:T(8,128)(2,1)S(1)}, bf16[8,64,128]{2,1,0:T(8,128)(2,1)S(1)}, bf16[8,64,128]{2,1,0:T(8,128)(2,1)S(1)}) custom-call(s32[4,16]{1,0:T(4,128)} %bitcast.17, bf16[8,8,32,128]{3,2,1,0:T(8,128)(2,1)} %bitcast.12), custom_call_target="tpu_custom_call" | custom-call | flops 1 | bytes 1 | tf_op jit(solution)/shard_map/pack_cotangents/pallas_call | solution.py:542
  2.6 4.7 %collective-permute-start = (bf16[8,64,128]{2,1,0:T(8,128)(2,1)S(1)}, bf16[8,64,128]{2,1,0:T(8,128)(2,1)S(1)}, u32[]{:S(2)}, u32[]{:S(2)}) collective-permute-start(bf16[8,64,128]{2,1,0:T(8,128)(2,1)S(1)} %get-tuple-element.67), channel_id=1, source_target_pairs={{0,12},{4,8},{8,4},{12,0},{1,13},{5,9},{9,5},{13,1},{2,14},{6,10},... | collective-permute-start | bytes 393224 | tf_op jit(solution)/shard_map/ppermute | solution.py:510
  9.6 1.6 %pack_saved.1 = (bf16[10,160,128]{2,1,0:T(8,128)(2,1)S(1)}, bf16[10,80,128]{2,1,0:T(8,128)(2,1)S(1)}, bf16[10,80,128]{2,1,0:T(8,128)(2,1)S(1)}, bf16[10,80,128]{2,1,0:T(8,128)(2,1)S(1)}, bf16[10,80,128]{2,1,0:T(8,128)(2,1)S(1)}) custom-call(s32[4,16]{1,0:T(4,128)S(1)} %bitcast.18, bf16[10,160,128]{2,1,0:T(8,128)(2,1)S(1)} %bitcast.16), custom_call_target="tpu_custom_call" | custom-call | flops 1 | bytes 1 | tf_op jit(solution)/shard_map/pack_saved/pallas_call | solution.py:559
  11.8 7.2 %collective-permute-done.1.refs_2_ = bf16[8,64,128]{2,1,0:T(8,128)(2,1)S(1)} collective-permute-done((bf16[8,64,128]{2,1,0:T(8,128)(2,1)S(1)}, bf16[8,64,128]{2,1,0:T(8,128)(2,1)S(1)}, u32[]{:S(2)}, u32[]{:S(2)}) %collective-permute-start.1) | collective-permute-done | bytes 131104 | tf_op jit(solution)/shard_map/ppermute | solution.py:510
  20.5 2.9 %collective-permute-start.11 = (bf16[10,80,128]{2,1,0:T(8,128)(2,1)S(1)}, bf16[10,80,128]{2,1,0:T(8,128)(2,1)S(1)}, u32[]{:S(2)}, u32[]{:S(2)}) collective-permute-start(bf16[10,80,128]{2,1,0:T(8,128)(2,1)S(1)} %get-tuple-element.85), channel_id=1, source_target_pairs={{0,4},{4,0},{8,12},{12,8},{1,5},{5,1},{9,13},{13,9},{2,6},{6,2},{1... | collective-permute-start | bytes 614408 | tf_op jit(solution)/shard_map/ppermute | solution.py:510
  23.4 1.3 %collective-permute-done.6.refs_7_ = bf16[8,64,128]{2,1,0:T(8,128)(2,1)S(1)} collective-permute-done((bf16[8,64,128]{2,1,0:T(8,128)(2,1)S(1)}, bf16[8,64,128]{2,1,0:T(8,128)(2,1)S(1)}, u32[]{:S(2)}, u32[]{:S(2)}) %collective-permute-start.6) | collective-permute-done | bytes 131104 | tf_op jit(solution)/shard_map/ppermute | solution.py:505
  24.8 6.5 %worker.1 = (f32[4,2,9,16,256]{4,3,2,1,0:T(8,128)S(1)}, bf16[2,2,9,16,256]{4,3,2,1,0:T(8,128)(2,1)S(1)}, bf16[2,2,9,16,256]{4,3,2,1,0:T(8,128)(2,1)S(1)}) custom-call(s32[4,16]{1,0:T(4,128)S(1)} %bitcast.19, bf16[8,64,128]{2,1,0:T(8,128)(2,1)S(1)} %get-tuple-element.76.refs_0_, bf16[8,64,128]{2,1,0:T(8,128)(2,1)S(1)} %collective-permute-done.2.refs_1_, ...), custom_call_target="tpu_custom_call" | custom-call | flops 1 | bytes 1 | tf_op jit(solution)/shard_map/worker/pallas_call | solution.py:577
  31.3 1.4 %collective-permute-done.10.refs_2_ = bf16[10,80,128]{2,1,0:T(8,128)(2,1)S(1)} collective-permute-done((bf16[10,80,128]{2,1,0:T(8,128)(2,1)S(1)}, bf16[10,80,128]{2,1,0:T(8,128)(2,1)S(1)}, u32[]{:S(2)}, u32[]{:S(2)}) %collective-permute-start.10) | collective-permute-done | bytes 204832 | tf_op jit(solution)/shard_map/ppermute | solution.py:510
  32.9 1.5 %collective-permute-start.13 = (bf16[2,2,9,16,256]{4,3,2,1,0:T(8,128)(2,1)S(1)}, bf16[2,2,9,16,256]{4,3,2,1,0:T(8,128)(2,1)S(1)}, u32[]{:S(2)}, u32[]{:S(2)}) collective-permute-start(bf16[2,2,9,16,256]{4,3,2,1,0:T(8,128)(2,1)S(1)} %get-tuple-element.92), channel_id=1, source_target_pairs={{0,2},{2,0},{1,3},{3,1},{4,6},{6,4},{5,7},{7,5},{8,10},{10,8},{9,1... | collective-permute-start | bytes 884744 | tf_op jit(solution)/shard_map/ppermute | solution.py:505
  34.4 1.8 %collective-permute-start.14 = (bf16[10,80,128]{2,1,0:T(8,128)(2,1)S(1)}, bf16[10,80,128]{2,1,0:T(8,128)(2,1)S(1)}, u32[]{:S(2)}, u32[]{:S(2)}) collective-permute-start(bf16[10,80,128]{2,1,0:T(8,128)(2,1)S(1)} %get-tuple-element.96), channel_id=1, source_target_pairs={{0,12},{4,8},{8,4},{12,0},{1,13},{5,9},{9,5},{13,1},{2,14},{6,10},... | collective-permute-start | bytes 614408 | tf_op jit(solution)/shard_map/ppermute | solution.py:510
  37.2 2.9 %owner_spread.1.refs_8_ = bf16[10,10,32,256]{3,2,1,0:T(8,128)(2,1)S(1)} custom-call(bf16[8,8,32,128]{3,2,1,0:T(8,128)(2,1)S(1)} %bitcast.14, bf16[8,8,32,128]{3,2,1,0:T(8,128)(2,1)S(1)} %collective-permute-done.12.tile_other, bf16[9,128,256]{2,1,0:T(8,128)(2,1)S(1)} %copy-done.1, bf16[9,128,256]{2,1,0:T(8,128)(2,1)S(1)} %collective-permute-done.8.refs_11_.second_other), custom_call_target="tpu_custom_call" | custom-call | flops 1 | bytes 1 | tf_op jit(solution)/shard_map/owner_spread/pallas_call | solution.py:603
  40.2 2.5 %collective-permute-done.13.got = bf16[2,2,9,16,256]{4,3,2,1,0:T(8,128)(2,1)S(1)} collective-permute-done((bf16[2,2,9,16,256]{4,3,2,1,0:T(8,128)(2,1)S(1)}, bf16[2,2,9,16,256]{4,3,2,1,0:T(8,128)(2,1)S(1)}, u32[]{:S(2)}, u32[]{:S(2)}) %collective-permute-start.13) | collective-permute-done | bytes 294944 | tf_op jit(solution)/shard_map/ppermute | solution.py:505
  43.5 1.8 %collective-permute-start.19 = (bf16[2,9,16,256]{3,2,1,0:T(8,128)(2,1)S(1)}, bf16[2,9,16,256]{3,2,1,0:T(8,128)(2,1)S(1)}, u32[]{:S(2)}, u32[]{:S(2)}) collective-permute-start(bf16[2,9,16,256]{3,2,1,0:T(8,128)(2,1)S(1)} %get-tuple-element.103), channel_id=1, source_target_pairs={{0,12},{4,8},{8,4},{12,0},{1,13},{5,9},{9,5},{13,1},{2,14},{6,10},... | collective-permute-start | bytes 442376 | tf_op jit(solution)/shard_map/ppermute | solution.py:510
  45.3 1.4 %collective-permute-start.20 = (bf16[2,9,16,256]{3,2,1,0:T(8,128)(2,1)S(1)}, bf16[2,9,16,256]{3,2,1,0:T(8,128)(2,1)S(1)}, u32[]{:S(2)}, u32[]{:S(2)}) collective-permute-start(bf16[2,9,16,256]{3,2,1,0:T(8,128)(2,1)S(1)} %get-tuple-element.104), channel_id=1, source_target_pairs={{0,8},{4,12},{8,0},{12,4},{1,9},{5,13},{9,1},{13,5},{2,10},{6,14},... | collective-permute-start | bytes 442376 | tf_op jit(solution)/shard_map/ppermute | solution.py:510
  46.8 5.8 %owner_canvas.1 = (f32[68,40,128]{2,1,0:T(8,128)S(1)}, bf16[48,256]{1,0:T(8,128)(2,1)S(1)}, bf16[48,256]{1,0:T(8,128)(2,1)S(1)}) custom-call(s32[4,16]{1,0:T(4,128)S(1)} %bitcast.20, bf16[10,80,128]{2,1,0:T(8,128)(2,1)S(1)} %get-tuple-element.82.refs_0_, bf16[10,80,128]{2,1,0:T(8,128)(2,1)S(1)} %collective-permute-done.11.refs_1_, ...), custom_call_target="tpu_custom_call" | custom-call | flops 1 | bytes 1 | tf_op jit(solution)/shard_map/owner_canvas/pallas_call | solution.py:617
  52.7 1.2 %collective-permute-start.21 = (bf16[2,9,16,256]{3,2,1,0:T(8,128)(2,1)S(1)}, bf16[2,9,16,256]{3,2,1,0:T(8,128)(2,1)S(1)}, u32[]{:S(2)}, u32[]{:S(2)}) collective-permute-start(bf16[2,9,16,256]{3,2,1,0:T(8,128)(2,1)S(1)} %get-tuple-element.105), channel_id=1, source_target_pairs={{0,4},{4,0},{8,12},{12,8},{1,5},{5,1},{9,13},{13,9},{2,6},{6,2},{1... | collective-permute-start | bytes 442376 | tf_op jit(solution)/shard_map/ppermute | solution.py:510
  53.9 6.7 %collective-permute-done.20.got_2 = bf16[2,9,16,256]{3,2,1,0:T(8,128)(2,1)S(1)} collective-permute-done((bf16[2,9,16,256]{3,2,1,0:T(8,128)(2,1)S(1)}, bf16[2,9,16,256]{3,2,1,0:T(8,128)(2,1)S(1)}, u32[]{:S(2)}, u32[]{:S(2)}) %collective-permute-start.20) | collective-permute-done | bytes 147488 | tf_op jit(solution)/shard_map/ppermute | solution.py:510
  60.6 1.0 %collective-permute-done.21.got_1 = bf16[2,9,16,256]{3,2,1,0:T(8,128)(2,1)S(1)} collective-permute-done((bf16[2,9,16,256]{3,2,1,0:T(8,128)(2,1)S(1)}, bf16[2,9,16,256]{3,2,1,0:T(8,128)(2,1)S(1)}, u32[]{:S(2)}, u32[]{:S(2)}) %collective-permute-start.21) | collective-permute-done | bytes 147488 | tf_op jit(solution)/shard_map/ppermute | solution.py:510
  61.7 2.5 %collective-permute-start.22 = (bf16[336,256]{1,0:T(8,128)(2,1)S(1)}, bf16[336,256]{1,0:T(8,128)(2,1)S(1)}, u32[]{:S(2)}, u32[]{:S(2)}) collective-permute-start(bf16[336,256]{1,0:T(8,128)(2,1)S(1)} %get-tuple-element.109), channel_id=1, source_target_pairs={{0,12},{4,8},{8,4},{12,0},{1,13},{5,9},{9,5},{13,1},{2,14},{6,10},... | collective-permute-start | bytes 516104 | tf_op jit(solution)/shard_map/ppermute | solution.py:510
  65.8 4.0 %collective-permute-done.24.refs_1_.got_1 = bf16[336,256]{1,0:T(8,128)(2,1)S(1)} collective-permute-done((bf16[336,256]{1,0:T(8,128)(2,1)S(1)}, bf16[336,256]{1,0:T(8,128)(2,1)S(1)}, u32[]{:S(2)}, u32[]{:S(2)}) %collective-permute-start.24) | collective-permute-done | bytes 172064 | tf_op jit(solution)/shard_map/ppermute | solution.py:510
  70.5 7.8 %collective-permute-done.23.refs_2_ = bf16[288,256]{1,0:T(8,128)(2,1)S(1)} collective-permute-done((bf16[288,256]{1,0:T(8,128)(2,1)S(1)}, bf16[288,256]{1,0:T(8,128)(2,1)S(1)}, u32[]{:S(2)}, u32[]{:S(2)}) %collective-permute-start.23) | collective-permute-done | bytes 147488 | tf_op jit(solution)/shard_map/ppermute | solution.py:510
  79.0 1.4 %collective-permute-start.28 = (bf16[288,256]{1,0:T(8,128)(2,1)S(1)}, bf16[288,256]{1,0:T(8,128)(2,1)S(1)}, u32[]{:S(2)}, u32[]{:S(2)}) collective-permute-start(bf16[288,256]{1,0:T(8,128)(2,1)S(1)} %collective-permute-done.23.refs_2_), channel_id=1, source_target_pairs={{0,2},{2,0},{1,3},{3,1},{4,6},{6,4},{5,7},{7,5},{8,10},{10,8},{9,1... | collective-permute-start | bytes 442376 | tf_op jit(solution)/shard_map/ppermute | solution.py:505
  80.4 1.7 %lay.1 = (bf16[64,32,128]{2,1,0:T(8,128)(2,1)}, f32[64,16,128]{2,1,0:T(8,128)S(1)}, f32[9,128,256]{2,1,0:T(8,128)}, f32[9,128,256]{2,1,0:T(8,128)}) custom-call(bf16[64,32,128]{2,1,0:T(8,128)(2,1)S(1)} %copy-done, f32[68,40,128]{2,1,0:T(8,128)S(1)} %get-tuple-element.100.canvas, bf16[288,256]{1,0:T(8,128)(2,1)S(1)} %get-tuple-element.108.refs_0_, ...), custom_call_target="tpu_custom_call" | custom-call | flops 1 | bytes 1 | tf_op jit(solution)/shard_map/lay/pallas_call | solution.py:660
  82.1 3.7 %collective-permute-done.28.late = bf16[288,256]{1,0:T(8,128)(2,1)S(1)} collective-permute-done((bf16[288,256]{1,0:T(8,128)(2,1)S(1)}, bf16[288,256]{1,0:T(8,128)(2,1)S(1)}, u32[]{:S(2)}, u32[]{:S(2)}) %collective-permute-start.28) | collective-permute-done | bytes 147488 | tf_op jit(solution)/shard_map/ppermute | solution.py:505
  (58 shorter events, 11.1 us)
Async XLA Ops:
  0.6 24.1 %collective-permute-start.8 = (bf16[9,128,256]{2,1,0:T(8,128)(2,1)}, bf16[9,128,256]{2,1,0:T(8,128)(2,1)S(1)}, u32[]{:S(2)}, u32[]{:S(2)}) collective-permute-start(bf16[9,128,256]{2,1,0:T(8,128)(2,1)} %second.1), channel_id=1, source_target_pairs={{0,1},{1,0},{2,3},{3,2},{4,5},{5,4},{6,7},{7,6},{8,9},{9,8},{10,11... | collective-permute-start | bytes 1769480 | tf_op jit(solution)/shard_map/ppermute | solution.py:505
  2.6 9.2 %collective-permute-start = (bf16[8,64,128]{2,1,0:T(8,128)(2,1)S(1)}, bf16[8,64,128]{2,1,0:T(8,128)(2,1)S(1)}, u32[]{:S(2)}, u32[]{:S(2)}) collective-permute-start(bf16[8,64,128]{2,1,0:T(8,128)(2,1)S(1)} %get-tuple-element.67), channel_id=1, source_target_pairs={{0,12},{4,8},{8,4},{12,0},{1,13},{5,9},{9,5},{13,1},{2,14},{6,10},... | collective-permute-start | bytes 393224 | tf_op jit(solution)/shard_map/ppermute | solution.py:510
  7.3 11.7 %collective-permute-start.1 = (bf16[8,64,128]{2,1,0:T(8,128)(2,1)S(1)}, bf16[8,64,128]{2,1,0:T(8,128)(2,1)S(1)}, u32[]{:S(2)}, u32[]{:S(2)}) collective-permute-start(bf16[8,64,128]{2,1,0:T(8,128)(2,1)S(1)} %get-tuple-element.68), channel_id=1, source_target_pairs={{0,8},{4,12},{8,0},{12,4},{1,9},{5,13},{9,1},{13,5},{2,10},{6,14},... | collective-permute-start | bytes 393224 | tf_op jit(solution)/shard_map/ppermute | solution.py:510
  7.3 11.7 %collective-permute-start.2 = (bf16[8,64,128]{2,1,0:T(8,128)(2,1)S(1)}, bf16[8,64,128]{2,1,0:T(8,128)(2,1)S(1)}, u32[]{:S(2)}, u32[]{:S(2)}) collective-permute-start(bf16[8,64,128]{2,1,0:T(8,128)(2,1)S(1)} %get-tuple-element.69), channel_id=1, source_target_pairs={{0,4},{4,0},{8,12},{12,8},{1,5},{5,1},{9,13},{13,9},{2,6},{6,2},{1... | collective-permute-start | bytes 393224 | tf_op jit(solution)/shard_map/ppermute | solution.py:510
  7.9 16.8 %collective-permute-start.7 = (bf16[10,160,128]{2,1,0:T(8,128)(2,1)}, bf16[10,160,128]{2,1,0:T(8,128)(2,1)S(1)}, u32[]{:S(2)}, u32[]{:S(2)}) collective-permute-start(bf16[10,160,128]{2,1,0:T(8,128)(2,1)} %bitcast.15), channel_id=1, source_target_pairs={{0,1},{1,0},{2,3},{3,2},{4,5},{5,4},{6,7},{7,6},{8,9},{9,8},{10,11... | collective-permute-start | bytes 1228808 | tf_op jit(solution)/shard_map/ppermute | solution.py:505
  19.5 3.9 %collective-permute-start.5 = (bf16[8,64,128]{2,1,0:T(8,128)(2,1)S(1)}, bf16[8,64,128]{2,1,0:T(8,128)(2,1)S(1)}, u32[]{:S(2)}, u32[]{:S(2)}) collective-permute-start(bf16[8,64,128]{2,1,0:T(8,128)(2,1)S(1)} %collective-permute-done.1.refs_2_), channel_id=1, source_target_pairs={{0,1},{1,0},{2,3},{3,2},{4,5},{5,4},{6,7},{7,6},{8,9},{9,8},{10,11... | collective-permute-start | bytes 393224 | tf_op jit(solution)/shard_map/ppermute | solution.py:505
  20.3 12.4 %collective-permute-start.10 = (bf16[10,80,128]{2,1,0:T(8,128)(2,1)S(1)}, bf16[10,80,128]{2,1,0:T(8,128)(2,1)S(1)}, u32[]{:S(2)}, u32[]{:S(2)}) collective-permute-start(bf16[10,80,128]{2,1,0:T(8,128)(2,1)S(1)} %get-tuple-element.84), channel_id=1, source_target_pairs={{0,8},{4,12},{8,0},{12,4},{1,9},{5,13},{9,1},{13,5},{2,10},{6,14},... | collective-permute-start | bytes 614408 | tf_op jit(solution)/shard_map/ppermute | solution.py:510
  20.5 12.3 %collective-permute-start.11 = (bf16[10,80,128]{2,1,0:T(8,128)(2,1)S(1)}, bf16[10,80,128]{2,1,0:T(8,128)(2,1)S(1)}, u32[]{:S(2)}, u32[]{:S(2)}) collective-permute-start(bf16[10,80,128]{2,1,0:T(8,128)(2,1)S(1)} %get-tuple-element.85), channel_id=1, source_target_pairs={{0,4},{4,0},{8,12},{12,8},{1,5},{5,1},{9,13},{13,9},{2,6},{6,2},{1... | collective-permute-start | bytes 614408 | tf_op jit(solution)/shard_map/ppermute | solution.py:510
  32.9 9.8 %collective-permute-start.13 = (bf16[2,2,9,16,256]{4,3,2,1,0:T(8,128)(2,1)S(1)}, bf16[2,2,9,16,256]{4,3,2,1,0:T(8,128)(2,1)S(1)}, u32[]{:S(2)}, u32[]{:S(2)}) collective-permute-start(bf16[2,2,9,16,256]{4,3,2,1,0:T(8,128)(2,1)S(1)} %get-tuple-element.92), channel_id=1, source_target_pairs={{0,2},{2,0},{1,3},{3,1},{4,6},{6,4},{5,7},{7,5},{8,10},{10,8},{9,1... | collective-permute-start | bytes 884744 | tf_op jit(solution)/shard_map/ppermute | solution.py:505
  34.4 9.1 %collective-permute-start.14 = (bf16[10,80,128]{2,1,0:T(8,128)(2,1)S(1)}, bf16[10,80,128]{2,1,0:T(8,128)(2,1)S(1)}, u32[]{:S(2)}, u32[]{:S(2)}) collective-permute-start(bf16[10,80,128]{2,1,0:T(8,128)(2,1)S(1)} %get-tuple-element.96), channel_id=1, source_target_pairs={{0,12},{4,8},{8,4},{12,0},{1,13},{5,9},{9,5},{13,1},{2,14},{6,10},... | collective-permute-start | bytes 614408 | tf_op jit(solution)/shard_map/ppermute | solution.py:510
  36.2 16.4 %collective-permute-start.9 = (bf16[2,2,9,16,256]{4,3,2,1,0:T(8,128)(2,1)S(1)}, bf16[2,2,9,16,256]{4,3,2,1,0:T(8,128)(2,1)S(1)}, u32[]{:S(2)}, u32[]{:S(2)}) collective-permute-start(bf16[2,2,9,16,256]{4,3,2,1,0:T(8,128)(2,1)S(1)} %get-tuple-element.81), channel_id=1, source_target_pairs={{0,2},{2,0},{1,3},{3,1},{4,6},{6,4},{5,7},{7,5},{8,10},{10,8},{9,1... | collective-permute-start | bytes 884744 | tf_op jit(solution)/shard_map/ppermute | solution.py:505
  36.7 6.8 %collective-permute-start.15 = (bf16[10,80,128]{2,1,0:T(8,128)(2,1)S(1)}, bf16[10,80,128]{2,1,0:T(8,128)(2,1)S(1)}, u32[]{:S(2)}, u32[]{:S(2)}) collective-permute-start(bf16[10,80,128]{2,1,0:T(8,128)(2,1)S(1)} %get-tuple-element.82.refs_0_), channel_id=1, source_target_pairs={{0,1},{1,0},{2,3},{3,2},{4,5},{5,4},{6,7},{7,6},{8,9},{9,8},{10,11... | collective-permute-start | bytes 614408 | tf_op jit(solution)/shard_map/ppermute | solution.py:505
  36.7 8.6 %collective-permute-start.16 = (bf16[10,80,128]{2,1,0:T(8,128)(2,1)S(1)}, bf16[10,80,128]{2,1,0:T(8,128)(2,1)S(1)}, u32[]{:S(2)}, u32[]{:S(2)}) collective-permute-start(bf16[10,80,128]{2,1,0:T(8,128)(2,1)S(1)} %collective-permute-done.11.refs_1_), channel_id=1, source_target_pairs={{0,1},{1,0},{2,3},{3,2},{4,5},{5,4},{6,7},{7,6},{8,9},{9,8},{10,11... | collective-permute-start | bytes 614408 | tf_op jit(solution)/shard_map/ppermute | solution.py:505
  42.7 4.1 %collective-permute-start.17 = (bf16[10,80,128]{2,1,0:T(8,128)(2,1)S(1)}, bf16[10,80,128]{2,1,0:T(8,128)(2,1)S(1)}, u32[]{:S(2)}, u32[]{:S(2)}) collective-permute-start(bf16[10,80,128]{2,1,0:T(8,128)(2,1)S(1)} %collective-permute-done.10.refs_2_), channel_id=1, source_target_pairs={{0,1},{1,0},{2,3},{3,2},{4,5},{5,4},{6,7},{7,6},{8,9},{9,8},{10,11... | collective-permute-start | bytes 614408 | tf_op jit(solution)/shard_map/ppermute | solution.py:505
  43.5 10.4 %collective-permute-start.19 = (bf16[2,9,16,256]{3,2,1,0:T(8,128)(2,1)S(1)}, bf16[2,9,16,256]{3,2,1,0:T(8,128)(2,1)S(1)}, u32[]{:S(2)}, u32[]{:S(2)}) collective-permute-start(bf16[2,9,16,256]{3,2,1,0:T(8,128)(2,1)S(1)} %get-tuple-element.103), channel_id=1, source_target_pairs={{0,12},{4,8},{8,4},{12,0},{1,13},{5,9},{9,5},{13,1},{2,14},{6,10},... | collective-permute-start | bytes 442376 | tf_op jit(solution)/shard_map/ppermute | solution.py:510
  45.3 15.3 %collective-permute-start.20 = (bf16[2,9,16,256]{3,2,1,0:T(8,128)(2,1)S(1)}, bf16[2,9,16,256]{3,2,1,0:T(8,128)(2,1)S(1)}, u32[]{:S(2)}, u32[]{:S(2)}) collective-permute-start(bf16[2,9,16,256]{3,2,1,0:T(8,128)(2,1)S(1)} %get-tuple-element.104), channel_id=1, source_target_pairs={{0,8},{4,12},{8,0},{12,4},{1,9},{5,13},{9,1},{13,5},{2,10},{6,14},... | collective-permute-start | bytes 442376 | tf_op jit(solution)/shard_map/ppermute | solution.py:510
  52.7 8.9 %collective-permute-start.21 = (bf16[2,9,16,256]{3,2,1,0:T(8,128)(2,1)S(1)}, bf16[2,9,16,256]{3,2,1,0:T(8,128)(2,1)S(1)}, u32[]{:S(2)}, u32[]{:S(2)}) collective-permute-start(bf16[2,9,16,256]{3,2,1,0:T(8,128)(2,1)S(1)} %get-tuple-element.105), channel_id=1, source_target_pairs={{0,4},{4,0},{8,12},{12,8},{1,5},{5,1},{9,13},{13,9},{2,6},{6,2},{1... | collective-permute-start | bytes 442376 | tf_op jit(solution)/shard_map/ppermute | solution.py:510
  61.7 8.1 %collective-permute-start.24 = (bf16[336,256]{1,0:T(8,128)(2,1)S(1)}, bf16[336,256]{1,0:T(8,128)(2,1)S(1)}, u32[]{:S(2)}, u32[]{:S(2)}) collective-permute-start(bf16[336,256]{1,0:T(8,128)(2,1)S(1)} %get-tuple-element.110), channel_id=1, source_target_pairs={{0,4},{4,0},{8,12},{12,8},{1,5},{5,1},{9,13},{13,9},{2,6},{6,2},{1... | collective-permute-start | bytes 516104 | tf_op jit(solution)/shard_map/ppermute | solution.py:510
  61.7 16.5 %collective-permute-start.22 = (bf16[336,256]{1,0:T(8,128)(2,1)S(1)}, bf16[336,256]{1,0:T(8,128)(2,1)S(1)}, u32[]{:S(2)}, u32[]{:S(2)}) collective-permute-start(bf16[336,256]{1,0:T(8,128)(2,1)S(1)} %get-tuple-element.109), channel_id=1, source_target_pairs={{0,12},{4,8},{8,4},{12,0},{1,13},{5,9},{9,5},{13,1},{2,14},{6,10},... | collective-permute-start | bytes 516104 | tf_op jit(solution)/shard_map/ppermute | solution.py:510
  64.3 6.2 %collective-permute-start.25 = (bf16[288,256]{1,0:T(8,128)(2,1)S(1)}, bf16[288,256]{1,0:T(8,128)(2,1)S(1)}, u32[]{:S(2)}, u32[]{:S(2)}) collective-permute-start(bf16[288,256]{1,0:T(8,128)(2,1)S(1)} %get-tuple-element.108.refs_0_), channel_id=1, source_target_pairs={{0,2},{2,0},{1,3},{3,1},{4,6},{6,4},{5,7},{7,5},{8,10},{10,8},{9,1... | collective-permute-start | bytes 442376 | tf_op jit(solution)/shard_map/ppermute | solution.py:505
  64.8 13.4 %collective-permute-start.23 = (bf16[288,256]{1,0:T(8,128)(2,1)S(1)}, bf16[288,256]{1,0:T(8,128)(2,1)S(1)}, u32[]{:S(2)}, u32[]{:S(2)}) collective-permute-start(bf16[288,256]{1,0:T(8,128)(2,1)S(1)} %get-tuple-element.108.refs_0_), channel_id=1, source_target_pairs={{0,8},{4,12},{8,0},{12,4},{1,9},{5,13},{9,1},{13,5},{2,10},{6,14},... | collective-permute-start | bytes 442376 | tf_op jit(solution)/shard_map/ppermute | solution.py:510
  69.8 8.5 %collective-permute-start.26 = (bf16[288,256]{1,0:T(8,128)(2,1)S(1)}, bf16[288,256]{1,0:T(8,128)(2,1)S(1)}, u32[]{:S(2)}, u32[]{:S(2)}) collective-permute-start(bf16[288,256]{1,0:T(8,128)(2,1)S(1)} %slice.4), channel_id=1, source_target_pairs={{0,2},{2,0},{1,3},{3,1},{4,6},{6,4},{5,7},{7,5},{8,10},{10,8},{9,1... | collective-permute-start | bytes 442376 | tf_op jit(solution)/shard_map/ppermute | solution.py:505
  78.3 7.6 %collective-permute-start.27 = (bf16[352,256]{1,0:T(8,128)(2,1)S(1)}, bf16[352,256]{1,0:T(8,128)(2,1)S(1)}, u32[]{:S(2)}, u32[]{:S(2)}) collective-permute-start(bf16[352,256]{1,0:T(8,128)(2,1)S(1)} %column_message.1), channel_id=1, source_target_pairs={{0,2},{2,0},{1,3},{3,1},{4,6},{6,4},{5,7},{7,5},{8,10},{10,8},{9,1... | collective-permute-start | bytes 540680 | tf_op jit(solution)/shard_map/ppermute | solution.py:505
  79.0 6.9 %collective-permute-start.28 = (bf16[288,256]{1,0:T(8,128)(2,1)S(1)}, bf16[288,256]{1,0:T(8,128)(2,1)S(1)}, u32[]{:S(2)}, u32[]{:S(2)}) collective-permute-start(bf16[288,256]{1,0:T(8,128)(2,1)S(1)} %collective-permute-done.23.refs_2_), channel_id=1, source_target_pairs={{0,2},{2,0},{1,3},{3,1},{4,6},{6,4},{5,7},{7,5},{8,10},{10,8},{9,1... | collective-permute-start | bytes 442376 | tf_op jit(solution)/shard_map/ppermute | solution.py:505
  (11 other events, 58.5 us)

commit v17 on v16

--- a/solution.py
+++ b/solution.py
@@ -468,23 +468,20 @@
     whole = total[...].reshape(image.shape)
     image[...] = whole.astype(BF16)
     slab[...] = jnp.where(lax.axis_index("col") == 0, whole[:, 16:], whole[:, :16])
-    for number, part in enumerate(parts):
+    for number, part in zip((0, 1, 2, 3, 4, 5, 6), parts):
         value = part[:PART].astype(F32).reshape(2, 9, ROWS, FULL)
         for out, grad in zip(outs, (0, 1)):
             out[:, rows_at(number), :] = value[grad]
 
 
-def finish(slab, last, late, old, old_0, old_1, image, out_0, out_1, total, side, laid, sems):
+def finish(slab, last, old, old_0, old_1, image, out_0, out_1, total, side, laid, sems):
     copies = []
-    for k, (number, part) in enumerate(((6, late), (7, last))):
-        laid[k] = part[:PART].astype(F32).reshape(2, 9, ROWS, FULL)
-        for grad, dest in enumerate((out_0, out_1)):
-            copies.append(
-                pltpu.make_async_copy(
-                    laid.at[k, grad], dest.at[:, rows_at(number), :], sems.at[k, grad]
-                )
-            )
-            copies[-1].start()
+    laid[...] = last[:PART].astype(F32).reshape(2, 9, ROWS, FULL)
+    for grad, dest in enumerate((out_0, out_1)):
+        copies.append(
+            pltpu.make_async_copy(laid.at[grad], dest.at[:, rows_at(7), :], sems.at[grad])
+        )
+        copies[-1].start()
     rows = TILE_ROWS * BLOCK * 16
     total[:rows] = slab[...].reshape(rows, HALF)
     strip = last[PART:].astype(F32)
@@ -495,7 +492,7 @@
         total[spot] = total[spot] + strip[:, j * HALF : (j + 1) * HALF]
     side[...] = total[:rows].astype(BF16).reshape(side.shape)
     columns = pl.ds(pl.multiple_of(jnp.where(left, 16, 0), 16), 16)
-    copies.append(pltpu.make_async_copy(side, image.at[:, columns, :], sems.at[2, 0]))
+    copies.append(pltpu.make_async_copy(side, image.at[:, columns, :], sems.at[2]))
     copies[-1].start()
     for copy in copies:
         copy.wait()
@@ -645,38 +642,40 @@
         own, *wides = call(
             add_workers, [message, wider, wider], [VMEM] * 6, [], (1, 1), "add_workers",
         )(keep, *got, *rims)
-        got_2, got_3, got_1 = flip(own, "blk", 2), flip(wides[1], "blk", 3), flip(wides[0], "blk", 1)
-        across = [swap(value, "col") for value in (own, got_1[:PART])]
-        got_3, got_2, got_1, across = tie((got_3, got_2, got_1, across))
+        got_2, got_1 = flip(own, "blk", 2), flip(wides[0], "blk", 1)
+        wide_3, got_2, across = tie((wides[1], got_2, swap(own, "col")))
+        got_3 = flip(wide_3, "blk", 3)
+        across = [across] + [swap(value, "col") for value in (got_1[:PART], got_2)]
+        got_3, got_1, across = tie((got_3, got_1, across))
         got = [got_1, got_2, got_3]
         last = call(
             column_message, shape((PART + 64, FULL), BF16), [VMEM] * 3,
             [pltpu.VMEM((RIM, FULL), F32), pltpu.VMEM((64, HALF), F32)],
             (1, 1), "column_message",
         )(canvas.reshape(HIGH * WIDE, HALF), got[0], got[2])
-        across += [swap(got_2, "col"), swap(last, "col")]
+        last = swap(last, "col")
         slab = (TILE_ROWS * BLOCK, 16, HALF)
         weights = [shape((9, HALF, FULL), F32)] * 2
         early, *outs = call(
-            lay, [shape(grad_out.shape, BF16), shape(slab, F32)] + weights, [VMEM] * 8,
+            lay, [shape(grad_out.shape, BF16), shape(slab, F32)] + weights, [VMEM] * 9,
             [pltpu.VMEM((TILE_ROWS * BLOCK * 32, HALF), F32)], (1, 1), "lay",
-        )(grad_out, canvas, own, *got, *across[:2])
+        )(grad_out, canvas, own, *got, *across)
         grad_in, grad_second, grad_first = pl.pallas_call(
             finish,
             out_shape=[shape(grad_out.shape, BF16)] + weights,
-            in_specs=[VMEM] * 3 + [HBM] * 3,
+            in_specs=[VMEM] * 2 + [HBM] * 3,
             out_specs=[HBM] * 3,
             scratch_shapes=[
                 pltpu.VMEM((TILE_ROWS * BLOCK * 16 + 16, HALF), F32),
                 pltpu.VMEM(slab, BF16),
-                pltpu.VMEM((2, 2, 9, ROWS, FULL), F32),
-                pltpu.SemaphoreType.DMA((3, 2)),
+                pltpu.VMEM((2, 9, ROWS, FULL), F32),
+                pltpu.SemaphoreType.DMA((3,)),
             ],
-            input_output_aliases={3: 0, 4: 1, 5: 2},
+            input_output_aliases={2: 0, 3: 1, 4: 2},
             compiler_params=pltpu.CompilerParams(vmem_limit_bytes=48 * 1024 * 1024),
             cost_estimate=pl.CostEstimate(flops=1, bytes_accessed=1, transcendentals=0),
             name="finish",
-        )(outs[0], across[3], across[2], early, *outs[1:])
+        )(outs[0], last, early, *outs[1:])
         return (grad_in, grad_first, grad_second)
 
     grad_first, grad_second = lax.psum((terms[0][1], terms[0][0]), ("blk", "col"))

time: 87.2 us -> 85.7 us (0.983)
  waiting for transfers between devices: 38.7 us -> 35.5 us
  starting transfers between devices: 24.4 us -> 26.3 us
    ppermute x12, waiting for transfers between devices: 29.6 us -> 22.8 us  [flip(): return lax.ppermute(value, axis, [(i, i ^ step) for i in range(size)])]
    ppermute x17, waiting for transfers between devices: 9.16 us -> 12.7 us  [swap(): return lax.ppermute(value, axis, [(0, 1), (1, 0)])]
    ppermute x17, starting transfers between devices: 6.34 us -> 7.55 us  [swap(): return lax.ppermute(value, axis, [(0, 1), (1, 0)])]
  transfers between devices with their start and end apart: 29 -> 29, of which waited for: 15 -> 17; matrix products, arithmetic and copies ran while one was open for 0% -> 0% of each run, Pallas kernels for 23% -> 24%
where the time goes in v17:
time: 85.7 us; the launch traced here: 85.5 us
  waiting for transfers between devices  35.5 us (41%)
  starting transfers between devices  26.3 us (31%)
  Pallas kernels  21.1 us (25%)
  local copies, waits for them, and re-layouts  1.72 us (2%)
  between operations  0.93 us (1%)
    ppermute x12, waiting for transfers between devices, flip(): return lax.ppermute(value, axis, [(i, i ^ step) for i in range(size)])  22.8 us
    ppermute x12, starting transfers between devices, flip(): return lax.ppermute(value, axis, [(i, i ^ step) for i in range(size)])  18.8 us
    ppermute x17, waiting for transfers between devices, swap(): return lax.ppermute(value, axis, [(0, 1), (1, 0)])  12.7 us
    ppermute x17, starting transfers between devices, swap(): return lax.ppermute(value, axis, [(0, 1), (1, 0)])  7.55 us
    pallas_call x1, Pallas kernels, shards(): call(functools.partial(worker, scale, owners, columns, capacity, permuted...  6.53 us
    pallas_call x1, Pallas kernels, owner(): call(functools.partial(owner_canvas, owners, capacity, wide, permuted), [...  5.8 us
    pallas_call x1, Pallas kernels, shards(): call(owner_spread, shape((MIDDLE, MIDDLE, TILE_BLOCKS, FULL), BF16), [VME...  2.93 us
    pallas_call x1, Pallas kernels, shards(): call(lay, [shape(grad_out.shape, BF16), shape(slab, F32)] + weights, [VME...  1.76 us
  transfers between devices with their start and end apart: 29, of which 17 were waited for; matrix products, arithmetic and copies ran while one was open for 0% of the time, Pallas kernels for 24%

profile of v17, /device:TPU:0, one launch (start us, length us, event | category | flops | bytes accessed | tf_op | source)
XLA Modules:
  0.0 85.5 jit_solution(7864530567959844687)
XLA Ops:
  1.2 1.4 %pack_cotangents.1 = (bf16[8,64,128]{2,1,0:T(8,128)(2,1)S(1)}, bf16[8,64,128]{2,1,0:T(8,128)(2,1)S(1)}, bf16[8,64,128]{2,1,0:T(8,128)(2,1)S(1)}, bf16[8,64,128]{2,1,0:T(8,128)(2,1)S(1)}) custom-call(s32[4,16]{1,0:T(4,128)} %bitcast.17, bf16[8,8,32,128]{3,2,1,0:T(8,128)(2,1)} %bitcast.12), custom_call_target="tpu_custom_call" | custom-call | flops 1 | bytes 1 | tf_op jit(solution)/shard_map/pack_cotangents/pallas_call | solution.py:539
  2.6 4.7 %collective-permute-start = (bf16[8,64,128]{2,1,0:T(8,128)(2,1)S(1)}, bf16[8,64,128]{2,1,0:T(8,128)(2,1)S(1)}, u32[]{:S(2)}, u32[]{:S(2)}) collective-permute-start(bf16[8,64,128]{2,1,0:T(8,128)(2,1)S(1)} %get-tuple-element.70), channel_id=1, source_target_pairs={{0,12},{4,8},{8,4},{12,0},{1,13},{5,9},{9,5},{13,1},{2,14},{6,10},... | collective-permute-start | bytes 393224 | tf_op jit(solution)/shard_map/ppermute | solution.py:507
  9.6 1.6 %pack_saved.1 = (bf16[10,160,128]{2,1,0:T(8,128)(2,1)S(1)}, bf16[10,80,128]{2,1,0:T(8,128)(2,1)S(1)}, bf16[10,80,128]{2,1,0:T(8,128)(2,1)S(1)}, bf16[10,80,128]{2,1,0:T(8,128)(2,1)S(1)}, bf16[10,80,128]{2,1,0:T(8,128)(2,1)S(1)}) custom-call(s32[4,16]{1,0:T(4,128)S(1)} %bitcast.18, bf16[10,160,128]{2,1,0:T(8,128)(2,1)S(1)} %bitcast.16), custom_call_target="tpu_custom_call" | custom-call | flops 1 | bytes 1 | tf_op jit(solution)/shard_map/pack_saved/pallas_call | solution.py:556
  11.8 7.2 %collective-permute-done.1.refs_2_ = bf16[8,64,128]{2,1,0:T(8,128)(2,1)S(1)} collective-permute-done((bf16[8,64,128]{2,1,0:T(8,128)(2,1)S(1)}, bf16[8,64,128]{2,1,0:T(8,128)(2,1)S(1)}, u32[]{:S(2)}, u32[]{:S(2)}) %collective-permute-start.1) | collective-permute-done | bytes 131104 | tf_op jit(solution)/shard_map/ppermute | solution.py:507
  20.5 2.9 %collective-permute-start.11 = (bf16[10,80,128]{2,1,0:T(8,128)(2,1)S(1)}, bf16[10,80,128]{2,1,0:T(8,128)(2,1)S(1)}, u32[]{:S(2)}, u32[]{:S(2)}) collective-permute-start(bf16[10,80,128]{2,1,0:T(8,128)(2,1)S(1)} %get-tuple-element.88), channel_id=1, source_target_pairs={{0,4},{4,0},{8,12},{12,8},{1,5},{5,1},{9,13},{13,9},{2,6},{6,2},{1... | collective-permute-start | bytes 614408 | tf_op jit(solution)/shard_map/ppermute | solution.py:507
  23.4 1.3 %collective-permute-done.6.refs_7_ = bf16[8,64,128]{2,1,0:T(8,128)(2,1)S(1)} collective-permute-done((bf16[8,64,128]{2,1,0:T(8,128)(2,1)S(1)}, bf16[8,64,128]{2,1,0:T(8,128)(2,1)S(1)}, u32[]{:S(2)}, u32[]{:S(2)}) %collective-permute-start.6) | collective-permute-done | bytes 131104 | tf_op jit(solution)/shard_map/ppermute | solution.py:502
  24.8 6.5 %worker.1 = (f32[4,2,9,16,256]{4,3,2,1,0:T(8,128)S(1)}, bf16[2,2,9,16,256]{4,3,2,1,0:T(8,128)(2,1)S(1)}, bf16[2,2,9,16,256]{4,3,2,1,0:T(8,128)(2,1)S(1)}) custom-call(s32[4,16]{1,0:T(4,128)S(1)} %bitcast.19, bf16[8,64,128]{2,1,0:T(8,128)(2,1)S(1)} %get-tuple-element.79.refs_0_, bf16[8,64,128]{2,1,0:T(8,128)(2,1)S(1)} %collective-permute-done.2.refs_1_, ...), custom_call_target="tpu_custom_call" | custom-call | flops 1 | bytes 1 | tf_op jit(solution)/shard_map/worker/pallas_call | solution.py:574
  31.3 1.4 %collective-permute-done.10.refs_2_ = bf16[10,80,128]{2,1,0:T(8,128)(2,1)S(1)} collective-permute-done((bf16[10,80,128]{2,1,0:T(8,128)(2,1)S(1)}, bf16[10,80,128]{2,1,0:T(8,128)(2,1)S(1)}, u32[]{:S(2)}, u32[]{:S(2)}) %collective-permute-start.10) | collective-permute-done | bytes 204832 | tf_op jit(solution)/shard_map/ppermute | solution.py:507
  32.9 1.5 %collective-permute-start.13 = (bf16[2,2,9,16,256]{4,3,2,1,0:T(8,128)(2,1)S(1)}, bf16[2,2,9,16,256]{4,3,2,1,0:T(8,128)(2,1)S(1)}, u32[]{:S(2)}, u32[]{:S(2)}) collective-permute-start(bf16[2,2,9,16,256]{4,3,2,1,0:T(8,128)(2,1)S(1)} %get-tuple-element.95), channel_id=1, source_target_pairs={{0,2},{2,0},{1,3},{3,1},{4,6},{6,4},{5,7},{7,5},{8,10},{10,8},{9,1... | collective-permute-start | bytes 884744 | tf_op jit(solution)/shard_map/ppermute | solution.py:502
  34.4 1.8 %collective-permute-start.14 = (bf16[10,80,128]{2,1,0:T(8,128)(2,1)S(1)}, bf16[10,80,128]{2,1,0:T(8,128)(2,1)S(1)}, u32[]{:S(2)}, u32[]{:S(2)}) collective-permute-start(bf16[10,80,128]{2,1,0:T(8,128)(2,1)S(1)} %get-tuple-element.99), channel_id=1, source_target_pairs={{0,12},{4,8},{8,4},{12,0},{1,13},{5,9},{9,5},{13,1},{2,14},{6,10},... | collective-permute-start | bytes 614408 | tf_op jit(solution)/shard_map/ppermute | solution.py:507
  37.2 2.9 %owner_spread.1.refs_8_ = bf16[10,10,32,256]{3,2,1,0:T(8,128)(2,1)S(1)} custom-call(bf16[8,8,32,128]{3,2,1,0:T(8,128)(2,1)S(1)} %bitcast.14, bf16[8,8,32,128]{3,2,1,0:T(8,128)(2,1)S(1)} %collective-permute-done.12.tile_other, bf16[9,128,256]{2,1,0:T(8,128)(2,1)S(1)} %copy-done.1, bf16[9,128,256]{2,1,0:T(8,128)(2,1)S(1)} %collective-permute-done.8.refs_11_.second_other), custom_call_target="tpu_custom_call" | custom-call | flops 1 | bytes 1 | tf_op jit(solution)/shard_map/owner_spread/pallas_call | solution.py:600
  40.2 2.5 %collective-permute-done.13.got = bf16[2,2,9,16,256]{4,3,2,1,0:T(8,128)(2,1)S(1)} collective-permute-done((bf16[2,2,9,16,256]{4,3,2,1,0:T(8,128)(2,1)S(1)}, bf16[2,2,9,16,256]{4,3,2,1,0:T(8,128)(2,1)S(1)}, u32[]{:S(2)}, u32[]{:S(2)}) %collective-permute-start.13) | collective-permute-done | bytes 294944 | tf_op jit(solution)/shard_map/ppermute | solution.py:502
  43.5 1.8 %collective-permute-start.19 = (bf16[2,9,16,256]{3,2,1,0:T(8,128)(2,1)S(1)}, bf16[2,9,16,256]{3,2,1,0:T(8,128)(2,1)S(1)}, u32[]{:S(2)}, u32[]{:S(2)}) collective-permute-start(bf16[2,9,16,256]{3,2,1,0:T(8,128)(2,1)S(1)} %get-tuple-element.106), channel_id=1, source_target_pairs={{0,12},{4,8},{8,4},{12,0},{1,13},{5,9},{9,5},{13,1},{2,14},{6,10},... | collective-permute-start | bytes 442376 | tf_op jit(solution)/shard_map/ppermute | solution.py:507
  45.3 1.4 %collective-permute-start.20 = (bf16[2,9,16,256]{3,2,1,0:T(8,128)(2,1)S(1)}, bf16[2,9,16,256]{3,2,1,0:T(8,128)(2,1)S(1)}, u32[]{:S(2)}, u32[]{:S(2)}) collective-permute-start(bf16[2,9,16,256]{3,2,1,0:T(8,128)(2,1)S(1)} %get-tuple-element.107), channel_id=1, source_target_pairs={{0,8},{4,12},{8,0},{12,4},{1,9},{5,13},{9,1},{13,5},{2,10},{6,14},... | collective-permute-start | bytes 442376 | tf_op jit(solution)/shard_map/ppermute | solution.py:507
  46.8 5.8 %owner_canvas.1 = (f32[68,40,128]{2,1,0:T(8,128)S(1)}, bf16[48,256]{1,0:T(8,128)(2,1)S(1)}, bf16[48,256]{1,0:T(8,128)(2,1)S(1)}) custom-call(s32[4,16]{1,0:T(4,128)S(1)} %bitcast.20, bf16[10,80,128]{2,1,0:T(8,128)(2,1)S(1)} %get-tuple-element.85.refs_0_, bf16[10,80,128]{2,1,0:T(8,128)(2,1)S(1)} %collective-permute-done.11.refs_1_, ...), custom_call_target="tpu_custom_call" | custom-call | flops 1 | bytes 1 | tf_op jit(solution)/shard_map/owner_canvas/pallas_call | solution.py:614
  53.9 6.7 %collective-permute-done.20.got_2 = bf16[2,9,16,256]{3,2,1,0:T(8,128)(2,1)S(1)} collective-permute-done((bf16[2,9,16,256]{3,2,1,0:T(8,128)(2,1)S(1)}, bf16[2,9,16,256]{3,2,1,0:T(8,128)(2,1)S(1)}, u32[]{:S(2)}, u32[]{:S(2)}) %collective-permute-start.20) | collective-permute-done | bytes 147488 | tf_op jit(solution)/shard_map/ppermute | solution.py:507
  62.8 2.5 %collective-permute-start.25 = (bf16[336,256]{1,0:T(8,128)(2,1)S(1)}, bf16[336,256]{1,0:T(8,128)(2,1)S(1)}, u32[]{:S(2)}, u32[]{:S(2)}) collective-permute-start(bf16[336,256]{1,0:T(8,128)(2,1)S(1)} %get-tuple-element.114), channel_id=1, source_target_pairs={{0,4},{4,0},{8,12},{12,8},{1,5},{5,1},{9,13},{13,9},{2,6},{6,2},{1... | collective-permute-start | bytes 516104 | tf_op jit(solution)/shard_map/ppermute | solution.py:507
  65.3 1.6 %collective-permute-done.23.refs_4_ = bf16[288,256]{1,0:T(8,128)(2,1)S(1)} collective-permute-done((bf16[288,256]{1,0:T(8,128)(2,1)S(1)}, bf16[288,256]{1,0:T(8,128)(2,1)S(1)}, u32[]{:S(2)}, u32[]{:S(2)}) %collective-permute-start.23) | collective-permute-done | bytes 147488 | tf_op jit(solution)/shard_map/ppermute | solution.py:502
  66.9 4.0 %collective-permute-done.22.refs_2_ = bf16[288,256]{1,0:T(8,128)(2,1)S(1)} collective-permute-done((bf16[288,256]{1,0:T(8,128)(2,1)S(1)}, bf16[288,256]{1,0:T(8,128)(2,1)S(1)}, u32[]{:S(2)}, u32[]{:S(2)}) %collective-permute-start.22) | collective-permute-done | bytes 147488 | tf_op jit(solution)/shard_map/ppermute | solution.py:507
  72.1 1.3 %collective-permute-start.27 = (bf16[288,256]{1,0:T(8,128)(2,1)S(1)}, bf16[288,256]{1,0:T(8,128)(2,1)S(1)}, u32[]{:S(2)}, u32[]{:S(2)}) collective-permute-start(bf16[288,256]{1,0:T(8,128)(2,1)S(1)} %collective-permute-done.22.refs_2_), channel_id=1, source_target_pairs={{0,2},{2,0},{1,3},{3,1},{4,6},{6,4},{5,7},{7,5},{8,10},{10,8},{9,1... | collective-permute-start | bytes 442376 | tf_op jit(solution)/shard_map/ppermute | solution.py:502
  74.2 3.0 %collective-permute-done.27.refs_6_ = bf16[288,256]{1,0:T(8,128)(2,1)S(1)} collective-permute-done((bf16[288,256]{1,0:T(8,128)(2,1)S(1)}, bf16[288,256]{1,0:T(8,128)(2,1)S(1)}, u32[]{:S(2)}, u32[]{:S(2)}) %collective-permute-start.27) | collective-permute-done | bytes 147488 | tf_op jit(solution)/shard_map/ppermute | solution.py:502
  79.0 1.3 %collective-permute-start.28 = (bf16[352,256]{1,0:T(8,128)(2,1)S(1)}, bf16[352,256]{1,0:T(8,128)(2,1)S(1)}, u32[]{:S(2)}, u32[]{:S(2)}) collective-permute-start(bf16[352,256]{1,0:T(8,128)(2,1)S(1)} %column_message.1), channel_id=1, source_target_pairs={{0,2},{2,0},{1,3},{3,1},{4,6},{6,4},{5,7},{7,5},{8,10},{10,8},{9,1... | collective-permute-start | bytes 540680 | tf_op jit(solution)/shard_map/ppermute | solution.py:502
  80.2 1.8 %lay.1 = (bf16[64,32,128]{2,1,0:T(8,128)(2,1)}, f32[64,16,128]{2,1,0:T(8,128)S(1)}, f32[9,128,256]{2,1,0:T(8,128)}, f32[9,128,256]{2,1,0:T(8,128)}) custom-call(bf16[64,32,128]{2,1,0:T(8,128)(2,1)S(1)} %copy-done, f32[68,40,128]{2,1,0:T(8,128)S(1)} %get-tuple-element.103.canvas, bf16[288,256]{1,0:T(8,128)(2,1)S(1)} %get-tuple-element.111.refs_0_, ...), custom_call_target="tpu_custom_call" | custom-call | flops 1 | bytes 1 | tf_op jit(solution)/shard_map/lay/pallas_call | solution.py:659
  82.0 2.5 %collective-permute-done.28.last = bf16[352,256]{1,0:T(8,128)(2,1)S(1)} collective-permute-done((bf16[352,256]{1,0:T(8,128)(2,1)S(1)}, bf16[352,256]{1,0:T(8,128)(2,1)S(1)}, u32[]{:S(2)}, u32[]{:S(2)}) %collective-permute-start.28) | collective-permute-done | bytes 180256 | tf_op jit(solution)/shard_map/ppermute | solution.py:502
  (58 shorter events, 15.1 us)
Async XLA Ops:
  0.6 24.1 %collective-permute-start.8 = (bf16[9,128,256]{2,1,0:T(8,128)(2,1)}, bf16[9,128,256]{2,1,0:T(8,128)(2,1)S(1)}, u32[]{:S(2)}, u32[]{:S(2)}) collective-permute-start(bf16[9,128,256]{2,1,0:T(8,128)(2,1)} %second.1), channel_id=1, source_target_pairs={{0,1},{1,0},{2,3},{3,2},{4,5},{5,4},{6,7},{7,6},{8,9},{9,8},{10,11... | collective-permute-start | bytes 1769480 | tf_op jit(solution)/shard_map/ppermute | solution.py:502
  2.6 9.2 %collective-permute-start = (bf16[8,64,128]{2,1,0:T(8,128)(2,1)S(1)}, bf16[8,64,128]{2,1,0:T(8,128)(2,1)S(1)}, u32[]{:S(2)}, u32[]{:S(2)}) collective-permute-start(bf16[8,64,128]{2,1,0:T(8,128)(2,1)S(1)} %get-tuple-element.70), channel_id=1, source_target_pairs={{0,12},{4,8},{8,4},{12,0},{1,13},{5,9},{9,5},{13,1},{2,14},{6,10},... | collective-permute-start | bytes 393224 | tf_op jit(solution)/shard_map/ppermute | solution.py:507
  7.3 11.7 %collective-permute-start.1 = (bf16[8,64,128]{2,1,0:T(8,128)(2,1)S(1)}, bf16[8,64,128]{2,1,0:T(8,128)(2,1)S(1)}, u32[]{:S(2)}, u32[]{:S(2)}) collective-permute-start(bf16[8,64,128]{2,1,0:T(8,128)(2,1)S(1)} %get-tuple-element.71), channel_id=1, source_target_pairs={{0,8},{4,12},{8,0},{12,4},{1,9},{5,13},{9,1},{13,5},{2,10},{6,14},... | collective-permute-start | bytes 393224 | tf_op jit(solution)/shard_map/ppermute | solution.py:507
  7.3 11.7 %collective-permute-start.2 = (bf16[8,64,128]{2,1,0:T(8,128)(2,1)S(1)}, bf16[8,64,128]{2,1,0:T(8,128)(2,1)S(1)}, u32[]{:S(2)}, u32[]{:S(2)}) collective-permute-start(bf16[8,64,128]{2,1,0:T(8,128)(2,1)S(1)} %get-tuple-element.72), channel_id=1, source_target_pairs={{0,4},{4,0},{8,12},{12,8},{1,5},{5,1},{9,13},{13,9},{2,6},{6,2},{1... | collective-permute-start | bytes 393224 | tf_op jit(solution)/shard_map/ppermute | solution.py:507
  7.9 16.8 %collective-permute-start.7 = (bf16[10,160,128]{2,1,0:T(8,128)(2,1)}, bf16[10,160,128]{2,1,0:T(8,128)(2,1)S(1)}, u32[]{:S(2)}, u32[]{:S(2)}) collective-permute-start(bf16[10,160,128]{2,1,0:T(8,128)(2,1)} %bitcast.15), channel_id=1, source_target_pairs={{0,1},{1,0},{2,3},{3,2},{4,5},{5,4},{6,7},{7,6},{8,9},{9,8},{10,11... | collective-permute-start | bytes 1228808 | tf_op jit(solution)/shard_map/ppermute | solution.py:502
  19.5 3.9 %collective-permute-start.5 = (bf16[8,64,128]{2,1,0:T(8,128)(2,1)S(1)}, bf16[8,64,128]{2,1,0:T(8,128)(2,1)S(1)}, u32[]{:S(2)}, u32[]{:S(2)}) collective-permute-start(bf16[8,64,128]{2,1,0:T(8,128)(2,1)S(1)} %collective-permute-done.1.refs_2_), channel_id=1, source_target_pairs={{0,1},{1,0},{2,3},{3,2},{4,5},{5,4},{6,7},{7,6},{8,9},{9,8},{10,11... | collective-permute-start | bytes 393224 | tf_op jit(solution)/shard_map/ppermute | solution.py:502
  20.3 12.4 %collective-permute-start.10 = (bf16[10,80,128]{2,1,0:T(8,128)(2,1)S(1)}, bf16[10,80,128]{2,1,0:T(8,128)(2,1)S(1)}, u32[]{:S(2)}, u32[]{:S(2)}) collective-permute-start(bf16[10,80,128]{2,1,0:T(8,128)(2,1)S(1)} %get-tuple-element.87), channel_id=1, source_target_pairs={{0,8},{4,12},{8,0},{12,4},{1,9},{5,13},{9,1},{13,5},{2,10},{6,14},... | collective-permute-start | bytes 614408 | tf_op jit(solution)/shard_map/ppermute | solution.py:507
  20.5 12.3 %collective-permute-start.11 = (bf16[10,80,128]{2,1,0:T(8,128)(2,1)S(1)}, bf16[10,80,128]{2,1,0:T(8,128)(2,1)S(1)}, u32[]{:S(2)}, u32[]{:S(2)}) collective-permute-start(bf16[10,80,128]{2,1,0:T(8,128)(2,1)S(1)} %get-tuple-element.88), channel_id=1, source_target_pairs={{0,4},{4,0},{8,12},{12,8},{1,5},{5,1},{9,13},{13,9},{2,6},{6,2},{1... | collective-permute-start | bytes 614408 | tf_op jit(solution)/shard_map/ppermute | solution.py:507
  32.9 9.8 %collective-permute-start.13 = (bf16[2,2,9,16,256]{4,3,2,1,0:T(8,128)(2,1)S(1)}, bf16[2,2,9,16,256]{4,3,2,1,0:T(8,128)(2,1)S(1)}, u32[]{:S(2)}, u32[]{:S(2)}) collective-permute-start(bf16[2,2,9,16,256]{4,3,2,1,0:T(8,128)(2,1)S(1)} %get-tuple-element.95), channel_id=1, source_target_pairs={{0,2},{2,0},{1,3},{3,1},{4,6},{6,4},{5,7},{7,5},{8,10},{10,8},{9,1... | collective-permute-start | bytes 884744 | tf_op jit(solution)/shard_map/ppermute | solution.py:502
  34.4 9.1 %collective-permute-start.14 = (bf16[10,80,128]{2,1,0:T(8,128)(2,1)S(1)}, bf16[10,80,128]{2,1,0:T(8,128)(2,1)S(1)}, u32[]{:S(2)}, u32[]{:S(2)}) collective-permute-start(bf16[10,80,128]{2,1,0:T(8,128)(2,1)S(1)} %get-tuple-element.99), channel_id=1, source_target_pairs={{0,12},{4,8},{8,4},{12,0},{1,13},{5,9},{9,5},{13,1},{2,14},{6,10},... | collective-permute-start | bytes 614408 | tf_op jit(solution)/shard_map/ppermute | solution.py:507
  36.2 16.4 %collective-permute-start.9 = (bf16[2,2,9,16,256]{4,3,2,1,0:T(8,128)(2,1)S(1)}, bf16[2,2,9,16,256]{4,3,2,1,0:T(8,128)(2,1)S(1)}, u32[]{:S(2)}, u32[]{:S(2)}) collective-permute-start(bf16[2,2,9,16,256]{4,3,2,1,0:T(8,128)(2,1)S(1)} %get-tuple-element.84), channel_id=1, source_target_pairs={{0,2},{2,0},{1,3},{3,1},{4,6},{6,4},{5,7},{7,5},{8,10},{10,8},{9,1... | collective-permute-start | bytes 884744 | tf_op jit(solution)/shard_map/ppermute | solution.py:502
  36.7 6.8 %collective-permute-start.15 = (bf16[10,80,128]{2,1,0:T(8,128)(2,1)S(1)}, bf16[10,80,128]{2,1,0:T(8,128)(2,1)S(1)}, u32[]{:S(2)}, u32[]{:S(2)}) collective-permute-start(bf16[10,80,128]{2,1,0:T(8,128)(2,1)S(1)} %get-tuple-element.85.refs_0_), channel_id=1, source_target_pairs={{0,1},{1,0},{2,3},{3,2},{4,5},{5,4},{6,7},{7,6},{8,9},{9,8},{10,11... | collective-permute-start | bytes 614408 | tf_op jit(solution)/shard_map/ppermute | solution.py:502
  36.7 8.6 %collective-permute-start.16 = (bf16[10,80,128]{2,1,0:T(8,128)(2,1)S(1)}, bf16[10,80,128]{2,1,0:T(8,128)(2,1)S(1)}, u32[]{:S(2)}, u32[]{:S(2)}) collective-permute-start(bf16[10,80,128]{2,1,0:T(8,128)(2,1)S(1)} %collective-permute-done.11.refs_1_), channel_id=1, source_target_pairs={{0,1},{1,0},{2,3},{3,2},{4,5},{5,4},{6,7},{7,6},{8,9},{9,8},{10,11... | collective-permute-start | bytes 614408 | tf_op jit(solution)/shard_map/ppermute | solution.py:502
  42.7 4.1 %collective-permute-start.17 = (bf16[10,80,128]{2,1,0:T(8,128)(2,1)S(1)}, bf16[10,80,128]{2,1,0:T(8,128)(2,1)S(1)}, u32[]{:S(2)}, u32[]{:S(2)}) collective-permute-start(bf16[10,80,128]{2,1,0:T(8,128)(2,1)S(1)} %collective-permute-done.10.refs_2_), channel_id=1, source_target_pairs={{0,1},{1,0},{2,3},{3,2},{4,5},{5,4},{6,7},{7,6},{8,9},{9,8},{10,11... | collective-permute-start | bytes 614408 | tf_op jit(solution)/shard_map/ppermute | solution.py:502
  43.5 10.4 %collective-permute-start.19 = (bf16[2,9,16,256]{3,2,1,0:T(8,128)(2,1)S(1)}, bf16[2,9,16,256]{3,2,1,0:T(8,128)(2,1)S(1)}, u32[]{:S(2)}, u32[]{:S(2)}) collective-permute-start(bf16[2,9,16,256]{3,2,1,0:T(8,128)(2,1)S(1)} %get-tuple-element.106), channel_id=1, source_target_pairs={{0,12},{4,8},{8,4},{12,0},{1,13},{5,9},{9,5},{13,1},{2,14},{6,10},... | collective-permute-start | bytes 442376 | tf_op jit(solution)/shard_map/ppermute | solution.py:507
  45.3 15.3 %collective-permute-start.20 = (bf16[2,9,16,256]{3,2,1,0:T(8,128)(2,1)S(1)}, bf16[2,9,16,256]{3,2,1,0:T(8,128)(2,1)S(1)}, u32[]{:S(2)}, u32[]{:S(2)}) collective-permute-start(bf16[2,9,16,256]{3,2,1,0:T(8,128)(2,1)S(1)} %get-tuple-element.107), channel_id=1, source_target_pairs={{0,8},{4,12},{8,0},{12,4},{1,9},{5,13},{9,1},{13,5},{2,10},{6,14},... | collective-permute-start | bytes 442376 | tf_op jit(solution)/shard_map/ppermute | solution.py:507
  52.7 8.9 %collective-permute-start.21 = (bf16[2,9,16,256]{3,2,1,0:T(8,128)(2,1)S(1)}, bf16[2,9,16,256]{3,2,1,0:T(8,128)(2,1)S(1)}, u32[]{:S(2)}, u32[]{:S(2)}) collective-permute-start(bf16[2,9,16,256]{3,2,1,0:T(8,128)(2,1)S(1)} %get-tuple-element.108), channel_id=1, source_target_pairs={{0,4},{4,0},{8,12},{12,8},{1,5},{5,1},{9,13},{13,9},{2,6},{6,2},{1... | collective-permute-start | bytes 442376 | tf_op jit(solution)/shard_map/ppermute | solution.py:507
  61.7 5.2 %collective-permute-start.23 = (bf16[288,256]{1,0:T(8,128)(2,1)S(1)}, bf16[288,256]{1,0:T(8,128)(2,1)S(1)}, u32[]{:S(2)}, u32[]{:S(2)}) collective-permute-start(bf16[288,256]{1,0:T(8,128)(2,1)S(1)} %get-tuple-element.111.refs_0_), channel_id=1, source_target_pairs={{0,2},{2,0},{1,3},{3,1},{4,6},{6,4},{5,7},{7,5},{8,10},{10,8},{9,1... | collective-permute-start | bytes 442376 | tf_op jit(solution)/shard_map/ppermute | solution.py:502
  62.3 8.6 %collective-permute-start.22 = (bf16[288,256]{1,0:T(8,128)(2,1)S(1)}, bf16[288,256]{1,0:T(8,128)(2,1)S(1)}, u32[]{:S(2)}, u32[]{:S(2)}) collective-permute-start(bf16[288,256]{1,0:T(8,128)(2,1)S(1)} %get-tuple-element.111.refs_0_), channel_id=1, source_target_pairs={{0,8},{4,12},{8,0},{12,4},{1,9},{5,13},{9,1},{13,5},{2,10},{6,14},... | collective-permute-start | bytes 442376 | tf_op jit(solution)/shard_map/ppermute | solution.py:507
  62.8 10.6 %collective-permute-start.25 = (bf16[336,256]{1,0:T(8,128)(2,1)S(1)}, bf16[336,256]{1,0:T(8,128)(2,1)S(1)}, u32[]{:S(2)}, u32[]{:S(2)}) collective-permute-start(bf16[336,256]{1,0:T(8,128)(2,1)S(1)} %get-tuple-element.114), channel_id=1, source_target_pairs={{0,4},{4,0},{8,12},{12,8},{1,5},{5,1},{9,13},{13,9},{2,6},{6,2},{1... | collective-permute-start | bytes 516104 | tf_op jit(solution)/shard_map/ppermute | solution.py:507
  70.9 7.3 %collective-permute-start.24 = (bf16[336,256]{1,0:T(8,128)(2,1)S(1)}, bf16[336,256]{1,0:T(8,128)(2,1)S(1)}, u32[]{:S(2)}, u32[]{:S(2)}) collective-permute-start(bf16[336,256]{1,0:T(8,128)(2,1)S(1)} %get-tuple-element.113), channel_id=1, source_target_pairs={{0,12},{4,8},{8,4},{12,0},{1,13},{5,9},{9,5},{13,1},{2,14},{6,10},... | collective-permute-start | bytes 516104 | tf_op jit(solution)/shard_map/ppermute | solution.py:507
  72.1 5.1 %collective-permute-start.27 = (bf16[288,256]{1,0:T(8,128)(2,1)S(1)}, bf16[288,256]{1,0:T(8,128)(2,1)S(1)}, u32[]{:S(2)}, u32[]{:S(2)}) collective-permute-start(bf16[288,256]{1,0:T(8,128)(2,1)S(1)} %collective-permute-done.22.refs_2_), channel_id=1, source_target_pairs={{0,2},{2,0},{1,3},{3,1},{4,6},{6,4},{5,7},{7,5},{8,10},{10,8},{9,1... | collective-permute-start | bytes 442376 | tf_op jit(solution)/shard_map/ppermute | solution.py:502
  73.4 5.5 %collective-permute-start.26 = (bf16[288,256]{1,0:T(8,128)(2,1)S(1)}, bf16[288,256]{1,0:T(8,128)(2,1)S(1)}, u32[]{:S(2)}, u32[]{:S(2)}) collective-permute-start(bf16[288,256]{1,0:T(8,128)(2,1)S(1)} %slice.4), channel_id=1, source_target_pairs={{0,2},{2,0},{1,3},{3,1},{4,6},{6,4},{5,7},{7,5},{8,10},{10,8},{9,1... | collective-permute-start | bytes 442376 | tf_op jit(solution)/shard_map/ppermute | solution.py:502
  79.0 5.6 %collective-permute-start.28 = (bf16[352,256]{1,0:T(8,128)(2,1)S(1)}, bf16[352,256]{1,0:T(8,128)(2,1)S(1)}, u32[]{:S(2)}, u32[]{:S(2)}) collective-permute-start(bf16[352,256]{1,0:T(8,128)(2,1)S(1)} %column_message.1), channel_id=1, source_target_pairs={{0,2},{2,0},{1,3},{3,1},{4,6},{6,4},{5,7},{7,5},{8,10},{10,8},{9,1... | collective-permute-start | bytes 540680 | tf_op jit(solution)/shard_map/ppermute | solution.py:502
  (11 other events, 58.5 us)

commit v18 on v17

--- a/solution.py
+++ b/solution.py
@@ -550,19 +550,20 @@
     )(*[pltpu.with_memory_space_constraint(value, pltpu.HBM) for value in (routing, tile)])
     saved_slots = saved_pre[0, 0].transpose(1, 2, 0, 3)
     saved_slots = saved_slots.reshape(MIDDLE, MIDDLE * PER_WORKER, HALF)
+    second_other, saved_other = swap(second_weight), swap(saved_slots)
     outgoing, saved_here = tie((outgoing, saved_slots))
     incoming = exchange(outgoing)
 
+    second_other, saved_here = tie((second_other, saved_here))
     masked, *to_owners = call(
         functools.partial(pack_saved, owners, columns, capacity, wide, permuted),
         [shape((MIDDLE, MIDDLE * PER_WORKER, HALF), BF16)] + pieces(MIDDLE, wide * capacity, HALF),
         [SMEM, VMEM], counts + tables, (1, 1), "pack_saved",
     )(routing, saved_here)
-    second_other, saved_other = swap(second_weight), swap(saved_slots)
-
-    incoming, to_owners = tie((incoming[::-1], to_owners[::-1]))
+    incoming_other = [swap(incoming[0])] if permuted else []
+    incoming, to_owners, incoming_other = tie((incoming[::-1], to_owners[::-1], incoming_other))
     incoming, to_owners = incoming[::-1], to_owners[::-1]
-    incoming_other = [swap(value) for value in incoming]
+    incoming_other += [swap(value) for value in incoming[len(incoming_other) :]]
     at_owner = exchange(to_owners)
 
     saved_tiles = saved_input[0, 0].transpose(1, 2, 0, 3)

time: 85.7 us -> 85.2 us (level)
  waiting for transfers between devices: 35.5 us -> 33.8 us
  starting transfers between devices: 26.3 us -> 27.5 us
    ppermute x12, waiting for transfers between devices: 22.8 us -> 19.7 us  [flip(): return lax.ppermute(value, axis, [(i, i ^ step) for i in range(size)])]
    ppermute x17, waiting for transfers between devices: 12.7 us -> 14.1 us  [swap(): return lax.ppermute(value, axis, [(0, 1), (1, 0)])]
  transfers between devices with their start and end apart: 29 -> 29, of which waited for: 17 -> 15; matrix products, arithmetic and copies ran while one was open for 0% -> 0% of each run, Pallas kernels for 24% -> 24%
where the time goes in v18:
time: 85.2 us; the launch traced here: 85 us
  waiting for transfers between devices  33.8 us (40%)
  starting transfers between devices  27.5 us (32%)
  Pallas kernels  21.1 us (25%)
  local copies, waits for them, and re-layouts  1.71 us (2%)
  between operations  0.93 us (1%)
    ppermute x12, waiting for transfers between devices, flip(): return lax.ppermute(value, axis, [(i, i ^ step) for i in range(size)])  19.7 us
    ppermute x12, starting transfers between devices, flip(): return lax.ppermute(value, axis, [(i, i ^ step) for i in range(size)])  19.5 us
    ppermute x17, waiting for transfers between devices, swap(): return lax.ppermute(value, axis, [(0, 1), (1, 0)])  14.1 us
    ppermute x17, starting transfers between devices, swap(): return lax.ppermute(value, axis, [(0, 1), (1, 0)])  8 us
    pallas_call x1, Pallas kernels, shards(): call(functools.partial(worker, scale, owners, columns, capacity, permuted...  6.52 us
    pallas_call x1, Pallas kernels, owner(): call(functools.partial(owner_canvas, owners, capacity, wide, permuted), [...  5.8 us
    pallas_call x1, Pallas kernels, shards(): call(owner_spread, shape((MIDDLE, MIDDLE, TILE_BLOCKS, FULL), BF16), [VME...  2.93 us
    pallas_call x1, Pallas kernels, shards(): call(lay, [shape(grad_out.shape, BF16), shape(slab, F32)] + weights, [VME...  1.76 us
  transfers between devices with their start and end apart: 29, of which 15 were waited for; matrix products, arithmetic and copies ran while one was open for 0% of the time, Pallas kernels for 24%

profile of v18, /device:TPU:0, one launch (start us, length us, event | category | flops | bytes accessed | tf_op | source)
XLA Modules:
  0.0 85.0 jit_solution(16040693618320192808)
XLA Ops:
  1.2 1.4 %pack_cotangents.1 = (bf16[8,64,128]{2,1,0:T(8,128)(2,1)S(1)}, bf16[8,64,128]{2,1,0:T(8,128)(2,1)S(1)}, bf16[8,64,128]{2,1,0:T(8,128)(2,1)S(1)}, bf16[8,64,128]{2,1,0:T(8,128)(2,1)S(1)}) custom-call(s32[4,16]{1,0:T(4,128)} %bitcast.17, bf16[8,8,32,128]{3,2,1,0:T(8,128)(2,1)} %bitcast.12), custom_call_target="tpu_custom_call" | custom-call | flops 1 | bytes 1 | tf_op jit(solution)/shard_map/pack_cotangents/pallas_call | solution.py:539
  2.7 5.1 %collective-permute-start = (bf16[8,64,128]{2,1,0:T(8,128)(2,1)S(1)}, bf16[8,64,128]{2,1,0:T(8,128)(2,1)S(1)}, u32[]{:S(2)}, u32[]{:S(2)}) collective-permute-start(bf16[8,64,128]{2,1,0:T(8,128)(2,1)S(1)} %get-tuple-element.73), channel_id=1, source_target_pairs={{0,12},{4,8},{8,4},{12,0},{1,13},{5,9},{9,5},{13,1},{2,14},{6,10},... | collective-permute-start | bytes 393224 | tf_op jit(solution)/shard_map/ppermute | solution.py:507
  10.1 1.6 %pack_saved.1 = (bf16[10,160,128]{2,1,0:T(8,128)(2,1)S(1)}, bf16[10,80,128]{2,1,0:T(8,128)(2,1)S(1)}, bf16[10,80,128]{2,1,0:T(8,128)(2,1)S(1)}, bf16[10,80,128]{2,1,0:T(8,128)(2,1)S(1)}, bf16[10,80,128]{2,1,0:T(8,128)(2,1)S(1)}) custom-call(s32[4,16]{1,0:T(4,128)S(1)} %bitcast.18, bf16[10,160,128]{2,1,0:T(8,128)(2,1)S(1)} %bitcast.16), custom_call_target="tpu_custom_call" | custom-call | flops 1 | bytes 1 | tf_op jit(solution)/shard_map/pack_saved/pallas_call | solution.py:558
  12.1 6.9 %collective-permute-done.1.refs_2_ = bf16[8,64,128]{2,1,0:T(8,128)(2,1)S(1)} collective-permute-done((bf16[8,64,128]{2,1,0:T(8,128)(2,1)S(1)}, bf16[8,64,128]{2,1,0:T(8,128)(2,1)S(1)}, u32[]{:S(2)}, u32[]{:S(2)}) %collective-permute-start.1) | collective-permute-done | bytes 131104 | tf_op jit(solution)/shard_map/ppermute | solution.py:507
  19.1 3.1 %collective-permute-start.11 = (bf16[10,80,128]{2,1,0:T(8,128)(2,1)S(1)}, bf16[10,80,128]{2,1,0:T(8,128)(2,1)S(1)}, u32[]{:S(2)}, u32[]{:S(2)}) collective-permute-start(bf16[10,80,128]{2,1,0:T(8,128)(2,1)S(1)} %get-tuple-element.94), channel_id=1, source_target_pairs={{0,4},{4,0},{8,12},{12,8},{1,5},{5,1},{9,13},{13,9},{2,6},{6,2},{1... | collective-permute-start | bytes 614408 | tf_op jit(solution)/shard_map/ppermute | solution.py:507
  24.0 6.5 %worker.1 = (f32[4,2,9,16,256]{4,3,2,1,0:T(8,128)S(1)}, bf16[2,2,9,16,256]{4,3,2,1,0:T(8,128)(2,1)S(1)}, bf16[2,2,9,16,256]{4,3,2,1,0:T(8,128)(2,1)S(1)}) custom-call(s32[4,16]{1,0:T(4,128)S(1)} %bitcast.19, bf16[8,64,128]{2,1,0:T(8,128)(2,1)S(1)} %get-tuple-element.83.refs_0_, bf16[8,64,128]{2,1,0:T(8,128)(2,1)S(1)} %collective-permute-done.2.refs_1_, ...), custom_call_target="tpu_custom_call" | custom-call | flops 1 | bytes 1 | tf_op jit(solution)/shard_map/worker/pallas_call | solution.py:575
  30.8 1.5 %collective-permute-start.13 = (bf16[2,2,9,16,256]{4,3,2,1,0:T(8,128)(2,1)S(1)}, bf16[2,2,9,16,256]{4,3,2,1,0:T(8,128)(2,1)S(1)}, u32[]{:S(2)}, u32[]{:S(2)}) collective-permute-start(bf16[2,2,9,16,256]{4,3,2,1,0:T(8,128)(2,1)S(1)} %get-tuple-element.101), channel_id=1, source_target_pairs={{0,2},{2,0},{1,3},{3,1},{4,6},{6,4},{5,7},{7,5},{8,10},{10,8},{9,1... | collective-permute-start | bytes 884744 | tf_op jit(solution)/shard_map/ppermute | solution.py:502
  32.3 1.4 %collective-permute-start.14 = (bf16[10,80,128]{2,1,0:T(8,128)(2,1)S(1)}, bf16[10,80,128]{2,1,0:T(8,128)(2,1)S(1)}, u32[]{:S(2)}, u32[]{:S(2)}) collective-permute-start(bf16[10,80,128]{2,1,0:T(8,128)(2,1)S(1)} %get-tuple-element.105), channel_id=1, source_target_pairs={{0,12},{4,8},{8,4},{12,0},{1,13},{5,9},{9,5},{13,1},{2,14},{6,10},... | collective-permute-start | bytes 614408 | tf_op jit(solution)/shard_map/ppermute | solution.py:507
  34.8 2.9 %owner_spread.1.refs_8_ = bf16[10,10,32,256]{3,2,1,0:T(8,128)(2,1)S(1)} custom-call(bf16[8,8,32,128]{3,2,1,0:T(8,128)(2,1)S(1)} %bitcast.14, bf16[8,8,32,128]{3,2,1,0:T(8,128)(2,1)S(1)} %collective-permute-done.12.tile_other, bf16[9,128,256]{2,1,0:T(8,128)(2,1)S(1)} %copy-done.1, bf16[9,128,256]{2,1,0:T(8,128)(2,1)S(1)} %collective-permute-done.3.refs_11_.second_other), custom_call_target="tpu_custom_call" | custom-call | flops 1 | bytes 1 | tf_op jit(solution)/shard_map/owner_spread/pallas_call | solution.py:601
  37.8 2.9 %collective-permute-done.13.got = bf16[2,2,9,16,256]{4,3,2,1,0:T(8,128)(2,1)S(1)} collective-permute-done((bf16[2,2,9,16,256]{4,3,2,1,0:T(8,128)(2,1)S(1)}, bf16[2,2,9,16,256]{4,3,2,1,0:T(8,128)(2,1)S(1)}, u32[]{:S(2)}, u32[]{:S(2)}) %collective-permute-start.13) | collective-permute-done | bytes 294944 | tf_op jit(solution)/shard_map/ppermute | solution.py:502
  41.4 1.5 %collective-permute-start.19 = (bf16[2,9,16,256]{3,2,1,0:T(8,128)(2,1)S(1)}, bf16[2,9,16,256]{3,2,1,0:T(8,128)(2,1)S(1)}, u32[]{:S(2)}, u32[]{:S(2)}) collective-permute-start(bf16[2,9,16,256]{3,2,1,0:T(8,128)(2,1)S(1)} %get-tuple-element.112), channel_id=1, source_target_pairs={{0,12},{4,8},{8,4},{12,0},{1,13},{5,9},{9,5},{13,1},{2,14},{6,10},... | collective-permute-start | bytes 442376 | tf_op jit(solution)/shard_map/ppermute | solution.py:507
  42.9 2.3 %collective-permute-start.20 = (bf16[2,9,16,256]{3,2,1,0:T(8,128)(2,1)S(1)}, bf16[2,9,16,256]{3,2,1,0:T(8,128)(2,1)S(1)}, u32[]{:S(2)}, u32[]{:S(2)}) collective-permute-start(bf16[2,9,16,256]{3,2,1,0:T(8,128)(2,1)S(1)} %get-tuple-element.113), channel_id=1, source_target_pairs={{0,8},{4,12},{8,0},{12,4},{1,9},{5,13},{9,1},{13,5},{2,10},{6,14},... | collective-permute-start | bytes 442376 | tf_op jit(solution)/shard_map/ppermute | solution.py:507
  45.2 5.8 %owner_canvas.1 = (f32[68,40,128]{2,1,0:T(8,128)S(1)}, bf16[48,256]{1,0:T(8,128)(2,1)S(1)}, bf16[48,256]{1,0:T(8,128)(2,1)S(1)}) custom-call(s32[4,16]{1,0:T(4,128)S(1)} %bitcast.20, bf16[10,80,128]{2,1,0:T(8,128)(2,1)S(1)} %get-tuple-element.91.refs_0_, bf16[10,80,128]{2,1,0:T(8,128)(2,1)S(1)} %collective-permute-done.11.refs_1_, ...), custom_call_target="tpu_custom_call" | custom-call | flops 1 | bytes 1 | tf_op jit(solution)/shard_map/owner_canvas/pallas_call | solution.py:615
  51.7 7.3 %collective-permute-done.20.got_2 = bf16[2,9,16,256]{3,2,1,0:T(8,128)(2,1)S(1)} collective-permute-done((bf16[2,9,16,256]{3,2,1,0:T(8,128)(2,1)S(1)}, bf16[2,9,16,256]{3,2,1,0:T(8,128)(2,1)S(1)}, u32[]{:S(2)}, u32[]{:S(2)}) %collective-permute-start.20) | collective-permute-done | bytes 147488 | tf_op jit(solution)/shard_map/ppermute | solution.py:507
  60.7 2.4 %collective-permute-start.25 = (bf16[336,256]{1,0:T(8,128)(2,1)S(1)}, bf16[336,256]{1,0:T(8,128)(2,1)S(1)}, u32[]{:S(2)}, u32[]{:S(2)}) collective-permute-start(bf16[336,256]{1,0:T(8,128)(2,1)S(1)} %get-tuple-element.120), channel_id=1, source_target_pairs={{0,4},{4,0},{8,12},{12,8},{1,5},{5,1},{9,13},{13,9},{2,6},{6,2},{1... | collective-permute-start | bytes 516104 | tf_op jit(solution)/shard_map/ppermute | solution.py:507
  63.2 2.2 %collective-permute-done.23.refs_4_ = bf16[288,256]{1,0:T(8,128)(2,1)S(1)} collective-permute-done((bf16[288,256]{1,0:T(8,128)(2,1)S(1)}, bf16[288,256]{1,0:T(8,128)(2,1)S(1)}, u32[]{:S(2)}, u32[]{:S(2)}) %collective-permute-start.23) | collective-permute-done | bytes 147488 | tf_op jit(solution)/shard_map/ppermute | solution.py:502
  65.3 3.1 %collective-permute-done.22.refs_2_ = bf16[288,256]{1,0:T(8,128)(2,1)S(1)} collective-permute-done((bf16[288,256]{1,0:T(8,128)(2,1)S(1)}, bf16[288,256]{1,0:T(8,128)(2,1)S(1)}, u32[]{:S(2)}, u32[]{:S(2)}) %collective-permute-start.22) | collective-permute-done | bytes 147488 | tf_op jit(solution)/shard_map/ppermute | solution.py:507
  68.5 2.4 %collective-permute-start.24 = (bf16[336,256]{1,0:T(8,128)(2,1)S(1)}, bf16[336,256]{1,0:T(8,128)(2,1)S(1)}, u32[]{:S(2)}, u32[]{:S(2)}) collective-permute-start(bf16[336,256]{1,0:T(8,128)(2,1)S(1)} %get-tuple-element.119), channel_id=1, source_target_pairs={{0,12},{4,8},{8,4},{12,0},{1,13},{5,9},{9,5},{13,1},{2,14},{6,10},... | collective-permute-start | bytes 516104 | tf_op jit(solution)/shard_map/ppermute | solution.py:507
  70.9 1.2 %collective-permute-start.27 = (bf16[288,256]{1,0:T(8,128)(2,1)S(1)}, bf16[288,256]{1,0:T(8,128)(2,1)S(1)}, u32[]{:S(2)}, u32[]{:S(2)}) collective-permute-start(bf16[288,256]{1,0:T(8,128)(2,1)S(1)} %collective-permute-done.22.refs_2_), channel_id=1, source_target_pairs={{0,2},{2,0},{1,3},{3,1},{4,6},{6,4},{5,7},{7,5},{8,10},{10,8},{9,1... | collective-permute-start | bytes 442376 | tf_op jit(solution)/shard_map/ppermute | solution.py:502
  73.0 3.9 %collective-permute-done.27.refs_6_ = bf16[288,256]{1,0:T(8,128)(2,1)S(1)} collective-permute-done((bf16[288,256]{1,0:T(8,128)(2,1)S(1)}, bf16[288,256]{1,0:T(8,128)(2,1)S(1)}, u32[]{:S(2)}, u32[]{:S(2)}) %collective-permute-start.27) | collective-permute-done | bytes 147488 | tf_op jit(solution)/shard_map/ppermute | solution.py:502
  76.8 1.6 %collective-permute-done.26.refs_5_ = bf16[288,256]{1,0:T(8,128)(2,1)S(1)} collective-permute-done((bf16[288,256]{1,0:T(8,128)(2,1)S(1)}, bf16[288,256]{1,0:T(8,128)(2,1)S(1)}, u32[]{:S(2)}, u32[]{:S(2)}) %collective-permute-start.26) | collective-permute-done | bytes 147488 | tf_op jit(solution)/shard_map/ppermute | solution.py:502
  78.5 1.6 %collective-permute-start.28 = (bf16[352,256]{1,0:T(8,128)(2,1)S(1)}, bf16[352,256]{1,0:T(8,128)(2,1)S(1)}, u32[]{:S(2)}, u32[]{:S(2)}) collective-permute-start(bf16[352,256]{1,0:T(8,128)(2,1)S(1)} %column_message.1), channel_id=1, source_target_pairs={{0,2},{2,0},{1,3},{3,1},{4,6},{6,4},{5,7},{7,5},{8,10},{10,8},{9,1... | collective-permute-start | bytes 540680 | tf_op jit(solution)/shard_map/ppermute | solution.py:502
  80.0 1.8 %lay.1 = (bf16[64,32,128]{2,1,0:T(8,128)(2,1)}, f32[64,16,128]{2,1,0:T(8,128)S(1)}, f32[9,128,256]{2,1,0:T(8,128)}, f32[9,128,256]{2,1,0:T(8,128)}) custom-call(bf16[64,32,128]{2,1,0:T(8,128)(2,1)S(1)} %copy-done, f32[68,40,128]{2,1,0:T(8,128)S(1)} %get-tuple-element.109.canvas, bf16[288,256]{1,0:T(8,128)(2,1)S(1)} %get-tuple-element.117.refs_0_, ...), custom_call_target="tpu_custom_call" | custom-call | flops 1 | bytes 1 | tf_op jit(solution)/shard_map/lay/pallas_call | solution.py:660
  81.8 2.2 %collective-permute-done.28.last = bf16[352,256]{1,0:T(8,128)(2,1)S(1)} collective-permute-done((bf16[352,256]{1,0:T(8,128)(2,1)S(1)}, bf16[352,256]{1,0:T(8,128)(2,1)S(1)}, u32[]{:S(2)}, u32[]{:S(2)}) %collective-permute-start.28) | collective-permute-done | bytes 180256 | tf_op jit(solution)/shard_map/ppermute | solution.py:502
  (58 shorter events, 11.5 us)
Async XLA Ops:
  0.6 7.8 %collective-permute-start.3 = (bf16[9,128,256]{2,1,0:T(8,128)(2,1)}, bf16[9,128,256]{2,1,0:T(8,128)(2,1)S(1)}, u32[]{:S(2)}, u32[]{:S(2)}) collective-permute-start(bf16[9,128,256]{2,1,0:T(8,128)(2,1)} %second.1), channel_id=1, source_target_pairs={{0,1},{1,0},{2,3},{3,2},{4,5},{5,4},{6,7},{7,6},{8,9},{9,8},{10,11... | collective-permute-start | bytes 1769480 | tf_op jit(solution)/shard_map/ppermute | solution.py:502
  1.2 21.5 %collective-permute-start.8 = (bf16[10,160,128]{2,1,0:T(8,128)(2,1)}, bf16[10,160,128]{2,1,0:T(8,128)(2,1)S(1)}, u32[]{:S(2)}, u32[]{:S(2)}) collective-permute-start(bf16[10,160,128]{2,1,0:T(8,128)(2,1)} %bitcast.15), channel_id=1, source_target_pairs={{0,1},{1,0},{2,3},{3,2},{4,5},{5,4},{6,7},{7,6},{8,9},{9,8},{10,11... | collective-permute-start | bytes 1228808 | tf_op jit(solution)/shard_map/ppermute | solution.py:502
  2.7 9.5 %collective-permute-start = (bf16[8,64,128]{2,1,0:T(8,128)(2,1)S(1)}, bf16[8,64,128]{2,1,0:T(8,128)(2,1)S(1)}, u32[]{:S(2)}, u32[]{:S(2)}) collective-permute-start(bf16[8,64,128]{2,1,0:T(8,128)(2,1)S(1)} %get-tuple-element.73), channel_id=1, source_target_pairs={{0,12},{4,8},{8,4},{12,0},{1,13},{5,9},{9,5},{13,1},{2,14},{6,10},... | collective-permute-start | bytes 393224 | tf_op jit(solution)/shard_map/ppermute | solution.py:507
  7.7 11.3 %collective-permute-start.1 = (bf16[8,64,128]{2,1,0:T(8,128)(2,1)S(1)}, bf16[8,64,128]{2,1,0:T(8,128)(2,1)S(1)}, u32[]{:S(2)}, u32[]{:S(2)}) collective-permute-start(bf16[8,64,128]{2,1,0:T(8,128)(2,1)S(1)} %get-tuple-element.74), channel_id=1, source_target_pairs={{0,8},{4,12},{8,0},{12,4},{1,9},{5,13},{9,1},{13,5},{2,10},{6,14},... | collective-permute-start | bytes 393224 | tf_op jit(solution)/shard_map/ppermute | solution.py:507
  7.8 11.3 %collective-permute-start.2 = (bf16[8,64,128]{2,1,0:T(8,128)(2,1)S(1)}, bf16[8,64,128]{2,1,0:T(8,128)(2,1)S(1)}, u32[]{:S(2)}, u32[]{:S(2)}) collective-permute-start(bf16[8,64,128]{2,1,0:T(8,128)(2,1)S(1)} %get-tuple-element.75), channel_id=1, source_target_pairs={{0,4},{4,0},{8,12},{12,8},{1,5},{5,1},{9,13},{13,9},{2,6},{6,2},{1... | collective-permute-start | bytes 393224 | tf_op jit(solution)/shard_map/ppermute | solution.py:507
  8.4 10.7 %collective-permute-start.4 = (bf16[8,64,128]{2,1,0:T(8,128)(2,1)S(1)}, bf16[8,64,128]{2,1,0:T(8,128)(2,1)S(1)}, u32[]{:S(2)}, u32[]{:S(2)}) collective-permute-start(bf16[8,64,128]{2,1,0:T(8,128)(2,1)S(1)} %get-tuple-element.83.refs_0_), channel_id=1, source_target_pairs={{0,1},{1,0},{2,3},{3,2},{4,5},{5,4},{6,7},{7,6},{8,9},{9,8},{10,11... | collective-permute-start | bytes 393224 | tf_op jit(solution)/shard_map/ppermute | solution.py:502
  19.1 11.5 %collective-permute-start.10 = (bf16[10,80,128]{2,1,0:T(8,128)(2,1)S(1)}, bf16[10,80,128]{2,1,0:T(8,128)(2,1)S(1)}, u32[]{:S(2)}, u32[]{:S(2)}) collective-permute-start(bf16[10,80,128]{2,1,0:T(8,128)(2,1)S(1)} %get-tuple-element.93), channel_id=1, source_target_pairs={{0,8},{4,12},{8,0},{12,4},{1,9},{5,13},{9,1},{13,5},{2,10},{6,14},... | collective-permute-start | bytes 614408 | tf_op jit(solution)/shard_map/ppermute | solution.py:507
  19.1 11.6 %collective-permute-start.11 = (bf16[10,80,128]{2,1,0:T(8,128)(2,1)S(1)}, bf16[10,80,128]{2,1,0:T(8,128)(2,1)S(1)}, u32[]{:S(2)}, u32[]{:S(2)}) collective-permute-start(bf16[10,80,128]{2,1,0:T(8,128)(2,1)S(1)} %get-tuple-element.94), channel_id=1, source_target_pairs={{0,4},{4,0},{8,12},{12,8},{1,5},{5,1},{9,13},{13,9},{2,6},{6,2},{1... | collective-permute-start | bytes 614408 | tf_op jit(solution)/shard_map/ppermute | solution.py:507
  30.8 9.8 %collective-permute-start.13 = (bf16[2,2,9,16,256]{4,3,2,1,0:T(8,128)(2,1)S(1)}, bf16[2,2,9,16,256]{4,3,2,1,0:T(8,128)(2,1)S(1)}, u32[]{:S(2)}, u32[]{:S(2)}) collective-permute-start(bf16[2,2,9,16,256]{4,3,2,1,0:T(8,128)(2,1)S(1)} %get-tuple-element.101), channel_id=1, source_target_pairs={{0,2},{2,0},{1,3},{3,1},{4,6},{6,4},{5,7},{7,5},{8,10},{10,8},{9,1... | collective-permute-start | bytes 884744 | tf_op jit(solution)/shard_map/ppermute | solution.py:502
  32.3 9.0 %collective-permute-start.14 = (bf16[10,80,128]{2,1,0:T(8,128)(2,1)S(1)}, bf16[10,80,128]{2,1,0:T(8,128)(2,1)S(1)}, u32[]{:S(2)}, u32[]{:S(2)}) collective-permute-start(bf16[10,80,128]{2,1,0:T(8,128)(2,1)S(1)} %get-tuple-element.105), channel_id=1, source_target_pairs={{0,12},{4,8},{8,4},{12,0},{1,13},{5,9},{9,5},{13,1},{2,14},{6,10},... | collective-permute-start | bytes 614408 | tf_op jit(solution)/shard_map/ppermute | solution.py:507
  33.8 17.3 %collective-permute-start.9 = (bf16[2,2,9,16,256]{4,3,2,1,0:T(8,128)(2,1)S(1)}, bf16[2,2,9,16,256]{4,3,2,1,0:T(8,128)(2,1)S(1)}, u32[]{:S(2)}, u32[]{:S(2)}) collective-permute-start(bf16[2,2,9,16,256]{4,3,2,1,0:T(8,128)(2,1)S(1)} %get-tuple-element.90), channel_id=1, source_target_pairs={{0,2},{2,0},{1,3},{3,1},{4,6},{6,4},{5,7},{7,5},{8,10},{10,8},{9,1... | collective-permute-start | bytes 884744 | tf_op jit(solution)/shard_map/ppermute | solution.py:502
  34.3 7.1 %collective-permute-start.15 = (bf16[10,80,128]{2,1,0:T(8,128)(2,1)S(1)}, bf16[10,80,128]{2,1,0:T(8,128)(2,1)S(1)}, u32[]{:S(2)}, u32[]{:S(2)}) collective-permute-start(bf16[10,80,128]{2,1,0:T(8,128)(2,1)S(1)} %get-tuple-element.91.refs_0_), channel_id=1, source_target_pairs={{0,1},{1,0},{2,3},{3,2},{4,5},{5,4},{6,7},{7,6},{8,9},{9,8},{10,11... | collective-permute-start | bytes 614408 | tf_op jit(solution)/shard_map/ppermute | solution.py:502
  34.3 8.6 %collective-permute-start.16 = (bf16[10,80,128]{2,1,0:T(8,128)(2,1)S(1)}, bf16[10,80,128]{2,1,0:T(8,128)(2,1)S(1)}, u32[]{:S(2)}, u32[]{:S(2)}) collective-permute-start(bf16[10,80,128]{2,1,0:T(8,128)(2,1)S(1)} %collective-permute-done.11.refs_1_), channel_id=1, source_target_pairs={{0,1},{1,0},{2,3},{3,2},{4,5},{5,4},{6,7},{7,6},{8,9},{9,8},{10,11... | collective-permute-start | bytes 614408 | tf_op jit(solution)/shard_map/ppermute | solution.py:502
  40.6 4.6 %collective-permute-start.17 = (bf16[10,80,128]{2,1,0:T(8,128)(2,1)S(1)}, bf16[10,80,128]{2,1,0:T(8,128)(2,1)S(1)}, u32[]{:S(2)}, u32[]{:S(2)}) collective-permute-start(bf16[10,80,128]{2,1,0:T(8,128)(2,1)S(1)} %collective-permute-done.10.refs_2_), channel_id=1, source_target_pairs={{0,1},{1,0},{2,3},{3,2},{4,5},{5,4},{6,7},{7,6},{8,9},{9,8},{10,11... | collective-permute-start | bytes 614408 | tf_op jit(solution)/shard_map/ppermute | solution.py:502
  41.4 10.4 %collective-permute-start.19 = (bf16[2,9,16,256]{3,2,1,0:T(8,128)(2,1)S(1)}, bf16[2,9,16,256]{3,2,1,0:T(8,128)(2,1)S(1)}, u32[]{:S(2)}, u32[]{:S(2)}) collective-permute-start(bf16[2,9,16,256]{3,2,1,0:T(8,128)(2,1)S(1)} %get-tuple-element.112), channel_id=1, source_target_pairs={{0,12},{4,8},{8,4},{12,0},{1,13},{5,9},{9,5},{13,1},{2,14},{6,10},... | collective-permute-start | bytes 442376 | tf_op jit(solution)/shard_map/ppermute | solution.py:507
  42.9 16.1 %collective-permute-start.20 = (bf16[2,9,16,256]{3,2,1,0:T(8,128)(2,1)S(1)}, bf16[2,9,16,256]{3,2,1,0:T(8,128)(2,1)S(1)}, u32[]{:S(2)}, u32[]{:S(2)}) collective-permute-start(bf16[2,9,16,256]{3,2,1,0:T(8,128)(2,1)S(1)} %get-tuple-element.113), channel_id=1, source_target_pairs={{0,8},{4,12},{8,0},{12,4},{1,9},{5,13},{9,1},{13,5},{2,10},{6,14},... | collective-permute-start | bytes 442376 | tf_op jit(solution)/shard_map/ppermute | solution.py:507
  51.1 8.9 %collective-permute-start.21 = (bf16[2,9,16,256]{3,2,1,0:T(8,128)(2,1)S(1)}, bf16[2,9,16,256]{3,2,1,0:T(8,128)(2,1)S(1)}, u32[]{:S(2)}, u32[]{:S(2)}) collective-permute-start(bf16[2,9,16,256]{3,2,1,0:T(8,128)(2,1)S(1)} %get-tuple-element.114), channel_id=1, source_target_pairs={{0,4},{4,0},{8,12},{12,8},{1,5},{5,1},{9,13},{13,9},{2,6},{6,2},{1... | collective-permute-start | bytes 442376 | tf_op jit(solution)/shard_map/ppermute | solution.py:507
  60.1 5.2 %collective-permute-start.23 = (bf16[288,256]{1,0:T(8,128)(2,1)S(1)}, bf16[288,256]{1,0:T(8,128)(2,1)S(1)}, u32[]{:S(2)}, u32[]{:S(2)}) collective-permute-start(bf16[288,256]{1,0:T(8,128)(2,1)S(1)} %get-tuple-element.117.refs_0_), channel_id=1, source_target_pairs={{0,2},{2,0},{1,3},{3,1},{4,6},{6,4},{5,7},{7,5},{8,10},{10,8},{9,1... | collective-permute-start | bytes 442376 | tf_op jit(solution)/shard_map/ppermute | solution.py:502
  60.7 7.8 %collective-permute-start.22 = (bf16[288,256]{1,0:T(8,128)(2,1)S(1)}, bf16[288,256]{1,0:T(8,128)(2,1)S(1)}, u32[]{:S(2)}, u32[]{:S(2)}) collective-permute-start(bf16[288,256]{1,0:T(8,128)(2,1)S(1)} %get-tuple-element.117.refs_0_), channel_id=1, source_target_pairs={{0,8},{4,12},{8,0},{12,4},{1,9},{5,13},{9,1},{13,5},{2,10},{6,14},... | collective-permute-start | bytes 442376 | tf_op jit(solution)/shard_map/ppermute | solution.py:507
  60.7 11.4 %collective-permute-start.25 = (bf16[336,256]{1,0:T(8,128)(2,1)S(1)}, bf16[336,256]{1,0:T(8,128)(2,1)S(1)}, u32[]{:S(2)}, u32[]{:S(2)}) collective-permute-start(bf16[336,256]{1,0:T(8,128)(2,1)S(1)} %get-tuple-element.120), channel_id=1, source_target_pairs={{0,4},{4,0},{8,12},{12,8},{1,5},{5,1},{9,13},{13,9},{2,6},{6,2},{1... | collective-permute-start | bytes 516104 | tf_op jit(solution)/shard_map/ppermute | solution.py:507
  68.5 8.4 %collective-permute-start.24 = (bf16[336,256]{1,0:T(8,128)(2,1)S(1)}, bf16[336,256]{1,0:T(8,128)(2,1)S(1)}, u32[]{:S(2)}, u32[]{:S(2)}) collective-permute-start(bf16[336,256]{1,0:T(8,128)(2,1)S(1)} %get-tuple-element.119), channel_id=1, source_target_pairs={{0,12},{4,8},{8,4},{12,0},{1,13},{5,9},{9,5},{13,1},{2,14},{6,10},... | collective-permute-start | bytes 516104 | tf_op jit(solution)/shard_map/ppermute | solution.py:507
  70.9 6.0 %collective-permute-start.27 = (bf16[288,256]{1,0:T(8,128)(2,1)S(1)}, bf16[288,256]{1,0:T(8,128)(2,1)S(1)}, u32[]{:S(2)}, u32[]{:S(2)}) collective-permute-start(bf16[288,256]{1,0:T(8,128)(2,1)S(1)} %collective-permute-done.22.refs_2_), channel_id=1, source_target_pairs={{0,2},{2,0},{1,3},{3,1},{4,6},{6,4},{5,7},{7,5},{8,10},{10,8},{9,1... | collective-permute-start | bytes 442376 | tf_op jit(solution)/shard_map/ppermute | solution.py:502
  72.1 6.3 %collective-permute-start.26 = (bf16[288,256]{1,0:T(8,128)(2,1)S(1)}, bf16[288,256]{1,0:T(8,128)(2,1)S(1)}, u32[]{:S(2)}, u32[]{:S(2)}) collective-permute-start(bf16[288,256]{1,0:T(8,128)(2,1)S(1)} %slice.4), channel_id=1, source_target_pairs={{0,2},{2,0},{1,3},{3,1},{4,6},{6,4},{5,7},{7,5},{8,10},{10,8},{9,1... | collective-permute-start | bytes 442376 | tf_op jit(solution)/shard_map/ppermute | solution.py:502
  78.5 5.6 %collective-permute-start.28 = (bf16[352,256]{1,0:T(8,128)(2,1)S(1)}, bf16[352,256]{1,0:T(8,128)(2,1)S(1)}, u32[]{:S(2)}, u32[]{:S(2)}) collective-permute-start(bf16[352,256]{1,0:T(8,128)(2,1)S(1)} %column_message.1), channel_id=1, source_target_pairs={{0,2},{2,0},{1,3},{3,1},{4,6},{6,4},{5,7},{7,5},{8,10},{10,8},{9,1... | collective-permute-start | bytes 540680 | tf_op jit(solution)/shard_map/ppermute | solution.py:502
  (11 other events, 58.4 us)

commit v19 on v18

--- a/solution.py
+++ b/solution.py
@@ -172,8 +172,10 @@
     return here
 
 
-def pack_saved(owners, columns, capacity, wide, permuted, routing, saved, masked, *refs):
+def pack_saved(owners, columns, capacity, wide, permuted, routing, saved, saved_other, *refs):
+    (weight, weight_other, masked, whole, full, pick_slots), refs = refs[:6], refs[6:]
     outs, counts, table = refs[:-2], refs[-2], refs[-1]
+    full[...] = ordered(weight[...], weight_other[...], 1)
 
     def clear(number, carry):
         table[number] = DEAD
@@ -186,7 +188,11 @@
         table[owner * capacity + rank] = slot
     outside = outside_image(slots, owners, columns)
     for m in range(MIDDLE):
-        masked[m] = jnp.where(outside(m), 0.0, saved[m].astype(F32)).astype(BF16)
+        here = outside(m)
+        masked[m] = jnp.where(here, 0.0, saved[m].astype(F32)).astype(BF16)
+        other = jnp.where(here, 0.0, saved_other[m].astype(F32)).astype(BF16)
+        whole[m] = ordered(masked[m], other, 1)
+    pick_slots[...] = slot_selection(slots, owners, capacity, permuted)
     size = wide * capacity
     row, lane = iota((size, FULL), 0), iota((size, FULL), 1)
     picks = []
@@ -259,24 +265,27 @@
             at += size
 
 
-def second_gradient(scale, owners, capacity, permuted, routing, *refs):
-    parts = 1 if not permuted else owners
-    own, other = views(refs[:parts], owners), views(refs[parts : 2 * parts], owners)
-    masked, cot = refs[2 * parts : 2 * parts + 2]
-    outs, counts = refs[2 * parts + 2 : -1], refs[-1]
-    slots = worker_codes(routing, counts, owners)
+def slot_selection(slots, owners, capacity, permuted):
     rows, inner = BLOCK * PER_WORKER, owners * BLOCK * capacity
     row, lane = iota((rows, inner), 0), iota((rows, inner), 1)
     target = jnp.full((rows, inner), DEAD, I32)
     for slot, (owner, place, rank) in enumerate(slots):
         step = partner("blk", owner, permuted)
         target = jnp.where(row % PER_WORKER == slot, step * (BLOCK * capacity) + rank, target)
-    pick = one_hot(lane == target + (row // PER_WORKER) * capacity)
+    return one_hot(lane == target + (row // PER_WORKER) * capacity)
+
+
+def second_gradient(scale, owners, capacity, permuted, *refs):
+    parts = 1 if not permuted else owners
+    own, other = views(refs[:parts], owners), views(refs[parts : 2 * parts], owners)
+    pick, masked, cot = refs[2 * parts : 2 * parts + 3]
+    outs = refs[2 * parts + 3 :]
+    rows = BLOCK * PER_WORKER
     for u in range(BLOCK):
         got = jnp.concatenate(
             [ordered(own[o][u], other[o][u], 1) for o in range(owners)], axis=0
         )
-        cot[u] = dot(pick, got).astype(BF16)
+        cot[u] = dot(pick[...], got).astype(BF16)
     grads = cot[...].reshape(BLOCK * rows, FULL)
     turned = []
     for dx in range(3):
@@ -287,18 +296,15 @@
         value = dot(turned[:, dy * rows : (dy + BLOCK) * rows], grads) * scale
         for dx in range(3):
             emit(value[dx * HALF : (dx + 1) * HALF], outs, 0, 3 * dy + dx)
-    return slots
 
 
 def first_gradient(
-    scale, outside, cot, masked, saved_other, weight, weight_other, saved, *refs
+    scale, cot, whole, full, saved, *refs
 ):
-    outs, (total, pre, full) = refs[:-3], refs[-3:]
-    full[...] = ordered(weight[...], weight_other[...], 1)
+    outs, (total, pre) = refs[:-2], refs[-2:]
     spread(cot, full, total, PER_WORKER)
     for m in range(MIDDLE):
-        other = jnp.where(outside(m), 0.0, saved_other[m].astype(F32)).astype(BF16)
-        live = ordered(masked[m], other, 1).astype(F32) > 0
+        live = whole[m].astype(F32) > 0
         value = jnp.where(live, total[m], 0.0)
         pre[m] = value.astype(BF16).reshape(MIDDLE, PER_WORKER, FULL)
     size = MIDDLE * MIDDLE * PER_WORKER
@@ -311,7 +317,7 @@
             emit(value[dx * HALF : (dx + 1) * HALF], outs, 1, 3 * dy + dx)
 
 
-def owner_spread(tile, tile_other, second, second_other, out, total, cot, full):
+def owner_spread(tile, tile_other, full, out, total, cot):
     row, lane = iota((FULL, FULL), 0), iota((FULL, FULL), 1)
     turn = one_hot(lane == (row % TILE_BLOCKS) * BLOCK + row // TILE_BLOCKS)
     for u in range(BLOCK):
@@ -319,31 +325,25 @@
             [ordered(tile[r, u], tile_other[r, u], 1) for r in range(TILE_ROWS)], axis=0
         )
         cot[u] = dot(turn, block).astype(BF16)
-    full[...] = ordered(second[...], second_other[...], 1)
     spread(cot, full, total, TILE_BLOCKS)
     out[...] = total[...].astype(BF16).reshape(out.shape)
 
 
-def worker(scale, owners, columns, capacity, permuted, routing, *refs):
+def worker(scale, owners, capacity, permuted, *refs):
     parts = 1 if not permuted else owners
     inputs, refs = refs[: 2 * parts], refs[2 * parts :]
-    (masked, saved_other, weight, weight_other, source), refs = refs[:5], refs[5:]
+    (pick, masked, whole, full, source), refs = refs[:5], refs[5:]
     if permuted:
         refs, sent = refs[:-1], refs[-1]
-    outs, (counts, cot, total, pre, full, saved, arrived) = refs[:-7], refs[-7:]
+    outs, (cot, total, pre, saved, arrived) = refs[:-5], refs[-5:]
     if permuted:
         kept, near, far = outs
         outs = (kept, sent)
     fetch = pltpu.make_async_copy(source, saved, arrived)
     fetch.start()
-    slots = second_gradient(
-        scale, owners, capacity, permuted, routing, *inputs, masked, cot, *outs, counts
-    )
+    second_gradient(scale, owners, capacity, permuted, *inputs, pick, masked, cot, *outs)
     fetch.wait()
-    first_gradient(
-        scale, outside_image(slots, owners, columns), cot, masked, saved_other, weight, weight_other,
-        saved, *outs, total, pre, full,
-    )
+    first_gradient(scale, cot, whole, full, saved, *outs, total, pre)
     if permuted:
         near[...] = sent[:2]
         far[...] = sent[2:]
@@ -554,12 +554,19 @@
     outgoing, saved_here = tie((outgoing, saved_slots))
     incoming = exchange(outgoing)
 
-    second_other, saved_here = tie((second_other, saved_here))
-    masked, *to_owners = call(
+    second_other, saved_other, saved_here = tie((second_other, saved_other, saved_here))
+    masked, whole, full, pick, *to_owners = call(
         functools.partial(pack_saved, owners, columns, capacity, wide, permuted),
-        [shape((MIDDLE, MIDDLE * PER_WORKER, HALF), BF16)] + pieces(MIDDLE, wide * capacity, HALF),
-        [SMEM, VMEM], counts + tables, (1, 1), "pack_saved",
-    )(routing, saved_here)
+        [
+            shape((MIDDLE, MIDDLE * PER_WORKER, HALF), BF16),
+            shape((MIDDLE, MIDDLE * PER_WORKER, FULL), BF16),
+            shape((9, FULL, FULL), BF16),
+            shape((BLOCK * PER_WORKER, owners * BLOCK * capacity), BF16),
+        ]
+        + pieces(MIDDLE, wide * capacity, HALF),
+        [SMEM] + [VMEM] * 4, counts + tables, (1, 1), "pack_saved",
+    )(routing, saved_here, saved_other, second_weight, second_other)
+
     incoming_other = [swap(incoming[0])] if permuted else []
     incoming, to_owners, incoming_other = tie((incoming[::-1], to_owners[::-1], incoming_other))
     incoming, to_owners = incoming[::-1], to_owners[::-1]
@@ -573,22 +580,20 @@
     else:
         halved = [shape((2, 9, HALF, FULL), F32)]
     terms = call(
-        functools.partial(worker, scale, owners, columns, capacity, permuted),
+        functools.partial(worker, scale, owners, capacity, permuted),
         halved,
-        [SMEM] + [VMEM] * (2 * parts + 4) + [HBM],
-        counts
-        + [
+        [VMEM] * (2 * parts + 4) + [HBM],
+        [
             pltpu.VMEM((BLOCK, BLOCK * PER_WORKER, FULL), BF16),
             pltpu.VMEM((MIDDLE, MIDDLE * PER_WORKER, FULL), F32),
             pltpu.VMEM((MIDDLE, MIDDLE, PER_WORKER, FULL), BF16),
-            pltpu.VMEM((9, FULL, FULL), BF16),
             pltpu.VMEM(saved_tiles.shape, BF16),
             pltpu.SemaphoreType.DMA,
         ]
         + ([pltpu.VMEM((4,) + part, BF16)] if permuted else []),
         (1, 1), "worker",
     )(
-        routing, *incoming, *incoming_other, masked, saved_other, second_weight, second_other,
+        *incoming, *incoming_other, pick, masked, whole, full,
         pltpu.with_memory_space_constraint(saved_tiles, pltpu.HBM),
     )
 
@@ -601,14 +606,13 @@
     total = call(
         owner_spread,
         shape((MIDDLE, MIDDLE, TILE_BLOCKS, FULL), BF16),
-        [VMEM] * 4,
+        [VMEM] * 3,
         [
             pltpu.VMEM((MIDDLE, MIDDLE * TILE_BLOCKS, FULL), F32),
             pltpu.VMEM((BLOCK, BLOCK * TILE_BLOCKS, FULL), BF16),
-            pltpu.VMEM((9, FULL, FULL), BF16),
         ],
         (1, 1), "owner_spread",
-    )(tile_here, swap(tile_mine), second_weight, second_other)
+    )(tile_here, swap(tile_mine), full)
 
     def owner(at_owner):
         at_owner_other = [swap(value) for value in at_owner]

time: 85.2 us -> 85.5 us (level)
  starting transfers between devices: 27.5 us -> 25.8 us
  local copies, waits for them, and re-layouts: 1.71 us -> 2.77 us
    ppermute x17, starting transfers between devices: 8 us -> 6.79 us  [swap(): return lax.ppermute(value, axis, [(0, 1), (1, 0)])]
    unnamed x12, local copies, waits for them, and re-layouts: 1.7 us -> 2.76 us
  transfers between devices with their start and end apart: 29 -> 29, of which waited for: 15 -> 13; matrix products, arithmetic and copies ran while one was open for 0% -> 0% of each run, Pallas kernels for 24% -> 24%
where the time goes in v19:
time: 85.5 us; the launch traced here: 85.2 us
  waiting for transfers between devices  34.3 us (40%)
  starting transfers between devices  25.8 us (30%)
  Pallas kernels  21.4 us (25%)
  local copies, waits for them, and re-layouts  2.77 us (3%)
  between operations  0.94 us (1%)
    ppermute x12, waiting for transfers between devices, flip(): return lax.ppermute(value, axis, [(i, i ^ step) for i in range(size)])  20.5 us
    ppermute x12, starting transfers between devices, flip(): return lax.ppermute(value, axis, [(i, i ^ step) for i in range(size)])  19 us
    ppermute x17, waiting for transfers between devices, swap(): return lax.ppermute(value, axis, [(0, 1), (1, 0)])  13.8 us
    ppermute x17, starting transfers between devices, swap(): return lax.ppermute(value, axis, [(0, 1), (1, 0)])  6.79 us
    pallas_call x1, Pallas kernels, shards(): call(functools.partial(worker, scale, owners, capacity, permuted), halved...  6.53 us
    pallas_call x1, Pallas kernels, owner(): call(functools.partial(owner_canvas, owners, capacity, wide, permuted), [...  5.8 us
    pallas_call x1, Pallas kernels, shards(): call(owner_spread, shape((MIDDLE, MIDDLE, TILE_BLOCKS, FULL), BF16), [VME...  2.92 us
    unnamed x12, local copies, waits for them, and re-layouts  2.76 us
  transfers between devices with their start and end apart: 29, of which 13 were waited for; matrix products, arithmetic and copies ran while one was open for 0% of the time, Pallas kernels for 24%

profile of v19, /device:TPU:0, one launch (start us, length us, event | category | flops | bytes accessed | tf_op | source)
XLA Modules:
  0.0 85.2 jit_solution(6484810444743866524)
XLA Ops:
  1.2 1.4 %pack_cotangents.1 = (bf16[8,64,128]{2,1,0:T(8,128)(2,1)S(1)}, bf16[8,64,128]{2,1,0:T(8,128)(2,1)S(1)}, bf16[8,64,128]{2,1,0:T(8,128)(2,1)S(1)}, bf16[8,64,128]{2,1,0:T(8,128)(2,1)S(1)}) custom-call(s32[4,16]{1,0:T(4,128)} %bitcast.17, bf16[8,8,32,128]{3,2,1,0:T(8,128)(2,1)} %bitcast.12), custom_call_target="tpu_custom_call" | custom-call | flops 1 | bytes 1 | tf_op jit(solution)/shard_map/pack_cotangents/pallas_call | solution.py:539
  2.6 5.1 %collective-permute-start = (bf16[8,64,128]{2,1,0:T(8,128)(2,1)S(1)}, bf16[8,64,128]{2,1,0:T(8,128)(2,1)S(1)}, u32[]{:S(2)}, u32[]{:S(2)}) collective-permute-start(bf16[8,64,128]{2,1,0:T(8,128)(2,1)S(1)} %get-tuple-element.77), channel_id=1, source_target_pairs={{0,12},{4,8},{8,4},{12,0},{1,13},{5,9},{9,5},{13,1},{2,14},{6,10},... | collective-permute-start | bytes 393224 | tf_op jit(solution)/shard_map/ppermute | solution.py:507
  8.4 1.1 %copy-done.1 = bf16[9,128,256]{2,1,0:T(8,128)(2,1)S(1)} copy-done((bf16[9,128,256]{2,1,0:T(8,128)(2,1)S(1)}, bf16[9,128,256]{2,1,0:T(8,128)(2,1)}, u32[]{:S(2)}) %copy-start.1) | copy-done | bytes 589848
  11.1 1.8 %pack_saved.1 = (bf16[10,160,128]{2,1,0:T(8,128)(2,1)S(1)}, bf16[10,160,256]{2,1,0:T(8,128)(2,1)S(1)}, bf16[9,256,256]{2,1,0:T(8,128)(2,1)S(1)}, bf16[128,256]{1...) custom-call(s32[4,16]{1,0:T(4,128)S(1)} %bitcast.18, ...), custom_call_target="tpu_custom_call" | custom-call | flops 1 | bytes 1 | tf_op jit(solution)/shard_map/pack_saved/pallas_call | solution.py:558
  13.0 6.1 %collective-permute-done.1.refs_2_ = bf16[8,64,128]{2,1,0:T(8,128)(2,1)S(1)} collective-permute-done((bf16[8,64,128]{2,1,0:T(8,128)(2,1)S(1)}, bf16[8,64,128]{2,1,0:T(8,128)(2,1)S(1)}, u32[]{:S(2)}, u32[]{:S(2)}) %collective-permute-start.1) | collective-permute-done | bytes 131104 | tf_op jit(solution)/shard_map/ppermute | solution.py:507
  19.1 3.1 %collective-permute-start.11 = (bf16[10,80,128]{2,1,0:T(8,128)(2,1)S(1)}, bf16[10,80,128]{2,1,0:T(8,128)(2,1)S(1)}, u32[]{:S(2)}, u32[]{:S(2)}) collective-permute-start(bf16[10,80,128]{2,1,0:T(8,128)(2,1)S(1)} %get-tuple-element.102), channel_id=1, source_target_pairs={{0,4},{4,0},{8,12},{12,8},{1,5},{5,1},{9,13},{13,9},{2,6},{6,2},{1... | collective-permute-start | bytes 614408 | tf_op jit(solution)/shard_map/ppermute | solution.py:507
  24.0 6.5 %worker.1 = (f32[4,2,9,16,256]{4,3,2,1,0:T(8,128)S(1)}, bf16[2,2,9,16,256]{4,3,2,1,0:T(8,128)(2,1)S(1)}, bf16[2,2,9,16,256]{4,3,2,1,0:T(8,128)(2,1)S(1)}) custom-call(bf16[8,64,128]{2,1,0:T(8,128)(2,1)S(1)} %get-tuple-element.89.refs_0_, bf16[8,64,128]{2,1,0:T(8,128)(2,1)S(1)} %collective-permute-done.2.refs_1_, ...), custom_call_target="tpu_custom_call" | custom-call | flops 1 | bytes 1 | tf_op jit(solution)/shard_map/worker/pallas_call | solution.py:582
  30.8 1.5 %collective-permute-start.13 = (bf16[2,2,9,16,256]{4,3,2,1,0:T(8,128)(2,1)S(1)}, bf16[2,2,9,16,256]{4,3,2,1,0:T(8,128)(2,1)S(1)}, u32[]{:S(2)}, u32[]{:S(2)}) collective-permute-start(bf16[2,2,9,16,256]{4,3,2,1,0:T(8,128)(2,1)S(1)} %get-tuple-element.109), channel_id=1, source_target_pairs={{0,2},{2,0},{1,3},{3,1},{4,6},{6,4},{5,7},{7,5},{8,10},{10,8},{9,1... | collective-permute-start | bytes 884744 | tf_op jit(solution)/shard_map/ppermute | solution.py:502
  32.3 1.4 %collective-permute-start.14 = (bf16[10,80,128]{2,1,0:T(8,128)(2,1)S(1)}, bf16[10,80,128]{2,1,0:T(8,128)(2,1)S(1)}, u32[]{:S(2)}, u32[]{:S(2)}) collective-permute-start(bf16[10,80,128]{2,1,0:T(8,128)(2,1)S(1)} %get-tuple-element.113), channel_id=1, source_target_pairs={{0,12},{4,8},{8,4},{12,0},{1,13},{5,9},{9,5},{13,1},{2,14},{6,10},... | collective-permute-start | bytes 614408 | tf_op jit(solution)/shard_map/ppermute | solution.py:507
  34.8 2.9 %owner_spread.1.refs_8_ = bf16[10,10,32,256]{3,2,1,0:T(8,128)(2,1)S(1)} custom-call(bf16[8,8,32,128]{3,2,1,0:T(8,128)(2,1)S(1)} %bitcast.14, bf16[8,8,32,128]{3,2,1,0:T(8,128)(2,1)S(1)} %collective-permute-done.12.tile_other, bf16[9,256,256]{2,1,0:T(8,128)(2,1)S(1)} %get-tuple-element.97.refs_11_.full), custom_call_target="tpu_custom_call" | custom-call | flops 1 | bytes 1 | tf_op jit(solution)/shard_map/owner_spread/pallas_call | solution.py:606
  37.8 2.9 %collective-permute-done.13.got = bf16[2,2,9,16,256]{4,3,2,1,0:T(8,128)(2,1)S(1)} collective-permute-done((bf16[2,2,9,16,256]{4,3,2,1,0:T(8,128)(2,1)S(1)}, bf16[2,2,9,16,256]{4,3,2,1,0:T(8,128)(2,1)S(1)}, u32[]{:S(2)}, u32[]{:S(2)}) %collective-permute-start.13) | collective-permute-done | bytes 294944 | tf_op jit(solution)/shard_map/ppermute | solution.py:502
  41.3 1.5 %collective-permute-start.19 = (bf16[2,9,16,256]{3,2,1,0:T(8,128)(2,1)S(1)}, bf16[2,9,16,256]{3,2,1,0:T(8,128)(2,1)S(1)}, u32[]{:S(2)}, u32[]{:S(2)}) collective-permute-start(bf16[2,9,16,256]{3,2,1,0:T(8,128)(2,1)S(1)} %get-tuple-element.120), channel_id=1, source_target_pairs={{0,12},{4,8},{8,4},{12,0},{1,13},{5,9},{9,5},{13,1},{2,14},{6,10},... | collective-permute-start | bytes 442376 | tf_op jit(solution)/shard_map/ppermute | solution.py:507
  42.9 2.3 %collective-permute-start.20 = (bf16[2,9,16,256]{3,2,1,0:T(8,128)(2,1)S(1)}, bf16[2,9,16,256]{3,2,1,0:T(8,128)(2,1)S(1)}, u32[]{:S(2)}, u32[]{:S(2)}) collective-permute-start(bf16[2,9,16,256]{3,2,1,0:T(8,128)(2,1)S(1)} %get-tuple-element.121), channel_id=1, source_target_pairs={{0,8},{4,12},{8,0},{12,4},{1,9},{5,13},{9,1},{13,5},{2,10},{6,14},... | collective-permute-start | bytes 442376 | tf_op jit(solution)/shard_map/ppermute | solution.py:507
  45.2 5.8 %owner_canvas.1 = (f32[68,40,128]{2,1,0:T(8,128)S(1)}, bf16[48,256]{1,0:T(8,128)(2,1)S(1)}, bf16[48,256]{1,0:T(8,128)(2,1)S(1)}) custom-call(s32[4,16]{1,0:T(4,128)S(1)} %bitcast.19, bf16[10,80,128]{2,1,0:T(8,128)(2,1)S(1)} %get-tuple-element.99.refs_0_, bf16[10,80,128]{2,1,0:T(8,128)(2,1)S(1)} %collective-permute-done.11.refs_1_, ...), custom_call_target="tpu_custom_call" | custom-call | flops 1 | bytes 1 | tf_op jit(solution)/shard_map/owner_canvas/pallas_call | solution.py:619
  51.7 7.3 %collective-permute-done.20.got_2 = bf16[2,9,16,256]{3,2,1,0:T(8,128)(2,1)S(1)} collective-permute-done((bf16[2,9,16,256]{3,2,1,0:T(8,128)(2,1)S(1)}, bf16[2,9,16,256]{3,2,1,0:T(8,128)(2,1)S(1)}, u32[]{:S(2)}, u32[]{:S(2)}) %collective-permute-start.20) | collective-permute-done | bytes 147488 | tf_op jit(solution)/shard_map/ppermute | solution.py:507
  59.0 1.0 %collective-permute-done.21.got_1 = bf16[2,9,16,256]{3,2,1,0:T(8,128)(2,1)S(1)} collective-permute-done((bf16[2,9,16,256]{3,2,1,0:T(8,128)(2,1)S(1)}, bf16[2,9,16,256]{3,2,1,0:T(8,128)(2,1)S(1)}, u32[]{:S(2)}, u32[]{:S(2)}) %collective-permute-start.21) | collective-permute-done | bytes 147488 | tf_op jit(solution)/shard_map/ppermute | solution.py:507
  60.8 2.4 %collective-permute-start.25 = (bf16[336,256]{1,0:T(8,128)(2,1)S(1)}, bf16[336,256]{1,0:T(8,128)(2,1)S(1)}, u32[]{:S(2)}, u32[]{:S(2)}) collective-permute-start(bf16[336,256]{1,0:T(8,128)(2,1)S(1)} %get-tuple-element.128), channel_id=1, source_target_pairs={{0,4},{4,0},{8,12},{12,8},{1,5},{5,1},{9,13},{13,9},{2,6},{6,2},{1... | collective-permute-start | bytes 516104 | tf_op jit(solution)/shard_map/ppermute | solution.py:507
  63.2 5.3 %collective-permute-done.22.refs_2_ = bf16[288,256]{1,0:T(8,128)(2,1)S(1)} collective-permute-done((bf16[288,256]{1,0:T(8,128)(2,1)S(1)}, bf16[288,256]{1,0:T(8,128)(2,1)S(1)}, u32[]{:S(2)}, u32[]{:S(2)}) %collective-permute-start.22) | collective-permute-done | bytes 147488 | tf_op jit(solution)/shard_map/ppermute | solution.py:507
  68.4 1.9 %collective-permute-start.24 = (bf16[336,256]{1,0:T(8,128)(2,1)S(1)}, bf16[336,256]{1,0:T(8,128)(2,1)S(1)}, u32[]{:S(2)}, u32[]{:S(2)}) collective-permute-start(bf16[336,256]{1,0:T(8,128)(2,1)S(1)} %get-tuple-element.127), channel_id=1, source_target_pairs={{0,12},{4,8},{8,4},{12,0},{1,13},{5,9},{9,5},{13,1},{2,14},{6,10},... | collective-permute-start | bytes 516104 | tf_op jit(solution)/shard_map/ppermute | solution.py:507
  70.5 1.9 %collective-permute-start.26 = (bf16[288,256]{1,0:T(8,128)(2,1)S(1)}, bf16[288,256]{1,0:T(8,128)(2,1)S(1)}, u32[]{:S(2)}, u32[]{:S(2)}) collective-permute-start(bf16[288,256]{1,0:T(8,128)(2,1)S(1)} %slice.4), channel_id=1, source_target_pairs={{0,2},{2,0},{1,3},{3,1},{4,6},{6,4},{5,7},{7,5},{8,10},{10,8},{9,1... | collective-permute-start | bytes 442376 | tf_op jit(solution)/shard_map/ppermute | solution.py:502
  72.4 4.6 %collective-permute-done.27.refs_6_ = bf16[288,256]{1,0:T(8,128)(2,1)S(1)} collective-permute-done((bf16[288,256]{1,0:T(8,128)(2,1)S(1)}, bf16[288,256]{1,0:T(8,128)(2,1)S(1)}, u32[]{:S(2)}, u32[]{:S(2)}) %collective-permute-start.27) | collective-permute-done | bytes 147488 | tf_op jit(solution)/shard_map/ppermute | solution.py:502
  77.0 1.6 %collective-permute-done.26.refs_5_ = bf16[288,256]{1,0:T(8,128)(2,1)S(1)} collective-permute-done((bf16[288,256]{1,0:T(8,128)(2,1)S(1)}, bf16[288,256]{1,0:T(8,128)(2,1)S(1)}, u32[]{:S(2)}, u32[]{:S(2)}) %collective-permute-start.26) | collective-permute-done | bytes 147488 | tf_op jit(solution)/shard_map/ppermute | solution.py:502
  79.0 1.8 %lay.1 = (bf16[64,32,128]{2,1,0:T(8,128)(2,1)}, f32[64,16,128]{2,1,0:T(8,128)S(1)}, f32[9,128,256]{2,1,0:T(8,128)}, f32[9,128,256]{2,1,0:T(8,128)}) custom-call(bf16[64,32,128]{2,1,0:T(8,128)(2,1)S(1)} %copy-done, f32[68,40,128]{2,1,0:T(8,128)S(1)} %get-tuple-element.117.canvas, bf16[288,256]{1,0:T(8,128)(2,1)S(1)} %get-tuple-element.125.refs_0_, ...), custom_call_target="tpu_custom_call" | custom-call | flops 1 | bytes 1 | tf_op jit(solution)/shard_map/lay/pallas_call | solution.py:664
  80.7 3.5 %collective-permute-done.28.last = bf16[352,256]{1,0:T(8,128)(2,1)S(1)} collective-permute-done((bf16[352,256]{1,0:T(8,128)(2,1)S(1)}, bf16[352,256]{1,0:T(8,128)(2,1)S(1)}, u32[]{:S(2)}, u32[]{:S(2)}) %collective-permute-start.28) | collective-permute-done | bytes 180256 | tf_op jit(solution)/shard_map/ppermute | solution.py:502
  (58 shorter events, 9.7 us)
Async XLA Ops:
  0.6 7.8 %collective-permute-start.3 = (bf16[9,128,256]{2,1,0:T(8,128)(2,1)}, bf16[9,128,256]{2,1,0:T(8,128)(2,1)S(1)}, u32[]{:S(2)}, u32[]{:S(2)}) collective-permute-start(bf16[9,128,256]{2,1,0:T(8,128)(2,1)} %refs_0_.1), channel_id=1, source_target_pairs={{0,1},{1,0},{2,3},{3,2},{4,5},{5,4},{6,7},{7,6},{8,9},{9,8},{10,11... | collective-permute-start | bytes 1769480 | tf_op jit(solution)/shard_map/ppermute | solution.py:502
  1.1 7.2 %collective-permute-start.4 = (bf16[10,160,128]{2,1,0:T(8,128)(2,1)}, bf16[10,160,128]{2,1,0:T(8,128)(2,1)S(1)}, u32[]{:S(2)}, u32[]{:S(2)}) collective-permute-start(bf16[10,160,128]{2,1,0:T(8,128)(2,1)} %bitcast.15), channel_id=1, source_target_pairs={{0,1},{1,0},{2,3},{3,2},{4,5},{5,4},{6,7},{7,6},{8,9},{9,8},{10,11... | collective-permute-start | bytes 1228808 | tf_op jit(solution)/shard_map/ppermute | solution.py:502
  2.6 10.3 %collective-permute-start = (bf16[8,64,128]{2,1,0:T(8,128)(2,1)S(1)}, bf16[8,64,128]{2,1,0:T(8,128)(2,1)S(1)}, u32[]{:S(2)}, u32[]{:S(2)}) collective-permute-start(bf16[8,64,128]{2,1,0:T(8,128)(2,1)S(1)} %get-tuple-element.77), channel_id=1, source_target_pairs={{0,12},{4,8},{8,4},{12,0},{1,13},{5,9},{9,5},{13,1},{2,14},{6,10},... | collective-permute-start | bytes 393224 | tf_op jit(solution)/shard_map/ppermute | solution.py:507
  7.7 11.3 %collective-permute-start.1 = (bf16[8,64,128]{2,1,0:T(8,128)(2,1)S(1)}, bf16[8,64,128]{2,1,0:T(8,128)(2,1)S(1)}, u32[]{:S(2)}, u32[]{:S(2)}) collective-permute-start(bf16[8,64,128]{2,1,0:T(8,128)(2,1)S(1)} %get-tuple-element.78), channel_id=1, source_target_pairs={{0,8},{4,12},{8,0},{12,4},{1,9},{5,13},{9,1},{13,5},{2,10},{6,14},... | collective-permute-start | bytes 393224 | tf_op jit(solution)/shard_map/ppermute | solution.py:507
  7.7 11.3 %collective-permute-start.2 = (bf16[8,64,128]{2,1,0:T(8,128)(2,1)S(1)}, bf16[8,64,128]{2,1,0:T(8,128)(2,1)S(1)}, u32[]{:S(2)}, u32[]{:S(2)}) collective-permute-start(bf16[8,64,128]{2,1,0:T(8,128)(2,1)S(1)} %get-tuple-element.79), channel_id=1, source_target_pairs={{0,4},{4,0},{8,12},{12,8},{1,5},{5,1},{9,13},{13,9},{2,6},{6,2},{1... | collective-permute-start | bytes 393224 | tf_op jit(solution)/shard_map/ppermute | solution.py:507
  8.4 10.7 %collective-permute-start.5 = (bf16[8,64,128]{2,1,0:T(8,128)(2,1)S(1)}, bf16[8,64,128]{2,1,0:T(8,128)(2,1)S(1)}, u32[]{:S(2)}, u32[]{:S(2)}) collective-permute-start(bf16[8,64,128]{2,1,0:T(8,128)(2,1)S(1)} %get-tuple-element.89.refs_0_), channel_id=1, source_target_pairs={{0,1},{1,0},{2,3},{3,2},{4,5},{5,4},{6,7},{7,6},{8,9},{9,8},{10,11... | collective-permute-start | bytes 393224 | tf_op jit(solution)/shard_map/ppermute | solution.py:502
  19.1 11.5 %collective-permute-start.10 = (bf16[10,80,128]{2,1,0:T(8,128)(2,1)S(1)}, bf16[10,80,128]{2,1,0:T(8,128)(2,1)S(1)}, u32[]{:S(2)}, u32[]{:S(2)}) collective-permute-start(bf16[10,80,128]{2,1,0:T(8,128)(2,1)S(1)} %get-tuple-element.101), channel_id=1, source_target_pairs={{0,8},{4,12},{8,0},{12,4},{1,9},{5,13},{9,1},{13,5},{2,10},{6,14},... | collective-permute-start | bytes 614408 | tf_op jit(solution)/shard_map/ppermute | solution.py:507
  19.1 11.6 %collective-permute-start.11 = (bf16[10,80,128]{2,1,0:T(8,128)(2,1)S(1)}, bf16[10,80,128]{2,1,0:T(8,128)(2,1)S(1)}, u32[]{:S(2)}, u32[]{:S(2)}) collective-permute-start(bf16[10,80,128]{2,1,0:T(8,128)(2,1)S(1)} %get-tuple-element.102), channel_id=1, source_target_pairs={{0,4},{4,0},{8,12},{12,8},{1,5},{5,1},{9,13},{13,9},{2,6},{6,2},{1... | collective-permute-start | bytes 614408 | tf_op jit(solution)/shard_map/ppermute | solution.py:507
  30.8 9.8 %collective-permute-start.13 = (bf16[2,2,9,16,256]{4,3,2,1,0:T(8,128)(2,1)S(1)}, bf16[2,2,9,16,256]{4,3,2,1,0:T(8,128)(2,1)S(1)}, u32[]{:S(2)}, u32[]{:S(2)}) collective-permute-start(bf16[2,2,9,16,256]{4,3,2,1,0:T(8,128)(2,1)S(1)} %get-tuple-element.109), channel_id=1, source_target_pairs={{0,2},{2,0},{1,3},{3,1},{4,6},{6,4},{5,7},{7,5},{8,10},{10,8},{9,1... | collective-permute-start | bytes 884744 | tf_op jit(solution)/shard_map/ppermute | solution.py:502
  32.3 9.0 %collective-permute-start.14 = (bf16[10,80,128]{2,1,0:T(8,128)(2,1)S(1)}, bf16[10,80,128]{2,1,0:T(8,128)(2,1)S(1)}, u32[]{:S(2)}, u32[]{:S(2)}) collective-permute-start(bf16[10,80,128]{2,1,0:T(8,128)(2,1)S(1)} %get-tuple-element.113), channel_id=1, source_target_pairs={{0,12},{4,8},{8,4},{12,0},{1,13},{5,9},{9,5},{13,1},{2,14},{6,10},... | collective-permute-start | bytes 614408 | tf_op jit(solution)/shard_map/ppermute | solution.py:507
  33.7 17.3 %collective-permute-start.9 = (bf16[2,2,9,16,256]{4,3,2,1,0:T(8,128)(2,1)S(1)}, bf16[2,2,9,16,256]{4,3,2,1,0:T(8,128)(2,1)S(1)}, u32[]{:S(2)}, u32[]{:S(2)}) collective-permute-start(bf16[2,2,9,16,256]{4,3,2,1,0:T(8,128)(2,1)S(1)} %get-tuple-element.98), channel_id=1, source_target_pairs={{0,2},{2,0},{1,3},{3,1},{4,6},{6,4},{5,7},{7,5},{8,10},{10,8},{9,1... | collective-permute-start | bytes 884744 | tf_op jit(solution)/shard_map/ppermute | solution.py:502
  34.3 7.1 %collective-permute-start.15 = (bf16[10,80,128]{2,1,0:T(8,128)(2,1)S(1)}, bf16[10,80,128]{2,1,0:T(8,128)(2,1)S(1)}, u32[]{:S(2)}, u32[]{:S(2)}) collective-permute-start(bf16[10,80,128]{2,1,0:T(8,128)(2,1)S(1)} %get-tuple-element.99.refs_0_), channel_id=1, source_target_pairs={{0,1},{1,0},{2,3},{3,2},{4,5},{5,4},{6,7},{7,6},{8,9},{9,8},{10,11... | collective-permute-start | bytes 614408 | tf_op jit(solution)/shard_map/ppermute | solution.py:502
  34.3 8.6 %collective-permute-start.16 = (bf16[10,80,128]{2,1,0:T(8,128)(2,1)S(1)}, bf16[10,80,128]{2,1,0:T(8,128)(2,1)S(1)}, u32[]{:S(2)}, u32[]{:S(2)}) collective-permute-start(bf16[10,80,128]{2,1,0:T(8,128)(2,1)S(1)} %collective-permute-done.11.refs_1_), channel_id=1, source_target_pairs={{0,1},{1,0},{2,3},{3,2},{4,5},{5,4},{6,7},{7,6},{8,9},{9,8},{10,11... | collective-permute-start | bytes 614408 | tf_op jit(solution)/shard_map/ppermute | solution.py:502
  40.6 4.6 %collective-permute-start.17 = (bf16[10,80,128]{2,1,0:T(8,128)(2,1)S(1)}, bf16[10,80,128]{2,1,0:T(8,128)(2,1)S(1)}, u32[]{:S(2)}, u32[]{:S(2)}) collective-permute-start(bf16[10,80,128]{2,1,0:T(8,128)(2,1)S(1)} %collective-permute-done.10.refs_2_), channel_id=1, source_target_pairs={{0,1},{1,0},{2,3},{3,2},{4,5},{5,4},{6,7},{7,6},{8,9},{9,8},{10,11... | collective-permute-start | bytes 614408 | tf_op jit(solution)/shard_map/ppermute | solution.py:502
  41.3 10.4 %collective-permute-start.19 = (bf16[2,9,16,256]{3,2,1,0:T(8,128)(2,1)S(1)}, bf16[2,9,16,256]{3,2,1,0:T(8,128)(2,1)S(1)}, u32[]{:S(2)}, u32[]{:S(2)}) collective-permute-start(bf16[2,9,16,256]{3,2,1,0:T(8,128)(2,1)S(1)} %get-tuple-element.120), channel_id=1, source_target_pairs={{0,12},{4,8},{8,4},{12,0},{1,13},{5,9},{9,5},{13,1},{2,14},{6,10},... | collective-permute-start | bytes 442376 | tf_op jit(solution)/shard_map/ppermute | solution.py:507
  42.9 16.1 %collective-permute-start.20 = (bf16[2,9,16,256]{3,2,1,0:T(8,128)(2,1)S(1)}, bf16[2,9,16,256]{3,2,1,0:T(8,128)(2,1)S(1)}, u32[]{:S(2)}, u32[]{:S(2)}) collective-permute-start(bf16[2,9,16,256]{3,2,1,0:T(8,128)(2,1)S(1)} %get-tuple-element.121), channel_id=1, source_target_pairs={{0,8},{4,12},{8,0},{12,4},{1,9},{5,13},{9,1},{13,5},{2,10},{6,14},... | collective-permute-start | bytes 442376 | tf_op jit(solution)/shard_map/ppermute | solution.py:507
  51.1 8.9 %collective-permute-start.21 = (bf16[2,9,16,256]{3,2,1,0:T(8,128)(2,1)S(1)}, bf16[2,9,16,256]{3,2,1,0:T(8,128)(2,1)S(1)}, u32[]{:S(2)}, u32[]{:S(2)}) collective-permute-start(bf16[2,9,16,256]{3,2,1,0:T(8,128)(2,1)S(1)} %get-tuple-element.122), channel_id=1, source_target_pairs={{0,4},{4,0},{8,12},{12,8},{1,5},{5,1},{9,13},{13,9},{2,6},{6,2},{1... | collective-permute-start | bytes 442376 | tf_op jit(solution)/shard_map/ppermute | solution.py:507
  60.1 8.3 %collective-permute-start.22 = (bf16[288,256]{1,0:T(8,128)(2,1)S(1)}, bf16[288,256]{1,0:T(8,128)(2,1)S(1)}, u32[]{:S(2)}, u32[]{:S(2)}) collective-permute-start(bf16[288,256]{1,0:T(8,128)(2,1)S(1)} %get-tuple-element.125.refs_0_), channel_id=1, source_target_pairs={{0,8},{4,12},{8,0},{12,4},{1,9},{5,13},{9,1},{13,5},{2,10},{6,14},... | collective-permute-start | bytes 442376 | tf_op jit(solution)/shard_map/ppermute | solution.py:507
  60.2 8.2 %collective-permute-start.23 = (bf16[288,256]{1,0:T(8,128)(2,1)S(1)}, bf16[288,256]{1,0:T(8,128)(2,1)S(1)}, u32[]{:S(2)}, u32[]{:S(2)}) collective-permute-start(bf16[288,256]{1,0:T(8,128)(2,1)S(1)} %get-tuple-element.125.refs_0_), channel_id=1, source_target_pairs={{0,2},{2,0},{1,3},{3,1},{4,6},{6,4},{5,7},{7,5},{8,10},{10,8},{9,1... | collective-permute-start | bytes 442376 | tf_op jit(solution)/shard_map/ppermute | solution.py:502
  60.8 9.7 %collective-permute-start.25 = (bf16[336,256]{1,0:T(8,128)(2,1)S(1)}, bf16[336,256]{1,0:T(8,128)(2,1)S(1)}, u32[]{:S(2)}, u32[]{:S(2)}) collective-permute-start(bf16[336,256]{1,0:T(8,128)(2,1)S(1)} %get-tuple-element.128), channel_id=1, source_target_pairs={{0,4},{4,0},{8,12},{12,8},{1,5},{5,1},{9,13},{13,9},{2,6},{6,2},{1... | collective-permute-start | bytes 516104 | tf_op jit(solution)/shard_map/ppermute | solution.py:507
  68.4 8.6 %collective-permute-start.24 = (bf16[336,256]{1,0:T(8,128)(2,1)S(1)}, bf16[336,256]{1,0:T(8,128)(2,1)S(1)}, u32[]{:S(2)}, u32[]{:S(2)}) collective-permute-start(bf16[336,256]{1,0:T(8,128)(2,1)S(1)} %get-tuple-element.127), channel_id=1, source_target_pairs={{0,12},{4,8},{8,4},{12,0},{1,13},{5,9},{9,5},{13,1},{2,14},{6,10},... | collective-permute-start | bytes 516104 | tf_op jit(solution)/shard_map/ppermute | solution.py:507
  70.3 6.7 %collective-permute-start.27 = (bf16[288,256]{1,0:T(8,128)(2,1)S(1)}, bf16[288,256]{1,0:T(8,128)(2,1)S(1)}, u32[]{:S(2)}, u32[]{:S(2)}) collective-permute-start(bf16[288,256]{1,0:T(8,128)(2,1)S(1)} %collective-permute-done.22.refs_2_), channel_id=1, source_target_pairs={{0,2},{2,0},{1,3},{3,1},{4,6},{6,4},{5,7},{7,5},{8,10},{10,8},{9,1... | collective-permute-start | bytes 442376 | tf_op jit(solution)/shard_map/ppermute | solution.py:502
  70.5 8.1 %collective-permute-start.26 = (bf16[288,256]{1,0:T(8,128)(2,1)S(1)}, bf16[288,256]{1,0:T(8,128)(2,1)S(1)}, u32[]{:S(2)}, u32[]{:S(2)}) collective-permute-start(bf16[288,256]{1,0:T(8,128)(2,1)S(1)} %slice.4), channel_id=1, source_target_pairs={{0,2},{2,0},{1,3},{3,1},{4,6},{6,4},{5,7},{7,5},{8,10},{10,8},{9,1... | collective-permute-start | bytes 442376 | tf_op jit(solution)/shard_map/ppermute | solution.py:502
  78.6 5.6 %collective-permute-start.28 = (bf16[352,256]{1,0:T(8,128)(2,1)S(1)}, bf16[352,256]{1,0:T(8,128)(2,1)S(1)}, u32[]{:S(2)}, u32[]{:S(2)}) collective-permute-start(bf16[352,256]{1,0:T(8,128)(2,1)S(1)} %column_message.1), channel_id=1, source_target_pairs={{0,2},{2,0},{1,3},{3,1},{4,6},{6,4},{5,7},{7,5},{8,10},{10,8},{9,1... | collective-permute-start | bytes 540680 | tf_op jit(solution)/shard_map/ppermute | solution.py:502
  (11 other events, 36.1 us)

commit v20 on v18

--- a/solution.py
+++ b/solution.py
@@ -644,7 +644,7 @@
             add_workers, [message, wider, wider], [VMEM] * 6, [], (1, 1), "add_workers",
         )(keep, *got, *rims)
         got_2, got_1 = flip(own, "blk", 2), flip(wides[0], "blk", 1)
-        wide_3, got_2, across = tie((wides[1], got_2, swap(own, "col")))
+        across, got_2, wide_3 = tie((swap(own, "col"), got_2, wides[1]))
         got_3 = flip(wide_3, "blk", 3)
         across = [across] + [swap(value, "col") for value in (got_1[:PART], got_2)]
         got_3, got_1, across = tie((got_3, got_1, across))

time: 85.2 us -> 85.4 us (level)
  waiting for transfers between devices: 33.8 us -> 35 us
  starting transfers between devices: 27.5 us -> 26.4 us
    ppermute x12, waiting for transfers between devices: 19.7 us -> 21.8 us  [flip(): return lax.ppermute(value, axis, [(i, i ^ step) for i in range(size)])]
    ppermute x17, waiting for transfers between devices: 14.1 us -> 13.2 us  [swap(): return lax.ppermute(value, axis, [(0, 1), (1, 0)])]
  transfers between devices with their start and end apart: 29 -> 29, of which waited for: 15 -> 14; matrix products, arithmetic and copies ran while one was open for 0% -> 0% of each run, Pallas kernels for 24% -> 24%
where the time goes in v20:
time: 85.4 us; the launch traced here: 85.2 us
  waiting for transfers between devices  35 us (41%)
  starting transfers between devices  26.4 us (31%)
  Pallas kernels  21.1 us (25%)
  local copies, waits for them, and re-layouts  1.71 us (2%)
  between operations  0.93 us (1%)
    ppermute x12, waiting for transfers between devices, flip(): return lax.ppermute(value, axis, [(i, i ^ step) for i in range(size)])  21.8 us
    ppermute x12, starting transfers between devices, flip(): return lax.ppermute(value, axis, [(i, i ^ step) for i in range(size)])  19 us
    ppermute x17, waiting for transfers between devices, swap(): return lax.ppermute(value, axis, [(0, 1), (1, 0)])  13.2 us
    ppermute x17, starting transfers between devices, swap(): return lax.ppermute(value, axis, [(0, 1), (1, 0)])  7.41 us
    pallas_call x1, Pallas kernels, shards(): call(functools.partial(worker, scale, owners, columns, capacity, permuted...  6.52 us
    pallas_call x1, Pallas kernels, owner(): call(functools.partial(owner_canvas, owners, capacity, wide, permuted), [...  5.8 us
    pallas_call x1, Pallas kernels, shards(): call(owner_spread, shape((MIDDLE, MIDDLE, TILE_BLOCKS, FULL), BF16), [VME...  2.93 us
    pallas_call x1, Pallas kernels, shards(): call(lay, [shape(grad_out.shape, BF16), shape(slab, F32)] + weights, [VME...  1.76 us
  transfers between devices with their start and end apart: 29, of which 14 were waited for; matrix products, arithmetic and copies ran while one was open for 0% of the time, Pallas kernels for 24%

profile of v20, /device:TPU:0, one launch (start us, length us, event | category | flops | bytes accessed | tf_op | source)
XLA Modules:
  0.0 85.2 jit_solution(5005317178327448672)
XLA Ops:
  1.2 1.4 %pack_cotangents.1 = (bf16[8,64,128]{2,1,0:T(8,128)(2,1)S(1)}, bf16[8,64,128]{2,1,0:T(8,128)(2,1)S(1)}, bf16[8,64,128]{2,1,0:T(8,128)(2,1)S(1)}, bf16[8,64,128]{2,1,0:T(8,128)(2,1)S(1)}) custom-call(s32[4,16]{1,0:T(4,128)} %bitcast.17, bf16[8,8,32,128]{3,2,1,0:T(8,128)(2,1)} %bitcast.12), custom_call_target="tpu_custom_call" | custom-call | flops 1 | bytes 1 | tf_op jit(solution)/shard_map/pack_cotangents/pallas_call | solution.py:539
  2.7 5.1 %collective-permute-start = (bf16[8,64,128]{2,1,0:T(8,128)(2,1)S(1)}, bf16[8,64,128]{2,1,0:T(8,128)(2,1)S(1)}, u32[]{:S(2)}, u32[]{:S(2)}) collective-permute-start(bf16[8,64,128]{2,1,0:T(8,128)(2,1)S(1)} %get-tuple-element.73), channel_id=1, source_target_pairs={{0,12},{4,8},{8,4},{12,0},{1,13},{5,9},{9,5},{13,1},{2,14},{6,10},... | collective-permute-start | bytes 393224 | tf_op jit(solution)/shard_map/ppermute | solution.py:507
  8.4 1.0 %copy-done.3 = bf16[1,1,16,10,10,128]{5,2,4,3,1,0:T(8,128)(2,1)S(1)} copy-done((bf16[1,1,16,10,10,128]{5,2,4,3,1,0:T(8,128)(2,1)S(1)}, bf16[1,1,16,10,10,128]{5,2,4,3,1,0:T(8,128)(2,1)}, u32[]{:S(2)}) %copy-start.3) | copy-done | bytes 409624
  10.1 1.6 %pack_saved.1 = (bf16[10,160,128]{2,1,0:T(8,128)(2,1)S(1)}, bf16[10,80,128]{2,1,0:T(8,128)(2,1)S(1)}, bf16[10,80,128]{2,1,0:T(8,128)(2,1)S(1)}, bf16[10,80,128]{2,1,0:T(8,128)(2,1)S(1)}, bf16[10,80,128]{2,1,0:T(8,128)(2,1)S(1)}) custom-call(s32[4,16]{1,0:T(4,128)S(1)} %bitcast.18, bf16[10,160,128]{2,1,0:T(8,128)(2,1)S(1)} %bitcast.16), custom_call_target="tpu_custom_call" | custom-call | flops 1 | bytes 1 | tf_op jit(solution)/shard_map/pack_saved/pallas_call | solution.py:558
  12.1 6.9 %collective-permute-done.1.refs_2_ = bf16[8,64,128]{2,1,0:T(8,128)(2,1)S(1)} collective-permute-done((bf16[8,64,128]{2,1,0:T(8,128)(2,1)S(1)}, bf16[8,64,128]{2,1,0:T(8,128)(2,1)S(1)}, u32[]{:S(2)}, u32[]{:S(2)}) %collective-permute-start.1) | collective-permute-done | bytes 131104 | tf_op jit(solution)/shard_map/ppermute | solution.py:507
  19.1 3.1 %collective-permute-start.11 = (bf16[10,80,128]{2,1,0:T(8,128)(2,1)S(1)}, bf16[10,80,128]{2,1,0:T(8,128)(2,1)S(1)}, u32[]{:S(2)}, u32[]{:S(2)}) collective-permute-start(bf16[10,80,128]{2,1,0:T(8,128)(2,1)S(1)} %get-tuple-element.94), channel_id=1, source_target_pairs={{0,4},{4,0},{8,12},{12,8},{1,5},{5,1},{9,13},{13,9},{2,6},{6,2},{1... | collective-permute-start | bytes 614408 | tf_op jit(solution)/shard_map/ppermute | solution.py:507
  24.0 6.5 %worker.1 = (f32[4,2,9,16,256]{4,3,2,1,0:T(8,128)S(1)}, bf16[2,2,9,16,256]{4,3,2,1,0:T(8,128)(2,1)S(1)}, bf16[2,2,9,16,256]{4,3,2,1,0:T(8,128)(2,1)S(1)}) custom-call(s32[4,16]{1,0:T(4,128)S(1)} %bitcast.19, bf16[8,64,128]{2,1,0:T(8,128)(2,1)S(1)} %get-tuple-element.83.refs_0_, bf16[8,64,128]{2,1,0:T(8,128)(2,1)S(1)} %collective-permute-done.2.refs_1_, ...), custom_call_target="tpu_custom_call" | custom-call | flops 1 | bytes 1 | tf_op jit(solution)/shard_map/worker/pallas_call | solution.py:575
  30.8 1.5 %collective-permute-start.13 = (bf16[2,2,9,16,256]{4,3,2,1,0:T(8,128)(2,1)S(1)}, bf16[2,2,9,16,256]{4,3,2,1,0:T(8,128)(2,1)S(1)}, u32[]{:S(2)}, u32[]{:S(2)}) collective-permute-start(bf16[2,2,9,16,256]{4,3,2,1,0:T(8,128)(2,1)S(1)} %get-tuple-element.101), channel_id=1, source_target_pairs={{0,2},{2,0},{1,3},{3,1},{4,6},{6,4},{5,7},{7,5},{8,10},{10,8},{9,1... | collective-permute-start | bytes 884744 | tf_op jit(solution)/shard_map/ppermute | solution.py:502
  32.3 1.4 %collective-permute-start.14 = (bf16[10,80,128]{2,1,0:T(8,128)(2,1)S(1)}, bf16[10,80,128]{2,1,0:T(8,128)(2,1)S(1)}, u32[]{:S(2)}, u32[]{:S(2)}) collective-permute-start(bf16[10,80,128]{2,1,0:T(8,128)(2,1)S(1)} %get-tuple-element.105), channel_id=1, source_target_pairs={{0,12},{4,8},{8,4},{12,0},{1,13},{5,9},{9,5},{13,1},{2,14},{6,10},... | collective-permute-start | bytes 614408 | tf_op jit(solution)/shard_map/ppermute | solution.py:507
  34.8 2.9 %owner_spread.1.refs_8_ = bf16[10,10,32,256]{3,2,1,0:T(8,128)(2,1)S(1)} custom-call(bf16[8,8,32,128]{3,2,1,0:T(8,128)(2,1)S(1)} %bitcast.14, bf16[8,8,32,128]{3,2,1,0:T(8,128)(2,1)S(1)} %collective-permute-done.12.tile_other, bf16[9,128,256]{2,1,0:T(8,128)(2,1)S(1)} %copy-done.1, bf16[9,128,256]{2,1,0:T(8,128)(2,1)S(1)} %collective-permute-done.3.refs_11_.second_other), custom_call_target="tpu_custom_call" | custom-call | flops 1 | bytes 1 | tf_op jit(solution)/shard_map/owner_spread/pallas_call | solution.py:601
  37.8 2.9 %collective-permute-done.13.got = bf16[2,2,9,16,256]{4,3,2,1,0:T(8,128)(2,1)S(1)} collective-permute-done((bf16[2,2,9,16,256]{4,3,2,1,0:T(8,128)(2,1)S(1)}, bf16[2,2,9,16,256]{4,3,2,1,0:T(8,128)(2,1)S(1)}, u32[]{:S(2)}, u32[]{:S(2)}) %collective-permute-start.13) | collective-permute-done | bytes 294944 | tf_op jit(solution)/shard_map/ppermute | solution.py:502
  41.4 1.5 %collective-permute-start.19 = (bf16[2,9,16,256]{3,2,1,0:T(8,128)(2,1)S(1)}, bf16[2,9,16,256]{3,2,1,0:T(8,128)(2,1)S(1)}, u32[]{:S(2)}, u32[]{:S(2)}) collective-permute-start(bf16[2,9,16,256]{3,2,1,0:T(8,128)(2,1)S(1)} %get-tuple-element.112), channel_id=1, source_target_pairs={{0,12},{4,8},{8,4},{12,0},{1,13},{5,9},{9,5},{13,1},{2,14},{6,10},... | collective-permute-start | bytes 442376 | tf_op jit(solution)/shard_map/ppermute | solution.py:507
  42.9 2.3 %collective-permute-start.20 = (bf16[2,9,16,256]{3,2,1,0:T(8,128)(2,1)S(1)}, bf16[2,9,16,256]{3,2,1,0:T(8,128)(2,1)S(1)}, u32[]{:S(2)}, u32[]{:S(2)}) collective-permute-start(bf16[2,9,16,256]{3,2,1,0:T(8,128)(2,1)S(1)} %get-tuple-element.113), channel_id=1, source_target_pairs={{0,8},{4,12},{8,0},{12,4},{1,9},{5,13},{9,1},{13,5},{2,10},{6,14},... | collective-permute-start | bytes 442376 | tf_op jit(solution)/shard_map/ppermute | solution.py:507
  45.2 5.8 %owner_canvas.1 = (f32[68,40,128]{2,1,0:T(8,128)S(1)}, bf16[48,256]{1,0:T(8,128)(2,1)S(1)}, bf16[48,256]{1,0:T(8,128)(2,1)S(1)}) custom-call(s32[4,16]{1,0:T(4,128)S(1)} %bitcast.20, bf16[10,80,128]{2,1,0:T(8,128)(2,1)S(1)} %get-tuple-element.91.refs_0_, bf16[10,80,128]{2,1,0:T(8,128)(2,1)S(1)} %collective-permute-done.11.refs_1_, ...), custom_call_target="tpu_custom_call" | custom-call | flops 1 | bytes 1 | tf_op jit(solution)/shard_map/owner_canvas/pallas_call | solution.py:615
  51.7 7.3 %collective-permute-done.20.got_2 = bf16[2,9,16,256]{3,2,1,0:T(8,128)(2,1)S(1)} collective-permute-done((bf16[2,9,16,256]{3,2,1,0:T(8,128)(2,1)S(1)}, bf16[2,9,16,256]{3,2,1,0:T(8,128)(2,1)S(1)}, u32[]{:S(2)}, u32[]{:S(2)}) %collective-permute-start.20) | collective-permute-done | bytes 147488 | tf_op jit(solution)/shard_map/ppermute | solution.py:507
  59.0 1.0 %collective-permute-done.21.got_1 = bf16[2,9,16,256]{3,2,1,0:T(8,128)(2,1)S(1)} collective-permute-done((bf16[2,9,16,256]{3,2,1,0:T(8,128)(2,1)S(1)}, bf16[2,9,16,256]{3,2,1,0:T(8,128)(2,1)S(1)}, u32[]{:S(2)}, u32[]{:S(2)}) %collective-permute-start.21) | collective-permute-done | bytes 147488 | tf_op jit(solution)/shard_map/ppermute | solution.py:507
  60.8 2.4 %collective-permute-start.25 = (bf16[336,256]{1,0:T(8,128)(2,1)S(1)}, bf16[336,256]{1,0:T(8,128)(2,1)S(1)}, u32[]{:S(2)}, u32[]{:S(2)}) collective-permute-start(bf16[336,256]{1,0:T(8,128)(2,1)S(1)} %get-tuple-element.120), channel_id=1, source_target_pairs={{0,4},{4,0},{8,12},{12,8},{1,5},{5,1},{9,13},{13,9},{2,6},{6,2},{1... | collective-permute-start | bytes 516104 | tf_op jit(solution)/shard_map/ppermute | solution.py:507
  63.2 5.3 %collective-permute-done.23.refs_2_ = bf16[288,256]{1,0:T(8,128)(2,1)S(1)} collective-permute-done((bf16[288,256]{1,0:T(8,128)(2,1)S(1)}, bf16[288,256]{1,0:T(8,128)(2,1)S(1)}, u32[]{:S(2)}, u32[]{:S(2)}) %collective-permute-start.23) | collective-permute-done | bytes 147488 | tf_op jit(solution)/shard_map/ppermute | solution.py:507
  68.4 1.9 %collective-permute-start.24 = (bf16[336,256]{1,0:T(8,128)(2,1)S(1)}, bf16[336,256]{1,0:T(8,128)(2,1)S(1)}, u32[]{:S(2)}, u32[]{:S(2)}) collective-permute-start(bf16[336,256]{1,0:T(8,128)(2,1)S(1)} %get-tuple-element.119), channel_id=1, source_target_pairs={{0,12},{4,8},{8,4},{12,0},{1,13},{5,9},{9,5},{13,1},{2,14},{6,10},... | collective-permute-start | bytes 516104 | tf_op jit(solution)/shard_map/ppermute | solution.py:507
  70.9 1.5 %collective-permute-start.26 = (bf16[288,256]{1,0:T(8,128)(2,1)S(1)}, bf16[288,256]{1,0:T(8,128)(2,1)S(1)}, u32[]{:S(2)}, u32[]{:S(2)}) collective-permute-start(bf16[288,256]{1,0:T(8,128)(2,1)S(1)} %slice.4), channel_id=1, source_target_pairs={{0,2},{2,0},{1,3},{3,1},{4,6},{6,4},{5,7},{7,5},{8,10},{10,8},{9,1... | collective-permute-start | bytes 442376 | tf_op jit(solution)/shard_map/ppermute | solution.py:502
  72.4 4.6 %collective-permute-done.27.refs_6_ = bf16[288,256]{1,0:T(8,128)(2,1)S(1)} collective-permute-done((bf16[288,256]{1,0:T(8,128)(2,1)S(1)}, bf16[288,256]{1,0:T(8,128)(2,1)S(1)}, u32[]{:S(2)}, u32[]{:S(2)}) %collective-permute-start.27) | collective-permute-done | bytes 147488 | tf_op jit(solution)/shard_map/ppermute | solution.py:502
  77.0 1.6 %collective-permute-done.26.refs_5_ = bf16[288,256]{1,0:T(8,128)(2,1)S(1)} collective-permute-done((bf16[288,256]{1,0:T(8,128)(2,1)S(1)}, bf16[288,256]{1,0:T(8,128)(2,1)S(1)}, u32[]{:S(2)}, u32[]{:S(2)}) %collective-permute-start.26) | collective-permute-done | bytes 147488 | tf_op jit(solution)/shard_map/ppermute | solution.py:502
  79.6 1.8 %lay.1 = (bf16[64,32,128]{2,1,0:T(8,128)(2,1)}, f32[64,16,128]{2,1,0:T(8,128)S(1)}, f32[9,128,256]{2,1,0:T(8,128)}, f32[9,128,256]{2,1,0:T(8,128)}) custom-call(bf16[64,32,128]{2,1,0:T(8,128)(2,1)S(1)} %copy-done, f32[68,40,128]{2,1,0:T(8,128)S(1)} %get-tuple-element.109.canvas, bf16[288,256]{1,0:T(8,128)(2,1)S(1)} %get-tuple-element.117.refs_0_, ...), custom_call_target="tpu_custom_call" | custom-call | flops 1 | bytes 1 | tf_op jit(solution)/shard_map/lay/pallas_call | solution.py:660
  81.4 2.8 %collective-permute-done.28.last = bf16[352,256]{1,0:T(8,128)(2,1)S(1)} collective-permute-done((bf16[352,256]{1,0:T(8,128)(2,1)S(1)}, bf16[352,256]{1,0:T(8,128)(2,1)S(1)}, u32[]{:S(2)}, u32[]{:S(2)}) %collective-permute-start.28) | collective-permute-done | bytes 180256 | tf_op jit(solution)/shard_map/ppermute | solution.py:502
  (58 shorter events, 10.2 us)
Async XLA Ops:
  0.6 7.8 %collective-permute-start.3 = (bf16[9,128,256]{2,1,0:T(8,128)(2,1)}, bf16[9,128,256]{2,1,0:T(8,128)(2,1)S(1)}, u32[]{:S(2)}, u32[]{:S(2)}) collective-permute-start(bf16[9,128,256]{2,1,0:T(8,128)(2,1)} %second.1), channel_id=1, source_target_pairs={{0,1},{1,0},{2,3},{3,2},{4,5},{5,4},{6,7},{7,6},{8,9},{9,8},{10,11... | collective-permute-start | bytes 1769480 | tf_op jit(solution)/shard_map/ppermute | solution.py:502
  1.2 21.5 %collective-permute-start.8 = (bf16[10,160,128]{2,1,0:T(8,128)(2,1)}, bf16[10,160,128]{2,1,0:T(8,128)(2,1)S(1)}, u32[]{:S(2)}, u32[]{:S(2)}) collective-permute-start(bf16[10,160,128]{2,1,0:T(8,128)(2,1)} %bitcast.15), channel_id=1, source_target_pairs={{0,1},{1,0},{2,3},{3,2},{4,5},{5,4},{6,7},{7,6},{8,9},{9,8},{10,11... | collective-permute-start | bytes 1228808 | tf_op jit(solution)/shard_map/ppermute | solution.py:502
  2.7 9.5 %collective-permute-start = (bf16[8,64,128]{2,1,0:T(8,128)(2,1)S(1)}, bf16[8,64,128]{2,1,0:T(8,128)(2,1)S(1)}, u32[]{:S(2)}, u32[]{:S(2)}) collective-permute-start(bf16[8,64,128]{2,1,0:T(8,128)(2,1)S(1)} %get-tuple-element.73), channel_id=1, source_target_pairs={{0,12},{4,8},{8,4},{12,0},{1,13},{5,9},{9,5},{13,1},{2,14},{6,10},... | collective-permute-start | bytes 393224 | tf_op jit(solution)/shard_map/ppermute | solution.py:507
  7.7 11.3 %collective-permute-start.1 = (bf16[8,64,128]{2,1,0:T(8,128)(2,1)S(1)}, bf16[8,64,128]{2,1,0:T(8,128)(2,1)S(1)}, u32[]{:S(2)}, u32[]{:S(2)}) collective-permute-start(bf16[8,64,128]{2,1,0:T(8,128)(2,1)S(1)} %get-tuple-element.74), channel_id=1, source_target_pairs={{0,8},{4,12},{8,0},{12,4},{1,9},{5,13},{9,1},{13,5},{2,10},{6,14},... | collective-permute-start | bytes 393224 | tf_op jit(solution)/shard_map/ppermute | solution.py:507
  7.8 11.3 %collective-permute-start.2 = (bf16[8,64,128]{2,1,0:T(8,128)(2,1)S(1)}, bf16[8,64,128]{2,1,0:T(8,128)(2,1)S(1)}, u32[]{:S(2)}, u32[]{:S(2)}) collective-permute-start(bf16[8,64,128]{2,1,0:T(8,128)(2,1)S(1)} %get-tuple-element.75), channel_id=1, source_target_pairs={{0,4},{4,0},{8,12},{12,8},{1,5},{5,1},{9,13},{13,9},{2,6},{6,2},{1... | collective-permute-start | bytes 393224 | tf_op jit(solution)/shard_map/ppermute | solution.py:507
  8.4 10.7 %collective-permute-start.4 = (bf16[8,64,128]{2,1,0:T(8,128)(2,1)S(1)}, bf16[8,64,128]{2,1,0:T(8,128)(2,1)S(1)}, u32[]{:S(2)}, u32[]{:S(2)}) collective-permute-start(bf16[8,64,128]{2,1,0:T(8,128)(2,1)S(1)} %get-tuple-element.83.refs_0_), channel_id=1, source_target_pairs={{0,1},{1,0},{2,3},{3,2},{4,5},{5,4},{6,7},{7,6},{8,9},{9,8},{10,11... | collective-permute-start | bytes 393224 | tf_op jit(solution)/shard_map/ppermute | solution.py:502
  19.1 11.5 %collective-permute-start.10 = (bf16[10,80,128]{2,1,0:T(8,128)(2,1)S(1)}, bf16[10,80,128]{2,1,0:T(8,128)(2,1)S(1)}, u32[]{:S(2)}, u32[]{:S(2)}) collective-permute-start(bf16[10,80,128]{2,1,0:T(8,128)(2,1)S(1)} %get-tuple-element.93), channel_id=1, source_target_pairs={{0,8},{4,12},{8,0},{12,4},{1,9},{5,13},{9,1},{13,5},{2,10},{6,14},... | collective-permute-start | bytes 614408 | tf_op jit(solution)/shard_map/ppermute | solution.py:507
  19.1 11.6 %collective-permute-start.11 = (bf16[10,80,128]{2,1,0:T(8,128)(2,1)S(1)}, bf16[10,80,128]{2,1,0:T(8,128)(2,1)S(1)}, u32[]{:S(2)}, u32[]{:S(2)}) collective-permute-start(bf16[10,80,128]{2,1,0:T(8,128)(2,1)S(1)} %get-tuple-element.94), channel_id=1, source_target_pairs={{0,4},{4,0},{8,12},{12,8},{1,5},{5,1},{9,13},{13,9},{2,6},{6,2},{1... | collective-permute-start | bytes 614408 | tf_op jit(solution)/shard_map/ppermute | solution.py:507
  30.8 9.8 %collective-permute-start.13 = (bf16[2,2,9,16,256]{4,3,2,1,0:T(8,128)(2,1)S(1)}, bf16[2,2,9,16,256]{4,3,2,1,0:T(8,128)(2,1)S(1)}, u32[]{:S(2)}, u32[]{:S(2)}) collective-permute-start(bf16[2,2,9,16,256]{4,3,2,1,0:T(8,128)(2,1)S(1)} %get-tuple-element.101), channel_id=1, source_target_pairs={{0,2},{2,0},{1,3},{3,1},{4,6},{6,4},{5,7},{7,5},{8,10},{10,8},{9,1... | collective-permute-start | bytes 884744 | tf_op jit(solution)/shard_map/ppermute | solution.py:502
  32.3 9.0 %collective-permute-start.14 = (bf16[10,80,128]{2,1,0:T(8,128)(2,1)S(1)}, bf16[10,80,128]{2,1,0:T(8,128)(2,1)S(1)}, u32[]{:S(2)}, u32[]{:S(2)}) collective-permute-start(bf16[10,80,128]{2,1,0:T(8,128)(2,1)S(1)} %get-tuple-element.105), channel_id=1, source_target_pairs={{0,12},{4,8},{8,4},{12,0},{1,13},{5,9},{9,5},{13,1},{2,14},{6,10},... | collective-permute-start | bytes 614408 | tf_op jit(solution)/shard_map/ppermute | solution.py:507
  33.8 17.3 %collective-permute-start.9 = (bf16[2,2,9,16,256]{4,3,2,1,0:T(8,128)(2,1)S(1)}, bf16[2,2,9,16,256]{4,3,2,1,0:T(8,128)(2,1)S(1)}, u32[]{:S(2)}, u32[]{:S(2)}) collective-permute-start(bf16[2,2,9,16,256]{4,3,2,1,0:T(8,128)(2,1)S(1)} %get-tuple-element.90), channel_id=1, source_target_pairs={{0,2},{2,0},{1,3},{3,1},{4,6},{6,4},{5,7},{7,5},{8,10},{10,8},{9,1... | collective-permute-start | bytes 884744 | tf_op jit(solution)/shard_map/ppermute | solution.py:502
  34.3 7.1 %collective-permute-start.15 = (bf16[10,80,128]{2,1,0:T(8,128)(2,1)S(1)}, bf16[10,80,128]{2,1,0:T(8,128)(2,1)S(1)}, u32[]{:S(2)}, u32[]{:S(2)}) collective-permute-start(bf16[10,80,128]{2,1,0:T(8,128)(2,1)S(1)} %get-tuple-element.91.refs_0_), channel_id=1, source_target_pairs={{0,1},{1,0},{2,3},{3,2},{4,5},{5,4},{6,7},{7,6},{8,9},{9,8},{10,11... | collective-permute-start | bytes 614408 | tf_op jit(solution)/shard_map/ppermute | solution.py:502
  34.3 8.6 %collective-permute-start.16 = (bf16[10,80,128]{2,1,0:T(8,128)(2,1)S(1)}, bf16[10,80,128]{2,1,0:T(8,128)(2,1)S(1)}, u32[]{:S(2)}, u32[]{:S(2)}) collective-permute-start(bf16[10,80,128]{2,1,0:T(8,128)(2,1)S(1)} %collective-permute-done.11.refs_1_), channel_id=1, source_target_pairs={{0,1},{1,0},{2,3},{3,2},{4,5},{5,4},{6,7},{7,6},{8,9},{9,8},{10,11... | collective-permute-start | bytes 614408 | tf_op jit(solution)/shard_map/ppermute | solution.py:502
  40.6 4.6 %collective-permute-start.17 = (bf16[10,80,128]{2,1,0:T(8,128)(2,1)S(1)}, bf16[10,80,128]{2,1,0:T(8,128)(2,1)S(1)}, u32[]{:S(2)}, u32[]{:S(2)}) collective-permute-start(bf16[10,80,128]{2,1,0:T(8,128)(2,1)S(1)} %collective-permute-done.10.refs_2_), channel_id=1, source_target_pairs={{0,1},{1,0},{2,3},{3,2},{4,5},{5,4},{6,7},{7,6},{8,9},{9,8},{10,11... | collective-permute-start | bytes 614408 | tf_op jit(solution)/shard_map/ppermute | solution.py:502
  41.4 10.4 %collective-permute-start.19 = (bf16[2,9,16,256]{3,2,1,0:T(8,128)(2,1)S(1)}, bf16[2,9,16,256]{3,2,1,0:T(8,128)(2,1)S(1)}, u32[]{:S(2)}, u32[]{:S(2)}) collective-permute-start(bf16[2,9,16,256]{3,2,1,0:T(8,128)(2,1)S(1)} %get-tuple-element.112), channel_id=1, source_target_pairs={{0,12},{4,8},{8,4},{12,0},{1,13},{5,9},{9,5},{13,1},{2,14},{6,10},... | collective-permute-start | bytes 442376 | tf_op jit(solution)/shard_map/ppermute | solution.py:507
  42.9 16.1 %collective-permute-start.20 = (bf16[2,9,16,256]{3,2,1,0:T(8,128)(2,1)S(1)}, bf16[2,9,16,256]{3,2,1,0:T(8,128)(2,1)S(1)}, u32[]{:S(2)}, u32[]{:S(2)}) collective-permute-start(bf16[2,9,16,256]{3,2,1,0:T(8,128)(2,1)S(1)} %get-tuple-element.113), channel_id=1, source_target_pairs={{0,8},{4,12},{8,0},{12,4},{1,9},{5,13},{9,1},{13,5},{2,10},{6,14},... | collective-permute-start | bytes 442376 | tf_op jit(solution)/shard_map/ppermute | solution.py:507
  51.1 8.9 %collective-permute-start.21 = (bf16[2,9,16,256]{3,2,1,0:T(8,128)(2,1)S(1)}, bf16[2,9,16,256]{3,2,1,0:T(8,128)(2,1)S(1)}, u32[]{:S(2)}, u32[]{:S(2)}) collective-permute-start(bf16[2,9,16,256]{3,2,1,0:T(8,128)(2,1)S(1)} %get-tuple-element.114), channel_id=1, source_target_pairs={{0,4},{4,0},{8,12},{12,8},{1,5},{5,1},{9,13},{13,9},{2,6},{6,2},{1... | collective-permute-start | bytes 442376 | tf_op jit(solution)/shard_map/ppermute | solution.py:507
  60.1 8.3 %collective-permute-start.23 = (bf16[288,256]{1,0:T(8,128)(2,1)S(1)}, bf16[288,256]{1,0:T(8,128)(2,1)S(1)}, u32[]{:S(2)}, u32[]{:S(2)}) collective-permute-start(bf16[288,256]{1,0:T(8,128)(2,1)S(1)} %get-tuple-element.117.refs_0_), channel_id=1, source_target_pairs={{0,8},{4,12},{8,0},{12,4},{1,9},{5,13},{9,1},{13,5},{2,10},{6,14},... | collective-permute-start | bytes 442376 | tf_op jit(solution)/shard_map/ppermute | solution.py:507
  60.2 8.2 %collective-permute-start.22 = (bf16[288,256]{1,0:T(8,128)(2,1)S(1)}, bf16[288,256]{1,0:T(8,128)(2,1)S(1)}, u32[]{:S(2)}, u32[]{:S(2)}) collective-permute-start(bf16[288,256]{1,0:T(8,128)(2,1)S(1)} %get-tuple-element.117.refs_0_), channel_id=1, source_target_pairs={{0,2},{2,0},{1,3},{3,1},{4,6},{6,4},{5,7},{7,5},{8,10},{10,8},{9,1... | collective-permute-start | bytes 442376 | tf_op jit(solution)/shard_map/ppermute | solution.py:502
  60.8 10.1 %collective-permute-start.25 = (bf16[336,256]{1,0:T(8,128)(2,1)S(1)}, bf16[336,256]{1,0:T(8,128)(2,1)S(1)}, u32[]{:S(2)}, u32[]{:S(2)}) collective-permute-start(bf16[336,256]{1,0:T(8,128)(2,1)S(1)} %get-tuple-element.120), channel_id=1, source_target_pairs={{0,4},{4,0},{8,12},{12,8},{1,5},{5,1},{9,13},{13,9},{2,6},{6,2},{1... | collective-permute-start | bytes 516104 | tf_op jit(solution)/shard_map/ppermute | solution.py:507
  68.4 8.6 %collective-permute-start.24 = (bf16[336,256]{1,0:T(8,128)(2,1)S(1)}, bf16[336,256]{1,0:T(8,128)(2,1)S(1)}, u32[]{:S(2)}, u32[]{:S(2)}) collective-permute-start(bf16[336,256]{1,0:T(8,128)(2,1)S(1)} %get-tuple-element.119), channel_id=1, source_target_pairs={{0,12},{4,8},{8,4},{12,0},{1,13},{5,9},{9,5},{13,1},{2,14},{6,10},... | collective-permute-start | bytes 516104 | tf_op jit(solution)/shard_map/ppermute | solution.py:507
  70.3 6.7 %collective-permute-start.27 = (bf16[288,256]{1,0:T(8,128)(2,1)S(1)}, bf16[288,256]{1,0:T(8,128)(2,1)S(1)}, u32[]{:S(2)}, u32[]{:S(2)}) collective-permute-start(bf16[288,256]{1,0:T(8,128)(2,1)S(1)} %collective-permute-done.23.refs_2_), channel_id=1, source_target_pairs={{0,2},{2,0},{1,3},{3,1},{4,6},{6,4},{5,7},{7,5},{8,10},{10,8},{9,1... | collective-permute-start | bytes 442376 | tf_op jit(solution)/shard_map/ppermute | solution.py:502
  70.9 7.7 %collective-permute-start.26 = (bf16[288,256]{1,0:T(8,128)(2,1)S(1)}, bf16[288,256]{1,0:T(8,128)(2,1)S(1)}, u32[]{:S(2)}, u32[]{:S(2)}) collective-permute-start(bf16[288,256]{1,0:T(8,128)(2,1)S(1)} %slice.4), channel_id=1, source_target_pairs={{0,2},{2,0},{1,3},{3,1},{4,6},{6,4},{5,7},{7,5},{8,10},{10,8},{9,1... | collective-permute-start | bytes 442376 | tf_op jit(solution)/shard_map/ppermute | solution.py:502
  78.6 5.6 %collective-permute-start.28 = (bf16[352,256]{1,0:T(8,128)(2,1)S(1)}, bf16[352,256]{1,0:T(8,128)(2,1)S(1)}, u32[]{:S(2)}, u32[]{:S(2)}) collective-permute-start(bf16[352,256]{1,0:T(8,128)(2,1)S(1)} %column_message.1), channel_id=1, source_target_pairs={{0,2},{2,0},{1,3},{3,1},{4,6},{6,4},{5,7},{7,5},{8,10},{10,8},{9,1... | collective-permute-start | bytes 540680 | tf_op jit(solution)/shard_map/ppermute | solution.py:502
  (11 other events, 58.4 us)

commit v21 on v20

--- a/solution.py
+++ b/solution.py
@@ -594,7 +594,7 @@
 
     if permuted:
         kept, near, far = terms
-        far, at_owner[2], at_owner[1] = tie((far, at_owner[2], at_owner[1]))
+        far, at_owner[1], at_owner[2] = tie((far, at_owner[1], at_owner[2]))
         far, tile_mine, tile_here = tie((far, tile, tile))
     else:
         terms, tile_mine, tile_here = tie((terms, tile, tile))

time: 85.4 us -> 86.1 us (level)
    ppermute x12, starting transfers between devices: 19 us -> 19.9 us  [flip(): return lax.ppermute(value, axis, [(i, i ^ step) for i in range(size)])]
  transfers between devices with their start and end apart: 29 -> 29, of which waited for: 14 -> 14; matrix products, arithmetic and copies ran while one was open for 0% -> 0% of each run, Pallas kernels for 24% -> 23%
where the time goes in v21:
time: 86.1 us; the launch traced here: 85.9 us
  waiting for transfers between devices  35.5 us (41%)
  starting transfers between devices  26.7 us (31%)
  Pallas kernels  21.1 us (25%)
  local copies, waits for them, and re-layouts  1.71 us (2%)
  between operations  0.94 us (1%)
    ppermute x12, waiting for transfers between devices, flip(): return lax.ppermute(value, axis, [(i, i ^ step) for i in range(size)])  22.4 us
    ppermute x12, starting transfers between devices, flip(): return lax.ppermute(value, axis, [(i, i ^ step) for i in range(size)])  19.9 us
    ppermute x17, waiting for transfers between devices, swap(): return lax.ppermute(value, axis, [(0, 1), (1, 0)])  13 us
    ppermute x17, starting transfers between devices, swap(): return lax.ppermute(value, axis, [(0, 1), (1, 0)])  6.73 us
    pallas_call x1, Pallas kernels, shards(): call(functools.partial(worker, scale, owners, columns, capacity, permuted...  6.52 us
    pallas_call x1, Pallas kernels, owner(): call(functools.partial(owner_canvas, owners, capacity, wide, permuted), [...  5.8 us
    pallas_call x1, Pallas kernels, shards(): call(owner_spread, shape((MIDDLE, MIDDLE, TILE_BLOCKS, FULL), BF16), [VME...  2.93 us
    pallas_call x1, Pallas kernels, shards(): call(lay, [shape(grad_out.shape, BF16), shape(slab, F32)] + weights, [VME...  1.76 us
  transfers between devices with their start and end apart: 29, of which 14 were waited for; matrix products, arithmetic and copies ran while one was open for 0% of the time, Pallas kernels for 23%

profile of v21, /device:TPU:0, one launch (start us, length us, event | category | flops | bytes accessed | tf_op | source)
XLA Modules:
  0.0 85.9 jit_solution(13105573793677112706)
XLA Ops:
  1.2 1.4 %pack_cotangents.1 = (bf16[8,64,128]{2,1,0:T(8,128)(2,1)S(1)}, bf16[8,64,128]{2,1,0:T(8,128)(2,1)S(1)}, bf16[8,64,128]{2,1,0:T(8,128)(2,1)S(1)}, bf16[8,64,128]{2,1,0:T(8,128)(2,1)S(1)}) custom-call(s32[4,16]{1,0:T(4,128)} %bitcast.17, bf16[8,8,32,128]{3,2,1,0:T(8,128)(2,1)} %bitcast.12), custom_call_target="tpu_custom_call" | custom-call | flops 1 | bytes 1 | tf_op jit(solution)/shard_map/pack_cotangents/pallas_call | solution.py:539
  2.7 5.1 %collective-permute-start = (bf16[8,64,128]{2,1,0:T(8,128)(2,1)S(1)}, bf16[8,64,128]{2,1,0:T(8,128)(2,1)S(1)}, u32[]{:S(2)}, u32[]{:S(2)}) collective-permute-start(bf16[8,64,128]{2,1,0:T(8,128)(2,1)S(1)} %get-tuple-element.73), channel_id=1, source_target_pairs={{0,12},{4,8},{8,4},{12,0},{1,13},{5,9},{9,5},{13,1},{2,14},{6,10},... | collective-permute-start | bytes 393224 | tf_op jit(solution)/shard_map/ppermute | solution.py:507
  8.4 1.0 %copy-done.3 = bf16[1,1,16,10,10,128]{5,2,4,3,1,0:T(8,128)(2,1)S(1)} copy-done((bf16[1,1,16,10,10,128]{5,2,4,3,1,0:T(8,128)(2,1)S(1)}, bf16[1,1,16,10,10,128]{5,2,4,3,1,0:T(8,128)(2,1)}, u32[]{:S(2)}) %copy-start.3) | copy-done | bytes 409624
  10.1 1.6 %pack_saved.1 = (bf16[10,160,128]{2,1,0:T(8,128)(2,1)S(1)}, bf16[10,80,128]{2,1,0:T(8,128)(2,1)S(1)}, bf16[10,80,128]{2,1,0:T(8,128)(2,1)S(1)}, bf16[10,80,128]{2,1,0:T(8,128)(2,1)S(1)}, bf16[10,80,128]{2,1,0:T(8,128)(2,1)S(1)}) custom-call(s32[4,16]{1,0:T(4,128)S(1)} %bitcast.18, bf16[10,160,128]{2,1,0:T(8,128)(2,1)S(1)} %bitcast.16), custom_call_target="tpu_custom_call" | custom-call | flops 1 | bytes 1 | tf_op jit(solution)/shard_map/pack_saved/pallas_call | solution.py:558
  12.1 6.9 %collective-permute-done.1.refs_2_ = bf16[8,64,128]{2,1,0:T(8,128)(2,1)S(1)} collective-permute-done((bf16[8,64,128]{2,1,0:T(8,128)(2,1)S(1)}, bf16[8,64,128]{2,1,0:T(8,128)(2,1)S(1)}, u32[]{:S(2)}, u32[]{:S(2)}) %collective-permute-start.1) | collective-permute-done | bytes 131104 | tf_op jit(solution)/shard_map/ppermute | solution.py:507
  19.1 3.1 %collective-permute-start.11 = (bf16[10,80,128]{2,1,0:T(8,128)(2,1)S(1)}, bf16[10,80,128]{2,1,0:T(8,128)(2,1)S(1)}, u32[]{:S(2)}, u32[]{:S(2)}) collective-permute-start(bf16[10,80,128]{2,1,0:T(8,128)(2,1)S(1)} %get-tuple-element.94), channel_id=1, source_target_pairs={{0,8},{4,12},{8,0},{12,4},{1,9},{5,13},{9,1},{13,5},{2,10},{6,14},... | collective-permute-start | bytes 614408 | tf_op jit(solution)/shard_map/ppermute | solution.py:507
  24.0 6.5 %worker.1 = (f32[4,2,9,16,256]{4,3,2,1,0:T(8,128)S(1)}, bf16[2,2,9,16,256]{4,3,2,1,0:T(8,128)(2,1)S(1)}, bf16[2,2,9,16,256]{4,3,2,1,0:T(8,128)(2,1)S(1)}) custom-call(s32[4,16]{1,0:T(4,128)S(1)} %bitcast.19, bf16[8,64,128]{2,1,0:T(8,128)(2,1)S(1)} %get-tuple-element.83.refs_0_, bf16[8,64,128]{2,1,0:T(8,128)(2,1)S(1)} %collective-permute-done.2.refs_1_, ...), custom_call_target="tpu_custom_call" | custom-call | flops 1 | bytes 1 | tf_op jit(solution)/shard_map/worker/pallas_call | solution.py:575
  30.8 1.5 %collective-permute-start.13 = (bf16[2,2,9,16,256]{4,3,2,1,0:T(8,128)(2,1)S(1)}, bf16[2,2,9,16,256]{4,3,2,1,0:T(8,128)(2,1)S(1)}, u32[]{:S(2)}, u32[]{:S(2)}) collective-permute-start(bf16[2,2,9,16,256]{4,3,2,1,0:T(8,128)(2,1)S(1)} %get-tuple-element.101), channel_id=1, source_target_pairs={{0,2},{2,0},{1,3},{3,1},{4,6},{6,4},{5,7},{7,5},{8,10},{10,8},{9,1... | collective-permute-start | bytes 884744 | tf_op jit(solution)/shard_map/ppermute | solution.py:502
  32.3 2.4 %collective-permute-start.14 = (bf16[10,80,128]{2,1,0:T(8,128)(2,1)S(1)}, bf16[10,80,128]{2,1,0:T(8,128)(2,1)S(1)}, u32[]{:S(2)}, u32[]{:S(2)}) collective-permute-start(bf16[10,80,128]{2,1,0:T(8,128)(2,1)S(1)} %get-tuple-element.105), channel_id=1, source_target_pairs={{0,12},{4,8},{8,4},{12,0},{1,13},{5,9},{9,5},{13,1},{2,14},{6,10},... | collective-permute-start | bytes 614408 | tf_op jit(solution)/shard_map/ppermute | solution.py:507
  35.8 2.9 %owner_spread.1.refs_8_ = bf16[10,10,32,256]{3,2,1,0:T(8,128)(2,1)S(1)} custom-call(bf16[8,8,32,128]{3,2,1,0:T(8,128)(2,1)S(1)} %bitcast.14, bf16[8,8,32,128]{3,2,1,0:T(8,128)(2,1)S(1)} %collective-permute-done.12.tile_other, bf16[9,128,256]{2,1,0:T(8,128)(2,1)S(1)} %copy-done.1, bf16[9,128,256]{2,1,0:T(8,128)(2,1)S(1)} %collective-permute-done.3.refs_11_.second_other), custom_call_target="tpu_custom_call" | custom-call | flops 1 | bytes 1 | tf_op jit(solution)/shard_map/owner_spread/pallas_call | solution.py:601
  38.7 1.9 %collective-permute-done.13.got = bf16[2,2,9,16,256]{4,3,2,1,0:T(8,128)(2,1)S(1)} collective-permute-done((bf16[2,2,9,16,256]{4,3,2,1,0:T(8,128)(2,1)S(1)}, bf16[2,2,9,16,256]{4,3,2,1,0:T(8,128)(2,1)S(1)}, u32[]{:S(2)}, u32[]{:S(2)}) %collective-permute-start.13) | collective-permute-done | bytes 294944 | tf_op jit(solution)/shard_map/ppermute | solution.py:502
  41.4 2.4 %collective-permute-start.19 = (bf16[2,9,16,256]{3,2,1,0:T(8,128)(2,1)S(1)}, bf16[2,9,16,256]{3,2,1,0:T(8,128)(2,1)S(1)}, u32[]{:S(2)}, u32[]{:S(2)}) collective-permute-start(bf16[2,9,16,256]{3,2,1,0:T(8,128)(2,1)S(1)} %get-tuple-element.112), channel_id=1, source_target_pairs={{0,12},{4,8},{8,4},{12,0},{1,13},{5,9},{9,5},{13,1},{2,14},{6,10},... | collective-permute-start | bytes 442376 | tf_op jit(solution)/shard_map/ppermute | solution.py:507
  43.8 1.9 %collective-permute-start.20 = (bf16[2,9,16,256]{3,2,1,0:T(8,128)(2,1)S(1)}, bf16[2,9,16,256]{3,2,1,0:T(8,128)(2,1)S(1)}, u32[]{:S(2)}, u32[]{:S(2)}) collective-permute-start(bf16[2,9,16,256]{3,2,1,0:T(8,128)(2,1)S(1)} %get-tuple-element.113), channel_id=1, source_target_pairs={{0,8},{4,12},{8,0},{12,4},{1,9},{5,13},{9,1},{13,5},{2,10},{6,14},... | collective-permute-start | bytes 442376 | tf_op jit(solution)/shard_map/ppermute | solution.py:507
  45.7 5.8 %owner_canvas.1 = (f32[68,40,128]{2,1,0:T(8,128)S(1)}, bf16[48,256]{1,0:T(8,128)(2,1)S(1)}, bf16[48,256]{1,0:T(8,128)(2,1)S(1)}) custom-call(s32[4,16]{1,0:T(4,128)S(1)} %bitcast.20, bf16[10,80,128]{2,1,0:T(8,128)(2,1)S(1)} %get-tuple-element.91.refs_0_, bf16[10,80,128]{2,1,0:T(8,128)(2,1)S(1)} %collective-permute-done.10.refs_1_, ...), custom_call_target="tpu_custom_call" | custom-call | flops 1 | bytes 1 | tf_op jit(solution)/shard_map/owner_canvas/pallas_call | solution.py:615
  51.8 7.3 %collective-permute-done.20.got_2 = bf16[2,9,16,256]{3,2,1,0:T(8,128)(2,1)S(1)} collective-permute-done((bf16[2,9,16,256]{3,2,1,0:T(8,128)(2,1)S(1)}, bf16[2,9,16,256]{3,2,1,0:T(8,128)(2,1)S(1)}, u32[]{:S(2)}, u32[]{:S(2)}) %collective-permute-start.20) | collective-permute-done | bytes 147488 | tf_op jit(solution)/shard_map/ppermute | solution.py:507
  59.0 1.5 %collective-permute-done.21.got_1 = bf16[2,9,16,256]{3,2,1,0:T(8,128)(2,1)S(1)} collective-permute-done((bf16[2,9,16,256]{3,2,1,0:T(8,128)(2,1)S(1)}, bf16[2,9,16,256]{3,2,1,0:T(8,128)(2,1)S(1)}, u32[]{:S(2)}, u32[]{:S(2)}) %collective-permute-start.21) | collective-permute-done | bytes 147488 | tf_op jit(solution)/shard_map/ppermute | solution.py:507
  61.3 1.8 %collective-permute-start.25 = (bf16[336,256]{1,0:T(8,128)(2,1)S(1)}, bf16[336,256]{1,0:T(8,128)(2,1)S(1)}, u32[]{:S(2)}, u32[]{:S(2)}) collective-permute-start(bf16[336,256]{1,0:T(8,128)(2,1)S(1)} %get-tuple-element.120), channel_id=1, source_target_pairs={{0,4},{4,0},{8,12},{12,8},{1,5},{5,1},{9,13},{13,9},{2,6},{6,2},{1... | collective-permute-start | bytes 516104 | tf_op jit(solution)/shard_map/ppermute | solution.py:507
  63.1 5.4 %collective-permute-done.23.refs_2_ = bf16[288,256]{1,0:T(8,128)(2,1)S(1)} collective-permute-done((bf16[288,256]{1,0:T(8,128)(2,1)S(1)}, bf16[288,256]{1,0:T(8,128)(2,1)S(1)}, u32[]{:S(2)}, u32[]{:S(2)}) %collective-permute-start.23) | collective-permute-done | bytes 147488 | tf_op jit(solution)/shard_map/ppermute | solution.py:507
  68.5 2.4 %collective-permute-start.24 = (bf16[336,256]{1,0:T(8,128)(2,1)S(1)}, bf16[336,256]{1,0:T(8,128)(2,1)S(1)}, u32[]{:S(2)}, u32[]{:S(2)}) collective-permute-start(bf16[336,256]{1,0:T(8,128)(2,1)S(1)} %get-tuple-element.119), channel_id=1, source_target_pairs={{0,12},{4,8},{8,4},{12,0},{1,13},{5,9},{9,5},{13,1},{2,14},{6,10},... | collective-permute-start | bytes 516104 | tf_op jit(solution)/shard_map/ppermute | solution.py:507
  71.1 1.8 %collective-permute-start.26 = (bf16[288,256]{1,0:T(8,128)(2,1)S(1)}, bf16[288,256]{1,0:T(8,128)(2,1)S(1)}, u32[]{:S(2)}, u32[]{:S(2)}) collective-permute-start(bf16[288,256]{1,0:T(8,128)(2,1)S(1)} %slice.4), channel_id=1, source_target_pairs={{0,2},{2,0},{1,3},{3,1},{4,6},{6,4},{5,7},{7,5},{8,10},{10,8},{9,1... | collective-permute-start | bytes 442376 | tf_op jit(solution)/shard_map/ppermute | solution.py:502
  73.0 4.7 %collective-permute-done.27.refs_6_ = bf16[288,256]{1,0:T(8,128)(2,1)S(1)} collective-permute-done((bf16[288,256]{1,0:T(8,128)(2,1)S(1)}, bf16[288,256]{1,0:T(8,128)(2,1)S(1)}, u32[]{:S(2)}, u32[]{:S(2)}) %collective-permute-start.27) | collective-permute-done | bytes 147488 | tf_op jit(solution)/shard_map/ppermute | solution.py:502
  77.6 1.6 %collective-permute-done.26.refs_5_ = bf16[288,256]{1,0:T(8,128)(2,1)S(1)} collective-permute-done((bf16[288,256]{1,0:T(8,128)(2,1)S(1)}, bf16[288,256]{1,0:T(8,128)(2,1)S(1)}, u32[]{:S(2)}, u32[]{:S(2)}) %collective-permute-start.26) | collective-permute-done | bytes 147488 | tf_op jit(solution)/shard_map/ppermute | solution.py:502
  79.7 1.8 %lay.1 = (bf16[64,32,128]{2,1,0:T(8,128)(2,1)}, f32[64,16,128]{2,1,0:T(8,128)S(1)}, f32[9,128,256]{2,1,0:T(8,128)}, f32[9,128,256]{2,1,0:T(8,128)}) custom-call(bf16[64,32,128]{2,1,0:T(8,128)(2,1)S(1)} %copy-done, f32[68,40,128]{2,1,0:T(8,128)S(1)} %get-tuple-element.109.canvas, bf16[288,256]{1,0:T(8,128)(2,1)S(1)} %get-tuple-element.117.refs_0_, ...), custom_call_target="tpu_custom_call" | custom-call | flops 1 | bytes 1 | tf_op jit(solution)/shard_map/lay/pallas_call | solution.py:660
  81.4 3.5 %collective-permute-done.28.last = bf16[352,256]{1,0:T(8,128)(2,1)S(1)} collective-permute-done((bf16[352,256]{1,0:T(8,128)(2,1)S(1)}, bf16[352,256]{1,0:T(8,128)(2,1)S(1)}, u32[]{:S(2)}, u32[]{:S(2)}) %collective-permute-start.28) | collective-permute-done | bytes 180256 | tf_op jit(solution)/shard_map/ppermute | solution.py:502
  (58 shorter events, 8.9 us)
Async XLA Ops:
  0.6 7.8 %collective-permute-start.3 = (bf16[9,128,256]{2,1,0:T(8,128)(2,1)}, bf16[9,128,256]{2,1,0:T(8,128)(2,1)S(1)}, u32[]{:S(2)}, u32[]{:S(2)}) collective-permute-start(bf16[9,128,256]{2,1,0:T(8,128)(2,1)} %second.1), channel_id=1, source_target_pairs={{0,1},{1,0},{2,3},{3,2},{4,5},{5,4},{6,7},{7,6},{8,9},{9,8},{10,11... | collective-permute-start | bytes 1769480 | tf_op jit(solution)/shard_map/ppermute | solution.py:502
  1.2 21.5 %collective-permute-start.8 = (bf16[10,160,128]{2,1,0:T(8,128)(2,1)}, bf16[10,160,128]{2,1,0:T(8,128)(2,1)S(1)}, u32[]{:S(2)}, u32[]{:S(2)}) collective-permute-start(bf16[10,160,128]{2,1,0:T(8,128)(2,1)} %bitcast.15), channel_id=1, source_target_pairs={{0,1},{1,0},{2,3},{3,2},{4,5},{5,4},{6,7},{7,6},{8,9},{9,8},{10,11... | collective-permute-start | bytes 1228808 | tf_op jit(solution)/shard_map/ppermute | solution.py:502
  2.7 9.5 %collective-permute-start = (bf16[8,64,128]{2,1,0:T(8,128)(2,1)S(1)}, bf16[8,64,128]{2,1,0:T(8,128)(2,1)S(1)}, u32[]{:S(2)}, u32[]{:S(2)}) collective-permute-start(bf16[8,64,128]{2,1,0:T(8,128)(2,1)S(1)} %get-tuple-element.73), channel_id=1, source_target_pairs={{0,12},{4,8},{8,4},{12,0},{1,13},{5,9},{9,5},{13,1},{2,14},{6,10},... | collective-permute-start | bytes 393224 | tf_op jit(solution)/shard_map/ppermute | solution.py:507
  7.7 11.3 %collective-permute-start.1 = (bf16[8,64,128]{2,1,0:T(8,128)(2,1)S(1)}, bf16[8,64,128]{2,1,0:T(8,128)(2,1)S(1)}, u32[]{:S(2)}, u32[]{:S(2)}) collective-permute-start(bf16[8,64,128]{2,1,0:T(8,128)(2,1)S(1)} %get-tuple-element.74), channel_id=1, source_target_pairs={{0,8},{4,12},{8,0},{12,4},{1,9},{5,13},{9,1},{13,5},{2,10},{6,14},... | collective-permute-start | bytes 393224 | tf_op jit(solution)/shard_map/ppermute | solution.py:507
  7.8 11.3 %collective-permute-start.2 = (bf16[8,64,128]{2,1,0:T(8,128)(2,1)S(1)}, bf16[8,64,128]{2,1,0:T(8,128)(2,1)S(1)}, u32[]{:S(2)}, u32[]{:S(2)}) collective-permute-start(bf16[8,64,128]{2,1,0:T(8,128)(2,1)S(1)} %get-tuple-element.75), channel_id=1, source_target_pairs={{0,4},{4,0},{8,12},{12,8},{1,5},{5,1},{9,13},{13,9},{2,6},{6,2},{1... | collective-permute-start | bytes 393224 | tf_op jit(solution)/shard_map/ppermute | solution.py:507
  8.4 10.7 %collective-permute-start.4 = (bf16[8,64,128]{2,1,0:T(8,128)(2,1)S(1)}, bf16[8,64,128]{2,1,0:T(8,128)(2,1)S(1)}, u32[]{:S(2)}, u32[]{:S(2)}) collective-permute-start(bf16[8,64,128]{2,1,0:T(8,128)(2,1)S(1)} %get-tuple-element.83.refs_0_), channel_id=1, source_target_pairs={{0,1},{1,0},{2,3},{3,2},{4,5},{5,4},{6,7},{7,6},{8,9},{9,8},{10,11... | collective-permute-start | bytes 393224 | tf_op jit(solution)/shard_map/ppermute | solution.py:502
  19.1 11.5 %collective-permute-start.10 = (bf16[10,80,128]{2,1,0:T(8,128)(2,1)S(1)}, bf16[10,80,128]{2,1,0:T(8,128)(2,1)S(1)}, u32[]{:S(2)}, u32[]{:S(2)}) collective-permute-start(bf16[10,80,128]{2,1,0:T(8,128)(2,1)S(1)} %get-tuple-element.93), channel_id=1, source_target_pairs={{0,4},{4,0},{8,12},{12,8},{1,5},{5,1},{9,13},{13,9},{2,6},{6,2},{1... | collective-permute-start | bytes 614408 | tf_op jit(solution)/shard_map/ppermute | solution.py:507
  19.1 11.7 %collective-permute-start.11 = (bf16[10,80,128]{2,1,0:T(8,128)(2,1)S(1)}, bf16[10,80,128]{2,1,0:T(8,128)(2,1)S(1)}, u32[]{:S(2)}, u32[]{:S(2)}) collective-permute-start(bf16[10,80,128]{2,1,0:T(8,128)(2,1)S(1)} %get-tuple-element.94), channel_id=1, source_target_pairs={{0,8},{4,12},{8,0},{12,4},{1,9},{5,13},{9,1},{13,5},{2,10},{6,14},... | collective-permute-start | bytes 614408 | tf_op jit(solution)/shard_map/ppermute | solution.py:507
  30.8 9.8 %collective-permute-start.13 = (bf16[2,2,9,16,256]{4,3,2,1,0:T(8,128)(2,1)S(1)}, bf16[2,2,9,16,256]{4,3,2,1,0:T(8,128)(2,1)S(1)}, u32[]{:S(2)}, u32[]{:S(2)}) collective-permute-start(bf16[2,2,9,16,256]{4,3,2,1,0:T(8,128)(2,1)S(1)} %get-tuple-element.101), channel_id=1, source_target_pairs={{0,2},{2,0},{1,3},{3,1},{4,6},{6,4},{5,7},{7,5},{8,10},{10,8},{9,1... | collective-permute-start | bytes 884744 | tf_op jit(solution)/shard_map/ppermute | solution.py:502
  32.3 9.1 %collective-permute-start.14 = (bf16[10,80,128]{2,1,0:T(8,128)(2,1)S(1)}, bf16[10,80,128]{2,1,0:T(8,128)(2,1)S(1)}, u32[]{:S(2)}, u32[]{:S(2)}) collective-permute-start(bf16[10,80,128]{2,1,0:T(8,128)(2,1)S(1)} %get-tuple-element.105), channel_id=1, source_target_pairs={{0,12},{4,8},{8,4},{12,0},{1,13},{5,9},{9,5},{13,1},{2,14},{6,10},... | collective-permute-start | bytes 614408 | tf_op jit(solution)/shard_map/ppermute | solution.py:507
  34.7 16.8 %collective-permute-start.9 = (bf16[2,2,9,16,256]{4,3,2,1,0:T(8,128)(2,1)S(1)}, bf16[2,2,9,16,256]{4,3,2,1,0:T(8,128)(2,1)S(1)}, u32[]{:S(2)}, u32[]{:S(2)}) collective-permute-start(bf16[2,2,9,16,256]{4,3,2,1,0:T(8,128)(2,1)S(1)} %get-tuple-element.90), channel_id=1, source_target_pairs={{0,2},{2,0},{1,3},{3,1},{4,6},{6,4},{5,7},{7,5},{8,10},{10,8},{9,1... | collective-permute-start | bytes 884744 | tf_op jit(solution)/shard_map/ppermute | solution.py:502
  35.2 6.2 %collective-permute-start.15 = (bf16[10,80,128]{2,1,0:T(8,128)(2,1)S(1)}, bf16[10,80,128]{2,1,0:T(8,128)(2,1)S(1)}, u32[]{:S(2)}, u32[]{:S(2)}) collective-permute-start(bf16[10,80,128]{2,1,0:T(8,128)(2,1)S(1)} %get-tuple-element.91.refs_0_), channel_id=1, source_target_pairs={{0,1},{1,0},{2,3},{3,2},{4,5},{5,4},{6,7},{7,6},{8,9},{9,8},{10,11... | collective-permute-start | bytes 614408 | tf_op jit(solution)/shard_map/ppermute | solution.py:502
  35.2 8.6 %collective-permute-start.16 = (bf16[10,80,128]{2,1,0:T(8,128)(2,1)S(1)}, bf16[10,80,128]{2,1,0:T(8,128)(2,1)S(1)}, u32[]{:S(2)}, u32[]{:S(2)}) collective-permute-start(bf16[10,80,128]{2,1,0:T(8,128)(2,1)S(1)} %collective-permute-done.10.refs_1_), channel_id=1, source_target_pairs={{0,1},{1,0},{2,3},{3,2},{4,5},{5,4},{6,7},{7,6},{8,9},{9,8},{10,11... | collective-permute-start | bytes 614408 | tf_op jit(solution)/shard_map/ppermute | solution.py:502
  40.6 5.1 %collective-permute-start.17 = (bf16[10,80,128]{2,1,0:T(8,128)(2,1)S(1)}, bf16[10,80,128]{2,1,0:T(8,128)(2,1)S(1)}, u32[]{:S(2)}, u32[]{:S(2)}) collective-permute-start(bf16[10,80,128]{2,1,0:T(8,128)(2,1)S(1)} %collective-permute-done.11.refs_2_), channel_id=1, source_target_pairs={{0,1},{1,0},{2,3},{3,2},{4,5},{5,4},{6,7},{7,6},{8,9},{9,8},{10,11... | collective-permute-start | bytes 614408 | tf_op jit(solution)/shard_map/ppermute | solution.py:502
  41.4 10.4 %collective-permute-start.19 = (bf16[2,9,16,256]{3,2,1,0:T(8,128)(2,1)S(1)}, bf16[2,9,16,256]{3,2,1,0:T(8,128)(2,1)S(1)}, u32[]{:S(2)}, u32[]{:S(2)}) collective-permute-start(bf16[2,9,16,256]{3,2,1,0:T(8,128)(2,1)S(1)} %get-tuple-element.112), channel_id=1, source_target_pairs={{0,12},{4,8},{8,4},{12,0},{1,13},{5,9},{9,5},{13,1},{2,14},{6,10},... | collective-permute-start | bytes 442376 | tf_op jit(solution)/shard_map/ppermute | solution.py:507
  43.8 15.2 %collective-permute-start.20 = (bf16[2,9,16,256]{3,2,1,0:T(8,128)(2,1)S(1)}, bf16[2,9,16,256]{3,2,1,0:T(8,128)(2,1)S(1)}, u32[]{:S(2)}, u32[]{:S(2)}) collective-permute-start(bf16[2,9,16,256]{3,2,1,0:T(8,128)(2,1)S(1)} %get-tuple-element.113), channel_id=1, source_target_pairs={{0,8},{4,12},{8,0},{12,4},{1,9},{5,13},{9,1},{13,5},{2,10},{6,14},... | collective-permute-start | bytes 442376 | tf_op jit(solution)/shard_map/ppermute | solution.py:507
  51.6 8.9 %collective-permute-start.21 = (bf16[2,9,16,256]{3,2,1,0:T(8,128)(2,1)S(1)}, bf16[2,9,16,256]{3,2,1,0:T(8,128)(2,1)S(1)}, u32[]{:S(2)}, u32[]{:S(2)}) collective-permute-start(bf16[2,9,16,256]{3,2,1,0:T(8,128)(2,1)S(1)} %get-tuple-element.114), channel_id=1, source_target_pairs={{0,4},{4,0},{8,12},{12,8},{1,5},{5,1},{9,13},{13,9},{2,6},{6,2},{1... | collective-permute-start | bytes 442376 | tf_op jit(solution)/shard_map/ppermute | solution.py:507
  60.6 7.9 %collective-permute-start.23 = (bf16[288,256]{1,0:T(8,128)(2,1)S(1)}, bf16[288,256]{1,0:T(8,128)(2,1)S(1)}, u32[]{:S(2)}, u32[]{:S(2)}) collective-permute-start(bf16[288,256]{1,0:T(8,128)(2,1)S(1)} %get-tuple-element.117.refs_0_), channel_id=1, source_target_pairs={{0,8},{4,12},{8,0},{12,4},{1,9},{5,13},{9,1},{13,5},{2,10},{6,14},... | collective-permute-start | bytes 442376 | tf_op jit(solution)/shard_map/ppermute | solution.py:507
  60.7 7.8 %collective-permute-start.22 = (bf16[288,256]{1,0:T(8,128)(2,1)S(1)}, bf16[288,256]{1,0:T(8,128)(2,1)S(1)}, u32[]{:S(2)}, u32[]{:S(2)}) collective-permute-start(bf16[288,256]{1,0:T(8,128)(2,1)S(1)} %get-tuple-element.117.refs_0_), channel_id=1, source_target_pairs={{0,2},{2,0},{1,3},{3,1},{4,6},{6,4},{5,7},{7,5},{8,10},{10,8},{9,1... | collective-permute-start | bytes 442376 | tf_op jit(solution)/shard_map/ppermute | solution.py:502
  61.3 9.8 %collective-permute-start.25 = (bf16[336,256]{1,0:T(8,128)(2,1)S(1)}, bf16[336,256]{1,0:T(8,128)(2,1)S(1)}, u32[]{:S(2)}, u32[]{:S(2)}) collective-permute-start(bf16[336,256]{1,0:T(8,128)(2,1)S(1)} %get-tuple-element.120), channel_id=1, source_target_pairs={{0,4},{4,0},{8,12},{12,8},{1,5},{5,1},{9,13},{13,9},{2,6},{6,2},{1... | collective-permute-start | bytes 516104 | tf_op jit(solution)/shard_map/ppermute | solution.py:507
  68.5 9.2 %collective-permute-start.24 = (bf16[336,256]{1,0:T(8,128)(2,1)S(1)}, bf16[336,256]{1,0:T(8,128)(2,1)S(1)}, u32[]{:S(2)}, u32[]{:S(2)}) collective-permute-start(bf16[336,256]{1,0:T(8,128)(2,1)S(1)} %get-tuple-element.119), channel_id=1, source_target_pairs={{0,12},{4,8},{8,4},{12,0},{1,13},{5,9},{9,5},{13,1},{2,14},{6,10},... | collective-permute-start | bytes 516104 | tf_op jit(solution)/shard_map/ppermute | solution.py:507
  70.9 6.8 %collective-permute-start.27 = (bf16[288,256]{1,0:T(8,128)(2,1)S(1)}, bf16[288,256]{1,0:T(8,128)(2,1)S(1)}, u32[]{:S(2)}, u32[]{:S(2)}) collective-permute-start(bf16[288,256]{1,0:T(8,128)(2,1)S(1)} %collective-permute-done.23.refs_2_), channel_id=1, source_target_pairs={{0,2},{2,0},{1,3},{3,1},{4,6},{6,4},{5,7},{7,5},{8,10},{10,8},{9,1... | collective-permute-start | bytes 442376 | tf_op jit(solution)/shard_map/ppermute | solution.py:502
  71.1 8.2 %collective-permute-start.26 = (bf16[288,256]{1,0:T(8,128)(2,1)S(1)}, bf16[288,256]{1,0:T(8,128)(2,1)S(1)}, u32[]{:S(2)}, u32[]{:S(2)}) collective-permute-start(bf16[288,256]{1,0:T(8,128)(2,1)S(1)} %slice.4), channel_id=1, source_target_pairs={{0,2},{2,0},{1,3},{3,1},{4,6},{6,4},{5,7},{7,5},{8,10},{10,8},{9,1... | collective-permute-start | bytes 442376 | tf_op jit(solution)/shard_map/ppermute | solution.py:502
  79.3 5.6 %collective-permute-start.28 = (bf16[352,256]{1,0:T(8,128)(2,1)S(1)}, bf16[352,256]{1,0:T(8,128)(2,1)S(1)}, u32[]{:S(2)}, u32[]{:S(2)}) collective-permute-start(bf16[352,256]{1,0:T(8,128)(2,1)S(1)} %column_message.1), channel_id=1, source_target_pairs={{0,2},{2,0},{1,3},{3,1},{4,6},{6,4},{5,7},{7,5},{8,10},{10,8},{9,1... | collective-permute-start | bytes 540680 | tf_op jit(solution)/shard_map/ppermute | solution.py:502
  (11 other events, 58.8 us)

commit v22 on v20

--- a/solution.py
+++ b/solution.py
@@ -413,9 +413,9 @@
     send[...] = (kept[1] + got[1].astype(F32)).astype(BF16)
 
 
-def add_workers(kept, got_3, got_2, got_1, rim_1, rim_3, out, out_1, out_3):
+def add_workers(kept, got_2, got_3, got_1, rim_1, rim_3, out, out_1, out_3):
     value = kept[...]
-    for part in (got_3, got_2, got_1):
+    for part in (got_2, got_3, got_1):
         value = value + part[...].astype(F32)
     value = value.astype(BF16).reshape(PART, FULL)
     out[...] = value
@@ -631,7 +631,7 @@
             kept, far_got
         )
         sends, at_owner[3] = tie((sends[::-1], at_owner[3]))
-        got = [flip(sends[0], "blk", 3), flip(sends[1], "blk", 2)]
+        got = [flip(sends[1], "blk", 2), flip(sends[0], "blk", 3)]
         canvas, *rims = owner(at_owner)
         near_got, canvas = tie((near_got, canvas))
         keep, send = call(

time: 85.4 us -> 84.6 us (level)
  waiting for transfers between devices: 35 us -> 33.6 us
    ppermute x12, waiting for transfers between devices: 21.8 us -> 20.5 us  [flip(): return lax.ppermute(value, axis, [(i, i ^ step) for i in range(size)])]
where the time goes in v22:
time: 84.6 us; the launch traced here: 84.4 us
  waiting for transfers between devices  33.6 us (40%)
  starting transfers between devices  27.1 us (32%)
  Pallas kernels  21.1 us (25%)
  local copies, waits for them, and re-layouts  1.71 us (2%)
  between operations  0.93 us (1%)
    ppermute x12, waiting for transfers between devices, flip(): return lax.ppermute(value, axis, [(i, i ^ step) for i in range(size)])  20.5 us
    ppermute x12, starting transfers between devices, flip(): return lax.ppermute(value, axis, [(i, i ^ step) for i in range(size)])  19.8 us
    ppermute x17, waiting for transfers between devices, swap(): return lax.ppermute(value, axis, [(0, 1), (1, 0)])  13 us
    ppermute x17, starting transfers between devices, swap(): return lax.ppermute(value, axis, [(0, 1), (1, 0)])  7.37 us
    pallas_call x1, Pallas kernels, shards(): call(functools.partial(worker, scale, owners, columns, capacity, permuted...  6.52 us
    pallas_call x1, Pallas kernels, owner(): call(functools.partial(owner_canvas, owners, capacity, wide, permuted), [...  5.8 us
    pallas_call x1, Pallas kernels, shards(): call(owner_spread, shape((MIDDLE, MIDDLE, TILE_BLOCKS, FULL), BF16), [VME...  2.93 us
    pallas_call x1, Pallas kernels, shards(): call(lay, [shape(grad_out.shape, BF16), shape(slab, F32)] + weights, [VME...  1.76 us
  transfers between devices with their start and end apart: 29, of which 14 were waited for; matrix products, arithmetic and copies ran while one was open for 0% of the time, Pallas kernels for 24%

profile of v22, /device:TPU:0, one launch (start us, length us, event | category | flops | bytes accessed | tf_op | source)
XLA Modules:
  0.0 84.4 jit_solution(10998256334946214385)
XLA Ops:
  1.2 1.4 %pack_cotangents.1 = (bf16[8,64,128]{2,1,0:T(8,128)(2,1)S(1)}, bf16[8,64,128]{2,1,0:T(8,128)(2,1)S(1)}, bf16[8,64,128]{2,1,0:T(8,128)(2,1)S(1)}, bf16[8,64,128]{2,1,0:T(8,128)(2,1)S(1)}) custom-call(s32[4,16]{1,0:T(4,128)} %bitcast.17, bf16[8,8,32,128]{3,2,1,0:T(8,128)(2,1)} %bitcast.12), custom_call_target="tpu_custom_call" | custom-call | flops 1 | bytes 1 | tf_op jit(solution)/shard_map/pack_cotangents/pallas_call | solution.py:539
  2.7 5.1 %collective-permute-start = (bf16[8,64,128]{2,1,0:T(8,128)(2,1)S(1)}, bf16[8,64,128]{2,1,0:T(8,128)(2,1)S(1)}, u32[]{:S(2)}, u32[]{:S(2)}) collective-permute-start(bf16[8,64,128]{2,1,0:T(8,128)(2,1)S(1)} %get-tuple-element.73), channel_id=1, source_target_pairs={{0,12},{4,8},{8,4},{12,0},{1,13},{5,9},{9,5},{13,1},{2,14},{6,10},... | collective-permute-start | bytes 393224 | tf_op jit(solution)/shard_map/ppermute | solution.py:507
  10.1 1.6 %pack_saved.1 = (bf16[10,160,128]{2,1,0:T(8,128)(2,1)S(1)}, bf16[10,80,128]{2,1,0:T(8,128)(2,1)S(1)}, bf16[10,80,128]{2,1,0:T(8,128)(2,1)S(1)}, bf16[10,80,128]{2,1,0:T(8,128)(2,1)S(1)}, bf16[10,80,128]{2,1,0:T(8,128)(2,1)S(1)}) custom-call(s32[4,16]{1,0:T(4,128)S(1)} %bitcast.18, bf16[10,160,128]{2,1,0:T(8,128)(2,1)S(1)} %bitcast.16), custom_call_target="tpu_custom_call" | custom-call | flops 1 | bytes 1 | tf_op jit(solution)/shard_map/pack_saved/pallas_call | solution.py:558
  12.1 6.9 %collective-permute-done.1.refs_2_ = bf16[8,64,128]{2,1,0:T(8,128)(2,1)S(1)} collective-permute-done((bf16[8,64,128]{2,1,0:T(8,128)(2,1)S(1)}, bf16[8,64,128]{2,1,0:T(8,128)(2,1)S(1)}, u32[]{:S(2)}, u32[]{:S(2)}) %collective-permute-start.1) | collective-permute-done | bytes 131104 | tf_op jit(solution)/shard_map/ppermute | solution.py:507
  19.1 3.1 %collective-permute-start.11 = (bf16[10,80,128]{2,1,0:T(8,128)(2,1)S(1)}, bf16[10,80,128]{2,1,0:T(8,128)(2,1)S(1)}, u32[]{:S(2)}, u32[]{:S(2)}) collective-permute-start(bf16[10,80,128]{2,1,0:T(8,128)(2,1)S(1)} %get-tuple-element.94), channel_id=1, source_target_pairs={{0,4},{4,0},{8,12},{12,8},{1,5},{5,1},{9,13},{13,9},{2,6},{6,2},{1... | collective-permute-start | bytes 614408 | tf_op jit(solution)/shard_map/ppermute | solution.py:507
  24.0 6.5 %worker.1 = (f32[4,2,9,16,256]{4,3,2,1,0:T(8,128)S(1)}, bf16[2,2,9,16,256]{4,3,2,1,0:T(8,128)(2,1)S(1)}, bf16[2,2,9,16,256]{4,3,2,1,0:T(8,128)(2,1)S(1)}) custom-call(s32[4,16]{1,0:T(4,128)S(1)} %bitcast.19, bf16[8,64,128]{2,1,0:T(8,128)(2,1)S(1)} %get-tuple-element.83.refs_0_, bf16[8,64,128]{2,1,0:T(8,128)(2,1)S(1)} %collective-permute-done.2.refs_1_, ...), custom_call_target="tpu_custom_call" | custom-call | flops 1 | bytes 1 | tf_op jit(solution)/shard_map/worker/pallas_call | solution.py:575
  30.8 1.5 %collective-permute-start.13 = (bf16[2,2,9,16,256]{4,3,2,1,0:T(8,128)(2,1)S(1)}, bf16[2,2,9,16,256]{4,3,2,1,0:T(8,128)(2,1)S(1)}, u32[]{:S(2)}, u32[]{:S(2)}) collective-permute-start(bf16[2,2,9,16,256]{4,3,2,1,0:T(8,128)(2,1)S(1)} %get-tuple-element.101), channel_id=1, source_target_pairs={{0,2},{2,0},{1,3},{3,1},{4,6},{6,4},{5,7},{7,5},{8,10},{10,8},{9,1... | collective-permute-start | bytes 884744 | tf_op jit(solution)/shard_map/ppermute | solution.py:502
  32.3 1.4 %collective-permute-start.14 = (bf16[10,80,128]{2,1,0:T(8,128)(2,1)S(1)}, bf16[10,80,128]{2,1,0:T(8,128)(2,1)S(1)}, u32[]{:S(2)}, u32[]{:S(2)}) collective-permute-start(bf16[10,80,128]{2,1,0:T(8,128)(2,1)S(1)} %get-tuple-element.105), channel_id=1, source_target_pairs={{0,12},{4,8},{8,4},{12,0},{1,13},{5,9},{9,5},{13,1},{2,14},{6,10},... | collective-permute-start | bytes 614408 | tf_op jit(solution)/shard_map/ppermute | solution.py:507
  34.8 2.9 %owner_spread.1.refs_8_ = bf16[10,10,32,256]{3,2,1,0:T(8,128)(2,1)S(1)} custom-call(bf16[8,8,32,128]{3,2,1,0:T(8,128)(2,1)S(1)} %bitcast.14, bf16[8,8,32,128]{3,2,1,0:T(8,128)(2,1)S(1)} %collective-permute-done.12.tile_other, bf16[9,128,256]{2,1,0:T(8,128)(2,1)S(1)} %copy-done.1, bf16[9,128,256]{2,1,0:T(8,128)(2,1)S(1)} %collective-permute-done.3.refs_11_.second_other), custom_call_target="tpu_custom_call" | custom-call | flops 1 | bytes 1 | tf_op jit(solution)/shard_map/owner_spread/pallas_call | solution.py:601
  37.8 2.9 %collective-permute-done.13.got = bf16[2,2,9,16,256]{4,3,2,1,0:T(8,128)(2,1)S(1)} collective-permute-done((bf16[2,2,9,16,256]{4,3,2,1,0:T(8,128)(2,1)S(1)}, bf16[2,2,9,16,256]{4,3,2,1,0:T(8,128)(2,1)S(1)}, u32[]{:S(2)}, u32[]{:S(2)}) %collective-permute-start.13) | collective-permute-done | bytes 294944 | tf_op jit(solution)/shard_map/ppermute | solution.py:502
  41.4 2.8 %collective-permute-start.19 = (bf16[2,9,16,256]{3,2,1,0:T(8,128)(2,1)S(1)}, bf16[2,9,16,256]{3,2,1,0:T(8,128)(2,1)S(1)}, u32[]{:S(2)}, u32[]{:S(2)}) collective-permute-start(bf16[2,9,16,256]{3,2,1,0:T(8,128)(2,1)S(1)} %get-tuple-element.112), channel_id=1, source_target_pairs={{0,8},{4,12},{8,0},{12,4},{1,9},{5,13},{9,1},{13,5},{2,10},{6,14},... | collective-permute-start | bytes 442376 | tf_op jit(solution)/shard_map/ppermute | solution.py:507
  44.2 2.0 %collective-permute-start.20 = (bf16[2,9,16,256]{3,2,1,0:T(8,128)(2,1)S(1)}, bf16[2,9,16,256]{3,2,1,0:T(8,128)(2,1)S(1)}, u32[]{:S(2)}, u32[]{:S(2)}) collective-permute-start(bf16[2,9,16,256]{3,2,1,0:T(8,128)(2,1)S(1)} %get-tuple-element.113), channel_id=1, source_target_pairs={{0,12},{4,8},{8,4},{12,0},{1,13},{5,9},{9,5},{13,1},{2,14},{6,10},... | collective-permute-start | bytes 442376 | tf_op jit(solution)/shard_map/ppermute | solution.py:507
  46.1 5.8 %owner_canvas.1 = (f32[68,40,128]{2,1,0:T(8,128)S(1)}, bf16[48,256]{1,0:T(8,128)(2,1)S(1)}, bf16[48,256]{1,0:T(8,128)(2,1)S(1)}) custom-call(s32[4,16]{1,0:T(4,128)S(1)} %bitcast.20, bf16[10,80,128]{2,1,0:T(8,128)(2,1)S(1)} %get-tuple-element.91.refs_0_, bf16[10,80,128]{2,1,0:T(8,128)(2,1)S(1)} %collective-permute-done.11.refs_1_, ...), custom_call_target="tpu_custom_call" | custom-call | flops 1 | bytes 1 | tf_op jit(solution)/shard_map/owner_canvas/pallas_call | solution.py:615
  52.1 3.2 %collective-permute-done.19.got_2 = bf16[2,9,16,256]{3,2,1,0:T(8,128)(2,1)S(1)} collective-permute-done((bf16[2,9,16,256]{3,2,1,0:T(8,128)(2,1)S(1)}, bf16[2,9,16,256]{3,2,1,0:T(8,128)(2,1)S(1)}, u32[]{:S(2)}, u32[]{:S(2)}) %collective-permute-start.19) | collective-permute-done | bytes 147488 | tf_op jit(solution)/shard_map/ppermute | solution.py:507
  55.3 2.8 %collective-permute-done.21.got_1 = bf16[2,9,16,256]{3,2,1,0:T(8,128)(2,1)S(1)} collective-permute-done((bf16[2,9,16,256]{3,2,1,0:T(8,128)(2,1)S(1)}, bf16[2,9,16,256]{3,2,1,0:T(8,128)(2,1)S(1)}, u32[]{:S(2)}, u32[]{:S(2)}) %collective-permute-start.21) | collective-permute-done | bytes 147488 | tf_op jit(solution)/shard_map/ppermute | solution.py:507
  58.2 1.1 %collective-permute-start.23 = (bf16[288,256]{1,0:T(8,128)(2,1)S(1)}, bf16[288,256]{1,0:T(8,128)(2,1)S(1)}, u32[]{:S(2)}, u32[]{:S(2)}) collective-permute-start(bf16[288,256]{1,0:T(8,128)(2,1)S(1)} %get-tuple-element.117.refs_0_), channel_id=1, source_target_pairs={{0,8},{4,12},{8,0},{12,4},{1,9},{5,13},{9,1},{13,5},{2,10},{6,14},... | collective-permute-start | bytes 442376 | tf_op jit(solution)/shard_map/ppermute | solution.py:507
  59.9 1.6 %collective-permute-start.25 = (bf16[336,256]{1,0:T(8,128)(2,1)S(1)}, bf16[336,256]{1,0:T(8,128)(2,1)S(1)}, u32[]{:S(2)}, u32[]{:S(2)}) collective-permute-start(bf16[336,256]{1,0:T(8,128)(2,1)S(1)} %get-tuple-element.120), channel_id=1, source_target_pairs={{0,4},{4,0},{8,12},{12,8},{1,5},{5,1},{9,13},{13,9},{2,6},{6,2},{1... | collective-permute-start | bytes 516104 | tf_op jit(solution)/shard_map/ppermute | solution.py:507
  61.4 6.2 %collective-permute-done.23.refs_2_ = bf16[288,256]{1,0:T(8,128)(2,1)S(1)} collective-permute-done((bf16[288,256]{1,0:T(8,128)(2,1)S(1)}, bf16[288,256]{1,0:T(8,128)(2,1)S(1)}, u32[]{:S(2)}, u32[]{:S(2)}) %collective-permute-start.23) | collective-permute-done | bytes 147488 | tf_op jit(solution)/shard_map/ppermute | solution.py:507
  67.7 2.0 %collective-permute-start.24 = (bf16[336,256]{1,0:T(8,128)(2,1)S(1)}, bf16[336,256]{1,0:T(8,128)(2,1)S(1)}, u32[]{:S(2)}, u32[]{:S(2)}) collective-permute-start(bf16[336,256]{1,0:T(8,128)(2,1)S(1)} %get-tuple-element.119), channel_id=1, source_target_pairs={{0,12},{4,8},{8,4},{12,0},{1,13},{5,9},{9,5},{13,1},{2,14},{6,10},... | collective-permute-start | bytes 516104 | tf_op jit(solution)/shard_map/ppermute | solution.py:507
  70.2 1.6 %collective-permute-start.26 = (bf16[288,256]{1,0:T(8,128)(2,1)S(1)}, bf16[288,256]{1,0:T(8,128)(2,1)S(1)}, u32[]{:S(2)}, u32[]{:S(2)}) collective-permute-start(bf16[288,256]{1,0:T(8,128)(2,1)S(1)} %slice.4), channel_id=1, source_target_pairs={{0,2},{2,0},{1,3},{3,1},{4,6},{6,4},{5,7},{7,5},{8,10},{10,8},{9,1... | collective-permute-start | bytes 442376 | tf_op jit(solution)/shard_map/ppermute | solution.py:502
  71.8 4.4 %collective-permute-done.27.refs_6_ = bf16[288,256]{1,0:T(8,128)(2,1)S(1)} collective-permute-done((bf16[288,256]{1,0:T(8,128)(2,1)S(1)}, bf16[288,256]{1,0:T(8,128)(2,1)S(1)}, u32[]{:S(2)}, u32[]{:S(2)}) %collective-permute-start.27) | collective-permute-done | bytes 147488 | tf_op jit(solution)/shard_map/ppermute | solution.py:502
  76.2 1.6 %collective-permute-done.26.refs_5_ = bf16[288,256]{1,0:T(8,128)(2,1)S(1)} collective-permute-done((bf16[288,256]{1,0:T(8,128)(2,1)S(1)}, bf16[288,256]{1,0:T(8,128)(2,1)S(1)}, u32[]{:S(2)}, u32[]{:S(2)}) %collective-permute-start.26) | collective-permute-done | bytes 147488 | tf_op jit(solution)/shard_map/ppermute | solution.py:502
  78.9 1.8 %lay.1 = (bf16[64,32,128]{2,1,0:T(8,128)(2,1)}, f32[64,16,128]{2,1,0:T(8,128)S(1)}, f32[9,128,256]{2,1,0:T(8,128)}, f32[9,128,256]{2,1,0:T(8,128)}) custom-call(bf16[64,32,128]{2,1,0:T(8,128)(2,1)S(1)} %copy-done, f32[68,40,128]{2,1,0:T(8,128)S(1)} %get-tuple-element.109.canvas, bf16[288,256]{1,0:T(8,128)(2,1)S(1)} %get-tuple-element.117.refs_0_, ...), custom_call_target="tpu_custom_call" | custom-call | flops 1 | bytes 1 | tf_op jit(solution)/shard_map/lay/pallas_call | solution.py:660
  80.6 2.8 %collective-permute-done.28.last = bf16[352,256]{1,0:T(8,128)(2,1)S(1)} collective-permute-done((bf16[352,256]{1,0:T(8,128)(2,1)S(1)}, bf16[352,256]{1,0:T(8,128)(2,1)S(1)}, u32[]{:S(2)}, u32[]{:S(2)}) %collective-permute-start.28) | collective-permute-done | bytes 180256 | tf_op jit(solution)/shard_map/ppermute | solution.py:502
  (58 shorter events, 10.5 us)
Async XLA Ops:
  0.6 7.8 %collective-permute-start.3 = (bf16[9,128,256]{2,1,0:T(8,128)(2,1)}, bf16[9,128,256]{2,1,0:T(8,128)(2,1)S(1)}, u32[]{:S(2)}, u32[]{:S(2)}) collective-permute-start(bf16[9,128,256]{2,1,0:T(8,128)(2,1)} %second.1), channel_id=1, source_target_pairs={{0,1},{1,0},{2,3},{3,2},{4,5},{5,4},{6,7},{7,6},{8,9},{9,8},{10,11... | collective-permute-start | bytes 1769480 | tf_op jit(solution)/shard_map/ppermute | solution.py:502
  1.2 21.5 %collective-permute-start.8 = (bf16[10,160,128]{2,1,0:T(8,128)(2,1)}, bf16[10,160,128]{2,1,0:T(8,128)(2,1)S(1)}, u32[]{:S(2)}, u32[]{:S(2)}) collective-permute-start(bf16[10,160,128]{2,1,0:T(8,128)(2,1)} %bitcast.15), channel_id=1, source_target_pairs={{0,1},{1,0},{2,3},{3,2},{4,5},{5,4},{6,7},{7,6},{8,9},{9,8},{10,11... | collective-permute-start | bytes 1228808 | tf_op jit(solution)/shard_map/ppermute | solution.py:502
  2.7 9.5 %collective-permute-start = (bf16[8,64,128]{2,1,0:T(8,128)(2,1)S(1)}, bf16[8,64,128]{2,1,0:T(8,128)(2,1)S(1)}, u32[]{:S(2)}, u32[]{:S(2)}) collective-permute-start(bf16[8,64,128]{2,1,0:T(8,128)(2,1)S(1)} %get-tuple-element.73), channel_id=1, source_target_pairs={{0,12},{4,8},{8,4},{12,0},{1,13},{5,9},{9,5},{13,1},{2,14},{6,10},... | collective-permute-start | bytes 393224 | tf_op jit(solution)/shard_map/ppermute | solution.py:507
  7.7 11.3 %collective-permute-start.1 = (bf16[8,64,128]{2,1,0:T(8,128)(2,1)S(1)}, bf16[8,64,128]{2,1,0:T(8,128)(2,1)S(1)}, u32[]{:S(2)}, u32[]{:S(2)}) collective-permute-start(bf16[8,64,128]{2,1,0:T(8,128)(2,1)S(1)} %get-tuple-element.74), channel_id=1, source_target_pairs={{0,8},{4,12},{8,0},{12,4},{1,9},{5,13},{9,1},{13,5},{2,10},{6,14},... | collective-permute-start | bytes 393224 | tf_op jit(solution)/shard_map/ppermute | solution.py:507
  7.8 11.3 %collective-permute-start.2 = (bf16[8,64,128]{2,1,0:T(8,128)(2,1)S(1)}, bf16[8,64,128]{2,1,0:T(8,128)(2,1)S(1)}, u32[]{:S(2)}, u32[]{:S(2)}) collective-permute-start(bf16[8,64,128]{2,1,0:T(8,128)(2,1)S(1)} %get-tuple-element.75), channel_id=1, source_target_pairs={{0,4},{4,0},{8,12},{12,8},{1,5},{5,1},{9,13},{13,9},{2,6},{6,2},{1... | collective-permute-start | bytes 393224 | tf_op jit(solution)/shard_map/ppermute | solution.py:507
  8.4 10.7 %collective-permute-start.4 = (bf16[8,64,128]{2,1,0:T(8,128)(2,1)S(1)}, bf16[8,64,128]{2,1,0:T(8,128)(2,1)S(1)}, u32[]{:S(2)}, u32[]{:S(2)}) collective-permute-start(bf16[8,64,128]{2,1,0:T(8,128)(2,1)S(1)} %get-tuple-element.83.refs_0_), channel_id=1, source_target_pairs={{0,1},{1,0},{2,3},{3,2},{4,5},{5,4},{6,7},{7,6},{8,9},{9,8},{10,11... | collective-permute-start | bytes 393224 | tf_op jit(solution)/shard_map/ppermute | solution.py:502
  19.1 11.5 %collective-permute-start.10 = (bf16[10,80,128]{2,1,0:T(8,128)(2,1)S(1)}, bf16[10,80,128]{2,1,0:T(8,128)(2,1)S(1)}, u32[]{:S(2)}, u32[]{:S(2)}) collective-permute-start(bf16[10,80,128]{2,1,0:T(8,128)(2,1)S(1)} %get-tuple-element.93), channel_id=1, source_target_pairs={{0,8},{4,12},{8,0},{12,4},{1,9},{5,13},{9,1},{13,5},{2,10},{6,14},... | collective-permute-start | bytes 614408 | tf_op jit(solution)/shard_map/ppermute | solution.py:507
  19.1 11.6 %collective-permute-start.11 = (bf16[10,80,128]{2,1,0:T(8,128)(2,1)S(1)}, bf16[10,80,128]{2,1,0:T(8,128)(2,1)S(1)}, u32[]{:S(2)}, u32[]{:S(2)}) collective-permute-start(bf16[10,80,128]{2,1,0:T(8,128)(2,1)S(1)} %get-tuple-element.94), channel_id=1, source_target_pairs={{0,4},{4,0},{8,12},{12,8},{1,5},{5,1},{9,13},{13,9},{2,6},{6,2},{1... | collective-permute-start | bytes 614408 | tf_op jit(solution)/shard_map/ppermute | solution.py:507
  30.8 9.8 %collective-permute-start.13 = (bf16[2,2,9,16,256]{4,3,2,1,0:T(8,128)(2,1)S(1)}, bf16[2,2,9,16,256]{4,3,2,1,0:T(8,128)(2,1)S(1)}, u32[]{:S(2)}, u32[]{:S(2)}) collective-permute-start(bf16[2,2,9,16,256]{4,3,2,1,0:T(8,128)(2,1)S(1)} %get-tuple-element.101), channel_id=1, source_target_pairs={{0,2},{2,0},{1,3},{3,1},{4,6},{6,4},{5,7},{7,5},{8,10},{10,8},{9,1... | collective-permute-start | bytes 884744 | tf_op jit(solution)/shard_map/ppermute | solution.py:502
  32.3 9.0 %collective-permute-start.14 = (bf16[10,80,128]{2,1,0:T(8,128)(2,1)S(1)}, bf16[10,80,128]{2,1,0:T(8,128)(2,1)S(1)}, u32[]{:S(2)}, u32[]{:S(2)}) collective-permute-start(bf16[10,80,128]{2,1,0:T(8,128)(2,1)S(1)} %get-tuple-element.105), channel_id=1, source_target_pairs={{0,12},{4,8},{8,4},{12,0},{1,13},{5,9},{9,5},{13,1},{2,14},{6,10},... | collective-permute-start | bytes 614408 | tf_op jit(solution)/shard_map/ppermute | solution.py:507
  33.8 18.2 %collective-permute-start.9 = (bf16[2,2,9,16,256]{4,3,2,1,0:T(8,128)(2,1)S(1)}, bf16[2,2,9,16,256]{4,3,2,1,0:T(8,128)(2,1)S(1)}, u32[]{:S(2)}, u32[]{:S(2)}) collective-permute-start(bf16[2,2,9,16,256]{4,3,2,1,0:T(8,128)(2,1)S(1)} %get-tuple-element.90), channel_id=1, source_target_pairs={{0,2},{2,0},{1,3},{3,1},{4,6},{6,4},{5,7},{7,5},{8,10},{10,8},{9,1... | collective-permute-start | bytes 884744 | tf_op jit(solution)/shard_map/ppermute | solution.py:502
  34.3 7.1 %collective-permute-start.15 = (bf16[10,80,128]{2,1,0:T(8,128)(2,1)S(1)}, bf16[10,80,128]{2,1,0:T(8,128)(2,1)S(1)}, u32[]{:S(2)}, u32[]{:S(2)}) collective-permute-start(bf16[10,80,128]{2,1,0:T(8,128)(2,1)S(1)} %get-tuple-element.91.refs_0_), channel_id=1, source_target_pairs={{0,1},{1,0},{2,3},{3,2},{4,5},{5,4},{6,7},{7,6},{8,9},{9,8},{10,11... | collective-permute-start | bytes 614408 | tf_op jit(solution)/shard_map/ppermute | solution.py:502
  34.3 9.9 %collective-permute-start.16 = (bf16[10,80,128]{2,1,0:T(8,128)(2,1)S(1)}, bf16[10,80,128]{2,1,0:T(8,128)(2,1)S(1)}, u32[]{:S(2)}, u32[]{:S(2)}) collective-permute-start(bf16[10,80,128]{2,1,0:T(8,128)(2,1)S(1)} %collective-permute-done.11.refs_1_), channel_id=1, source_target_pairs={{0,1},{1,0},{2,3},{3,2},{4,5},{5,4},{6,7},{7,6},{8,9},{9,8},{10,11... | collective-permute-start | bytes 614408 | tf_op jit(solution)/shard_map/ppermute | solution.py:502
  40.6 5.5 %collective-permute-start.17 = (bf16[10,80,128]{2,1,0:T(8,128)(2,1)S(1)}, bf16[10,80,128]{2,1,0:T(8,128)(2,1)S(1)}, u32[]{:S(2)}, u32[]{:S(2)}) collective-permute-start(bf16[10,80,128]{2,1,0:T(8,128)(2,1)S(1)} %collective-permute-done.10.refs_2_), channel_id=1, source_target_pairs={{0,1},{1,0},{2,3},{3,2},{4,5},{5,4},{6,7},{7,6},{8,9},{9,8},{10,11... | collective-permute-start | bytes 614408 | tf_op jit(solution)/shard_map/ppermute | solution.py:502
  41.4 13.9 %collective-permute-start.19 = (bf16[2,9,16,256]{3,2,1,0:T(8,128)(2,1)S(1)}, bf16[2,9,16,256]{3,2,1,0:T(8,128)(2,1)S(1)}, u32[]{:S(2)}, u32[]{:S(2)}) collective-permute-start(bf16[2,9,16,256]{3,2,1,0:T(8,128)(2,1)S(1)} %get-tuple-element.112), channel_id=1, source_target_pairs={{0,8},{4,12},{8,0},{12,4},{1,9},{5,13},{9,1},{13,5},{2,10},{6,14},... | collective-permute-start | bytes 442376 | tf_op jit(solution)/shard_map/ppermute | solution.py:507
  44.2 11.1 %collective-permute-start.20 = (bf16[2,9,16,256]{3,2,1,0:T(8,128)(2,1)S(1)}, bf16[2,9,16,256]{3,2,1,0:T(8,128)(2,1)S(1)}, u32[]{:S(2)}, u32[]{:S(2)}) collective-permute-start(bf16[2,9,16,256]{3,2,1,0:T(8,128)(2,1)S(1)} %get-tuple-element.113), channel_id=1, source_target_pairs={{0,12},{4,8},{8,4},{12,0},{1,13},{5,9},{9,5},{13,1},{2,14},{6,10},... | collective-permute-start | bytes 442376 | tf_op jit(solution)/shard_map/ppermute | solution.py:507
  52.0 6.1 %collective-permute-start.21 = (bf16[2,9,16,256]{3,2,1,0:T(8,128)(2,1)S(1)}, bf16[2,9,16,256]{3,2,1,0:T(8,128)(2,1)S(1)}, u32[]{:S(2)}, u32[]{:S(2)}) collective-permute-start(bf16[2,9,16,256]{3,2,1,0:T(8,128)(2,1)S(1)} %get-tuple-element.114), channel_id=1, source_target_pairs={{0,4},{4,0},{8,12},{12,8},{1,5},{5,1},{9,13},{13,9},{2,6},{6,2},{1... | collective-permute-start | bytes 442376 | tf_op jit(solution)/shard_map/ppermute | solution.py:507
  58.2 9.4 %collective-permute-start.23 = (bf16[288,256]{1,0:T(8,128)(2,1)S(1)}, bf16[288,256]{1,0:T(8,128)(2,1)S(1)}, u32[]{:S(2)}, u32[]{:S(2)}) collective-permute-start(bf16[288,256]{1,0:T(8,128)(2,1)S(1)} %get-tuple-element.117.refs_0_), channel_id=1, source_target_pairs={{0,8},{4,12},{8,0},{12,4},{1,9},{5,13},{9,1},{13,5},{2,10},{6,14},... | collective-permute-start | bytes 442376 | tf_op jit(solution)/shard_map/ppermute | solution.py:507
  59.3 8.3 %collective-permute-start.22 = (bf16[288,256]{1,0:T(8,128)(2,1)S(1)}, bf16[288,256]{1,0:T(8,128)(2,1)S(1)}, u32[]{:S(2)}, u32[]{:S(2)}) collective-permute-start(bf16[288,256]{1,0:T(8,128)(2,1)S(1)} %get-tuple-element.117.refs_0_), channel_id=1, source_target_pairs={{0,2},{2,0},{1,3},{3,1},{4,6},{6,4},{5,7},{7,5},{8,10},{10,8},{9,1... | collective-permute-start | bytes 442376 | tf_op jit(solution)/shard_map/ppermute | solution.py:502
  59.9 10.3 %collective-permute-start.25 = (bf16[336,256]{1,0:T(8,128)(2,1)S(1)}, bf16[336,256]{1,0:T(8,128)(2,1)S(1)}, u32[]{:S(2)}, u32[]{:S(2)}) collective-permute-start(bf16[336,256]{1,0:T(8,128)(2,1)S(1)} %get-tuple-element.120), channel_id=1, source_target_pairs={{0,4},{4,0},{8,12},{12,8},{1,5},{5,1},{9,13},{13,9},{2,6},{6,2},{1... | collective-permute-start | bytes 516104 | tf_op jit(solution)/shard_map/ppermute | solution.py:507
  67.7 8.6 %collective-permute-start.24 = (bf16[336,256]{1,0:T(8,128)(2,1)S(1)}, bf16[336,256]{1,0:T(8,128)(2,1)S(1)}, u32[]{:S(2)}, u32[]{:S(2)}) collective-permute-start(bf16[336,256]{1,0:T(8,128)(2,1)S(1)} %get-tuple-element.119), channel_id=1, source_target_pairs={{0,12},{4,8},{8,4},{12,0},{1,13},{5,9},{9,5},{13,1},{2,14},{6,10},... | collective-permute-start | bytes 516104 | tf_op jit(solution)/shard_map/ppermute | solution.py:507
  69.7 6.5 %collective-permute-start.27 = (bf16[288,256]{1,0:T(8,128)(2,1)S(1)}, bf16[288,256]{1,0:T(8,128)(2,1)S(1)}, u32[]{:S(2)}, u32[]{:S(2)}) collective-permute-start(bf16[288,256]{1,0:T(8,128)(2,1)S(1)} %collective-permute-done.23.refs_2_), channel_id=1, source_target_pairs={{0,2},{2,0},{1,3},{3,1},{4,6},{6,4},{5,7},{7,5},{8,10},{10,8},{9,1... | collective-permute-start | bytes 442376 | tf_op jit(solution)/shard_map/ppermute | solution.py:502
  70.2 7.6 %collective-permute-start.26 = (bf16[288,256]{1,0:T(8,128)(2,1)S(1)}, bf16[288,256]{1,0:T(8,128)(2,1)S(1)}, u32[]{:S(2)}, u32[]{:S(2)}) collective-permute-start(bf16[288,256]{1,0:T(8,128)(2,1)S(1)} %slice.4), channel_id=1, source_target_pairs={{0,2},{2,0},{1,3},{3,1},{4,6},{6,4},{5,7},{7,5},{8,10},{10,8},{9,1... | collective-permute-start | bytes 442376 | tf_op jit(solution)/shard_map/ppermute | solution.py:502
  77.9 5.6 %collective-permute-start.28 = (bf16[352,256]{1,0:T(8,128)(2,1)S(1)}, bf16[352,256]{1,0:T(8,128)(2,1)S(1)}, u32[]{:S(2)}, u32[]{:S(2)}) collective-permute-start(bf16[352,256]{1,0:T(8,128)(2,1)S(1)} %column_message.1), channel_id=1, source_target_pairs={{0,2},{2,0},{1,3},{3,1},{4,6},{6,4},{5,7},{7,5},{8,10},{10,8},{9,1... | collective-permute-start | bytes 540680 | tf_op jit(solution)/shard_map/ppermute | solution.py:502
  (11 other events, 61.1 us)
